TPU v7x, 32 devices: a whole 2x2x4 slice. The times are simulated.
32 devices in a mesh: member: 2 (over y), lat: 4 (over z), lev: 2 (over x), sub: 2 (over core).
Axes of the slice: x: 2, y: 2, z: 4, core: 2. Of those that a mesh axis runs over, the one named last changes fastest.
Arguments:
- thickness: float32 [32, 64, 1152], P(('member', 'lev', 'sub'), 'lat'), parts along dimension 0, may hold values from 0.5 to 1.5
- wind_u: float32 [32, 64, 1152], P(('member', 'lev', 'sub'), 'lat'), parts along dimension 0, may hold values from -0.2 to 0.2
- wind_v: float32 [32, 64, 1152], P(('member', 'lev', 'sub'), 'lat'), parts along dimension 0, may hold values from -0.2 to 0.2
- tracers: float32 [8, 16, 64, 1152], P('member', ('lev', 'sub'), 'lat'), parts along dimension 0, may hold values from 0 to 1
- level_weights: float32 [16], replicated, may hold values from 0.3 to 3
- cutoff: int32 [64], P('lat'), may hold values from 1 to 576, as said below
Outputs:
- thickness_out: float32 [32, 64, 1152], P(('member', 'lev', 'sub'), 'lat'), parts along dimension 0
- wind_u_out: float32 [32, 64, 1152], P(('member', 'lev', 'sub'), 'lat'), parts along dimension 0
- wind_v_out: float32 [32, 64, 1152], P(('member', 'lev', 'sub'), 'lat'), parts along dimension 0
- tracers_out: float32 [8, 16, 64, 1152], P('member', ('lev', 'sub'), 'lat'), parts along dimension 0
There are 2 independent parts, one for each index of `member`. A program takes and returns all parts, laid end to end along the dimension named above; an argument that names none is the same for every part. Nothing has to cross between parts.
Inputs may be any that keep to these rules, and one draw needn't show every extreme that they name: cutoff is 576 on every row 16 or more rows away from both poles; it is 1 on the two pole rows.
All inputs are finite; a program needn't handle non-finite values.
Results may differ from a plain program's by a relative error of at most 0.0003.
Values sent between devices are 32-bit elements; how exact they have to be, the bound alone decides.
No kernel may reach another device: no remote copies, remote signals or barrier semaphores. Data moves between devices by JAX's collectives and lax.ppermute only.
A program may use at most 64 MiB of HBM per device.

v0:
```python
import jax
import jax.numpy as jnp
from jax import lax
from jax.sharding import PartitionSpec as P


def extended_2(value, sides, width):
    for axis, dim in sides:
        size, length = (lax.axis_size(axis), value.shape[dim])
        up = [(i, (i + 1) % size) for i in range(size - 1)]
        down = [(j, i) for i, j in up]
        last = lax.slice_in_dim(value, length - width, length, axis=dim)
        leading = lax.slice_in_dim(value, 0, width, axis=dim)
        before = lax.ppermute(last, axis, up)
        after = lax.ppermute(leading, axis, down)
        value = jnp.concatenate([before, value, after], axis=dim)
    return value


def face_weight(faces, lat_rows):
    inside = (faces > 0) & (faces < lat_rows)
    return jnp.where(inside, jnp.sin(faces.astype(jnp.float32) * (jnp.pi / lat_rows)), 0.0)


def mass_fluxes(thick_ext, u_mid, v_ext, first_row, lat_rows):
    n = u_mid.shape[1]
    row_ids = first_row + jnp.arange(n, dtype=jnp.int32)
    south_wt = face_weight(row_ids, lat_rows)
    north_wt = face_weight(row_ids + 1, lat_rows)
    center = jnp.sin((row_ids.astype(jnp.float32) + 0.5) * (jnp.pi / lat_rows))
    thick_mid = thick_ext[:, 1:-1]
    eastward = u_mid * jnp.where(u_mid > 0, thick_mid, jnp.roll(thick_mid, -1, axis=-1))
    v_north = v_ext[:, 1:-1]
    v_south = v_ext[:, :-2]
    north_flux = v_north * jnp.where(v_north > 0, thick_mid, thick_ext[:, 2:]) * north_wt[:, None]
    south_flux = v_south * jnp.where(v_south > 0, thick_ext[:, :-2], thick_mid) * south_wt[:, None]
    thick_new = (
        thick_mid
        - (eastward - jnp.roll(eastward, 1, axis=-1))
        - (north_flux - south_flux) / center[:, None]
    )
    return (thick_new, eastward, north_flux, south_flux, center)


def tracer_step(
    tracer_ext, thick_mid, thick_new, eastward, north_flux, south_flux, v_ext, u_mid, center
):
    tracer_mid = tracer_ext[:, :, 1:-1]
    v_north = v_ext[:, 1:-1]
    v_south = v_ext[:, :-2]
    tracer_east = eastward * jnp.where(u_mid > 0, tracer_mid, jnp.roll(tracer_mid, -1, axis=-1))
    tracer_north = north_flux * jnp.where(v_north > 0, tracer_mid, tracer_ext[:, :, 2:])
    tracer_south = south_flux * jnp.where(v_south > 0, tracer_ext[:, :, :-2], tracer_mid)
    changed = thick_mid * tracer_mid - (tracer_east - jnp.roll(tracer_east, 1, axis=-1))
    changed = changed - (tracer_north - tracer_south) / center[:, None]
    return changed / thick_new


def spectral_filter(fields, kept_modes):
    N = fields.shape[-1]
    half_modes = N // 2 + 1
    width = (half_modes + 127) // 128 * 128
    points = jnp.arange(N, dtype=jnp.int32)
    wave_ids = jnp.arange(width, dtype=jnp.int32)
    angles = (points[:, None] * wave_ids[None, :] % N).astype(jnp.float32) * (2.0 * jnp.pi / N)
    table = jnp.concatenate([jnp.cos(angles), jnp.sin(angles)], axis=1)
    double = jnp.where((wave_ids == 0) | (wave_ids == N // 2), 1.0, 2.0)
    double = jnp.where(wave_ids < half_modes, double, 0.0)
    kept_half = (
        jnp.pad(kept_modes[:, :half_modes], ((0, 0), (0, width - half_modes))) * double[None, :]
    )
    kept_both = jnp.concatenate([kept_half, kept_half], axis=1)
    spectrum = jnp.einsum("arm,mk->ark", fields, table, precision=lax.Precision.HIGH) * kept_both
    summed = jnp.einsum("ark,mk->arm", spectrum, table, precision=lax.Precision.HIGH)
    return summed / N


def remap(thick_new, fields, weights):
    levels = thick_new.shape[0]
    column_mass = jnp.sum(thick_new, axis=0)
    fraction = weights / jnp.sum(weights)
    targets = column_mass[None] * jnp.cumsum(fraction)[:, None]
    source_low = jnp.cumsum(thick_new, axis=0) - thick_new

    def integrate(target_block):
        w = jnp.minimum(
            jnp.maximum(target_block[:, None, :] - source_low[None], 0.0), thick_new[None]
        )
        return jnp.sum(fields[:, None] * w[None], axis=2)

    integral = lax.map(integrate, targets.reshape(levels // 4, 4, targets.shape[1]))
    integral = jnp.transpose(integral, (1, 0, 2, 3)).reshape(
        fields.shape[0], levels, targets.shape[1]
    )
    integral_low = jnp.concatenate([jnp.zeros_like(integral[:, :1]), integral[:, :-1]], axis=1)
    target_thick = column_mass[None] * fraction[:, None]
    return jnp.concatenate(
        [target_thick[None], (integral - integral_low) / target_thick[None]], axis=0
    )


def per_device(thickness, wind_u, wind_v, tracers, level_weights, cutoff):
    L, R, N = thickness.shape
    lat_rows = R * lax.axis_size("lat")
    first_row = lax.axis_index("lat") * R
    stacked = jnp.concatenate([thickness[None], wind_v[None], wind_u[None], tracers], axis=0)
    extended = extended_2(stacked, (("lat", 2),), 2)
    thick_all, east_all, north_all, south_all, center_all = mass_fluxes(
        extended[0, :, 1:], extended[2, :, 2 : R + 3], extended[1, :, 1:], first_row, lat_rows
    )
    thick_new = thick_all[:, :R]
    thick_next = thick_all[:, 1:]
    eastward = east_all[:, :R]
    north_flux = north_all[:, :R]
    south_flux = south_all[:, :R]
    center = center_all[:R]
    v_ext = extended[1, :, 1 : R + 3]
    tracer_ext = extended[3:, :, 1 : R + 3]
    tracer_new = tracer_step(
        tracer_ext, thickness, thick_new, eastward, north_flux, south_flux, v_ext, wind_u, center
    )
    row_ids = first_row + jnp.arange(R, dtype=jnp.int32)
    new_u = wind_u - 0.05 * (jnp.roll(thick_new, -1, axis=-1) - thick_new)
    new_v = (wind_v - 0.05 * (thick_next - thick_new)) * (row_ids < lat_rows - 1)[:, None]
    wave_ids = jnp.arange(N, dtype=jnp.int32)
    wave_num = jnp.minimum(wave_ids, N - wave_ids)
    kept_modes = (wave_num[None, :] <= cutoff[:, None]).astype(jnp.float32)
    wind_pair = jnp.concatenate([new_u, new_v], axis=0)
    wind_pair = spectral_filter(wind_pair, kept_modes)
    stacked = jnp.concatenate([thick_new[None], wind_pair.reshape(2, L, R, N), tracer_new], axis=0)
    fields_count = stacked.shape[0]
    lev_count = lax.axis_size("lev")
    sub_count = lax.axis_size("sub")
    group_rows = R // (lev_count * sub_count)
    levels = L * lev_count * sub_count
    columns = lax.all_to_all(stacked, ("lev", "sub"), split_axis=2, concat_axis=1, tiled=True)
    flat = columns.reshape(fields_count, levels, group_rows * N)
    remapped = remap(flat[0], flat[1:], level_weights).reshape(fields_count, levels, group_rows, N)
    levels_back = lax.all_to_all(remapped, ("lev", "sub"), split_axis=1, concat_axis=2, tiled=True)
    return (levels_back[0], levels_back[1], levels_back[2], levels_back[3:])


def solution(mesh):
    placed = (
        P(("member", "lev", "sub"), "lat", None),
        P(("member", "lev", "sub"), "lat", None),
        P(("member", "lev", "sub"), "lat", None),
        P("member", ("lev", "sub"), "lat", None),
        P(),
        P("lat"),
    )
    return jax.shard_map(
        per_device,
        mesh=mesh,
        in_specs=placed,
        out_specs=(
            P(("member", "lev", "sub"), "lat", None),
            P(("member", "lev", "sub"), "lat", None),
            P(("member", "lev", "sub"), "lat", None),
            P("member", ("lev", "sub"), "lat", None),
        ),
        check_vma=False,
    )
```

profile of v0, /device:TPU:0, one launch (start us, length us, event | category | flops | bytes accessed | tf_op | source)
XLA Modules:
  0.0 116.8 jit_solution(704928468921031025)
XLA Ops:
  0.6 1.7 %pad_maximum_fusion.15 = (f32[7,4,2,1152]{3,2,1,0:T(2,128)S(1)}, f32[7,4,2,1152]{3,2,1,0:T(2,128)S(1)}) fusion(f32[4,4,16,1152]{3,2,1,0:T(8,128)} %param.11, f32[1,4,16,1152]{3,2,1,0:T(8,128)} %bitcast.58, f32[1,4,16,1152]{3,2,1,0:T(8,128)} %bitcast.64, f32[1,4,16,1152]{3,2,1,0:T(8,128)} %bitcast.69), kind=kLoop, calls=%fused_computation.74 | loop fusion | flops 387072 | bytes 2580480 | tf_op jit(solution)/shard_map/concatenate | solution.py:106
  2.4 4.9 %collective-permute-start = (f32[7,4,2,1152]{3,2,1,0:T(2,128)S(1)}, f32[7,4,2,1152]{3,2,1,0:T(2,128)S(1)}, u32[]{:S(2)}, u32[]{:S(2)}) collective-permute-start(f32[7,4,2,1152]{3,2,1,0:T(2,128)S(1)} %get-tuple-element.72), channel_id=1, source_target_pairs={{0,4},{4,8},{8,12},{1,5},{5,9},{9,13},{2,6},{6,10},{10,14},{3,7},{... | collective-permute-start | bytes 774152 | tf_op jit(solution)/shard_map/ppermute | solution.py:14
  7.3 1.3 %collective-permute-start.1 = (f32[7,4,2,1152]{3,2,1,0:T(2,128)S(1)}, f32[7,4,2,1152]{3,2,1,0:T(2,128)S(1)}, u32[]{:S(2)}, u32[]{:S(2)}) collective-permute-start(f32[7,4,2,1152]{3,2,1,0:T(2,128)S(1)} %get-tuple-element.71), channel_id=1, source_target_pairs={{4,0},{8,4},{12,8},{5,1},{9,5},{13,9},{6,2},{10,6},{14,10},{7,3},{... | collective-permute-start | bytes 774152 | tf_op jit(solution)/shard_map/ppermute | solution.py:15
  8.8 12.0 %fusion.6 = (f32[1152,640]{1,0:T(8,128)S(1)}, f32[1152,640]{1,0:T(8,128)S(1)}) fusion(), kind=kLoop, calls=%fused_computation.13 | loop fusion | flops 6635520 | bytes 5898240 | tf_op jit(solution)/shard_map/sin | solution.py:66
  24.5 1.9 %fusion.10 = f32[8,16,1280]{2,1,0:T(8,128)S(1)} fusion(f32[1152,640]{1,0:T(8,128)S(1)} %get-tuple-element.81, f32[1152,640]{1,0:T(8,128)S(1)} %get-tuple-element.82, f32[4,16,1152]{2,1,0:T(8,128)S(1)} %get-tuple-element.75, f32[4,16,1152]{2,1,0:T(8,128)S(1)} %get-tuple-element.74, f32[16,1280]{1,0:T(8,128)S(1)} %pad_maximum_fusion.19), kind=kOutput, calls=%fused_computation.17 | convolution fusion | flops 1134247936 | bytes 7225344 | tf_op jit(solution)/shard_map/arm,mk->ark/dot_general | solution.py:73
  26.4 2.8 %fusion.9 = f32[8,16,1152]{2,1,0:T(8,128)S(1)} fusion(f32[8,16,1280]{2,1,0:T(8,128)S(1)} %fusion.10, f32[1152,640]{1,0:T(8,128)S(1)} %get-tuple-element.81, f32[1152,640]{1,0:T(8,128)S(1)} %get-tuple-element.82), kind=kOutput, calls=%fused_computation.16 | convolution fusion | flops 1134084096 | bytes 7143424 | tf_op jit(solution)/shard_map/ark,mk->arm/dot_general | solution.py:74
  29.2 1.1 fusion.16
  30.4 2.1 %copy.42 = f32[7,4,16,1152]{3,1,0,2:T(4,128)} copy(f32[7,4,16,1152]{3,2,1,0:T(8,128)S(1)} %pad_maximum_fusion) | data formatting | bytes 4128768 | tf_op jit(solution)/shard_map/concatenate | solution.py:130
  32.5 4.0 %all-to-all-start = ((f32[7,4,16,1152]{3,1,0,2:T(4,128)}), f32[7,4,16,1152]{3,1,0,2:T(4,128)S(1)}, u32[]{:S(2)}, u32[]{:S(2)}) async-start(f32[7,4,16,1152]{3,1,0,2:T(4,128)} %copy.42), calls=%async_computation | async-start | bytes 4128768 | tf_op jit(solution)/shard_map/all_to_all | solution.py:136
  38.8 22.8 %all-to-all-done = f32[7,4,16,1152]{3,1,0,2:T(4,128)S(1)} async-done(((f32[7,4,16,1152]{3,1,0,2:T(4,128)}), f32[7,4,16,1152]{3,1,0,2:T(4,128)S(1)}, u32[]{:S(2)}, u32[]{:S(2)}) %all-to-all-start) | async-done | bytes 2064416 | tf_op jit(solution)/shard_map/all_to_all | solution.py:136
  65.3 1.5 %broadcast_multiply_fusion = f32[16,4608]{1,0:T(8,128)} fusion(f32[16]{0:T(128)S(1)} %broadcast_divide_fusion, f32[4608]{0:T(1024)} %mul.234), kind=kLoop, calls=%fused_computation.78 | loop fusion | flops 73728 | bytes 313408 | tf_op jit(solution)/shard_map/mul | solution.py:96
  66.8 0.8 broadcast_multiply_fusion.1
  67.7 1.1 slice.189
  68.8 1.0 copy.56
  70.1 9.0 %while.10 = (s32[]{:T(128)}, f32[4,6,4,4608]{3,2,1,0:T(4,128)}, f32[6,16,4608]{2,1,0:T(8,128)S(1)}, f32[4,4,4608]{2,1,0:T(4,128)S(1)}, f32[16,4608]{1,0:T(8,128)S(1)}, /*index=5*/f32[1,16,4608]{2,1,0:T(8,128)S(1)}, s32[]{:T(128)}) while((s32[]{:T(128)}, f32[4,6,4,4608]{3,2,1,0:T(4,128)}, f32[6,16,4608]{2,1,0:T(8,128)S(1)}, ...), condition=%wide.region_6.7_spmd, body=%wide.region_4.6_spmd.sunk | while | flops 4313090 | bytes 6266973 | solution.py:91
  70.2 1.3 %multiply_reduce_fusion.2 = f32[6,4,4608]{2,1,0:T(4,128)S(1)} fusion(f32[4,16,4608]{2,1,0:T(8,128)S(1)} %maximum_minimum_fusion.2, f32[6,16,4608]{2,1,0:T(8,128)S(1)} %get-tuple-element.136), kind=kLoop, calls=%fused_computation.clone.1 | loop fusion | flops 3428352 | bytes 3391488 | tf_op jit(solution)/shard_map/while/body/eval_jaxpr/reduce_sum | solution.py:89
  72.5 1.3 %multiply_reduce_fusion.2 = f32[6,4,4608]{2,1,0:T(4,128)S(1)} fusion(f32[4,16,4608]{2,1,0:T(8,128)S(1)} %maximum_minimum_fusion.2, f32[6,16,4608]{2,1,0:T(8,128)S(1)} %get-tuple-element.136), kind=kLoop, calls=%fused_computation.clone.1 | loop fusion | flops 3428352 | bytes 3391488 | tf_op jit(solution)/shard_map/while/body/eval_jaxpr/reduce_sum | solution.py:89
  74.7 1.3 %multiply_reduce_fusion.2 = f32[6,4,4608]{2,1,0:T(4,128)S(1)} fusion(f32[4,16,4608]{2,1,0:T(8,128)S(1)} %maximum_minimum_fusion.2, f32[6,16,4608]{2,1,0:T(8,128)S(1)} %get-tuple-element.136), kind=kLoop, calls=%fused_computation.clone.1 | loop fusion | flops 3428352 | bytes 3391488 | tf_op jit(solution)/shard_map/while/body/eval_jaxpr/reduce_sum | solution.py:89
  77.0 1.3 %multiply_reduce_fusion.2 = f32[6,4,4608]{2,1,0:T(4,128)S(1)} fusion(f32[4,16,4608]{2,1,0:T(8,128)S(1)} %maximum_minimum_fusion.2, f32[6,16,4608]{2,1,0:T(8,128)S(1)} %get-tuple-element.136), kind=kLoop, calls=%fused_computation.clone.1 | loop fusion | flops 3428352 | bytes 3391488 | tf_op jit(solution)/shard_map/while/body/eval_jaxpr/reduce_sum | solution.py:89
  79.1 1.6 %copy.45 = f32[6,4,4,4608]{3,2,1,0:T(4,128)S(1)} copy(f32[6,4,4,4608]{3,2,0,1:T(4,128)} %bitcast.86) | data formatting | bytes 3538944 | tf_op jit(solution)/shard_map/transpose | solution.py:92
  81.3 1.3 %subtract_divide_fusion = f32[6,16,4608]{2,1,0:T(8,128)S(1)} fusion(f32[6,16,4608]{2,1,0:T(8,128)S(1)} %reshape.157, f32[6,15,4608]{2,1,0:T(8,128)S(1)} %bitcast.57, f32[16,4608]{1,0:T(8,128)} %broadcast_multiply_fusion), kind=kLoop, calls=%fused_computation.21 | loop fusion | flops 884736 | bytes 5492736 | tf_op jit(solution)/shard_map/div | solution.py:98
  83.3 1.4 %pad_maximum_fusion.1 = f32[7,16,4,1152]{3,2,0,1:T(4,128)S(1)} fusion(f32[1,16,4,1152]{3,2,0,1:T(4,128)} %broadcast_multiply_fusion.2, f32[6,16,4,1152]{3,2,1,0:T(4,128)S(1)} %concatenate.68), kind=kLoop, calls=%fused_computation.19 | loop fusion | flops 516096 | bytes 4128768 | tf_op jit(solution)/shard_map/concatenate | solution.py:97
  84.7 27.8 %all_to_all.30 = f32[7,16,4,1152]{3,2,0,1:T(4,128)S(1)} all-to-all(f32[7,16,4,1152]{3,2,0,1:T(4,128)S(1)} %pad_maximum_fusion.1), channel_id=1, replica_groups=mesh['member'=2,'lat'=4,'lev'=2,'sub'=2] {'lev','sub'}, dimensions={1} | all-to-all | bytes 4128768 | tf_op jit(solution)/shard_map/all_to_all | solution.py:139
  115.7 1.1 copy.55
  (87 shorter events, 18.2 us)
Async XLA Ops:
  0.6 8.0 %copy-start.2 = (f32[4,16,1152]{2,1,0:T(8,128)S(1)}, f32[4,16,1152]{2,1,0:T(8,128)}, u32[]{:S(2)}) copy-start(f32[4,16,1152]{2,1,0:T(8,128)} %param.9) | copy-start | bytes 884740
  2.4 19.1 %collective-permute-start = (f32[7,4,2,1152]{3,2,1,0:T(2,128)S(1)}, f32[7,4,2,1152]{3,2,1,0:T(2,128)S(1)}, u32[]{:S(2)}, u32[]{:S(2)}) collective-permute-start(f32[7,4,2,1152]{3,2,1,0:T(2,128)S(1)} %get-tuple-element.72), channel_id=1, source_target_pairs={{0,4},{4,8},{8,12},{1,5},{5,9},{9,13},{2,6},{6,10},{10,14},{3,7},{... | collective-permute-start | bytes 774152 | tf_op jit(solution)/shard_map/ppermute | solution.py:14
  7.3 14.1 %collective-permute-start.1 = (f32[7,4,2,1152]{3,2,1,0:T(2,128)S(1)}, f32[7,4,2,1152]{3,2,1,0:T(2,128)S(1)}, u32[]{:S(2)}, u32[]{:S(2)}) collective-permute-start(f32[7,4,2,1152]{3,2,1,0:T(2,128)S(1)} %get-tuple-element.71), channel_id=1, source_target_pairs={{4,0},{8,4},{12,8},{5,1},{9,5},{13,9},{6,2},{10,6},{14,10},{7,3},{... | collective-permute-start | bytes 774152 | tf_op jit(solution)/shard_map/ppermute | solution.py:15
  8.8 12.1 %copy-start.5 = (pred[640]{0:T(1024)(128)(4,1)S(1)}, pred[640]{0:T(1024)(128)(4,1)}, u32[]{:S(2)}) copy-start(pred[640]{0:T(1024)(128)(4,1)} %constant.44.clone.1) | copy-start | bytes 1924
  8.8 12.1 %copy-start.6 = (s32[16]{0:T(128)S(1)}, s32[16]{0:T(128)}, u32[]{:S(2)}) copy-start(s32[16]{0:T(128)} %param.13) | copy-start | bytes 196
  8.8 12.2 %copy-start = (f32[4,4,16,1152]{3,2,1,0:T(8,128)S(1)}, f32[4,4,16,1152]{3,2,1,0:T(8,128)}, u32[]{:S(2)}) copy-start(f32[4,4,16,1152]{3,2,1,0:T(8,128)} %param.11) | copy-start | bytes 3538948
  20.9 1.0 copy-start.3
  20.9 1.0 copy-start.4
  22.5 1.3 %copy-start.1 = (f32[4,4,16,1152]{3,2,1,0:T(8,128)S(1)}, f32[4,4,16,1152]{3,2,1,0:T(8,128)}, u32[]{:S(2)}) copy-start(f32[4,4,16,1152]{3,2,1,0:T(8,128)} %param.11) | copy-start | bytes 3538948
  22.5 1.3 %slice-start = ((f32[4,4,16,1152]{3,2,1,0:T(8,128)}), f32[4,4,16,1]{3,2,1,0:T(8,128)S(1)}, s32[]{:S(2)}) async-start(f32[4,4,16,1152]{3,2,1,0:T(8,128)} %param.11), calls=%async_computation.2 | async-start | bytes 262144 | tf_op jit(solution)/shard_map/jit(_roll_static)/slice | solution.py:51
  32.5 4.0 %copy-start.7 = (f32[16]{0:T(128)S(1)}, f32[16]{0:T(128)}, u32[]{:S(2)}) copy-start(f32[16]{0:T(128)} %param.12) | copy-start | bytes 196
  32.5 29.1 %all-to-all-start = ((f32[7,4,16,1152]{3,1,0,2:T(4,128)}), f32[7,4,16,1152]{3,1,0,2:T(4,128)S(1)}, u32[]{:S(2)}, u32[]{:S(2)}) async-start(f32[7,4,16,1152]{3,1,0,2:T(4,128)} %copy.42), calls=%async_computation | async-start | bytes 4128768 | tf_op jit(solution)/shard_map/all_to_all | solution.py:136
where the time goes:
time: 117 us
  other arithmetic  31 us (26%)
  blocking collectives  27.8 us (24%)
  waiting for transfers between devices  22.8 us (19%)
  local copies, waits for them, and re-layouts  19.1 us (16%)
  starting transfers between devices  10.2 us (9%)
  matrix products  4.68 us (4%)
    all_to_all x1, blocking collectives, per_device(): lax.all_to_all(remapped, ('lev', 'sub'), split_axis=1, concat_axis=2, til...  27.8 us
    all_to_all x1, waiting for transfers between devices, per_device(): lax.all_to_all(stacked, ('lev', 'sub'), split_axis=2, concat_axis=1, tile...  22.8 us
    sin x1, other arithmetic, spectral_filter(): table = jnp.concatenate([jnp.cos(angles), jnp.sin(angles)], axis=1)  12 us
    unnamed x21, local copies, waits for them, and re-layouts  5.58 us
    reduce_sum x4, other arithmetic, integrate(): return jnp.sum(fields[:, None] * w[None], axis=2)  5.24 us
    ppermute x1, starting transfers between devices, extended_2(): before = lax.ppermute(last, axis, up)  4.94 us
    all_to_all x1, starting transfers between devices, per_device(): lax.all_to_all(stacked, ('lev', 'sub'), split_axis=2, concat_axis=1, tile...  3.96 us
    dynamic_update_slice x4, local copies, waits for them, and re-layouts, remap(): lax.map(integrate, targets.reshape(levels // 4, 4, targets.shape[1]))  3.2 us
  transfers between devices with their start and end apart: 3, of which 1 were waited for; matrix products, arithmetic and copies ran while one was open for 13% of the time, Pallas kernels for 0%

commit v1 on v0

v1 whole, which is shorter than its diff:
```python
import functools

import jax
import jax.numpy as jnp
import ml_dtypes
import numpy as np
from jax import lax
from jax.experimental import pallas as pl
from jax.experimental.pallas import tpu as pltpu
from jax.sharding import PartitionSpec as P

LANES = 128
VMEM = pl.BlockSpec(memory_space=pltpu.VMEM)
SMEM = pl.BlockSpec(memory_space=pltpu.SMEM)


def params():
    return pltpu.CompilerParams(vmem_limit_bytes=48 * 1024 * 1024)


def cost(flops, bytes_accessed):
    return pl.CostEstimate(flops=int(flops), bytes_accessed=int(bytes_accessed), transcendentals=0)


def geometry_table(lat_rows, band_rows):
    bands = lat_rows // band_rows
    table = np.zeros((bands, band_rows + 8, LANES), np.float32)
    for band in range(bands):
        for j in range(band_rows + 1):
            row = band * band_rows + j
            south = np.sin(row * np.pi / lat_rows) if 0 < row < lat_rows else 0.0
            north = np.sin((row + 1) * np.pi / lat_rows) if row + 1 < lat_rows else 0.0
            table[band, j, 0] = south
            table[band, j, 1] = north
            table[band, j, 2] = 1.0 / np.sin((row + 0.5) * np.pi / lat_rows)
    return table


def east_of(value):
    return pltpu.roll(value, value.shape[1] - 1, 1)


def west_of(value):
    return pltpu.roll(value, 1, 1)


def row_ids(shape):
    return lax.broadcasted_iota(jnp.int32, shape, 0)


def north_of(value, beyond):
    rows = value.shape[0]
    return jnp.where(row_ids(value.shape) == rows - 1, beyond, pltpu.roll(value, rows - 1, 0))


def south_of(value, beyond):
    return jnp.where(row_ids(value.shape) == 0, beyond, pltpu.roll(value, 1, 0))


def fluxes(geo_ref, thick, u, v, thick_s, v_s, thick_n):
    rows = thick.shape[0]
    east = u * jnp.where(u > 0, thick, east_of(thick))
    north = v * jnp.where(v > 0, thick, north_of(thick, thick_n)) * geo_ref[0:rows, 1:2]
    below = v_s * jnp.where(v_s > 0, thick_s, thick[0:1]) * geo_ref[0:1, 0:1]
    return east, north, below


def thickness_kernel(lat_rows, geo_ref, first_ref, thick_ref, u_ref, v_ref, up_ref, down_ref, new_ref, wind_ref, sum_ref):
    rows = thick_ref.shape[1]
    thick, u, v = thick_ref[0], u_ref[0], v_ref[0]
    thick_s, v_s = up_ref[0, 0], up_ref[1, 0]
    thick_n, thick_nn, u_n, v_n = (down_ref[i, 0] for i in range(4))
    east, north, below = fluxes(geo_ref, thick, u, v, thick_s, v_s, thick_n)
    inverse = geo_ref[0:rows, 2:3]
    new = thick - (east - west_of(east)) - (north - south_of(north, below)) * inverse
    east_n = u_n * jnp.where(u_n > 0, thick_n, east_of(thick_n))
    north_n = v_n * jnp.where(v_n > 0, thick_n, thick_nn) * geo_ref[rows : rows + 1, 1:2]
    new_n = (
        thick_n
        - (east_n - west_of(east_n))
        - (north_n - north[rows - 1 : rows]) * geo_ref[rows : rows + 1, 2:3]
    )
    new_ref[0] = new
    wind_ref[0, 0] = u - 0.05 * (east_of(new) - new)
    inside = first_ref[0] + row_ids(new.shape) < lat_rows - 1
    wind_ref[1, 0] = jnp.where(inside, v - 0.05 * (north_of(new, new_n) - new), 0.0)

    @pl.when(pl.program_id(0) == 0)
    def _():
        sum_ref[...] = new

    @pl.when(pl.program_id(0) > 0)
    def _():
        sum_ref[...] += new


def thickness_step(geo, first, lat_rows, thickness, wind_u, wind_v, up, down):
    L, R, N = thickness.shape
    level = pl.BlockSpec((1, R, N), lambda k: (k, 0, 0))
    unit = 4 * R * N
    return pl.pallas_call(
        functools.partial(thickness_kernel, lat_rows),
        grid=(L,),
        in_specs=[
            pl.BlockSpec(geo.shape, lambda k: (0, 0)),
            SMEM,
            level,
            level,
            level,
            pl.BlockSpec((2, 1, 1, N), lambda k: (0, k, 0, 0)),
            pl.BlockSpec((4, 1, 1, N), lambda k: (0, k, 0, 0)),
        ],
        out_specs=[
            level,
            pl.BlockSpec((2, 1, R, N), lambda k: (0, k, 0, 0)),
            pl.BlockSpec((R, N), lambda k: (0, 0)),
        ],
        out_shape=[
            jax.ShapeDtypeStruct((L, R, N), jnp.float32),
            jax.ShapeDtypeStruct((2, L, R, N), jnp.float32),
            jax.ShapeDtypeStruct((R, N), jnp.float32),
        ],
        compiler_params=params(),
        cost_estimate=cost(40 * L * R * N, 7 * L * unit),
        name="thickness_step",
    )(geo, first, thickness, wind_u, wind_v, up, down)


def tracer_kernel(geo_ref, thick_ref, u_ref, v_ref, new_ref, up_ref, down_ref, tracer_ref, up_t_ref, down_t_ref, *out_refs):
    rows = thick_ref.shape[1]
    thick, u, v = thick_ref[0], u_ref[0], v_ref[0]
    east, north, below = fluxes(geo_ref, thick, u, v, up_ref[0, 0], up_ref[1, 0], down_ref[0, 0])
    v_s = up_ref[1, 0]
    inverse = geo_ref[0:rows, 2:3]
    scale = 1.0 / new_ref[0]
    per_out = out_refs[0].shape[0]
    for c in range(tracer_ref.shape[0]):
        q = tracer_ref[c, 0]
        t_east = east * jnp.where(u > 0, q, east_of(q))
        t_north = north * jnp.where(v > 0, q, north_of(q, down_t_ref[c, 0]))
        t_below = below * jnp.where(v_s > 0, up_t_ref[c, 0], q[0:1])
        change = thick * q - (t_east - west_of(t_east))
        change = change - (t_north - south_of(t_north, t_below)) * inverse
        out_refs[c // per_out][c % per_out, 0] = change * scale


def tracer_step(geo, thickness, wind_u, wind_v, thick_new, up, down, tracers, up_t, down_t, parts):
    L, R, N = thickness.shape
    T = tracers.shape[0]
    level = pl.BlockSpec((1, R, N), lambda k: (k, 0, 0))
    edge = lambda n: pl.BlockSpec((n, 1, 1, N), lambda k: (0, k, 0, 0))
    unit = 4 * R * N
    return pl.pallas_call(
        tracer_kernel,
        grid=(L,),
        in_specs=[
            pl.BlockSpec(geo.shape, lambda k: (0, 0)),
            level,
            level,
            level,
            level,
            edge(2),
            edge(1),
            pl.BlockSpec((T, 1, R, N), lambda k: (0, k, 0, 0)),
            edge(T),
            edge(T),
        ],
        out_specs=[pl.BlockSpec((T // parts, 1, R, N), lambda k: (0, k, 0, 0))] * parts,
        out_shape=[jax.ShapeDtypeStruct((T // parts, L, R, N), jnp.float32)] * parts,
        compiler_params=params(),
        cost_estimate=cost(90 * L * R * N, (2 * T + 4) * L * unit),
        name="tracer_step",
    )(geo, thickness, wind_u, wind_v, thick_new, up, down, tracers, up_t, down_t)


def filter_tables(N):
    A = N // LANES
    b = np.arange(LANES)[:, None]
    p = np.arange(LANES)[None, :]
    tables = []
    for q in range(A // 2 + 1):
        angle = 2.0 * np.pi * ((b * (A * p + q)) % N) / N
        c, s = np.cos(angle), np.sin(angle)
        tables.append(np.block([[c, -s], [s, c]]))
    table = np.stack(tables)
    high = table.astype(np.float32).astype(ml_dtypes.bfloat16)
    low = (table - high.astype(np.float64)).astype(np.float32).astype(ml_dtypes.bfloat16)
    return high, low


def split(value):
    high = value.astype(jnp.bfloat16)
    return high, (value - high.astype(jnp.float32)).astype(jnp.bfloat16)


def product(value, high, low, transposed):
    dims = (((1,), (1 if transposed else 0,)), ((), ()))
    dot = lambda x, y: lax.dot_general(x, y, dims, preferred_element_type=jnp.float32)
    v_high, v_low = split(value)
    return dot(v_high, high) + (dot(v_high, low) + dot(v_low, high))


def filter_kernel(N, wind_ref, cutoff_ref, high_ref, low_ref, out_ref):
    A = N // LANES
    half = A // 2
    F, L, R, _ = wind_ref.shape
    rows = F * L * R
    piece = lambda a: wind_ref[:, :, :, a * LANES : (a + 1) * LANES].reshape(rows, LANES)
    x = [piece(a) for a in range(A)]
    even = [x[a] + x[A - a] for a in range(1, half + 1)]
    odd = [x[a] - x[A - a] for a in range(1, half + 1)]
    angle = lambda q, a: 2.0 * np.pi * ((q * a) % A) / A
    cutoff = cutoff_ref[...]
    p = lax.broadcasted_iota(jnp.int32, (R, LANES), 1)
    real, imag = [], []
    for q in range(half + 1):
        re = x[0]
        for a in range(1, half + 1):
            re = re + (even[a - 1] if q == 0 else float(np.cos(angle(q, a))) * even[a - 1])
        if q == 0:
            spectrum = product(re, high_ref[0, 0:LANES], low_ref[0, 0:LANES], False)
        else:
            im = -float(np.sin(angle(q, 1))) * odd[0]
            for a in range(2, half + 1):
                im = im - float(np.sin(angle(q, a))) * odd[a - 1]
            spectrum = product(jnp.concatenate([re, im], axis=1), high_ref[q], low_ref[q], False)
        mode = A * p + q
        factor = 1.0 / N if q == 0 else 2.0 / N
        kept = jnp.where(jnp.minimum(mode, N - mode) <= cutoff, factor, 0.0)
        kept = jnp.concatenate([kept, kept], axis=1)
        spectrum = (spectrum.reshape(F * L, R, 2 * LANES) * kept[None]).reshape(rows, 2 * LANES)
        if q == 0:
            real.append(product(spectrum, high_ref[0, 0:LANES], low_ref[0, 0:LANES], True))
            imag.append(None)
        else:
            back = product(spectrum, high_ref[q], low_ref[q], True)
            real.append(back[:, :LANES])
            imag.append(back[:, LANES:])

    def store(a, value):
        out_ref[:, :, :, a * LANES : (a + 1) * LANES] = value.reshape(F, L, R, LANES)

    first = real[0]
    for q in range(1, half + 1):
        first = first + real[q]
    store(0, first)
    for a in range(1, half + 1):
        even_part = real[0]
        odd_part = None
        for q in range(1, half + 1):
            even_part = even_part + float(np.cos(angle(q, a))) * real[q]
            term = float(np.sin(angle(q, a))) * imag[q]
            odd_part = term if odd_part is None else odd_part + term
        store(a, even_part - odd_part)
        store(A - a, even_part + odd_part)


def fourier_filter(wind, cutoff):
    F, L, R, N = wind.shape
    high, low = filter_tables(N)
    macs = F * L * R * high.size
    return pl.pallas_call(
        functools.partial(filter_kernel, N),
        in_specs=[VMEM] * 4,
        out_specs=VMEM,
        out_shape=jax.ShapeDtypeStruct(wind.shape, jnp.float32),
        compiler_params=params(),
        cost_estimate=cost(2 * 6 * macs, 8 * F * L * R * N + 4 * high.size),
        name="fourier_filter",
    )(wind, jnp.broadcast_to(cutoff[:, None], (R, LANES)), jnp.asarray(high), jnp.asarray(low))


def remap_kernel(lev_count, sub_count, with_thickness, place_ref, cum_ref, frac_ref, inv_ref, *refs):
    S, C = sub_count, lev_count
    thick_refs, refs = refs[:S], refs[S:]
    field_refs, refs = refs[:S], refs[S:]
    other_refs, refs = refs[: (C - 1) * S], refs[(C - 1) * S :]
    out_refs = refs[:C]
    F, L, R, N = field_refs[0].shape
    lev, sub = place_ref[0], place_ref[1]
    spot = [lax.rem(sub + S - t, S) for t in range(S)]

    def tile(rows, columns):
        thick = [[thick_refs[t][m, rows, columns] for m in range(L)] for t in range(S)]
        group = [functools.reduce(jnp.add, levels) for levels in thick]
        mass = functools.reduce(jnp.add, group)
        base = jnp.zeros_like(mass)
        for s in range(1, C):
            other = other_refs[(s - 1) * S][rows, columns]
            for t in range(1, S):
                other = other + other_refs[(s - 1) * S + t][rows, columns]
            mass = mass + other
            base = base + jnp.where(lev >= s, other, 0.0)
        sources = []
        for t in range(S):
            low = base
            for other in range(S):
                if other != t:
                    low = low + jnp.where(spot[other] < spot[t], group[other], 0.0)
            for m in range(L):
                sources.append((t, m, low, thick[t][m]))
                low = low + thick[t][m]
        inverse = 1.0 / mass
        for s in range(C):
            first = (lax.rem(lev + s, C) * S + sub) * L

            def covered(i):
                top = mass * cum_ref[first + i]
                return [jnp.minimum(jnp.maximum(top - low, 0.0), h) for _, _, low, h in sources]

            below = covered(0)
            for i in range(L):
                upto = covered(i + 1)
                part = [a - b for a, b in zip(upto, below)]
                below = upto
                scale = inverse * inv_ref[first + i]
                for f in range(F):
                    total = None
                    for (t, m, _, _), w in zip(sources, part):
                        term = field_refs[t][f, m, rows, columns] * w
                        total = term if total is None else total + term
                    out_refs[s][f, i, rows, columns] = total * scale
                if with_thickness and s == 0:
                    refs[C][i, rows, columns] = mass * frac_ref[first + i]

    for r in range(0, R, 8):

        def body(c, carry):
            tile(slice(r, r + 8), pl.ds(pl.multiple_of(c * LANES, LANES), LANES))
            return carry

        lax.fori_loop(0, N // LANES, body, 0)


def remap_parts(counts, place, cum, frac, inv, thick, fields, others, with_thickness):
    C, S = counts
    F, L, R, N = fields[0].shape
    shape = jax.ShapeDtypeStruct((F, L, R, N), jnp.float32)
    out_shape = [shape] * C
    if with_thickness:
        out_shape = out_shape + [jax.ShapeDtypeStruct((L, R, N), jnp.float32)]
    return pl.pallas_call(
        functools.partial(remap_kernel, C, S, with_thickness),
        in_specs=[SMEM] * 4 + [VMEM] * (2 * S + len(others)),
        out_specs=[VMEM] * len(out_shape),
        out_shape=out_shape,
        compiler_params=params(),
        cost_estimate=cost(C * S * L * L * R * N * (5 + 2 * F), 4 * R * N * L * (F + 1) * (S + C)),
        name="remap_parts",
    )(place, cum, frac, inv, *thick, *fields, *others)


def add_kernel(groups, *refs):
    outs = refs[-1]
    at = 0
    each = len(refs[:-1]) // groups
    for g in range(groups):
        total = refs[g * each][...]
        for i in range(1, each):
            total = total + refs[g * each + i][...]
        n = total.shape[0]
        outs[at : at + n] = total
        at += n


def add_parts(groups):
    flat = [a for group in groups for a in group]
    total = sum(group[0].shape[0] for group in groups)
    L, R, N = flat[0].shape[1:]
    return pl.pallas_call(
        functools.partial(add_kernel, len(groups)),
        in_specs=[VMEM] * len(flat),
        out_specs=VMEM,
        out_shape=jax.ShapeDtypeStruct((total, L, R, N), jnp.float32),
        compiler_params=params(),
        cost_estimate=cost(total * L * R * N, 4 * total * L * R * N * 3),
        name="add_parts",
    )(*flat)


def shifted(value, lev_count, sub_count, s, t):
    if t == 0:
        return lax.ppermute(value, "lev", [(i, (i + s) % lev_count) for i in range(lev_count)])
    if s == 0:
        return lax.ppermute(value, "sub", [(i, (i + t) % sub_count) for i in range(sub_count)])
    pairs = [
        (i * sub_count + j, (i + s) % lev_count * sub_count + (j + t) % sub_count)
        for i in range(lev_count)
        for j in range(sub_count)
    ]
    return lax.ppermute(value, ("lev", "sub"), pairs)


def per_device(thickness, wind_u, wind_v, tracers, level_weights, cutoff):
    L, R, N = thickness.shape
    lat_count = lax.axis_size("lat")
    C, S = lax.axis_size("lev"), lax.axis_size("sub")
    lat_rows = R * lat_count
    send = functools.partial(shifted, lev_count=C, sub_count=S)

    last = jnp.concatenate([thickness[None, :, R - 1 :], wind_v[None, :, R - 1 :], tracers[:, :, R - 1 :]], axis=0)
    leading = jnp.concatenate(
        [
            thickness[None, :, 0:1],
            thickness[None, :, 1:2],
            wind_u[None, :, 0:1],
            wind_v[None, :, 0:1],
            tracers[:, :, 0:1],
        ],
        axis=0,
    )
    northward = [(i, i + 1) for i in range(lat_count - 1)]
    up = lax.ppermute(last, "lat", northward)
    down = lax.ppermute(leading, "lat", [(j, i) for i, j in northward])

    band = lax.axis_index("lat")
    geo = lax.dynamic_index_in_dim(jnp.asarray(geometry_table(lat_rows, R)), band, 0, keepdims=False)
    first = (band * R).astype(jnp.int32).reshape(1)
    place = jnp.stack([lax.axis_index("lev"), lax.axis_index("sub")]).astype(jnp.int32)
    levels = level_weights.shape[0]
    fraction = level_weights / jnp.sum(level_weights)
    lower = np.tril(np.ones((levels + 1, levels), np.float32), -1)
    cum = jnp.sum(jnp.asarray(lower) * fraction[None, :], axis=1)
    inv = 1.0 / fraction

    up_h, up_t = up[:2], up[2:]
    down_h, down_t = down[:4], down[4:]
    thick_new, wind, own_sum = thickness_step(geo, first, lat_rows, thickness, wind_u, wind_v, up_h, down_h)
    others = [send(own_sum, s=s, t=t) for s in range(1, C) for t in range(S)]
    thick = [thick_new] + [send(thick_new, s=0, t=t) for t in range(1, S)]
    parts = 2
    tracer_new = tracer_step(
        geo, thickness, wind_u, wind_v, thick_new, up_h, down_h, tracers, up_t, down_t, parts
    )
    filtered = fourier_filter(wind, cutoff)
    results = []
    thickness_out = None
    for index, own in enumerate(list(tracer_new) + [filtered]):
        fields = [own] + [send(own, s=0, t=t) for t in range(1, S)]
        with_thickness = index == 1
        out = remap_parts((C, S), place, cum, fraction, inv, thick, fields, others, with_thickness)
        if with_thickness:
            thickness_out = out[C]
        results.append([out[0]] + [send(out[s], s=s, t=0) for s in range(1, C)])
    tracers_out = add_parts(results[:parts])
    winds = functools.reduce(jnp.add, results[parts])
    return thickness_out, winds[0], winds[1], tracers_out


def solution(mesh):
    placed = (
        P(("member", "lev", "sub"), "lat", None),
        P(("member", "lev", "sub"), "lat", None),
        P(("member", "lev", "sub"), "lat", None),
        P("member", ("lev", "sub"), "lat", None),
        P(),
        P("lat"),
    )
    return jax.shard_map(
        per_device,
        mesh=mesh,
        in_specs=placed,
        out_specs=(
            P(("member", "lev", "sub"), "lat", None),
            P(("member", "lev", "sub"), "lat", None),
            P(("member", "lev", "sub"), "lat", None),
            P("member", ("lev", "sub"), "lat", None),
        ),
        check_vma=False,
    )
```

time: 117 us -> 75.1 us (0.64)
  other arithmetic: 31 us -> 1.57 us
  blocking collectives: 27.8 us -> 0 us
  Pallas kernels: 0 us -> 13.6 us
  waiting for transfers between devices: 22.8 us -> 34.3 us
  local copies, waits for them, and re-layouts: 19.1 us -> 11.4 us
  matrix products: 4.68 us -> 0 us
  starting transfers between devices: 10.2 us -> 13 us
    ppermute x2 -> x11, waiting for transfers between devices: 0.01 us -> 34.3 us  [the longest x4 32.8 us: shifted(): lax.ppermute(value, 'lev', [(i, (i + s) % lev_count) for i in range(lev_c...]
    all_to_all x1 -> x0, blocking collectives: 27.8 us -> none  [per_device(): lax.all_to_all(remapped, ('lev', 'sub'), split_axis=1, concat_axis=2, til...]
    all_to_all x1 -> x0, waiting for transfers between devices: 22.8 us -> none  [per_device(): lax.all_to_all(stacked, ('lev', 'sub'), split_axis=2, concat_axis=1, tile...]
    pallas_call x0 -> x7, Pallas kernels: none -> 13.6 us  [the longest x3 8.2 us: remap_parts(): pl.pallas_call(functools.partial(remap_kernel, C, S, with_thickness), in_...]
    sin x2 -> x0, other arithmetic: 12.1 us -> none  [the longest x1 12 us: spectral_filter(): table = jnp.concatenate([jnp.cos(angles), jnp.sin(angles)], axis=1)]
    ppermute x2 -> x11, starting transfers between devices: 6.24 us -> 13 us  [the longest x1 5.56 us: per_device(): up = lax.ppermute(last, 'lat', northward)]
    reduce_sum x5 -> x2, other arithmetic: 5.84 us -> 0.69 us  [the longest x1 0.6 us: per_device(): fraction = level_weights / jnp.sum(level_weights)]
    dot_general x2 -> x0, matrix products: 4.68 us -> none  [the longest x1 2.79 us: spectral_filter(): jnp.einsum('ark,mk->arm', spectrum, table, precision=lax.Precision.HIGH)]
  transfers between devices with their start and end apart: 3 -> 11, of which waited for: 1 -> 5; matrix products, arithmetic and copies ran while one was open for 13% -> 8% of each run, Pallas kernels for 0% -> 14%
where the time goes in v1:
time: 75.1 us; the launch traced here: 74.7 us
  waiting for transfers between devices  34.3 us (46%)
  Pallas kernels  13.6 us (18%)
  starting transfers between devices  13 us (17%)
  local copies, waits for them, and re-layouts  11.4 us (15%)
  other arithmetic  1.57 us (2%)
  between operations  0.81 us (1%)
    ppermute x4, waiting for transfers between devices, shifted(): lax.ppermute(value, 'lev', [(i, (i + s) % lev_count) for i in range(lev_c...  32.8 us
    pallas_call x3, Pallas kernels, remap_parts(): pl.pallas_call(functools.partial(remap_kernel, C, S, with_thickness), in_...  8.2 us
    ppermute x1, starting transfers between devices, per_device(): up = lax.ppermute(last, 'lat', northward)  5.56 us
    unnamed x24, local copies, waits for them, and re-layouts  5.52 us
    ppermute x4, starting transfers between devices, shifted(): lax.ppermute(value, 'lev', [(i, (i + s) % lev_count) for i in range(lev_c...  3.42 us
    pallas_call x1, Pallas kernels, tracer_step(): pl.pallas_call(tracer_kernel, grid=(L,), in_specs=[pl.BlockSpec(geo.shape...  1.89 us
    ppermute x1, starting transfers between devices, shifted(): return lax.ppermute(value, ('lev', 'sub'), pairs)  1.62 us
    ppermute x1, waiting for transfers between devices, per_device(): up = lax.ppermute(last, 'lat', northward)  1.51 us
  transfers between devices with their start and end apart: 11, of which 5 were waited for; matrix products, arithmetic and copies ran while one was open for 8% of the time, Pallas kernels for 14%

profile of v1, /device:TPU:0, one launch (start us, length us, event | category | flops | bytes accessed | tf_op | source)
XLA Modules:
  0.0 74.7 jit_solution(9794341622649760564)
XLA Ops:
  0.7 1.0 %bitcast_dynamic-update-slice_fusion.3 = f32[8,4,1,1152]{3,2,1,0:T(1,128)S(1)} fusion(f32[4,16,1152]{2,1,0:T(8,128)} %thick_ref.3), kind=kLoop, calls=%fused_computation.7 | loop fusion | bytes 36864
  1.7 0.9 %bitcast_dynamic-update-slice_fusion.2 = f32[8,4,1,1152]{3,2,1,0:T(1,128)S(1)} fusion(f32[8,4,1,1152]{3,2,1,0:T(1,128)S(1)} %bitcast_dynamic-update-slice_fusion.3, f32[4,16,1152]{2,1,0:T(8,128)} %thick_ref.3), kind=kLoop, calls=%fused_computation.6 | loop fusion | bytes 36864
  2.6 0.9 %bitcast_dynamic-update-slice_fusion.1 = f32[8,4,1,1152]{3,2,1,0:T(1,128)S(1)} fusion(f32[8,4,1,1152]{3,2,1,0:T(1,128)S(1)} %bitcast_dynamic-update-slice_fusion.2, f32[4,16,1152]{2,1,0:T(8,128)} %u_ref.3), kind=kLoop, calls=%fused_computation.5 | loop fusion | bytes 36864
  3.5 0.9 %bitcast_dynamic-update-slice_fusion = f32[8,4,1,1152]{3,2,1,0:T(1,128)S(1)} fusion(f32[8,4,1,1152]{3,2,1,0:T(1,128)S(1)} %bitcast_dynamic-update-slice_fusion.1, f32[4,16,1152]{2,1,0:T(8,128)} %v_ref.3), kind=kLoop, calls=%fused_computation.4 | loop fusion | bytes 36864
  4.5 1.4 %slice_dynamic-update-slice_fusion = (f32[8,4,1,1152]{3,2,1,0:T(1,128)S(1)}, f32[4,4,1,1152]{3,2,1,0:T(1,128)S(1)}) fusion(f32[8,4,1,1152]{3,2,1,0:T(1,128)S(1)} %bitcast_dynamic-update-slice_fusion, f32[4,4,16,1152]{3,2,1,0:T(8,128)} %tracer_ref.1), kind=kLoop, calls=%fused_computation.3 | loop fusion | bytes 294912 | tf_op jit(solution)/shard_map/concatenate | solution.py:402
  5.8 1.3 %collective-permute-start.1 = (f32[8,4,1,1152]{3,2,1,0:T(1,128)S(1)}, f32[8,4,1,1152]{3,2,1,0:T(1,128)S(1)}, u32[]{:S(2)}, u32[]{:S(2)}) collective-permute-start(f32[8,4,1,1152]{3,2,1,0:T(1,128)S(1)} %get-tuple-element.28), channel_id=1, source_target_pairs={{4,0},{8,4},{12,8},{5,1},{9,5},{13,9},{6,2},{10,6},{14,10},{7,3},{... | collective-permute-start | bytes 442376 | tf_op jit(solution)/shard_map/ppermute | solution.py:414
  7.1 0.9 %slice_bitcast_fusion.2 = f32[1,4,1,1152]{3,2,1,0:T(1,128)S(1)} fusion(f32[4,16,1152]{2,1,0:T(8,128)} %v_ref.3), kind=kLoop, calls=%fused_computation.8 | loop fusion | bytes 36864 | tf_op jit(solution)/shard_map/broadcast_in_dim | solution.py:401
  8.1 0.9 %slice_bitcast_fusion.3 = f32[1,4,1,1152]{3,2,1,0:T(1,128)S(1)} fusion(f32[4,16,1152]{2,1,0:T(8,128)} %thick_ref.3), kind=kLoop, calls=%fused_computation.9 | loop fusion | bytes 36864 | tf_op jit(solution)/shard_map/broadcast_in_dim | solution.py:401
  9.1 5.6 %collective-permute-start = (f32[6,4,1,1152]{3,2,1,0:T(1,128)S(1)}, f32[6,4,1,1152]{3,2,1,0:T(1,128)S(1)}, u32[]{:S(2)}, u32[]{:S(2)}) collective-permute-start(f32[6,4,1,1152]{3,2,1,0:T(1,128)S(1)} %pad_maximum_fusion), channel_id=1, source_target_pairs={{0,4},{4,8},{8,12},{1,5},{5,9},{9,13},{2,6},{6,10},{10,14},{3,7},{... | collective-permute-start | bytes 331784 | tf_op jit(solution)/shard_map/ppermute | solution.py:413
  15.5 1.5 %collective-permute-done = f32[6,4,1,1152]{3,2,1,0:T(1,128)S(1)} collective-permute-done((f32[6,4,1,1152]{3,2,1,0:T(1,128)S(1)}, f32[6,4,1,1152]{3,2,1,0:T(1,128)S(1)}, u32[]{:S(2)}, u32[]{:S(2)}) %collective-permute-start) | collective-permute-done | bytes 110624 | tf_op jit(solution)/shard_map/ppermute | solution.py:413
  17.6 1.2 %thickness_step.1 = (f32[4,16,1152]{2,1,0:T(8,128)S(1)}, f32[2,4,16,1152]{3,2,1,0:T(8,128)S(1)}, f32[16,1152]{1,0:T(8,128)S(1)}) custom-call(f32[24,128]{1,0:T(8,128)S(1)} %dynamic-slice_bitcast_fusion.geo_ref, s32[1]{0:T(128)} %bitcast.3.first_ref, f32[4,16,1152]{2,1,0:T(8,128)S(1)} %copy-done.1, f32[4,16,1152]{2,1,0:T(8,128)S(1)} %copy-done.3, ...), custom_call_target="tpu_custom_call" | custom-call | flops 2949120 | bytes 2064384 | tf_op jit(solution)/shard_map/thickness_step/pallas_call | solution.py:101
  18.9 1.1 %copy-done.5 = bf16[5,256,256]{2,1,0:T(8,128)(2,1)S(1)} copy-done((bf16[5,256,256]{2,1,0:T(8,128)(2,1)S(1)}, bf16[5,256,256]{2,1,0:T(8,128)(2,1)}, u32[]{:S(2)}) %copy-start.5) | copy-done | bytes 655384
  20.0 1.2 %fourier_filter.1.refs_2_ = f32[2,4,16,1152]{3,2,1,0:T(8,128)S(1)} custom-call(f32[2,4,16,1152]{3,2,1,0:T(8,128)S(1)} %get-tuple-element.20.wind_ref, s32[16,128]{1,0:T(8,128)S(1)} %broadcast_in_dim.31.cutoff_ref, bf16[5,256,256]{2,1,0:T(8,128)(2,1)S(1)} %copy-done.5, bf16[5,256,256]{2,1,0:T(8,128)(2,1)S(1)} %copy-done.4), custom_call_target="tpu_custom_call" | custom-call | flops 503316480 | bytes 2490368 | tf_op jit(solution)/shard_map/fourier_filter/pallas_call | solution.py:262
  23.0 1.6 %collective-permute-start.5 = (f32[16,1152]{1,0:T(8,128)S(1)}, f32[16,1152]{1,0:T(8,128)S(1)}, u32[]{:S(2)}, u32[]{:S(2)}) collective-permute-start(f32[16,1152]{1,0:T(8,128)S(1)} %get-tuple-element.18), channel_id=1, source_target_pairs={{0,3},{1,2},{2,1},{3,0},{4,7},{5,6},{6,5},{7,4},{8,11},{9,10},{10,... | collective-permute-start | bytes 221192 | tf_op jit(solution)/shard_map/ppermute | solution.py:391
  26.1 1.9 %tracer_step.1 = (f32[2,4,16,1152]{3,2,1,0:T(8,128)S(1)}, f32[2,4,16,1152]{3,2,1,0:T(8,128)S(1)}) custom-call(f32[24,128]{1,0:T(8,128)S(1)} %dynamic-slice_bitcast_fusion.geo_ref, f32[4,16,1152]{2,1,0:T(8,128)S(1)} %copy-done.1, f32[4,16,1152]{2,1,0:T(8,128)S(1)} %copy-done.3, f32[4,16,1152]{2,1,0:T(8,128)S(1)} %copy-done.2, ...), custom_call_target="tpu_custom_call" | custom-call | flops 6635520 | bytes 3538944 | tf_op jit(solution)/shard_map/tracer_step/pallas_call | solution.py:153
  28.7 1.7 %collective-permute-done.4.refs_4_ = f32[16,1152]{1,0:T(8,128)S(1)} collective-permute-done((f32[16,1152]{1,0:T(8,128)S(1)}, f32[16,1152]{1,0:T(8,128)S(1)}, u32[]{:S(2)}, u32[]{:S(2)}) %collective-permute-start.4) | collective-permute-done | bytes 73760 | tf_op jit(solution)/shard_map/ppermute | solution.py:383
  30.4 2.9 %remap_parts.4 = (f32[2,4,16,1152]{3,2,1,0:T(8,128)S(1)}, f32[2,4,16,1152]{3,2,1,0:T(8,128)S(1)}) custom-call(s32[2]{0:T(128)S(1)} %pad_add_fusion.place_ref, f32[17]{0:T(128)S(1)} %multiply_reduce_fusion.cum_ref, f32[16]{0:T(128)S(1)} %get-tuple-element.35.frac_ref, f32[16]{0:T(128)S(1)} %get-tuple-element.34.inv_ref, ...), custom_call_target="tpu_custom_call" | custom-call | flops 10616832 | bytes 3538944 | tf_op jit(solution)/shard_map/remap_parts/pallas_call | solution.py:342
  34.1 3.0 %remap_parts.3 = (f32[2,4,16,1152]{3,2,1,0:T(8,128)S(1)}, f32[2,4,16,1152]{3,2,1,0:T(8,128)S(1)}, f32[4,16,1152]{2,1,0:T(8,128)}) custom-call(s32[2]{0:T(128)S(1)} %pad_add_fusion.place_ref, f32[17]{0:T(128)S(1)} %multiply_reduce_fusion.cum_ref, f32[16]{0:T(128)S(1)} %get-tuple-element.35.frac_ref, f32[16]{0:T(128)S(1)} %get-tuple-element.34.inv_ref, ...), custom_call_target="tpu_custom_call" | custom-call | flops 10616832 | bytes 3538944 | tf_op jit(solution)/shard_map/remap_parts/pallas_call | solution.py:342
  37.2 1.2 %collective-permute-start.10 = (f32[2,4,16,1152]{3,2,1,0:T(8,128)S(1)}, f32[2,4,16,1152]{3,2,1,0:T(8,128)S(1)}, u32[]{:S(2)}, u32[]{:S(2)}) collective-permute-start(f32[2,4,16,1152]{3,2,1,0:T(8,128)S(1)} %get-tuple-element.27), channel_id=1, source_target_pairs={{0,2},{2,0},{1,3},{3,1},{4,6},{6,4},{5,7},{7,5},{8,10},{10,8},{9,1... | collective-permute-start | bytes 1769480 | tf_op jit(solution)/shard_map/ppermute | solution.py:383
  38.4 2.3 %remap_parts.5 = (f32[2,4,16,1152]{3,2,1,0:T(8,128)S(1)}, f32[2,4,16,1152]{3,2,1,0:T(8,128)S(1)}) custom-call(s32[2]{0:T(128)S(1)} %pad_add_fusion.place_ref, f32[17]{0:T(128)S(1)} %multiply_reduce_fusion.cum_ref, f32[16]{0:T(128)S(1)} %get-tuple-element.35.frac_ref, f32[16]{0:T(128)S(1)} %get-tuple-element.34.inv_ref, ...), custom_call_target="tpu_custom_call" | custom-call | flops 10616832 | bytes 3538944 | tf_op jit(solution)/shard_map/remap_parts/pallas_call | solution.py:342
  41.6 8.0 %collective-permute-done.7 = f32[2,4,16,1152]{3,2,1,0:T(8,128)S(1)} collective-permute-done((f32[2,4,16,1152]{3,2,1,0:T(8,128)S(1)}, f32[2,4,16,1152]{3,2,1,0:T(8,128)S(1)}, u32[]{:S(2)}, u32[]{:S(2)}) %collective-permute-start.7) | collective-permute-done | bytes 589856 | tf_op jit(solution)/shard_map/ppermute | solution.py:383
  50.5 11.7 %collective-permute-done.10.refs_3_ = f32[2,4,16,1152]{3,2,1,0:T(8,128)S(1)} collective-permute-done((f32[2,4,16,1152]{3,2,1,0:T(8,128)S(1)}, f32[2,4,16,1152]{3,2,1,0:T(8,128)S(1)}, u32[]{:S(2)}, u32[]{:S(2)}) %collective-permute-start.10) | collective-permute-done | bytes 589856 | tf_op jit(solution)/shard_map/ppermute | solution.py:383
  62.2 11.3 %collective-permute-done.9.refs_1_ = f32[2,4,16,1152]{3,2,1,0:T(8,128)S(1)} collective-permute-done((f32[2,4,16,1152]{3,2,1,0:T(8,128)S(1)}, f32[2,4,16,1152]{3,2,1,0:T(8,128)S(1)}, u32[]{:S(2)}, u32[]{:S(2)}) %collective-permute-start.9) | collective-permute-done | bytes 589856 | tf_op jit(solution)/shard_map/ppermute | solution.py:383
  73.5 1.1 %add_parts.1 = f32[4,4,16,1152]{3,2,1,0:T(8,128)} custom-call(f32[2,4,16,1152]{3,2,1,0:T(8,128)S(1)} %get-tuple-element.24.refs_0_, f32[2,4,16,1152]{3,2,1,0:T(8,128)S(1)} %collective-permute-done.9.refs_1_, f32[2,4,16,1152]{3,2,1,0:T(8,128)S(1)} %get-tuple-element.26.refs_2_, f32[2,4,16,1152]{3,2,1,0:T(8,128)S(1)} %collective-permute-done.10.refs_3_), custom_call_target="tpu_custom_call" | custom-call | flops 294912 | bytes 3538944 | tf_op jit(solution)/shard_map/add_parts/pallas_call | solution.py:370
  (44 shorter events, 8.2 us)
Async XLA Ops:
  0.6 17.0 %copy-start.1 = (f32[4,16,1152]{2,1,0:T(8,128)S(1)}, f32[4,16,1152]{2,1,0:T(8,128)}, u32[]{:S(2)}) copy-start(f32[4,16,1152]{2,1,0:T(8,128)} %thick_ref.3) | copy-start | bytes 884740
  0.6 17.0 %copy-start.3 = (f32[4,16,1152]{2,1,0:T(8,128)S(1)}, f32[4,16,1152]{2,1,0:T(8,128)}, u32[]{:S(2)}) copy-start(f32[4,16,1152]{2,1,0:T(8,128)} %u_ref.3) | copy-start | bytes 884740
  0.7 17.0 %copy-start.2 = (f32[4,16,1152]{2,1,0:T(8,128)S(1)}, f32[4,16,1152]{2,1,0:T(8,128)}, u32[]{:S(2)}) copy-start(f32[4,16,1152]{2,1,0:T(8,128)} %v_ref.3) | copy-start | bytes 884740
  0.7 18.2 %copy-start.8 = (s32[16]{0:T(128)S(1)}, s32[16]{0:T(128)}, u32[]{:S(2)}) copy-start(s32[16]{0:T(128)} %param.15) | copy-start | bytes 196
  5.8 11.2 %collective-permute-start.1 = (f32[8,4,1,1152]{3,2,1,0:T(1,128)S(1)}, f32[8,4,1,1152]{3,2,1,0:T(1,128)S(1)}, u32[]{:S(2)}, u32[]{:S(2)}) collective-permute-start(f32[8,4,1,1152]{3,2,1,0:T(1,128)S(1)} %get-tuple-element.28), channel_id=1, source_target_pairs={{4,0},{8,4},{12,8},{5,1},{9,5},{13,9},{6,2},{10,6},{14,10},{7,3},{... | collective-permute-start | bytes 442376 | tf_op jit(solution)/shard_map/ppermute | solution.py:414
  9.1 7.9 %collective-permute-start = (f32[6,4,1,1152]{3,2,1,0:T(1,128)S(1)}, f32[6,4,1,1152]{3,2,1,0:T(1,128)S(1)}, u32[]{:S(2)}, u32[]{:S(2)}) collective-permute-start(f32[6,4,1,1152]{3,2,1,0:T(1,128)S(1)} %pad_maximum_fusion), channel_id=1, source_target_pairs={{0,4},{4,8},{8,12},{1,5},{5,9},{9,13},{2,6},{6,10},{10,14},{3,7},{... | collective-permute-start | bytes 331784 | tf_op jit(solution)/shard_map/ppermute | solution.py:413
  14.7 4.2 %copy-start.4 = (bf16[5,256,256]{2,1,0:T(8,128)(2,1)S(1)}, bf16[5,256,256]{2,1,0:T(8,128)(2,1)}, u32[]{:S(2)}) copy-start(bf16[5,256,256]{2,1,0:T(8,128)(2,1)} %constant.33.clone.low_ref) | copy-start | bytes 1966084
  17.0 0.6 copy-start.6
  18.9 1.1 %copy-start.5 = (bf16[5,256,256]{2,1,0:T(8,128)(2,1)S(1)}, bf16[5,256,256]{2,1,0:T(8,128)(2,1)}, u32[]{:S(2)}) copy-start(bf16[5,256,256]{2,1,0:T(8,128)(2,1)} %constant.32.clone.high_ref) | copy-start | bytes 1966084
  20.0 1.3 %copy-start.9 = (f32[16]{0:T(128)S(1)}, f32[16]{0:T(128)}, u32[]{:S(2)}) copy-start(f32[16]{0:T(128)} %param.14) | copy-start | bytes 196
  20.0 4.7 %copy-start.7 = (f32[17,16]{0,1:T(8,128)S(1)}, f32[17,16]{0,1:T(8,128)}, u32[]{:S(2)}) copy-start(f32[17,16]{0,1:T(8,128)} %constant.31.clone) | copy-start | bytes 3268
  20.0 6.1 %copy-start = (f32[4,4,16,1152]{3,2,1,0:T(8,128)S(1)}, f32[4,4,16,1152]{3,2,1,0:T(8,128)}, u32[]{:S(2)}) copy-start(f32[4,4,16,1152]{3,2,1,0:T(8,128)} %tracer_ref.1) | copy-start | bytes 3538948
  21.2 9.2 %collective-permute-start.6 = (f32[2,4,16,1152]{3,2,1,0:T(8,128)S(1)}, f32[2,4,16,1152]{3,2,1,0:T(8,128)}, u32[]{:S(2)}, u32[]{:S(2)}) collective-permute-start(f32[2,4,16,1152]{3,2,1,0:T(8,128)S(1)} %fourier_filter.1.refs_2_), channel_id=1, source_target_pairs={{0,1},{1,0},{2,3},{3,2},{4,5},{5,4},{6,7},{7,6},{8,9},{9,8},{10,11... | collective-permute-start | bytes 1769480 | tf_op jit(solution)/shard_map/ppermute | solution.py:385
  21.9 8.5 %collective-permute-start.2 = (f32[4,16,1152]{2,1,0:T(8,128)S(1)}, f32[4,16,1152]{2,1,0:T(8,128)S(1)}, u32[]{:S(2)}, u32[]{:S(2)}) collective-permute-start(f32[4,16,1152]{2,1,0:T(8,128)S(1)} %get-tuple-element.16.new_ref.refs_0_), channel_id=1, source_target_pairs={{0,1},{1,0},{2,3},{3,2},{4,5},{5,4},{6,7},{7,6},{8,9},{9,8},{10,11... | collective-permute-start | bytes 884744 | tf_op jit(solution)/shard_map/ppermute | solution.py:385
  23.0 5.2 %collective-permute-start.5 = (f32[16,1152]{1,0:T(8,128)S(1)}, f32[16,1152]{1,0:T(8,128)S(1)}, u32[]{:S(2)}, u32[]{:S(2)}) collective-permute-start(f32[16,1152]{1,0:T(8,128)S(1)} %get-tuple-element.18), channel_id=1, source_target_pairs={{0,3},{1,2},{2,1},{3,0},{4,7},{5,6},{6,5},{7,4},{8,11},{9,10},{10,... | collective-permute-start | bytes 221192 | tf_op jit(solution)/shard_map/ppermute | solution.py:391
  25.7 4.7 %collective-permute-start.4 = (f32[16,1152]{1,0:T(8,128)S(1)}, f32[16,1152]{1,0:T(8,128)S(1)}, u32[]{:S(2)}, u32[]{:S(2)}) collective-permute-start(f32[16,1152]{1,0:T(8,128)S(1)} %get-tuple-element.18), channel_id=1, source_target_pairs={{0,2},{2,0},{1,3},{3,1},{4,6},{6,4},{5,7},{7,5},{8,10},{10,8},{9,1... | collective-permute-start | bytes 221192 | tf_op jit(solution)/shard_map/ppermute | solution.py:383
  28.0 6.1 %collective-permute-start.3 = (f32[2,4,16,1152]{3,2,1,0:T(8,128)S(1)}, f32[2,4,16,1152]{3,2,1,0:T(8,128)S(1)}, u32[]{:S(2)}, u32[]{:S(2)}) collective-permute-start(f32[2,4,16,1152]{3,2,1,0:T(8,128)S(1)} %get-tuple-element.17.refs_2_), channel_id=1, source_target_pairs={{0,1},{1,0},{2,3},{3,2},{4,5},{5,4},{6,7},{7,6},{8,9},{9,8},{10,11... | collective-permute-start | bytes 1769480 | tf_op jit(solution)/shard_map/ppermute | solution.py:385
  28.2 10.2 %collective-permute-start.8 = (f32[2,4,16,1152]{3,2,1,0:T(8,128)S(1)}, f32[2,4,16,1152]{3,2,1,0:T(8,128)S(1)}, u32[]{:S(2)}, u32[]{:S(2)}) collective-permute-start(f32[2,4,16,1152]{3,2,1,0:T(8,128)S(1)} %get-tuple-element.23.refs_2_), channel_id=1, source_target_pairs={{0,1},{1,0},{2,3},{3,2},{4,5},{5,4},{6,7},{7,6},{8,9},{9,8},{10,11... | collective-permute-start | bytes 1769480 | tf_op jit(solution)/shard_map/ppermute | solution.py:385
  33.2 16.3 %collective-permute-start.7 = (f32[2,4,16,1152]{3,2,1,0:T(8,128)S(1)}, f32[2,4,16,1152]{3,2,1,0:T(8,128)S(1)}, u32[]{:S(2)}, u32[]{:S(2)}) collective-permute-start(f32[2,4,16,1152]{3,2,1,0:T(8,128)S(1)} %get-tuple-element.22), channel_id=1, source_target_pairs={{0,2},{2,0},{1,3},{3,1},{4,6},{6,4},{5,7},{7,5},{8,10},{10,8},{9,1... | collective-permute-start | bytes 1769480 | tf_op jit(solution)/shard_map/ppermute | solution.py:383
  37.2 25.0 %collective-permute-start.10 = (f32[2,4,16,1152]{3,2,1,0:T(8,128)S(1)}, f32[2,4,16,1152]{3,2,1,0:T(8,128)S(1)}, u32[]{:S(2)}, u32[]{:S(2)}) collective-permute-start(f32[2,4,16,1152]{3,2,1,0:T(8,128)S(1)} %get-tuple-element.27), channel_id=1, source_target_pairs={{0,2},{2,0},{1,3},{3,1},{4,6},{6,4},{5,7},{7,5},{8,10},{10,8},{9,1... | collective-permute-start | bytes 1769480 | tf_op jit(solution)/shard_map/ppermute | solution.py:383
  40.7 32.8 %collective-permute-start.9 = (f32[2,4,16,1152]{3,2,1,0:T(8,128)S(1)}, f32[2,4,16,1152]{3,2,1,0:T(8,128)S(1)}, u32[]{:S(2)}, u32[]{:S(2)}) collective-permute-start(f32[2,4,16,1152]{3,2,1,0:T(8,128)S(1)} %get-tuple-element.25), channel_id=1, source_target_pairs={{0,2},{2,0},{1,3},{3,1},{4,6},{6,4},{5,7},{7,5},{8,10},{10,8},{9,1... | collective-permute-start | bytes 1769480 | tf_op jit(solution)/shard_map/ppermute | solution.py:383

commit v2 on v1

--- a/solution.py
+++ b/solution.py
@@ -57,32 +57,68 @@
     return jnp.where(row_ids(value.shape) == 0, beyond, pltpu.roll(value, 1, 0))
 
 
-def fluxes(geo_ref, thick, u, v, thick_s, v_s, thick_n):
+def fluxes(geo, thick, u, v, thick_s, v_s, thick_n):
     rows = thick.shape[0]
     east = u * jnp.where(u > 0, thick, east_of(thick))
-    north = v * jnp.where(v > 0, thick, north_of(thick, thick_n)) * geo_ref[0:rows, 1:2]
-    below = v_s * jnp.where(v_s > 0, thick_s, thick[0:1]) * geo_ref[0:1, 0:1]
+    north = v * jnp.where(v > 0, thick, north_of(thick, thick_n)) * geo[0:rows, 1:2]
+    below = v_s * jnp.where(v_s > 0, thick_s, thick[0:1]) * geo[0:1, 0:1]
     return east, north, below
 
 
-def thickness_kernel(lat_rows, geo_ref, first_ref, thick_ref, u_ref, v_ref, up_ref, down_ref, new_ref, wind_ref, sum_ref):
+def edge_kernel(thick_top, v_top, tracer_top, thick_low, u_low, v_low, tracer_low, last_ref, leading_ref):
+    T = tracer_top.shape[0]
+    rows = thick_top.shape[1]
+    last_ref[0] = thick_top[:, rows - 1 : rows]
+    last_ref[1] = v_top[:, rows - 1 : rows]
+    last_ref[2 : 2 + T] = tracer_top[:, :, rows - 1 : rows]
+    leading_ref[0] = thick_low[:, 0:1]
+    leading_ref[1] = thick_low[:, 1:2]
+    leading_ref[2] = u_low[:, 0:1]
+    leading_ref[3] = v_low[:, 0:1]
+    leading_ref[4 : 4 + T] = tracer_low[:, :, 0:1]
+
+
+def edge_rows(thickness, wind_u, wind_v, tracers):
+    L, R, N = thickness.shape
+    T = tracers.shape[0]
+    block = lambda at: pl.BlockSpec((L, 8, N), lambda i: (0, at, 0))
+    blocks = lambda at: pl.BlockSpec((T, L, 8, N), lambda i: (0, 0, at, 0))
+    top = R // 8 - 1
+    whole = lambda n: pl.BlockSpec((n, L, 1, N), lambda i: (0, 0, 0, 0))
+    return pl.pallas_call(
+        edge_kernel,
+        grid=(1,),
+        in_specs=[block(top), block(top), blocks(top), block(0), block(0), block(0), blocks(0)],
+        out_specs=[whole(2 + T), whole(4 + T)],
+        out_shape=[
+            jax.ShapeDtypeStruct((2 + T, L, 1, N), jnp.float32),
+            jax.ShapeDtypeStruct((4 + T, L, 1, N), jnp.float32),
+        ],
+        compiler_params=params(),
+        cost_estimate=cost(0, 4 * L * N * 8 * (5 + 2 * T)),
+        name="edge_rows",
+    )(thickness, wind_v, tracers, thickness, wind_u, wind_v, tracers)
+
+
+def thickness_kernel(lat_rows, band_ref, table_ref, thick_ref, u_ref, v_ref, up_ref, down_ref, new_ref, wind_ref, sum_ref):
     rows = thick_ref.shape[1]
+    geo = table_ref[band_ref[0]]
     thick, u, v = thick_ref[0], u_ref[0], v_ref[0]
     thick_s, v_s = up_ref[0, 0], up_ref[1, 0]
     thick_n, thick_nn, u_n, v_n = (down_ref[i, 0] for i in range(4))
-    east, north, below = fluxes(geo_ref, thick, u, v, thick_s, v_s, thick_n)
-    inverse = geo_ref[0:rows, 2:3]
+    east, north, below = fluxes(geo, thick, u, v, thick_s, v_s, thick_n)
+    inverse = geo[0:rows, 2:3]
     new = thick - (east - west_of(east)) - (north - south_of(north, below)) * inverse
     east_n = u_n * jnp.where(u_n > 0, thick_n, east_of(thick_n))
-    north_n = v_n * jnp.where(v_n > 0, thick_n, thick_nn) * geo_ref[rows : rows + 1, 1:2]
+    north_n = v_n * jnp.where(v_n > 0, thick_n, thick_nn) * geo[rows : rows + 1, 1:2]
     new_n = (
         thick_n
         - (east_n - west_of(east_n))
-        - (north_n - north[rows - 1 : rows]) * geo_ref[rows : rows + 1, 2:3]
+        - (north_n - north[rows - 1 : rows]) * geo[rows : rows + 1, 2:3]
     )
     new_ref[0] = new
     wind_ref[0, 0] = u - 0.05 * (east_of(new) - new)
-    inside = first_ref[0] + row_ids(new.shape) < lat_rows - 1
+    inside = band_ref[0] * rows + row_ids(new.shape) < lat_rows - 1
     wind_ref[1, 0] = jnp.where(inside, v - 0.05 * (north_of(new, new_n) - new), 0.0)
 
     @pl.when(pl.program_id(0) == 0)
@@ -94,7 +130,7 @@
         sum_ref[...] += new
 
 
-def thickness_step(geo, first, lat_rows, thickness, wind_u, wind_v, up, down):
+def thickness_step(band, table, lat_rows, thickness, wind_u, wind_v, up, down):
     L, R, N = thickness.shape
     level = pl.BlockSpec((1, R, N), lambda k: (k, 0, 0))
     unit = 4 * R * N
@@ -102,8 +138,8 @@
         functools.partial(thickness_kernel, lat_rows),
         grid=(L,),
         in_specs=[
-            pl.BlockSpec(geo.shape, lambda k: (0, 0)),
             SMEM,
+            pl.BlockSpec(table.shape, lambda k: (0, 0, 0)),
             level,
             level,
             level,
@@ -123,54 +159,64 @@
         compiler_params=params(),
         cost_estimate=cost(40 * L * R * N, 7 * L * unit),
         name="thickness_step",
-    )(geo, first, thickness, wind_u, wind_v, up, down)
-
-
-def tracer_kernel(geo_ref, thick_ref, u_ref, v_ref, new_ref, up_ref, down_ref, tracer_ref, up_t_ref, down_t_ref, *out_refs):
+    )(band, table, thickness, wind_u, wind_v, up, down)
+
+
+def tracer_kernel(band_ref, table_ref, thick_ref, u_ref, v_ref, new_ref, up_ref, down_ref, tracer_ref, up_t_ref, down_t_ref, out_ref):
     rows = thick_ref.shape[1]
+    geo = table_ref[band_ref[0]]
     thick, u, v = thick_ref[0], u_ref[0], v_ref[0]
-    east, north, below = fluxes(geo_ref, thick, u, v, up_ref[0, 0], up_ref[1, 0], down_ref[0, 0])
     v_s = up_ref[1, 0]
-    inverse = geo_ref[0:rows, 2:3]
+    east, north, below = fluxes(geo, thick, u, v, up_ref[0, 0], v_s, down_ref[0, 0])
+    inverse = geo[0:rows, 2:3]
     scale = 1.0 / new_ref[0]
-    per_out = out_refs[0].shape[0]
-    for c in range(tracer_ref.shape[0]):
+    count = tracer_ref.shape[0]
+    extra = out_ref.shape[0] - count
+    if extra:
+        out_ref[0, 0] = new_ref[0]
+    for c in range(count):
         q = tracer_ref[c, 0]
         t_east = east * jnp.where(u > 0, q, east_of(q))
         t_north = north * jnp.where(v > 0, q, north_of(q, down_t_ref[c, 0]))
         t_below = below * jnp.where(v_s > 0, up_t_ref[c, 0], q[0:1])
         change = thick * q - (t_east - west_of(t_east))
         change = change - (t_north - south_of(t_north, t_below)) * inverse
-        out_refs[c // per_out][c % per_out, 0] = change * scale
-
-
-def tracer_step(geo, thickness, wind_u, wind_v, thick_new, up, down, tracers, up_t, down_t, parts):
+        out_ref[extra + c, 0] = change * scale
+
+
+def tracer_step(band, table, thickness, wind_u, wind_v, thick_new, up, down, tracers, begin, count, with_thickness):
     L, R, N = thickness.shape
-    T = tracers.shape[0]
     level = pl.BlockSpec((1, R, N), lambda k: (k, 0, 0))
     edge = lambda n: pl.BlockSpec((n, 1, 1, N), lambda k: (0, k, 0, 0))
+    some = lambda at: pl.BlockSpec(
+        (pl.Element(count), pl.Element(1), pl.Element(1), pl.Element(N)), lambda k: (at, k, 0, 0)
+    )
+    total = count + (1 if with_thickness else 0)
     unit = 4 * R * N
     return pl.pallas_call(
         tracer_kernel,
         grid=(L,),
         in_specs=[
-            pl.BlockSpec(geo.shape, lambda k: (0, 0)),
+            SMEM,
+            pl.BlockSpec(table.shape, lambda k: (0, 0, 0)),
             level,
             level,
             level,
             level,
             edge(2),
             edge(1),
-            pl.BlockSpec((T, 1, R, N), lambda k: (0, k, 0, 0)),
-            edge(T),
-            edge(T),
+            pl.BlockSpec(
+                (pl.Element(count), pl.Element(1), pl.Element(R), pl.Element(N)), lambda k: (begin, k, 0, 0)
+            ),
+            some(2 + begin),
+            some(4 + begin),
         ],
-        out_specs=[pl.BlockSpec((T // parts, 1, R, N), lambda k: (0, k, 0, 0))] * parts,
-        out_shape=[jax.ShapeDtypeStruct((T // parts, L, R, N), jnp.float32)] * parts,
+        out_specs=pl.BlockSpec((total, 1, R, N), lambda k: (0, k, 0, 0)),
+        out_shape=jax.ShapeDtypeStruct((total, L, R, N), jnp.float32),
         compiler_params=params(),
-        cost_estimate=cost(90 * L * R * N, (2 * T + 4) * L * unit),
+        cost_estimate=cost(30 * (count + 1) * L * R * N, (2 * count + 5) * L * unit),
         name="tracer_step",
-    )(geo, thickness, wind_u, wind_v, thick_new, up, down, tracers, up_t, down_t)
+    )(band, table, thickness, wind_u, wind_v, thick_new, up, down, tracers, up, down)
 
 
 def filter_tables(N):
@@ -270,18 +316,33 @@
     )(wind, jnp.broadcast_to(cutoff[:, None], (R, LANES)), jnp.asarray(high), jnp.asarray(low))
 
 
-def remap_kernel(lev_count, sub_count, with_thickness, place_ref, cum_ref, frac_ref, inv_ref, *refs):
+def remap_kernel(lev_count, sub_count, with_thickness, place_ref, weight_ref, *refs):
     S, C = sub_count, lev_count
     thick_refs, refs = refs[:S], refs[S:]
     field_refs, refs = refs[:S], refs[S:]
     other_refs, refs = refs[: (C - 1) * S], refs[(C - 1) * S :]
     out_refs = refs[:C]
-    F, L, R, N = field_refs[0].shape
+    F, L, R, N = out_refs[0].shape
+    extra = field_refs[0].shape[0] - F
     lev, sub = place_ref[0], place_ref[1]
     spot = [lax.rem(sub + S - t, S) for t in range(S)]
+    targets = [(lax.rem(lev + s, C) * S + sub) * L for s in range(C)]
+    below_sum = [jnp.float32(0.0) for _ in range(C)]
+    weight_sum = jnp.float32(0.0)
+    for k in range(C * S * L):
+        w = weight_ref[k]
+        for s in range(C):
+            below_sum[s] = below_sum[s] + jnp.where(k < targets[s], w, 0.0)
+        weight_sum = weight_sum + w
+    weights = [[weight_ref[first + i] for i in range(L)] for first in targets]
+    sums = []
+    for s in range(C):
+        sums.append([below_sum[s]])
+        for w in weights[s]:
+            sums[s].append(sums[s][-1] + w)
 
     def tile(rows, columns):
-        thick = [[thick_refs[t][m, rows, columns] for m in range(L)] for t in range(S)]
+        thick = [[thick_refs[t][0, m, rows, columns] for m in range(L)] for t in range(S)]
         group = [functools.reduce(jnp.add, levels) for levels in thick]
         mass = functools.reduce(jnp.add, group)
         base = jnp.zeros_like(mass)
@@ -300,12 +361,11 @@
             for m in range(L):
                 sources.append((t, m, low, thick[t][m]))
                 low = low + thick[t][m]
-        inverse = 1.0 / mass
+        unit = mass / weight_sum
         for s in range(C):
-            first = (lax.rem(lev + s, C) * S + sub) * L
 
             def covered(i):
-                top = mass * cum_ref[first + i]
+                top = unit * sums[s][i]
                 return [jnp.minimum(jnp.maximum(top - low, 0.0), h) for _, _, low, h in sources]
 
             below = covered(0)
@@ -313,15 +373,16 @@
                 upto = covered(i + 1)
                 part = [a - b for a, b in zip(upto, below)]
                 below = upto
-                scale = inverse * inv_ref[first + i]
+                target = unit * weights[s][i]
+                scale = 1.0 / target
                 for f in range(F):
                     total = None
                     for (t, m, _, _), w in zip(sources, part):
-                        term = field_refs[t][f, m, rows, columns] * w
+                        term = field_refs[t][extra + f, m, rows, columns] * w
                         total = term if total is None else total + term
                     out_refs[s][f, i, rows, columns] = total * scale
                 if with_thickness and s == 0:
-                    refs[C][i, rows, columns] = mass * frac_ref[first + i]
+                    refs[C][i, rows, columns] = target
 
     for r in range(0, R, 8):
 
@@ -332,46 +393,56 @@
         lax.fori_loop(0, N // LANES, body, 0)
 
 
-def remap_parts(counts, place, cum, frac, inv, thick, fields, others, with_thickness):
+def remap_parts(counts, place, weights, thick, fields, others, with_thickness, extra):
     C, S = counts
     F, L, R, N = fields[0].shape
+    F = F - extra
     shape = jax.ShapeDtypeStruct((F, L, R, N), jnp.float32)
     out_shape = [shape] * C
     if with_thickness:
         out_shape = out_shape + [jax.ShapeDtypeStruct((L, R, N), jnp.float32)]
     return pl.pallas_call(
         functools.partial(remap_kernel, C, S, with_thickness),
-        in_specs=[SMEM] * 4 + [VMEM] * (2 * S + len(others)),
+        in_specs=[SMEM] * 2 + [VMEM] * (2 * S + len(others)),
         out_specs=[VMEM] * len(out_shape),
         out_shape=out_shape,
         compiler_params=params(),
         cost_estimate=cost(C * S * L * L * R * N * (5 + 2 * F), 4 * R * N * L * (F + 1) * (S + C)),
         name="remap_parts",
-    )(place, cum, frac, inv, *thick, *fields, *others)
-
-
-def add_kernel(groups, *refs):
-    outs = refs[-1]
+    )(place, weights, *thick, *fields, *others)
+
+
+def add_kernel(groups, outs_count, *refs):
+    outs = refs[len(refs) - outs_count :]
+    refs = refs[: len(refs) - outs_count]
     at = 0
-    each = len(refs[:-1]) // groups
+    each = len(refs) // groups
     for g in range(groups):
         total = refs[g * each][...]
         for i in range(1, each):
             total = total + refs[g * each + i][...]
         n = total.shape[0]
-        outs[at : at + n] = total
+        if outs_count == 1:
+            outs[0][at : at + n] = total
+        else:
+            for i in range(n):
+                outs[at + i][...] = total[i]
         at += n
 
 
-def add_parts(groups):
+def add_parts(groups, outs_count):
     flat = [a for group in groups for a in group]
     total = sum(group[0].shape[0] for group in groups)
     L, R, N = flat[0].shape[1:]
+    if outs_count == 1:
+        out_shape = jax.ShapeDtypeStruct((total, L, R, N), jnp.float32)
+    else:
+        out_shape = [jax.ShapeDtypeStruct((L, R, N), jnp.float32)] * total
     return pl.pallas_call(
-        functools.partial(add_kernel, len(groups)),
+        functools.partial(add_kernel, len(groups), outs_count),
         in_specs=[VMEM] * len(flat),
-        out_specs=VMEM,
-        out_shape=jax.ShapeDtypeStruct((total, L, R, N), jnp.float32),
+        out_specs=VMEM if outs_count == 1 else [VMEM] * total,
+        out_shape=out_shape,
         compiler_params=params(),
         cost_estimate=cost(total * L * R * N, 4 * total * L * R * N * 3),
         name="add_parts",
@@ -398,53 +469,33 @@
     lat_rows = R * lat_count
     send = functools.partial(shifted, lev_count=C, sub_count=S)
 
-    last = jnp.concatenate([thickness[None, :, R - 1 :], wind_v[None, :, R - 1 :], tracers[:, :, R - 1 :]], axis=0)
-    leading = jnp.concatenate(
-        [
-            thickness[None, :, 0:1],
-            thickness[None, :, 1:2],
-            wind_u[None, :, 0:1],
-            wind_v[None, :, 0:1],
-            tracers[:, :, 0:1],
-        ],
-        axis=0,
-    )
+    last, leading = edge_rows(thickness, wind_u, wind_v, tracers)
     northward = [(i, i + 1) for i in range(lat_count - 1)]
     up = lax.ppermute(last, "lat", northward)
     down = lax.ppermute(leading, "lat", [(j, i) for i, j in northward])
 
-    band = lax.axis_index("lat")
-    geo = lax.dynamic_index_in_dim(jnp.asarray(geometry_table(lat_rows, R)), band, 0, keepdims=False)
-    first = (band * R).astype(jnp.int32).reshape(1)
+    band = lax.axis_index("lat").astype(jnp.int32).reshape(1)
+    table = jnp.asarray(geometry_table(lat_rows, R))
     place = jnp.stack([lax.axis_index("lev"), lax.axis_index("sub")]).astype(jnp.int32)
-    levels = level_weights.shape[0]
-    fraction = level_weights / jnp.sum(level_weights)
-    lower = np.tril(np.ones((levels + 1, levels), np.float32), -1)
-    cum = jnp.sum(jnp.asarray(lower) * fraction[None, :], axis=1)
-    inv = 1.0 / fraction
-
-    up_h, up_t = up[:2], up[2:]
-    down_h, down_t = down[:4], down[4:]
-    thick_new, wind, own_sum = thickness_step(geo, first, lat_rows, thickness, wind_u, wind_v, up_h, down_h)
+
+    thick_new, wind, own_sum = thickness_step(band, table, lat_rows, thickness, wind_u, wind_v, up, down)
     others = [send(own_sum, s=s, t=t) for s in range(1, C) for t in range(S)]
-    thick = [thick_new] + [send(thick_new, s=0, t=t) for t in range(1, S)]
-    parts = 2
-    tracer_new = tracer_step(
-        geo, thickness, wind_u, wind_v, thick_new, up_h, down_h, tracers, up_t, down_t, parts
-    )
-    filtered = fourier_filter(wind, cutoff)
+    step = functools.partial(tracer_step, band, table, thickness, wind_u, wind_v, thick_new, up, down, tracers)
+    T = tracers.shape[0]
+    sources = [step(0, 1, True), step(1, T - 1, False), fourier_filter(wind, cutoff)]
+    gathered = [[own] + [send(own, s=0, t=t) for t in range(1, S)] for own in sources]
     results = []
     thickness_out = None
-    for index, own in enumerate(list(tracer_new) + [filtered]):
-        fields = [own] + [send(own, s=0, t=t) for t in range(1, S)]
-        with_thickness = index == 1
-        out = remap_parts((C, S), place, cum, fraction, inv, thick, fields, others, with_thickness)
+    for index, fields in enumerate(gathered):
+        with_thickness = index == 2
+        extra = 1 if index == 0 else 0
+        out = remap_parts((C, S), place, level_weights, gathered[0], fields, others, with_thickness, extra)
         if with_thickness:
             thickness_out = out[C]
         results.append([out[0]] + [send(out[s], s=s, t=0) for s in range(1, C)])
-    tracers_out = add_parts(results[:parts])
-    winds = functools.reduce(jnp.add, results[parts])
-    return thickness_out, winds[0], winds[1], tracers_out
+    tracers_out = add_parts(results[:2], 1)
+    u_out, v_out = add_parts(results[2:], 2)
+    return thickness_out, u_out, v_out, tracers_out
 
 
 def solution(mesh):

time: 75.1 us -> 73 us (0.972)
  local copies, waits for them, and re-layouts: 11.4 us -> 4.25 us
  waiting for transfers between devices: 34.3 us -> 37.5 us
  Pallas kernels: 13.6 us -> 16.7 us
  other arithmetic: 1.57 us -> 0.07 us
    pallas_call x2 -> x5, Pallas kernels: 3.03 us -> 5.61 us  [the longest x2 3.4 us: tracer_step(): pl.pallas_call(tracer_kernel, grid=(L,), in_specs=[SMEM, pl.BlockSpec(tab...]
    ppermute x4, starting transfers between devices: 3.42 us -> 5.63 us  [shifted(): lax.ppermute(value, 'lev', [(i, (i + s) % lev_count) for i in range(lev_c...]
    broadcast_in_dim x2 -> x0, local copies, waits for them, and re-layouts: 1.86 us -> none  [the longest x1 0.93 us: per_device(): wind_v[None, :, R - 1:]]
    squeeze x2 -> x0, local copies, waits for them, and re-layouts: 1.63 us -> none  [the longest x1 0.85 us: per_device(): return (thickness_out, winds[0], winds[1], tracers_out)]
    ppermute x1, starting transfers between devices: 1.62 us -> 0.06 us  [shifted(): return lax.ppermute(value, ('lev', 'sub'), pairs)]
    ppermute x1, waiting for transfers between devices: 0.01 us -> 1.37 us  [shifted(): return lax.ppermute(value, ('lev', 'sub'), pairs)]
    concatenate x1 -> x0, local copies, waits for them, and re-layouts: 1.36 us -> none  [per_device(): jnp.concatenate([thickness[None, :, 0:1], thickness[None, :, 1:2], wind_u...]
    unnamed x24 -> x26, local copies, waits for them, and re-layouts: 5.52 us -> 4.18 us
  transfers between devices with their start and end apart: 11 -> 10, of which waited for: 5 -> 5; matrix products, arithmetic and copies ran while one was open for 8% -> 0% of each run, Pallas kernels for 14% -> 16%
where the time goes in v2:
time: 73 us; the launch traced here: 72.6 us
  waiting for transfers between devices  37.5 us (51%)
  Pallas kernels  16.7 us (23%)
  starting transfers between devices  13.3 us (18%)
  local copies, waits for them, and re-layouts  4.25 us (6%)
  between operations  0.77 us (1%)
    ppermute x4, waiting for transfers between devices, shifted(): lax.ppermute(value, 'lev', [(i, (i + s) % lev_count) for i in range(lev_c...  33.8 us
    pallas_call x3, Pallas kernels, remap_parts(): pl.pallas_call(functools.partial(remap_kernel, C, S, with_thickness), in_...  8.64 us
    ppermute x4, starting transfers between devices, shifted(): lax.ppermute(value, 'lev', [(i, (i + s) % lev_count) for i in range(lev_c...  5.63 us
    ppermute x1, starting transfers between devices, per_device(): up = lax.ppermute(last, 'lat', northward)  5.56 us
    unnamed x26, local copies, waits for them, and re-layouts  4.18 us
    pallas_call x2, Pallas kernels, tracer_step(): pl.pallas_call(tracer_kernel, grid=(L,), in_specs=[SMEM, pl.BlockSpec(tab...  3.4 us
    ppermute x1, waiting for transfers between devices, per_device(): up = lax.ppermute(last, 'lat', northward)  2.3 us
    pallas_call x2, Pallas kernels, add_parts(): pl.pallas_call(functools.partial(add_kernel, len(groups), outs_count), in...  2.01 us
  transfers between devices with their start and end apart: 10, of which 5 were waited for; matrix products, arithmetic and copies ran while one was open for 0% of the time, Pallas kernels for 16%

profile of v2, /device:TPU:0, one launch (start us, length us, event | category | flops | bytes accessed | tf_op | source)
XLA Modules:
  0.0 72.6 jit_solution(2202379338005375218)
XLA Ops:
  0.6 1.3 %copy-done = f32[4,4,16,1152]{3,2,1,0:T(8,128)S(1)} copy-done((f32[4,4,16,1152]{3,2,1,0:T(8,128)S(1)}, f32[4,4,16,1152]{3,2,1,0:T(8,128)}, u32[]{:S(2)}) %copy-start) | copy-done | bytes 1179672
  1.9 1.0 %copy-done.2 = f32[4,16,1152]{2,1,0:T(8,128)S(1)} copy-done((f32[4,16,1152]{2,1,0:T(8,128)S(1)}, f32[4,16,1152]{2,1,0:T(8,128)}, u32[]{:S(2)}) %copy-start.2) | copy-done | bytes 294936
  2.9 1.0 %copy-done.4 = f32[4,16,1152]{2,1,0:T(8,128)S(1)} copy-done((f32[4,16,1152]{2,1,0:T(8,128)S(1)}, f32[4,16,1152]{2,1,0:T(8,128)}, u32[]{:S(2)}) %copy-start.4) | copy-done | bytes 294936
  3.8 1.0 %copy-done.6 = f32[4,16,1152]{2,1,0:T(8,128)S(1)} copy-done((f32[4,16,1152]{2,1,0:T(8,128)S(1)}, f32[4,16,1152]{2,1,0:T(8,128)}, u32[]{:S(2)}) %copy-start.6) | copy-done | bytes 294936
  5.0 1.4 %collective-permute-start.1 = (f32[8,4,1,1152]{3,2,1,0:T(1,128)S(1)}, f32[8,4,1,1152]{3,2,1,0:T(1,128)S(1)}, u32[]{:S(2)}, u32[]{:S(2)}) collective-permute-start(f32[8,4,1,1152]{3,2,1,0:T(1,128)S(1)} %get-tuple-element.19), channel_id=1, source_target_pairs={{4,0},{8,4},{12,8},{5,1},{9,5},{13,9},{6,2},{10,6},{14,10},{7,3},{... | collective-permute-start | bytes 442376 | tf_op jit(solution)/shard_map/ppermute | solution.py:475
  6.5 5.6 %collective-permute-start = (f32[6,4,1,1152]{3,2,1,0:T(1,128)S(1)}, f32[6,4,1,1152]{3,2,1,0:T(1,128)S(1)}, u32[]{:S(2)}, u32[]{:S(2)}) collective-permute-start(f32[6,4,1,1152]{3,2,1,0:T(1,128)S(1)} %get-tuple-element.18), channel_id=1, source_target_pairs={{0,4},{4,8},{8,12},{1,5},{5,9},{9,13},{2,6},{6,10},{10,14},{3,7},{... | collective-permute-start | bytes 331784 | tf_op jit(solution)/shard_map/ppermute | solution.py:474
  12.0 2.3 %collective-permute-done.up_ref.up_t_ref = f32[6,4,1,1152]{3,2,1,0:T(1,128)S(1)} collective-permute-done((f32[6,4,1,1152]{3,2,1,0:T(1,128)S(1)}, f32[6,4,1,1152]{3,2,1,0:T(1,128)S(1)}, u32[]{:S(2)}, u32[]{:S(2)}) %collective-permute-start) | collective-permute-done | bytes 110624 | tf_op jit(solution)/shard_map/ppermute | solution.py:474
  14.4 1.2 %thickness_step.1 = (f32[4,16,1152]{2,1,0:T(8,128)S(1)}, f32[2,4,16,1152]{3,2,1,0:T(8,128)S(1)}, f32[16,1152]{1,0:T(8,128)S(1)}) custom-call(s32[1]{0:T(128)} %bitcast.2.band_ref, f32[4,24,128]{2,1,0:T(8,128)S(1)} %copy-done.10, f32[4,16,1152]{2,1,0:T(8,128)S(1)} %copy-done.3, f32[4,16,1152]{2,1,0:T(8,128)S(1)} %copy-done.7, f32[4,16,1152]{2,1,0:T(8,128)S(1)} %copy-done.5, ...), custom_call_target="tpu_custom_call" | custom-call | flops 2949120 | bytes 2064384 | tf_op jit(solution)/shard_map/thickness_step/pallas_call | solution.py:137
  15.6 2.4 %tracer_step.3.refs_2_ = f32[3,4,16,1152]{3,2,1,0:T(8,128)} custom-call(s32[1]{0:T(128)} %bitcast.2.band_ref, f32[4,24,128]{2,1,0:T(8,128)S(1)} %copy-done.10, f32[4,16,1152]{2,1,0:T(8,128)S(1)} %copy-done.3, f32[4,16,1152]{2,1,0:T(8,128)S(1)} %copy-done.7, f32[4,16,1152]{2,1,0:T(8,128)S(1)} %copy-done.5, f32[4,16,1152]{2,1,0:T(8,128)S(1)} %get-tuple-element.20.new_ref, ...), custom_call_target="tpu_custom_call" | custom-call | flops 8847360 | bytes 3244032 | tf_op jit(solution)/shard_map/tracer_step/pallas_call | solution.py:196
  18.0 1.0 %tracer_step.2.refs_0_.refs_2_ = f32[2,4,16,1152]{3,2,1,0:T(8,128)S(1)} custom-call(s32[1]{0:T(128)} %bitcast.2.band_ref, f32[4,24,128]{2,1,0:T(8,128)S(1)} %copy-done.10, f32[4,16,1152]{2,1,0:T(8,128)S(1)} %copy-done.3, f32[4,16,1152]{2,1,0:T(8,128)S(1)} %copy-done.7, f32[4,16,1152]{2,1,0:T(8,128)S(1)} %copy-done.5, ...), custom_call_target="tpu_custom_call" | custom-call | flops 4423680 | bytes 2064384 | tf_op jit(solution)/shard_map/tracer_step/pallas_call | solution.py:196
  19.0 0.5 collective-permute-start.2
  19.6 1.2 %fourier_filter.1.refs_2_ = f32[2,4,16,1152]{3,2,1,0:T(8,128)S(1)} custom-call(f32[2,4,16,1152]{3,2,1,0:T(8,128)S(1)} %get-tuple-element.21.wind_ref, s32[16,128]{1,0:T(8,128)S(1)} %broadcast_in_dim.2.cutoff_ref, bf16[5,256,256]{2,1,0:T(8,128)(2,1)S(1)} %copy-done.8, bf16[5,256,256]{2,1,0:T(8,128)(2,1)S(1)} %copy-done.9), custom_call_target="tpu_custom_call" | custom-call | flops 503316480 | bytes 2490368 | tf_op jit(solution)/shard_map/fourier_filter/pallas_call | solution.py:308
  21.0 2.0 %collective-permute-start.4 = (f32[16,1152]{1,0:T(8,128)S(1)}, f32[16,1152]{1,0:T(8,128)S(1)}, u32[]{:S(2)}, u32[]{:S(2)}) collective-permute-start(f32[16,1152]{1,0:T(8,128)S(1)} %get-tuple-element.22), channel_id=1, source_target_pairs={{0,2},{2,0},{1,3},{3,1},{4,6},{6,4},{5,7},{7,5},{8,10},{10,8},{9,1... | collective-permute-start | bytes 221192 | tf_op jit(solution)/shard_map/ppermute | solution.py:454
  23.1 2.7 %collective-permute-done.4.refs_4_ = f32[16,1152]{1,0:T(8,128)S(1)} collective-permute-done((f32[16,1152]{1,0:T(8,128)S(1)}, f32[16,1152]{1,0:T(8,128)S(1)}, u32[]{:S(2)}, u32[]{:S(2)}) %collective-permute-start.4) | collective-permute-done | bytes 73760 | tf_op jit(solution)/shard_map/ppermute | solution.py:454
  25.8 1.4 %collective-permute-done.5.refs_5_ = f32[16,1152]{1,0:T(8,128)S(1)} collective-permute-done((f32[16,1152]{1,0:T(8,128)S(1)}, f32[16,1152]{1,0:T(8,128)S(1)}, u32[]{:S(2)}, u32[]{:S(2)}) %collective-permute-start.5) | collective-permute-done | bytes 73760 | tf_op jit(solution)/shard_map/ppermute | solution.py:462
  27.2 3.6 %remap_parts.5 = (f32[3,4,16,1152]{3,2,1,0:T(8,128)S(1)}, f32[3,4,16,1152]{3,2,1,0:T(8,128)S(1)}) custom-call(s32[2]{0:T(128)S(1)} %pad_add_fusion.place_ref, f32[16]{0:T(128)S(1)} %copy-done.11, f32[2,4,16,1152]{3,2,1,0:T(8,128)S(1)} %tracer_step.2.refs_0_.refs_2_, f32[2,4,16,1152]{3,2,1,0:T(8,128)S(1)} %collective-permute-done.2.refs_1_.refs_3_, ...), custom_call_target="tpu_custom_call" | custom-call | flops 12976128 | bytes 4718592 | tf_op jit(solution)/shard_map/remap_parts/pallas_call | solution.py:404
  30.7 1.6 %collective-permute-start.9 = (f32[3,4,16,1152]{3,2,1,0:T(8,128)S(1)}, f32[3,4,16,1152]{3,2,1,0:T(8,128)S(1)}, u32[]{:S(2)}, u32[]{:S(2)}) collective-permute-start(f32[3,4,16,1152]{3,2,1,0:T(8,128)S(1)} %get-tuple-element.31), channel_id=1, source_target_pairs={{0,2},{2,0},{1,3},{3,1},{4,6},{6,4},{5,7},{7,5},{8,10},{10,8},{9,1... | collective-permute-start | bytes 2654216 | tf_op jit(solution)/shard_map/ppermute | solution.py:454
  32.3 3.0 %remap_parts.3 = (f32[2,4,16,1152]{3,2,1,0:T(8,128)S(1)}, f32[2,4,16,1152]{3,2,1,0:T(8,128)S(1)}, f32[4,16,1152]{2,1,0:T(8,128)}) custom-call(s32[2]{0:T(128)S(1)} %pad_add_fusion.place_ref, f32[16]{0:T(128)S(1)} %copy-done.11, f32[2,4,16,1152]{3,2,1,0:T(8,128)S(1)} %tracer_step.2.refs_0_.refs_2_, ...), custom_call_target="tpu_custom_call" | custom-call | flops 10616832 | bytes 3538944 | tf_op jit(solution)/shard_map/remap_parts/pallas_call | solution.py:404
  35.9 2.0 %remap_parts.4 = (f32[1,4,16,1152]{3,2,1,0:T(8,128)S(1)}, f32[1,4,16,1152]{3,2,1,0:T(8,128)S(1)}) custom-call(s32[2]{0:T(128)S(1)} %pad_add_fusion.place_ref, f32[16]{0:T(128)S(1)} %copy-done.11, f32[2,4,16,1152]{3,2,1,0:T(8,128)S(1)} %tracer_step.2.refs_0_.refs_2_, f32[2,4,16,1152]{3,2,1,0:T(8,128)S(1)} %collective-permute-done.2.refs_1_.refs_3_, ...), custom_call_target="tpu_custom_call" | custom-call | flops 8257536 | bytes 2359296 | tf_op jit(solution)/shard_map/remap_parts/pallas_call | solution.py:404
  37.9 1.6 %collective-permute-start.7 = (f32[1,4,16,1152]{3,2,1,0:T(8,128)S(1)}, f32[1,4,16,1152]{3,2,1,0:T(8,128)S(1)}, u32[]{:S(2)}, u32[]{:S(2)}) collective-permute-start(f32[1,4,16,1152]{3,2,1,0:T(8,128)S(1)} %get-tuple-element.29), channel_id=1, source_target_pairs={{0,2},{2,0},{1,3},{3,1},{4,6},{6,4},{5,7},{7,5},{8,10},{10,8},{9,1... | collective-permute-start | bytes 884744 | tf_op jit(solution)/shard_map/ppermute | solution.py:454
  39.5 26.5 %collective-permute-done.6.refs_1_ = f32[2,4,16,1152]{3,2,1,0:T(8,128)S(1)} collective-permute-done((f32[2,4,16,1152]{3,2,1,0:T(8,128)S(1)}, f32[2,4,16,1152]{3,2,1,0:T(8,128)S(1)}, u32[]{:S(2)}, u32[]{:S(2)}) %collective-permute-start.6) | collective-permute-done | bytes 589856 | tf_op jit(solution)/shard_map/ppermute | solution.py:454
  65.9 0.9 %add_parts.2 = (f32[4,16,1152]{2,1,0:T(8,128)}, f32[4,16,1152]{2,1,0:T(8,128)}) custom-call(f32[2,4,16,1152]{3,2,1,0:T(8,128)S(1)} %get-tuple-element.24.refs_0_, f32[2,4,16,1152]{3,2,1,0:T(8,128)S(1)} %collective-permute-done.6.refs_1_), custom_call_target="tpu_custom_call" | custom-call | flops 147456 | bytes 1769472 | tf_op jit(solution)/shard_map/add_parts/pallas_call | solution.py:441
  66.8 4.7 %collective-permute-done.7.refs_1_ = f32[1,4,16,1152]{3,2,1,0:T(8,128)S(1)} collective-permute-done((f32[1,4,16,1152]{3,2,1,0:T(8,128)S(1)}, f32[1,4,16,1152]{3,2,1,0:T(8,128)S(1)}, u32[]{:S(2)}, u32[]{:S(2)}) %collective-permute-start.7) | collective-permute-done | bytes 294944 | tf_op jit(solution)/shard_map/ppermute | solution.py:454
  71.5 1.1 %add_parts.3 = f32[4,4,16,1152]{3,2,1,0:T(8,128)} custom-call(f32[1,4,16,1152]{3,2,1,0:T(8,128)S(1)} %get-tuple-element.28.refs_0_, f32[1,4,16,1152]{3,2,1,0:T(8,128)S(1)} %collective-permute-done.7.refs_1_, f32[3,4,16,1152]{3,2,1,0:T(8,128)S(1)} %get-tuple-element.30.refs_2_, f32[3,4,16,1152]{3,2,1,0:T(8,128)S(1)} %collective-permute-done.9.refs_3_), custom_call_target="tpu_custom_call" | custom-call | flops 294912 | bytes 3538944 | tf_op jit(solution)/shard_map/add_parts/pallas_call | solution.py:441
  (34 shorter events, 1.1 us)
Async XLA Ops:
  0.6 1.3 %copy-start = (f32[4,4,16,1152]{3,2,1,0:T(8,128)S(1)}, f32[4,4,16,1152]{3,2,1,0:T(8,128)}, u32[]{:S(2)}) copy-start(f32[4,4,16,1152]{3,2,1,0:T(8,128)} %tracer_ref.3) | copy-start | bytes 3538948
  1.9 1.0 %copy-start.2 = (f32[4,16,1152]{2,1,0:T(8,128)S(1)}, f32[4,16,1152]{2,1,0:T(8,128)}, u32[]{:S(2)}) copy-start(f32[4,16,1152]{2,1,0:T(8,128)} %thick_ref.5) | copy-start | bytes 884740
  2.9 1.0 %copy-start.4 = (f32[4,16,1152]{2,1,0:T(8,128)S(1)}, f32[4,16,1152]{2,1,0:T(8,128)}, u32[]{:S(2)}) copy-start(f32[4,16,1152]{2,1,0:T(8,128)} %v_ref.5) | copy-start | bytes 884740
  3.8 1.0 %copy-start.6 = (f32[4,16,1152]{2,1,0:T(8,128)S(1)}, f32[4,16,1152]{2,1,0:T(8,128)}, u32[]{:S(2)}) copy-start(f32[4,16,1152]{2,1,0:T(8,128)} %u_ref.5) | copy-start | bytes 884740
  4.8 9.5 %copy-start.3 = (f32[4,16,1152]{2,1,0:T(8,128)S(1)}, f32[4,16,1152]{2,1,0:T(8,128)}, u32[]{:S(2)}) copy-start(f32[4,16,1152]{2,1,0:T(8,128)} %thick_ref.5) | copy-start | bytes 884740
  4.8 9.5 %copy-start.5 = (f32[4,16,1152]{2,1,0:T(8,128)S(1)}, f32[4,16,1152]{2,1,0:T(8,128)}, u32[]{:S(2)}) copy-start(f32[4,16,1152]{2,1,0:T(8,128)} %v_ref.5) | copy-start | bytes 884740
  4.8 9.5 %copy-start.7 = (f32[4,16,1152]{2,1,0:T(8,128)S(1)}, f32[4,16,1152]{2,1,0:T(8,128)}, u32[]{:S(2)}) copy-start(f32[4,16,1152]{2,1,0:T(8,128)} %u_ref.5) | copy-start | bytes 884740
  4.8 9.5 %copy-start.10 = (f32[4,24,128]{2,1,0:T(8,128)S(1)}, f32[4,24,128]{2,1,0:T(8,128)}, u32[]{:S(2)}) copy-start(f32[4,24,128]{2,1,0:T(8,128)} %constant.17.clone.table_ref) | copy-start | bytes 147460
  5.0 10.6 %copy-start.1 = (f32[4,4,16,1152]{3,2,1,0:T(8,128)S(1)}, f32[4,4,16,1152]{3,2,1,0:T(8,128)}, u32[]{:S(2)}) copy-start(f32[4,4,16,1152]{3,2,1,0:T(8,128)} %tracer_ref.3) | copy-start | bytes 3538948
  5.0 9.3 %collective-permute-start.1 = (f32[8,4,1,1152]{3,2,1,0:T(1,128)S(1)}, f32[8,4,1,1152]{3,2,1,0:T(1,128)S(1)}, u32[]{:S(2)}, u32[]{:S(2)}) collective-permute-start(f32[8,4,1,1152]{3,2,1,0:T(1,128)S(1)} %get-tuple-element.19), channel_id=1, source_target_pairs={{4,0},{8,4},{12,8},{5,1},{9,5},{13,9},{6,2},{10,6},{14,10},{7,3},{... | collective-permute-start | bytes 442376 | tf_op jit(solution)/shard_map/ppermute | solution.py:475
  6.5 7.9 %collective-permute-start = (f32[6,4,1,1152]{3,2,1,0:T(1,128)S(1)}, f32[6,4,1,1152]{3,2,1,0:T(1,128)S(1)}, u32[]{:S(2)}, u32[]{:S(2)}) collective-permute-start(f32[6,4,1,1152]{3,2,1,0:T(1,128)S(1)} %get-tuple-element.18), channel_id=1, source_target_pairs={{0,4},{4,8},{8,12},{1,5},{5,9},{9,13},{2,6},{6,10},{10,14},{3,7},{... | collective-permute-start | bytes 331784 | tf_op jit(solution)/shard_map/ppermute | solution.py:474
  18.0 1.5 %copy-start.12 = (s32[16]{0:T(128)S(1)}, s32[16]{0:T(128)}, u32[]{:S(2)}) copy-start(s32[16]{0:T(128)} %param.14) | copy-start | bytes 196
  18.0 1.6 %copy-start.8 = (bf16[5,256,256]{2,1,0:T(8,128)(2,1)S(1)}, bf16[5,256,256]{2,1,0:T(8,128)(2,1)}, u32[]{:S(2)}) copy-start(bf16[5,256,256]{2,1,0:T(8,128)(2,1)} %constant.18.clone.high_ref) | copy-start | bytes 1966084
  18.0 1.6 %copy-start.9 = (bf16[5,256,256]{2,1,0:T(8,128)(2,1)S(1)}, bf16[5,256,256]{2,1,0:T(8,128)(2,1)}, u32[]{:S(2)}) copy-start(bf16[5,256,256]{2,1,0:T(8,128)(2,1)} %constant.19.clone.low_ref) | copy-start | bytes 1966084
  18.0 9.1 %collective-permute-start.8 = (f32[3,4,16,1152]{3,2,1,0:T(8,128)}, f32[3,4,16,1152]{3,2,1,0:T(8,128)}, u32[]{:S(2)}, u32[]{:S(2)}) collective-permute-start(f32[3,4,16,1152]{3,2,1,0:T(8,128)} %tracer_step.3.refs_2_), channel_id=1, source_target_pairs={{0,1},{1,0},{2,3},{3,2},{4,5},{5,4},{6,7},{7,6},{8,9},{9,8},{10,11... | collective-permute-start | bytes 2654216 | tf_op jit(solution)/shard_map/ppermute | solution.py:456
  19.0 8.2 %collective-permute-start.2 = (f32[2,4,16,1152]{3,2,1,0:T(8,128)S(1)}, f32[2,4,16,1152]{3,2,1,0:T(8,128)S(1)}, u32[]{:S(2)}, u32[]{:S(2)}) collective-permute-start(f32[2,4,16,1152]{3,2,1,0:T(8,128)S(1)} %tracer_step.2.refs_0_.refs_2_), channel_id=1, source_target_pairs={{0,1},{1,0},{2,3},{3,2},{4,5},{5,4},{6,7},{7,6},{8,9},{9,8},{10,11... | collective-permute-start | bytes 1769480 | tf_op jit(solution)/shard_map/ppermute | solution.py:456
  19.6 7.6 %copy-start.11 = (f32[16]{0:T(128)S(1)}, f32[16]{0:T(128)}, u32[]{:S(2)}) copy-start(f32[16]{0:T(128)} %weight_ref.5) | copy-start | bytes 196
  20.8 11.5 %collective-permute-start.3 = (f32[2,4,16,1152]{3,2,1,0:T(8,128)S(1)}, f32[2,4,16,1152]{3,2,1,0:T(8,128)S(1)}, u32[]{:S(2)}, u32[]{:S(2)}) collective-permute-start(f32[2,4,16,1152]{3,2,1,0:T(8,128)S(1)} %fourier_filter.1.refs_2_), channel_id=1, source_target_pairs={{0,1},{1,0},{2,3},{3,2},{4,5},{5,4},{6,7},{7,6},{8,9},{9,8},{10,11... | collective-permute-start | bytes 1769480 | tf_op jit(solution)/shard_map/ppermute | solution.py:456
  21.0 4.8 %collective-permute-start.4 = (f32[16,1152]{1,0:T(8,128)S(1)}, f32[16,1152]{1,0:T(8,128)S(1)}, u32[]{:S(2)}, u32[]{:S(2)}) collective-permute-start(f32[16,1152]{1,0:T(8,128)S(1)} %get-tuple-element.22), channel_id=1, source_target_pairs={{0,2},{2,0},{1,3},{3,1},{4,6},{6,4},{5,7},{7,5},{8,10},{10,8},{9,1... | collective-permute-start | bytes 221192 | tf_op jit(solution)/shard_map/ppermute | solution.py:454
  22.9 4.2 %collective-permute-start.5 = (f32[16,1152]{1,0:T(8,128)S(1)}, f32[16,1152]{1,0:T(8,128)S(1)}, u32[]{:S(2)}, u32[]{:S(2)}) collective-permute-start(f32[16,1152]{1,0:T(8,128)S(1)} %get-tuple-element.22), channel_id=1, source_target_pairs={{0,3},{1,2},{2,1},{3,0},{4,7},{5,6},{6,5},{7,4},{8,11},{9,10},{10,... | collective-permute-start | bytes 221192 | tf_op jit(solution)/shard_map/ppermute | solution.py:462
  30.7 40.7 %collective-permute-start.9 = (f32[3,4,16,1152]{3,2,1,0:T(8,128)S(1)}, f32[3,4,16,1152]{3,2,1,0:T(8,128)S(1)}, u32[]{:S(2)}, u32[]{:S(2)}) collective-permute-start(f32[3,4,16,1152]{3,2,1,0:T(8,128)S(1)} %get-tuple-element.31), channel_id=1, source_target_pairs={{0,2},{2,0},{1,3},{3,1},{4,6},{6,4},{5,7},{7,5},{8,10},{10,8},{9,1... | collective-permute-start | bytes 2654216 | tf_op jit(solution)/shard_map/ppermute | solution.py:454
  35.4 30.6 %collective-permute-start.6 = (f32[2,4,16,1152]{3,2,1,0:T(8,128)S(1)}, f32[2,4,16,1152]{3,2,1,0:T(8,128)S(1)}, u32[]{:S(2)}, u32[]{:S(2)}) collective-permute-start(f32[2,4,16,1152]{3,2,1,0:T(8,128)S(1)} %get-tuple-element.25), channel_id=1, source_target_pairs={{0,2},{2,0},{1,3},{3,1},{4,6},{6,4},{5,7},{7,5},{8,10},{10,8},{9,1... | collective-permute-start | bytes 1769480 | tf_op jit(solution)/shard_map/ppermute | solution.py:454
  37.9 33.6 %collective-permute-start.7 = (f32[1,4,16,1152]{3,2,1,0:T(8,128)S(1)}, f32[1,4,16,1152]{3,2,1,0:T(8,128)S(1)}, u32[]{:S(2)}, u32[]{:S(2)}) collective-permute-start(f32[1,4,16,1152]{3,2,1,0:T(8,128)S(1)} %get-tuple-element.29), channel_id=1, source_target_pairs={{0,2},{2,0},{1,3},{3,1},{4,6},{6,4},{5,7},{7,5},{8,10},{10,8},{9,1... | collective-permute-start | bytes 884744 | tf_op jit(solution)/shard_map/ppermute | solution.py:454

commit v3 on v2

--- a/solution.py
+++ b/solution.py
@@ -20,6 +20,10 @@
 
 def cost(flops, bytes_accessed):
     return pl.CostEstimate(flops=int(flops), bytes_accessed=int(bytes_accessed), transcendentals=0)
+
+
+def after(*arrays):
+    return [pl.BlockSpec(memory_space=pl.ANY)] * len(arrays)
 
 
 def geometry_table(lat_rows, band_rows):
@@ -65,7 +69,8 @@
     return east, north, below
 
 
-def edge_kernel(thick_top, v_top, tracer_top, thick_low, u_low, v_low, tracer_low, last_ref, leading_ref):
+def edge_kernel(thick_top, v_top, tracer_top, thick_low, u_low, v_low, tracer_low, *refs):
+    last_ref, leading_ref = refs[-2:]
     T = tracer_top.shape[0]
     rows = thick_top.shape[1]
     last_ref[0] = thick_top[:, rows - 1 : rows]
@@ -78,7 +83,7 @@
     leading_ref[4 : 4 + T] = tracer_low[:, :, 0:1]
 
 
-def edge_rows(thickness, wind_u, wind_v, tracers):
+def edge_rows(thickness, wind_u, wind_v, tracers, wait):
     L, R, N = thickness.shape
     T = tracers.shape[0]
     block = lambda at: pl.BlockSpec((L, 8, N), lambda i: (0, at, 0))
@@ -88,7 +93,7 @@
     return pl.pallas_call(
         edge_kernel,
         grid=(1,),
-        in_specs=[block(top), block(top), blocks(top), block(0), block(0), block(0), blocks(0)],
+        in_specs=[block(top), block(top), blocks(top), block(0), block(0), block(0), blocks(0)] + after(*wait),
         out_specs=[whole(2 + T), whole(4 + T)],
         out_shape=[
             jax.ShapeDtypeStruct((2 + T, L, 1, N), jnp.float32),
@@ -97,7 +102,43 @@
         compiler_params=params(),
         cost_estimate=cost(0, 4 * L * N * 8 * (5 + 2 * T)),
         name="edge_rows",
-    )(thickness, wind_v, tracers, thickness, wind_u, wind_v, tracers)
+    )(thickness, wind_v, tracers, thickness, wind_u, wind_v, tracers, *wait)
+
+
+def first_kernel(band_ref, table_ref, thick_ref, u_ref, v_ref, new_ref, sum_ref):
+    geo = table_ref[band_ref[0]]
+    thick, u, v = thick_ref[0], u_ref[0], v_ref[0]
+    nothing = jnp.zeros((1, thick.shape[1]), jnp.float32)
+    east, north, below = fluxes(geo, thick, u, v, nothing, nothing, nothing)
+    new = thick - (east - west_of(east)) - (north - south_of(north, below)) * geo[0 : thick.shape[0], 2:3]
+    new_ref[0] = new
+
+    @pl.when(pl.program_id(0) == 0)
+    def _():
+        sum_ref[...] = new
+
+    @pl.when(pl.program_id(0) > 0)
+    def _():
+        sum_ref[...] += new
+
+
+def first_step(band, table, thickness, wind_u, wind_v):
+    L, R, N = thickness.shape
+    level = pl.BlockSpec((1, R, N), lambda k: (k, 0, 0))
+    in_hbm = lambda x: pltpu.with_memory_space_constraint(x, pltpu.HBM)
+    return pl.pallas_call(
+        first_kernel,
+        grid=(L,),
+        in_specs=[SMEM, pl.BlockSpec(table.shape, lambda k: (0, 0, 0)), level, level, level],
+        out_specs=[level, pl.BlockSpec((R, N), lambda k: (0, 0))],
+        out_shape=[
+            jax.ShapeDtypeStruct((L, R, N), jnp.float32),
+            jax.ShapeDtypeStruct((R, N), jnp.float32),
+        ],
+        compiler_params=params(),
+        cost_estimate=cost(1, 1),
+        name="first_step",
+    )(band, in_hbm(table), in_hbm(thickness), in_hbm(wind_u), in_hbm(wind_v))
 
 
 def thickness_kernel(lat_rows, band_ref, table_ref, thick_ref, u_ref, v_ref, up_ref, down_ref, new_ref, wind_ref, sum_ref):
@@ -123,17 +164,18 @@
 
     @pl.when(pl.program_id(0) == 0)
     def _():
-        sum_ref[...] = new
+        sum_ref[0:1] = new[0:1]
+        sum_ref[1:2] = new[rows - 1 : rows]
 
     @pl.when(pl.program_id(0) > 0)
     def _():
-        sum_ref[...] += new
+        sum_ref[0:1] += new[0:1]
+        sum_ref[1:2] += new[rows - 1 : rows]
 
 
 def thickness_step(band, table, lat_rows, thickness, wind_u, wind_v, up, down):
     L, R, N = thickness.shape
     level = pl.BlockSpec((1, R, N), lambda k: (k, 0, 0))
-    unit = 4 * R * N
     return pl.pallas_call(
         functools.partial(thickness_kernel, lat_rows),
         grid=(L,),
@@ -149,52 +191,63 @@
         out_specs=[
             level,
             pl.BlockSpec((2, 1, R, N), lambda k: (0, k, 0, 0)),
-            pl.BlockSpec((R, N), lambda k: (0, 0)),
+            pl.BlockSpec((2, N), lambda k: (0, 0)),
         ],
         out_shape=[
             jax.ShapeDtypeStruct((L, R, N), jnp.float32),
             jax.ShapeDtypeStruct((2, L, R, N), jnp.float32),
-            jax.ShapeDtypeStruct((R, N), jnp.float32),
+            jax.ShapeDtypeStruct((2, N), jnp.float32),
         ],
         compiler_params=params(),
-        cost_estimate=cost(40 * L * R * N, 7 * L * unit),
+        cost_estimate=cost(1, 1),
         name="thickness_step",
     )(band, table, thickness, wind_u, wind_v, up, down)
 
 
-def tracer_kernel(band_ref, table_ref, thick_ref, u_ref, v_ref, new_ref, up_ref, down_ref, tracer_ref, up_t_ref, down_t_ref, out_ref):
-    rows = thick_ref.shape[1]
+def tracer_kernel(edges, band_ref, table_ref, thick_ref, u_ref, v_ref, new_ref, tracer_ref, *refs):
+    rows, width = thick_ref.shape[1:]
+    out_ref = refs[-1]
     geo = table_ref[band_ref[0]]
     thick, u, v = thick_ref[0], u_ref[0], v_ref[0]
-    v_s = up_ref[1, 0]
-    east, north, below = fluxes(geo, thick, u, v, up_ref[0, 0], v_s, down_ref[0, 0])
+    nothing = jnp.zeros((1, width), jnp.float32)
+    if edges:
+        up_ref, down_ref = refs[:2]
+        thick_s, v_s, thick_n = up_ref[0, 0], up_ref[1, 0], down_ref[0, 0]
+    else:
+        thick_s, v_s, thick_n = nothing, nothing, nothing
+    east, north, below = fluxes(geo, thick, u, v, thick_s, v_s, thick_n)
     inverse = geo[0:rows, 2:3]
     scale = 1.0 / new_ref[0]
+
+    def store(at, value):
+        if edges:
+            out_ref[at, 0, 0:1] = value[0:1]
+            out_ref[at, 0, 1:2] = value[rows - 1 : rows]
+        else:
+            out_ref[at, 0] = value
+
     count = tracer_ref.shape[0]
     extra = out_ref.shape[0] - count
     if extra:
-        out_ref[0, 0] = new_ref[0]
+        store(0, new_ref[0])
     for c in range(count):
         q = tracer_ref[c, 0]
+        q_s, q_n = (up_ref[2 + c, 0], down_ref[4 + c, 0]) if edges else (nothing, nothing)
         t_east = east * jnp.where(u > 0, q, east_of(q))
-        t_north = north * jnp.where(v > 0, q, north_of(q, down_t_ref[c, 0]))
-        t_below = below * jnp.where(v_s > 0, up_t_ref[c, 0], q[0:1])
+        t_north = north * jnp.where(v > 0, q, north_of(q, q_n))
+        t_below = below * jnp.where(v_s > 0, q_s, q[0:1])
         change = thick * q - (t_east - west_of(t_east))
         change = change - (t_north - south_of(t_north, t_below)) * inverse
-        out_ref[extra + c, 0] = change * scale
-
-
-def tracer_step(band, table, thickness, wind_u, wind_v, thick_new, up, down, tracers, begin, count, with_thickness):
+        store(extra + c, change * scale)
+
+
+def tracer_step(band, table, thickness, wind_u, wind_v, thick_new, tracers, begin, count, with_thickness, halo, wait):
     L, R, N = thickness.shape
     level = pl.BlockSpec((1, R, N), lambda k: (k, 0, 0))
-    edge = lambda n: pl.BlockSpec((n, 1, 1, N), lambda k: (0, k, 0, 0))
-    some = lambda at: pl.BlockSpec(
-        (pl.Element(count), pl.Element(1), pl.Element(1), pl.Element(N)), lambda k: (at, k, 0, 0)
-    )
     total = count + (1 if with_thickness else 0)
-    unit = 4 * R * N
-    return pl.pallas_call(
-        tracer_kernel,
+    rows = 2 if halo else R
+    return pl.pallas_call(
+        functools.partial(tracer_kernel, bool(halo)),
         grid=(L,),
         in_specs=[
             SMEM,
@@ -203,20 +256,18 @@
             level,
             level,
             level,
-            edge(2),
-            edge(1),
             pl.BlockSpec(
                 (pl.Element(count), pl.Element(1), pl.Element(R), pl.Element(N)), lambda k: (begin, k, 0, 0)
             ),
-            some(2 + begin),
-            some(4 + begin),
-        ],
-        out_specs=pl.BlockSpec((total, 1, R, N), lambda k: (0, k, 0, 0)),
-        out_shape=jax.ShapeDtypeStruct((total, L, R, N), jnp.float32),
-        compiler_params=params(),
-        cost_estimate=cost(30 * (count + 1) * L * R * N, (2 * count + 5) * L * unit),
+        ]
+        + [pl.BlockSpec((a.shape[0], 1, 1, N), lambda k: (0, k, 0, 0)) for a in halo]
+        + after(*wait),
+        out_specs=pl.BlockSpec((total, 1, rows, N), lambda k: (0, k, 0, 0)),
+        out_shape=jax.ShapeDtypeStruct((total, L, rows, N), jnp.float32),
+        compiler_params=params(),
+        cost_estimate=cost(1, 1),
         name="tracer_step",
-    )(band, table, thickness, wind_u, wind_v, thick_new, up, down, tracers, up, down)
+    )(band, table, thickness, wind_u, wind_v, thick_new, tracers, *halo, *wait)
 
 
 def filter_tables(N):
@@ -246,7 +297,7 @@
     return dot(v_high, high) + (dot(v_high, low) + dot(v_low, high))
 
 
-def filter_kernel(N, wind_ref, cutoff_ref, high_ref, low_ref, out_ref):
+def filter_kernel(N, wind_ref, new_ref, cutoff_ref, high_ref, low_ref, out_ref):
     A = N // LANES
     half = A // 2
     F, L, R, _ = wind_ref.shape
@@ -284,8 +335,9 @@
             imag.append(back[:, LANES:])
 
     def store(a, value):
-        out_ref[:, :, :, a * LANES : (a + 1) * LANES] = value.reshape(F, L, R, LANES)
-
+        out_ref[1:, :, :, a * LANES : (a + 1) * LANES] = value.reshape(F, L, R, LANES)
+
+    out_ref[0] = new_ref[...]
     first = real[0]
     for q in range(1, half + 1):
         first = first + real[q]
@@ -301,55 +353,61 @@
         store(A - a, even_part + odd_part)
 
 
-def fourier_filter(wind, cutoff):
+def fourier_filter(wind, thick_new, cutoff):
     F, L, R, N = wind.shape
     high, low = filter_tables(N)
-    macs = F * L * R * high.size
     return pl.pallas_call(
         functools.partial(filter_kernel, N),
-        in_specs=[VMEM] * 4,
+        in_specs=[VMEM] * 5,
         out_specs=VMEM,
-        out_shape=jax.ShapeDtypeStruct(wind.shape, jnp.float32),
-        compiler_params=params(),
-        cost_estimate=cost(2 * 6 * macs, 8 * F * L * R * N + 4 * high.size),
+        out_shape=jax.ShapeDtypeStruct((F + 1, L, R, N), jnp.float32),
+        compiler_params=params(),
+        cost_estimate=cost(1, 1),
         name="fourier_filter",
-    )(wind, jnp.broadcast_to(cutoff[:, None], (R, LANES)), jnp.asarray(high), jnp.asarray(low))
-
-
-def remap_kernel(lev_count, sub_count, with_thickness, place_ref, weight_ref, *refs):
-    S, C = sub_count, lev_count
+    )(wind, thick_new, jnp.broadcast_to(cutoff[:, None], (R, LANES)), jnp.asarray(high), jnp.asarray(low))
+
+
+def remap_kernel(C, S, steps, begin, compact, with_thickness, others, patches, place_ref, weight_ref, *refs):
     thick_refs, refs = refs[:S], refs[S:]
     field_refs, refs = refs[:S], refs[S:]
-    other_refs, refs = refs[: (C - 1) * S], refs[(C - 1) * S :]
-    out_refs = refs[:C]
-    F, L, R, N = out_refs[0].shape
-    extra = field_refs[0].shape[0] - F
+    other_refs, refs = refs[:others], refs[others:]
+    patch_refs, refs = refs[:patches], refs[patches:]
+    out_refs = refs[len(refs) - len(steps) - with_thickness :]
+    F = field_refs[0].shape[0] - begin
+    _, L, R, N = field_refs[0].shape
     lev, sub = place_ref[0], place_ref[1]
     spot = [lax.rem(sub + S - t, S) for t in range(S)]
-    targets = [(lax.rem(lev + s, C) * S + sub) * L for s in range(C)]
-    below_sum = [jnp.float32(0.0) for _ in range(C)]
+    targets = [(lax.rem(lev + s, C) * S + sub) * L for s in steps]
     weight_sum = jnp.float32(0.0)
+    below_sum = [jnp.float32(0.0) for _ in steps]
     for k in range(C * S * L):
         w = weight_ref[k]
-        for s in range(C):
-            below_sum[s] = below_sum[s] + jnp.where(k < targets[s], w, 0.0)
+        below_sum = [b + jnp.where(k < first, w, 0.0) for b, first in zip(below_sum, targets)]
         weight_sum = weight_sum + w
     weights = [[weight_ref[first + i] for i in range(L)] for first in targets]
     sums = []
-    for s in range(C):
-        sums.append([below_sum[s]])
-        for w in weights[s]:
-            sums[s].append(sums[s][-1] + w)
-
-    def tile(rows, columns):
-        thick = [[thick_refs[t][0, m, rows, columns] for m in range(L)] for t in range(S)]
+    for below, row in zip(below_sum, weights):
+        sums.append([below])
+        for w in row:
+            sums[-1].append(sums[-1][-1] + w)
+
+    def tile(r, rows, columns):
+        at = slice(r, r + rows)
+
+        def other_sum(index):
+            value = other_refs[index][at, columns]
+            if patches:
+                row = r + lax.broadcasted_iota(jnp.int32, value.shape, 0)
+                value = jnp.where(row == 0, patch_refs[index][0:1, columns], value)
+                value = jnp.where(row == R - 1, patch_refs[index][1:2, columns], value)
+            return value
+
+        thick = [[thick_refs[t][0, m, at, columns] for m in range(L)] for t in range(S)]
         group = [functools.reduce(jnp.add, levels) for levels in thick]
         mass = functools.reduce(jnp.add, group)
         base = jnp.zeros_like(mass)
         for s in range(1, C):
-            other = other_refs[(s - 1) * S][rows, columns]
-            for t in range(1, S):
-                other = other + other_refs[(s - 1) * S + t][rows, columns]
+            other = functools.reduce(jnp.add, [other_sum((s - 1) * S + t) for t in range(S)])
             mass = mass + other
             base = base + jnp.where(lev >= s, other, 0.0)
         sources = []
@@ -362,10 +420,10 @@
                 sources.append((t, m, low, thick[t][m]))
                 low = low + thick[t][m]
         unit = mass / weight_sum
-        for s in range(C):
+        for index, s in enumerate(steps):
 
             def covered(i):
-                top = unit * sums[s][i]
+                top = unit * sums[index][i]
                 return [jnp.minimum(jnp.maximum(top - low, 0.0), h) for _, _, low, h in sources]
 
             below = covered(0)
@@ -373,80 +431,112 @@
                 upto = covered(i + 1)
                 part = [a - b for a, b in zip(upto, below)]
                 below = upto
-                target = unit * weights[s][i]
+                target = unit * weights[index][i]
                 scale = 1.0 / target
                 for f in range(F):
                     total = None
                     for (t, m, _, _), w in zip(sources, part):
-                        term = field_refs[t][extra + f, m, rows, columns] * w
+                        term = field_refs[t][begin + f, m, at, columns] * w
                         total = term if total is None else total + term
-                    out_refs[s][f, i, rows, columns] = total * scale
+                    total = total * scale
+                    if compact and s > 0:
+                        lower, upper = max(r, 1), min(r + rows, R - 1)
+                        start = (f * L + i) * (R - 2) - 1
+                        out_refs[index][start + lower : start + upper, columns] = total[lower - r : upper - r]
+                    else:
+                        out_refs[index][f, i, at, columns] = total
                 if with_thickness and s == 0:
-                    refs[C][i, rows, columns] = target
-
-    for r in range(0, R, 8):
+                    out_refs[len(steps)][i, at, columns] = target
+
+    rows = min(R, 8)
+    for r in range(0, R, rows):
 
         def body(c, carry):
-            tile(slice(r, r + 8), pl.ds(pl.multiple_of(c * LANES, LANES), LANES))
+            tile(r, rows, pl.ds(pl.multiple_of(c * LANES, LANES), LANES))
             return carry
 
         lax.fori_loop(0, N // LANES, body, 0)
 
 
-def remap_parts(counts, place, weights, thick, fields, others, with_thickness, extra):
+def remap_parts(
+    counts, place, weights, thick, fields, others, patches=(), steps=None, begin=0, compact=False, with_thickness=False, wait=()
+):
     C, S = counts
+    steps = tuple(range(C)) if steps is None else steps
     F, L, R, N = fields[0].shape
-    F = F - extra
-    shape = jax.ShapeDtypeStruct((F, L, R, N), jnp.float32)
-    out_shape = [shape] * C
+    F = F - begin
+    whole = jax.ShapeDtypeStruct((F, L, R, N), jnp.float32)
+    inner = jax.ShapeDtypeStruct((F * L * (R - 2), N), jnp.float32)
+    out_shape = [inner if compact and s > 0 else whole for s in steps]
     if with_thickness:
         out_shape = out_shape + [jax.ShapeDtypeStruct((L, R, N), jnp.float32)]
     return pl.pallas_call(
-        functools.partial(remap_kernel, C, S, with_thickness),
-        in_specs=[SMEM] * 2 + [VMEM] * (2 * S + len(others)),
+        functools.partial(
+            remap_kernel, C, S, steps, begin, compact, int(with_thickness), len(others), len(patches)
+        ),
+        in_specs=[SMEM] * 2 + [VMEM] * (2 * S + len(others) + len(patches)) + after(*wait),
         out_specs=[VMEM] * len(out_shape),
         out_shape=out_shape,
         compiler_params=params(),
-        cost_estimate=cost(C * S * L * L * R * N * (5 + 2 * F), 4 * R * N * L * (F + 1) * (S + C)),
+        cost_estimate=cost(1, 1),
         name="remap_parts",
-    )(place, weights, *thick, *fields, *others)
-
-
-def add_kernel(groups, outs_count, *refs):
-    outs = refs[len(refs) - outs_count :]
-    refs = refs[: len(refs) - outs_count]
+    )(place, weights, *thick, *fields, *others, *patches, *wait)
+
+
+def tracer_sum_kernel(chunks, sent, *refs):
+    out_ref = refs[-1]
+    T, L, R, N = out_ref.shape
+    inner, edge = refs[: chunks * (1 + sent)], refs[chunks * (1 + sent) : -1]
     at = 0
-    each = len(refs) // groups
-    for g in range(groups):
-        total = refs[g * each][...]
-        for i in range(1, each):
-            total = total + refs[g * each + i][...]
-        n = total.shape[0]
-        if outs_count == 1:
-            outs[0][at : at + n] = total
-        else:
-            for i in range(n):
-                outs[at + i][...] = total[i]
-        at += n
-
-
-def add_parts(groups, outs_count):
-    flat = [a for group in groups for a in group]
-    total = sum(group[0].shape[0] for group in groups)
-    L, R, N = flat[0].shape[1:]
-    if outs_count == 1:
-        out_shape = jax.ShapeDtypeStruct((total, L, R, N), jnp.float32)
-    else:
-        out_shape = [jax.ShapeDtypeStruct((L, R, N), jnp.float32)] * total
-    return pl.pallas_call(
-        functools.partial(add_kernel, len(groups), outs_count),
+    for chunk in range(chunks):
+        own, *arrived = inner[chunk * (1 + sent) : (chunk + 1) * (1 + sent)]
+        for f in range(own.shape[0]):
+            for i in range(L):
+                start = (f * L + i) * (R - 2)
+                total = own[f, i, 1 : R - 1]
+                for ref in arrived:
+                    total = total + ref[start : start + R - 2]
+                out_ref[at + f, i, 1 : R - 1] = total
+        at += own.shape[0]
+    for f in range(T):
+        for i in range(L):
+            total = functools.reduce(jnp.add, [ref[f, i] for ref in edge])
+            out_ref[f, i, 0:1] = total[0:1]
+            out_ref[f, i, R - 1 : R] = total[1:2]
+
+
+def tracer_sum(chunks, edge):
+    T = edge[0].shape[0]
+    _, L, R, N = chunks[0][0].shape
+    flat = [a for chunk in chunks for a in chunk] + list(edge)
+    return pl.pallas_call(
+        functools.partial(tracer_sum_kernel, len(chunks), len(edge) - 1),
         in_specs=[VMEM] * len(flat),
-        out_specs=VMEM if outs_count == 1 else [VMEM] * total,
-        out_shape=out_shape,
-        compiler_params=params(),
-        cost_estimate=cost(total * L * R * N, 4 * total * L * R * N * 3),
-        name="add_parts",
+        out_specs=VMEM,
+        out_shape=jax.ShapeDtypeStruct((T, L, R, N), jnp.float32),
+        compiler_params=params(),
+        cost_estimate=cost(1, 1),
+        name="tracer_sum",
     )(*flat)
+
+
+def wind_sum_kernel(parts, *refs):
+    u_ref, v_ref = refs[parts:]
+    u_ref[...] = functools.reduce(jnp.add, [ref[0] for ref in refs[:parts]])
+    v_ref[...] = functools.reduce(jnp.add, [ref[1] for ref in refs[:parts]])
+
+
+def wind_sum(parts):
+    shape = jax.ShapeDtypeStruct(parts[0].shape[1:], jnp.float32)
+    return pl.pallas_call(
+        functools.partial(wind_sum_kernel, len(parts)),
+        in_specs=[VMEM] * len(parts),
+        out_specs=[VMEM] * 2,
+        out_shape=[shape] * 2,
+        compiler_params=params(),
+        cost_estimate=cost(1, 1),
+        name="wind_sum",
+    )(*parts)
 
 
 def shifted(value, lev_count, sub_count, s, t):
@@ -469,33 +559,55 @@
     lat_rows = R * lat_count
     send = functools.partial(shifted, lev_count=C, sub_count=S)
 
-    last, leading = edge_rows(thickness, wind_u, wind_v, tracers)
+    T = tracers.shape[0]
     northward = [(i, i + 1) for i in range(lat_count - 1)]
-    up = lax.ppermute(last, "lat", northward)
-    down = lax.ppermute(leading, "lat", [(j, i) for i, j in northward])
-
+    southward = [(j, i) for i, j in northward]
     band = lax.axis_index("lat").astype(jnp.int32).reshape(1)
     table = jnp.asarray(geometry_table(lat_rows, R))
     place = jnp.stack([lax.axis_index("lev"), lax.axis_index("sub")]).astype(jnp.int32)
 
-    thick_new, wind, own_sum = thickness_step(band, table, lat_rows, thickness, wind_u, wind_v, up, down)
-    others = [send(own_sum, s=s, t=t) for s in range(1, C) for t in range(S)]
-    step = functools.partial(tracer_step, band, table, thickness, wind_u, wind_v, thick_new, up, down, tracers)
-    T = tracers.shape[0]
-    sources = [step(0, 1, True), step(1, T - 1, False), fourier_filter(wind, cutoff)]
-    gathered = [[own] + [send(own, s=0, t=t) for t in range(1, S)] for own in sources]
-    results = []
-    thickness_out = None
-    for index, fields in enumerate(gathered):
-        with_thickness = index == 2
-        extra = 1 if index == 0 else 0
-        out = remap_parts((C, S), place, level_weights, gathered[0], fields, others, with_thickness, extra)
-        if with_thickness:
-            thickness_out = out[C]
-        results.append([out[0]] + [send(out[s], s=s, t=0) for s in range(1, C)])
-    tracers_out = add_parts(results[:2], 1)
-    u_out, v_out = add_parts(results[2:], 2)
-    return thickness_out, u_out, v_out, tracers_out
+    def with_others_of_chip(own):
+        return [own] + [send(own, s=0, t=t) for t in range(1, S)]
+
+    def sums_of_other_chips(own):
+        return [send(own, s=s, t=t) for s in range(1, C) for t in range(S)]
+
+    def exchanged(parts):
+        return [parts[0]] + [send(parts[s], s=s, t=0) for s in range(1, C)]
+
+    remap = functools.partial(remap_parts, (C, S), place, level_weights)
+    step = functools.partial(tracer_step, band, table, thickness, wind_u, wind_v)
+
+    new_inner, sum_inner = first_step(band, table, thickness, wind_u, wind_v)
+    others = sums_of_other_chips(sum_inner)
+    one = step(new_inner, tracers, 0, 1, True, (), ())
+    one_group = with_others_of_chip(one)
+    rest = step(new_inner, tracers, 1, T - 1, False, (), (one,))
+    rest_group = with_others_of_chip(rest)
+    one_away = remap(
+        one_group, one_group, others, steps=tuple(range(1, C)), begin=1, compact=True, wait=(rest,)
+    )
+    one_arrived = [send(one_away[s - 1], s=s, t=0) for s in range(1, C)]
+    rest_parts = exchanged(remap(one_group, rest_group, others, compact=True, wait=(one_away[0],)))
+
+    last, leading = edge_rows(thickness, wind_u, wind_v, tracers, (rest_parts[0],))
+    up = lax.ppermute(last, "lat", northward)
+    down = lax.ppermute(leading, "lat", southward)
+    thick_new, wind, sum_edge = thickness_step(band, table, lat_rows, thickness, wind_u, wind_v, up, down)
+    others_edge = sums_of_other_chips(sum_edge)
+    winds = fourier_filter(wind, thick_new, cutoff)
+    winds_group = with_others_of_chip(winds)
+    edge_group = with_others_of_chip(step(thick_new, tracers, 0, T, True, (up, down), (winds,)))
+    edge_parts = exchanged(remap(edge_group, edge_group, others_edge, begin=1))
+    wind_out = remap(
+        winds_group, winds_group, others, others_edge, begin=1, with_thickness=True, wait=(edge_parts[0],)
+    )
+    wind_parts = exchanged(wind_out[:C])
+    (one_own,) = remap(one_group, one_group, others, steps=(0,), begin=1, wait=(wind_out[0],))
+
+    tracers_out = tracer_sum([[one_own] + one_arrived, rest_parts], edge_parts)
+    u_out, v_out = wind_sum(wind_parts)
+    return wind_out[C], u_out, v_out, tracers_out
 
 
 def solution(mesh):

time: 73 us -> 87.3 us (1.20)
  Pallas kernels: 16.7 us -> 22 us
  waiting for transfers between devices: 37.5 us -> 41.6 us
  starting transfers between devices: 13.3 us -> 17.2 us
    ppermute x1 -> x2, waiting for transfers between devices: 1.37 us -> 17.9 us  [shifted(): return lax.ppermute(value, ('lev', 'sub'), pairs)]
    ppermute x4 -> x6, waiting for transfers between devices: 33.8 us -> 21.4 us  [shifted(): lax.ppermute(value, 'lev', [(i, (i + s) % lev_count) for i in range(lev_c...]
    pallas_call x8 -> x12, Pallas kernels: 15.3 us -> 20.6 us  [the longest x5 10.4 us: remap_parts(): pl.pallas_call(functools.partial(remap_kernel, C, S, steps, begin, compac...]
    ppermute x1 -> x2, starting transfers between devices: 0.06 us -> 2.6 us  [shifted(): return lax.ppermute(value, ('lev', 'sub'), pairs)]
    ppermute x4 -> x6, starting transfers between devices: 5.63 us -> 7.39 us  [shifted(): lax.ppermute(value, 'lev', [(i, (i + s) % lev_count) for i in range(lev_c...]
    ppermute x1, starting transfers between devices: 5.56 us -> 4.55 us  [per_device(): up = lax.ppermute(last, 'lat', northward)]
    unnamed x26 -> x28, local copies, waits for them, and re-layouts: 4.18 us -> 5.01 us
  transfers between devices with their start and end apart: 10 -> 14, of which waited for: 5 -> 7; matrix products, arithmetic and copies ran while one was open for 0% -> 0% of each run, Pallas kernels for 16% -> 13%
where the time goes in v3:
time: 87.3 us; the launch traced here: 86.9 us
  waiting for transfers between devices  41.6 us (48%)
  Pallas kernels  22 us (25%)
  starting transfers between devices  17.2 us (20%)
  local copies, waits for them, and re-layouts  5.08 us (6%)
  between operations  0.89 us (1%)
    ppermute x6, waiting for transfers between devices, shifted(): lax.ppermute(value, 'lev', [(i, (i + s) % lev_count) for i in range(lev_c...  21.4 us
    ppermute x2, waiting for transfers between devices, shifted(): return lax.ppermute(value, ('lev', 'sub'), pairs)  17.9 us
    pallas_call x5, Pallas kernels, remap_parts(): pl.pallas_call(functools.partial(remap_kernel, C, S, steps, begin, compac...  10.4 us
    ppermute x6, starting transfers between devices, shifted(): lax.ppermute(value, 'lev', [(i, (i + s) % lev_count) for i in range(lev_c...  7.39 us
    unnamed x28, local copies, waits for them, and re-layouts  5.01 us
    ppermute x1, starting transfers between devices, per_device(): up = lax.ppermute(last, 'lat', northward)  4.55 us
    pallas_call x3, Pallas kernels, tracer_step(): pl.pallas_call(functools.partial(tracer_kernel, bool(halo)), grid=(L,), i...  4.18 us
    ppermute x2, starting transfers between devices, shifted(): return lax.ppermute(value, ('lev', 'sub'), pairs)  2.6 us
  transfers between devices with their start and end apart: 14, of which 7 were waited for; matrix products, arithmetic and copies ran while one was open for 0% of the time, Pallas kernels for 13%

profile of v3, /device:TPU:0, one launch (start us, length us, event | category | flops | bytes accessed | tf_op | source)
XLA Modules:
  0.0 86.9 jit_solution(3966629037965367853)
XLA Ops:
  0.6 2.5 %first_step.1 = (f32[4,16,1152]{2,1,0:T(8,128)S(1)}, f32[16,1152]{1,0:T(8,128)S(1)}) custom-call(s32[1]{0:T(128)} %bitcast.2.band_ref, f32[4,24,128]{2,1,0:T(8,128)} %constant.17.clone.table_ref, f32[4,16,1152]{2,1,0:T(8,128)} %thick_ref.9, f32[4,16,1152]{2,1,0:T(8,128)} %u_ref.9, f32[4,16,1152]{2,1,0:T(8,128)} %v_ref.9), custom_call_target="tpu_custom_call" | custom-call | flops 1 | bytes 1 | tf_op jit(solution)/shard_map/first_step/pallas_call | solution.py:129
  3.2 1.3 %copy-done = f32[4,4,16,1152]{3,2,1,0:T(8,128)S(1)} copy-done((f32[4,4,16,1152]{3,2,1,0:T(8,128)S(1)}, f32[4,4,16,1152]{3,2,1,0:T(8,128)}, u32[]{:S(2)}) %copy-start) | copy-done | bytes 1179672
  9.0 1.4 %tracer_step.4.refs_6_.refs_2_ = f32[3,4,16,1152]{3,2,1,0:T(8,128)S(1)} custom-call(s32[1]{0:T(128)} %bitcast.2.band_ref, f32[4,24,128]{2,1,0:T(8,128)S(1)} %copy-done.8, f32[4,16,1152]{2,1,0:T(8,128)S(1)} %copy-done.2, f32[4,16,1152]{2,1,0:T(8,128)S(1)} %copy-done.6, f32[4,16,1152]{2,1,0:T(8,128)S(1)} %copy-done.4, ...), custom_call_target="tpu_custom_call" | custom-call | flops 1 | bytes 1 | tf_op jit(solution)/shard_map/tracer_step/pallas_call | solution.py:249
  11.0 2.6 %collective-permute-start.3 = (f32[16,1152]{1,0:T(8,128)S(1)}, f32[16,1152]{1,0:T(8,128)S(1)}, u32[]{:S(2)}, u32[]{:S(2)}) collective-permute-start(f32[16,1152]{1,0:T(8,128)S(1)} %get-tuple-element.21), channel_id=1, source_target_pairs={{0,3},{1,2},{2,1},{3,0},{4,7},{5,6},{6,5},{7,4},{8,11},{9,10},{10,... | collective-permute-start | bytes 221192 | tf_op jit(solution)/shard_map/ppermute | solution.py:552
  14.1 2.2 %collective-permute-done.3.refs_5_ = f32[16,1152]{1,0:T(8,128)S(1)} collective-permute-done((f32[16,1152]{1,0:T(8,128)S(1)}, f32[16,1152]{1,0:T(8,128)S(1)}, u32[]{:S(2)}, u32[]{:S(2)}) %collective-permute-start.3) | collective-permute-done | bytes 73760 | tf_op jit(solution)/shard_map/ppermute | solution.py:552
  16.3 2.0 %collective-permute-done.2.refs_4_ = f32[16,1152]{1,0:T(8,128)S(1)} collective-permute-done((f32[16,1152]{1,0:T(8,128)S(1)}, f32[16,1152]{1,0:T(8,128)S(1)}, u32[]{:S(2)}, u32[]{:S(2)}) %collective-permute-start.2) | collective-permute-done | bytes 73760 | tf_op jit(solution)/shard_map/ppermute | solution.py:544
  18.3 1.4 %remap_parts.5.refs_6_ = f32[56,1152]{1,0:T(8,128)S(1)} custom-call(s32[2]{0:T(128)S(1)} %pad_add_fusion.place_ref, f32[16]{0:T(128)S(1)} %copy-done.12, f32[2,4,16,1152]{3,2,1,0:T(8,128)S(1)} %tracer_step.3.refs_0_.refs_2_, f32[2,4,16,1152]{3,2,1,0:T(8,128)S(1)} %collective-permute-done.refs_1_.refs_3_, f32[2,4,16,1152]{3,2,1,0:T(8,128)S(1)} %tracer_step.3.refs_0_.refs_2_, ...), custom_call_target="tpu_custom_call" | custom-call | flops 1 | bytes 1 | tf_op jit(solution)/shard_map/remap_parts/pallas_call | solution.py:473
  19.8 2.7 %remap_parts.6 = (f32[3,4,16,1152]{3,2,1,0:T(8,128)S(1)}, f32[168,1152]{1,0:T(8,128)S(1)}) custom-call(s32[2]{0:T(128)S(1)} %pad_add_fusion.place_ref, f32[16]{0:T(128)S(1)} %copy-done.12, f32[2,4,16,1152]{3,2,1,0:T(8,128)S(1)} %tracer_step.3.refs_0_.refs_2_, f32[2,4,16,1152]{3,2,1,0:T(8,128)S(1)} %collective-permute-done.refs_1_.refs_3_, ...), custom_call_target="tpu_custom_call" | custom-call | flops 1 | bytes 1 | tf_op jit(solution)/shard_map/remap_parts/pallas_call | solution.py:473
  22.8 1.4 %collective-permute-start.5 = (f32[8,4,1,1152]{3,2,1,0:T(1,128)S(1)}, f32[8,4,1,1152]{3,2,1,0:T(1,128)S(1)}, u32[]{:S(2)}, u32[]{:S(2)}) collective-permute-start(f32[8,4,1,1152]{3,2,1,0:T(1,128)S(1)} %get-tuple-element.24), channel_id=1, source_target_pairs={{4,0},{8,4},{12,8},{5,1},{9,5},{13,9},{6,2},{10,6},{14,10},{7,3},{... | collective-permute-start | bytes 442376 | tf_op jit(solution)/shard_map/ppermute | solution.py:595
  24.2 4.6 %collective-permute-start.4 = (f32[6,4,1,1152]{3,2,1,0:T(1,128)S(1)}, f32[6,4,1,1152]{3,2,1,0:T(1,128)S(1)}, u32[]{:S(2)}, u32[]{:S(2)}) collective-permute-start(f32[6,4,1,1152]{3,2,1,0:T(1,128)S(1)} %get-tuple-element.23), channel_id=1, source_target_pairs={{0,4},{4,8},{8,12},{1,5},{5,9},{9,13},{2,6},{6,10},{10,14},{3,7},{... | collective-permute-start | bytes 331784 | tf_op jit(solution)/shard_map/ppermute | solution.py:594
  28.8 2.3 %collective-permute-done.4.up_ref.refs_0_ = f32[6,4,1,1152]{3,2,1,0:T(1,128)S(1)} collective-permute-done((f32[6,4,1,1152]{3,2,1,0:T(1,128)S(1)}, f32[6,4,1,1152]{3,2,1,0:T(1,128)S(1)}, u32[]{:S(2)}, u32[]{:S(2)}) %collective-permute-start.4) | collective-permute-done | bytes 110624 | tf_op jit(solution)/shard_map/ppermute | solution.py:594
  32.4 1.2 %fourier_filter.1.refs_2_.refs_0_ = f32[3,4,16,1152]{3,2,1,0:T(8,128)S(1)} custom-call(f32[2,4,16,1152]{3,2,1,0:T(8,128)S(1)} %get-tuple-element.25.wind_ref, f32[4,16,1152]{2,1,0:T(8,128)S(1)} %get-tuple-element.26.new_ref, s32[16,128]{1,0:T(8,128)S(1)} %broadcast_in_dim.2.cutoff_ref, bf16[5,256,256]{2,1,0:T(8,128)(2,1)S(1)} %copy-done.11, ...), custom_call_target="tpu_custom_call" | custom-call | flops 1 | bytes 1 | tf_op jit(solution)/shard_map/fourier_filter/pallas_call | solution.py:359
  33.7 1.9 %tracer_step.5.refs_0_.refs_2_ = f32[5,4,2,1152]{3,2,1,0:T(2,128)S(1)} custom-call(s32[1]{0:T(128)} %bitcast.2.band_ref, f32[4,24,128]{2,1,0:T(8,128)S(1)} %copy-done.9, f32[4,16,1152]{2,1,0:T(8,128)S(1)} %copy-done.3, f32[4,16,1152]{2,1,0:T(8,128)S(1)} %copy-done.7, f32[4,16,1152]{2,1,0:T(8,128)S(1)} %copy-done.5, ...), custom_call_target="tpu_custom_call" | custom-call | flops 1 | bytes 1 | tf_op jit(solution)/shard_map/tracer_step/pallas_call | solution.py:249
  36.2 1.8 %collective-permute-start.12 = (f32[168,1152]{1,0:T(8,128)S(1)}, f32[168,1152]{1,0:T(8,128)S(1)}, u32[]{:S(2)}, u32[]{:S(2)}) collective-permute-start(f32[168,1152]{1,0:T(8,128)S(1)} %get-tuple-element.34), channel_id=1, source_target_pairs={{0,2},{2,0},{1,3},{3,1},{4,6},{6,4},{5,7},{7,5},{8,10},{10,8},{9,1... | collective-permute-start | bytes 2322440 | tf_op jit(solution)/shard_map/ppermute | solution.py:544
  38.0 1.4 %collective-permute-start.7 = (f32[2,1152]{1,0:T(2,128)S(1)}, f32[2,1152]{1,0:T(2,128)S(1)}, u32[]{:S(2)}, u32[]{:S(2)}) collective-permute-start(f32[2,1152]{1,0:T(2,128)S(1)} %get-tuple-element.27), channel_id=1, source_target_pairs={{0,2},{2,0},{1,3},{3,1},{4,6},{6,4},{5,7},{7,5},{8,10},{10,8},{9,1... | collective-permute-start | bytes 27656 | tf_op jit(solution)/shard_map/ppermute | solution.py:544
  39.4 15.6 %collective-permute-done.8.refs_5_.refs_7_ = f32[2,1152]{1,0:T(2,128)S(1)} collective-permute-done((f32[2,1152]{1,0:T(2,128)S(1)}, f32[2,1152]{1,0:T(2,128)S(1)}, u32[]{:S(2)}, u32[]{:S(2)}) %collective-permute-start.8) | collective-permute-done | bytes 9248 | tf_op jit(solution)/shard_map/ppermute | solution.py:552
  55.9 1.8 %remap_parts.7 = (f32[4,4,2,1152]{3,2,1,0:T(2,128)S(1)}, f32[4,4,2,1152]{3,2,1,0:T(2,128)S(1)}) custom-call(s32[2]{0:T(128)S(1)} %pad_add_fusion.place_ref, f32[16]{0:T(128)S(1)} %copy-done.12, f32[5,4,2,1152]{3,2,1,0:T(2,128)S(1)} %tracer_step.5.refs_0_.refs_2_, f32[5,4,2,1152]{3,2,1,0:T(2,128)S(1)} %collective-permute-done.9.refs_1_.refs_3_, ...), custom_call_target="tpu_custom_call" | custom-call | flops 1 | bytes 1 | tf_op jit(solution)/shard_map/remap_parts/pallas_call | solution.py:473
  57.7 3.1 %remap_parts.8 = (f32[2,4,16,1152]{3,2,1,0:T(8,128)S(1)}, f32[2,4,16,1152]{3,2,1,0:T(8,128)S(1)}, f32[4,16,1152]{2,1,0:T(8,128)}) custom-call(s32[2]{0:T(128)S(1)} %pad_add_fusion.place_ref, f32[16]{0:T(128)S(1)} %copy-done.12, f32[3,4,16,1152]{3,2,1,0:T(8,128)S(1)} %fourier_filter.1.refs_2_.refs_0_, ...), custom_call_target="tpu_custom_call" | custom-call | flops 1 | bytes 1 | tf_op jit(solution)/shard_map/remap_parts/pallas_call | solution.py:473
  60.8 1.7 %collective-permute-start.10 = (f32[2,4,16,1152]{3,2,1,0:T(8,128)S(1)}, f32[2,4,16,1152]{3,2,1,0:T(8,128)S(1)}, u32[]{:S(2)}, u32[]{:S(2)}) collective-permute-start(f32[2,4,16,1152]{3,2,1,0:T(8,128)S(1)} %get-tuple-element.31), channel_id=1, source_target_pairs={{0,2},{2,0},{1,3},{3,1},{4,6},{6,4},{5,7},{7,5},{8,10},{10,8},{9,1... | collective-permute-start | bytes 1769480 | tf_op jit(solution)/shard_map/ppermute | solution.py:544
  62.9 1.7 %collective-permute-start.13 = (f32[4,4,2,1152]{3,2,1,0:T(2,128)S(1)}, f32[4,4,2,1152]{3,2,1,0:T(2,128)S(1)}, u32[]{:S(2)}, u32[]{:S(2)}) collective-permute-start(f32[4,4,2,1152]{3,2,1,0:T(2,128)S(1)} %get-tuple-element.35), channel_id=1, source_target_pairs={{0,2},{2,0},{1,3},{3,1},{4,6},{6,4},{5,7},{7,5},{8,10},{10,8},{9,1... | collective-permute-start | bytes 442376 | tf_op jit(solution)/shard_map/ppermute | solution.py:544
  64.6 1.4 %remap_parts.9.refs_0_ = f32[1,4,16,1152]{3,2,1,0:T(8,128)S(1)} custom-call(s32[2]{0:T(128)S(1)} %pad_add_fusion.place_ref, f32[16]{0:T(128)S(1)} %copy-done.12, f32[2,4,16,1152]{3,2,1,0:T(8,128)S(1)} %tracer_step.3.refs_0_.refs_2_, f32[2,4,16,1152]{3,2,1,0:T(8,128)S(1)} %collective-permute-done.refs_1_.refs_3_, ...), custom_call_target="tpu_custom_call" | custom-call | flops 1 | bytes 1 | tf_op jit(solution)/shard_map/remap_parts/pallas_call | solution.py:473
  66.0 16.5 %collective-permute-done.11.refs_1_ = f32[56,1152]{1,0:T(8,128)S(1)} collective-permute-done((f32[56,1152]{1,0:T(8,128)S(1)}, f32[56,1152]{1,0:T(8,128)S(1)}, u32[]{:S(2)}, u32[]{:S(2)}) %collective-permute-start.11) | collective-permute-done | bytes 258080 | tf_op jit(solution)/shard_map/ppermute | solution.py:544
  82.6 2.1 %collective-permute-done.13.refs_5_ = f32[4,4,2,1152]{3,2,1,0:T(2,128)S(1)} collective-permute-done((f32[4,4,2,1152]{3,2,1,0:T(2,128)S(1)}, f32[4,4,2,1152]{3,2,1,0:T(2,128)S(1)}, u32[]{:S(2)}, u32[]{:S(2)}) %collective-permute-start.13) | collective-permute-done | bytes 147488 | tf_op jit(solution)/shard_map/ppermute | solution.py:544
  84.7 1.3 %tracer_sum.1 = f32[4,4,16,1152]{3,2,1,0:T(8,128)} custom-call(f32[1,4,16,1152]{3,2,1,0:T(8,128)S(1)} %remap_parts.9.refs_0_, f32[56,1152]{1,0:T(8,128)S(1)} %collective-permute-done.11.refs_1_, f32[3,4,16,1152]{3,2,1,0:T(8,128)S(1)} %get-tuple-element.22.refs_0_.refs_2_, f32[168,1152]{1,0:T(8,128)S(1)} %collective-permute-done.12.refs_3_, ...), custom_call_target="tpu_custom_call" | custom-call | flops 1 | bytes 1 | tf_op jit(solution)/shard_map/tracer_sum/pallas_call | solution.py:512
  (48 shorter events, 9.7 us)
Async XLA Ops:
  3.2 1.3 %copy-start = (f32[4,4,16,1152]{3,2,1,0:T(8,128)S(1)}, f32[4,4,16,1152]{3,2,1,0:T(8,128)}, u32[]{:S(2)}) copy-start(f32[4,4,16,1152]{3,2,1,0:T(8,128)} %tracer_ref.5) | copy-start | bytes 3538948
  9.0 9.3 %copy-start.12 = (f32[16]{0:T(128)S(1)}, f32[16]{0:T(128)}, u32[]{:S(2)}) copy-start(f32[16]{0:T(128)} %weight_ref.9) | copy-start | bytes 196
  10.4 9.3 %collective-permute-start.1 = (f32[3,4,16,1152]{3,2,1,0:T(8,128)S(1)}, f32[3,4,16,1152]{3,2,1,0:T(8,128)S(1)}, u32[]{:S(2)}, u32[]{:S(2)}) collective-permute-start(f32[3,4,16,1152]{3,2,1,0:T(8,128)S(1)} %tracer_step.4.refs_6_.refs_2_), channel_id=1, source_target_pairs={{0,1},{1,0},{2,3},{3,2},{4,5},{5,4},{6,7},{7,6},{8,9},{9,8},{10,11... | collective-permute-start | bytes 2654216 | tf_op jit(solution)/shard_map/ppermute | solution.py:546
  11.0 7.3 %collective-permute-start = (f32[2,4,16,1152]{3,2,1,0:T(8,128)S(1)}, f32[2,4,16,1152]{3,2,1,0:T(8,128)S(1)}, u32[]{:S(2)}, u32[]{:S(2)}) collective-permute-start(f32[2,4,16,1152]{3,2,1,0:T(8,128)S(1)} %tracer_step.3.refs_0_.refs_2_), channel_id=1, source_target_pairs={{0,1},{1,0},{2,3},{3,2},{4,5},{5,4},{6,7},{7,6},{8,9},{9,8},{10,11... | collective-permute-start | bytes 1769480 | tf_op jit(solution)/shard_map/ppermute | solution.py:546
  11.0 5.3 %collective-permute-start.3 = (f32[16,1152]{1,0:T(8,128)S(1)}, f32[16,1152]{1,0:T(8,128)S(1)}, u32[]{:S(2)}, u32[]{:S(2)}) collective-permute-start(f32[16,1152]{1,0:T(8,128)S(1)} %get-tuple-element.21), channel_id=1, source_target_pairs={{0,3},{1,2},{2,1},{3,0},{4,7},{5,6},{6,5},{7,4},{8,11},{9,10},{10,... | collective-permute-start | bytes 221192 | tf_op jit(solution)/shard_map/ppermute | solution.py:552
  13.6 4.6 %collective-permute-start.2 = (f32[16,1152]{1,0:T(8,128)S(1)}, f32[16,1152]{1,0:T(8,128)S(1)}, u32[]{:S(2)}, u32[]{:S(2)}) collective-permute-start(f32[16,1152]{1,0:T(8,128)S(1)} %get-tuple-element.21), channel_id=1, source_target_pairs={{0,2},{2,0},{1,3},{3,1},{4,6},{6,4},{5,7},{7,5},{8,10},{10,8},{9,1... | collective-permute-start | bytes 221192 | tf_op jit(solution)/shard_map/ppermute | solution.py:544
  19.7 2.8 %copy-start.1 = (f32[4,4,16,1152]{3,2,1,0:T(8,128)S(1)}, f32[4,4,16,1152]{3,2,1,0:T(8,128)}, u32[]{:S(2)}) copy-start(f32[4,4,16,1152]{3,2,1,0:T(8,128)} %tracer_ref.5) | copy-start | bytes 3538948
  19.7 2.8 %copy-start.3 = (f32[4,16,1152]{2,1,0:T(8,128)S(1)}, f32[4,16,1152]{2,1,0:T(8,128)}, u32[]{:S(2)}) copy-start(f32[4,16,1152]{2,1,0:T(8,128)} %thick_ref.9) | copy-start | bytes 884740
  19.7 2.8 %copy-start.5 = (f32[4,16,1152]{2,1,0:T(8,128)S(1)}, f32[4,16,1152]{2,1,0:T(8,128)}, u32[]{:S(2)}) copy-start(f32[4,16,1152]{2,1,0:T(8,128)} %v_ref.9) | copy-start | bytes 884740
  19.8 2.8 %copy-start.7 = (f32[4,16,1152]{2,1,0:T(8,128)S(1)}, f32[4,16,1152]{2,1,0:T(8,128)}, u32[]{:S(2)}) copy-start(f32[4,16,1152]{2,1,0:T(8,128)} %u_ref.9) | copy-start | bytes 884740
  22.5 8.6 %copy-start.9 = (f32[4,24,128]{2,1,0:T(8,128)S(1)}, f32[4,24,128]{2,1,0:T(8,128)}, u32[]{:S(2)}) copy-start(f32[4,24,128]{2,1,0:T(8,128)} %constant.17.clone.table_ref) | copy-start | bytes 147460
  22.5 9.8 %copy-start.11 = (bf16[5,256,256]{2,1,0:T(8,128)(2,1)S(1)}, bf16[5,256,256]{2,1,0:T(8,128)(2,1)}, u32[]{:S(2)}) copy-start(bf16[5,256,256]{2,1,0:T(8,128)(2,1)} %constant.18.clone.high_ref) | copy-start | bytes 1966084
  22.8 9.5 %copy-start.13 = (s32[16]{0:T(128)S(1)}, s32[16]{0:T(128)}, u32[]{:S(2)}) copy-start(s32[16]{0:T(128)} %param.14) | copy-start | bytes 196
  22.8 9.6 %copy-start.10 = (bf16[5,256,256]{2,1,0:T(8,128)(2,1)S(1)}, bf16[5,256,256]{2,1,0:T(8,128)(2,1)}, u32[]{:S(2)}) copy-start(bf16[5,256,256]{2,1,0:T(8,128)(2,1)} %constant.19.clone.low_ref) | copy-start | bytes 1966084
  22.8 8.3 %collective-permute-start.5 = (f32[8,4,1,1152]{3,2,1,0:T(1,128)S(1)}, f32[8,4,1,1152]{3,2,1,0:T(1,128)S(1)}, u32[]{:S(2)}, u32[]{:S(2)}) collective-permute-start(f32[8,4,1,1152]{3,2,1,0:T(1,128)S(1)} %get-tuple-element.24), channel_id=1, source_target_pairs={{4,0},{8,4},{12,8},{5,1},{9,5},{13,9},{6,2},{10,6},{14,10},{7,3},{... | collective-permute-start | bytes 442376 | tf_op jit(solution)/shard_map/ppermute | solution.py:595
  24.2 6.9 %collective-permute-start.4 = (f32[6,4,1,1152]{3,2,1,0:T(1,128)S(1)}, f32[6,4,1,1152]{3,2,1,0:T(1,128)S(1)}, u32[]{:S(2)}, u32[]{:S(2)}) collective-permute-start(f32[6,4,1,1152]{3,2,1,0:T(1,128)S(1)} %get-tuple-element.23), channel_id=1, source_target_pairs={{0,4},{4,8},{8,12},{1,5},{5,9},{9,13},{2,6},{6,10},{10,14},{3,7},{... | collective-permute-start | bytes 331784 | tf_op jit(solution)/shard_map/ppermute | solution.py:594
  33.6 24.1 %collective-permute-start.6 = (f32[3,4,16,1152]{3,2,1,0:T(8,128)S(1)}, f32[3,4,16,1152]{3,2,1,0:T(8,128)S(1)}, u32[]{:S(2)}, u32[]{:S(2)}) collective-permute-start(f32[3,4,16,1152]{3,2,1,0:T(8,128)S(1)} %fourier_filter.1.refs_2_.refs_0_), channel_id=1, source_target_pairs={{0,1},{1,0},{2,3},{3,2},{4,5},{5,4},{6,7},{7,6},{8,9},{9,8},{10,11... | collective-permute-start | bytes 2654216 | tf_op jit(solution)/shard_map/ppermute | solution.py:546
  35.6 20.3 %collective-permute-start.9 = (f32[5,4,2,1152]{3,2,1,0:T(2,128)S(1)}, f32[5,4,2,1152]{3,2,1,0:T(2,128)S(1)}, u32[]{:S(2)}, u32[]{:S(2)}) collective-permute-start(f32[5,4,2,1152]{3,2,1,0:T(2,128)S(1)} %tracer_step.5.refs_0_.refs_2_), channel_id=1, source_target_pairs={{0,1},{1,0},{2,3},{3,2},{4,5},{5,4},{6,7},{7,6},{8,9},{9,8},{10,11... | collective-permute-start | bytes 552968 | tf_op jit(solution)/shard_map/ppermute | solution.py:546
  36.2 48.5 %collective-permute-start.12 = (f32[168,1152]{1,0:T(8,128)S(1)}, f32[168,1152]{1,0:T(8,128)S(1)}, u32[]{:S(2)}, u32[]{:S(2)}) collective-permute-start(f32[168,1152]{1,0:T(8,128)S(1)} %get-tuple-element.34), channel_id=1, source_target_pairs={{0,2},{2,0},{1,3},{3,1},{4,6},{6,4},{5,7},{7,5},{8,10},{10,8},{9,1... | collective-permute-start | bytes 2322440 | tf_op jit(solution)/shard_map/ppermute | solution.py:544
  38.0 17.1 %collective-permute-start.8 = (f32[2,1152]{1,0:T(2,128)S(1)}, f32[2,1152]{1,0:T(2,128)S(1)}, u32[]{:S(2)}, u32[]{:S(2)}) collective-permute-start(f32[2,1152]{1,0:T(2,128)S(1)} %get-tuple-element.27), channel_id=1, source_target_pairs={{0,3},{1,2},{2,1},{3,0},{4,7},{5,6},{6,5},{7,4},{8,11},{9,10},{10,... | collective-permute-start | bytes 27656 | tf_op jit(solution)/shard_map/ppermute | solution.py:552
  38.0 17.9 %collective-permute-start.7 = (f32[2,1152]{1,0:T(2,128)S(1)}, f32[2,1152]{1,0:T(2,128)S(1)}, u32[]{:S(2)}, u32[]{:S(2)}) collective-permute-start(f32[2,1152]{1,0:T(2,128)S(1)} %get-tuple-element.27), channel_id=1, source_target_pairs={{0,2},{2,0},{1,3},{3,1},{4,6},{6,4},{5,7},{7,5},{8,10},{10,8},{9,1... | collective-permute-start | bytes 27656 | tf_op jit(solution)/shard_map/ppermute | solution.py:544
  60.8 25.1 %collective-permute-start.10 = (f32[2,4,16,1152]{3,2,1,0:T(8,128)S(1)}, f32[2,4,16,1152]{3,2,1,0:T(8,128)S(1)}, u32[]{:S(2)}, u32[]{:S(2)}) collective-permute-start(f32[2,4,16,1152]{3,2,1,0:T(8,128)S(1)} %get-tuple-element.31), channel_id=1, source_target_pairs={{0,2},{2,0},{1,3},{3,1},{4,6},{6,4},{5,7},{7,5},{8,10},{10,8},{9,1... | collective-permute-start | bytes 1769480 | tf_op jit(solution)/shard_map/ppermute | solution.py:544
  62.6 20.0 %collective-permute-start.11 = (f32[56,1152]{1,0:T(8,128)S(1)}, f32[56,1152]{1,0:T(8,128)S(1)}, u32[]{:S(2)}, u32[]{:S(2)}) collective-permute-start(f32[56,1152]{1,0:T(8,128)S(1)} %remap_parts.5.refs_6_), channel_id=1, source_target_pairs={{0,2},{2,0},{1,3},{3,1},{4,6},{6,4},{5,7},{7,5},{8,10},{10,8},{9,1... | collective-permute-start | bytes 774152 | tf_op jit(solution)/shard_map/ppermute | solution.py:544
  62.9 21.8 %collective-permute-start.13 = (f32[4,4,2,1152]{3,2,1,0:T(2,128)S(1)}, f32[4,4,2,1152]{3,2,1,0:T(2,128)S(1)}, u32[]{:S(2)}, u32[]{:S(2)}) collective-permute-start(f32[4,4,2,1152]{3,2,1,0:T(2,128)S(1)} %get-tuple-element.35), channel_id=1, source_target_pairs={{0,2},{2,0},{1,3},{3,1},{4,6},{6,4},{5,7},{7,5},{8,10},{10,8},{9,1... | collective-permute-start | bytes 442376 | tf_op jit(solution)/shard_map/ppermute | solution.py:544
  (4 other events, 3.7 us)

commit v4 on v0

v4 whole, which is shorter than its diff:
```python
import functools

import jax
import jax.numpy as jnp
import ml_dtypes
import numpy as np
from jax import lax
from jax.experimental import pallas as pl
from jax.experimental.pallas import tpu as pltpu
from jax.sharding import PartitionSpec as P

LANES = 128
VMEM = pl.BlockSpec(memory_space=pltpu.VMEM)
SMEM = pl.BlockSpec(memory_space=pltpu.SMEM)


def params():
    return pltpu.CompilerParams(vmem_limit_bytes=48 * 1024 * 1024)


def cost(flops, bytes_accessed):
    return pl.CostEstimate(flops=int(flops), bytes_accessed=int(bytes_accessed), transcendentals=0)


def after(arrays):
    return [pl.BlockSpec(memory_space=pl.ANY)] * len(arrays)


def geometry_table(lat_rows, band_rows):
    bands = lat_rows // band_rows
    table = np.zeros((bands, band_rows + 8, LANES), np.float32)
    for band in range(bands):
        for j in range(band_rows + 1):
            row = band * band_rows + j
            south = np.sin(row * np.pi / lat_rows) if 0 < row < lat_rows else 0.0
            north = np.sin((row + 1) * np.pi / lat_rows) if row + 1 < lat_rows else 0.0
            table[band, j, 0] = south
            table[band, j, 1] = north
            table[band, j, 2] = 1.0 / np.sin((row + 0.5) * np.pi / lat_rows)
    return table


def east_of(value):
    return pltpu.roll(value, value.shape[1] - 1, 1)


def west_of(value):
    return pltpu.roll(value, 1, 1)


def row_ids(shape):
    return lax.broadcasted_iota(jnp.int32, shape, 0)


def north_of(value, beyond):
    rows = value.shape[0]
    return jnp.where(row_ids(value.shape) == rows - 1, beyond, pltpu.roll(value, rows - 1, 0))


def south_of(value, beyond):
    return jnp.where(row_ids(value.shape) == 0, beyond, pltpu.roll(value, 1, 0))


def fluxes(geo, thick, u, v, thick_s, v_s, thick_n):
    rows = thick.shape[0]
    east = u * jnp.where(u > 0, thick, east_of(thick))
    north = v * jnp.where(v > 0, thick, north_of(thick, thick_n)) * geo[0:rows, 1:2]
    below = v_s * jnp.where(v_s > 0, thick_s, thick[0:1]) * geo[0:1, 0:1]
    return east, north, below


def tracer_change(q, q_s, q_n, thick, u, v, v_s, east, north, below, inverse):
    t_east = east * jnp.where(u > 0, q, east_of(q))
    t_north = north * jnp.where(v > 0, q, north_of(q, q_n))
    t_below = below * jnp.where(v_s > 0, q_s, q[0:1])
    change = thick * q - (t_east - west_of(t_east))
    return change - (t_north - south_of(t_north, t_below)) * inverse


def inner_kernel(band_ref, table_ref, thick_ref, u_ref, v_ref, tracer_ref, out_ref, sum_ref, last_ref, leading_ref):
    rows, width = thick_ref.shape[1:]
    geo = table_ref[band_ref[0]]
    thick, u, v = thick_ref[0], u_ref[0], v_ref[0]
    nothing = jnp.zeros((1, width), jnp.float32)
    east, north, below = fluxes(geo, thick, u, v, nothing, nothing, nothing)
    inverse = geo[0:rows, 2:3]
    new = thick - (east - west_of(east)) - (north - south_of(north, below)) * inverse
    out_ref[0, 0] = new
    last_ref[0, 0] = thick[rows - 1 : rows]
    last_ref[1, 0] = v[rows - 1 : rows]
    leading_ref[0, 0] = thick[0:1]
    leading_ref[1, 0] = thick[1:2]
    leading_ref[2, 0] = u[0:1]
    leading_ref[3, 0] = v[0:1]

    @pl.when(pl.program_id(0) == 0)
    def _():
        sum_ref[...] = new

    @pl.when(pl.program_id(0) > 0)
    def _():
        sum_ref[...] += new

    scale = 1.0 / new
    for c in range(tracer_ref.shape[0]):
        q = tracer_ref[c, 0]
        last_ref[2 + c, 0] = q[rows - 1 : rows]
        leading_ref[4 + c, 0] = q[0:1]
        change = tracer_change(q, nothing, nothing, thick, u, v, nothing, east, north, below, inverse)
        out_ref[1 + c, 0] = change * scale


def inner_step(band, table, thickness, wind_u, wind_v, tracers):
    L, R, N = thickness.shape
    T = tracers.shape[0]
    level = pl.BlockSpec((1, R, N), lambda k: (k, 0, 0))
    some = lambda n, rows: pl.BlockSpec((n, 1, rows, N), lambda k: (0, k, 0, 0))
    in_hbm = lambda x: pltpu.with_memory_space_constraint(x, pltpu.HBM)
    return pl.pallas_call(
        inner_kernel,
        grid=(L,),
        in_specs=[SMEM, pl.BlockSpec(table.shape, lambda k: (0, 0, 0)), level, level, level, some(T, R)],
        out_specs=[some(1 + T, R), pl.BlockSpec((R, N), lambda k: (0, 0)), some(2 + T, 1), some(4 + T, 1)],
        out_shape=[
            jax.ShapeDtypeStruct((1 + T, L, R, N), jnp.float32),
            jax.ShapeDtypeStruct((R, N), jnp.float32),
            jax.ShapeDtypeStruct((2 + T, L, 1, N), jnp.float32),
            jax.ShapeDtypeStruct((4 + T, L, 1, N), jnp.float32),
        ],
        compiler_params=params(),
        cost_estimate=cost(130 * L * R * N, 4 * L * R * N * (8 + 2 * T)),
        name="inner_step",
    )(band, in_hbm(table), in_hbm(thickness), in_hbm(wind_u), in_hbm(wind_v), in_hbm(tracers))


def filter_tables(N):
    A = N // LANES
    b = np.arange(LANES)[:, None]
    p = np.arange(LANES)[None, :]
    tables = []
    for q in range(A // 2 + 1):
        angle = 2.0 * np.pi * ((b * (A * p + q)) % N) / N
        c, s = np.cos(angle), np.sin(angle)
        tables.append(np.block([[c, -s], [s, c]]))
    table = np.stack(tables)
    high = table.astype(np.float32).astype(ml_dtypes.bfloat16)
    low = (table - high.astype(np.float64)).astype(np.float32).astype(ml_dtypes.bfloat16)
    return high, low


def split(value):
    high = value.astype(jnp.bfloat16)
    return high, (value - high.astype(jnp.float32)).astype(jnp.bfloat16)


def product(value, high, low, transposed):
    dims = (((1,), (1 if transposed else 0,)), ((), ()))
    dot = lambda x, y: lax.dot_general(x, y, dims, preferred_element_type=jnp.float32)
    v_high, v_low = split(value)
    return dot(v_high, high) + (dot(v_high, low) + dot(v_low, high))


def filter_rows(x, cutoff, high_ref, low_ref):
    A = len(x)
    N = A * LANES
    half = A // 2
    even = [x[a] + x[A - a] for a in range(1, half + 1)]
    odd = [x[a] - x[A - a] for a in range(1, half + 1)]
    angle = lambda q, a: 2.0 * np.pi * ((q * a) % A) / A
    p = lax.broadcasted_iota(jnp.int32, cutoff.shape, 1)
    real, imag = [], []
    for q in range(half + 1):
        re = x[0]
        for a in range(1, half + 1):
            re = re + (even[a - 1] if q == 0 else float(np.cos(angle(q, a))) * even[a - 1])
        if q == 0:
            high, low = high_ref[0, 0:LANES], low_ref[0, 0:LANES]
            spectrum = product(re, high, low, False)
        else:
            high, low = high_ref[q], low_ref[q]
            im = -float(np.sin(angle(q, 1))) * odd[0]
            for a in range(2, half + 1):
                im = im - float(np.sin(angle(q, a))) * odd[a - 1]
            spectrum = product(jnp.concatenate([re, im], axis=1), high, low, False)
        mode = A * p + q
        factor = 1.0 / N if q == 0 else 2.0 / N
        kept = jnp.where(jnp.minimum(mode, N - mode) <= cutoff, factor, 0.0)
        back = product(spectrum * jnp.concatenate([kept, kept], axis=1), high, low, True)
        real.append(back[:, :LANES])
        imag.append(back[:, LANES:])
    out = [None] * A
    out[0] = functools.reduce(jnp.add, real)
    for a in range(1, half + 1):
        even_part, odd_part = real[0], None
        for q in range(1, half + 1):
            even_part = even_part + float(np.cos(angle(q, a))) * real[q]
            term = float(np.sin(angle(q, a))) * imag[q]
            odd_part = term if odd_part is None else odd_part + term
        out[a] = even_part - odd_part
        out[A - a] = even_part + odd_part
    return out


def second_kernel(
    lat_rows, band_ref, table_ref, thick_ref, u_ref, v_ref, tracer_ref, up_ref, down_ref, cutoff_ref, high_ref, low_ref, *refs
):
    wind_ref, edge_ref, new_wind = refs[-3:]
    k = pl.program_id(0)
    _, L, rows, width = wind_ref.shape
    geo = table_ref[band_ref[0]]
    thick, u, v = thick_ref[0], u_ref[0], v_ref[0]
    thick_s, v_s = up_ref[0, 0], up_ref[1, 0]
    thick_n, thick_nn, u_n, v_n = (down_ref[i, 0] for i in range(4))
    east, north, below = fluxes(geo, thick, u, v, thick_s, v_s, thick_n)
    inverse = geo[0:rows, 2:3]
    new = thick - (east - west_of(east)) - (north - south_of(north, below)) * inverse
    east_n = u_n * jnp.where(u_n > 0, thick_n, east_of(thick_n))
    north_n = v_n * jnp.where(v_n > 0, thick_n, thick_nn) * geo[rows : rows + 1, 1:2]
    new_n = (
        thick_n
        - (east_n - west_of(east_n))
        - (north_n - north[rows - 1 : rows]) * geo[rows : rows + 1, 2:3]
    )
    new_wind[0, k] = u - 0.05 * (east_of(new) - new)
    inside = band_ref[0] * rows + row_ids(new.shape) < lat_rows - 1
    new_wind[1, k] = jnp.where(inside, v - 0.05 * (north_of(new, new_n) - new), 0.0)

    def store_edges(field, level, value):
        edge_ref[field, level, 0:1] = value[0:1]
        edge_ref[field, level, 1:2] = value[rows - 1 : rows]

    store_edges(0, k, new)
    scale = 1.0 / new
    for c in range(tracer_ref.shape[0]):
        change = tracer_change(
            tracer_ref[c, 0], up_ref[2 + c, 0], down_ref[4 + c, 0], thick, u, v, v_s, east, north, below, inverse
        )
        store_edges(3 + c, k, change * scale)

    @pl.when(k == L - 1)
    def _():
        pieces = [
            new_wind[:, :, :, a * LANES : (a + 1) * LANES].reshape(2 * L * rows, LANES) for a in range(width // LANES)
        ]
        cutoff = jnp.broadcast_to(cutoff_ref[...][None], (2 * L, rows, LANES)).reshape(2 * L * rows, LANES)
        for a, piece in enumerate(filter_rows(pieces, cutoff, high_ref, low_ref)):
            wind_ref[:, :, :, a * LANES : (a + 1) * LANES] = piece.reshape(2, L, rows, LANES)
        for f in range(2):
            for level in range(L):
                store_edges(1 + f, level, wind_ref[f, level])


def second_step(band, table, lat_rows, thickness, wind_u, wind_v, tracers, up, down, cutoff, wait):
    L, R, N = thickness.shape
    T = tracers.shape[0]
    high, low = filter_tables(N)
    level = pl.BlockSpec((1, R, N), lambda k: (k, 0, 0))
    some = lambda n, rows: pl.BlockSpec((n, 1, rows, N), lambda k: (0, k, 0, 0))
    whole = lambda shape: pl.BlockSpec(shape, lambda k: (0,) * len(shape))
    return pl.pallas_call(
        functools.partial(second_kernel, lat_rows),
        grid=(L,),
        in_specs=[SMEM, whole(table.shape), level, level, level, some(T, R), some(2 + T, 1), some(4 + T, 1)]
        + [whole((R, LANES)), whole(high.shape), whole(low.shape)]
        + after(wait),
        out_specs=[whole((2, L, R, N)), whole((3 + T, L, 2, N))],
        out_shape=[
            jax.ShapeDtypeStruct((2, L, R, N), jnp.float32),
            jax.ShapeDtypeStruct((3 + T, L, 2, N), jnp.float32),
        ],
        scratch_shapes=[pltpu.VMEM((2, L, R, N), jnp.float32)],
        compiler_params=params(),
        cost_estimate=cost(12 * 2 * L * R * high.size, 4 * L * R * N * (8 + T)),
        name="second_step",
    )(
        band, table, thickness, wind_u, wind_v, tracers, up, down,
        jnp.broadcast_to(cutoff[:, None], (R, LANES)), jnp.asarray(high), jnp.asarray(low), *wait,
    )


def weight_sums(weight_ref, firsts, L, levels):
    total = jnp.float32(0.0)
    below = [jnp.float32(0.0) for _ in firsts]
    for k in range(levels):
        w = weight_ref[k]
        below = [b + jnp.where(k < first, w, 0.0) for b, first in zip(below, firsts)]
        total = total + w
    weights = [[weight_ref[first + i] for i in range(L)] for first in firsts]
    sums = []
    for start, row in zip(below, weights):
        sums.append([start])
        for w in row:
            sums[-1].append(sums[-1][-1] + w)
    return total, weights, sums


def source_levels(place, counts, thick, others):
    C, S = counts
    lev, sub = place
    spot = [lax.rem(lev - g // S + C, C) * S + lax.rem(sub - g % S + S, S) for g in range(len(thick))]
    group = [functools.reduce(jnp.add, levels) for levels in thick]
    mass = functools.reduce(jnp.add, group)
    base = jnp.zeros_like(mass)
    for s, other in enumerate(others, 1):
        mass = mass + other
        base = base + jnp.where(lev >= s, other, 0.0)
    sources = []
    for g, levels in enumerate(thick):
        low = base
        for other in range(len(thick)):
            if other != g:
                low = low + jnp.where(spot[other] < spot[g], group[other], 0.0)
        for m, value in enumerate(levels):
            sources.append((g, m, low, value))
            low = low + value
    return mass, sources


def covered(top, sources):
    return [jnp.minimum(jnp.maximum(top - low, 0.0), value) for _, _, low, value in sources]


def remap_kernel(C, S, G, steps, fields, compact, with_thickness, carried, place_ref, weight_ref, *refs):
    if carried:
        for source_ref, copy_ref in zip(refs[:carried], refs[len(refs) - carried :]):
            copy_ref[...] = source_ref[...]
        refs = refs[carried : len(refs) - carried]
    thick_refs, refs = refs[: G * S], refs[G * S :]
    field_refs, refs = refs[: G * S], refs[G * S :]
    other_refs, out_refs = refs[: (C - G) * S], refs[len(refs) - len(steps) - with_thickness :]
    _, L, R, N = field_refs[0].shape
    lev, sub = place_ref[0], place_ref[1]
    firsts = [(lax.rem(lev + s, C) * S + sub) * L for s in steps]
    weight_sum, weights, sums = weight_sums(weight_ref, firsts, L, C * S * L)

    def tile(r, rows, columns):
        at = slice(r, r + rows)
        thick = [[ref[0, m, at, columns] for m in range(L)] for ref in thick_refs]
        others = [
            functools.reduce(jnp.add, [ref[at, columns] for ref in other_refs[s * S : (s + 1) * S]])
            for s in range(C - G)
        ]
        mass, sources = source_levels((lev, sub), (C, S), thick, others)
        unit = mass / weight_sum
        for index, s in enumerate(steps):
            below = covered(unit * sums[index][0], sources)
            for i in range(L):
                upto = covered(unit * sums[index][i + 1], sources)
                part = [a - b for a, b in zip(upto, below)]
                below = upto
                target = unit * weights[index][i]
                scale = 1.0 / target
                for f, field in enumerate(fields):
                    terms = [field_refs[g][field, m, at, columns] * w for (g, m, _, _), w in zip(sources, part)]
                    total = functools.reduce(jnp.add, terms) * scale
                    if compact and s > 0:
                        lower, upper = max(r, 1), min(r + rows, R - 1)
                        start = (f * L + i) * (R - 2) - 1
                        out_refs[index][start + lower : start + upper, columns] = total[lower - r : upper - r]
                    else:
                        out_refs[index][f, i, at, columns] = total
                if with_thickness and s == 0:
                    out_refs[len(steps)][i, at, columns] = target

    rows = min(R, 8)
    for r in range(0, R, rows):

        def body(c, carry):
            tile(r, rows, pl.ds(pl.multiple_of(c * LANES, LANES), LANES))
            return carry

        lax.fori_loop(0, N // LANES, body, 0)


def remap_parts(counts, place, weights, thick, sources, others, fields, steps, compact=False, with_thickness=False, carry=(), wait=()):
    C, S = counts
    _, L, R, N = sources[0].shape
    F = len(fields)
    whole = jax.ShapeDtypeStruct((F, L, R, N), jnp.float32)
    inner = jax.ShapeDtypeStruct((F * L * (R - 2), N), jnp.float32)
    out_shape = [inner if compact and s > 0 else whole for s in steps]
    if with_thickness:
        out_shape = out_shape + [jax.ShapeDtypeStruct((L, R, N), jnp.float32)]
    out_shape = out_shape + [jax.ShapeDtypeStruct(a.shape, a.dtype) for a in carry]
    G = len(thick) // S
    return pl.pallas_call(
        functools.partial(remap_kernel, C, S, G, tuple(steps), tuple(fields), compact, with_thickness, len(carry)),
        in_specs=[SMEM] * 2 + [VMEM] * (len(carry) + len(thick) + len(sources) + len(others)) + after(wait),
        out_specs=[VMEM] * len(out_shape),
        out_shape=out_shape,
        compiler_params=params(),
        cost_estimate=cost(len(steps) * G * S * L * L * R * N * (5 + 2 * F), 4 * R * N * L * (F + 1) * (S * G + len(steps))),
        name="remap_parts",
    )(place, weights, *carry, *thick, *sources, *others, *wait)


def finish_kernel(C, S, chunks, place_ref, weight_ref, *refs):
    group_refs, refs = refs[:S], refs[S:]
    other_refs, refs = refs[: (C - 1) * S], refs[(C - 1) * S :]
    *arrived_refs, edge_ref, thick_edge_ref, out_ref, thick_out_ref = refs
    T, L, R, N = out_ref.shape
    lev, sub = place_ref[0], place_ref[1]
    weight_sum, weights, sums = weight_sums(weight_ref, [(lev * S + sub) * L], L, C * S * L)
    where = [(chunk, at) for chunk, count in enumerate(chunks) for at in range(count)]

    def tile(r, columns):
        at = slice(r, r + 8)
        thick = [[ref[0, m, at, columns] for m in range(L)] for ref in group_refs]
        others = [
            functools.reduce(jnp.add, [ref[at, columns] for ref in other_refs[s * S : (s + 1) * S]])
            for s in range(C - 1)
        ]
        mass, sources = source_levels((lev, sub), (C, S), thick, others)
        unit = mass / weight_sum
        below = covered(unit * sums[0][0], sources)
        lower, upper = max(r, 1), min(r + 8, R - 1)
        for i in range(L):
            upto = covered(unit * sums[0][i + 1], sources)
            part = [a - b for a, b in zip(upto, below)]
            below = upto
            target = unit * weights[0][i]
            thick_out_ref[i, at, columns] = target
            scale = 1.0 / target
            for f in range(T):
                terms = [group_refs[g][1 + f, m, at, columns] * w for (g, m, _, _), w in zip(sources, part)]
                total = (functools.reduce(jnp.add, terms) * scale)[lower - r : upper - r]
                chunk, place = where[f]
                start = (place * L + i) * (R - 2) - 1
                for s in range(C - 1):
                    total = total + arrived_refs[chunk * (C - 1) + s][start + lower : start + upper, columns]
                out_ref[f, i, lower:upper, columns] = total

    for r in range(0, R, 8):

        def body(c, carry):
            tile(r, pl.ds(pl.multiple_of(c * LANES, LANES), LANES))
            return carry

        lax.fori_loop(0, N // LANES, body, 0)
    for i in range(L):
        for row, j in ((0, 0), (R - 1, 1)):
            thick_out_ref[i, row : row + 1] = thick_edge_ref[i, j : j + 1]
            for f in range(T):
                out_ref[f, i, row : row + 1] = edge_ref[2 + f, i, j : j + 1]


def finish_tracers(counts, place, weights, group, others, arrived, edge, thick_edge):
    C, S = counts
    T = group[0].shape[0] - 1
    _, L, R, N = group[0].shape
    chunks = tuple(a[0].shape[0] // (L * (R - 2)) for a in arrived)
    flat = [a for chunk in arrived for a in chunk]
    operands = list(group) + list(others) + flat + [edge, thick_edge]
    return pl.pallas_call(
        functools.partial(finish_kernel, C, S, chunks),
        in_specs=[SMEM] * 2 + [VMEM] * len(operands),
        out_specs=[VMEM] * 2,
        out_shape=[
            jax.ShapeDtypeStruct((T, L, R, N), jnp.float32),
            jax.ShapeDtypeStruct((L, R, N), jnp.float32),
        ],
        compiler_params=params(),
        cost_estimate=cost(S * L * L * R * N * (5 + 2 * T), 4 * R * N * L * (T + 1) * (S + 2)),
        name="finish_tracers",
    )(place, weights, *operands)


def finish_winds_kernel(count, own_ref, edge_ref, *refs):
    arrived_refs, (u_ref, v_ref) = refs[:count], refs[-2:]
    _, L, R, N = own_ref.shape
    for f, out_ref in enumerate((u_ref, v_ref)):
        for i in range(L):
            start = (f * L + i) * (R - 2)
            total = own_ref[f, i, 1 : R - 1]
            for ref in arrived_refs:
                total = total + ref[start : start + R - 2]
            out_ref[i, 1 : R - 1] = total
            out_ref[i, 0:1] = edge_ref[f, i, 0:1]
            out_ref[i, R - 1 : R] = edge_ref[f, i, 1:2]


def finish_winds(own, arrived, edge, wait):
    shape = jax.ShapeDtypeStruct(own.shape[1:], jnp.float32)
    return pl.pallas_call(
        functools.partial(finish_winds_kernel, len(arrived)),
        in_specs=[VMEM] * (2 + len(arrived)) + after(wait),
        out_specs=[VMEM] * 2,
        out_shape=[shape] * 2,
        compiler_params=params(),
        cost_estimate=cost(own.size, 12 * own.size),
        name="finish_winds",
    )(own, edge, *arrived, *wait)


def shifted(value, lev_count, sub_count, s, t):
    if t == 0:
        return lax.ppermute(value, "lev", [(i, (i + s) % lev_count) for i in range(lev_count)])
    if s == 0:
        return lax.ppermute(value, "sub", [(i, (i + t) % sub_count) for i in range(sub_count)])
    pairs = [
        (i * sub_count + j, (i + s) % lev_count * sub_count + (j + t) % sub_count)
        for i in range(lev_count)
        for j in range(sub_count)
    ]
    return lax.ppermute(value, ("lev", "sub"), pairs)


def per_device(thickness, wind_u, wind_v, tracers, level_weights, cutoff):
    L, R, N = thickness.shape
    lat_count = lax.axis_size("lat")
    C, S = lax.axis_size("lev"), lax.axis_size("sub")
    lat_rows = R * lat_count
    send = functools.partial(shifted, lev_count=C, sub_count=S)

    T = tracers.shape[0]
    northward = [(i, i + 1) for i in range(lat_count - 1)]
    southward = [(j, i) for i, j in northward]
    band = lax.axis_index("lat").astype(jnp.int32).reshape(1)
    table = jnp.asarray(geometry_table(lat_rows, R))
    place = jnp.stack([lax.axis_index("lev"), lax.axis_index("sub")]).astype(jnp.int32)
    away = range(1, C)

    def with_others_of_chip(own):
        return [own] + [send(own, s=0, t=t) for t in range(1, S)]

    def sent(parts):
        return [send(part, s=s, t=0) for s, part in zip(away, parts)]

    remap = functools.partial(remap_parts, (C, S), place, level_weights)

    inner, own_sum, last, leading = inner_step(band, table, thickness, wind_u, wind_v, tracers)
    others = [send(own_sum, s=s, t=t) for s in away for t in range(S)]
    group = with_others_of_chip(inner)
    first_away = remap(group, group, others, range(1, 2), away, compact=True)
    *rest_away, last, leading = remap(
        group, group, others, range(2, 1 + T), away, compact=True, carry=(last, leading), wait=first_away[:1]
    )
    arrived = [sent(first_away), sent(rest_away)]

    up = lax.ppermute(last, "lat", northward)
    down = lax.ppermute(leading, "lat", southward)
    winds, edge = second_step(
        band, table, lat_rows, thickness, wind_u, wind_v, tracers, up, down, cutoff, [rest_away[0], *arrived[0][:1]]
    )
    edges = [edge] + [send(edge, s=s, t=0) for s in away]
    winds_own, *winds_away = remap(
        group, with_others_of_chip(winds), others, range(2), range(C), compact=True, wait=arrived[1][:1]
    )
    winds_arrived = sent(winds_away)
    edges = [a for own in edges for a in with_others_of_chip(own)]
    edge_out, thick_edge = remap(
        edges, edges, [], range(1, 3 + T), (0,), with_thickness=True, wait=winds_away[:1]
    )

    tracers_out, thickness_out = finish_tracers(
        (C, S), place, level_weights, group, others, arrived, edge_out, thick_edge
    )
    u_out, v_out = finish_winds(winds_own, winds_arrived, edge_out, [tracers_out])
    return thickness_out, u_out, v_out, tracers_out


def solution(mesh):
    placed = (
        P(("member", "lev", "sub"), "lat", None),
        P(("member", "lev", "sub"), "lat", None),
        P(("member", "lev", "sub"), "lat", None),
        P("member", ("lev", "sub"), "lat", None),
        P(),
        P("lat"),
    )
    return jax.shard_map(
        per_device,
        mesh=mesh,
        in_specs=placed,
        out_specs=(
            P(("member", "lev", "sub"), "lat", None),
            P(("member", "lev", "sub"), "lat", None),
            P(("member", "lev", "sub"), "lat", None),
            P("member", ("lev", "sub"), "lat", None),
        ),
        check_vma=False,
    )
```

time: 117 us -> 57.2 us (0.49)
  other arithmetic: 31 us -> 0.07 us
  blocking collectives: 27.8 us -> 0 us
  Pallas kernels: 0 us -> 19.7 us
  local copies, waits for them, and re-layouts: 19.1 us -> 1.39 us
  matrix products: 4.68 us -> 0 us
  starting transfers between devices: 10.2 us -> 14.4 us
  waiting for transfers between devices: 22.8 us -> 20.7 us
    all_to_all x1 -> x0, blocking collectives: 27.8 us -> none  [per_device(): lax.all_to_all(remapped, ('lev', 'sub'), split_axis=1, concat_axis=2, til...]
    all_to_all x1 -> x0, waiting for transfers between devices: 22.8 us -> none  [per_device(): lax.all_to_all(stacked, ('lev', 'sub'), split_axis=2, concat_axis=1, tile...]
    ppermute x2 -> x12, waiting for transfers between devices: 0.01 us -> 20.7 us  [the longest x5 15.5 us: shifted(): lax.ppermute(value, 'lev', [(i, (i + s) % lev_count) for i in range(lev_c...]
    pallas_call x0 -> x8, Pallas kernels: none -> 19.7 us  [the longest x4 8.07 us: remap_parts(): pl.pallas_call(functools.partial(remap_kernel, C, S, G, tuple(steps), tup...]
    sin x2 -> x0, other arithmetic: 12.1 us -> none  [the longest x1 12 us: spectral_filter(): table = jnp.concatenate([jnp.cos(angles), jnp.sin(angles)], axis=1)]
    ppermute x2 -> x12, starting transfers between devices: 6.24 us -> 14.4 us  [the longest x5 7.87 us: shifted(): lax.ppermute(value, 'lev', [(i, (i + s) % lev_count) for i in range(lev_c...]
    reduce_sum x5 -> x0, other arithmetic: 5.84 us -> none  [the longest x4 5.24 us: integrate(): return jnp.sum(fields[:, None] * w[None], axis=2)]
    dot_general x2 -> x0, matrix products: 4.68 us -> none  [the longest x1 2.79 us: spectral_filter(): jnp.einsum('ark,mk->arm', spectrum, table, precision=lax.Precision.HIGH)]
  transfers between devices with their start and end apart: 3 -> 12, of which waited for: 1 -> 7; matrix products, arithmetic and copies ran while one was open for 13% -> 0% of each run, Pallas kernels for 0% -> 24%
where the time goes in v4:
time: 57.2 us; the launch traced here: 57 us
  waiting for transfers between devices  20.7 us (36%)
  Pallas kernels  19.7 us (34%)
  starting transfers between devices  14.4 us (25%)
  local copies, waits for them, and re-layouts  1.39 us (2%)
  between operations  0.79 us (1%)
    ppermute x5, waiting for transfers between devices, shifted(): lax.ppermute(value, 'lev', [(i, (i + s) % lev_count) for i in range(lev_c...  15.5 us
    pallas_call x4, Pallas kernels, remap_parts(): pl.pallas_call(functools.partial(remap_kernel, C, S, G, tuple(steps), tup...  8.07 us
    ppermute x5, starting transfers between devices, shifted(): lax.ppermute(value, 'lev', [(i, (i + s) % lev_count) for i in range(lev_c...  7.87 us
    ppermute x1, starting transfers between devices, per_device(): up = lax.ppermute(last, 'lat', northward)  4.54 us
    pallas_call x1, Pallas kernels, inner_step(): pl.pallas_call(inner_kernel, grid=(L,), in_specs=[SMEM, pl.BlockSpec(tabl...  3.82 us
    pallas_call x1, Pallas kernels, second_step(): pl.pallas_call(functools.partial(second_kernel, lat_rows), grid=(L,), in_...  3.65 us
    pallas_call x1, Pallas kernels, finish_tracers(): pl.pallas_call(functools.partial(finish_kernel, C, S, chunks), in_specs=[...  3.25 us
    ppermute x1, waiting for transfers between devices, per_device(): up = lax.ppermute(last, 'lat', northward)  2.3 us
  transfers between devices with their start and end apart: 12, of which 7 were waited for; matrix products, arithmetic and copies ran while one was open for 0% of the time, Pallas kernels for 24%

profile of v4, /device:TPU:0, one launch (start us, length us, event | category | flops | bytes accessed | tf_op | source)
XLA Modules:
  0.0 57.0 jit_solution(1674723716341562789)
XLA Ops:
  0.6 3.8 %inner_step.1 = (f32[5,4,16,1152]{3,2,1,0:T(8,128)S(1)}, f32[16,1152]{1,0:T(8,128)S(1)}, f32[6,4,1,1152]{3,2,1,0:T(1,128)S(1)}, f32[8,4,1,1152]{3,2,1,0:T(1,128)S(1)}) custom-call(s32[1]{0:T(128)} %bitcast.2.band_ref, f32[4,24,128]{2,1,0:T(8,128)} %constant.17.clone.table_ref, f32[4,16,1152]{2,1,0:T(8,128)} %thick_ref.3, f32[4,16,1152]{2,1,0:T(8,128)} %u_ref.3, ...), custom_call_target="tpu_custom_call" | custom-call | flops 9584640 | bytes 4718592 | tf_op jit(solution)/shard_map/inner_step/pallas_call | solution.py:119
  4.5 0.5 collective-permute-start
  5.0 2.6 %collective-permute-start.1 = (f32[16,1152]{1,0:T(8,128)S(1)}, f32[16,1152]{1,0:T(8,128)S(1)}, u32[]{:S(2)}, u32[]{:S(2)}) collective-permute-start(f32[16,1152]{1,0:T(8,128)S(1)} %get-tuple-element.22), channel_id=1, source_target_pairs={{0,2},{2,0},{1,3},{3,1},{4,6},{6,4},{5,7},{7,5},{8,10},{10,8},{9,1... | collective-permute-start | bytes 221192 | tf_op jit(solution)/shard_map/ppermute | solution.py:497
  7.7 2.7 %collective-permute-done.1.refs_4_.refs_6_.refs_2_ = f32[16,1152]{1,0:T(8,128)S(1)} collective-permute-done((f32[16,1152]{1,0:T(8,128)S(1)}, f32[16,1152]{1,0:T(8,128)S(1)}, u32[]{:S(2)}, u32[]{:S(2)}) %collective-permute-start.1) | collective-permute-done | bytes 73760 | tf_op jit(solution)/shard_map/ppermute | solution.py:497
  10.4 1.4 %collective-permute-done.2.refs_5_.refs_7_.refs_3_ = f32[16,1152]{1,0:T(8,128)S(1)} collective-permute-done((f32[16,1152]{1,0:T(8,128)S(1)}, f32[16,1152]{1,0:T(8,128)S(1)}, u32[]{:S(2)}, u32[]{:S(2)}) %collective-permute-start.2) | collective-permute-done | bytes 73760 | tf_op jit(solution)/shard_map/ppermute | solution.py:505
  11.8 1.5 %remap_parts.4.refs_8_ = f32[56,1152]{1,0:T(8,128)S(1)} custom-call(s32[2]{0:T(128)S(1)} %pad_add_fusion.place_ref, f32[16]{0:T(128)S(1)} %copy-done.8, f32[5,4,16,1152]{3,2,1,0:T(8,128)S(1)} %get-tuple-element.21.refs_0_.refs_2_.refs_4_, f32[5,4,16,1152]{3,2,1,0:T(8,128)S(1)} %collective-permute-done.refs_1_.refs_3_.refs_5_, ...), custom_call_target="tpu_custom_call" | custom-call | flops 4128768 | bytes 1769472 | tf_op jit(solution)/shard_map/remap_parts/pallas_call | solution.py:386
  13.3 1.6 %collective-permute-start.3 = (f32[56,1152]{1,0:T(8,128)S(1)}, f32[56,1152]{1,0:T(8,128)S(1)}, u32[]{:S(2)}, u32[]{:S(2)}) collective-permute-start(f32[56,1152]{1,0:T(8,128)S(1)} %remap_parts.4.refs_8_), channel_id=1, source_target_pairs={{0,2},{2,0},{1,3},{3,1},{4,6},{6,4},{5,7},{7,5},{8,10},{10,8},{9,1... | collective-permute-start | bytes 774152 | tf_op jit(solution)/shard_map/ppermute | solution.py:497
  14.9 1.8 %remap_parts.5 = (f32[168,1152]{1,0:T(8,128)S(1)}, f32[6,4,1,1152]{3,2,1,0:T(1,128)S(1)}, f32[8,4,1,1152]{3,2,1,0:T(1,128)S(1)}) custom-call(s32[2]{0:T(128)S(1)} %pad_add_fusion.place_ref, f32[16]{0:T(128)S(1)} %copy-done.8, f32[6,4,1,1152]{3,2,1,0:T(1,128)S(1)} %get-tuple-element.23.refs_0_, f32[8,4,1,1152]{3,2,1,0:T(1,128)S(1)} %get-tuple-element.24.refs_1_, ...), custom_call_target="tpu_custom_call" | custom-call | flops 6488064 | bytes 3538944 | tf_op jit(solution)/shard_map/remap_parts/pallas_call | solution.py:386
  16.7 1.3 %collective-permute-start.6 = (f32[8,4,1,1152]{3,2,1,0:T(1,128)S(1)}, f32[8,4,1,1152]{3,2,1,0:T(1,128)S(1)}, u32[]{:S(2)}, u32[]{:S(2)}) collective-permute-start(f32[8,4,1,1152]{3,2,1,0:T(1,128)S(1)} %get-tuple-element.27), channel_id=1, source_target_pairs={{4,0},{8,4},{12,8},{5,1},{9,5},{13,9},{6,2},{10,6},{14,10},{7,3},{... | collective-permute-start | bytes 442376 | tf_op jit(solution)/shard_map/ppermute | solution.py:541
  18.0 0.6 %collective-permute-start.4 = (f32[168,1152]{1,0:T(8,128)S(1)}, f32[168,1152]{1,0:T(8,128)S(1)}, u32[]{:S(2)}, u32[]{:S(2)}) collective-permute-start(f32[168,1152]{1,0:T(8,128)S(1)} %get-tuple-element.25.refs_0_), channel_id=1, source_target_pairs={{0,2},{2,0},{1,3},{3,1},{4,6},{6,4},{5,7},{7,5},{8,10},{10,8},{9,1... | collective-permute-start | bytes 2322440 | tf_op jit(solution)/shard_map/ppermute | solution.py:497
  18.6 4.5 %collective-permute-start.5 = (f32[6,4,1,1152]{3,2,1,0:T(1,128)S(1)}, f32[6,4,1,1152]{3,2,1,0:T(1,128)S(1)}, u32[]{:S(2)}, u32[]{:S(2)}) collective-permute-start(f32[6,4,1,1152]{3,2,1,0:T(1,128)S(1)} %get-tuple-element.26), channel_id=1, source_target_pairs={{0,4},{4,8},{8,12},{1,5},{5,9},{9,13},{2,6},{6,10},{10,14},{3,7},{... | collective-permute-start | bytes 331784 | tf_op jit(solution)/shard_map/ppermute | solution.py:540
  23.1 2.3 %collective-permute-done.5.up_ref = f32[6,4,1,1152]{3,2,1,0:T(1,128)S(1)} collective-permute-done((f32[6,4,1,1152]{3,2,1,0:T(1,128)S(1)}, f32[6,4,1,1152]{3,2,1,0:T(1,128)S(1)}, u32[]{:S(2)}, u32[]{:S(2)}) %collective-permute-start.5) | collective-permute-done | bytes 110624 | tf_op jit(solution)/shard_map/ppermute | solution.py:540
  25.6 3.7 %second_step.1 = (f32[2,4,16,1152]{3,2,1,0:T(8,128)S(1)}, f32[7,4,2,1152]{3,2,1,0:T(2,128)S(1)}) custom-call(s32[1]{0:T(128)} %bitcast.2.band_ref, f32[4,24,128]{2,1,0:T(8,128)S(1)} %copy-done.7, f32[4,16,1152]{2,1,0:T(8,128)S(1)} %copy-done.1, f32[4,16,1152]{2,1,0:T(8,128)S(1)} %copy-done.2, f32[4,16,1152]{2,1,0:T(8,128)S(1)} %copy-done.3, ...), custom_call_target="tpu_custom_call" | custom-call | flops 503316480 | bytes 3538944 | tf_op jit(solution)/shard_map/second_step/pallas_call | solution.py:260
  29.3 1.6 %collective-permute-start.8 = (f32[7,4,2,1152]{3,2,1,0:T(2,128)S(1)}, f32[7,4,2,1152]{3,2,1,0:T(2,128)S(1)}, u32[]{:S(2)}, u32[]{:S(2)}) collective-permute-start(f32[7,4,2,1152]{3,2,1,0:T(2,128)S(1)} %get-tuple-element.28.refs_0_.refs_4_), channel_id=1, source_target_pairs={{0,2},{2,0},{1,3},{3,1},{4,6},{6,4},{5,7},{7,5},{8,10},{10,8},{9,1... | collective-permute-start | bytes 774152 | tf_op jit(solution)/shard_map/ppermute | solution.py:497
  30.9 8.1 %collective-permute-done.4.refs_6_.refs_5_ = f32[168,1152]{1,0:T(8,128)S(1)} collective-permute-done((f32[168,1152]{1,0:T(8,128)S(1)}, f32[168,1152]{1,0:T(8,128)S(1)}, u32[]{:S(2)}, u32[]{:S(2)}) %collective-permute-start.4) | collective-permute-done | bytes 774176 | tf_op jit(solution)/shard_map/ppermute | solution.py:497
  39.0 2.4 %remap_parts.6 = (f32[2,4,16,1152]{3,2,1,0:T(8,128)S(1)}, f32[112,1152]{1,0:T(8,128)S(1)}) custom-call(s32[2]{0:T(128)S(1)} %pad_add_fusion.place_ref, f32[16]{0:T(128)S(1)} %copy-done.8, f32[5,4,16,1152]{3,2,1,0:T(8,128)S(1)} %get-tuple-element.21.refs_0_.refs_2_.refs_4_, f32[5,4,16,1152]{3,2,1,0:T(8,128)S(1)} %collective-permute-done.refs_1_.refs_3_.refs_5_, ...), custom_call_target="tpu_custom_call" | custom-call | flops 10616832 | bytes 3538944 | tf_op jit(solution)/shard_map/remap_parts/pallas_call | solution.py:386
  41.4 1.6 %collective-permute-start.11 = (f32[112,1152]{1,0:T(8,128)S(1)}, f32[112,1152]{1,0:T(8,128)S(1)}, u32[]{:S(2)}, u32[]{:S(2)}) collective-permute-start(f32[112,1152]{1,0:T(8,128)S(1)} %get-tuple-element.30.refs_8_), channel_id=1, source_target_pairs={{0,2},{2,0},{1,3},{3,1},{4,6},{6,4},{5,7},{7,5},{8,10},{10,8},{9,1... | collective-permute-start | bytes 1548296 | tf_op jit(solution)/shard_map/ppermute | solution.py:497
  43.0 1.6 %collective-permute-done.8.refs_2_.refs_6_ = f32[7,4,2,1152]{3,2,1,0:T(2,128)S(1)} collective-permute-done((f32[7,4,2,1152]{3,2,1,0:T(2,128)S(1)}, f32[7,4,2,1152]{3,2,1,0:T(2,128)S(1)}, u32[]{:S(2)}, u32[]{:S(2)}) %collective-permute-start.8) | collective-permute-done | bytes 258080 | tf_op jit(solution)/shard_map/ppermute | solution.py:497
  44.5 1.5 %collective-permute-done.9.refs_3_.refs_7_ = f32[7,4,2,1152]{3,2,1,0:T(2,128)S(1)} collective-permute-done((f32[7,4,2,1152]{3,2,1,0:T(2,128)S(1)}, f32[7,4,2,1152]{3,2,1,0:T(2,128)S(1)}, u32[]{:S(2)}, u32[]{:S(2)}) %collective-permute-start.9) | collective-permute-done | bytes 258080 | tf_op jit(solution)/shard_map/ppermute | solution.py:499
  46.0 2.4 %remap_parts.7 = (f32[6,4,2,1152]{3,2,1,0:T(2,128)S(1)}, f32[4,2,1152]{2,1,0:T(2,128)S(1)}) custom-call(s32[2]{0:T(128)S(1)} %pad_add_fusion.place_ref, f32[16]{0:T(128)S(1)} %copy-done.8, f32[7,4,2,1152]{3,2,1,0:T(2,128)S(1)} %get-tuple-element.28.refs_0_.refs_4_, f32[7,4,2,1152]{3,2,1,0:T(2,128)S(1)} %collective-permute-done.7.refs_1_.refs_5_, ...), custom_call_target="tpu_custom_call" | custom-call | flops 2506752 | bytes 1290240 | tf_op jit(solution)/shard_map/remap_parts/pallas_call | solution.py:386
  48.4 3.2 %finish_tracers.1 = (f32[4,4,16,1152]{3,2,1,0:T(8,128)}, f32[4,16,1152]{2,1,0:T(8,128)}) custom-call(s32[2]{0:T(128)S(1)} %pad_add_fusion.place_ref, f32[16]{0:T(128)S(1)} %copy-done.8, f32[5,4,16,1152]{3,2,1,0:T(8,128)S(1)} %get-tuple-element.21.refs_0_.refs_2_.refs_4_, f32[5,4,16,1152]{3,2,1,0:T(8,128)S(1)} %collective-permute-done.refs_1_.refs_3_.refs_5_, ...), custom_call_target="tpu_custom_call" | custom-call | flops 7667712 | bytes 5898240 | tf_op jit(solution)/shard_map/finish_tracers/pallas_call | solution.py:454
  51.7 3.1 %collective-permute-done.11.refs_0_ = f32[112,1152]{1,0:T(8,128)S(1)} collective-permute-done((f32[112,1152]{1,0:T(8,128)S(1)}, f32[112,1152]{1,0:T(8,128)S(1)}, u32[]{:S(2)}, u32[]{:S(2)}) %collective-permute-start.11) | collective-permute-done | bytes 516128 | tf_op jit(solution)/shard_map/ppermute | solution.py:497
  54.8 1.3 %copy-done.4 = f32[4,4,16,1152]{3,2,1,0:T(8,128)S(1)} copy-done((f32[4,4,16,1152]{3,2,1,0:T(8,128)S(1)}, f32[4,4,16,1152]{3,2,1,0:T(8,128)}, u32[]{:S(2)}) %copy-start.4) | copy-done | bytes 1179672
  56.1 0.9 %finish_winds.1 = (f32[4,16,1152]{2,1,0:T(8,128)}, f32[4,16,1152]{2,1,0:T(8,128)}) custom-call(f32[2,4,16,1152]{3,2,1,0:T(8,128)S(1)} %get-tuple-element.34.own_ref, f32[6,4,2,1152]{3,2,1,0:T(2,128)S(1)} %get-tuple-element.31.refs_6_.edge_ref, f32[112,1152]{1,0:T(8,128)S(1)} %collective-permute-done.11.refs_0_, f32[4,4,16,1152]{3,2,1,0:T(8,128)S(1)} %copy-done.4), custom_call_target="tpu_custom_call" | custom-call | flops 147456 | bytes 1769472 | tf_op jit(solution)/shard_map/finish_winds/pallas_call | solution.py:484
  (30 shorter events, 0.4 us)
Async XLA Ops:
  0.6 11.2 %copy-start.8 = (f32[16]{0:T(128)S(1)}, f32[16]{0:T(128)}, u32[]{:S(2)}) copy-start(f32[16]{0:T(128)} %weight_ref.9) | copy-start | bytes 196
  4.5 7.3 %collective-permute-start = (f32[5,4,16,1152]{3,2,1,0:T(8,128)S(1)}, f32[5,4,16,1152]{3,2,1,0:T(8,128)S(1)}, u32[]{:S(2)}, u32[]{:S(2)}) collective-permute-start(f32[5,4,16,1152]{3,2,1,0:T(8,128)S(1)} %get-tuple-element.21.refs_0_.refs_2_.refs_4_), channel_id=1, source_target_pairs={{0,1},{1,0},{2,3},{3,2},{4,5},{5,4},{6,7},{7,6},{8,9},{9,8},{10,11... | collective-permute-start | bytes 4423688 | tf_op jit(solution)/shard_map/ppermute | solution.py:499
  5.0 5.4 %collective-permute-start.1 = (f32[16,1152]{1,0:T(8,128)S(1)}, f32[16,1152]{1,0:T(8,128)S(1)}, u32[]{:S(2)}, u32[]{:S(2)}) collective-permute-start(f32[16,1152]{1,0:T(8,128)S(1)} %get-tuple-element.22), channel_id=1, source_target_pairs={{0,2},{2,0},{1,3},{3,1},{4,6},{6,4},{5,7},{7,5},{8,10},{10,8},{9,1... | collective-permute-start | bytes 221192 | tf_op jit(solution)/shard_map/ppermute | solution.py:497
  7.6 4.2 %collective-permute-start.2 = (f32[16,1152]{1,0:T(8,128)S(1)}, f32[16,1152]{1,0:T(8,128)S(1)}, u32[]{:S(2)}, u32[]{:S(2)}) collective-permute-start(f32[16,1152]{1,0:T(8,128)S(1)} %get-tuple-element.22), channel_id=1, source_target_pairs={{0,3},{1,2},{2,1},{3,0},{4,7},{5,6},{6,5},{7,4},{8,11},{9,10},{10,... | collective-permute-start | bytes 221192 | tf_op jit(solution)/shard_map/ppermute | solution.py:505
  13.3 12.2 %collective-permute-start.3 = (f32[56,1152]{1,0:T(8,128)S(1)}, f32[56,1152]{1,0:T(8,128)S(1)}, u32[]{:S(2)}, u32[]{:S(2)}) collective-permute-start(f32[56,1152]{1,0:T(8,128)S(1)} %remap_parts.4.refs_8_), channel_id=1, source_target_pairs={{0,2},{2,0},{1,3},{3,1},{4,6},{6,4},{5,7},{7,5},{8,10},{10,8},{9,1... | collective-permute-start | bytes 774152 | tf_op jit(solution)/shard_map/ppermute | solution.py:497
  14.8 10.6 %copy-start.9 = (s32[16]{0:T(128)S(1)}, s32[16]{0:T(128)}, u32[]{:S(2)}) copy-start(s32[16]{0:T(128)} %param.14) | copy-start | bytes 196
  14.8 10.7 %copy-start = (f32[4,4,16,1152]{3,2,1,0:T(8,128)S(1)}, f32[4,4,16,1152]{3,2,1,0:T(8,128)}, u32[]{:S(2)}) copy-start(f32[4,4,16,1152]{3,2,1,0:T(8,128)} %tracer_ref.3) | copy-start | bytes 3538948
  14.8 10.7 %copy-start.1 = (f32[4,16,1152]{2,1,0:T(8,128)S(1)}, f32[4,16,1152]{2,1,0:T(8,128)}, u32[]{:S(2)}) copy-start(f32[4,16,1152]{2,1,0:T(8,128)} %thick_ref.3) | copy-start | bytes 884740
  14.8 10.7 %copy-start.2 = (f32[4,16,1152]{2,1,0:T(8,128)S(1)}, f32[4,16,1152]{2,1,0:T(8,128)}, u32[]{:S(2)}) copy-start(f32[4,16,1152]{2,1,0:T(8,128)} %u_ref.3) | copy-start | bytes 884740
  14.9 10.7 %copy-start.3 = (f32[4,16,1152]{2,1,0:T(8,128)S(1)}, f32[4,16,1152]{2,1,0:T(8,128)}, u32[]{:S(2)}) copy-start(f32[4,16,1152]{2,1,0:T(8,128)} %v_ref.3) | copy-start | bytes 884740
  14.9 10.7 %copy-start.5 = (bf16[5,256,256]{2,1,0:T(8,128)(2,1)S(1)}, bf16[5,256,256]{2,1,0:T(8,128)(2,1)}, u32[]{:S(2)}) copy-start(bf16[5,256,256]{2,1,0:T(8,128)(2,1)} %constant.18.clone.high_ref) | copy-start | bytes 1966084
  14.9 10.7 %copy-start.6 = (bf16[5,256,256]{2,1,0:T(8,128)(2,1)S(1)}, bf16[5,256,256]{2,1,0:T(8,128)(2,1)}, u32[]{:S(2)}) copy-start(bf16[5,256,256]{2,1,0:T(8,128)(2,1)} %constant.19.clone.low_ref) | copy-start | bytes 1966084
  14.9 10.7 %copy-start.7 = (f32[4,24,128]{2,1,0:T(8,128)S(1)}, f32[4,24,128]{2,1,0:T(8,128)}, u32[]{:S(2)}) copy-start(f32[4,24,128]{2,1,0:T(8,128)} %constant.17.clone.table_ref) | copy-start | bytes 147460
  16.7 8.7 %collective-permute-start.6 = (f32[8,4,1,1152]{3,2,1,0:T(1,128)S(1)}, f32[8,4,1,1152]{3,2,1,0:T(1,128)S(1)}, u32[]{:S(2)}, u32[]{:S(2)}) collective-permute-start(f32[8,4,1,1152]{3,2,1,0:T(1,128)S(1)} %get-tuple-element.27), channel_id=1, source_target_pairs={{4,0},{8,4},{12,8},{5,1},{9,5},{13,9},{6,2},{10,6},{14,10},{7,3},{... | collective-permute-start | bytes 442376 | tf_op jit(solution)/shard_map/ppermute | solution.py:541
  18.0 20.9 %collective-permute-start.4 = (f32[168,1152]{1,0:T(8,128)S(1)}, f32[168,1152]{1,0:T(8,128)S(1)}, u32[]{:S(2)}, u32[]{:S(2)}) collective-permute-start(f32[168,1152]{1,0:T(8,128)S(1)} %get-tuple-element.25.refs_0_), channel_id=1, source_target_pairs={{0,2},{2,0},{1,3},{3,1},{4,6},{6,4},{5,7},{7,5},{8,10},{10,8},{9,1... | collective-permute-start | bytes 2322440 | tf_op jit(solution)/shard_map/ppermute | solution.py:497
  18.6 6.9 %collective-permute-start.5 = (f32[6,4,1,1152]{3,2,1,0:T(1,128)S(1)}, f32[6,4,1,1152]{3,2,1,0:T(1,128)S(1)}, u32[]{:S(2)}, u32[]{:S(2)}) collective-permute-start(f32[6,4,1,1152]{3,2,1,0:T(1,128)S(1)} %get-tuple-element.26), channel_id=1, source_target_pairs={{0,4},{4,8},{8,12},{1,5},{5,9},{9,13},{2,6},{6,10},{10,14},{3,7},{... | collective-permute-start | bytes 331784 | tf_op jit(solution)/shard_map/ppermute | solution.py:540
  29.2 9.7 %collective-permute-start.10 = (f32[2,4,16,1152]{3,2,1,0:T(8,128)S(1)}, f32[2,4,16,1152]{3,2,1,0:T(8,128)S(1)}, u32[]{:S(2)}, u32[]{:S(2)}) collective-permute-start(f32[2,4,16,1152]{3,2,1,0:T(8,128)S(1)} %get-tuple-element.29.refs_2_), channel_id=1, source_target_pairs={{0,1},{1,0},{2,3},{3,2},{4,5},{5,4},{6,7},{7,6},{8,9},{9,8},{10,11... | collective-permute-start | bytes 1769480 | tf_op jit(solution)/shard_map/ppermute | solution.py:499
  29.3 15.2 %collective-permute-start.8 = (f32[7,4,2,1152]{3,2,1,0:T(2,128)S(1)}, f32[7,4,2,1152]{3,2,1,0:T(2,128)S(1)}, u32[]{:S(2)}, u32[]{:S(2)}) collective-permute-start(f32[7,4,2,1152]{3,2,1,0:T(2,128)S(1)} %get-tuple-element.28.refs_0_.refs_4_), channel_id=1, source_target_pairs={{0,2},{2,0},{1,3},{3,1},{4,6},{6,4},{5,7},{7,5},{8,10},{10,8},{9,1... | collective-permute-start | bytes 774152 | tf_op jit(solution)/shard_map/ppermute | solution.py:497
  41.4 13.4 %collective-permute-start.11 = (f32[112,1152]{1,0:T(8,128)S(1)}, f32[112,1152]{1,0:T(8,128)S(1)}, u32[]{:S(2)}, u32[]{:S(2)}) collective-permute-start(f32[112,1152]{1,0:T(8,128)S(1)} %get-tuple-element.30.refs_8_), channel_id=1, source_target_pairs={{0,2},{2,0},{1,3},{3,1},{4,6},{6,4},{5,7},{7,5},{8,10},{10,8},{9,1... | collective-permute-start | bytes 1548296 | tf_op jit(solution)/shard_map/ppermute | solution.py:497
  42.9 1.6 %collective-permute-start.7 = (f32[7,4,2,1152]{3,2,1,0:T(2,128)S(1)}, f32[7,4,2,1152]{3,2,1,0:T(2,128)S(1)}, u32[]{:S(2)}, u32[]{:S(2)}) collective-permute-start(f32[7,4,2,1152]{3,2,1,0:T(2,128)S(1)} %get-tuple-element.28.refs_0_.refs_4_), channel_id=1, source_target_pairs={{0,1},{1,0},{2,3},{3,2},{4,5},{5,4},{6,7},{7,6},{8,9},{9,8},{10,11... | collective-permute-start | bytes 774152 | tf_op jit(solution)/shard_map/ppermute | solution.py:499
  44.5 1.5 %collective-permute-start.9 = (f32[7,4,2,1152]{3,2,1,0:T(2,128)S(1)}, f32[7,4,2,1152]{3,2,1,0:T(2,128)S(1)}, u32[]{:S(2)}, u32[]{:S(2)}) collective-permute-start(f32[7,4,2,1152]{3,2,1,0:T(2,128)S(1)} %collective-permute-done.8.refs_2_.refs_6_), channel_id=1, source_target_pairs={{0,1},{1,0},{2,3},{3,2},{4,5},{5,4},{6,7},{7,6},{8,9},{9,8},{10,11... | collective-permute-start | bytes 774152 | tf_op jit(solution)/shard_map/ppermute | solution.py:499
  54.8 1.3 %copy-start.4 = (f32[4,4,16,1152]{3,2,1,0:T(8,128)S(1)}, f32[4,4,16,1152]{3,2,1,0:T(8,128)}, u32[]{:S(2)}) copy-start(f32[4,4,16,1152]{3,2,1,0:T(8,128)} %get-tuple-element.20.refs_1_) | copy-start | bytes 3538948

commit v5 on v4

--- a/solution.py
+++ b/solution.py
@@ -77,7 +77,7 @@
     return change - (t_north - south_of(t_north, t_below)) * inverse
 
 
-def inner_kernel(band_ref, table_ref, thick_ref, u_ref, v_ref, tracer_ref, out_ref, sum_ref, last_ref, leading_ref):
+def inner_kernel(band_ref, table_ref, thick_ref, u_ref, v_ref, tracer_ref, out_ref, sum_ref, last_ref, leading_ref, near_ref, near_rest_ref):
     rows, width = thick_ref.shape[1:]
     geo = table_ref[band_ref[0]]
     thick, u, v = thick_ref[0], u_ref[0], v_ref[0]
@@ -85,7 +85,13 @@
     east, north, below = fluxes(geo, thick, u, v, nothing, nothing, nothing)
     inverse = geo[0:rows, 2:3]
     new = thick - (east - west_of(east)) - (north - south_of(north, below)) * inverse
-    out_ref[0, 0] = new
+    def store(field, value):
+        out_ref[field, 0] = value
+        ref, at = (near_ref, field) if field < 2 else (near_rest_ref, field - 2)
+        ref[at, 0, 0:1] = value[1:2]
+        ref[at, 0, 1:2] = value[rows - 2 : rows - 1]
+
+    store(0, new)
     last_ref[0, 0] = thick[rows - 1 : rows]
     last_ref[1, 0] = v[rows - 1 : rows]
     leading_ref[0, 0] = thick[0:1]
@@ -107,7 +113,7 @@
         last_ref[2 + c, 0] = q[rows - 1 : rows]
         leading_ref[4 + c, 0] = q[0:1]
         change = tracer_change(q, nothing, nothing, thick, u, v, nothing, east, north, below, inverse)
-        out_ref[1 + c, 0] = change * scale
+        store(1 + c, change * scale)
 
 
 def inner_step(band, table, thickness, wind_u, wind_v, tracers):
@@ -120,12 +126,14 @@
         inner_kernel,
         grid=(L,),
         in_specs=[SMEM, pl.BlockSpec(table.shape, lambda k: (0, 0, 0)), level, level, level, some(T, R)],
-        out_specs=[some(1 + T, R), pl.BlockSpec((R, N), lambda k: (0, 0)), some(2 + T, 1), some(4 + T, 1)],
+        out_specs=[some(1 + T, R), pl.BlockSpec((R, N), lambda k: (0, 0)), some(2 + T, 1), some(4 + T, 1), some(2, 2), some(T - 1, 2)],
         out_shape=[
             jax.ShapeDtypeStruct((1 + T, L, R, N), jnp.float32),
             jax.ShapeDtypeStruct((R, N), jnp.float32),
             jax.ShapeDtypeStruct((2 + T, L, 1, N), jnp.float32),
             jax.ShapeDtypeStruct((4 + T, L, 1, N), jnp.float32),
+            jax.ShapeDtypeStruct((2, L, 2, N), jnp.float32),
+            jax.ShapeDtypeStruct((T - 1, L, 2, N), jnp.float32),
         ],
         compiler_params=params(),
         cost_estimate=cost(130 * L * R * N, 4 * L * R * N * (8 + 2 * T)),
@@ -204,9 +212,9 @@
 def second_kernel(
     lat_rows, band_ref, table_ref, thick_ref, u_ref, v_ref, tracer_ref, up_ref, down_ref, cutoff_ref, high_ref, low_ref, *refs
 ):
-    wind_ref, edge_ref, new_wind = refs[-3:]
+    *wind_refs, edge_ref, new_wind = refs
     k = pl.program_id(0)
-    _, L, rows, width = wind_ref.shape
+    _, L, rows, width = new_wind.shape
     geo = table_ref[band_ref[0]]
     thick, u, v = thick_ref[0], u_ref[0], v_ref[0]
     thick_s, v_s = up_ref[0, 0], up_ref[1, 0]
@@ -244,13 +252,15 @@
         ]
         cutoff = jnp.broadcast_to(cutoff_ref[...][None], (2 * L, rows, LANES)).reshape(2 * L * rows, LANES)
         for a, piece in enumerate(filter_rows(pieces, cutoff, high_ref, low_ref)):
-            wind_ref[:, :, :, a * LANES : (a + 1) * LANES] = piece.reshape(2, L, rows, LANES)
+            piece = piece.reshape(2, L, rows, LANES)
+            for f in range(2):
+                wind_refs[f][0, :, :, a * LANES : (a + 1) * LANES] = piece[f]
         for f in range(2):
             for level in range(L):
-                store_edges(1 + f, level, wind_ref[f, level])
-
-
-def second_step(band, table, lat_rows, thickness, wind_u, wind_v, tracers, up, down, cutoff, wait):
+                store_edges(1 + f, level, wind_refs[f][0, level])
+
+
+def second_step(band, table, lat_rows, thickness, wind_u, wind_v, tracers, up, down, cutoff):
     L, R, N = thickness.shape
     T = tracers.shape[0]
     high, low = filter_tables(N)
@@ -261,11 +271,11 @@
         functools.partial(second_kernel, lat_rows),
         grid=(L,),
         in_specs=[SMEM, whole(table.shape), level, level, level, some(T, R), some(2 + T, 1), some(4 + T, 1)]
-        + [whole((R, LANES)), whole(high.shape), whole(low.shape)]
-        + after(wait),
-        out_specs=[whole((2, L, R, N)), whole((3 + T, L, 2, N))],
+        + [whole((R, LANES)), whole(high.shape), whole(low.shape)],
+        out_specs=[whole((1, L, R, N)), whole((1, L, R, N)), whole((3 + T, L, 2, N))],
         out_shape=[
-            jax.ShapeDtypeStruct((2, L, R, N), jnp.float32),
+            jax.ShapeDtypeStruct((1, L, R, N), jnp.float32),
+            jax.ShapeDtypeStruct((1, L, R, N), jnp.float32),
             jax.ShapeDtypeStruct((3 + T, L, 2, N), jnp.float32),
         ],
         scratch_shapes=[pltpu.VMEM((2, L, R, N), jnp.float32)],
@@ -274,7 +284,7 @@
         name="second_step",
     )(
         band, table, thickness, wind_u, wind_v, tracers, up, down,
-        jnp.broadcast_to(cutoff[:, None], (R, LANES)), jnp.asarray(high), jnp.asarray(low), *wait,
+        jnp.broadcast_to(cutoff[:, None], (R, LANES)), jnp.asarray(high), jnp.asarray(low),
     )
 
 
@@ -320,27 +330,21 @@
     return [jnp.minimum(jnp.maximum(top - low, 0.0), value) for _, _, low, value in sources]
 
 
-def remap_kernel(C, S, G, steps, fields, compact, with_thickness, carried, place_ref, weight_ref, *refs):
-    if carried:
-        for source_ref, copy_ref in zip(refs[:carried], refs[len(refs) - carried :]):
-            copy_ref[...] = source_ref[...]
-        refs = refs[carried : len(refs) - carried]
-    thick_refs, refs = refs[: G * S], refs[G * S :]
-    field_refs, refs = refs[: G * S], refs[G * S :]
-    other_refs, out_refs = refs[: (C - G) * S], refs[len(refs) - len(steps) - with_thickness :]
-    _, L, R, N = field_refs[0].shape
-    lev, sub = place_ref[0], place_ref[1]
+def remap_rows(place, weight_ref, counts, steps, thick_refs, field_refs, other_refs, store):
+    C, S = counts
+    G = len(thick_refs) // S
+    _, L, R, N = thick_refs[0].shape
+    lev, sub = place
     firsts = [(lax.rem(lev + s, C) * S + sub) * L for s in steps]
     weight_sum, weights, sums = weight_sums(weight_ref, firsts, L, C * S * L)
 
-    def tile(r, rows, columns):
-        at = slice(r, r + rows)
+    def tile(at, columns):
         thick = [[ref[0, m, at, columns] for m in range(L)] for ref in thick_refs]
         others = [
             functools.reduce(jnp.add, [ref[at, columns] for ref in other_refs[s * S : (s + 1) * S]])
             for s in range(C - G)
         ]
-        mass, sources = source_levels((lev, sub), (C, S), thick, others)
+        mass, sources = source_levels(place, counts, thick, others)
         unit = mass / weight_sum
         for index, s in enumerate(steps):
             below = covered(unit * sums[index][0], sources)
@@ -350,114 +354,156 @@
                 below = upto
                 target = unit * weights[index][i]
                 scale = 1.0 / target
-                for f, field in enumerate(fields):
-                    terms = [field_refs[g][field, m, at, columns] * w for (g, m, _, _), w in zip(sources, part)]
-                    total = functools.reduce(jnp.add, terms) * scale
-                    if compact and s > 0:
-                        lower, upper = max(r, 1), min(r + rows, R - 1)
-                        start = (f * L + i) * (R - 2) - 1
-                        out_refs[index][start + lower : start + upper, columns] = total[lower - r : upper - r]
-                    else:
-                        out_refs[index][f, i, at, columns] = total
-                if with_thickness and s == 0:
-                    out_refs[len(steps)][i, at, columns] = target
+                means = []
+                for refs in field_refs:
+                    terms = [refs[g][0][refs[g][1], m, at, columns] * w for (g, m, _, _), w in zip(sources, part)]
+                    means.append(functools.reduce(jnp.add, terms) * scale)
+                store(s, i, at, columns, target, means)
 
     rows = min(R, 8)
     for r in range(0, R, rows):
 
         def body(c, carry):
-            tile(r, rows, pl.ds(pl.multiple_of(c * LANES, LANES), LANES))
+            tile(slice(r, r + rows), pl.ds(pl.multiple_of(c * LANES, LANES), LANES))
             return carry
 
         lax.fori_loop(0, N // LANES, body, 0)
 
 
-def remap_parts(counts, place, weights, thick, sources, others, fields, steps, compact=False, with_thickness=False, carry=(), wait=()):
+def inner_part(at, margin, rows):
+    return max(at.start, margin), min(at.stop, rows - margin)
+
+
+def remap_kernel(counts, steps, fields, margin, sizes, place_ref, weight_ref, *refs):
     C, S = counts
-    _, L, R, N = sources[0].shape
+    thick_refs, refs = refs[:S], refs[S:]
+    bundles = []
+    for _ in range(sizes[0]):
+        bundles.append(refs[:S])
+        refs = refs[S:]
+    other_refs, out_refs = refs[: (C - 1) * S], refs[len(refs) - len(steps) :]
+    _, L, R, _ = thick_refs[0].shape
+    field_refs = [[(ref, index) for ref in bundles[which]] for which, index in fields]
+
+    def store(s, i, at, columns, target, means):
+        out_ref = out_refs[steps.index(s)]
+        for f, value in enumerate(means):
+            if s == 0:
+                out_ref[f, i, at, columns] = value
+            else:
+                lower, upper = inner_part(at, margin, R)
+                start = (f * L + i) * (R - 2 * margin) - margin
+                out_ref[start + lower : start + upper, columns] = value[lower - at.start : upper - at.start]
+
+    remap_rows(
+        (place_ref[0], place_ref[1]), weight_ref, counts, steps, thick_refs, field_refs, other_refs, store
+    )
+
+
+def remap_parts(counts, place, weights, thick, bundles, others, fields, steps, margin, wait=()):
+    C, S = counts
+    _, L, R, N = thick[0].shape
     F = len(fields)
     whole = jax.ShapeDtypeStruct((F, L, R, N), jnp.float32)
-    inner = jax.ShapeDtypeStruct((F * L * (R - 2), N), jnp.float32)
-    out_shape = [inner if compact and s > 0 else whole for s in steps]
-    if with_thickness:
-        out_shape = out_shape + [jax.ShapeDtypeStruct((L, R, N), jnp.float32)]
-    out_shape = out_shape + [jax.ShapeDtypeStruct(a.shape, a.dtype) for a in carry]
-    G = len(thick) // S
+    inner = jax.ShapeDtypeStruct((F * L * (R - 2 * margin), N), jnp.float32)
+    flat = [a for bundle in bundles for a in bundle]
     return pl.pallas_call(
-        functools.partial(remap_kernel, C, S, G, tuple(steps), tuple(fields), compact, with_thickness, len(carry)),
-        in_specs=[SMEM] * 2 + [VMEM] * (len(carry) + len(thick) + len(sources) + len(others)) + after(wait),
-        out_specs=[VMEM] * len(out_shape),
-        out_shape=out_shape,
+        functools.partial(remap_kernel, counts, tuple(steps), tuple(fields), margin, (len(bundles),)),
+        in_specs=[SMEM] * 2 + [VMEM] * (len(thick) + len(flat) + len(others)) + after(wait),
+        out_specs=[VMEM] * len(steps),
+        out_shape=[whole if s == 0 else inner for s in steps],
         compiler_params=params(),
-        cost_estimate=cost(len(steps) * G * S * L * L * R * N * (5 + 2 * F), 4 * R * N * L * (F + 1) * (S * G + len(steps))),
+        cost_estimate=cost(len(steps) * S * L * L * R * N * (5 + 2 * F), 4 * R * N * L * (F + 1) * (S + len(steps))),
         name="remap_parts",
-    )(place, weights, *carry, *thick, *sources, *others, *wait)
-
-
-def finish_kernel(C, S, chunks, place_ref, weight_ref, *refs):
+    )(place, weights, *thick, *flat, *others, *wait)
+
+
+def remap_edge_kernel(counts, near_fields, place_ref, weight_ref, *refs):
+    G = counts[0] * counts[1]
+    edge_refs, near_refs, rest_refs = refs[:G], refs[G : 2 * G], refs[2 * G : 3 * G]
+    edge_out_ref, thick_out_ref, near_out_ref = refs[-3:]
+    place = (place_ref[0], place_ref[1])
+
+    def store_edge(s, i, at, columns, target, means):
+        thick_out_ref[i, at, columns] = target
+        for f, value in enumerate(means):
+            edge_out_ref[f, i, at, columns] = value
+
+    def store_near(s, i, at, columns, target, means):
+        for f, value in enumerate(means):
+            near_out_ref[f, i, at, columns] = value
+
+    fields = [[(ref, f) for ref in edge_refs] for f in range(1, edge_refs[0].shape[0])]
+    remap_rows(place, weight_ref, counts, (0,), edge_refs, fields, [], store_edge)
+    bundles = (near_refs, rest_refs)
+    fields = [[(ref, index) for ref in bundles[which]] for which, index in near_fields]
+    remap_rows(place, weight_ref, counts, (0,), near_refs, fields, [], store_near)
+
+
+def remap_edges(counts, place, weights, edges, near, near_rest, wait=()):
+    F, L, R, N = edges[0].shape
+    T = F - 3
+    near_fields = tuple((0, 1) if f == 0 else (1, f - 1) for f in range(T))
+    operands = [*edges, *near, *near_rest]
+    return pl.pallas_call(
+        functools.partial(remap_edge_kernel, counts, near_fields),
+        in_specs=[SMEM] * 2 + [VMEM] * len(operands) + after(wait),
+        out_specs=[VMEM] * 3,
+        out_shape=[
+            jax.ShapeDtypeStruct((F - 1, L, R, N), jnp.float32),
+            jax.ShapeDtypeStruct((L, R, N), jnp.float32),
+            jax.ShapeDtypeStruct((T, L, R, N), jnp.float32),
+        ],
+        compiler_params=params(),
+        cost_estimate=cost(len(edges) * L * L * R * N * 40, 4 * R * N * L * len(operands) * F),
+        name="remap_edges",
+    )(place, weights, *operands, *wait)
+
+
+def finish_kernel(counts, margin, place_ref, weight_ref, *refs):
+    C, S = counts
     group_refs, refs = refs[:S], refs[S:]
     other_refs, refs = refs[: (C - 1) * S], refs[(C - 1) * S :]
-    *arrived_refs, edge_ref, thick_edge_ref, out_ref, thick_out_ref = refs
-    T, L, R, N = out_ref.shape
-    lev, sub = place_ref[0], place_ref[1]
-    weight_sum, weights, sums = weight_sums(weight_ref, [(lev * S + sub) * L], L, C * S * L)
-    where = [(chunk, at) for chunk, count in enumerate(chunks) for at in range(count)]
-
-    def tile(r, columns):
-        at = slice(r, r + 8)
-        thick = [[ref[0, m, at, columns] for m in range(L)] for ref in group_refs]
-        others = [
-            functools.reduce(jnp.add, [ref[at, columns] for ref in other_refs[s * S : (s + 1) * S]])
-            for s in range(C - 1)
-        ]
-        mass, sources = source_levels((lev, sub), (C, S), thick, others)
-        unit = mass / weight_sum
-        below = covered(unit * sums[0][0], sources)
-        lower, upper = max(r, 1), min(r + 8, R - 1)
-        for i in range(L):
-            upto = covered(unit * sums[0][i + 1], sources)
-            part = [a - b for a, b in zip(upto, below)]
-            below = upto
-            target = unit * weights[0][i]
-            thick_out_ref[i, at, columns] = target
-            scale = 1.0 / target
-            for f in range(T):
-                terms = [group_refs[g][1 + f, m, at, columns] * w for (g, m, _, _), w in zip(sources, part)]
-                total = (functools.reduce(jnp.add, terms) * scale)[lower - r : upper - r]
-                chunk, place = where[f]
-                start = (place * L + i) * (R - 2) - 1
-                for s in range(C - 1):
-                    total = total + arrived_refs[chunk * (C - 1) + s][start + lower : start + upper, columns]
-                out_ref[f, i, lower:upper, columns] = total
-
-    for r in range(0, R, 8):
-
-        def body(c, carry):
-            tile(r, pl.ds(pl.multiple_of(c * LANES, LANES), LANES))
-            return carry
-
-        lax.fori_loop(0, N // LANES, body, 0)
+    *arrived_refs, near_ref, edge_ref, thick_edge_ref, out_ref, thick_out_ref, token_ref = refs
+    token_ref[...] = jnp.zeros_like(token_ref)
+    T, L, R, _ = out_ref.shape
+
+    def store(s, i, at, columns, target, means):
+        thick_out_ref[i, at, columns] = target
+        lower, upper = inner_part(at, margin, R)
+        for f, value in enumerate(means):
+            total = value[lower - at.start : upper - at.start]
+            start = (f * L + i) * (R - 2 * margin) - margin
+            for ref in arrived_refs:
+                total = total + ref[start + lower : start + upper, columns]
+            out_ref[f, i, lower:upper, columns] = total
+
+    fields = [[(ref, 1 + f) for ref in group_refs] for f in range(T)]
+    remap_rows((place_ref[0], place_ref[1]), weight_ref, counts, (0,), group_refs, fields, other_refs, store)
     for i in range(L):
         for row, j in ((0, 0), (R - 1, 1)):
             thick_out_ref[i, row : row + 1] = thick_edge_ref[i, j : j + 1]
             for f in range(T):
                 out_ref[f, i, row : row + 1] = edge_ref[2 + f, i, j : j + 1]
-
-
-def finish_tracers(counts, place, weights, group, others, arrived, edge, thick_edge):
+        for row, j in ((1, 0), (R - 2, 1)):
+            for f in range(T):
+                out_ref[f, i, row : row + 1] = near_ref[f, i, j : j + 1]
+
+
+def finish_tracers(counts, place, weights, group, others, arrived, near, edge, thick_edge):
+    margin = 2
     C, S = counts
     T = group[0].shape[0] - 1
     _, L, R, N = group[0].shape
-    chunks = tuple(a[0].shape[0] // (L * (R - 2)) for a in arrived)
-    flat = [a for chunk in arrived for a in chunk]
-    operands = list(group) + list(others) + flat + [edge, thick_edge]
+    operands = list(group) + list(others) + list(arrived) + [near, edge, thick_edge]
     return pl.pallas_call(
-        functools.partial(finish_kernel, C, S, chunks),
+        functools.partial(finish_kernel, counts, margin),
         in_specs=[SMEM] * 2 + [VMEM] * len(operands),
-        out_specs=[VMEM] * 2,
+        out_specs=[VMEM] * 3,
         out_shape=[
             jax.ShapeDtypeStruct((T, L, R, N), jnp.float32),
             jax.ShapeDtypeStruct((L, R, N), jnp.float32),
+            jax.ShapeDtypeStruct((8, LANES), jnp.float32),
         ],
         compiler_params=params(),
         cost_estimate=cost(S * L * L * R * N * (5 + 2 * T), 4 * R * N * L * (T + 1) * (S + 2)),
@@ -466,9 +512,9 @@
 
 
 def finish_winds_kernel(count, own_ref, edge_ref, *refs):
-    arrived_refs, (u_ref, v_ref) = refs[:count], refs[-2:]
+    arrived_refs, out_refs = refs[:count], refs[-2:]
     _, L, R, N = own_ref.shape
-    for f, out_ref in enumerate((u_ref, v_ref)):
+    for f, out_ref in enumerate(out_refs):
         for i in range(L):
             start = (f * L + i) * (R - 2)
             total = own_ref[f, i, 1 : R - 1]
@@ -480,16 +526,32 @@
 
 
 def finish_winds(own, arrived, edge, wait):
-    shape = jax.ShapeDtypeStruct(own.shape[1:], jnp.float32)
     return pl.pallas_call(
         functools.partial(finish_winds_kernel, len(arrived)),
         in_specs=[VMEM] * (2 + len(arrived)) + after(wait),
         out_specs=[VMEM] * 2,
-        out_shape=[shape] * 2,
+        out_shape=[jax.ShapeDtypeStruct(own.shape[1:], jnp.float32)] * 2,
         compiler_params=params(),
         cost_estimate=cost(own.size, 12 * own.size),
         name="finish_winds",
     )(own, edge, *arrived, *wait)
+
+
+def hand_on_kernel(count, *refs):
+    for source_ref, copy_ref in zip(refs[:count], refs[len(refs) - count :]):
+        copy_ref[...] = source_ref[...]
+
+
+def hand_on(arrays, wait):
+    return pl.pallas_call(
+        functools.partial(hand_on_kernel, len(arrays)),
+        in_specs=[VMEM] * len(arrays) + after(wait),
+        out_specs=[VMEM] * len(arrays),
+        out_shape=[jax.ShapeDtypeStruct(a.shape, a.dtype) for a in arrays],
+        compiler_params=params(),
+        cost_estimate=cost(1e10, 1e9),
+        name="hand_on",
+    )(*arrays, *wait)
 
 
 def shifted(value, lev_count, sub_count, s, t):
@@ -528,34 +590,34 @@
 
     remap = functools.partial(remap_parts, (C, S), place, level_weights)
 
-    inner, own_sum, last, leading = inner_step(band, table, thickness, wind_u, wind_v, tracers)
+    inner, own_sum, last, leading, near, near_rest = inner_step(band, table, thickness, wind_u, wind_v, tracers)
     others = [send(own_sum, s=s, t=t) for s in away for t in range(S)]
     group = with_others_of_chip(inner)
-    first_away = remap(group, group, others, range(1, 2), away, compact=True)
-    *rest_away, last, leading = remap(
-        group, group, others, range(2, 1 + T), away, compact=True, carry=(last, leading), wait=first_away[:1]
-    )
-    arrived = [sent(first_away), sent(rest_away)]
-
+    near = [near] + [send(near, s=s, t=0) for s in away]
+    near_rest = [near_rest] + [send(near_rest, s=s, t=0) for s in away]
+    tracer_fields = [(0, 1 + c) for c in range(T)]
+    away_parts = remap(group, [group], others, tracer_fields, away, 2)
+    arrived = sent(away_parts)
+
+    last, leading = hand_on((last, leading), [away_parts[0], *near[1:2], *near_rest[1:2]])
     up = lax.ppermute(last, "lat", northward)
     down = lax.ppermute(leading, "lat", southward)
-    winds, edge = second_step(
-        band, table, lat_rows, thickness, wind_u, wind_v, tracers, up, down, cutoff, [rest_away[0], *arrived[0][:1]]
-    )
+    u, v, edge = second_step(band, table, lat_rows, thickness, wind_u, wind_v, tracers, up, down, cutoff)
     edges = [edge] + [send(edge, s=s, t=0) for s in away]
-    winds_own, *winds_away = remap(
-        group, with_others_of_chip(winds), others, range(2), range(C), compact=True, wait=arrived[1][:1]
-    )
+    winds = [with_others_of_chip(u), with_others_of_chip(v)]
+    winds_own, *winds_away = remap(group, winds, others, [(0, 0), (1, 0)], range(C), 1, wait=arrived[:1])
     winds_arrived = sent(winds_away)
-    edges = [a for own in edges for a in with_others_of_chip(own)]
-    edge_out, thick_edge = remap(
-        edges, edges, [], range(1, 3 + T), (0,), with_thickness=True, wait=winds_away[:1]
-    )
-
-    tracers_out, thickness_out = finish_tracers(
-        (C, S), place, level_weights, group, others, arrived, edge_out, thick_edge
-    )
-    u_out, v_out = finish_winds(winds_own, winds_arrived, edge_out, [tracers_out])
+    near, near_rest, edges = (
+        [a for own in sources for a in with_others_of_chip(own)] for sources in (near, near_rest, edges)
+    )
+    edge_out, thick_edge, near_out = remap_edges(
+        (C, S), place, level_weights, edges, near, near_rest, wait=winds_away[:1]
+    )
+
+    tracers_out, thickness_out, token = finish_tracers(
+        (C, S), place, level_weights, group, others, arrived, near_out, edge_out, thick_edge
+    )
+    u_out, v_out = finish_winds(winds_own, winds_arrived, edge_out, [token])
     return thickness_out, u_out, v_out, tracers_out
 
 

time: 57.2 us -> 55.1 us (0.963)
  waiting for transfers between devices: 20.7 us -> 13.6 us
  starting transfers between devices: 14.4 us -> 18.2 us
  Pallas kernels: 19.7 us -> 20.7 us
    ppermute x5 -> x6, waiting for transfers between devices: 15.5 us -> 7.92 us  [shifted(): lax.ppermute(value, 'lev', [(i, (i + s) % lev_count) for i in range(lev_c...]
    ppermute x4 -> x9, starting transfers between devices: 0.59 us -> 2.37 us  [shifted(): lax.ppermute(value, 'sub', [(i, (i + t) % sub_count) for i in range(sub_c...]
    ppermute x5 -> x6, starting transfers between devices: 7.87 us -> 9.57 us  [shifted(): lax.ppermute(value, 'lev', [(i, (i + s) % lev_count) for i in range(lev_c...]
    pallas_call x5, Pallas kernels: 11.3 us -> 12.2 us  [the longest x2 5.2 us: remap_parts(): pl.pallas_call(functools.partial(remap_kernel, counts, tuple(steps), tupl...]
    ppermute x4 -> x9, waiting for transfers between devices: 1.53 us -> 2.07 us  [shifted(): lax.ppermute(value, 'sub', [(i, (i + t) % sub_count) for i in range(sub_c...]
    unnamed x20 -> x30, local copies, waits for them, and re-layouts: 1.32 us -> 1.37 us
  transfers between devices with their start and end apart: 12 -> 18, of which waited for: 7 -> 9; matrix products, arithmetic and copies ran while one was open for 0% -> 0% of each run, Pallas kernels for 24% -> 29%
where the time goes in v5:
time: 55.1 us; the launch traced here: 54.8 us
  Pallas kernels  20.7 us (38%)
  starting transfers between devices  18.2 us (33%)
  waiting for transfers between devices  13.6 us (25%)
  local copies, waits for them, and re-layouts  1.44 us (3%)
  between operations  0.87 us (2%)
    ppermute x6, starting transfers between devices, shifted(): lax.ppermute(value, 'lev', [(i, (i + s) % lev_count) for i in range(lev_c...  9.57 us
    ppermute x6, waiting for transfers between devices, shifted(): lax.ppermute(value, 'lev', [(i, (i + s) % lev_count) for i in range(lev_c...  7.92 us
    pallas_call x2, Pallas kernels, remap_parts(): pl.pallas_call(functools.partial(remap_kernel, counts, tuple(steps), tupl...  5.2 us
    ppermute x1, starting transfers between devices, per_device(): up = lax.ppermute(last, 'lat', northward)  4.55 us
    pallas_call x1, Pallas kernels, inner_step(): pl.pallas_call(inner_kernel, grid=(L,), in_specs=[SMEM, pl.BlockSpec(tabl...  3.88 us
    pallas_call x1, Pallas kernels, remap_edges(): pl.pallas_call(functools.partial(remap_edge_kernel, counts, near_fields),...  3.66 us
    pallas_call x1, Pallas kernels, second_step(): pl.pallas_call(functools.partial(second_kernel, lat_rows), grid=(L,), in_...  3.65 us
    pallas_call x1, Pallas kernels, finish_tracers(): pl.pallas_call(functools.partial(finish_kernel, counts, margin), in_specs...  3.32 us
  transfers between devices with their start and end apart: 18, of which 9 were waited for; matrix products, arithmetic and copies ran while one was open for 0% of the time, Pallas kernels for 29%

profile of v5, /device:TPU:0, one launch (start us, length us, event | category | flops | bytes accessed | tf_op | source)
XLA Modules:
  0.0 54.8 jit_solution(5946381183785293840)
XLA Ops:
  0.6 3.9 %inner_step.1 = (f32[5,4,16,1152]{3,2,1,0:T(8,128)S(1)}, f32[16,1152]{1,0:T(8,128)S(1)}, f32[6,4,1,1152]{3,2,1,0:T(1,128)S(1)}, f32[8,4,1,1152]{3,2,1,0:T(1,128)...) custom-call(s32[1]{0:T(128)} %bitcast.2.band_ref, f32[4,24,128]{2,1,0:T(8,128)} %constant.17.clone.table_ref, ...), custom_call_target="tpu_custom_call" | custom-call | flops 9584640 | bytes 4718592 | tf_op jit(solution)/shard_map/inner_step/pallas_call | solution.py:125
  4.5 0.7 %copy-done.10 = f32[8,4,1,1152]{3,2,1,0:T(1,128)} copy-done((f32[8,4,1,1152]{3,2,1,0:T(1,128)}, f32[8,4,1,1152]{3,2,1,0:T(1,128)S(1)}, u32[]{:S(2)}) %copy-start.10) | copy-done | bytes 147480
  5.2 0.6 %copy-done.12 = f32[6,4,1,1152]{3,2,1,0:T(1,128)} copy-done((f32[6,4,1,1152]{3,2,1,0:T(1,128)}, f32[6,4,1,1152]{3,2,1,0:T(1,128)S(1)}, u32[]{:S(2)}) %copy-start.12) | copy-done | bytes 110616
  6.3 2.5 %collective-permute-start.1 = (f32[16,1152]{1,0:T(8,128)S(1)}, f32[16,1152]{1,0:T(8,128)S(1)}, u32[]{:S(2)}, u32[]{:S(2)}) collective-permute-start(f32[16,1152]{1,0:T(8,128)S(1)} %get-tuple-element.26), channel_id=1, source_target_pairs={{0,2},{2,0},{1,3},{3,1},{4,6},{6,4},{5,7},{7,5},{8,10},{10,8},{9,1... | collective-permute-start | bytes 221192 | tf_op jit(solution)/shard_map/ppermute | solution.py:559
  8.9 1.7 %collective-permute-start.5 = (f32[3,4,2,1152]{3,2,1,0:T(2,128)S(1)}, f32[3,4,2,1152]{3,2,1,0:T(2,128)S(1)}, u32[]{:S(2)}, u32[]{:S(2)}) collective-permute-start(f32[3,4,2,1152]{3,2,1,0:T(2,128)S(1)} %get-tuple-element.30.refs_8_), channel_id=1, source_target_pairs={{0,2},{2,0},{1,3},{3,1},{4,6},{6,4},{5,7},{7,5},{8,10},{10,8},{9,1... | collective-permute-start | bytes 331784 | tf_op jit(solution)/shard_map/ppermute | solution.py:559
  11.0 0.7 %collective-permute-done.1.refs_4_.refs_6_.refs_2_ = f32[16,1152]{1,0:T(8,128)S(1)} collective-permute-done((f32[16,1152]{1,0:T(8,128)S(1)}, f32[16,1152]{1,0:T(8,128)S(1)}, u32[]{:S(2)}, u32[]{:S(2)}) %collective-permute-start.1) | collective-permute-done | bytes 73760 | tf_op jit(solution)/shard_map/ppermute | solution.py:559
  11.7 1.3 %collective-permute-done.2.refs_5_.refs_7_.refs_3_ = f32[16,1152]{1,0:T(8,128)S(1)} collective-permute-done((f32[16,1152]{1,0:T(8,128)S(1)}, f32[16,1152]{1,0:T(8,128)S(1)}, u32[]{:S(2)}, u32[]{:S(2)}) %collective-permute-start.2) | collective-permute-done | bytes 73760 | tf_op jit(solution)/shard_map/ppermute | solution.py:567
  13.0 2.0 %remap_parts.2.refs_2_ = f32[192,1152]{1,0:T(8,128)S(1)} custom-call(s32[2]{0:T(128)S(1)} %pad_add_fusion.place_ref, f32[16]{0:T(128)S(1)} %copy-done.9, f32[5,4,16,1152]{3,2,1,0:T(8,128)S(1)} %get-tuple-element.25.refs_0_.refs_2_, f32[5,4,16,1152]{3,2,1,0:T(8,128)S(1)} %collective-permute-done.refs_1_.refs_3_, ...), custom_call_target="tpu_custom_call" | custom-call | flops 7667712 | bytes 4423680 | tf_op jit(solution)/shard_map/remap_parts/pallas_call | solution.py:410
  15.0 1.7 %collective-permute-start.3 = (f32[192,1152]{1,0:T(8,128)S(1)}, f32[192,1152]{1,0:T(8,128)S(1)}, u32[]{:S(2)}, u32[]{:S(2)}) collective-permute-start(f32[192,1152]{1,0:T(8,128)S(1)} %remap_parts.2.refs_2_), channel_id=1, source_target_pairs={{0,2},{2,0},{1,3},{3,1},{4,6},{6,4},{5,7},{7,5},{8,10},{10,8},{9,1... | collective-permute-start | bytes 2654216 | tf_op jit(solution)/shard_map/ppermute | solution.py:559
  16.7 0.6 %collective-permute-done.4.refs_3_.refs_6_ = f32[2,4,2,1152]{3,2,1,0:T(2,128)S(1)} collective-permute-done((f32[2,4,2,1152]{3,2,1,0:T(2,128)S(1)}, f32[2,4,2,1152]{3,2,1,0:T(2,128)S(1)}, u32[]{:S(2)}, u32[]{:S(2)}) %collective-permute-start.4) | collective-permute-done | bytes 73760 | tf_op jit(solution)/shard_map/ppermute | solution.py:559
  17.5 1.6 %collective-permute-start.7 = (f32[8,4,1,1152]{3,2,1,0:T(1,128)S(1)}, f32[8,4,1,1152]{3,2,1,0:T(1,128)S(1)}, u32[]{:S(2)}, u32[]{:S(2)}) collective-permute-start(f32[8,4,1,1152]{3,2,1,0:T(1,128)S(1)} %get-tuple-element.32), channel_id=1, source_target_pairs={{4,0},{8,4},{12,8},{5,1},{9,5},{13,9},{6,2},{10,6},{14,10},{7,3},{... | collective-permute-start | bytes 442376 | tf_op jit(solution)/shard_map/ppermute | solution.py:604
  19.0 4.6 %collective-permute-start.6 = (f32[6,4,1,1152]{3,2,1,0:T(1,128)S(1)}, f32[6,4,1,1152]{3,2,1,0:T(1,128)S(1)}, u32[]{:S(2)}, u32[]{:S(2)}) collective-permute-start(f32[6,4,1,1152]{3,2,1,0:T(1,128)S(1)} %get-tuple-element.31), channel_id=1, source_target_pairs={{0,4},{4,8},{8,12},{1,5},{5,9},{9,13},{2,6},{6,10},{10,14},{3,7},{... | collective-permute-start | bytes 331784 | tf_op jit(solution)/shard_map/ppermute | solution.py:603
  23.6 2.3 %collective-permute-done.6.up_ref = f32[6,4,1,1152]{3,2,1,0:T(1,128)S(1)} collective-permute-done((f32[6,4,1,1152]{3,2,1,0:T(1,128)S(1)}, f32[6,4,1,1152]{3,2,1,0:T(1,128)S(1)}, u32[]{:S(2)}, u32[]{:S(2)}) %collective-permute-start.6) | collective-permute-done | bytes 110624 | tf_op jit(solution)/shard_map/ppermute | solution.py:603
  26.0 3.7 %second_step.1 = (f32[1,4,16,1152]{3,2,1,0:T(8,128)S(1)}, f32[1,4,16,1152]{3,2,1,0:T(8,128)S(1)}, f32[7,4,2,1152]{3,2,1,0:T(2,128)S(1)}) custom-call(s32[1]{0:T(128)} %bitcast.2.band_ref, f32[4,24,128]{2,1,0:T(8,128)S(1)} %copy-done.8, f32[4,16,1152]{2,1,0:T(8,128)S(1)} %copy-done.3, f32[4,16,1152]{2,1,0:T(8,128)S(1)} %copy-done.4, ...), custom_call_target="tpu_custom_call" | custom-call | flops 503316480 | bytes 3538944 | tf_op jit(solution)/shard_map/second_step/pallas_call | solution.py:270
  30.3 1.7 %collective-permute-start.9 = (f32[7,4,2,1152]{3,2,1,0:T(2,128)S(1)}, f32[7,4,2,1152]{3,2,1,0:T(2,128)S(1)}, u32[]{:S(2)}, u32[]{:S(2)}) collective-permute-start(f32[7,4,2,1152]{3,2,1,0:T(2,128)S(1)} %get-tuple-element.33.refs_0_), channel_id=1, source_target_pairs={{0,2},{2,0},{1,3},{3,1},{4,6},{6,4},{5,7},{7,5},{8,10},{10,8},{9,1... | collective-permute-start | bytes 774152 | tf_op jit(solution)/shard_map/ppermute | solution.py:559
  31.9 5.6 %collective-permute-done.3.refs_8_.refs_4_ = f32[192,1152]{1,0:T(8,128)S(1)} collective-permute-done((f32[192,1152]{1,0:T(8,128)S(1)}, f32[192,1152]{1,0:T(8,128)S(1)}, u32[]{:S(2)}, u32[]{:S(2)}) %collective-permute-start.3) | collective-permute-done | bytes 884768 | tf_op jit(solution)/shard_map/ppermute | solution.py:559
  37.5 3.2 %remap_parts.3 = (f32[2,4,16,1152]{3,2,1,0:T(8,128)S(1)}, f32[112,1152]{1,0:T(8,128)S(1)}) custom-call(s32[2]{0:T(128)S(1)} %pad_add_fusion.place_ref, f32[16]{0:T(128)S(1)} %copy-done.9, f32[5,4,16,1152]{3,2,1,0:T(8,128)S(1)} %get-tuple-element.25.refs_0_.refs_2_, f32[5,4,16,1152]{3,2,1,0:T(8,128)} %copy-done, ...), custom_call_target="tpu_custom_call" | custom-call | flops 10616832 | bytes 3538944 | tf_op jit(solution)/shard_map/remap_parts/pallas_call | solution.py:410
  40.8 1.7 %collective-permute-start.17 = (f32[112,1152]{1,0:T(8,128)S(1)}, f32[112,1152]{1,0:T(8,128)S(1)}, u32[]{:S(2)}, u32[]{:S(2)}) collective-permute-start(f32[112,1152]{1,0:T(8,128)S(1)} %get-tuple-element.36.refs_12_), channel_id=1, source_target_pairs={{0,2},{2,0},{1,3},{3,1},{4,6},{6,4},{5,7},{7,5},{8,10},{10,8},{9,1... | collective-permute-start | bytes 1548296 | tf_op jit(solution)/shard_map/ppermute | solution.py:559
  43.5 1.1 %collective-permute-done.11.refs_5_ = f32[2,4,2,1152]{3,2,1,0:T(2,128)S(1)} collective-permute-done((f32[2,4,2,1152]{3,2,1,0:T(2,128)S(1)}, f32[2,4,2,1152]{3,2,1,0:T(2,128)S(1)}, u32[]{:S(2)}, u32[]{:S(2)}) %collective-permute-start.11) | collective-permute-done | bytes 73760 | tf_op jit(solution)/shard_map/ppermute | solution.py:561
  45.1 0.9 %collective-permute-done.12.refs_7_ = f32[2,4,2,1152]{3,2,1,0:T(2,128)S(1)} collective-permute-done((f32[2,4,2,1152]{3,2,1,0:T(2,128)S(1)}, f32[2,4,2,1152]{3,2,1,0:T(2,128)S(1)}, u32[]{:S(2)}, u32[]{:S(2)}) %collective-permute-start.12) | collective-permute-done | bytes 73760 | tf_op jit(solution)/shard_map/ppermute | solution.py:561
  46.1 3.7 %remap_edges.1 = (f32[6,4,2,1152]{3,2,1,0:T(2,128)S(1)}, f32[4,2,1152]{2,1,0:T(2,128)S(1)}, f32[4,4,2,1152]{3,2,1,0:T(2,128)S(1)}) custom-call(s32[2]{0:T(128)S(1)} %pad_add_fusion.place_ref, f32[16]{0:T(128)S(1)} %copy-done.9, f32[7,4,2,1152]{3,2,1,0:T(2,128)S(1)} %get-tuple-element.33.refs_0_, f32[7,4,2,1152]{3,2,1,0:T(2,128)S(1)} %collective-permute-done.8.refs_1_, ...), custom_call_target="tpu_custom_call" | custom-call | flops 5898240 | bytes 3096576 | tf_op jit(solution)/shard_map/remap_edges/pallas_call | solution.py:448
  49.7 3.3 %finish_tracers.1 = (f32[4,4,16,1152]{3,2,1,0:T(8,128)}, f32[4,16,1152]{2,1,0:T(8,128)}, f32[8,128]{1,0:T(8,128)S(1)}) custom-call(s32[2]{0:T(128)S(1)} %pad_add_fusion.place_ref, f32[16]{0:T(128)S(1)} %copy-done.9, f32[5,4,16,1152]{3,2,1,0:T(8,128)S(1)} %get-tuple-element.25.refs_0_.refs_2_, f32[5,4,16,1152]{3,2,1,0:T(8,128)S(1)} %copy-done.1, ...), custom_call_target="tpu_custom_call" | custom-call | flops 7667712 | bytes 5898240 | tf_op jit(solution)/shard_map/finish_tracers/pallas_call | solution.py:499
  53.1 0.9 %collective-permute-done.17.refs_0_ = f32[112,1152]{1,0:T(8,128)S(1)} collective-permute-done((f32[112,1152]{1,0:T(8,128)S(1)}, f32[112,1152]{1,0:T(8,128)S(1)}, u32[]{:S(2)}, u32[]{:S(2)}) %collective-permute-start.17) | collective-permute-done | bytes 516128 | tf_op jit(solution)/shard_map/ppermute | solution.py:559
  53.9 0.9 %finish_winds.1 = (f32[4,16,1152]{2,1,0:T(8,128)}, f32[4,16,1152]{2,1,0:T(8,128)}) custom-call(f32[2,4,16,1152]{3,2,1,0:T(8,128)S(1)} %get-tuple-element.41.own_ref, f32[6,4,2,1152]{3,2,1,0:T(2,128)S(1)} %get-tuple-element.38.refs_6_.edge_ref, f32[112,1152]{1,0:T(8,128)S(1)} %collective-permute-done.17.refs_0_, f32[8,128]{1,0:T(8,128)S(1)} %get-tuple-element.42.refs_1_), custom_call_target="tpu_custom_call" | custom-call | flops 147456 | bytes 1769472 | tf_op jit(solution)/shard_map/finish_winds/pallas_call | solution.py:529
  (52 shorter events, 3.3 us)
Async XLA Ops:
  0.6 12.4 %copy-start.9 = (f32[16]{0:T(128)S(1)}, f32[16]{0:T(128)}, u32[]{:S(2)}) copy-start(f32[16]{0:T(128)} %weight_ref.7) | copy-start | bytes 196
  5.8 7.2 %collective-permute-start = (f32[5,4,16,1152]{3,2,1,0:T(8,128)S(1)}, f32[5,4,16,1152]{3,2,1,0:T(8,128)S(1)}, u32[]{:S(2)}, u32[]{:S(2)}) collective-permute-start(f32[5,4,16,1152]{3,2,1,0:T(8,128)S(1)} %get-tuple-element.25.refs_0_.refs_2_), channel_id=1, source_target_pairs={{0,1},{1,0},{2,3},{3,2},{4,5},{5,4},{6,7},{7,6},{8,9},{9,8},{10,11... | collective-permute-start | bytes 4423688 | tf_op jit(solution)/shard_map/ppermute | solution.py:561
  6.3 5.4 %collective-permute-start.1 = (f32[16,1152]{1,0:T(8,128)S(1)}, f32[16,1152]{1,0:T(8,128)S(1)}, u32[]{:S(2)}, u32[]{:S(2)}) collective-permute-start(f32[16,1152]{1,0:T(8,128)S(1)} %get-tuple-element.26), channel_id=1, source_target_pairs={{0,2},{2,0},{1,3},{3,1},{4,6},{6,4},{5,7},{7,5},{8,10},{10,8},{9,1... | collective-permute-start | bytes 221192 | tf_op jit(solution)/shard_map/ppermute | solution.py:559
  8.8 4.2 %collective-permute-start.2 = (f32[16,1152]{1,0:T(8,128)S(1)}, f32[16,1152]{1,0:T(8,128)S(1)}, u32[]{:S(2)}, u32[]{:S(2)}) collective-permute-start(f32[16,1152]{1,0:T(8,128)S(1)} %get-tuple-element.26), channel_id=1, source_target_pairs={{0,3},{1,2},{2,1},{3,0},{4,7},{5,6},{6,5},{7,4},{8,11},{9,10},{10,... | collective-permute-start | bytes 221192 | tf_op jit(solution)/shard_map/ppermute | solution.py:567
  8.9 8.4 %collective-permute-start.5 = (f32[3,4,2,1152]{3,2,1,0:T(2,128)S(1)}, f32[3,4,2,1152]{3,2,1,0:T(2,128)S(1)}, u32[]{:S(2)}, u32[]{:S(2)}) collective-permute-start(f32[3,4,2,1152]{3,2,1,0:T(2,128)S(1)} %get-tuple-element.30.refs_8_), channel_id=1, source_target_pairs={{0,2},{2,0},{1,3},{3,1},{4,6},{6,4},{5,7},{7,5},{8,10},{10,8},{9,1... | collective-permute-start | bytes 331784 | tf_op jit(solution)/shard_map/ppermute | solution.py:559
  10.6 6.7 %collective-permute-start.4 = (f32[2,4,2,1152]{3,2,1,0:T(2,128)S(1)}, f32[2,4,2,1152]{3,2,1,0:T(2,128)S(1)}, u32[]{:S(2)}, u32[]{:S(2)}) collective-permute-start(f32[2,4,2,1152]{3,2,1,0:T(2,128)S(1)} %get-tuple-element.29.refs_4_), channel_id=1, source_target_pairs={{0,2},{2,0},{1,3},{3,1},{4,6},{6,4},{5,7},{7,5},{8,10},{10,8},{9,1... | collective-permute-start | bytes 221192 | tf_op jit(solution)/shard_map/ppermute | solution.py:559
  15.0 22.5 %collective-permute-start.3 = (f32[192,1152]{1,0:T(8,128)S(1)}, f32[192,1152]{1,0:T(8,128)S(1)}, u32[]{:S(2)}, u32[]{:S(2)}) collective-permute-start(f32[192,1152]{1,0:T(8,128)S(1)} %remap_parts.2.refs_2_), channel_id=1, source_target_pairs={{0,2},{2,0},{1,3},{3,1},{4,6},{6,4},{5,7},{7,5},{8,10},{10,8},{9,1... | collective-permute-start | bytes 2654216 | tf_op jit(solution)/shard_map/ppermute | solution.py:559
  17.3 8.6 %copy-start.2 = (f32[4,4,16,1152]{3,2,1,0:T(8,128)S(1)}, f32[4,4,16,1152]{3,2,1,0:T(8,128)}, u32[]{:S(2)}) copy-start(f32[4,4,16,1152]{3,2,1,0:T(8,128)} %tracer_ref.3) | copy-start | bytes 3538948
  17.3 8.6 %copy-start.3 = (f32[4,16,1152]{2,1,0:T(8,128)S(1)}, f32[4,16,1152]{2,1,0:T(8,128)}, u32[]{:S(2)}) copy-start(f32[4,16,1152]{2,1,0:T(8,128)} %thick_ref.3) | copy-start | bytes 884740
  17.4 8.6 %copy-start.4 = (f32[4,16,1152]{2,1,0:T(8,128)S(1)}, f32[4,16,1152]{2,1,0:T(8,128)}, u32[]{:S(2)}) copy-start(f32[4,16,1152]{2,1,0:T(8,128)} %u_ref.3) | copy-start | bytes 884740
  17.4 8.6 %copy-start.5 = (f32[4,16,1152]{2,1,0:T(8,128)S(1)}, f32[4,16,1152]{2,1,0:T(8,128)}, u32[]{:S(2)}) copy-start(f32[4,16,1152]{2,1,0:T(8,128)} %v_ref.3) | copy-start | bytes 884740
  17.5 8.4 %collective-permute-start.7 = (f32[8,4,1,1152]{3,2,1,0:T(1,128)S(1)}, f32[8,4,1,1152]{3,2,1,0:T(1,128)S(1)}, u32[]{:S(2)}, u32[]{:S(2)}) collective-permute-start(f32[8,4,1,1152]{3,2,1,0:T(1,128)S(1)} %get-tuple-element.32), channel_id=1, source_target_pairs={{4,0},{8,4},{12,8},{5,1},{9,5},{13,9},{6,2},{10,6},{14,10},{7,3},{... | collective-permute-start | bytes 442376 | tf_op jit(solution)/shard_map/ppermute | solution.py:604
  19.0 6.9 %collective-permute-start.6 = (f32[6,4,1,1152]{3,2,1,0:T(1,128)S(1)}, f32[6,4,1,1152]{3,2,1,0:T(1,128)S(1)}, u32[]{:S(2)}, u32[]{:S(2)}) collective-permute-start(f32[6,4,1,1152]{3,2,1,0:T(1,128)S(1)} %get-tuple-element.31), channel_id=1, source_target_pairs={{0,4},{4,8},{8,12},{1,5},{5,9},{9,13},{2,6},{6,10},{10,14},{3,7},{... | collective-permute-start | bytes 331784 | tf_op jit(solution)/shard_map/ppermute | solution.py:603
  29.7 2.3 %collective-permute-start.15 = (f32[1,4,16,1152]{3,2,1,0:T(8,128)S(1)}, f32[1,4,16,1152]{3,2,1,0:T(8,128)S(1)}, u32[]{:S(2)}, u32[]{:S(2)}) collective-permute-start(f32[1,4,16,1152]{3,2,1,0:T(8,128)S(1)} %get-tuple-element.34.refs_2_), channel_id=1, source_target_pairs={{0,1},{1,0},{2,3},{3,2},{4,5},{5,4},{6,7},{7,6},{8,9},{9,8},{10,11... | collective-permute-start | bytes 884744 | tf_op jit(solution)/shard_map/ppermute | solution.py:561
  29.8 2.2 %collective-permute-start.16 = (f32[1,4,16,1152]{3,2,1,0:T(8,128)S(1)}, f32[1,4,16,1152]{3,2,1,0:T(8,128)S(1)}, u32[]{:S(2)}, u32[]{:S(2)}) collective-permute-start(f32[1,4,16,1152]{3,2,1,0:T(8,128)S(1)} %get-tuple-element.35.refs_4_), channel_id=1, source_target_pairs={{0,1},{1,0},{2,3},{3,2},{4,5},{5,4},{6,7},{7,6},{8,9},{9,8},{10,11... | collective-permute-start | bytes 884744 | tf_op jit(solution)/shard_map/ppermute | solution.py:561
  30.3 12.4 %collective-permute-start.9 = (f32[7,4,2,1152]{3,2,1,0:T(2,128)S(1)}, f32[7,4,2,1152]{3,2,1,0:T(2,128)S(1)}, u32[]{:S(2)}, u32[]{:S(2)}) collective-permute-start(f32[7,4,2,1152]{3,2,1,0:T(2,128)S(1)} %get-tuple-element.33.refs_0_), channel_id=1, source_target_pairs={{0,2},{2,0},{1,3},{3,1},{4,6},{6,4},{5,7},{7,5},{8,10},{10,8},{9,1... | collective-permute-start | bytes 774152 | tf_op jit(solution)/shard_map/ppermute | solution.py:559
  40.8 8.9 %copy-start.1 = (f32[5,4,16,1152]{3,2,1,0:T(8,128)S(1)}, f32[5,4,16,1152]{3,2,1,0:T(8,128)}, u32[]{:S(2)}) copy-start(f32[5,4,16,1152]{3,2,1,0:T(8,128)} %copy-done) | copy-start | bytes 4423684
  40.8 13.1 %collective-permute-start.17 = (f32[112,1152]{1,0:T(8,128)S(1)}, f32[112,1152]{1,0:T(8,128)S(1)}, u32[]{:S(2)}, u32[]{:S(2)}) collective-permute-start(f32[112,1152]{1,0:T(8,128)S(1)} %get-tuple-element.36.refs_12_), channel_id=1, source_target_pairs={{0,2},{2,0},{1,3},{3,1},{4,6},{6,4},{5,7},{7,5},{8,10},{10,8},{9,1... | collective-permute-start | bytes 1548296 | tf_op jit(solution)/shard_map/ppermute | solution.py:559
  42.5 3.6 %collective-permute-start.8 = (f32[7,4,2,1152]{3,2,1,0:T(2,128)S(1)}, f32[7,4,2,1152]{3,2,1,0:T(2,128)S(1)}, u32[]{:S(2)}, u32[]{:S(2)}) collective-permute-start(f32[7,4,2,1152]{3,2,1,0:T(2,128)S(1)} %get-tuple-element.33.refs_0_), channel_id=1, source_target_pairs={{0,1},{1,0},{2,3},{3,2},{4,5},{5,4},{6,7},{7,6},{8,9},{9,8},{10,11... | collective-permute-start | bytes 774152 | tf_op jit(solution)/shard_map/ppermute | solution.py:561
  42.7 3.4 %collective-permute-start.10 = (f32[7,4,2,1152]{3,2,1,0:T(2,128)S(1)}, f32[7,4,2,1152]{3,2,1,0:T(2,128)S(1)}, u32[]{:S(2)}, u32[]{:S(2)}) collective-permute-start(f32[7,4,2,1152]{3,2,1,0:T(2,128)S(1)} %collective-permute-done.9.refs_2_), channel_id=1, source_target_pairs={{0,1},{1,0},{2,3},{3,2},{4,5},{5,4},{6,7},{7,6},{8,9},{9,8},{10,11... | collective-permute-start | bytes 774152 | tf_op jit(solution)/shard_map/ppermute | solution.py:561
  43.0 1.8 %collective-permute-start.13 = (f32[3,4,2,1152]{3,2,1,0:T(2,128)S(1)}, f32[3,4,2,1152]{3,2,1,0:T(2,128)S(1)}, u32[]{:S(2)}, u32[]{:S(2)}) collective-permute-start(f32[3,4,2,1152]{3,2,1,0:T(2,128)S(1)} %get-tuple-element.30.refs_8_), channel_id=1, source_target_pairs={{0,1},{1,0},{2,3},{3,2},{4,5},{5,4},{6,7},{7,6},{8,9},{9,8},{10,11... | collective-permute-start | bytes 331784 | tf_op jit(solution)/shard_map/ppermute | solution.py:561
  43.2 1.5 %collective-permute-start.11 = (f32[2,4,2,1152]{3,2,1,0:T(2,128)S(1)}, f32[2,4,2,1152]{3,2,1,0:T(2,128)S(1)}, u32[]{:S(2)}, u32[]{:S(2)}) collective-permute-start(f32[2,4,2,1152]{3,2,1,0:T(2,128)S(1)} %get-tuple-element.29.refs_4_), channel_id=1, source_target_pairs={{0,1},{1,0},{2,3},{3,2},{4,5},{5,4},{6,7},{7,6},{8,9},{9,8},{10,11... | collective-permute-start | bytes 221192 | tf_op jit(solution)/shard_map/ppermute | solution.py:561
  44.6 1.4 %collective-permute-start.14 = (f32[3,4,2,1152]{3,2,1,0:T(2,128)S(1)}, f32[3,4,2,1152]{3,2,1,0:T(2,128)S(1)}, u32[]{:S(2)}, u32[]{:S(2)}) collective-permute-start(f32[3,4,2,1152]{3,2,1,0:T(2,128)S(1)} %collective-permute-done.5.refs_4_.refs_10_), channel_id=1, source_target_pairs={{0,1},{1,0},{2,3},{3,2},{4,5},{5,4},{6,7},{7,6},{8,9},{9,8},{10,11... | collective-permute-start | bytes 331784 | tf_op jit(solution)/shard_map/ppermute | solution.py:561
  44.8 1.3 %collective-permute-start.12 = (f32[2,4,2,1152]{3,2,1,0:T(2,128)S(1)}, f32[2,4,2,1152]{3,2,1,0:T(2,128)S(1)}, u32[]{:S(2)}, u32[]{:S(2)}) collective-permute-start(f32[2,4,2,1152]{3,2,1,0:T(2,128)S(1)} %collective-permute-done.4.refs_3_.refs_6_), channel_id=1, source_target_pairs={{0,1},{1,0},{2,3},{3,2},{4,5},{5,4},{6,7},{7,6},{8,9},{9,8},{10,11... | collective-permute-start | bytes 221192 | tf_op jit(solution)/shard_map/ppermute | solution.py:561
  (9 other events, 50.2 us)

commit v6 on v5

--- a/solution.py
+++ b/solution.py
@@ -15,7 +15,7 @@
 
 
 def params():
-    return pltpu.CompilerParams(vmem_limit_bytes=48 * 1024 * 1024)
+    return pltpu.CompilerParams(vmem_limit_bytes=16 * 1024 * 1024)
 
 
 def cost(flops, bytes_accessed):
@@ -77,14 +77,52 @@
     return change - (t_north - south_of(t_north, t_below)) * inverse
 
 
-def inner_kernel(band_ref, table_ref, thick_ref, u_ref, v_ref, tracer_ref, out_ref, sum_ref, last_ref, leading_ref, near_ref, near_rest_ref):
+def in_hbm(*arrays):
+    return [pltpu.with_memory_space_constraint(a, pltpu.HBM) for a in arrays]
+
+
+def first_kernel(band_ref, table_ref, thick_ref, u_ref, v_ref, new_ref, sum_ref):
     rows, width = thick_ref.shape[1:]
     geo = table_ref[band_ref[0]]
     thick, u, v = thick_ref[0], u_ref[0], v_ref[0]
     nothing = jnp.zeros((1, width), jnp.float32)
     east, north, below = fluxes(geo, thick, u, v, nothing, nothing, nothing)
+    new = thick - (east - west_of(east)) - (north - south_of(north, below)) * geo[0:rows, 2:3]
+    new_ref[0] = new
+
+    @pl.when(pl.program_id(0) == 0)
+    def _():
+        sum_ref[...] = new
+
+    @pl.when(pl.program_id(0) > 0)
+    def _():
+        sum_ref[...] += new
+
+
+def first_step(band, table, thickness, wind_u, wind_v):
+    L, R, N = thickness.shape
+    level = pl.BlockSpec((1, R, N), lambda k: (k, 0, 0))
+    return pl.pallas_call(
+        first_kernel,
+        grid=(L,),
+        in_specs=[SMEM, pl.BlockSpec(table.shape, lambda k: (0, 0, 0)), level, level, level],
+        out_specs=[level, pl.BlockSpec((R, N), lambda k: (0, 0))],
+        out_shape=[jax.ShapeDtypeStruct((L, R, N), jnp.float32), jax.ShapeDtypeStruct((R, N), jnp.float32)],
+        compiler_params=params(),
+        cost_estimate=cost(40 * L * R * N, 4 * L * R * N * 5),
+        name="first_step",
+    )(band, *in_hbm(table, thickness, wind_u, wind_v))
+
+
+def inner_kernel(band_ref, table_ref, thick_ref, u_ref, v_ref, new_ref, tracer_ref, *refs):
+    out_ref, last_ref, leading_ref, near_ref, near_rest_ref = refs
+    rows, width = thick_ref.shape[1:]
+    geo = table_ref[band_ref[0]]
+    thick, u, v, new = thick_ref[0], u_ref[0], v_ref[0], new_ref[0]
+    nothing = jnp.zeros((1, width), jnp.float32)
+    east, north, below = fluxes(geo, thick, u, v, nothing, nothing, nothing)
     inverse = geo[0:rows, 2:3]
-    new = thick - (east - west_of(east)) - (north - south_of(north, below)) * inverse
+
     def store(field, value):
         out_ref[field, 0] = value
         ref, at = (near_ref, field) if field < 2 else (near_rest_ref, field - 2)
@@ -98,15 +136,6 @@
     leading_ref[1, 0] = thick[1:2]
     leading_ref[2, 0] = u[0:1]
     leading_ref[3, 0] = v[0:1]
-
-    @pl.when(pl.program_id(0) == 0)
-    def _():
-        sum_ref[...] = new
-
-    @pl.when(pl.program_id(0) > 0)
-    def _():
-        sum_ref[...] += new
-
     scale = 1.0 / new
     for c in range(tracer_ref.shape[0]):
         q = tracer_ref[c, 0]
@@ -116,29 +145,22 @@
         store(1 + c, change * scale)
 
 
-def inner_step(band, table, thickness, wind_u, wind_v, tracers):
+def inner_step(band, table, thickness, wind_u, wind_v, new, tracers):
     L, R, N = thickness.shape
     T = tracers.shape[0]
     level = pl.BlockSpec((1, R, N), lambda k: (k, 0, 0))
     some = lambda n, rows: pl.BlockSpec((n, 1, rows, N), lambda k: (0, k, 0, 0))
-    in_hbm = lambda x: pltpu.with_memory_space_constraint(x, pltpu.HBM)
+    shape = lambda n, rows: jax.ShapeDtypeStruct((n, L, rows, N), jnp.float32)
     return pl.pallas_call(
         inner_kernel,
         grid=(L,),
-        in_specs=[SMEM, pl.BlockSpec(table.shape, lambda k: (0, 0, 0)), level, level, level, some(T, R)],
-        out_specs=[some(1 + T, R), pl.BlockSpec((R, N), lambda k: (0, 0)), some(2 + T, 1), some(4 + T, 1), some(2, 2), some(T - 1, 2)],
-        out_shape=[
-            jax.ShapeDtypeStruct((1 + T, L, R, N), jnp.float32),
-            jax.ShapeDtypeStruct((R, N), jnp.float32),
-            jax.ShapeDtypeStruct((2 + T, L, 1, N), jnp.float32),
-            jax.ShapeDtypeStruct((4 + T, L, 1, N), jnp.float32),
-            jax.ShapeDtypeStruct((2, L, 2, N), jnp.float32),
-            jax.ShapeDtypeStruct((T - 1, L, 2, N), jnp.float32),
-        ],
+        in_specs=[SMEM, pl.BlockSpec(table.shape, lambda k: (0, 0, 0)), level, level, level, level, some(T, R)],
+        out_specs=[some(1 + T, R), some(2 + T, 1), some(4 + T, 1), some(2, 2), some(T - 1, 2)],
+        out_shape=[shape(1 + T, R), shape(2 + T, 1), shape(4 + T, 1), shape(2, 2), shape(T - 1, 2)],
         compiler_params=params(),
         cost_estimate=cost(130 * L * R * N, 4 * L * R * N * (8 + 2 * T)),
         name="inner_step",
-    )(band, in_hbm(table), in_hbm(thickness), in_hbm(wind_u), in_hbm(wind_v), in_hbm(tracers))
+    )(band, *in_hbm(table, thickness, wind_u, wind_v), new, *in_hbm(tracers))
 
 
 def filter_tables(N):
@@ -288,6 +310,31 @@
     )
 
 
+def mass_kernel(C, S, place_ref, new_ref, *refs):
+    base_ref, mass_ref = refs[-2:]
+    lev = place_ref[0]
+    others_mass, base = None, None
+    for s in range(1, C):
+        other = functools.reduce(jnp.add, [ref[...] for ref in refs[(s - 1) * S : s * S]])
+        below = jnp.where(lev >= s, other, 0.0)
+        others_mass = other if others_mass is None else others_mass + other
+        base = below if base is None else base + below
+    base_ref[...] = base
+    mass_ref[...] = others_mass
+
+
+def other_chips(counts, place, new, others):
+    return pl.pallas_call(
+        functools.partial(mass_kernel, *counts),
+        in_specs=[SMEM] + [VMEM] * (1 + len(others)),
+        out_specs=[VMEM] * 2,
+        out_shape=[jax.ShapeDtypeStruct(new.shape, jnp.float32)] * 2,
+        compiler_params=params(),
+        cost_estimate=cost(1e11, 1e9),
+        name="other_chips",
+    )(place, new, *others)
+
+
 def weight_sums(weight_ref, firsts, L, levels):
     total = jnp.float32(0.0)
     below = [jnp.float32(0.0) for _ in firsts]
@@ -311,9 +358,8 @@
     group = [functools.reduce(jnp.add, levels) for levels in thick]
     mass = functools.reduce(jnp.add, group)
     base = jnp.zeros_like(mass)
-    for s, other in enumerate(others, 1):
-        mass = mass + other
-        base = base + jnp.where(lev >= s, other, 0.0)
+    if others:
+        base, mass = others[0], mass + others[1]
     sources = []
     for g, levels in enumerate(thick):
         low = base
@@ -332,7 +378,6 @@
 
 def remap_rows(place, weight_ref, counts, steps, thick_refs, field_refs, other_refs, store):
     C, S = counts
-    G = len(thick_refs) // S
     _, L, R, N = thick_refs[0].shape
     lev, sub = place
     firsts = [(lax.rem(lev + s, C) * S + sub) * L for s in steps]
@@ -340,10 +385,7 @@
 
     def tile(at, columns):
         thick = [[ref[0, m, at, columns] for m in range(L)] for ref in thick_refs]
-        others = [
-            functools.reduce(jnp.add, [ref[at, columns] for ref in other_refs[s * S : (s + 1) * S]])
-            for s in range(C - G)
-        ]
+        others = [ref[at, columns] for ref in other_refs]
         mass, sources = source_levels(place, counts, thick, others)
         unit = mass / weight_sum
         for index, s in enumerate(steps):
@@ -381,7 +423,7 @@
     for _ in range(sizes[0]):
         bundles.append(refs[:S])
         refs = refs[S:]
-    other_refs, out_refs = refs[: (C - 1) * S], refs[len(refs) - len(steps) :]
+    other_refs, out_refs = refs[:2], refs[len(refs) - len(steps) :]
     _, L, R, _ = thick_refs[0].shape
     field_refs = [[(ref, index) for ref in bundles[which]] for which, index in fields]
 
@@ -463,7 +505,7 @@
 def finish_kernel(counts, margin, place_ref, weight_ref, *refs):
     C, S = counts
     group_refs, refs = refs[:S], refs[S:]
-    other_refs, refs = refs[: (C - 1) * S], refs[(C - 1) * S :]
+    other_refs, refs = refs[:2], refs[2:]
     *arrived_refs, near_ref, edge_ref, thick_edge_ref, out_ref, thick_out_ref, token_ref = refs
     token_ref[...] = jnp.zeros_like(token_ref)
     T, L, R, _ = out_ref.shape
@@ -590,11 +632,13 @@
 
     remap = functools.partial(remap_parts, (C, S), place, level_weights)
 
-    inner, own_sum, last, leading, near, near_rest = inner_step(band, table, thickness, wind_u, wind_v, tracers)
+    new, own_sum = first_step(band, table, thickness, wind_u, wind_v)
     others = [send(own_sum, s=s, t=t) for s in away for t in range(S)]
+    inner, last, leading, near, near_rest = inner_step(band, table, thickness, wind_u, wind_v, new, tracers)
     group = with_others_of_chip(inner)
     near = [near] + [send(near, s=s, t=0) for s in away]
     near_rest = [near_rest] + [send(near_rest, s=s, t=0) for s in away]
+    others = other_chips((C, S), place, own_sum, others)
     tracer_fields = [(0, 1 + c) for c in range(T)]
     away_parts = remap(group, [group], others, tracer_fields, away, 2)
     arrived = sent(away_parts)

time: 55.1 us -> 55.6 us (level)
  Pallas kernels: 20.7 us -> 23 us
  waiting for transfers between devices: 13.6 us -> 12.2 us
  local copies, waits for them, and re-layouts: 1.44 us -> 0.77 us
    pallas_call x0 -> x2, Pallas kernels: none -> 3.49 us  [the longest x1 2.55 us: first_step(): pl.pallas_call(first_kernel, grid=(L,), in_specs=[SMEM, pl.BlockSpec(tabl...]
    ppermute x1, waiting for transfers between devices: 1.31 us -> 0.01 us  [shifted(): return lax.ppermute(value, ('lev', 'sub'), pairs)]
    ppermute x6, starting transfers between devices: 9.57 us -> 10.5 us  [shifted(): lax.ppermute(value, 'lev', [(i, (i + s) % lev_count) for i in range(lev_c...]
    pallas_call x2, Pallas kernels: 5.2 us -> 4.36 us  [remap_parts(): pl.pallas_call(functools.partial(remap_kernel, counts, tuple(steps), tupl...]
    unnamed x30 -> x22, local copies, waits for them, and re-layouts: 1.37 us -> 0.7 us
    ppermute x9, starting transfers between devices: 2.37 us -> 1.79 us  [shifted(): lax.ppermute(value, 'sub', [(i, (i + t) % sub_count) for i in range(sub_c...]
  transfers between devices with their start and end apart: 18 -> 18, of which waited for: 9 -> 7; matrix products, arithmetic and copies ran while one was open for 0% -> 0% of each run, Pallas kernels for 29% -> 35%
where the time goes in v6:
time: 55.6 us; the launch traced here: 55.2 us
  Pallas kernels  23 us (41%)
  starting transfers between devices  18.4 us (33%)
  waiting for transfers between devices  12.2 us (22%)
  between operations  0.87 us (2%)
  local copies, waits for them, and re-layouts  0.77 us (1%)
    ppermute x6, starting transfers between devices, shifted(): lax.ppermute(value, 'lev', [(i, (i + s) % lev_count) for i in range(lev_c...  10.5 us
    ppermute x6, waiting for transfers between devices, shifted(): lax.ppermute(value, 'lev', [(i, (i + s) % lev_count) for i in range(lev_c...  7.53 us
    ppermute x1, starting transfers between devices, per_device(): up = lax.ppermute(last, 'lat', northward)  4.55 us
    pallas_call x2, Pallas kernels, remap_parts(): pl.pallas_call(functools.partial(remap_kernel, counts, tuple(steps), tupl...  4.36 us
    pallas_call x1, Pallas kernels, remap_edges(): pl.pallas_call(functools.partial(remap_edge_kernel, counts, near_fields),...  3.67 us
    pallas_call x1, Pallas kernels, second_step(): pl.pallas_call(functools.partial(second_kernel, lat_rows), grid=(L,), in_...  3.65 us
    pallas_call x1, Pallas kernels, inner_step(): pl.pallas_call(inner_kernel, grid=(L,), in_specs=[SMEM, pl.BlockSpec(tabl...  3.62 us
    pallas_call x1, Pallas kernels, finish_tracers(): pl.pallas_call(functools.partial(finish_kernel, counts, margin), in_specs...  3.25 us
  transfers between devices with their start and end apart: 18, of which 7 were waited for; matrix products, arithmetic and copies ran while one was open for 0% of the time, Pallas kernels for 35%

profile of v6, /device:TPU:0, one launch (start us, length us, event | category | flops | bytes accessed | tf_op | source)
XLA Modules:
  0.0 55.2 jit_solution(6692922694740062845)
XLA Ops:
  0.6 2.5 %first_step.1 = (f32[4,16,1152]{2,1,0:T(8,128)S(1)}, f32[16,1152]{1,0:T(8,128)S(1)}) custom-call(s32[1]{0:T(128)} %bitcast.2.band_ref, f32[4,24,128]{2,1,0:T(8,128)} %constant.17.clone.table_ref, f32[4,16,1152]{2,1,0:T(8,128)} %thick_ref.5, f32[4,16,1152]{2,1,0:T(8,128)} %u_ref.5, f32[4,16,1152]{2,1,0:T(8,128)} %v_ref.5), custom_call_target="tpu_custom_call" | custom-call | flops 2949120 | bytes 1474560 | tf_op jit(solution)/shard_map/first_step/pallas_call | solution.py:105
  3.2 3.0 %collective-permute-start.1 = (f32[16,1152]{1,0:T(8,128)S(1)}, f32[16,1152]{1,0:T(8,128)}, u32[]{:S(2)}, u32[]{:S(2)}) collective-permute-start(f32[16,1152]{1,0:T(8,128)S(1)} %get-tuple-element.30.new_ref), channel_id=1, source_target_pairs={{0,2},{2,0},{1,3},{3,1},{4,6},{6,4},{5,7},{7,5},{8,10},{10,8},{9,1... | collective-permute-start | bytes 221192 | tf_op jit(solution)/shard_map/ppermute | solution.py:601
  6.2 3.6 %inner_step.1 = (f32[5,4,16,1152]{3,2,1,0:T(8,128)S(1)}, f32[6,4,1,1152]{3,2,1,0:T(1,128)S(1)}, f32[8,4,1,1152]{3,2,1,0:T(1,128)S(1)}, f32[2,4,2,1152]{3,2,1,0:T(2,128)S(1)}, f32[3,4,2,1152]{3,2,1,0:T(2,128)S(1)}) custom-call(s32[1]{0:T(128)} %bitcast.2.band_ref, f32[4,24,128]{2,1,0:T(8,128)} %constant.17.clone.table_ref, f32[4,16,1152]{2,1,0:T(8,128)} %thick_ref.5, ...), custom_call_target="tpu_custom_call" | custom-call | flops 9584640 | bytes 4718592 | tf_op jit(solution)/shard_map/inner_step/pallas_call | solution.py:154
  9.8 0.6 %copy-done.8 = f32[6,4,1,1152]{3,2,1,0:T(1,128)} copy-done((f32[6,4,1,1152]{3,2,1,0:T(1,128)}, f32[6,4,1,1152]{3,2,1,0:T(1,128)S(1)}, u32[]{:S(2)}) %copy-start.8) | copy-done | bytes 110616
  10.7 1.9 %collective-permute-start.5 = (f32[3,4,2,1152]{3,2,1,0:T(2,128)S(1)}, f32[3,4,2,1152]{3,2,1,0:T(2,128)S(1)}, u32[]{:S(2)}, u32[]{:S(2)}) collective-permute-start(f32[3,4,2,1152]{3,2,1,0:T(2,128)S(1)} %get-tuple-element.36.refs_8_), channel_id=1, source_target_pairs={{0,2},{2,0},{1,3},{3,1},{4,6},{6,4},{5,7},{7,5},{8,10},{10,8},{9,1... | collective-permute-start | bytes 331784 | tf_op jit(solution)/shard_map/ppermute | solution.py:601
  12.8 0.9 %other_chips.1 = (f32[16,1152]{1,0:T(8,128)S(1)}, f32[16,1152]{1,0:T(8,128)S(1)}) custom-call(s32[2]{0:T(128)S(1)} %pad_add_fusion.place_ref, f32[16,1152]{1,0:T(8,128)S(1)} %get-tuple-element.30.new_ref, f32[16,1152]{1,0:T(8,128)} %collective-permute-done.1.refs_0_, f32[16,1152]{1,0:T(8,128)} %collective-permute-done.2.refs_1_), custom_call_target="tpu_custom_call" | custom-call | flops 99999997952 | bytes 1000000000 | tf_op jit(solution)/shard_map/other_chips/pallas_call | solution.py:327
  13.8 2.0 %remap_parts.2.refs_2_ = f32[192,1152]{1,0:T(8,128)S(1)} custom-call(s32[2]{0:T(128)S(1)} %pad_add_fusion.place_ref, f32[16]{0:T(128)S(1)} %copy-done.7, f32[5,4,16,1152]{3,2,1,0:T(8,128)S(1)} %get-tuple-element.29.refs_0_.refs_2_, f32[5,4,16,1152]{3,2,1,0:T(8,128)S(1)} %collective-permute-done.refs_1_.refs_3_, ...), custom_call_target="tpu_custom_call" | custom-call | flops 7667712 | bytes 4423680 | tf_op jit(solution)/shard_map/remap_parts/pallas_call | solution.py:452
  15.7 2.0 %collective-permute-start.3 = (f32[192,1152]{1,0:T(8,128)S(1)}, f32[192,1152]{1,0:T(8,128)S(1)}, u32[]{:S(2)}, u32[]{:S(2)}) collective-permute-start(f32[192,1152]{1,0:T(8,128)S(1)} %remap_parts.2.refs_2_), channel_id=1, source_target_pairs={{0,2},{2,0},{1,3},{3,1},{4,6},{6,4},{5,7},{7,5},{8,10},{10,8},{9,1... | collective-permute-start | bytes 2654216 | tf_op jit(solution)/shard_map/ppermute | solution.py:601
  17.9 1.6 %collective-permute-start.7 = (f32[8,4,1,1152]{3,2,1,0:T(1,128)S(1)}, f32[8,4,1,1152]{3,2,1,0:T(1,128)S(1)}, u32[]{:S(2)}, u32[]{:S(2)}) collective-permute-start(f32[8,4,1,1152]{3,2,1,0:T(1,128)S(1)} %get-tuple-element.38), channel_id=1, source_target_pairs={{4,0},{8,4},{12,8},{5,1},{9,5},{13,9},{6,2},{10,6},{14,10},{7,3},{... | collective-permute-start | bytes 442376 | tf_op jit(solution)/shard_map/ppermute | solution.py:648
  19.5 4.6 %collective-permute-start.6 = (f32[6,4,1,1152]{3,2,1,0:T(1,128)S(1)}, f32[6,4,1,1152]{3,2,1,0:T(1,128)S(1)}, u32[]{:S(2)}, u32[]{:S(2)}) collective-permute-start(f32[6,4,1,1152]{3,2,1,0:T(1,128)S(1)} %get-tuple-element.37), channel_id=1, source_target_pairs={{0,4},{4,8},{8,12},{1,5},{5,9},{9,13},{2,6},{6,10},{10,14},{3,7},{... | collective-permute-start | bytes 331784 | tf_op jit(solution)/shard_map/ppermute | solution.py:647
  24.0 2.3 %collective-permute-done.6.up_ref = f32[6,4,1,1152]{3,2,1,0:T(1,128)S(1)} collective-permute-done((f32[6,4,1,1152]{3,2,1,0:T(1,128)S(1)}, f32[6,4,1,1152]{3,2,1,0:T(1,128)S(1)}, u32[]{:S(2)}, u32[]{:S(2)}) %collective-permute-start.6) | collective-permute-done | bytes 110624 | tf_op jit(solution)/shard_map/ppermute | solution.py:647
  26.5 3.7 %second_step.1 = (f32[1,4,16,1152]{3,2,1,0:T(8,128)S(1)}, f32[1,4,16,1152]{3,2,1,0:T(8,128)S(1)}, f32[7,4,2,1152]{3,2,1,0:T(2,128)S(1)}) custom-call(s32[1]{0:T(128)} %bitcast.2.band_ref, f32[4,24,128]{2,1,0:T(8,128)S(1)} %copy-done.6, f32[4,16,1152]{2,1,0:T(8,128)S(1)} %copy-done.1, f32[4,16,1152]{2,1,0:T(8,128)S(1)} %copy-done.2, ...), custom_call_target="tpu_custom_call" | custom-call | flops 503316480 | bytes 3538944 | tf_op jit(solution)/shard_map/second_step/pallas_call | solution.py:292
  30.2 0.5 collective-permute-start.16
  30.7 1.4 %collective-permute-start.9 = (f32[7,4,2,1152]{3,2,1,0:T(2,128)S(1)}, f32[7,4,2,1152]{3,2,1,0:T(2,128)S(1)}, u32[]{:S(2)}, u32[]{:S(2)}) collective-permute-start(f32[7,4,2,1152]{3,2,1,0:T(2,128)S(1)} %get-tuple-element.39.refs_0_), channel_id=1, source_target_pairs={{0,2},{2,0},{1,3},{3,1},{4,6},{6,4},{5,7},{7,5},{8,10},{10,8},{9,1... | collective-permute-start | bytes 774152 | tf_op jit(solution)/shard_map/ppermute | solution.py:601
  32.2 6.1 %collective-permute-done.3.refs_8_.refs_4_ = f32[192,1152]{1,0:T(8,128)S(1)} collective-permute-done((f32[192,1152]{1,0:T(8,128)S(1)}, f32[192,1152]{1,0:T(8,128)S(1)}, u32[]{:S(2)}, u32[]{:S(2)}) %collective-permute-start.3) | collective-permute-done | bytes 884768 | tf_op jit(solution)/shard_map/ppermute | solution.py:601
  38.3 2.4 %remap_parts.3 = (f32[2,4,16,1152]{3,2,1,0:T(8,128)S(1)}, f32[112,1152]{1,0:T(8,128)S(1)}) custom-call(s32[2]{0:T(128)S(1)} %pad_add_fusion.place_ref, f32[16]{0:T(128)S(1)} %copy-done.7, f32[5,4,16,1152]{3,2,1,0:T(8,128)S(1)} %get-tuple-element.29.refs_0_.refs_2_, f32[5,4,16,1152]{3,2,1,0:T(8,128)S(1)} %collective-permute-done.refs_1_.refs_3_, ...), custom_call_target="tpu_custom_call" | custom-call | flops 10616832 | bytes 3538944 | tf_op jit(solution)/shard_map/remap_parts/pallas_call | solution.py:452
  40.7 2.0 %collective-permute-start.17 = (f32[112,1152]{1,0:T(8,128)S(1)}, f32[112,1152]{1,0:T(8,128)S(1)}, u32[]{:S(2)}, u32[]{:S(2)}) collective-permute-start(f32[112,1152]{1,0:T(8,128)S(1)} %get-tuple-element.42.refs_12_), channel_id=1, source_target_pairs={{0,2},{2,0},{1,3},{3,1},{4,6},{6,4},{5,7},{7,5},{8,10},{10,8},{9,1... | collective-permute-start | bytes 1548296 | tf_op jit(solution)/shard_map/ppermute | solution.py:601
  42.7 1.1 %collective-permute-done.9.refs_2_ = f32[7,4,2,1152]{3,2,1,0:T(2,128)S(1)} collective-permute-done((f32[7,4,2,1152]{3,2,1,0:T(2,128)S(1)}, f32[7,4,2,1152]{3,2,1,0:T(2,128)S(1)}, u32[]{:S(2)}, u32[]{:S(2)}) %collective-permute-start.9) | collective-permute-done | bytes 258080 | tf_op jit(solution)/shard_map/ppermute | solution.py:601
  43.8 0.5 collective-permute-start.13
  44.3 1.3 %collective-permute-done.11.refs_5_ = f32[2,4,2,1152]{3,2,1,0:T(2,128)S(1)} collective-permute-done((f32[2,4,2,1152]{3,2,1,0:T(2,128)S(1)}, f32[2,4,2,1152]{3,2,1,0:T(2,128)S(1)}, u32[]{:S(2)}, u32[]{:S(2)}) %collective-permute-start.11) | collective-permute-done | bytes 73760 | tf_op jit(solution)/shard_map/ppermute | solution.py:603
  46.1 0.9 %collective-permute-done.12.refs_7_ = f32[2,4,2,1152]{3,2,1,0:T(2,128)S(1)} collective-permute-done((f32[2,4,2,1152]{3,2,1,0:T(2,128)S(1)}, f32[2,4,2,1152]{3,2,1,0:T(2,128)S(1)}, u32[]{:S(2)}, u32[]{:S(2)}) %collective-permute-start.12) | collective-permute-done | bytes 73760 | tf_op jit(solution)/shard_map/ppermute | solution.py:603
  47.0 3.7 %remap_edges.1 = (f32[6,4,2,1152]{3,2,1,0:T(2,128)S(1)}, f32[4,2,1152]{2,1,0:T(2,128)S(1)}, f32[4,4,2,1152]{3,2,1,0:T(2,128)S(1)}) custom-call(s32[2]{0:T(128)S(1)} %pad_add_fusion.place_ref, f32[16]{0:T(128)S(1)} %copy-done.7, f32[7,4,2,1152]{3,2,1,0:T(2,128)S(1)} %get-tuple-element.39.refs_0_, f32[7,4,2,1152]{3,2,1,0:T(2,128)S(1)} %collective-permute-done.8.refs_1_, ...), custom_call_target="tpu_custom_call" | custom-call | flops 5898240 | bytes 3096576 | tf_op jit(solution)/shard_map/remap_edges/pallas_call | solution.py:490
  50.7 3.3 %finish_tracers.1 = (f32[4,4,16,1152]{3,2,1,0:T(8,128)}, f32[4,16,1152]{2,1,0:T(8,128)}, f32[8,128]{1,0:T(8,128)S(1)}) custom-call(s32[2]{0:T(128)S(1)} %pad_add_fusion.place_ref, f32[16]{0:T(128)S(1)} %copy-done.7, f32[5,4,16,1152]{3,2,1,0:T(8,128)S(1)} %get-tuple-element.29.refs_0_.refs_2_, f32[5,4,16,1152]{3,2,1,0:T(8,128)S(1)} %collective-permute-done.refs_1_.refs_3_, ...), custom_call_target="tpu_custom_call" | custom-call | flops 7667712 | bytes 5898240 | tf_op jit(solution)/shard_map/finish_tracers/pallas_call | solution.py:541
  54.3 0.9 %finish_winds.1 = (f32[4,16,1152]{2,1,0:T(8,128)}, f32[4,16,1152]{2,1,0:T(8,128)}) custom-call(f32[2,4,16,1152]{3,2,1,0:T(8,128)S(1)} %get-tuple-element.47.own_ref, f32[6,4,2,1152]{3,2,1,0:T(2,128)S(1)} %get-tuple-element.44.refs_6_.edge_ref, f32[112,1152]{1,0:T(8,128)S(1)} %collective-permute-done.17.refs_0_, f32[8,128]{1,0:T(8,128)S(1)} %get-tuple-element.48.refs_1_), custom_call_target="tpu_custom_call" | custom-call | flops 147456 | bytes 1769472 | tf_op jit(solution)/shard_map/finish_winds/pallas_call | solution.py:571
  (46 shorter events, 1.6 us)
Async XLA Ops:
  3.2 9.6 %collective-permute-start.1 = (f32[16,1152]{1,0:T(8,128)S(1)}, f32[16,1152]{1,0:T(8,128)}, u32[]{:S(2)}, u32[]{:S(2)}) collective-permute-start(f32[16,1152]{1,0:T(8,128)S(1)} %get-tuple-element.30.new_ref), channel_id=1, source_target_pairs={{0,2},{2,0},{1,3},{3,1},{4,6},{6,4},{5,7},{7,5},{8,10},{10,8},{9,1... | collective-permute-start | bytes 221192 | tf_op jit(solution)/shard_map/ppermute | solution.py:601
  6.2 6.6 %collective-permute-start.2 = (f32[16,1152]{1,0:T(8,128)S(1)}, f32[16,1152]{1,0:T(8,128)}, u32[]{:S(2)}, u32[]{:S(2)}) collective-permute-start(f32[16,1152]{1,0:T(8,128)S(1)} %get-tuple-element.30.new_ref), channel_id=1, source_target_pairs={{0,3},{1,2},{2,1},{3,0},{4,7},{5,6},{6,5},{7,4},{8,11},{9,10},{10,... | collective-permute-start | bytes 221192 | tf_op jit(solution)/shard_map/ppermute | solution.py:609
  10.5 3.3 %collective-permute-start = (f32[5,4,16,1152]{3,2,1,0:T(8,128)S(1)}, f32[5,4,16,1152]{3,2,1,0:T(8,128)S(1)}, u32[]{:S(2)}, u32[]{:S(2)}) collective-permute-start(f32[5,4,16,1152]{3,2,1,0:T(8,128)S(1)} %get-tuple-element.29.refs_0_.refs_2_), channel_id=1, source_target_pairs={{0,1},{1,0},{2,3},{3,2},{4,5},{5,4},{6,7},{7,6},{8,9},{9,8},{10,11... | collective-permute-start | bytes 4423688 | tf_op jit(solution)/shard_map/ppermute | solution.py:603
  10.7 7.1 %collective-permute-start.5 = (f32[3,4,2,1152]{3,2,1,0:T(2,128)S(1)}, f32[3,4,2,1152]{3,2,1,0:T(2,128)S(1)}, u32[]{:S(2)}, u32[]{:S(2)}) collective-permute-start(f32[3,4,2,1152]{3,2,1,0:T(2,128)S(1)} %get-tuple-element.36.refs_8_), channel_id=1, source_target_pairs={{0,2},{2,0},{1,3},{3,1},{4,6},{6,4},{5,7},{7,5},{8,10},{10,8},{9,1... | collective-permute-start | bytes 331784 | tf_op jit(solution)/shard_map/ppermute | solution.py:601
  12.6 5.1 %collective-permute-start.4 = (f32[2,4,2,1152]{3,2,1,0:T(2,128)S(1)}, f32[2,4,2,1152]{3,2,1,0:T(2,128)S(1)}, u32[]{:S(2)}, u32[]{:S(2)}) collective-permute-start(f32[2,4,2,1152]{3,2,1,0:T(2,128)S(1)} %get-tuple-element.35.refs_4_), channel_id=1, source_target_pairs={{0,2},{2,0},{1,3},{3,1},{4,6},{6,4},{5,7},{7,5},{8,10},{10,8},{9,1... | collective-permute-start | bytes 221192 | tf_op jit(solution)/shard_map/ppermute | solution.py:601
  15.7 22.5 %collective-permute-start.3 = (f32[192,1152]{1,0:T(8,128)S(1)}, f32[192,1152]{1,0:T(8,128)S(1)}, u32[]{:S(2)}, u32[]{:S(2)}) collective-permute-start(f32[192,1152]{1,0:T(8,128)S(1)} %remap_parts.2.refs_2_), channel_id=1, source_target_pairs={{0,2},{2,0},{1,3},{3,1},{4,6},{6,4},{5,7},{7,5},{8,10},{10,8},{9,1... | collective-permute-start | bytes 2654216 | tf_op jit(solution)/shard_map/ppermute | solution.py:601
  17.8 8.6 %copy-start = (f32[4,4,16,1152]{3,2,1,0:T(8,128)S(1)}, f32[4,4,16,1152]{3,2,1,0:T(8,128)}, u32[]{:S(2)}) copy-start(f32[4,4,16,1152]{3,2,1,0:T(8,128)} %tracer_ref.3) | copy-start | bytes 3538948
  17.8 8.6 %copy-start.1 = (f32[4,16,1152]{2,1,0:T(8,128)S(1)}, f32[4,16,1152]{2,1,0:T(8,128)}, u32[]{:S(2)}) copy-start(f32[4,16,1152]{2,1,0:T(8,128)} %thick_ref.5) | copy-start | bytes 884740
  17.8 8.6 %copy-start.2 = (f32[4,16,1152]{2,1,0:T(8,128)S(1)}, f32[4,16,1152]{2,1,0:T(8,128)}, u32[]{:S(2)}) copy-start(f32[4,16,1152]{2,1,0:T(8,128)} %u_ref.5) | copy-start | bytes 884740
  17.8 8.6 %copy-start.3 = (f32[4,16,1152]{2,1,0:T(8,128)S(1)}, f32[4,16,1152]{2,1,0:T(8,128)}, u32[]{:S(2)}) copy-start(f32[4,16,1152]{2,1,0:T(8,128)} %v_ref.5) | copy-start | bytes 884740
  17.8 8.6 %copy-start.4 = (bf16[5,256,256]{2,1,0:T(8,128)(2,1)S(1)}, bf16[5,256,256]{2,1,0:T(8,128)(2,1)}, u32[]{:S(2)}) copy-start(bf16[5,256,256]{2,1,0:T(8,128)(2,1)} %constant.18.clone.high_ref) | copy-start | bytes 1966084
  17.8 8.6 %copy-start.5 = (bf16[5,256,256]{2,1,0:T(8,128)(2,1)S(1)}, bf16[5,256,256]{2,1,0:T(8,128)(2,1)}, u32[]{:S(2)}) copy-start(bf16[5,256,256]{2,1,0:T(8,128)(2,1)} %constant.19.clone.low_ref) | copy-start | bytes 1966084
  17.9 8.4 %collective-permute-start.7 = (f32[8,4,1,1152]{3,2,1,0:T(1,128)S(1)}, f32[8,4,1,1152]{3,2,1,0:T(1,128)S(1)}, u32[]{:S(2)}, u32[]{:S(2)}) collective-permute-start(f32[8,4,1,1152]{3,2,1,0:T(1,128)S(1)} %get-tuple-element.38), channel_id=1, source_target_pairs={{4,0},{8,4},{12,8},{5,1},{9,5},{13,9},{6,2},{10,6},{14,10},{7,3},{... | collective-permute-start | bytes 442376 | tf_op jit(solution)/shard_map/ppermute | solution.py:648
  19.5 6.9 %collective-permute-start.6 = (f32[6,4,1,1152]{3,2,1,0:T(1,128)S(1)}, f32[6,4,1,1152]{3,2,1,0:T(1,128)S(1)}, u32[]{:S(2)}, u32[]{:S(2)}) collective-permute-start(f32[6,4,1,1152]{3,2,1,0:T(1,128)S(1)} %get-tuple-element.37), channel_id=1, source_target_pairs={{0,4},{4,8},{8,12},{1,5},{5,9},{9,13},{2,6},{6,10},{10,14},{3,7},{... | collective-permute-start | bytes 331784 | tf_op jit(solution)/shard_map/ppermute | solution.py:647
  30.1 2.0 %collective-permute-start.15 = (f32[1,4,16,1152]{3,2,1,0:T(8,128)S(1)}, f32[1,4,16,1152]{3,2,1,0:T(8,128)S(1)}, u32[]{:S(2)}, u32[]{:S(2)}) collective-permute-start(f32[1,4,16,1152]{3,2,1,0:T(8,128)S(1)} %get-tuple-element.40.refs_2_), channel_id=1, source_target_pairs={{0,1},{1,0},{2,3},{3,2},{4,5},{5,4},{6,7},{7,6},{8,9},{9,8},{10,11... | collective-permute-start | bytes 884744 | tf_op jit(solution)/shard_map/ppermute | solution.py:603
  30.2 2.0 %collective-permute-start.16 = (f32[1,4,16,1152]{3,2,1,0:T(8,128)S(1)}, f32[1,4,16,1152]{3,2,1,0:T(8,128)S(1)}, u32[]{:S(2)}, u32[]{:S(2)}) collective-permute-start(f32[1,4,16,1152]{3,2,1,0:T(8,128)S(1)} %get-tuple-element.41.refs_4_), channel_id=1, source_target_pairs={{0,1},{1,0},{2,3},{3,2},{4,5},{5,4},{6,7},{7,6},{8,9},{9,8},{10,11... | collective-permute-start | bytes 884744 | tf_op jit(solution)/shard_map/ppermute | solution.py:603
  30.7 13.1 %collective-permute-start.9 = (f32[7,4,2,1152]{3,2,1,0:T(2,128)S(1)}, f32[7,4,2,1152]{3,2,1,0:T(2,128)S(1)}, u32[]{:S(2)}, u32[]{:S(2)}) collective-permute-start(f32[7,4,2,1152]{3,2,1,0:T(2,128)S(1)} %get-tuple-element.39.refs_0_), channel_id=1, source_target_pairs={{0,2},{2,0},{1,3},{3,1},{4,6},{6,4},{5,7},{7,5},{8,10},{10,8},{9,1... | collective-permute-start | bytes 774152 | tf_op jit(solution)/shard_map/ppermute | solution.py:601
  40.7 13.7 %collective-permute-start.17 = (f32[112,1152]{1,0:T(8,128)S(1)}, f32[112,1152]{1,0:T(8,128)S(1)}, u32[]{:S(2)}, u32[]{:S(2)}) collective-permute-start(f32[112,1152]{1,0:T(8,128)S(1)} %get-tuple-element.42.refs_12_), channel_id=1, source_target_pairs={{0,2},{2,0},{1,3},{3,1},{4,6},{6,4},{5,7},{7,5},{8,10},{10,8},{9,1... | collective-permute-start | bytes 1548296 | tf_op jit(solution)/shard_map/ppermute | solution.py:601
  42.7 4.3 %collective-permute-start.8 = (f32[7,4,2,1152]{3,2,1,0:T(2,128)S(1)}, f32[7,4,2,1152]{3,2,1,0:T(2,128)S(1)}, u32[]{:S(2)}, u32[]{:S(2)}) collective-permute-start(f32[7,4,2,1152]{3,2,1,0:T(2,128)S(1)} %get-tuple-element.39.refs_0_), channel_id=1, source_target_pairs={{0,1},{1,0},{2,3},{3,2},{4,5},{5,4},{6,7},{7,6},{8,9},{9,8},{10,11... | collective-permute-start | bytes 774152 | tf_op jit(solution)/shard_map/ppermute | solution.py:603
  43.8 3.2 %collective-permute-start.10 = (f32[7,4,2,1152]{3,2,1,0:T(2,128)S(1)}, f32[7,4,2,1152]{3,2,1,0:T(2,128)S(1)}, u32[]{:S(2)}, u32[]{:S(2)}) collective-permute-start(f32[7,4,2,1152]{3,2,1,0:T(2,128)S(1)} %collective-permute-done.9.refs_2_), channel_id=1, source_target_pairs={{0,1},{1,0},{2,3},{3,2},{4,5},{5,4},{6,7},{7,6},{8,9},{9,8},{10,11... | collective-permute-start | bytes 774152 | tf_op jit(solution)/shard_map/ppermute | solution.py:603
  43.8 1.9 %collective-permute-start.13 = (f32[3,4,2,1152]{3,2,1,0:T(2,128)S(1)}, f32[3,4,2,1152]{3,2,1,0:T(2,128)S(1)}, u32[]{:S(2)}, u32[]{:S(2)}) collective-permute-start(f32[3,4,2,1152]{3,2,1,0:T(2,128)S(1)} %get-tuple-element.36.refs_8_), channel_id=1, source_target_pairs={{0,1},{1,0},{2,3},{3,2},{4,5},{5,4},{6,7},{7,6},{8,9},{9,8},{10,11... | collective-permute-start | bytes 331784 | tf_op jit(solution)/shard_map/ppermute | solution.py:603
  44.3 1.3 %collective-permute-start.11 = (f32[2,4,2,1152]{3,2,1,0:T(2,128)S(1)}, f32[2,4,2,1152]{3,2,1,0:T(2,128)S(1)}, u32[]{:S(2)}, u32[]{:S(2)}) collective-permute-start(f32[2,4,2,1152]{3,2,1,0:T(2,128)S(1)} %get-tuple-element.35.refs_4_), channel_id=1, source_target_pairs={{0,1},{1,0},{2,3},{3,2},{4,5},{5,4},{6,7},{7,6},{8,9},{9,8},{10,11... | collective-permute-start | bytes 221192 | tf_op jit(solution)/shard_map/ppermute | solution.py:603
  45.6 1.4 %collective-permute-start.14 = (f32[3,4,2,1152]{3,2,1,0:T(2,128)S(1)}, f32[3,4,2,1152]{3,2,1,0:T(2,128)S(1)}, u32[]{:S(2)}, u32[]{:S(2)}) collective-permute-start(f32[3,4,2,1152]{3,2,1,0:T(2,128)S(1)} %collective-permute-done.5.refs_4_.refs_10_), channel_id=1, source_target_pairs={{0,1},{1,0},{2,3},{3,2},{4,5},{5,4},{6,7},{7,6},{8,9},{9,8},{10,11... | collective-permute-start | bytes 331784 | tf_op jit(solution)/shard_map/ppermute | solution.py:603
  45.7 1.3 %collective-permute-start.12 = (f32[2,4,2,1152]{3,2,1,0:T(2,128)S(1)}, f32[2,4,2,1152]{3,2,1,0:T(2,128)S(1)}, u32[]{:S(2)}, u32[]{:S(2)}) collective-permute-start(f32[2,4,2,1152]{3,2,1,0:T(2,128)S(1)} %collective-permute-done.4.refs_3_.refs_6_), channel_id=1, source_target_pairs={{0,1},{1,0},{2,3},{3,2},{4,5},{5,4},{6,7},{7,6},{8,9},{9,8},{10,11... | collective-permute-start | bytes 221192 | tf_op jit(solution)/shard_map/ppermute | solution.py:603
  (5 other events, 22.8 us)

commit v7 on v5

--- a/solution.py
+++ b/solution.py
@@ -15,7 +15,7 @@
 
 
 def params():
-    return pltpu.CompilerParams(vmem_limit_bytes=48 * 1024 * 1024)
+    return pltpu.CompilerParams(vmem_limit_bytes=16 * 1024 * 1024)
 
 
 def cost(flops, bytes_accessed):
@@ -77,68 +77,91 @@
     return change - (t_north - south_of(t_north, t_below)) * inverse
 
 
-def inner_kernel(band_ref, table_ref, thick_ref, u_ref, v_ref, tracer_ref, out_ref, sum_ref, last_ref, leading_ref, near_ref, near_rest_ref):
-    rows, width = thick_ref.shape[1:]
-    geo = table_ref[band_ref[0]]
-    thick, u, v = thick_ref[0], u_ref[0], v_ref[0]
+def inner_kernel(band_ref, table_hbm, thick_hbm, u_hbm, v_hbm, tracer_hbm, *refs):
+    out_ref, sum_ref, last_ref, leading_ref, near_ref, near_rest_ref, geo_ref, wind_ref, tracer_ref, sems = refs
+    T, L, rows, width = tracer_ref.shape
+
+    def copies(k):
+        return [
+            pltpu.make_async_copy(thick_hbm.at[k], wind_ref.at[0, k], sems.at[0, k]),
+            pltpu.make_async_copy(u_hbm.at[k], wind_ref.at[1, k], sems.at[1, k]),
+            pltpu.make_async_copy(v_hbm.at[k], wind_ref.at[2, k], sems.at[2, k]),
+        ] + [
+            pltpu.make_async_copy(tracer_hbm.at[c, k], tracer_ref.at[c, k], sems.at[3 + c, k]) for c in range(T)
+        ]
+
+    table_copy = pltpu.make_async_copy(table_hbm.at[band_ref[0]], geo_ref, sems.at[3 + T, 0])
+    table_copy.start()
+    for k in range(L):
+        for copy in copies(k):
+            copy.start()
+    table_copy.wait()
+    geo = geo_ref[...]
     nothing = jnp.zeros((1, width), jnp.float32)
-    east, north, below = fluxes(geo, thick, u, v, nothing, nothing, nothing)
     inverse = geo[0:rows, 2:3]
-    new = thick - (east - west_of(east)) - (north - south_of(north, below)) * inverse
-    def store(field, value):
-        out_ref[field, 0] = value
-        ref, at = (near_ref, field) if field < 2 else (near_rest_ref, field - 2)
-        ref[at, 0, 0:1] = value[1:2]
-        ref[at, 0, 1:2] = value[rows - 2 : rows - 1]
-
-    store(0, new)
-    last_ref[0, 0] = thick[rows - 1 : rows]
-    last_ref[1, 0] = v[rows - 1 : rows]
-    leading_ref[0, 0] = thick[0:1]
-    leading_ref[1, 0] = thick[1:2]
-    leading_ref[2, 0] = u[0:1]
-    leading_ref[3, 0] = v[0:1]
-
-    @pl.when(pl.program_id(0) == 0)
-    def _():
-        sum_ref[...] = new
-
-    @pl.when(pl.program_id(0) > 0)
-    def _():
+    sum_ref[...] = jnp.zeros_like(sum_ref)
+
+    def level(k, carry):
+        for copy in copies(k):
+            copy.wait()
+        thick, u, v = wind_ref[0, k], wind_ref[1, k], wind_ref[2, k]
+        east, north, below = fluxes(geo, thick, u, v, nothing, nothing, nothing)
+        new = thick - (east - west_of(east)) - (north - south_of(north, below)) * inverse
+
+        def store(field, value):
+            out_ref[field, k] = value
+            ref, at = (near_ref, field) if field < 2 else (near_rest_ref, field - 2)
+            ref[at, k, 0:1] = value[1:2]
+            ref[at, k, 1:2] = value[rows - 2 : rows - 1]
+
+        store(0, new)
         sum_ref[...] += new
-
-    scale = 1.0 / new
-    for c in range(tracer_ref.shape[0]):
-        q = tracer_ref[c, 0]
-        last_ref[2 + c, 0] = q[rows - 1 : rows]
-        leading_ref[4 + c, 0] = q[0:1]
-        change = tracer_change(q, nothing, nothing, thick, u, v, nothing, east, north, below, inverse)
-        store(1 + c, change * scale)
+        last_ref[0, k] = thick[rows - 1 : rows]
+        last_ref[1, k] = v[rows - 1 : rows]
+        leading_ref[0, k] = thick[0:1]
+        leading_ref[1, k] = thick[1:2]
+        leading_ref[2, k] = u[0:1]
+        leading_ref[3, k] = v[0:1]
+        scale = 1.0 / new
+        for c in range(T):
+            q = tracer_ref[c, k]
+            last_ref[2 + c, k] = q[rows - 1 : rows]
+            leading_ref[4 + c, k] = q[0:1]
+            change = tracer_change(q, nothing, nothing, thick, u, v, nothing, east, north, below, inverse)
+            store(1 + c, change * scale)
+        return carry
+
+    lax.fori_loop(0, L, level, 0)
 
 
 def inner_step(band, table, thickness, wind_u, wind_v, tracers):
     L, R, N = thickness.shape
     T = tracers.shape[0]
-    level = pl.BlockSpec((1, R, N), lambda k: (k, 0, 0))
-    some = lambda n, rows: pl.BlockSpec((n, 1, rows, N), lambda k: (0, k, 0, 0))
+    shape = lambda n, rows: jax.ShapeDtypeStruct((n, L, rows, N), jnp.float32)
     in_hbm = lambda x: pltpu.with_memory_space_constraint(x, pltpu.HBM)
+    out_shape = [
+        shape(1 + T, R),
+        jax.ShapeDtypeStruct((R, N), jnp.float32),
+        shape(2 + T, 1),
+        shape(4 + T, 1),
+        shape(2, 2),
+        shape(T - 1, 2),
+    ]
     return pl.pallas_call(
         inner_kernel,
-        grid=(L,),
-        in_specs=[SMEM, pl.BlockSpec(table.shape, lambda k: (0, 0, 0)), level, level, level, some(T, R)],
-        out_specs=[some(1 + T, R), pl.BlockSpec((R, N), lambda k: (0, 0)), some(2 + T, 1), some(4 + T, 1), some(2, 2), some(T - 1, 2)],
-        out_shape=[
-            jax.ShapeDtypeStruct((1 + T, L, R, N), jnp.float32),
-            jax.ShapeDtypeStruct((R, N), jnp.float32),
-            jax.ShapeDtypeStruct((2 + T, L, 1, N), jnp.float32),
-            jax.ShapeDtypeStruct((4 + T, L, 1, N), jnp.float32),
-            jax.ShapeDtypeStruct((2, L, 2, N), jnp.float32),
-            jax.ShapeDtypeStruct((T - 1, L, 2, N), jnp.float32),
+        in_specs=[SMEM] + after([table, thickness, wind_u, wind_v, tracers]),
+        out_specs=[VMEM] * len(out_shape),
+        out_shape=out_shape,
+        scratch_shapes=[
+            pltpu.VMEM(table.shape[1:], jnp.float32),
+            pltpu.VMEM((3, L, R, N), jnp.float32),
+            pltpu.VMEM((T, L, R, N), jnp.float32),
+            pltpu.SemaphoreType.DMA((4 + T, L)),
         ],
         compiler_params=params(),
         cost_estimate=cost(130 * L * R * N, 4 * L * R * N * (8 + 2 * T)),
         name="inner_step",
-    )(band, in_hbm(table), in_hbm(thickness), in_hbm(wind_u), in_hbm(wind_v), in_hbm(tracers))
+    )(band, *[in_hbm(a) for a in (table, thickness, wind_u, wind_v, tracers)])
 
 
 def filter_tables(N):

time: 55.1 us -> 54.2 us (0.984)
  Pallas kernels: 20.7 us -> 19.1 us
  waiting for transfers between devices: 13.6 us -> 14.6 us
    ppermute x6, waiting for transfers between devices: 7.92 us -> 8.79 us  [shifted(): lax.ppermute(value, 'lev', [(i, (i + s) % lev_count) for i in range(lev_c...]
    pallas_call x2, Pallas kernels: 5.2 us -> 4.36 us  [remap_parts(): pl.pallas_call(functools.partial(remap_kernel, counts, tuple(steps), tupl...]
    pallas_call x1, Pallas kernels: 3.88 us -> 3.23 us  [inner_step(): pl.pallas_call(inner_kernel, in_specs=[SMEM] + after([table, thickness, w...]
    unnamed x30 -> x26, local copies, waits for them, and re-layouts: 1.37 us -> 1.36 us
  transfers between devices with their start and end apart: 18 -> 18, of which waited for: 9 -> 9; matrix products, arithmetic and copies ran while one was open for 0% -> 0% of each run, Pallas kernels for 29% -> 28%
where the time goes in v7:
time: 54.2 us; the launch traced here: 54 us
  Pallas kernels  19.1 us (35%)
  starting transfers between devices  17.9 us (33%)
  waiting for transfers between devices  14.6 us (27%)
  local copies, waits for them, and re-layouts  1.43 us (3%)
  between operations  0.85 us (2%)
    ppermute x6, starting transfers between devices, shifted(): lax.ppermute(value, 'lev', [(i, (i + s) % lev_count) for i in range(lev_c...  9.57 us
    ppermute x6, waiting for transfers between devices, shifted(): lax.ppermute(value, 'lev', [(i, (i + s) % lev_count) for i in range(lev_c...  8.79 us
    ppermute x1, starting transfers between devices, per_device(): up = lax.ppermute(last, 'lat', northward)  4.55 us
    pallas_call x2, Pallas kernels, remap_parts(): pl.pallas_call(functools.partial(remap_kernel, counts, tuple(steps), tupl...  4.36 us
    pallas_call x1, Pallas kernels, remap_edges(): pl.pallas_call(functools.partial(remap_edge_kernel, counts, near_fields),...  3.66 us
    pallas_call x1, Pallas kernels, second_step(): pl.pallas_call(functools.partial(second_kernel, lat_rows), grid=(L,), in_...  3.66 us
    pallas_call x1, Pallas kernels, finish_tracers(): pl.pallas_call(functools.partial(finish_kernel, counts, margin), in_specs...  3.26 us
    pallas_call x1, Pallas kernels, inner_step(): pl.pallas_call(inner_kernel, in_specs=[SMEM] + after([table, thickness, w...  3.23 us
  transfers between devices with their start and end apart: 18, of which 9 were waited for; matrix products, arithmetic and copies ran while one was open for 0% of the time, Pallas kernels for 28%

profile of v7, /device:TPU:0, one launch (start us, length us, event | category | flops | bytes accessed | tf_op | source)
XLA Modules:
  0.0 54.0 jit_solution(9533486223131193651)
XLA Ops:
  0.6 3.2 %inner_step.1 = (f32[5,4,16,1152]{3,2,1,0:T(8,128)S(1)}, f32[16,1152]{1,0:T(8,128)S(1)}, f32[6,4,1,1152]{3,2,1,0:T(1,128)S(1)}, f32[8,4,1,1152]{3,2,1,0:T(1,128)...) custom-call(s32[1]{0:T(128)} %bitcast.2.band_ref, f32[4,24,128]{2,1,0:T(8,128)} %constant.17.clone.table_hbm.table_ref, ...), custom_call_target="tpu_custom_call" | custom-call | flops 9584640 | bytes 4718592 | tf_op jit(solution)/shard_map/inner_step/pallas_call | solution.py:150
  3.9 0.7 %copy-done.8 = f32[8,4,1,1152]{3,2,1,0:T(1,128)} copy-done((f32[8,4,1,1152]{3,2,1,0:T(1,128)}, f32[8,4,1,1152]{3,2,1,0:T(1,128)S(1)}, u32[]{:S(2)}) %copy-start.8) | copy-done | bytes 147480
  4.5 0.6 %copy-done.10 = f32[6,4,1,1152]{3,2,1,0:T(1,128)} copy-done((f32[6,4,1,1152]{3,2,1,0:T(1,128)}, f32[6,4,1,1152]{3,2,1,0:T(1,128)S(1)}, u32[]{:S(2)}) %copy-start.10) | copy-done | bytes 110616
  5.6 2.5 %collective-permute-start.1 = (f32[16,1152]{1,0:T(8,128)S(1)}, f32[16,1152]{1,0:T(8,128)S(1)}, u32[]{:S(2)}, u32[]{:S(2)}) collective-permute-start(f32[16,1152]{1,0:T(8,128)S(1)} %get-tuple-element.26), channel_id=1, source_target_pairs={{0,2},{2,0},{1,3},{3,1},{4,6},{6,4},{5,7},{7,5},{8,10},{10,8},{9,1... | collective-permute-start | bytes 221192 | tf_op jit(solution)/shard_map/ppermute | solution.py:582
  8.3 1.7 %collective-permute-start.5 = (f32[3,4,2,1152]{3,2,1,0:T(2,128)S(1)}, f32[3,4,2,1152]{3,2,1,0:T(2,128)S(1)}, u32[]{:S(2)}, u32[]{:S(2)}) collective-permute-start(f32[3,4,2,1152]{3,2,1,0:T(2,128)S(1)} %get-tuple-element.30.refs_8_), channel_id=1, source_target_pairs={{0,2},{2,0},{1,3},{3,1},{4,6},{6,4},{5,7},{7,5},{8,10},{10,8},{9,1... | collective-permute-start | bytes 331784 | tf_op jit(solution)/shard_map/ppermute | solution.py:582
  10.4 0.7 %collective-permute-done.1.refs_4_.refs_6_.refs_2_ = f32[16,1152]{1,0:T(8,128)S(1)} collective-permute-done((f32[16,1152]{1,0:T(8,128)S(1)}, f32[16,1152]{1,0:T(8,128)S(1)}, u32[]{:S(2)}, u32[]{:S(2)}) %collective-permute-start.1) | collective-permute-done | bytes 73760 | tf_op jit(solution)/shard_map/ppermute | solution.py:582
  11.1 1.3 %collective-permute-done.2.refs_5_.refs_7_.refs_3_ = f32[16,1152]{1,0:T(8,128)S(1)} collective-permute-done((f32[16,1152]{1,0:T(8,128)S(1)}, f32[16,1152]{1,0:T(8,128)S(1)}, u32[]{:S(2)}, u32[]{:S(2)}) %collective-permute-start.2) | collective-permute-done | bytes 73760 | tf_op jit(solution)/shard_map/ppermute | solution.py:590
  12.4 2.0 %remap_parts.2.refs_2_ = f32[192,1152]{1,0:T(8,128)S(1)} custom-call(s32[2]{0:T(128)S(1)} %pad_add_fusion.place_ref, f32[16]{0:T(128)S(1)} %copy-done.7, f32[5,4,16,1152]{3,2,1,0:T(8,128)S(1)} %get-tuple-element.25.refs_0_.refs_2_, f32[5,4,16,1152]{3,2,1,0:T(8,128)S(1)} %collective-permute-done.refs_1_.refs_3_, ...), custom_call_target="tpu_custom_call" | custom-call | flops 7667712 | bytes 4423680 | tf_op jit(solution)/shard_map/remap_parts/pallas_call | solution.py:433
  14.3 1.7 %collective-permute-start.3 = (f32[192,1152]{1,0:T(8,128)S(1)}, f32[192,1152]{1,0:T(8,128)S(1)}, u32[]{:S(2)}, u32[]{:S(2)}) collective-permute-start(f32[192,1152]{1,0:T(8,128)S(1)} %remap_parts.2.refs_2_), channel_id=1, source_target_pairs={{0,2},{2,0},{1,3},{3,1},{4,6},{6,4},{5,7},{7,5},{8,10},{10,8},{9,1... | collective-permute-start | bytes 2654216 | tf_op jit(solution)/shard_map/ppermute | solution.py:582
  16.0 0.6 %collective-permute-done.4.refs_3_.refs_6_ = f32[2,4,2,1152]{3,2,1,0:T(2,128)S(1)} collective-permute-done((f32[2,4,2,1152]{3,2,1,0:T(2,128)S(1)}, f32[2,4,2,1152]{3,2,1,0:T(2,128)S(1)}, u32[]{:S(2)}, u32[]{:S(2)}) %collective-permute-start.4) | collective-permute-done | bytes 73760 | tf_op jit(solution)/shard_map/ppermute | solution.py:582
  16.8 1.6 %collective-permute-start.7 = (f32[8,4,1,1152]{3,2,1,0:T(1,128)S(1)}, f32[8,4,1,1152]{3,2,1,0:T(1,128)S(1)}, u32[]{:S(2)}, u32[]{:S(2)}) collective-permute-start(f32[8,4,1,1152]{3,2,1,0:T(1,128)S(1)} %get-tuple-element.32), channel_id=1, source_target_pairs={{4,0},{8,4},{12,8},{5,1},{9,5},{13,9},{6,2},{10,6},{14,10},{7,3},{... | collective-permute-start | bytes 442376 | tf_op jit(solution)/shard_map/ppermute | solution.py:627
  18.4 4.6 %collective-permute-start.6 = (f32[6,4,1,1152]{3,2,1,0:T(1,128)S(1)}, f32[6,4,1,1152]{3,2,1,0:T(1,128)S(1)}, u32[]{:S(2)}, u32[]{:S(2)}) collective-permute-start(f32[6,4,1,1152]{3,2,1,0:T(1,128)S(1)} %get-tuple-element.31), channel_id=1, source_target_pairs={{0,4},{4,8},{8,12},{1,5},{5,9},{9,13},{2,6},{6,10},{10,14},{3,7},{... | collective-permute-start | bytes 331784 | tf_op jit(solution)/shard_map/ppermute | solution.py:626
  22.9 2.3 %collective-permute-done.6.up_ref = f32[6,4,1,1152]{3,2,1,0:T(1,128)S(1)} collective-permute-done((f32[6,4,1,1152]{3,2,1,0:T(1,128)S(1)}, f32[6,4,1,1152]{3,2,1,0:T(1,128)S(1)}, u32[]{:S(2)}, u32[]{:S(2)}) %collective-permute-start.6) | collective-permute-done | bytes 110624 | tf_op jit(solution)/shard_map/ppermute | solution.py:626
  25.4 3.7 %second_step.1 = (f32[1,4,16,1152]{3,2,1,0:T(8,128)S(1)}, f32[1,4,16,1152]{3,2,1,0:T(8,128)S(1)}, f32[7,4,2,1152]{3,2,1,0:T(2,128)S(1)}) custom-call(s32[1]{0:T(128)} %bitcast.2.band_ref, f32[4,24,128]{2,1,0:T(8,128)S(1)} %copy-done.6, f32[4,16,1152]{2,1,0:T(8,128)S(1)} %copy-done.1, f32[4,16,1152]{2,1,0:T(8,128)S(1)} %copy-done.2, ...), custom_call_target="tpu_custom_call" | custom-call | flops 503316480 | bytes 3538944 | tf_op jit(solution)/shard_map/second_step/pallas_call | solution.py:293
  29.6 1.7 %collective-permute-start.9 = (f32[7,4,2,1152]{3,2,1,0:T(2,128)S(1)}, f32[7,4,2,1152]{3,2,1,0:T(2,128)S(1)}, u32[]{:S(2)}, u32[]{:S(2)}) collective-permute-start(f32[7,4,2,1152]{3,2,1,0:T(2,128)S(1)} %get-tuple-element.33.refs_0_), channel_id=1, source_target_pairs={{0,2},{2,0},{1,3},{3,1},{4,6},{6,4},{5,7},{7,5},{8,10},{10,8},{9,1... | collective-permute-start | bytes 774152 | tf_op jit(solution)/shard_map/ppermute | solution.py:582
  31.3 5.6 %collective-permute-done.3.refs_8_.refs_4_ = f32[192,1152]{1,0:T(8,128)S(1)} collective-permute-done((f32[192,1152]{1,0:T(8,128)S(1)}, f32[192,1152]{1,0:T(8,128)S(1)}, u32[]{:S(2)}, u32[]{:S(2)}) %collective-permute-start.3) | collective-permute-done | bytes 884768 | tf_op jit(solution)/shard_map/ppermute | solution.py:582
  36.9 2.4 %remap_parts.3 = (f32[2,4,16,1152]{3,2,1,0:T(8,128)S(1)}, f32[112,1152]{1,0:T(8,128)S(1)}) custom-call(s32[2]{0:T(128)S(1)} %pad_add_fusion.place_ref, f32[16]{0:T(128)S(1)} %copy-done.7, f32[5,4,16,1152]{3,2,1,0:T(8,128)S(1)} %get-tuple-element.25.refs_0_.refs_2_, f32[5,4,16,1152]{3,2,1,0:T(8,128)S(1)} %collective-permute-done.refs_1_.refs_3_, ...), custom_call_target="tpu_custom_call" | custom-call | flops 10616832 | bytes 3538944 | tf_op jit(solution)/shard_map/remap_parts/pallas_call | solution.py:433
  39.3 1.7 %collective-permute-start.17 = (f32[112,1152]{1,0:T(8,128)S(1)}, f32[112,1152]{1,0:T(8,128)S(1)}, u32[]{:S(2)}, u32[]{:S(2)}) collective-permute-start(f32[112,1152]{1,0:T(8,128)S(1)} %get-tuple-element.36.refs_12_), channel_id=1, source_target_pairs={{0,2},{2,0},{1,3},{3,1},{4,6},{6,4},{5,7},{7,5},{8,10},{10,8},{9,1... | collective-permute-start | bytes 1548296 | tf_op jit(solution)/shard_map/ppermute | solution.py:582
  40.9 1.4 %collective-permute-done.9.refs_2_ = f32[7,4,2,1152]{3,2,1,0:T(2,128)S(1)} collective-permute-done((f32[7,4,2,1152]{3,2,1,0:T(2,128)S(1)}, f32[7,4,2,1152]{3,2,1,0:T(2,128)S(1)}, u32[]{:S(2)}, u32[]{:S(2)}) %collective-permute-start.9) | collective-permute-done | bytes 258080 | tf_op jit(solution)/shard_map/ppermute | solution.py:582
  42.9 1.3 %collective-permute-done.11.refs_5_ = f32[2,4,2,1152]{3,2,1,0:T(2,128)S(1)} collective-permute-done((f32[2,4,2,1152]{3,2,1,0:T(2,128)S(1)}, f32[2,4,2,1152]{3,2,1,0:T(2,128)S(1)}, u32[]{:S(2)}, u32[]{:S(2)}) %collective-permute-start.11) | collective-permute-done | bytes 73760 | tf_op jit(solution)/shard_map/ppermute | solution.py:584
  44.7 0.9 %collective-permute-done.12.refs_7_ = f32[2,4,2,1152]{3,2,1,0:T(2,128)S(1)} collective-permute-done((f32[2,4,2,1152]{3,2,1,0:T(2,128)S(1)}, f32[2,4,2,1152]{3,2,1,0:T(2,128)S(1)}, u32[]{:S(2)}, u32[]{:S(2)}) %collective-permute-start.12) | collective-permute-done | bytes 73760 | tf_op jit(solution)/shard_map/ppermute | solution.py:584
  45.6 3.7 %remap_edges.1 = (f32[6,4,2,1152]{3,2,1,0:T(2,128)S(1)}, f32[4,2,1152]{2,1,0:T(2,128)S(1)}, f32[4,4,2,1152]{3,2,1,0:T(2,128)S(1)}) custom-call(s32[2]{0:T(128)S(1)} %pad_add_fusion.place_ref, f32[16]{0:T(128)S(1)} %copy-done.7, f32[7,4,2,1152]{3,2,1,0:T(2,128)S(1)} %get-tuple-element.33.refs_0_, f32[7,4,2,1152]{3,2,1,0:T(2,128)S(1)} %collective-permute-done.8.refs_1_, ...), custom_call_target="tpu_custom_call" | custom-call | flops 5898240 | bytes 3096576 | tf_op jit(solution)/shard_map/remap_edges/pallas_call | solution.py:471
  49.3 3.3 %finish_tracers.1 = (f32[4,4,16,1152]{3,2,1,0:T(8,128)}, f32[4,16,1152]{2,1,0:T(8,128)}, f32[8,128]{1,0:T(8,128)S(1)}) custom-call(s32[2]{0:T(128)S(1)} %pad_add_fusion.place_ref, f32[16]{0:T(128)S(1)} %copy-done.7, f32[5,4,16,1152]{3,2,1,0:T(8,128)S(1)} %get-tuple-element.25.refs_0_.refs_2_, f32[5,4,16,1152]{3,2,1,0:T(8,128)S(1)} %collective-permute-done.refs_1_.refs_3_, ...), custom_call_target="tpu_custom_call" | custom-call | flops 7667712 | bytes 5898240 | tf_op jit(solution)/shard_map/finish_tracers/pallas_call | solution.py:522
  53.0 0.9 %finish_winds.1 = (f32[4,16,1152]{2,1,0:T(8,128)}, f32[4,16,1152]{2,1,0:T(8,128)}) custom-call(f32[2,4,16,1152]{3,2,1,0:T(8,128)S(1)} %get-tuple-element.41.own_ref, f32[6,4,2,1152]{3,2,1,0:T(2,128)S(1)} %get-tuple-element.38.refs_6_.edge_ref, f32[112,1152]{1,0:T(8,128)S(1)} %collective-permute-done.17.refs_0_, f32[8,128]{1,0:T(8,128)S(1)} %get-tuple-element.42.refs_1_), custom_call_target="tpu_custom_call" | custom-call | flops 147456 | bytes 1769472 | tf_op jit(solution)/shard_map/finish_winds/pallas_call | solution.py:552
  (48 shorter events, 3.3 us)
Async XLA Ops:
  0.6 11.8 %copy-start.7 = (f32[16]{0:T(128)S(1)}, f32[16]{0:T(128)}, u32[]{:S(2)}) copy-start(f32[16]{0:T(128)} %weight_ref.7) | copy-start | bytes 196
  5.2 7.2 %collective-permute-start = (f32[5,4,16,1152]{3,2,1,0:T(8,128)S(1)}, f32[5,4,16,1152]{3,2,1,0:T(8,128)S(1)}, u32[]{:S(2)}, u32[]{:S(2)}) collective-permute-start(f32[5,4,16,1152]{3,2,1,0:T(8,128)S(1)} %get-tuple-element.25.refs_0_.refs_2_), channel_id=1, source_target_pairs={{0,1},{1,0},{2,3},{3,2},{4,5},{5,4},{6,7},{7,6},{8,9},{9,8},{10,11... | collective-permute-start | bytes 4423688 | tf_op jit(solution)/shard_map/ppermute | solution.py:584
  5.6 5.4 %collective-permute-start.1 = (f32[16,1152]{1,0:T(8,128)S(1)}, f32[16,1152]{1,0:T(8,128)S(1)}, u32[]{:S(2)}, u32[]{:S(2)}) collective-permute-start(f32[16,1152]{1,0:T(8,128)S(1)} %get-tuple-element.26), channel_id=1, source_target_pairs={{0,2},{2,0},{1,3},{3,1},{4,6},{6,4},{5,7},{7,5},{8,10},{10,8},{9,1... | collective-permute-start | bytes 221192 | tf_op jit(solution)/shard_map/ppermute | solution.py:582
  8.1 4.2 %collective-permute-start.2 = (f32[16,1152]{1,0:T(8,128)S(1)}, f32[16,1152]{1,0:T(8,128)S(1)}, u32[]{:S(2)}, u32[]{:S(2)}) collective-permute-start(f32[16,1152]{1,0:T(8,128)S(1)} %get-tuple-element.26), channel_id=1, source_target_pairs={{0,3},{1,2},{2,1},{3,0},{4,7},{5,6},{6,5},{7,4},{8,11},{9,10},{10,... | collective-permute-start | bytes 221192 | tf_op jit(solution)/shard_map/ppermute | solution.py:590
  8.3 8.4 %collective-permute-start.5 = (f32[3,4,2,1152]{3,2,1,0:T(2,128)S(1)}, f32[3,4,2,1152]{3,2,1,0:T(2,128)S(1)}, u32[]{:S(2)}, u32[]{:S(2)}) collective-permute-start(f32[3,4,2,1152]{3,2,1,0:T(2,128)S(1)} %get-tuple-element.30.refs_8_), channel_id=1, source_target_pairs={{0,2},{2,0},{1,3},{3,1},{4,6},{6,4},{5,7},{7,5},{8,10},{10,8},{9,1... | collective-permute-start | bytes 331784 | tf_op jit(solution)/shard_map/ppermute | solution.py:582
  10.0 6.7 %collective-permute-start.4 = (f32[2,4,2,1152]{3,2,1,0:T(2,128)S(1)}, f32[2,4,2,1152]{3,2,1,0:T(2,128)S(1)}, u32[]{:S(2)}, u32[]{:S(2)}) collective-permute-start(f32[2,4,2,1152]{3,2,1,0:T(2,128)S(1)} %get-tuple-element.29.refs_4_), channel_id=1, source_target_pairs={{0,2},{2,0},{1,3},{3,1},{4,6},{6,4},{5,7},{7,5},{8,10},{10,8},{9,1... | collective-permute-start | bytes 221192 | tf_op jit(solution)/shard_map/ppermute | solution.py:582
  14.3 22.5 %collective-permute-start.3 = (f32[192,1152]{1,0:T(8,128)S(1)}, f32[192,1152]{1,0:T(8,128)S(1)}, u32[]{:S(2)}, u32[]{:S(2)}) collective-permute-start(f32[192,1152]{1,0:T(8,128)S(1)} %remap_parts.2.refs_2_), channel_id=1, source_target_pairs={{0,2},{2,0},{1,3},{3,1},{4,6},{6,4},{5,7},{7,5},{8,10},{10,8},{9,1... | collective-permute-start | bytes 2654216 | tf_op jit(solution)/shard_map/ppermute | solution.py:582
  16.7 8.6 %copy-start = (f32[4,4,16,1152]{3,2,1,0:T(8,128)S(1)}, f32[4,4,16,1152]{3,2,1,0:T(8,128)}, u32[]{:S(2)}) copy-start(f32[4,4,16,1152]{3,2,1,0:T(8,128)} %tracer_ref.1) | copy-start | bytes 3538948
  16.7 8.6 %copy-start.1 = (f32[4,16,1152]{2,1,0:T(8,128)S(1)}, f32[4,16,1152]{2,1,0:T(8,128)}, u32[]{:S(2)}) copy-start(f32[4,16,1152]{2,1,0:T(8,128)} %thick_ref.1) | copy-start | bytes 884740
  16.7 8.6 %copy-start.2 = (f32[4,16,1152]{2,1,0:T(8,128)S(1)}, f32[4,16,1152]{2,1,0:T(8,128)}, u32[]{:S(2)}) copy-start(f32[4,16,1152]{2,1,0:T(8,128)} %u_ref.1) | copy-start | bytes 884740
  16.7 8.6 %copy-start.3 = (f32[4,16,1152]{2,1,0:T(8,128)S(1)}, f32[4,16,1152]{2,1,0:T(8,128)}, u32[]{:S(2)}) copy-start(f32[4,16,1152]{2,1,0:T(8,128)} %v_ref.1) | copy-start | bytes 884740
  16.7 8.6 %copy-start.4 = (bf16[5,256,256]{2,1,0:T(8,128)(2,1)S(1)}, bf16[5,256,256]{2,1,0:T(8,128)(2,1)}, u32[]{:S(2)}) copy-start(bf16[5,256,256]{2,1,0:T(8,128)(2,1)} %constant.18.clone.high_ref) | copy-start | bytes 1966084
  16.8 8.4 %collective-permute-start.7 = (f32[8,4,1,1152]{3,2,1,0:T(1,128)S(1)}, f32[8,4,1,1152]{3,2,1,0:T(1,128)S(1)}, u32[]{:S(2)}, u32[]{:S(2)}) collective-permute-start(f32[8,4,1,1152]{3,2,1,0:T(1,128)S(1)} %get-tuple-element.32), channel_id=1, source_target_pairs={{4,0},{8,4},{12,8},{5,1},{9,5},{13,9},{6,2},{10,6},{14,10},{7,3},{... | collective-permute-start | bytes 442376 | tf_op jit(solution)/shard_map/ppermute | solution.py:627
  18.4 6.9 %collective-permute-start.6 = (f32[6,4,1,1152]{3,2,1,0:T(1,128)S(1)}, f32[6,4,1,1152]{3,2,1,0:T(1,128)S(1)}, u32[]{:S(2)}, u32[]{:S(2)}) collective-permute-start(f32[6,4,1,1152]{3,2,1,0:T(1,128)S(1)} %get-tuple-element.31), channel_id=1, source_target_pairs={{0,4},{4,8},{8,12},{1,5},{5,9},{9,13},{2,6},{6,10},{10,14},{3,7},{... | collective-permute-start | bytes 331784 | tf_op jit(solution)/shard_map/ppermute | solution.py:626
  29.0 2.3 %collective-permute-start.15 = (f32[1,4,16,1152]{3,2,1,0:T(8,128)S(1)}, f32[1,4,16,1152]{3,2,1,0:T(8,128)S(1)}, u32[]{:S(2)}, u32[]{:S(2)}) collective-permute-start(f32[1,4,16,1152]{3,2,1,0:T(8,128)S(1)} %get-tuple-element.34.refs_2_), channel_id=1, source_target_pairs={{0,1},{1,0},{2,3},{3,2},{4,5},{5,4},{6,7},{7,6},{8,9},{9,8},{10,11... | collective-permute-start | bytes 884744 | tf_op jit(solution)/shard_map/ppermute | solution.py:584
  29.1 2.2 %collective-permute-start.16 = (f32[1,4,16,1152]{3,2,1,0:T(8,128)S(1)}, f32[1,4,16,1152]{3,2,1,0:T(8,128)S(1)}, u32[]{:S(2)}, u32[]{:S(2)}) collective-permute-start(f32[1,4,16,1152]{3,2,1,0:T(8,128)S(1)} %get-tuple-element.35.refs_4_), channel_id=1, source_target_pairs={{0,1},{1,0},{2,3},{3,2},{4,5},{5,4},{6,7},{7,6},{8,9},{9,8},{10,11... | collective-permute-start | bytes 884744 | tf_op jit(solution)/shard_map/ppermute | solution.py:584
  29.6 12.8 %collective-permute-start.9 = (f32[7,4,2,1152]{3,2,1,0:T(2,128)S(1)}, f32[7,4,2,1152]{3,2,1,0:T(2,128)S(1)}, u32[]{:S(2)}, u32[]{:S(2)}) collective-permute-start(f32[7,4,2,1152]{3,2,1,0:T(2,128)S(1)} %get-tuple-element.33.refs_0_), channel_id=1, source_target_pairs={{0,2},{2,0},{1,3},{3,1},{4,6},{6,4},{5,7},{7,5},{8,10},{10,8},{9,1... | collective-permute-start | bytes 774152 | tf_op jit(solution)/shard_map/ppermute | solution.py:582
  39.3 13.8 %collective-permute-start.17 = (f32[112,1152]{1,0:T(8,128)S(1)}, f32[112,1152]{1,0:T(8,128)S(1)}, u32[]{:S(2)}, u32[]{:S(2)}) collective-permute-start(f32[112,1152]{1,0:T(8,128)S(1)} %get-tuple-element.36.refs_12_), channel_id=1, source_target_pairs={{0,2},{2,0},{1,3},{3,1},{4,6},{6,4},{5,7},{7,5},{8,10},{10,8},{9,1... | collective-permute-start | bytes 1548296 | tf_op jit(solution)/shard_map/ppermute | solution.py:582
  40.9 4.7 %collective-permute-start.8 = (f32[7,4,2,1152]{3,2,1,0:T(2,128)S(1)}, f32[7,4,2,1152]{3,2,1,0:T(2,128)S(1)}, u32[]{:S(2)}, u32[]{:S(2)}) collective-permute-start(f32[7,4,2,1152]{3,2,1,0:T(2,128)S(1)} %get-tuple-element.33.refs_0_), channel_id=1, source_target_pairs={{0,1},{1,0},{2,3},{3,2},{4,5},{5,4},{6,7},{7,6},{8,9},{9,8},{10,11... | collective-permute-start | bytes 774152 | tf_op jit(solution)/shard_map/ppermute | solution.py:584
  42.4 3.2 %collective-permute-start.10 = (f32[7,4,2,1152]{3,2,1,0:T(2,128)S(1)}, f32[7,4,2,1152]{3,2,1,0:T(2,128)S(1)}, u32[]{:S(2)}, u32[]{:S(2)}) collective-permute-start(f32[7,4,2,1152]{3,2,1,0:T(2,128)S(1)} %collective-permute-done.9.refs_2_), channel_id=1, source_target_pairs={{0,1},{1,0},{2,3},{3,2},{4,5},{5,4},{6,7},{7,6},{8,9},{9,8},{10,11... | collective-permute-start | bytes 774152 | tf_op jit(solution)/shard_map/ppermute | solution.py:584
  42.4 1.9 %collective-permute-start.13 = (f32[3,4,2,1152]{3,2,1,0:T(2,128)S(1)}, f32[3,4,2,1152]{3,2,1,0:T(2,128)S(1)}, u32[]{:S(2)}, u32[]{:S(2)}) collective-permute-start(f32[3,4,2,1152]{3,2,1,0:T(2,128)S(1)} %get-tuple-element.30.refs_8_), channel_id=1, source_target_pairs={{0,1},{1,0},{2,3},{3,2},{4,5},{5,4},{6,7},{7,6},{8,9},{9,8},{10,11... | collective-permute-start | bytes 331784 | tf_op jit(solution)/shard_map/ppermute | solution.py:584
  42.9 1.3 %collective-permute-start.11 = (f32[2,4,2,1152]{3,2,1,0:T(2,128)S(1)}, f32[2,4,2,1152]{3,2,1,0:T(2,128)S(1)}, u32[]{:S(2)}, u32[]{:S(2)}) collective-permute-start(f32[2,4,2,1152]{3,2,1,0:T(2,128)S(1)} %get-tuple-element.29.refs_4_), channel_id=1, source_target_pairs={{0,1},{1,0},{2,3},{3,2},{4,5},{5,4},{6,7},{7,6},{8,9},{9,8},{10,11... | collective-permute-start | bytes 221192 | tf_op jit(solution)/shard_map/ppermute | solution.py:584
  44.2 1.4 %collective-permute-start.14 = (f32[3,4,2,1152]{3,2,1,0:T(2,128)S(1)}, f32[3,4,2,1152]{3,2,1,0:T(2,128)S(1)}, u32[]{:S(2)}, u32[]{:S(2)}) collective-permute-start(f32[3,4,2,1152]{3,2,1,0:T(2,128)S(1)} %collective-permute-done.5.refs_4_.refs_10_), channel_id=1, source_target_pairs={{0,1},{1,0},{2,3},{3,2},{4,5},{5,4},{6,7},{7,6},{8,9},{9,8},{10,11... | collective-permute-start | bytes 331784 | tf_op jit(solution)/shard_map/ppermute | solution.py:584
  44.3 1.3 %collective-permute-start.12 = (f32[2,4,2,1152]{3,2,1,0:T(2,128)S(1)}, f32[2,4,2,1152]{3,2,1,0:T(2,128)S(1)}, u32[]{:S(2)}, u32[]{:S(2)}) collective-permute-start(f32[2,4,2,1152]{3,2,1,0:T(2,128)S(1)} %collective-permute-done.4.refs_3_.refs_6_), channel_id=1, source_target_pairs={{0,1},{1,0},{2,3},{3,2},{4,5},{5,4},{6,7},{7,6},{8,9},{9,8},{10,11... | collective-permute-start | bytes 221192 | tf_op jit(solution)/shard_map/ppermute | solution.py:584
  (7 other events, 39.6 us)

commit v8 on v7

--- a/solution.py
+++ b/solution.py
@@ -78,7 +78,7 @@
 
 
 def inner_kernel(band_ref, table_hbm, thick_hbm, u_hbm, v_hbm, tracer_hbm, *refs):
-    out_ref, sum_ref, last_ref, leading_ref, near_ref, near_rest_ref, geo_ref, wind_ref, tracer_ref, sems = refs
+    out_ref, sum_ref, near_ref, near_rest_ref, geo_ref, wind_ref, tracer_ref, sems = refs
     T, L, rows, width = tracer_ref.shape
 
     def copies(k):
@@ -116,17 +116,9 @@
 
         store(0, new)
         sum_ref[...] += new
-        last_ref[0, k] = thick[rows - 1 : rows]
-        last_ref[1, k] = v[rows - 1 : rows]
-        leading_ref[0, k] = thick[0:1]
-        leading_ref[1, k] = thick[1:2]
-        leading_ref[2, k] = u[0:1]
-        leading_ref[3, k] = v[0:1]
         scale = 1.0 / new
         for c in range(T):
             q = tracer_ref[c, k]
-            last_ref[2 + c, k] = q[rows - 1 : rows]
-            leading_ref[4 + c, k] = q[0:1]
             change = tracer_change(q, nothing, nothing, thick, u, v, nothing, east, north, below, inverse)
             store(1 + c, change * scale)
         return carry
@@ -142,8 +134,6 @@
     out_shape = [
         shape(1 + T, R),
         jax.ShapeDtypeStruct((R, N), jnp.float32),
-        shape(2 + T, 1),
-        shape(4 + T, 1),
         shape(2, 2),
         shape(T - 1, 2),
     ]
@@ -560,21 +550,53 @@
     )(own, edge, *arrived, *wait)
 
 
-def hand_on_kernel(count, *refs):
-    for source_ref, copy_ref in zip(refs[:count], refs[len(refs) - count :]):
-        copy_ref[...] = source_ref[...]
-
-
-def hand_on(arrays, wait):
+def edge_kernel(thick_hbm, u_hbm, v_hbm, tracer_hbm, *refs):
+    last_ref, leading_ref, top_ref, low_ref, tracer_ref, sems = refs[-6:]
+    T, L, R, _ = tracer_hbm.shape
+    top = pl.ds(R - 8, 8)
+    copies = [
+        pltpu.make_async_copy(thick_hbm.at[:, top], top_ref.at[0], sems.at[0]),
+        pltpu.make_async_copy(v_hbm.at[:, top], top_ref.at[1], sems.at[1]),
+        pltpu.make_async_copy(thick_hbm.at[:, pl.ds(0, 8)], low_ref.at[0], sems.at[2]),
+        pltpu.make_async_copy(u_hbm.at[:, pl.ds(0, 8)], low_ref.at[1], sems.at[3]),
+        pltpu.make_async_copy(v_hbm.at[:, pl.ds(0, 8)], low_ref.at[2], sems.at[4]),
+        pltpu.make_async_copy(tracer_hbm.at[:, :, top], tracer_ref.at[0], sems.at[5]),
+        pltpu.make_async_copy(tracer_hbm.at[:, :, pl.ds(0, 8)], tracer_ref.at[1], sems.at[6]),
+    ]
+    for copy in copies:
+        copy.start()
+    for copy in copies:
+        copy.wait()
+    last_ref[0:2] = top_ref[:, :, 7:8]
+    last_ref[2 : 2 + T] = tracer_ref[0, :, :, 7:8]
+    leading_ref[0] = low_ref[0, :, 0:1]
+    leading_ref[1] = low_ref[0, :, 1:2]
+    leading_ref[2:4] = low_ref[1:3, :, 0:1]
+    leading_ref[4 : 4 + T] = tracer_ref[1, :, :, 0:1]
+
+
+def edge_rows(thickness, wind_u, wind_v, tracers, wait):
+    L, R, N = thickness.shape
+    T = tracers.shape[0]
+    operands = [pltpu.with_memory_space_constraint(a, pltpu.HBM) for a in (thickness, wind_u, wind_v, tracers)]
     return pl.pallas_call(
-        functools.partial(hand_on_kernel, len(arrays)),
-        in_specs=[VMEM] * len(arrays) + after(wait),
-        out_specs=[VMEM] * len(arrays),
-        out_shape=[jax.ShapeDtypeStruct(a.shape, a.dtype) for a in arrays],
+        edge_kernel,
+        in_specs=after(operands) + after(wait),
+        out_specs=[VMEM] * 2,
+        out_shape=[
+            jax.ShapeDtypeStruct((2 + T, L, 1, N), jnp.float32),
+            jax.ShapeDtypeStruct((4 + T, L, 1, N), jnp.float32),
+        ],
+        scratch_shapes=[
+            pltpu.VMEM((2, L, 8, N), jnp.float32),
+            pltpu.VMEM((3, L, 8, N), jnp.float32),
+            pltpu.VMEM((2, T, L, 8, N), jnp.float32),
+            pltpu.SemaphoreType.DMA((7,)),
+        ],
         compiler_params=params(),
         cost_estimate=cost(1e10, 1e9),
-        name="hand_on",
-    )(*arrays, *wait)
+        name="edge_rows",
+    )(*operands, *wait)
 
 
 def shifted(value, lev_count, sub_count, s, t):
@@ -613,7 +635,7 @@
 
     remap = functools.partial(remap_parts, (C, S), place, level_weights)
 
-    inner, own_sum, last, leading, near, near_rest = inner_step(band, table, thickness, wind_u, wind_v, tracers)
+    inner, own_sum, near, near_rest = inner_step(band, table, thickness, wind_u, wind_v, tracers)
     others = [send(own_sum, s=s, t=t) for s in away for t in range(S)]
     group = with_others_of_chip(inner)
     near = [near] + [send(near, s=s, t=0) for s in away]
@@ -622,7 +644,9 @@
     away_parts = remap(group, [group], others, tracer_fields, away, 2)
     arrived = sent(away_parts)
 
-    last, leading = hand_on((last, leading), [away_parts[0], *near[1:2], *near_rest[1:2]])
+    last, leading = edge_rows(
+        thickness, wind_u, wind_v, tracers, [away_parts[0], *near[1:2], *near_rest[1:2]]
+    )
     up = lax.ppermute(last, "lat", northward)
     down = lax.ppermute(leading, "lat", southward)
     u, v, edge = second_step(band, table, lat_rows, thickness, wind_u, wind_v, tracers, up, down, cutoff)

time: 54.2 us -> 53.2 us (0.982)
  Pallas kernels: 19.1 us -> 20.8 us
  local copies, waits for them, and re-layouts: 1.43 us -> 0.13 us
  waiting for transfers between devices: 14.6 us -> 13.6 us
    pallas_call x1, Pallas kernels: 0.03 us -> 1.72 us  [edge_rows(): pl.pallas_call(edge_kernel, in_specs=after(operands) + after(wait), out_s...]
    unnamed x26 -> x18, local copies, waits for them, and re-layouts: 1.36 us -> 0.06 us
    ppermute x6, waiting for transfers between devices: 8.79 us -> 7.7 us  [shifted(): lax.ppermute(value, 'lev', [(i, (i + s) % lev_count) for i in range(lev_c...]
  transfers between devices with their start and end apart: 18 -> 18, of which waited for: 9 -> 9; matrix products, arithmetic and copies ran while one was open for 0% -> 0% of each run, Pallas kernels for 28% -> 31%
where the time goes in v8:
time: 53.2 us; the launch traced here: 52.9 us
  Pallas kernels  20.8 us (39%)
  starting transfers between devices  17.5 us (33%)
  waiting for transfers between devices  13.6 us (26%)
  between operations  0.83 us (2%)
    ppermute x6, starting transfers between devices, shifted(): lax.ppermute(value, 'lev', [(i, (i + s) % lev_count) for i in range(lev_c...  9.47 us
    ppermute x6, waiting for transfers between devices, shifted(): lax.ppermute(value, 'lev', [(i, (i + s) % lev_count) for i in range(lev_c...  7.7 us
    ppermute x1, starting transfers between devices, per_device(): up = lax.ppermute(last, 'lat', northward)  4.55 us
    pallas_call x2, Pallas kernels, remap_parts(): pl.pallas_call(functools.partial(remap_kernel, counts, tuple(steps), tupl...  4.35 us
    pallas_call x1, Pallas kernels, remap_edges(): pl.pallas_call(functools.partial(remap_edge_kernel, counts, near_fields),...  3.66 us
    pallas_call x1, Pallas kernels, second_step(): pl.pallas_call(functools.partial(second_kernel, lat_rows), grid=(L,), in_...  3.66 us
    pallas_call x1, Pallas kernels, inner_step(): pl.pallas_call(inner_kernel, in_specs=[SMEM] + after([table, thickness, w...  3.26 us
    pallas_call x1, Pallas kernels, finish_tracers(): pl.pallas_call(functools.partial(finish_kernel, counts, margin), in_specs...  3.26 us
  transfers between devices with their start and end apart: 18, of which 9 were waited for; matrix products, arithmetic and copies ran while one was open for 0% of the time, Pallas kernels for 31%

profile of v8, /device:TPU:0, one launch (start us, length us, event | category | flops | bytes accessed | tf_op | source)
XLA Modules:
  0.0 52.9 jit_solution(6722557053235496460)
XLA Ops:
  0.6 3.3 %inner_step.1 = (f32[5,4,16,1152]{3,2,1,0:T(8,128)S(1)}, f32[16,1152]{1,0:T(8,128)S(1)}, f32[2,4,2,1152]{3,2,1,0:T(2,128)S(1)}, f32[3,4,2,1152]{3,2,1,0:T(2,128)S(1)}) custom-call(s32[1]{0:T(128)} %bitcast.2.band_ref, f32[4,24,128]{2,1,0:T(8,128)} %constant.17.clone.table_hbm.table_ref, f32[4,16,1152]{2,1,0:T(8,128)} %thick_ref.1, f32[4,16,1152]{2,1,0:T(8,128)} %u_ref.1, ...), custom_call_target="tpu_custom_call" | custom-call | flops 9584640 | bytes 4718592 | tf_op jit(solution)/shard_map/inner_step/pallas_call | solution.py:140
  3.9 0.5 collective-permute-start
  4.4 2.6 %collective-permute-start.1 = (f32[16,1152]{1,0:T(8,128)S(1)}, f32[16,1152]{1,0:T(8,128)S(1)}, u32[]{:S(2)}, u32[]{:S(2)}) collective-permute-start(f32[16,1152]{1,0:T(8,128)S(1)} %get-tuple-element.24), channel_id=1, source_target_pairs={{0,2},{2,0},{1,3},{3,1},{4,6},{6,4},{5,7},{7,5},{8,10},{10,8},{9,1... | collective-permute-start | bytes 221192 | tf_op jit(solution)/shard_map/ppermute | solution.py:604
  7.1 1.7 %collective-permute-start.5 = (f32[3,4,2,1152]{3,2,1,0:T(2,128)S(1)}, f32[3,4,2,1152]{3,2,1,0:T(2,128)S(1)}, u32[]{:S(2)}, u32[]{:S(2)}) collective-permute-start(f32[3,4,2,1152]{3,2,1,0:T(2,128)S(1)} %get-tuple-element.26.refs_8_), channel_id=1, source_target_pairs={{0,2},{2,0},{1,3},{3,1},{4,6},{6,4},{5,7},{7,5},{8,10},{10,8},{9,1... | collective-permute-start | bytes 331784 | tf_op jit(solution)/shard_map/ppermute | solution.py:604
  9.2 0.7 %collective-permute-done.1.refs_4_.refs_6_.refs_2_ = f32[16,1152]{1,0:T(8,128)S(1)} collective-permute-done((f32[16,1152]{1,0:T(8,128)S(1)}, f32[16,1152]{1,0:T(8,128)S(1)}, u32[]{:S(2)}, u32[]{:S(2)}) %collective-permute-start.1) | collective-permute-done | bytes 73760 | tf_op jit(solution)/shard_map/ppermute | solution.py:604
  9.9 1.4 %collective-permute-done.2.refs_5_.refs_7_.refs_3_ = f32[16,1152]{1,0:T(8,128)S(1)} collective-permute-done((f32[16,1152]{1,0:T(8,128)S(1)}, f32[16,1152]{1,0:T(8,128)S(1)}, u32[]{:S(2)}, u32[]{:S(2)}) %collective-permute-start.2) | collective-permute-done | bytes 73760 | tf_op jit(solution)/shard_map/ppermute | solution.py:612
  11.2 2.0 %remap_parts.2.refs_0_ = f32[192,1152]{1,0:T(8,128)S(1)} custom-call(s32[2]{0:T(128)S(1)} %pad_add_fusion.place_ref, f32[16]{0:T(128)S(1)} %copy-done.7, f32[5,4,16,1152]{3,2,1,0:T(8,128)S(1)} %get-tuple-element.23.refs_0_.refs_2_, f32[5,4,16,1152]{3,2,1,0:T(8,128)S(1)} %collective-permute-done.refs_1_.refs_3_, ...), custom_call_target="tpu_custom_call" | custom-call | flops 7667712 | bytes 4423680 | tf_op jit(solution)/shard_map/remap_parts/pallas_call | solution.py:423
  13.3 1.6 %collective-permute-start.3 = (f32[192,1152]{1,0:T(8,128)S(1)}, f32[192,1152]{1,0:T(8,128)S(1)}, u32[]{:S(2)}, u32[]{:S(2)}) collective-permute-start(f32[192,1152]{1,0:T(8,128)S(1)} %remap_parts.2.refs_0_), channel_id=1, source_target_pairs={{0,2},{2,0},{1,3},{3,1},{4,6},{6,4},{5,7},{7,5},{8,10},{10,8},{9,1... | collective-permute-start | bytes 2654216 | tf_op jit(solution)/shard_map/ppermute | solution.py:604
  14.9 0.6 %collective-permute-done.4.refs_1_.refs_6_ = f32[2,4,2,1152]{3,2,1,0:T(2,128)S(1)} collective-permute-done((f32[2,4,2,1152]{3,2,1,0:T(2,128)S(1)}, f32[2,4,2,1152]{3,2,1,0:T(2,128)S(1)}, u32[]{:S(2)}, u32[]{:S(2)}) %collective-permute-start.4) | collective-permute-done | bytes 73760 | tf_op jit(solution)/shard_map/ppermute | solution.py:604
  15.5 1.7 %edge_rows.1 = (f32[6,4,1,1152]{3,2,1,0:T(1,128)S(1)}, f32[8,4,1,1152]{3,2,1,0:T(1,128)S(1)}) custom-call(f32[4,16,1152]{2,1,0:T(8,128)} %thick_ref.1, f32[4,16,1152]{2,1,0:T(8,128)} %u_ref.1, f32[4,16,1152]{2,1,0:T(8,128)} %v_ref.1, f32[4,4,16,1152]{3,2,1,0:T(8,128)} %tracer_ref.1, f32[192,1152]{1,0:T(8,128)S(1)} %remap_parts.2.refs_0_, ...), custom_call_target="tpu_custom_call" | custom-call | flops 10000000000 | bytes 1000000000 | tf_op jit(solution)/shard_map/edge_rows/pallas_call | solution.py:582
  17.2 1.3 %collective-permute-start.7 = (f32[8,4,1,1152]{3,2,1,0:T(1,128)S(1)}, f32[8,4,1,1152]{3,2,1,0:T(1,128)S(1)}, u32[]{:S(2)}, u32[]{:S(2)}) collective-permute-start(f32[8,4,1,1152]{3,2,1,0:T(1,128)S(1)} %get-tuple-element.28), channel_id=1, source_target_pairs={{4,0},{8,4},{12,8},{5,1},{9,5},{13,9},{6,2},{10,6},{14,10},{7,3},{... | collective-permute-start | bytes 442376 | tf_op jit(solution)/shard_map/ppermute | solution.py:651
  18.5 4.6 %collective-permute-start.6 = (f32[6,4,1,1152]{3,2,1,0:T(1,128)S(1)}, f32[6,4,1,1152]{3,2,1,0:T(1,128)S(1)}, u32[]{:S(2)}, u32[]{:S(2)}) collective-permute-start(f32[6,4,1,1152]{3,2,1,0:T(1,128)S(1)} %get-tuple-element.27), channel_id=1, source_target_pairs={{0,4},{4,8},{8,12},{1,5},{5,9},{9,13},{2,6},{6,10},{10,14},{3,7},{... | collective-permute-start | bytes 331784 | tf_op jit(solution)/shard_map/ppermute | solution.py:650
  23.1 2.3 %collective-permute-done.6.up_ref = f32[6,4,1,1152]{3,2,1,0:T(1,128)S(1)} collective-permute-done((f32[6,4,1,1152]{3,2,1,0:T(1,128)S(1)}, f32[6,4,1,1152]{3,2,1,0:T(1,128)S(1)}, u32[]{:S(2)}, u32[]{:S(2)}) %collective-permute-start.6) | collective-permute-done | bytes 110624 | tf_op jit(solution)/shard_map/ppermute | solution.py:650
  25.5 3.7 %second_step.1 = (f32[1,4,16,1152]{3,2,1,0:T(8,128)S(1)}, f32[1,4,16,1152]{3,2,1,0:T(8,128)S(1)}, f32[7,4,2,1152]{3,2,1,0:T(2,128)S(1)}) custom-call(s32[1]{0:T(128)} %bitcast.2.band_ref, f32[4,24,128]{2,1,0:T(8,128)S(1)} %copy-done.6, f32[4,16,1152]{2,1,0:T(8,128)S(1)} %copy-done.1, f32[4,16,1152]{2,1,0:T(8,128)S(1)} %copy-done.2, ...), custom_call_target="tpu_custom_call" | custom-call | flops 503316480 | bytes 3538944 | tf_op jit(solution)/shard_map/second_step/pallas_call | solution.py:283
  29.8 1.6 %collective-permute-start.9 = (f32[7,4,2,1152]{3,2,1,0:T(2,128)S(1)}, f32[7,4,2,1152]{3,2,1,0:T(2,128)S(1)}, u32[]{:S(2)}, u32[]{:S(2)}) collective-permute-start(f32[7,4,2,1152]{3,2,1,0:T(2,128)S(1)} %get-tuple-element.29.refs_0_), channel_id=1, source_target_pairs={{0,2},{2,0},{1,3},{3,1},{4,6},{6,4},{5,7},{7,5},{8,10},{10,8},{9,1... | collective-permute-start | bytes 774152 | tf_op jit(solution)/shard_map/ppermute | solution.py:604
  31.4 4.4 %collective-permute-done.3.refs_8_.refs_4_ = f32[192,1152]{1,0:T(8,128)S(1)} collective-permute-done((f32[192,1152]{1,0:T(8,128)S(1)}, f32[192,1152]{1,0:T(8,128)S(1)}, u32[]{:S(2)}, u32[]{:S(2)}) %collective-permute-start.3) | collective-permute-done | bytes 884768 | tf_op jit(solution)/shard_map/ppermute | solution.py:604
  35.8 2.4 %remap_parts.3 = (f32[2,4,16,1152]{3,2,1,0:T(8,128)S(1)}, f32[112,1152]{1,0:T(8,128)S(1)}) custom-call(s32[2]{0:T(128)S(1)} %pad_add_fusion.place_ref, f32[16]{0:T(128)S(1)} %copy-done.7, f32[5,4,16,1152]{3,2,1,0:T(8,128)S(1)} %get-tuple-element.23.refs_0_.refs_2_, f32[5,4,16,1152]{3,2,1,0:T(8,128)S(1)} %collective-permute-done.refs_1_.refs_3_, ...), custom_call_target="tpu_custom_call" | custom-call | flops 10616832 | bytes 3538944 | tf_op jit(solution)/shard_map/remap_parts/pallas_call | solution.py:423
  38.2 1.7 %collective-permute-start.17 = (f32[112,1152]{1,0:T(8,128)S(1)}, f32[112,1152]{1,0:T(8,128)S(1)}, u32[]{:S(2)}, u32[]{:S(2)}) collective-permute-start(f32[112,1152]{1,0:T(8,128)S(1)} %get-tuple-element.32.refs_12_), channel_id=1, source_target_pairs={{0,2},{2,0},{1,3},{3,1},{4,6},{6,4},{5,7},{7,5},{8,10},{10,8},{9,1... | collective-permute-start | bytes 1548296 | tf_op jit(solution)/shard_map/ppermute | solution.py:604
  39.9 1.5 %collective-permute-done.9.refs_2_ = f32[7,4,2,1152]{3,2,1,0:T(2,128)S(1)} collective-permute-done((f32[7,4,2,1152]{3,2,1,0:T(2,128)S(1)}, f32[7,4,2,1152]{3,2,1,0:T(2,128)S(1)}, u32[]{:S(2)}, u32[]{:S(2)}) %collective-permute-start.9) | collective-permute-done | bytes 258080 | tf_op jit(solution)/shard_map/ppermute | solution.py:604
  41.8 1.3 %collective-permute-done.11.refs_5_ = f32[2,4,2,1152]{3,2,1,0:T(2,128)S(1)} collective-permute-done((f32[2,4,2,1152]{3,2,1,0:T(2,128)S(1)}, f32[2,4,2,1152]{3,2,1,0:T(2,128)S(1)}, u32[]{:S(2)}, u32[]{:S(2)}) %collective-permute-start.11) | collective-permute-done | bytes 73760 | tf_op jit(solution)/shard_map/ppermute | solution.py:606
  43.6 0.9 %collective-permute-done.12.refs_7_ = f32[2,4,2,1152]{3,2,1,0:T(2,128)S(1)} collective-permute-done((f32[2,4,2,1152]{3,2,1,0:T(2,128)S(1)}, f32[2,4,2,1152]{3,2,1,0:T(2,128)S(1)}, u32[]{:S(2)}, u32[]{:S(2)}) %collective-permute-start.12) | collective-permute-done | bytes 73760 | tf_op jit(solution)/shard_map/ppermute | solution.py:606
  44.6 3.7 %remap_edges.1 = (f32[6,4,2,1152]{3,2,1,0:T(2,128)S(1)}, f32[4,2,1152]{2,1,0:T(2,128)S(1)}, f32[4,4,2,1152]{3,2,1,0:T(2,128)S(1)}) custom-call(s32[2]{0:T(128)S(1)} %pad_add_fusion.place_ref, f32[16]{0:T(128)S(1)} %copy-done.7, f32[7,4,2,1152]{3,2,1,0:T(2,128)S(1)} %get-tuple-element.29.refs_0_, f32[7,4,2,1152]{3,2,1,0:T(2,128)S(1)} %collective-permute-done.8.refs_1_, ...), custom_call_target="tpu_custom_call" | custom-call | flops 5898240 | bytes 3096576 | tf_op jit(solution)/shard_map/remap_edges/pallas_call | solution.py:461
  48.2 3.3 %finish_tracers.1 = (f32[4,4,16,1152]{3,2,1,0:T(8,128)}, f32[4,16,1152]{2,1,0:T(8,128)}, f32[8,128]{1,0:T(8,128)S(1)}) custom-call(s32[2]{0:T(128)S(1)} %pad_add_fusion.place_ref, f32[16]{0:T(128)S(1)} %copy-done.7, f32[5,4,16,1152]{3,2,1,0:T(8,128)S(1)} %get-tuple-element.23.refs_0_.refs_2_, f32[5,4,16,1152]{3,2,1,0:T(8,128)S(1)} %collective-permute-done.refs_1_.refs_3_, ...), custom_call_target="tpu_custom_call" | custom-call | flops 7667712 | bytes 5898240 | tf_op jit(solution)/shard_map/finish_tracers/pallas_call | solution.py:512
  52.0 0.9 %finish_winds.1 = (f32[4,16,1152]{2,1,0:T(8,128)}, f32[4,16,1152]{2,1,0:T(8,128)}) custom-call(f32[2,4,16,1152]{3,2,1,0:T(8,128)S(1)} %get-tuple-element.37.own_ref, f32[6,4,2,1152]{3,2,1,0:T(2,128)S(1)} %get-tuple-element.34.refs_6_.edge_ref, f32[112,1152]{1,0:T(8,128)S(1)} %collective-permute-done.17.refs_0_, f32[8,128]{1,0:T(8,128)S(1)} %get-tuple-element.38.refs_1_), custom_call_target="tpu_custom_call" | custom-call | flops 147456 | bytes 1769472 | tf_op jit(solution)/shard_map/finish_winds/pallas_call | solution.py:542
  (40 shorter events, 2.7 us)
Async XLA Ops:
  3.9 7.3 %collective-permute-start = (f32[5,4,16,1152]{3,2,1,0:T(8,128)S(1)}, f32[5,4,16,1152]{3,2,1,0:T(8,128)S(1)}, u32[]{:S(2)}, u32[]{:S(2)}) collective-permute-start(f32[5,4,16,1152]{3,2,1,0:T(8,128)S(1)} %get-tuple-element.23.refs_0_.refs_2_), channel_id=1, source_target_pairs={{0,1},{1,0},{2,3},{3,2},{4,5},{5,4},{6,7},{7,6},{8,9},{9,8},{10,11... | collective-permute-start | bytes 4423688 | tf_op jit(solution)/shard_map/ppermute | solution.py:606
  4.4 5.4 %collective-permute-start.1 = (f32[16,1152]{1,0:T(8,128)S(1)}, f32[16,1152]{1,0:T(8,128)S(1)}, u32[]{:S(2)}, u32[]{:S(2)}) collective-permute-start(f32[16,1152]{1,0:T(8,128)S(1)} %get-tuple-element.24), channel_id=1, source_target_pairs={{0,2},{2,0},{1,3},{3,1},{4,6},{6,4},{5,7},{7,5},{8,10},{10,8},{9,1... | collective-permute-start | bytes 221192 | tf_op jit(solution)/shard_map/ppermute | solution.py:604
  7.0 4.2 %collective-permute-start.2 = (f32[16,1152]{1,0:T(8,128)S(1)}, f32[16,1152]{1,0:T(8,128)S(1)}, u32[]{:S(2)}, u32[]{:S(2)}) collective-permute-start(f32[16,1152]{1,0:T(8,128)S(1)} %get-tuple-element.24), channel_id=1, source_target_pairs={{0,3},{1,2},{2,1},{3,0},{4,7},{5,6},{6,5},{7,4},{8,11},{9,10},{10,... | collective-permute-start | bytes 221192 | tf_op jit(solution)/shard_map/ppermute | solution.py:612
  7.1 8.5 %collective-permute-start.5 = (f32[3,4,2,1152]{3,2,1,0:T(2,128)S(1)}, f32[3,4,2,1152]{3,2,1,0:T(2,128)S(1)}, u32[]{:S(2)}, u32[]{:S(2)}) collective-permute-start(f32[3,4,2,1152]{3,2,1,0:T(2,128)S(1)} %get-tuple-element.26.refs_8_), channel_id=1, source_target_pairs={{0,2},{2,0},{1,3},{3,1},{4,6},{6,4},{5,7},{7,5},{8,10},{10,8},{9,1... | collective-permute-start | bytes 331784 | tf_op jit(solution)/shard_map/ppermute | solution.py:604
  8.8 6.7 %collective-permute-start.4 = (f32[2,4,2,1152]{3,2,1,0:T(2,128)S(1)}, f32[2,4,2,1152]{3,2,1,0:T(2,128)S(1)}, u32[]{:S(2)}, u32[]{:S(2)}) collective-permute-start(f32[2,4,2,1152]{3,2,1,0:T(2,128)S(1)} %get-tuple-element.25.refs_4_), channel_id=1, source_target_pairs={{0,2},{2,0},{1,3},{3,1},{4,6},{6,4},{5,7},{7,5},{8,10},{10,8},{9,1... | collective-permute-start | bytes 221192 | tf_op jit(solution)/shard_map/ppermute | solution.py:604
  13.2 12.3 %copy-start = (f32[4,4,16,1152]{3,2,1,0:T(8,128)S(1)}, f32[4,4,16,1152]{3,2,1,0:T(8,128)}, u32[]{:S(2)}) copy-start(f32[4,4,16,1152]{3,2,1,0:T(8,128)} %tracer_ref.1) | copy-start | bytes 3538948
  13.2 12.3 %copy-start.1 = (f32[4,16,1152]{2,1,0:T(8,128)S(1)}, f32[4,16,1152]{2,1,0:T(8,128)}, u32[]{:S(2)}) copy-start(f32[4,16,1152]{2,1,0:T(8,128)} %thick_ref.1) | copy-start | bytes 884740
  13.2 12.3 %copy-start.2 = (f32[4,16,1152]{2,1,0:T(8,128)S(1)}, f32[4,16,1152]{2,1,0:T(8,128)}, u32[]{:S(2)}) copy-start(f32[4,16,1152]{2,1,0:T(8,128)} %u_ref.1) | copy-start | bytes 884740
  13.2 12.3 %copy-start.3 = (f32[4,16,1152]{2,1,0:T(8,128)S(1)}, f32[4,16,1152]{2,1,0:T(8,128)}, u32[]{:S(2)}) copy-start(f32[4,16,1152]{2,1,0:T(8,128)} %v_ref.1) | copy-start | bytes 884740
  13.3 12.3 %copy-start.4 = (bf16[5,256,256]{2,1,0:T(8,128)(2,1)S(1)}, bf16[5,256,256]{2,1,0:T(8,128)(2,1)}, u32[]{:S(2)}) copy-start(bf16[5,256,256]{2,1,0:T(8,128)(2,1)} %constant.18.clone.high_ref) | copy-start | bytes 1966084
  13.3 12.3 %copy-start.5 = (bf16[5,256,256]{2,1,0:T(8,128)(2,1)S(1)}, bf16[5,256,256]{2,1,0:T(8,128)(2,1)}, u32[]{:S(2)}) copy-start(bf16[5,256,256]{2,1,0:T(8,128)(2,1)} %constant.19.clone.low_ref) | copy-start | bytes 1966084
  13.3 22.5 %collective-permute-start.3 = (f32[192,1152]{1,0:T(8,128)S(1)}, f32[192,1152]{1,0:T(8,128)S(1)}, u32[]{:S(2)}, u32[]{:S(2)}) collective-permute-start(f32[192,1152]{1,0:T(8,128)S(1)} %remap_parts.2.refs_0_), channel_id=1, source_target_pairs={{0,2},{2,0},{1,3},{3,1},{4,6},{6,4},{5,7},{7,5},{8,10},{10,8},{9,1... | collective-permute-start | bytes 2654216 | tf_op jit(solution)/shard_map/ppermute | solution.py:604
  17.2 8.2 %collective-permute-start.7 = (f32[8,4,1,1152]{3,2,1,0:T(1,128)S(1)}, f32[8,4,1,1152]{3,2,1,0:T(1,128)S(1)}, u32[]{:S(2)}, u32[]{:S(2)}) collective-permute-start(f32[8,4,1,1152]{3,2,1,0:T(1,128)S(1)} %get-tuple-element.28), channel_id=1, source_target_pairs={{4,0},{8,4},{12,8},{5,1},{9,5},{13,9},{6,2},{10,6},{14,10},{7,3},{... | collective-permute-start | bytes 442376 | tf_op jit(solution)/shard_map/ppermute | solution.py:651
  18.5 6.9 %collective-permute-start.6 = (f32[6,4,1,1152]{3,2,1,0:T(1,128)S(1)}, f32[6,4,1,1152]{3,2,1,0:T(1,128)S(1)}, u32[]{:S(2)}, u32[]{:S(2)}) collective-permute-start(f32[6,4,1,1152]{3,2,1,0:T(1,128)S(1)} %get-tuple-element.27), channel_id=1, source_target_pairs={{0,4},{4,8},{8,12},{1,5},{5,9},{9,13},{2,6},{6,10},{10,14},{3,7},{... | collective-permute-start | bytes 331784 | tf_op jit(solution)/shard_map/ppermute | solution.py:650
  29.2 2.2 %collective-permute-start.15 = (f32[1,4,16,1152]{3,2,1,0:T(8,128)S(1)}, f32[1,4,16,1152]{3,2,1,0:T(8,128)S(1)}, u32[]{:S(2)}, u32[]{:S(2)}) collective-permute-start(f32[1,4,16,1152]{3,2,1,0:T(8,128)S(1)} %get-tuple-element.30.refs_2_), channel_id=1, source_target_pairs={{0,1},{1,0},{2,3},{3,2},{4,5},{5,4},{6,7},{7,6},{8,9},{9,8},{10,11... | collective-permute-start | bytes 884744 | tf_op jit(solution)/shard_map/ppermute | solution.py:606
  29.3 2.1 %collective-permute-start.16 = (f32[1,4,16,1152]{3,2,1,0:T(8,128)S(1)}, f32[1,4,16,1152]{3,2,1,0:T(8,128)S(1)}, u32[]{:S(2)}, u32[]{:S(2)}) collective-permute-start(f32[1,4,16,1152]{3,2,1,0:T(8,128)S(1)} %get-tuple-element.31.refs_4_), channel_id=1, source_target_pairs={{0,1},{1,0},{2,3},{3,2},{4,5},{5,4},{6,7},{7,6},{8,9},{9,8},{10,11... | collective-permute-start | bytes 884744 | tf_op jit(solution)/shard_map/ppermute | solution.py:606
  29.8 11.6 %collective-permute-start.9 = (f32[7,4,2,1152]{3,2,1,0:T(2,128)S(1)}, f32[7,4,2,1152]{3,2,1,0:T(2,128)S(1)}, u32[]{:S(2)}, u32[]{:S(2)}) collective-permute-start(f32[7,4,2,1152]{3,2,1,0:T(2,128)S(1)} %get-tuple-element.29.refs_0_), channel_id=1, source_target_pairs={{0,2},{2,0},{1,3},{3,1},{4,6},{6,4},{5,7},{7,5},{8,10},{10,8},{9,1... | collective-permute-start | bytes 774152 | tf_op jit(solution)/shard_map/ppermute | solution.py:604
  38.2 13.8 %collective-permute-start.17 = (f32[112,1152]{1,0:T(8,128)S(1)}, f32[112,1152]{1,0:T(8,128)S(1)}, u32[]{:S(2)}, u32[]{:S(2)}) collective-permute-start(f32[112,1152]{1,0:T(8,128)S(1)} %get-tuple-element.32.refs_12_), channel_id=1, source_target_pairs={{0,2},{2,0},{1,3},{3,1},{4,6},{6,4},{5,7},{7,5},{8,10},{10,8},{9,1... | collective-permute-start | bytes 1548296 | tf_op jit(solution)/shard_map/ppermute | solution.py:604
  39.9 4.7 %collective-permute-start.8 = (f32[7,4,2,1152]{3,2,1,0:T(2,128)S(1)}, f32[7,4,2,1152]{3,2,1,0:T(2,128)S(1)}, u32[]{:S(2)}, u32[]{:S(2)}) collective-permute-start(f32[7,4,2,1152]{3,2,1,0:T(2,128)S(1)} %get-tuple-element.29.refs_0_), channel_id=1, source_target_pairs={{0,1},{1,0},{2,3},{3,2},{4,5},{5,4},{6,7},{7,6},{8,9},{9,8},{10,11... | collective-permute-start | bytes 774152 | tf_op jit(solution)/shard_map/ppermute | solution.py:606
  41.3 3.2 %collective-permute-start.10 = (f32[7,4,2,1152]{3,2,1,0:T(2,128)S(1)}, f32[7,4,2,1152]{3,2,1,0:T(2,128)S(1)}, u32[]{:S(2)}, u32[]{:S(2)}) collective-permute-start(f32[7,4,2,1152]{3,2,1,0:T(2,128)S(1)} %collective-permute-done.9.refs_2_), channel_id=1, source_target_pairs={{0,1},{1,0},{2,3},{3,2},{4,5},{5,4},{6,7},{7,6},{8,9},{9,8},{10,11... | collective-permute-start | bytes 774152 | tf_op jit(solution)/shard_map/ppermute | solution.py:606
  41.3 1.9 %collective-permute-start.13 = (f32[3,4,2,1152]{3,2,1,0:T(2,128)S(1)}, f32[3,4,2,1152]{3,2,1,0:T(2,128)S(1)}, u32[]{:S(2)}, u32[]{:S(2)}) collective-permute-start(f32[3,4,2,1152]{3,2,1,0:T(2,128)S(1)} %get-tuple-element.26.refs_8_), channel_id=1, source_target_pairs={{0,1},{1,0},{2,3},{3,2},{4,5},{5,4},{6,7},{7,6},{8,9},{9,8},{10,11... | collective-permute-start | bytes 331784 | tf_op jit(solution)/shard_map/ppermute | solution.py:606
  41.8 1.3 %collective-permute-start.11 = (f32[2,4,2,1152]{3,2,1,0:T(2,128)S(1)}, f32[2,4,2,1152]{3,2,1,0:T(2,128)S(1)}, u32[]{:S(2)}, u32[]{:S(2)}) collective-permute-start(f32[2,4,2,1152]{3,2,1,0:T(2,128)S(1)} %get-tuple-element.25.refs_4_), channel_id=1, source_target_pairs={{0,1},{1,0},{2,3},{3,2},{4,5},{5,4},{6,7},{7,6},{8,9},{9,8},{10,11... | collective-permute-start | bytes 221192 | tf_op jit(solution)/shard_map/ppermute | solution.py:606
  43.1 1.4 %collective-permute-start.14 = (f32[3,4,2,1152]{3,2,1,0:T(2,128)S(1)}, f32[3,4,2,1152]{3,2,1,0:T(2,128)S(1)}, u32[]{:S(2)}, u32[]{:S(2)}) collective-permute-start(f32[3,4,2,1152]{3,2,1,0:T(2,128)S(1)} %collective-permute-done.5.refs_2_.refs_10_), channel_id=1, source_target_pairs={{0,1},{1,0},{2,3},{3,2},{4,5},{5,4},{6,7},{7,6},{8,9},{9,8},{10,11... | collective-permute-start | bytes 331784 | tf_op jit(solution)/shard_map/ppermute | solution.py:606
  43.3 1.3 %collective-permute-start.12 = (f32[2,4,2,1152]{3,2,1,0:T(2,128)S(1)}, f32[2,4,2,1152]{3,2,1,0:T(2,128)S(1)}, u32[]{:S(2)}, u32[]{:S(2)}) collective-permute-start(f32[2,4,2,1152]{3,2,1,0:T(2,128)S(1)} %collective-permute-done.4.refs_1_.refs_6_), channel_id=1, source_target_pairs={{0,1},{1,0},{2,3},{3,2},{4,5},{5,4},{6,7},{7,6},{8,9},{9,8},{10,11... | collective-permute-start | bytes 221192 | tf_op jit(solution)/shard_map/ppermute | solution.py:606
  (3 other events, 35.1 us)

commit v9 on v8

--- a/solution.py
+++ b/solution.py
@@ -54,59 +54,89 @@
 
 def north_of(value, beyond):
     rows = value.shape[0]
-    return jnp.where(row_ids(value.shape) == rows - 1, beyond, pltpu.roll(value, rows - 1, 0))
+    rolled = pltpu.roll(value, rows - 1, 0)
+    return rolled if beyond is None else jnp.where(row_ids(value.shape) == rows - 1, beyond, rolled)
 
 
 def south_of(value, beyond):
-    return jnp.where(row_ids(value.shape) == 0, beyond, pltpu.roll(value, 1, 0))
+    rolled = pltpu.roll(value, 1, 0)
+    return rolled if beyond is None else jnp.where(row_ids(value.shape) == 0, beyond, rolled)
 
 
 def fluxes(geo, thick, u, v, thick_s, v_s, thick_n):
     rows = thick.shape[0]
     east = u * jnp.where(u > 0, thick, east_of(thick))
     north = v * jnp.where(v > 0, thick, north_of(thick, thick_n)) * geo[0:rows, 1:2]
-    below = v_s * jnp.where(v_s > 0, thick_s, thick[0:1]) * geo[0:1, 0:1]
+    below = None if v_s is None else v_s * jnp.where(v_s > 0, thick_s, thick[0:1]) * geo[0:1, 0:1]
     return east, north, below
 
 
 def tracer_change(q, q_s, q_n, thick, u, v, v_s, east, north, below, inverse):
     t_east = east * jnp.where(u > 0, q, east_of(q))
     t_north = north * jnp.where(v > 0, q, north_of(q, q_n))
-    t_below = below * jnp.where(v_s > 0, q_s, q[0:1])
+    t_below = None if v_s is None else below * jnp.where(v_s > 0, q_s, q[0:1])
     change = thick * q - (t_east - west_of(t_east))
     return change - (t_north - south_of(t_north, t_below)) * inverse
 
 
-def inner_kernel(band_ref, table_hbm, thick_hbm, u_hbm, v_hbm, tracer_hbm, *refs):
-    out_ref, sum_ref, near_ref, near_rest_ref, geo_ref, wind_ref, tracer_ref, sems = refs
-    T, L, rows, width = tracer_ref.shape
+def first_kernel(band_ref, table_hbm, thick_hbm, u_hbm, v_hbm, tracer_hbm, *refs):
+    new_ref, sum_ref, thick_ref, u_ref, v_ref, tracer_ref, geo_ref, sems = refs
+    L, rows, _ = thick_ref.shape
+    table_copy = pltpu.make_async_copy(table_hbm.at[band_ref[0]], geo_ref, sems.at[3, 0])
+    table_copy.start()
+    pairs = ((thick_hbm, thick_ref), (u_hbm, u_ref), (v_hbm, v_ref))
 
     def copies(k):
-        return [
-            pltpu.make_async_copy(thick_hbm.at[k], wind_ref.at[0, k], sems.at[0, k]),
-            pltpu.make_async_copy(u_hbm.at[k], wind_ref.at[1, k], sems.at[1, k]),
-            pltpu.make_async_copy(v_hbm.at[k], wind_ref.at[2, k], sems.at[2, k]),
-        ] + [
-            pltpu.make_async_copy(tracer_hbm.at[c, k], tracer_ref.at[c, k], sems.at[3 + c, k]) for c in range(T)
-        ]
-
-    table_copy = pltpu.make_async_copy(table_hbm.at[band_ref[0]], geo_ref, sems.at[3 + T, 0])
-    table_copy.start()
+        return [pltpu.make_async_copy(a.at[k], b.at[k], sems.at[i, k]) for i, (a, b) in enumerate(pairs)]
+
     for k in range(L):
         for copy in copies(k):
             copy.start()
+    tracer_copy = pltpu.make_async_copy(tracer_hbm, tracer_ref, sems.at[3, 1])
+    tracer_copy.start()
     table_copy.wait()
     geo = geo_ref[...]
-    nothing = jnp.zeros((1, width), jnp.float32)
-    inverse = geo[0:rows, 2:3]
     sum_ref[...] = jnp.zeros_like(sum_ref)
 
     def level(k, carry):
         for copy in copies(k):
             copy.wait()
-        thick, u, v = wind_ref[0, k], wind_ref[1, k], wind_ref[2, k]
-        east, north, below = fluxes(geo, thick, u, v, nothing, nothing, nothing)
-        new = thick - (east - west_of(east)) - (north - south_of(north, below)) * inverse
+        thick, u, v = thick_ref[k], u_ref[k], v_ref[k]
+        east, north, _ = fluxes(geo, thick, u, v, None, None, None)
+        new = thick - (east - west_of(east)) - (north - south_of(north, None)) * geo[0:rows, 2:3]
+        new_ref[k] = new
+        sum_ref[...] += new
+        return carry
+
+    lax.fori_loop(0, L, level, 0)
+    tracer_copy.wait()
+
+
+def first_step(band, table, thickness, wind_u, wind_v, tracers):
+    L, R, N = thickness.shape
+    arguments = (thickness, wind_u, wind_v, tracers)
+    operands = [pltpu.with_memory_space_constraint(a, pltpu.HBM) for a in (table, *arguments)]
+    shapes = [(L, R, N), (R, N)] + [a.shape for a in arguments]
+    return pl.pallas_call(
+        first_kernel,
+        in_specs=[SMEM] + after(operands),
+        out_specs=[VMEM] * len(shapes),
+        out_shape=[jax.ShapeDtypeStruct(shape, jnp.float32) for shape in shapes],
+        scratch_shapes=[pltpu.VMEM(table.shape[1:], jnp.float32), pltpu.SemaphoreType.DMA((4, max(L, 2)))],
+        compiler_params=params(),
+        cost_estimate=cost(40 * L * R * N, 4 * L * R * N * (7 + 2 * tracers.shape[0])),
+        name="first_step",
+    )(band, *operands)
+
+
+def inner_kernel(band_ref, table_ref, new_ref, thick_ref, u_ref, v_ref, tracer_ref, out_ref, near_ref, near_rest_ref):
+    T, L, rows, _ = tracer_ref.shape
+    geo = table_ref[band_ref[0]]
+    inverse = geo[0:rows, 2:3]
+
+    def level(k, carry):
+        thick, u, v, new = thick_ref[k], u_ref[k], v_ref[k], new_ref[k]
+        east, north, _ = fluxes(geo, thick, u, v, None, None, None)
 
         def store(field, value):
             out_ref[field, k] = value
@@ -115,43 +145,30 @@
             ref[at, k, 1:2] = value[rows - 2 : rows - 1]
 
         store(0, new)
-        sum_ref[...] += new
         scale = 1.0 / new
         for c in range(T):
-            q = tracer_ref[c, k]
-            change = tracer_change(q, nothing, nothing, thick, u, v, nothing, east, north, below, inverse)
+            change = tracer_change(
+                tracer_ref[c, k], None, None, thick, u, v, None, east, north, None, inverse
+            )
             store(1 + c, change * scale)
         return carry
 
     lax.fori_loop(0, L, level, 0)
 
 
-def inner_step(band, table, thickness, wind_u, wind_v, tracers):
+def inner_step(band, table, new, thickness, wind_u, wind_v, tracers):
     L, R, N = thickness.shape
     T = tracers.shape[0]
     shape = lambda n, rows: jax.ShapeDtypeStruct((n, L, rows, N), jnp.float32)
-    in_hbm = lambda x: pltpu.with_memory_space_constraint(x, pltpu.HBM)
-    out_shape = [
-        shape(1 + T, R),
-        jax.ShapeDtypeStruct((R, N), jnp.float32),
-        shape(2, 2),
-        shape(T - 1, 2),
-    ]
     return pl.pallas_call(
         inner_kernel,
-        in_specs=[SMEM] + after([table, thickness, wind_u, wind_v, tracers]),
-        out_specs=[VMEM] * len(out_shape),
-        out_shape=out_shape,
-        scratch_shapes=[
-            pltpu.VMEM(table.shape[1:], jnp.float32),
-            pltpu.VMEM((3, L, R, N), jnp.float32),
-            pltpu.VMEM((T, L, R, N), jnp.float32),
-            pltpu.SemaphoreType.DMA((4 + T, L)),
-        ],
+        in_specs=[SMEM] + [VMEM] * 6,
+        out_specs=[VMEM] * 3,
+        out_shape=[shape(1 + T, R), shape(2, 2), shape(T - 1, 2)],
         compiler_params=params(),
         cost_estimate=cost(130 * L * R * N, 4 * L * R * N * (8 + 2 * T)),
         name="inner_step",
-    )(band, *[in_hbm(a) for a in (table, thickness, wind_u, wind_v, tracers)])
+    )(band, table, new, thickness, wind_u, wind_v, tracers)
 
 
 def filter_tables(N):
@@ -301,6 +318,31 @@
     )
 
 
+def mass_kernel(C, S, place_ref, new_ref, *refs):
+    base_ref, mass_ref = refs[-2:]
+    lev = place_ref[0]
+    others_mass, base = None, None
+    for s in range(1, C):
+        other = functools.reduce(jnp.add, [ref[...] for ref in refs[(s - 1) * S : s * S]])
+        below = jnp.where(lev >= s, other, 0.0)
+        others_mass = other if others_mass is None else others_mass + other
+        base = below if base is None else base + below
+    base_ref[...] = base
+    mass_ref[...] = others_mass
+
+
+def other_chips(counts, place, new, others):
+    return pl.pallas_call(
+        functools.partial(mass_kernel, *counts),
+        in_specs=[SMEM] + [VMEM] * (1 + len(others)),
+        out_specs=[VMEM] * 2,
+        out_shape=[jax.ShapeDtypeStruct(new.shape, jnp.float32)] * 2,
+        compiler_params=params(),
+        cost_estimate=cost(1e11, 1e9),
+        name="other_chips",
+    )(place, new, *others)
+
+
 def weight_sums(weight_ref, firsts, L, levels):
     total = jnp.float32(0.0)
     below = [jnp.float32(0.0) for _ in firsts]
@@ -324,9 +366,8 @@
     group = [functools.reduce(jnp.add, levels) for levels in thick]
     mass = functools.reduce(jnp.add, group)
     base = jnp.zeros_like(mass)
-    for s, other in enumerate(others, 1):
-        mass = mass + other
-        base = base + jnp.where(lev >= s, other, 0.0)
+    if others:
+        base, mass = others[0], mass + others[1]
     sources = []
     for g, levels in enumerate(thick):
         low = base
@@ -345,7 +386,6 @@
 
 def remap_rows(place, weight_ref, counts, steps, thick_refs, field_refs, other_refs, store):
     C, S = counts
-    G = len(thick_refs) // S
     _, L, R, N = thick_refs[0].shape
     lev, sub = place
     firsts = [(lax.rem(lev + s, C) * S + sub) * L for s in steps]
@@ -353,10 +393,7 @@
 
     def tile(at, columns):
         thick = [[ref[0, m, at, columns] for m in range(L)] for ref in thick_refs]
-        others = [
-            functools.reduce(jnp.add, [ref[at, columns] for ref in other_refs[s * S : (s + 1) * S]])
-            for s in range(C - G)
-        ]
+        others = [ref[at, columns] for ref in other_refs]
         mass, sources = source_levels(place, counts, thick, others)
         unit = mass / weight_sum
         for index, s in enumerate(steps):
@@ -394,7 +431,7 @@
     for _ in range(sizes[0]):
         bundles.append(refs[:S])
         refs = refs[S:]
-    other_refs, out_refs = refs[: (C - 1) * S], refs[len(refs) - len(steps) :]
+    other_refs, out_refs = refs[:2], refs[len(refs) - len(steps) :]
     _, L, R, _ = thick_refs[0].shape
     field_refs = [[(ref, index) for ref in bundles[which]] for which, index in fields]
 
@@ -476,7 +513,7 @@
 def finish_kernel(counts, margin, place_ref, weight_ref, *refs):
     C, S = counts
     group_refs, refs = refs[:S], refs[S:]
-    other_refs, refs = refs[: (C - 1) * S], refs[(C - 1) * S :]
+    other_refs, refs = refs[:2], refs[2:]
     *arrived_refs, near_ref, edge_ref, thick_edge_ref, out_ref, thick_out_ref, token_ref = refs
     token_ref[...] = jnp.zeros_like(token_ref)
     T, L, R, _ = out_ref.shape
@@ -635,11 +672,13 @@
 
     remap = functools.partial(remap_parts, (C, S), place, level_weights)
 
-    inner, own_sum, near, near_rest = inner_step(band, table, thickness, wind_u, wind_v, tracers)
+    new, own_sum, *arguments = first_step(band, table, thickness, wind_u, wind_v, tracers)
     others = [send(own_sum, s=s, t=t) for s in away for t in range(S)]
+    inner, near, near_rest = inner_step(band, table, new, *arguments)
     group = with_others_of_chip(inner)
     near = [near] + [send(near, s=s, t=0) for s in away]
     near_rest = [near_rest] + [send(near_rest, s=s, t=0) for s in away]
+    others = other_chips((C, S), place, own_sum, others)
     tracer_fields = [(0, 1 + c) for c in range(T)]
     away_parts = remap(group, [group], others, tracer_fields, away, 2)
     arrived = sent(away_parts)

time: 53.2 us -> 52.4 us (0.985)
  waiting for transfers between devices: 13.6 us -> 11.6 us
  Pallas kernels: 20.8 us -> 22 us
    pallas_call x1 -> x3, Pallas kernels: 3.26 us -> 4.39 us  [the longest x1 1.83 us: first_step(): pl.pallas_call(first_kernel, in_specs=[SMEM] + after(operands), out_specs...]
    ppermute x6, waiting for transfers between devices: 7.7 us -> 6.69 us  [shifted(): lax.ppermute(value, 'lev', [(i, (i + s) % lev_count) for i in range(lev_c...]
    ppermute x1, waiting for transfers between devices: 1.36 us -> 0.37 us  [shifted(): return lax.ppermute(value, ('lev', 'sub'), pairs)]
  transfers between devices with their start and end apart: 18 -> 18, of which waited for: 9 -> 7; matrix products, arithmetic and copies ran while one was open for 0% -> 0% of each run, Pallas kernels for 31% -> 37%
where the time goes in v9:
time: 52.4 us; the launch traced here: 52.1 us
  Pallas kernels  22 us (42%)
  starting transfers between devices  17.4 us (33%)
  waiting for transfers between devices  11.6 us (22%)
  between operations  0.85 us (2%)
    ppermute x6, starting transfers between devices, shifted(): lax.ppermute(value, 'lev', [(i, (i + s) % lev_count) for i in range(lev_c...  9.75 us
    ppermute x6, waiting for transfers between devices, shifted(): lax.ppermute(value, 'lev', [(i, (i + s) % lev_count) for i in range(lev_c...  6.69 us
    ppermute x1, starting transfers between devices, per_device(): up = lax.ppermute(last, 'lat', northward)  4.55 us
    pallas_call x2, Pallas kernels, remap_parts(): pl.pallas_call(functools.partial(remap_kernel, counts, tuple(steps), tupl...  4.36 us
    pallas_call x1, Pallas kernels, remap_edges(): pl.pallas_call(functools.partial(remap_edge_kernel, counts, near_fields),...  3.66 us
    pallas_call x1, Pallas kernels, second_step(): pl.pallas_call(functools.partial(second_kernel, lat_rows), grid=(L,), in_...  3.66 us
    pallas_call x1, Pallas kernels, finish_tracers(): pl.pallas_call(functools.partial(finish_kernel, counts, margin), in_specs...  3.25 us
    ppermute x1, waiting for transfers between devices, per_device(): up = lax.ppermute(last, 'lat', northward)  2.3 us
  transfers between devices with their start and end apart: 18, of which 7 were waited for; matrix products, arithmetic and copies ran while one was open for 0% of the time, Pallas kernels for 37%

profile of v9, /device:TPU:0, one launch (start us, length us, event | category | flops | bytes accessed | tf_op | source)
XLA Modules:
  0.0 52.1 jit_solution(425380171090128234)
XLA Ops:
  0.6 1.8 %first_step.1 = (f32[4,16,1152]{2,1,0:T(8,128)S(1)}, f32[16,1152]{1,0:T(8,128)S(1)}, f32[4,16,1152]{2,1,0:T(8,128)S(1)}, f32[4,16,1152]{2,1,0:T(8,128)S(1)}, f32...) custom-call(s32[1]{0:T(128)} %bitcast.2.band_ref, f32[4,24,128]{2,1,0:T(8,128)} %constant.17.clone.table_hbm.table_ref, ...), custom_call_target="tpu_custom_call" | custom-call | flops 2949120 | bytes 4423680 | tf_op jit(solution)/shard_map/first_step/pallas_call | solution.py:120
  2.5 3.0 %collective-permute-start.1 = (f32[16,1152]{1,0:T(8,128)S(1)}, f32[16,1152]{1,0:T(8,128)S(1)}, u32[]{:S(2)}, u32[]{:S(2)}) collective-permute-start(f32[16,1152]{1,0:T(8,128)S(1)} %get-tuple-element.36.new_ref), channel_id=1, source_target_pairs={{0,2},{2,0},{1,3},{3,1},{4,6},{6,4},{5,7},{7,5},{8,10},{10,8},{9,1... | collective-permute-start | bytes 221192 | tf_op jit(solution)/shard_map/ppermute | solution.py:641
  5.5 1.7 %inner_step.1 = (f32[5,4,16,1152]{3,2,1,0:T(8,128)S(1)}, f32[2,4,2,1152]{3,2,1,0:T(2,128)S(1)}, f32[3,4,2,1152]{3,2,1,0:T(2,128)S(1)}) custom-call(s32[1]{0:T(128)} %bitcast.2.band_ref, f32[4,24,128]{2,1,0:T(8,128)S(1)} %copy-done.6, f32[4,16,1152]{2,1,0:T(8,128)S(1)} %get-tuple-element.30.new_ref, f32[4,16,1152]{2,1,0:T(8,128)S(1)} %get-tuple-element.31.thick_ref, ...), custom_call_target="tpu_custom_call" | custom-call | flops 9584640 | bytes 4718592 | tf_op jit(solution)/shard_map/inner_step/pallas_call | solution.py:163
  7.4 1.9 %collective-permute-start.5 = (f32[3,4,2,1152]{3,2,1,0:T(2,128)S(1)}, f32[3,4,2,1152]{3,2,1,0:T(2,128)S(1)}, u32[]{:S(2)}, u32[]{:S(2)}) collective-permute-start(f32[3,4,2,1152]{3,2,1,0:T(2,128)S(1)} %get-tuple-element.40.refs_8_), channel_id=1, source_target_pairs={{0,2},{2,0},{1,3},{3,1},{4,6},{6,4},{5,7},{7,5},{8,10},{10,8},{9,1... | collective-permute-start | bytes 331784 | tf_op jit(solution)/shard_map/ppermute | solution.py:641
  9.9 0.9 %other_chips.1 = (f32[16,1152]{1,0:T(8,128)S(1)}, f32[16,1152]{1,0:T(8,128)S(1)}) custom-call(s32[2]{0:T(128)S(1)} %pad_add_fusion.place_ref, f32[16,1152]{1,0:T(8,128)S(1)} %get-tuple-element.36.new_ref, f32[16,1152]{1,0:T(8,128)S(1)} %collective-permute-done.1.refs_0_, f32[16,1152]{1,0:T(8,128)} %collective-permute-done.2.refs_1_), custom_call_target="tpu_custom_call" | custom-call | flops 99999997952 | bytes 1000000000 | tf_op jit(solution)/shard_map/other_chips/pallas_call | solution.py:335
  10.8 2.0 %remap_parts.2.refs_0_ = f32[192,1152]{1,0:T(8,128)S(1)} custom-call(s32[2]{0:T(128)S(1)} %pad_add_fusion.place_ref, f32[16]{0:T(128)S(1)} %copy-done.7, f32[5,4,16,1152]{3,2,1,0:T(8,128)S(1)} %get-tuple-element.35.refs_0_.refs_2_, f32[5,4,16,1152]{3,2,1,0:T(8,128)S(1)} %collective-permute-done.refs_1_.refs_3_, ...), custom_call_target="tpu_custom_call" | custom-call | flops 7667712 | bytes 4423680 | tf_op jit(solution)/shard_map/remap_parts/pallas_call | solution.py:460
  12.9 1.6 %collective-permute-start.3 = (f32[192,1152]{1,0:T(8,128)S(1)}, f32[192,1152]{1,0:T(8,128)S(1)}, u32[]{:S(2)}, u32[]{:S(2)}) collective-permute-start(f32[192,1152]{1,0:T(8,128)S(1)} %remap_parts.2.refs_0_), channel_id=1, source_target_pairs={{0,2},{2,0},{1,3},{3,1},{4,6},{6,4},{5,7},{7,5},{8,10},{10,8},{9,1... | collective-permute-start | bytes 2654216 | tf_op jit(solution)/shard_map/ppermute | solution.py:641
  14.5 1.7 %edge_rows.1 = (f32[6,4,1,1152]{3,2,1,0:T(1,128)S(1)}, f32[8,4,1,1152]{3,2,1,0:T(1,128)S(1)}) custom-call(f32[4,16,1152]{2,1,0:T(8,128)} %thick_ref.1, f32[4,16,1152]{2,1,0:T(8,128)} %u_ref.1, f32[4,16,1152]{2,1,0:T(8,128)} %v_ref.1, f32[4,4,16,1152]{3,2,1,0:T(8,128)} %tracer_ref.1, f32[192,1152]{1,0:T(8,128)S(1)} %remap_parts.2.refs_0_, ...), custom_call_target="tpu_custom_call" | custom-call | flops 10000000000 | bytes 1000000000 | tf_op jit(solution)/shard_map/edge_rows/pallas_call | solution.py:619
  16.3 1.3 %collective-permute-start.7 = (f32[8,4,1,1152]{3,2,1,0:T(1,128)S(1)}, f32[8,4,1,1152]{3,2,1,0:T(1,128)S(1)}, u32[]{:S(2)}, u32[]{:S(2)}) collective-permute-start(f32[8,4,1,1152]{3,2,1,0:T(1,128)S(1)} %get-tuple-element.42), channel_id=1, source_target_pairs={{4,0},{8,4},{12,8},{5,1},{9,5},{13,9},{6,2},{10,6},{14,10},{7,3},{... | collective-permute-start | bytes 442376 | tf_op jit(solution)/shard_map/ppermute | solution.py:690
  17.6 4.6 %collective-permute-start.6 = (f32[6,4,1,1152]{3,2,1,0:T(1,128)S(1)}, f32[6,4,1,1152]{3,2,1,0:T(1,128)S(1)}, u32[]{:S(2)}, u32[]{:S(2)}) collective-permute-start(f32[6,4,1,1152]{3,2,1,0:T(1,128)S(1)} %get-tuple-element.41), channel_id=1, source_target_pairs={{0,4},{4,8},{8,12},{1,5},{5,9},{9,13},{2,6},{6,10},{10,14},{3,7},{... | collective-permute-start | bytes 331784 | tf_op jit(solution)/shard_map/ppermute | solution.py:689
  22.1 2.3 %collective-permute-done.6.up_ref = f32[6,4,1,1152]{3,2,1,0:T(1,128)S(1)} collective-permute-done((f32[6,4,1,1152]{3,2,1,0:T(1,128)S(1)}, f32[6,4,1,1152]{3,2,1,0:T(1,128)S(1)}, u32[]{:S(2)}, u32[]{:S(2)}) %collective-permute-start.6) | collective-permute-done | bytes 110624 | tf_op jit(solution)/shard_map/ppermute | solution.py:689
  24.6 3.7 %second_step.1 = (f32[1,4,16,1152]{3,2,1,0:T(8,128)S(1)}, f32[1,4,16,1152]{3,2,1,0:T(8,128)S(1)}, f32[7,4,2,1152]{3,2,1,0:T(2,128)S(1)}) custom-call(s32[1]{0:T(128)} %bitcast.2.band_ref, f32[4,24,128]{2,1,0:T(8,128)S(1)} %copy-done.6, f32[4,16,1152]{2,1,0:T(8,128)S(1)} %copy-done.1, f32[4,16,1152]{2,1,0:T(8,128)S(1)} %copy-done.2, ...), custom_call_target="tpu_custom_call" | custom-call | flops 503316480 | bytes 3538944 | tf_op jit(solution)/shard_map/second_step/pallas_call | solution.py:300
  28.3 0.5 collective-permute-start.16
  28.8 1.4 %collective-permute-start.9 = (f32[7,4,2,1152]{3,2,1,0:T(2,128)S(1)}, f32[7,4,2,1152]{3,2,1,0:T(2,128)S(1)}, u32[]{:S(2)}, u32[]{:S(2)}) collective-permute-start(f32[7,4,2,1152]{3,2,1,0:T(2,128)S(1)} %get-tuple-element.43.refs_0_), channel_id=1, source_target_pairs={{0,2},{2,0},{1,3},{3,1},{4,6},{6,4},{5,7},{7,5},{8,10},{10,8},{9,1... | collective-permute-start | bytes 774152 | tf_op jit(solution)/shard_map/ppermute | solution.py:641
  30.3 5.2 %collective-permute-done.3.refs_8_.refs_4_ = f32[192,1152]{1,0:T(8,128)S(1)} collective-permute-done((f32[192,1152]{1,0:T(8,128)S(1)}, f32[192,1152]{1,0:T(8,128)S(1)}, u32[]{:S(2)}, u32[]{:S(2)}) %collective-permute-start.3) | collective-permute-done | bytes 884768 | tf_op jit(solution)/shard_map/ppermute | solution.py:641
  35.5 2.4 %remap_parts.3 = (f32[2,4,16,1152]{3,2,1,0:T(8,128)S(1)}, f32[112,1152]{1,0:T(8,128)S(1)}) custom-call(s32[2]{0:T(128)S(1)} %pad_add_fusion.place_ref, f32[16]{0:T(128)S(1)} %copy-done.7, f32[5,4,16,1152]{3,2,1,0:T(8,128)S(1)} %get-tuple-element.35.refs_0_.refs_2_, f32[5,4,16,1152]{3,2,1,0:T(8,128)S(1)} %collective-permute-done.refs_1_.refs_3_, ...), custom_call_target="tpu_custom_call" | custom-call | flops 10616832 | bytes 3538944 | tf_op jit(solution)/shard_map/remap_parts/pallas_call | solution.py:460
  37.9 1.6 %collective-permute-start.17 = (f32[112,1152]{1,0:T(8,128)S(1)}, f32[112,1152]{1,0:T(8,128)S(1)}, u32[]{:S(2)}, u32[]{:S(2)}) collective-permute-start(f32[112,1152]{1,0:T(8,128)S(1)} %get-tuple-element.46.refs_12_), channel_id=1, source_target_pairs={{0,2},{2,0},{1,3},{3,1},{4,6},{6,4},{5,7},{7,5},{8,10},{10,8},{9,1... | collective-permute-start | bytes 1548296 | tf_op jit(solution)/shard_map/ppermute | solution.py:641
  39.5 1.5 %collective-permute-done.9.refs_2_ = f32[7,4,2,1152]{3,2,1,0:T(2,128)S(1)} collective-permute-done((f32[7,4,2,1152]{3,2,1,0:T(2,128)S(1)}, f32[7,4,2,1152]{3,2,1,0:T(2,128)S(1)}, u32[]{:S(2)}, u32[]{:S(2)}) %collective-permute-start.9) | collective-permute-done | bytes 258080 | tf_op jit(solution)/shard_map/ppermute | solution.py:641
  41.0 0.5 collective-permute-start.13
  41.5 1.3 %collective-permute-done.11.refs_5_ = f32[2,4,2,1152]{3,2,1,0:T(2,128)S(1)} collective-permute-done((f32[2,4,2,1152]{3,2,1,0:T(2,128)S(1)}, f32[2,4,2,1152]{3,2,1,0:T(2,128)S(1)}, u32[]{:S(2)}, u32[]{:S(2)}) %collective-permute-start.11) | collective-permute-done | bytes 73760 | tf_op jit(solution)/shard_map/ppermute | solution.py:643
  43.3 0.9 %collective-permute-done.12.refs_7_ = f32[2,4,2,1152]{3,2,1,0:T(2,128)S(1)} collective-permute-done((f32[2,4,2,1152]{3,2,1,0:T(2,128)S(1)}, f32[2,4,2,1152]{3,2,1,0:T(2,128)S(1)}, u32[]{:S(2)}, u32[]{:S(2)}) %collective-permute-start.12) | collective-permute-done | bytes 73760 | tf_op jit(solution)/shard_map/ppermute | solution.py:643
  44.2 3.7 %remap_edges.1 = (f32[6,4,2,1152]{3,2,1,0:T(2,128)S(1)}, f32[4,2,1152]{2,1,0:T(2,128)S(1)}, f32[4,4,2,1152]{3,2,1,0:T(2,128)S(1)}) custom-call(s32[2]{0:T(128)S(1)} %pad_add_fusion.place_ref, f32[16]{0:T(128)S(1)} %copy-done.7, f32[7,4,2,1152]{3,2,1,0:T(2,128)S(1)} %get-tuple-element.43.refs_0_, f32[7,4,2,1152]{3,2,1,0:T(2,128)S(1)} %collective-permute-done.8.refs_1_, ...), custom_call_target="tpu_custom_call" | custom-call | flops 5898240 | bytes 3096576 | tf_op jit(solution)/shard_map/remap_edges/pallas_call | solution.py:498
  47.9 3.3 %finish_tracers.1 = (f32[4,4,16,1152]{3,2,1,0:T(8,128)}, f32[4,16,1152]{2,1,0:T(8,128)}, f32[8,128]{1,0:T(8,128)S(1)}) custom-call(s32[2]{0:T(128)S(1)} %pad_add_fusion.place_ref, f32[16]{0:T(128)S(1)} %copy-done.7, f32[5,4,16,1152]{3,2,1,0:T(8,128)S(1)} %get-tuple-element.35.refs_0_.refs_2_, f32[5,4,16,1152]{3,2,1,0:T(8,128)S(1)} %collective-permute-done.refs_1_.refs_3_, ...), custom_call_target="tpu_custom_call" | custom-call | flops 7667712 | bytes 5898240 | tf_op jit(solution)/shard_map/finish_tracers/pallas_call | solution.py:549
  51.2 0.9 %finish_winds.1 = (f32[4,16,1152]{2,1,0:T(8,128)}, f32[4,16,1152]{2,1,0:T(8,128)}) custom-call(f32[2,4,16,1152]{3,2,1,0:T(8,128)S(1)} %get-tuple-element.51.own_ref, f32[6,4,2,1152]{3,2,1,0:T(2,128)S(1)} %get-tuple-element.48.refs_6_.edge_ref, f32[112,1152]{1,0:T(8,128)S(1)} %collective-permute-done.17.refs_0_, f32[8,128]{1,0:T(8,128)S(1)} %get-tuple-element.52.refs_1_), custom_call_target="tpu_custom_call" | custom-call | flops 147456 | bytes 1769472 | tf_op jit(solution)/shard_map/finish_winds/pallas_call | solution.py:579
  (42 shorter events, 1.6 us)
Async XLA Ops:
  2.5 7.0 %collective-permute-start.1 = (f32[16,1152]{1,0:T(8,128)S(1)}, f32[16,1152]{1,0:T(8,128)S(1)}, u32[]{:S(2)}, u32[]{:S(2)}) collective-permute-start(f32[16,1152]{1,0:T(8,128)S(1)} %get-tuple-element.36.new_ref), channel_id=1, source_target_pairs={{0,2},{2,0},{1,3},{3,1},{4,6},{6,4},{5,7},{7,5},{8,10},{10,8},{9,1... | collective-permute-start | bytes 221192 | tf_op jit(solution)/shard_map/ppermute | solution.py:641
  5.5 4.4 %collective-permute-start.2 = (f32[16,1152]{1,0:T(8,128)S(1)}, f32[16,1152]{1,0:T(8,128)}, u32[]{:S(2)}, u32[]{:S(2)}) collective-permute-start(f32[16,1152]{1,0:T(8,128)S(1)} %get-tuple-element.36.new_ref), channel_id=1, source_target_pairs={{0,3},{1,2},{2,1},{3,0},{4,7},{5,6},{6,5},{7,4},{8,11},{9,10},{10,... | collective-permute-start | bytes 221192 | tf_op jit(solution)/shard_map/ppermute | solution.py:649
  7.2 3.7 %collective-permute-start = (f32[5,4,16,1152]{3,2,1,0:T(8,128)S(1)}, f32[5,4,16,1152]{3,2,1,0:T(8,128)S(1)}, u32[]{:S(2)}, u32[]{:S(2)}) collective-permute-start(f32[5,4,16,1152]{3,2,1,0:T(8,128)S(1)} %get-tuple-element.35.refs_0_.refs_2_), channel_id=1, source_target_pairs={{0,1},{1,0},{2,3},{3,2},{4,5},{5,4},{6,7},{7,6},{8,9},{9,8},{10,11... | collective-permute-start | bytes 4423688 | tf_op jit(solution)/shard_map/ppermute | solution.py:643
  7.4 7.1 %collective-permute-start.5 = (f32[3,4,2,1152]{3,2,1,0:T(2,128)S(1)}, f32[3,4,2,1152]{3,2,1,0:T(2,128)S(1)}, u32[]{:S(2)}, u32[]{:S(2)}) collective-permute-start(f32[3,4,2,1152]{3,2,1,0:T(2,128)S(1)} %get-tuple-element.40.refs_8_), channel_id=1, source_target_pairs={{0,2},{2,0},{1,3},{3,1},{4,6},{6,4},{5,7},{7,5},{8,10},{10,8},{9,1... | collective-permute-start | bytes 331784 | tf_op jit(solution)/shard_map/ppermute | solution.py:641
  9.4 5.2 %collective-permute-start.4 = (f32[2,4,2,1152]{3,2,1,0:T(2,128)S(1)}, f32[2,4,2,1152]{3,2,1,0:T(2,128)S(1)}, u32[]{:S(2)}, u32[]{:S(2)}) collective-permute-start(f32[2,4,2,1152]{3,2,1,0:T(2,128)S(1)} %get-tuple-element.39.refs_4_), channel_id=1, source_target_pairs={{0,2},{2,0},{1,3},{3,1},{4,6},{6,4},{5,7},{7,5},{8,10},{10,8},{9,1... | collective-permute-start | bytes 221192 | tf_op jit(solution)/shard_map/ppermute | solution.py:641
  12.8 11.7 %copy-start = (f32[4,4,16,1152]{3,2,1,0:T(8,128)S(1)}, f32[4,4,16,1152]{3,2,1,0:T(8,128)}, u32[]{:S(2)}) copy-start(f32[4,4,16,1152]{3,2,1,0:T(8,128)} %tracer_ref.1) | copy-start | bytes 3538948
  12.8 11.7 %copy-start.1 = (f32[4,16,1152]{2,1,0:T(8,128)S(1)}, f32[4,16,1152]{2,1,0:T(8,128)}, u32[]{:S(2)}) copy-start(f32[4,16,1152]{2,1,0:T(8,128)} %thick_ref.1) | copy-start | bytes 884740
  12.8 11.7 %copy-start.2 = (f32[4,16,1152]{2,1,0:T(8,128)S(1)}, f32[4,16,1152]{2,1,0:T(8,128)}, u32[]{:S(2)}) copy-start(f32[4,16,1152]{2,1,0:T(8,128)} %u_ref.1) | copy-start | bytes 884740
  12.9 11.7 %copy-start.3 = (f32[4,16,1152]{2,1,0:T(8,128)S(1)}, f32[4,16,1152]{2,1,0:T(8,128)}, u32[]{:S(2)}) copy-start(f32[4,16,1152]{2,1,0:T(8,128)} %v_ref.1) | copy-start | bytes 884740
  12.9 11.7 %copy-start.4 = (bf16[5,256,256]{2,1,0:T(8,128)(2,1)S(1)}, bf16[5,256,256]{2,1,0:T(8,128)(2,1)}, u32[]{:S(2)}) copy-start(bf16[5,256,256]{2,1,0:T(8,128)(2,1)} %constant.18.clone.high_ref) | copy-start | bytes 1966084
  12.9 11.7 %copy-start.5 = (bf16[5,256,256]{2,1,0:T(8,128)(2,1)S(1)}, bf16[5,256,256]{2,1,0:T(8,128)(2,1)}, u32[]{:S(2)}) copy-start(bf16[5,256,256]{2,1,0:T(8,128)(2,1)} %constant.19.clone.low_ref) | copy-start | bytes 1966084
  12.9 22.6 %collective-permute-start.3 = (f32[192,1152]{1,0:T(8,128)S(1)}, f32[192,1152]{1,0:T(8,128)S(1)}, u32[]{:S(2)}, u32[]{:S(2)}) collective-permute-start(f32[192,1152]{1,0:T(8,128)S(1)} %remap_parts.2.refs_0_), channel_id=1, source_target_pairs={{0,2},{2,0},{1,3},{3,1},{4,6},{6,4},{5,7},{7,5},{8,10},{10,8},{9,1... | collective-permute-start | bytes 2654216 | tf_op jit(solution)/shard_map/ppermute | solution.py:641
  16.3 8.2 %collective-permute-start.7 = (f32[8,4,1,1152]{3,2,1,0:T(1,128)S(1)}, f32[8,4,1,1152]{3,2,1,0:T(1,128)S(1)}, u32[]{:S(2)}, u32[]{:S(2)}) collective-permute-start(f32[8,4,1,1152]{3,2,1,0:T(1,128)S(1)} %get-tuple-element.42), channel_id=1, source_target_pairs={{4,0},{8,4},{12,8},{5,1},{9,5},{13,9},{6,2},{10,6},{14,10},{7,3},{... | collective-permute-start | bytes 442376 | tf_op jit(solution)/shard_map/ppermute | solution.py:690
  17.6 6.9 %collective-permute-start.6 = (f32[6,4,1,1152]{3,2,1,0:T(1,128)S(1)}, f32[6,4,1,1152]{3,2,1,0:T(1,128)S(1)}, u32[]{:S(2)}, u32[]{:S(2)}) collective-permute-start(f32[6,4,1,1152]{3,2,1,0:T(1,128)S(1)} %get-tuple-element.41), channel_id=1, source_target_pairs={{0,4},{4,8},{8,12},{1,5},{5,9},{9,13},{2,6},{6,10},{10,14},{3,7},{... | collective-permute-start | bytes 331784 | tf_op jit(solution)/shard_map/ppermute | solution.py:689
  28.2 2.0 %collective-permute-start.15 = (f32[1,4,16,1152]{3,2,1,0:T(8,128)S(1)}, f32[1,4,16,1152]{3,2,1,0:T(8,128)S(1)}, u32[]{:S(2)}, u32[]{:S(2)}) collective-permute-start(f32[1,4,16,1152]{3,2,1,0:T(8,128)S(1)} %get-tuple-element.44.refs_2_), channel_id=1, source_target_pairs={{0,1},{1,0},{2,3},{3,2},{4,5},{5,4},{6,7},{7,6},{8,9},{9,8},{10,11... | collective-permute-start | bytes 884744 | tf_op jit(solution)/shard_map/ppermute | solution.py:643
  28.3 2.0 %collective-permute-start.16 = (f32[1,4,16,1152]{3,2,1,0:T(8,128)S(1)}, f32[1,4,16,1152]{3,2,1,0:T(8,128)S(1)}, u32[]{:S(2)}, u32[]{:S(2)}) collective-permute-start(f32[1,4,16,1152]{3,2,1,0:T(8,128)S(1)} %get-tuple-element.45.refs_4_), channel_id=1, source_target_pairs={{0,1},{1,0},{2,3},{3,2},{4,5},{5,4},{6,7},{7,6},{8,9},{9,8},{10,11... | collective-permute-start | bytes 884744 | tf_op jit(solution)/shard_map/ppermute | solution.py:643
  28.8 12.2 %collective-permute-start.9 = (f32[7,4,2,1152]{3,2,1,0:T(2,128)S(1)}, f32[7,4,2,1152]{3,2,1,0:T(2,128)S(1)}, u32[]{:S(2)}, u32[]{:S(2)}) collective-permute-start(f32[7,4,2,1152]{3,2,1,0:T(2,128)S(1)} %get-tuple-element.43.refs_0_), channel_id=1, source_target_pairs={{0,2},{2,0},{1,3},{3,1},{4,6},{6,4},{5,7},{7,5},{8,10},{10,8},{9,1... | collective-permute-start | bytes 774152 | tf_op jit(solution)/shard_map/ppermute | solution.py:641
  37.9 13.3 %collective-permute-start.17 = (f32[112,1152]{1,0:T(8,128)S(1)}, f32[112,1152]{1,0:T(8,128)S(1)}, u32[]{:S(2)}, u32[]{:S(2)}) collective-permute-start(f32[112,1152]{1,0:T(8,128)S(1)} %get-tuple-element.46.refs_12_), channel_id=1, source_target_pairs={{0,2},{2,0},{1,3},{3,1},{4,6},{6,4},{5,7},{7,5},{8,10},{10,8},{9,1... | collective-permute-start | bytes 1548296 | tf_op jit(solution)/shard_map/ppermute | solution.py:641
  39.5 4.7 %collective-permute-start.8 = (f32[7,4,2,1152]{3,2,1,0:T(2,128)S(1)}, f32[7,4,2,1152]{3,2,1,0:T(2,128)S(1)}, u32[]{:S(2)}, u32[]{:S(2)}) collective-permute-start(f32[7,4,2,1152]{3,2,1,0:T(2,128)S(1)} %get-tuple-element.43.refs_0_), channel_id=1, source_target_pairs={{0,1},{1,0},{2,3},{3,2},{4,5},{5,4},{6,7},{7,6},{8,9},{9,8},{10,11... | collective-permute-start | bytes 774152 | tf_op jit(solution)/shard_map/ppermute | solution.py:643
  41.0 3.2 %collective-permute-start.10 = (f32[7,4,2,1152]{3,2,1,0:T(2,128)S(1)}, f32[7,4,2,1152]{3,2,1,0:T(2,128)S(1)}, u32[]{:S(2)}, u32[]{:S(2)}) collective-permute-start(f32[7,4,2,1152]{3,2,1,0:T(2,128)S(1)} %collective-permute-done.9.refs_2_), channel_id=1, source_target_pairs={{0,1},{1,0},{2,3},{3,2},{4,5},{5,4},{6,7},{7,6},{8,9},{9,8},{10,11... | collective-permute-start | bytes 774152 | tf_op jit(solution)/shard_map/ppermute | solution.py:643
  41.0 1.9 %collective-permute-start.13 = (f32[3,4,2,1152]{3,2,1,0:T(2,128)S(1)}, f32[3,4,2,1152]{3,2,1,0:T(2,128)S(1)}, u32[]{:S(2)}, u32[]{:S(2)}) collective-permute-start(f32[3,4,2,1152]{3,2,1,0:T(2,128)S(1)} %get-tuple-element.40.refs_8_), channel_id=1, source_target_pairs={{0,1},{1,0},{2,3},{3,2},{4,5},{5,4},{6,7},{7,6},{8,9},{9,8},{10,11... | collective-permute-start | bytes 331784 | tf_op jit(solution)/shard_map/ppermute | solution.py:643
  41.5 1.3 %collective-permute-start.11 = (f32[2,4,2,1152]{3,2,1,0:T(2,128)S(1)}, f32[2,4,2,1152]{3,2,1,0:T(2,128)S(1)}, u32[]{:S(2)}, u32[]{:S(2)}) collective-permute-start(f32[2,4,2,1152]{3,2,1,0:T(2,128)S(1)} %get-tuple-element.39.refs_4_), channel_id=1, source_target_pairs={{0,1},{1,0},{2,3},{3,2},{4,5},{5,4},{6,7},{7,6},{8,9},{9,8},{10,11... | collective-permute-start | bytes 221192 | tf_op jit(solution)/shard_map/ppermute | solution.py:643
  42.8 1.4 %collective-permute-start.14 = (f32[3,4,2,1152]{3,2,1,0:T(2,128)S(1)}, f32[3,4,2,1152]{3,2,1,0:T(2,128)S(1)}, u32[]{:S(2)}, u32[]{:S(2)}) collective-permute-start(f32[3,4,2,1152]{3,2,1,0:T(2,128)S(1)} %collective-permute-done.5.refs_2_.refs_10_), channel_id=1, source_target_pairs={{0,1},{1,0},{2,3},{3,2},{4,5},{5,4},{6,7},{7,6},{8,9},{9,8},{10,11... | collective-permute-start | bytes 331784 | tf_op jit(solution)/shard_map/ppermute | solution.py:643
  42.9 1.3 %collective-permute-start.12 = (f32[2,4,2,1152]{3,2,1,0:T(2,128)S(1)}, f32[2,4,2,1152]{3,2,1,0:T(2,128)S(1)}, u32[]{:S(2)}, u32[]{:S(2)}) collective-permute-start(f32[2,4,2,1152]{3,2,1,0:T(2,128)S(1)} %collective-permute-done.4.refs_1_.refs_6_), channel_id=1, source_target_pairs={{0,1},{1,0},{2,3},{3,2},{4,5},{5,4},{6,7},{7,6},{8,9},{9,8},{10,11... | collective-permute-start | bytes 221192 | tf_op jit(solution)/shard_map/ppermute | solution.py:643
  (3 other events, 17.8 us)

commit v10 on v9

--- a/solution.py
+++ b/solution.py
@@ -11,7 +11,6 @@
 
 LANES = 128
 VMEM = pl.BlockSpec(memory_space=pltpu.VMEM)
-SMEM = pl.BlockSpec(memory_space=pltpu.SMEM)
 
 
 def params():
@@ -79,10 +78,10 @@
     return change - (t_north - south_of(t_north, t_below)) * inverse
 
 
-def first_kernel(band_ref, table_hbm, thick_hbm, u_hbm, v_hbm, tracer_hbm, *refs):
+def first_kernel(table_hbm, thick_hbm, u_hbm, v_hbm, tracer_hbm, *refs):
     new_ref, sum_ref, thick_ref, u_ref, v_ref, tracer_ref, geo_ref, sems = refs
     L, rows, _ = thick_ref.shape
-    table_copy = pltpu.make_async_copy(table_hbm.at[band_ref[0]], geo_ref, sems.at[3, 0])
+    table_copy = pltpu.make_async_copy(table_hbm.at[lax.axis_index("lat")], geo_ref, sems.at[3, 0])
     table_copy.start()
     pairs = ((thick_hbm, thick_ref), (u_hbm, u_ref), (v_hbm, v_ref))
 
@@ -112,26 +111,26 @@
     tracer_copy.wait()
 
 
-def first_step(band, table, thickness, wind_u, wind_v, tracers):
+def first_step(table, thickness, wind_u, wind_v, tracers):
     L, R, N = thickness.shape
     arguments = (thickness, wind_u, wind_v, tracers)
     operands = [pltpu.with_memory_space_constraint(a, pltpu.HBM) for a in (table, *arguments)]
     shapes = [(L, R, N), (R, N)] + [a.shape for a in arguments]
     return pl.pallas_call(
         first_kernel,
-        in_specs=[SMEM] + after(operands),
+        in_specs=after(operands),
         out_specs=[VMEM] * len(shapes),
         out_shape=[jax.ShapeDtypeStruct(shape, jnp.float32) for shape in shapes],
         scratch_shapes=[pltpu.VMEM(table.shape[1:], jnp.float32), pltpu.SemaphoreType.DMA((4, max(L, 2)))],
         compiler_params=params(),
         cost_estimate=cost(40 * L * R * N, 4 * L * R * N * (7 + 2 * tracers.shape[0])),
         name="first_step",
-    )(band, *operands)
-
-
-def inner_kernel(band_ref, table_ref, new_ref, thick_ref, u_ref, v_ref, tracer_ref, out_ref, near_ref, near_rest_ref):
+    )(*operands)
+
+
+def inner_kernel(table_ref, new_ref, thick_ref, u_ref, v_ref, tracer_ref, out_ref, near_ref, near_rest_ref):
     T, L, rows, _ = tracer_ref.shape
-    geo = table_ref[band_ref[0]]
+    geo = table_ref[lax.axis_index("lat")]
     inverse = geo[0:rows, 2:3]
 
     def level(k, carry):
@@ -156,19 +155,19 @@
     lax.fori_loop(0, L, level, 0)
 
 
-def inner_step(band, table, new, thickness, wind_u, wind_v, tracers):
+def inner_step(table, new, thickness, wind_u, wind_v, tracers):
     L, R, N = thickness.shape
     T = tracers.shape[0]
     shape = lambda n, rows: jax.ShapeDtypeStruct((n, L, rows, N), jnp.float32)
     return pl.pallas_call(
         inner_kernel,
-        in_specs=[SMEM] + [VMEM] * 6,
+        in_specs=[VMEM] * 6,
         out_specs=[VMEM] * 3,
         out_shape=[shape(1 + T, R), shape(2, 2), shape(T - 1, 2)],
         compiler_params=params(),
         cost_estimate=cost(130 * L * R * N, 4 * L * R * N * (8 + 2 * T)),
         name="inner_step",
-    )(band, table, new, thickness, wind_u, wind_v, tracers)
+    )(table, new, thickness, wind_u, wind_v, tracers)
 
 
 def filter_tables(N):
@@ -240,12 +239,13 @@
 
 
 def second_kernel(
-    lat_rows, band_ref, table_ref, thick_ref, u_ref, v_ref, tracer_ref, up_ref, down_ref, cutoff_ref, high_ref, low_ref, *refs
+    lat_rows, table_ref, thick_ref, u_ref, v_ref, tracer_ref, up_ref, down_ref, cutoff_ref, high_ref, low_ref, *refs
 ):
     *wind_refs, edge_ref, new_wind = refs
     k = pl.program_id(0)
     _, L, rows, width = new_wind.shape
-    geo = table_ref[band_ref[0]]
+    band = lax.axis_index("lat")
+    geo = table_ref[band]
     thick, u, v = thick_ref[0], u_ref[0], v_ref[0]
     thick_s, v_s = up_ref[0, 0], up_ref[1, 0]
     thick_n, thick_nn, u_n, v_n = (down_ref[i, 0] for i in range(4))
@@ -260,7 +260,7 @@
         - (north_n - north[rows - 1 : rows]) * geo[rows : rows + 1, 2:3]
     )
     new_wind[0, k] = u - 0.05 * (east_of(new) - new)
-    inside = band_ref[0] * rows + row_ids(new.shape) < lat_rows - 1
+    inside = band * rows + row_ids(new.shape) < lat_rows - 1
     new_wind[1, k] = jnp.where(inside, v - 0.05 * (north_of(new, new_n) - new), 0.0)
 
     def store_edges(field, level, value):
@@ -290,7 +290,7 @@
                 store_edges(1 + f, level, wind_refs[f][0, level])
 
 
-def second_step(band, table, lat_rows, thickness, wind_u, wind_v, tracers, up, down, cutoff):
+def second_step(table, lat_rows, thickness, wind_u, wind_v, tracers, up, down, cutoff):
     L, R, N = thickness.shape
     T = tracers.shape[0]
     high, low = filter_tables(N)
@@ -300,7 +300,7 @@
     return pl.pallas_call(
         functools.partial(second_kernel, lat_rows),
         grid=(L,),
-        in_specs=[SMEM, whole(table.shape), level, level, level, some(T, R), some(2 + T, 1), some(4 + T, 1)]
+        in_specs=[whole(table.shape), level, level, level, some(T, R), some(2 + T, 1), some(4 + T, 1)]
         + [whole((R, LANES)), whole(high.shape), whole(low.shape)],
         out_specs=[whole((1, L, R, N)), whole((1, L, R, N)), whole((3 + T, L, 2, N))],
         out_shape=[
@@ -313,14 +313,14 @@
         cost_estimate=cost(12 * 2 * L * R * high.size, 4 * L * R * N * (8 + T)),
         name="second_step",
     )(
-        band, table, thickness, wind_u, wind_v, tracers, up, down,
+        table, thickness, wind_u, wind_v, tracers, up, down,
         jnp.broadcast_to(cutoff[:, None], (R, LANES)), jnp.asarray(high), jnp.asarray(low),
     )
 
 
-def mass_kernel(C, S, place_ref, new_ref, *refs):
+def mass_kernel(C, S, *refs):
     base_ref, mass_ref = refs[-2:]
-    lev = place_ref[0]
+    lev = lax.axis_index("lev")
     others_mass, base = None, None
     for s in range(1, C):
         other = functools.reduce(jnp.add, [ref[...] for ref in refs[(s - 1) * S : s * S]])
@@ -331,32 +331,25 @@
     mass_ref[...] = others_mass
 
 
-def other_chips(counts, place, new, others):
+def other_chips(counts, others):
     return pl.pallas_call(
         functools.partial(mass_kernel, *counts),
-        in_specs=[SMEM] + [VMEM] * (1 + len(others)),
+        in_specs=[VMEM] * len(others),
         out_specs=[VMEM] * 2,
-        out_shape=[jax.ShapeDtypeStruct(new.shape, jnp.float32)] * 2,
+        out_shape=[jax.ShapeDtypeStruct(others[0].shape, jnp.float32)] * 2,
         compiler_params=params(),
         cost_estimate=cost(1e11, 1e9),
         name="other_chips",
-    )(place, new, *others)
-
-
-def weight_sums(weight_ref, firsts, L, levels):
-    total = jnp.float32(0.0)
-    below = [jnp.float32(0.0) for _ in firsts]
-    for k in range(levels):
-        w = weight_ref[k]
-        below = [b + jnp.where(k < first, w, 0.0) for b, first in zip(below, firsts)]
-        total = total + w
-    weights = [[weight_ref[first + i] for i in range(L)] for first in firsts]
-    sums = []
-    for start, row in zip(below, weights):
-        sums.append([start])
-        for w in row:
-            sums[-1].append(sums[-1][-1] + w)
-    return total, weights, sums
+    )(*others)
+
+
+def add_weights(weight_ref, sum_ref):
+    total = jnp.zeros(weight_ref.shape[1:], jnp.float32)
+    for k in range(weight_ref.shape[0]):
+        sum_ref[k] = total
+        total = total + weight_ref[k]
+    sum_ref[weight_ref.shape[0]] = total
+    return total
 
 
 def source_levels(place, counts, thick, others):
@@ -384,12 +377,13 @@
     return [jnp.minimum(jnp.maximum(top - low, 0.0), value) for _, _, low, value in sources]
 
 
-def remap_rows(place, weight_ref, counts, steps, thick_refs, field_refs, other_refs, store):
+def remap_rows(weight_ref, sum_ref, counts, steps, thick_refs, field_refs, other_refs, store):
     C, S = counts
     _, L, R, N = thick_refs[0].shape
-    lev, sub = place
+    rows = min(R, 8)
+    place = lev, sub = lax.axis_index("lev"), lax.axis_index("sub")
     firsts = [(lax.rem(lev + s, C) * S + sub) * L for s in steps]
-    weight_sum, weights, sums = weight_sums(weight_ref, firsts, L, C * S * L)
+    weight_sum = add_weights(weight_ref, sum_ref)[0:rows]
 
     def tile(at, columns):
         thick = [[ref[0, m, at, columns] for m in range(L)] for ref in thick_refs]
@@ -397,12 +391,12 @@
         mass, sources = source_levels(place, counts, thick, others)
         unit = mass / weight_sum
         for index, s in enumerate(steps):
-            below = covered(unit * sums[index][0], sources)
+            below = covered(unit * sum_ref[firsts[index], 0:rows], sources)
             for i in range(L):
-                upto = covered(unit * sums[index][i + 1], sources)
+                upto = covered(unit * sum_ref[firsts[index] + i + 1, 0:rows], sources)
                 part = [a - b for a, b in zip(upto, below)]
                 below = upto
-                target = unit * weights[index][i]
+                target = unit * weight_ref[firsts[index] + i, 0:rows]
                 scale = 1.0 / target
                 means = []
                 for refs in field_refs:
@@ -410,7 +404,6 @@
                     means.append(functools.reduce(jnp.add, terms) * scale)
                 store(s, i, at, columns, target, means)
 
-    rows = min(R, 8)
     for r in range(0, R, rows):
 
         def body(c, carry):
@@ -424,19 +417,23 @@
     return max(at.start, margin), min(at.stop, rows - margin)
 
 
-def remap_kernel(counts, steps, fields, margin, sizes, place_ref, weight_ref, *refs):
+def remap_kernel(counts, steps, fields, margin, with_thickness, sizes, weight_ref, *refs):
+    *refs, sum_ref = refs
     C, S = counts
     thick_refs, refs = refs[:S], refs[S:]
     bundles = []
     for _ in range(sizes[0]):
         bundles.append(refs[:S])
         refs = refs[S:]
-    other_refs, out_refs = refs[:2], refs[len(refs) - len(steps) :]
+    other_refs, out_refs = refs[:2], refs[len(refs) - len(steps) - with_thickness :]
     _, L, R, _ = thick_refs[0].shape
+    thick_out_ref = out_refs[-1]
     field_refs = [[(ref, index) for ref in bundles[which]] for which, index in fields]
 
     def store(s, i, at, columns, target, means):
         out_ref = out_refs[steps.index(s)]
+        if with_thickness and s == 0:
+            thick_out_ref[i, at, columns] = target
         for f, value in enumerate(means):
             if s == 0:
                 out_ref[f, i, at, columns] = value
@@ -446,33 +443,37 @@
                 out_ref[start + lower : start + upper, columns] = value[lower - at.start : upper - at.start]
 
     remap_rows(
-        (place_ref[0], place_ref[1]), weight_ref, counts, steps, thick_refs, field_refs, other_refs, store
-    )
-
-
-def remap_parts(counts, place, weights, thick, bundles, others, fields, steps, margin, wait=()):
+        weight_ref, sum_ref, counts, steps, thick_refs, field_refs, other_refs, store
+    )
+
+
+def remap_parts(counts, weights, thick, bundles, others, fields, steps, margin, with_thickness=False, wait=()):
     C, S = counts
     _, L, R, N = thick[0].shape
     F = len(fields)
     whole = jax.ShapeDtypeStruct((F, L, R, N), jnp.float32)
     inner = jax.ShapeDtypeStruct((F * L * (R - 2 * margin), N), jnp.float32)
     flat = [a for bundle in bundles for a in bundle]
-    return pl.pallas_call(
-        functools.partial(remap_kernel, counts, tuple(steps), tuple(fields), margin, (len(bundles),)),
-        in_specs=[SMEM] * 2 + [VMEM] * (len(thick) + len(flat) + len(others)) + after(wait),
-        out_specs=[VMEM] * len(steps),
-        out_shape=[whole if s == 0 else inner for s in steps],
+    out_shape = [whole if s == 0 else inner for s in steps]
+    if with_thickness:
+        out_shape.append(jax.ShapeDtypeStruct((L, R, N), jnp.float32))
+    return pl.pallas_call(
+        functools.partial(remap_kernel, counts, tuple(steps), tuple(fields), margin, with_thickness, (len(bundles),)),
+        in_specs=[VMEM] * (1 + len(thick) + len(flat) + len(others)) + after(wait),
+        out_specs=[VMEM] * len(out_shape),
+        out_shape=out_shape,
+        scratch_shapes=[pltpu.VMEM((weights.shape[0] + 1, 8, LANES), jnp.float32)],
         compiler_params=params(),
         cost_estimate=cost(len(steps) * S * L * L * R * N * (5 + 2 * F), 4 * R * N * L * (F + 1) * (S + len(steps))),
         name="remap_parts",
-    )(place, weights, *thick, *flat, *others, *wait)
-
-
-def remap_edge_kernel(counts, near_fields, place_ref, weight_ref, *refs):
+    )(weights, *thick, *flat, *others, *wait)
+
+
+def remap_edge_kernel(counts, near_fields, weight_ref, *refs):
+    *refs, sum_ref = refs
     G = counts[0] * counts[1]
     edge_refs, near_refs, rest_refs = refs[:G], refs[G : 2 * G], refs[2 * G : 3 * G]
     edge_out_ref, thick_out_ref, near_out_ref = refs[-3:]
-    place = (place_ref[0], place_ref[1])
 
     def store_edge(s, i, at, columns, target, means):
         thick_out_ref[i, at, columns] = target
@@ -484,81 +485,68 @@
             near_out_ref[f, i, at, columns] = value
 
     fields = [[(ref, f) for ref in edge_refs] for f in range(1, edge_refs[0].shape[0])]
-    remap_rows(place, weight_ref, counts, (0,), edge_refs, fields, [], store_edge)
+    remap_rows(weight_ref, sum_ref, counts, (0,), edge_refs, fields, [], store_edge)
     bundles = (near_refs, rest_refs)
     fields = [[(ref, index) for ref in bundles[which]] for which, index in near_fields]
-    remap_rows(place, weight_ref, counts, (0,), near_refs, fields, [], store_near)
-
-
-def remap_edges(counts, place, weights, edges, near, near_rest, wait=()):
+    remap_rows(weight_ref, sum_ref, counts, (0,), near_refs, fields, [], store_near)
+
+
+def remap_edges(counts, weights, edges, near, near_rest, wait=()):
     F, L, R, N = edges[0].shape
     T = F - 3
     near_fields = tuple((0, 1) if f == 0 else (1, f - 1) for f in range(T))
     operands = [*edges, *near, *near_rest]
     return pl.pallas_call(
         functools.partial(remap_edge_kernel, counts, near_fields),
-        in_specs=[SMEM] * 2 + [VMEM] * len(operands) + after(wait),
+        in_specs=[VMEM] * (1 + len(operands)) + after(wait),
         out_specs=[VMEM] * 3,
         out_shape=[
             jax.ShapeDtypeStruct((F - 1, L, R, N), jnp.float32),
             jax.ShapeDtypeStruct((L, R, N), jnp.float32),
             jax.ShapeDtypeStruct((T, L, R, N), jnp.float32),
         ],
+        scratch_shapes=[pltpu.VMEM((weights.shape[0] + 1, 8, LANES), jnp.float32)],
         compiler_params=params(),
         cost_estimate=cost(len(edges) * L * L * R * N * 40, 4 * R * N * L * len(operands) * F),
         name="remap_edges",
-    )(place, weights, *operands, *wait)
-
-
-def finish_kernel(counts, margin, place_ref, weight_ref, *refs):
-    C, S = counts
-    group_refs, refs = refs[:S], refs[S:]
-    other_refs, refs = refs[:2], refs[2:]
-    *arrived_refs, near_ref, edge_ref, thick_edge_ref, out_ref, thick_out_ref, token_ref = refs
+    )(weights, *operands, *wait)
+
+
+def finish_kernel(margin, own_ref, near_ref, edge_ref, thick_ref, thick_edge_ref, *refs):
+    *arrived_refs, out_ref, thick_out_ref, token_ref = refs
     token_ref[...] = jnp.zeros_like(token_ref)
     T, L, R, _ = out_ref.shape
-
-    def store(s, i, at, columns, target, means):
-        thick_out_ref[i, at, columns] = target
-        lower, upper = inner_part(at, margin, R)
-        for f, value in enumerate(means):
-            total = value[lower - at.start : upper - at.start]
-            start = (f * L + i) * (R - 2 * margin) - margin
-            for ref in arrived_refs:
-                total = total + ref[start + lower : start + upper, columns]
-            out_ref[f, i, lower:upper, columns] = total
-
-    fields = [[(ref, 1 + f) for ref in group_refs] for f in range(T)]
-    remap_rows((place_ref[0], place_ref[1]), weight_ref, counts, (0,), group_refs, fields, other_refs, store)
+    thick_out_ref[...] = thick_ref[...]
     for i in range(L):
         for row, j in ((0, 0), (R - 1, 1)):
             thick_out_ref[i, row : row + 1] = thick_edge_ref[i, j : j + 1]
-            for f in range(T):
+    for f in range(T):
+        for i in range(L):
+            start = (f * L + i) * (R - 2 * margin)
+            total = own_ref[f, i, margin : R - margin]
+            for ref in arrived_refs:
+                total = total + ref[start : start + R - 2 * margin]
+            out_ref[f, i, margin : R - margin] = total
+            for row, j in ((0, 0), (R - 1, 1)):
                 out_ref[f, i, row : row + 1] = edge_ref[2 + f, i, j : j + 1]
-        for row, j in ((1, 0), (R - 2, 1)):
-            for f in range(T):
+            for row, j in ((1, 0), (R - 2, 1)):
                 out_ref[f, i, row : row + 1] = near_ref[f, i, j : j + 1]
 
 
-def finish_tracers(counts, place, weights, group, others, arrived, near, edge, thick_edge):
-    margin = 2
-    C, S = counts
-    T = group[0].shape[0] - 1
-    _, L, R, N = group[0].shape
-    operands = list(group) + list(others) + list(arrived) + [near, edge, thick_edge]
-    return pl.pallas_call(
-        functools.partial(finish_kernel, counts, margin),
-        in_specs=[SMEM] * 2 + [VMEM] * len(operands),
+def finish_tracers(own, near, edge, thick, thick_edge, arrived):
+    return pl.pallas_call(
+        functools.partial(finish_kernel, 2),
+        in_specs=[VMEM] * (5 + len(arrived)),
         out_specs=[VMEM] * 3,
         out_shape=[
-            jax.ShapeDtypeStruct((T, L, R, N), jnp.float32),
-            jax.ShapeDtypeStruct((L, R, N), jnp.float32),
+            jax.ShapeDtypeStruct(own.shape, jnp.float32),
+            jax.ShapeDtypeStruct(thick.shape, jnp.float32),
             jax.ShapeDtypeStruct((8, LANES), jnp.float32),
         ],
         compiler_params=params(),
-        cost_estimate=cost(S * L * L * R * N * (5 + 2 * T), 4 * R * N * L * (T + 1) * (S + 2)),
+        cost_estimate=cost(2 * own.size, 12 * own.size),
         name="finish_tracers",
-    )(place, weights, *operands)
+    )(own, near, edge, thick, thick_edge, *arrived)
 
 
 def finish_winds_kernel(count, own_ref, edge_ref, *refs):
@@ -659,9 +647,8 @@
     T = tracers.shape[0]
     northward = [(i, i + 1) for i in range(lat_count - 1)]
     southward = [(j, i) for i, j in northward]
-    band = lax.axis_index("lat").astype(jnp.int32).reshape(1)
     table = jnp.asarray(geometry_table(lat_rows, R))
-    place = jnp.stack([lax.axis_index("lev"), lax.axis_index("sub")]).astype(jnp.int32)
+    weights = jnp.broadcast_to(level_weights[:, None, None], (level_weights.shape[0], 8, LANES))
     away = range(1, C)
 
     def with_others_of_chip(own):
@@ -670,15 +657,15 @@
     def sent(parts):
         return [send(part, s=s, t=0) for s, part in zip(away, parts)]
 
-    remap = functools.partial(remap_parts, (C, S), place, level_weights)
-
-    new, own_sum, *arguments = first_step(band, table, thickness, wind_u, wind_v, tracers)
+    remap = functools.partial(remap_parts, (C, S), weights)
+
+    new, own_sum, *arguments = first_step(table, thickness, wind_u, wind_v, tracers)
     others = [send(own_sum, s=s, t=t) for s in away for t in range(S)]
-    inner, near, near_rest = inner_step(band, table, new, *arguments)
+    inner, near, near_rest = inner_step(table, new, *arguments)
     group = with_others_of_chip(inner)
     near = [near] + [send(near, s=s, t=0) for s in away]
     near_rest = [near_rest] + [send(near_rest, s=s, t=0) for s in away]
-    others = other_chips((C, S), place, own_sum, others)
+    others = other_chips((C, S), others)
     tracer_fields = [(0, 1 + c) for c in range(T)]
     away_parts = remap(group, [group], others, tracer_fields, away, 2)
     arrived = sent(away_parts)
@@ -688,20 +675,23 @@
     )
     up = lax.ppermute(last, "lat", northward)
     down = lax.ppermute(leading, "lat", southward)
-    u, v, edge = second_step(band, table, lat_rows, thickness, wind_u, wind_v, tracers, up, down, cutoff)
+    u, v, edge = second_step(table, lat_rows, thickness, wind_u, wind_v, tracers, up, down, cutoff)
     edges = [edge] + [send(edge, s=s, t=0) for s in away]
     winds = [with_others_of_chip(u), with_others_of_chip(v)]
-    winds_own, *winds_away = remap(group, winds, others, [(0, 0), (1, 0)], range(C), 1, wait=arrived[:1])
+    tracers_own, thick_inner = remap(group, [group], others, tracer_fields, (0,), 0, with_thickness=True, wait=[edge])
+    winds_own, *winds_away = remap(
+        group, winds, others, [(0, 0), (1, 0)], range(C), 1, wait=[tracers_own, *arrived[:1]]
+    )
     winds_arrived = sent(winds_away)
     near, near_rest, edges = (
         [a for own in sources for a in with_others_of_chip(own)] for sources in (near, near_rest, edges)
     )
     edge_out, thick_edge, near_out = remap_edges(
-        (C, S), place, level_weights, edges, near, near_rest, wait=winds_away[:1]
+        (C, S), weights, edges, near, near_rest, wait=winds_away[:1]
     )
 
     tracers_out, thickness_out, token = finish_tracers(
-        (C, S), place, level_weights, group, others, arrived, near_out, edge_out, thick_edge
+        tracers_own, near_out, edge_out, thick_inner, thick_edge, arrived
     )
     u_out, v_out = finish_winds(winds_own, winds_arrived, edge_out, [token])
     return thickness_out, u_out, v_out, tracers_out

time: 52.4 us -> 51.8 us (0.989)
  Pallas kernels: 22 us -> 18.7 us
  waiting for transfers between devices: 11.6 us -> 13.7 us
  starting transfers between devices: 17.4 us -> 18.1 us
    pallas_call x4, Pallas kernels: 7.64 us -> 4.86 us  [the longest x1 1.83 us: first_step(): pl.pallas_call(first_kernel, in_specs=after(operands), out_specs=[VMEM] *...]
    ppermute x6, waiting for transfers between devices: 6.69 us -> 8.17 us  [shifted(): lax.ppermute(value, 'lev', [(i, (i + s) % lev_count) for i in range(lev_c...]
    ppermute x6, starting transfers between devices: 9.75 us -> 10.4 us  [shifted(): lax.ppermute(value, 'lev', [(i, (i + s) % lev_count) for i in range(lev_c...]
    ppermute x9, waiting for transfers between devices: 2.26 us -> 2.86 us  [shifted(): lax.ppermute(value, 'sub', [(i, (i + t) % sub_count) for i in range(sub_c...]
    pallas_call x1, Pallas kernels: 3.66 us -> 3.07 us  [remap_edges(): pl.pallas_call(functools.partial(remap_edge_kernel, counts, near_fields),...]
    pallas_call x2 -> x3, Pallas kernels: 4.36 us -> 4.48 us  [remap_parts(): pl.pallas_call(functools.partial(remap_kernel, counts, tuple(steps), tupl...]
  transfers between devices with their start and end apart: 18 -> 18, of which waited for: 7 -> 9; matrix products, arithmetic and copies ran while one was open for 0% -> 0% of each run, Pallas kernels for 37% -> 31%
where the time goes in v10:
time: 51.8 us; the launch traced here: 51.5 us
  Pallas kernels  18.7 us (36%)
  starting transfers between devices  18.1 us (35%)
  waiting for transfers between devices  13.7 us (26%)
  between operations  0.85 us (2%)
    ppermute x6, starting transfers between devices, shifted(): lax.ppermute(value, 'lev', [(i, (i + s) % lev_count) for i in range(lev_c...  10.4 us
    ppermute x6, waiting for transfers between devices, shifted(): lax.ppermute(value, 'lev', [(i, (i + s) % lev_count) for i in range(lev_c...  8.17 us
    ppermute x1, starting transfers between devices, per_device(): up = lax.ppermute(last, 'lat', northward)  4.55 us
    pallas_call x3, Pallas kernels, remap_parts(): pl.pallas_call(functools.partial(remap_kernel, counts, tuple(steps), tupl...  4.48 us
    pallas_call x1, Pallas kernels, second_step(): pl.pallas_call(functools.partial(second_kernel, lat_rows), grid=(L,), in_...  3.61 us
    pallas_call x1, Pallas kernels, remap_edges(): pl.pallas_call(functools.partial(remap_edge_kernel, counts, near_fields),...  3.07 us
    ppermute x9, waiting for transfers between devices, shifted(): lax.ppermute(value, 'sub', [(i, (i + t) % sub_count) for i in range(sub_c...  2.86 us
    ppermute x1, waiting for transfers between devices, per_device(): up = lax.ppermute(last, 'lat', northward)  2.3 us
  transfers between devices with their start and end apart: 18, of which 9 were waited for; matrix products, arithmetic and copies ran while one was open for 0% of the time, Pallas kernels for 31%

profile of v10, /device:TPU:0, one launch (start us, length us, event | category | flops | bytes accessed | tf_op | source)
XLA Modules:
  0.0 51.5 jit_solution(12177340209011717377)
XLA Ops:
  0.6 1.8 %first_step.1 = (f32[4,16,1152]{2,1,0:T(8,128)S(1)}, f32[16,1152]{1,0:T(8,128)S(1)}, f32[4,16,1152]{2,1,0:T(8,128)S(1)}, f32[4,16,1152]{2,1,0:T(8,128)S(1)}, f32...) custom-call(f32[4,24,128]{2,1,0:T(8,128)} %constant.6.clone.table_hbm.table_ref, f32[4,16,1152]{2,1,0:T(8,128)} %thick_ref.1, ...), custom_call_target="tpu_custom_call" | custom-call | flops 2949120 | bytes 4423680 | tf_op jit(solution)/shard_map/first_step/pallas_call | solution.py:119
  2.5 3.0 %collective-permute-start.1 = (f32[16,1152]{1,0:T(8,128)S(1)}, f32[16,1152]{1,0:T(8,128)S(1)}, u32[]{:S(2)}, u32[]{:S(2)}) collective-permute-start(f32[16,1152]{1,0:T(8,128)S(1)} %get-tuple-element.38), channel_id=1, source_target_pairs={{0,2},{2,0},{1,3},{3,1},{4,6},{6,4},{5,7},{7,5},{8,10},{10,8},{9,1... | collective-permute-start | bytes 221192 | tf_op jit(solution)/shard_map/ppermute | solution.py:629
  5.5 1.6 %inner_step.1 = (f32[5,4,16,1152]{3,2,1,0:T(8,128)S(1)}, f32[2,4,2,1152]{3,2,1,0:T(2,128)S(1)}, f32[3,4,2,1152]{3,2,1,0:T(2,128)S(1)}) custom-call(f32[4,24,128]{2,1,0:T(8,128)S(1)} %copy-done.6, f32[4,16,1152]{2,1,0:T(8,128)S(1)} %get-tuple-element.32.new_ref, f32[4,16,1152]{2,1,0:T(8,128)S(1)} %get-tuple-element.33.thick_ref, ...), custom_call_target="tpu_custom_call" | custom-call | flops 9584640 | bytes 4718592 | tf_op jit(solution)/shard_map/inner_step/pallas_call | solution.py:162
  7.4 1.9 %collective-permute-start.4 = (f32[3,4,2,1152]{3,2,1,0:T(2,128)S(1)}, f32[3,4,2,1152]{3,2,1,0:T(2,128)S(1)}, u32[]{:S(2)}, u32[]{:S(2)}) collective-permute-start(f32[3,4,2,1152]{3,2,1,0:T(2,128)S(1)} %get-tuple-element.42.refs_8_), channel_id=1, source_target_pairs={{0,2},{2,0},{1,3},{3,1},{4,6},{6,4},{5,7},{7,5},{8,10},{10,8},{9,1... | collective-permute-start | bytes 331784 | tf_op jit(solution)/shard_map/ppermute | solution.py:629
  9.8 0.7 %collective-permute-done.refs_1_.refs_3_ = f32[5,4,16,1152]{3,2,1,0:T(8,128)S(1)} collective-permute-done((f32[5,4,16,1152]{3,2,1,0:T(8,128)S(1)}, f32[5,4,16,1152]{3,2,1,0:T(8,128)S(1)}, u32[]{:S(2)}, u32[]{:S(2)}) %collective-permute-start) | collective-permute-done | bytes 1474592 | tf_op jit(solution)/shard_map/ppermute | solution.py:631
  10.5 1.4 %remap_parts.3.refs_0_ = f32[192,1152]{1,0:T(8,128)S(1)} custom-call(f32[16,8,128]{2,1,0:T(8,128)S(1)} %broadcast_in_dim.4.weight_ref, f32[5,4,16,1152]{3,2,1,0:T(8,128)S(1)} %get-tuple-element.37.refs_0_.refs_2_, f32[5,4,16,1152]{3,2,1,0:T(8,128)S(1)} %collective-permute-done.refs_1_.refs_3_, f32[5,4,16,1152]{3,2,1,0:T(8,128)S(1)} %get-tuple-element.37.refs_0_.refs_2_, ...), custom_call_target="tpu_custom_call" | custom-call | flops 7667712 | bytes 4423680 | tf_op jit(solution)/shard_map/remap_parts/pallas_call | solution.py:460
  12.0 1.8 %collective-permute-start.16 = (f32[192,1152]{1,0:T(8,128)S(1)}, f32[192,1152]{1,0:T(8,128)S(1)}, u32[]{:S(2)}, u32[]{:S(2)}) collective-permute-start(f32[192,1152]{1,0:T(8,128)S(1)} %remap_parts.3.refs_0_), channel_id=1, source_target_pairs={{0,2},{2,0},{1,3},{3,1},{4,6},{6,4},{5,7},{7,5},{8,10},{10,8},{9,1... | collective-permute-start | bytes 2654216 | tf_op jit(solution)/shard_map/ppermute | solution.py:629
  14.3 1.7 %edge_rows.1 = (f32[6,4,1,1152]{3,2,1,0:T(1,128)S(1)}, f32[8,4,1,1152]{3,2,1,0:T(1,128)S(1)}) custom-call(f32[4,16,1152]{2,1,0:T(8,128)} %thick_ref.1, f32[4,16,1152]{2,1,0:T(8,128)} %u_ref.1, f32[4,16,1152]{2,1,0:T(8,128)} %v_ref.1, f32[4,4,16,1152]{3,2,1,0:T(8,128)} %tracer_ref.1, f32[192,1152]{1,0:T(8,128)S(1)} %remap_parts.3.refs_0_, ...), custom_call_target="tpu_custom_call" | custom-call | flops 10000000000 | bytes 1000000000 | tf_op jit(solution)/shard_map/edge_rows/pallas_call | solution.py:607
  16.0 1.3 %collective-permute-start.6 = (f32[8,4,1,1152]{3,2,1,0:T(1,128)S(1)}, f32[8,4,1,1152]{3,2,1,0:T(1,128)S(1)}, u32[]{:S(2)}, u32[]{:S(2)}) collective-permute-start(f32[8,4,1,1152]{3,2,1,0:T(1,128)S(1)} %get-tuple-element.44), channel_id=1, source_target_pairs={{4,0},{8,4},{12,8},{5,1},{9,5},{13,9},{6,2},{10,6},{14,10},{7,3},{... | collective-permute-start | bytes 442376 | tf_op jit(solution)/shard_map/ppermute | solution.py:677
  17.3 4.6 %collective-permute-start.5 = (f32[6,4,1,1152]{3,2,1,0:T(1,128)S(1)}, f32[6,4,1,1152]{3,2,1,0:T(1,128)S(1)}, u32[]{:S(2)}, u32[]{:S(2)}) collective-permute-start(f32[6,4,1,1152]{3,2,1,0:T(1,128)S(1)} %get-tuple-element.43), channel_id=1, source_target_pairs={{0,4},{4,8},{8,12},{1,5},{5,9},{9,13},{2,6},{6,10},{10,14},{3,7},{... | collective-permute-start | bytes 331784 | tf_op jit(solution)/shard_map/ppermute | solution.py:676
  21.8 2.3 %collective-permute-done.5.up_ref = f32[6,4,1,1152]{3,2,1,0:T(1,128)S(1)} collective-permute-done((f32[6,4,1,1152]{3,2,1,0:T(1,128)S(1)}, f32[6,4,1,1152]{3,2,1,0:T(1,128)S(1)}, u32[]{:S(2)}, u32[]{:S(2)}) %collective-permute-start.5) | collective-permute-done | bytes 110624 | tf_op jit(solution)/shard_map/ppermute | solution.py:676
  24.3 3.6 %second_step.1 = (f32[1,4,16,1152]{3,2,1,0:T(8,128)S(1)}, f32[1,4,16,1152]{3,2,1,0:T(8,128)S(1)}, f32[7,4,2,1152]{3,2,1,0:T(2,128)S(1)}) custom-call(f32[4,24,128]{2,1,0:T(8,128)S(1)} %copy-done.6, f32[4,16,1152]{2,1,0:T(8,128)S(1)} %copy-done.1, f32[4,16,1152]{2,1,0:T(8,128)S(1)} %copy-done.2, f32[4,16,1152]{2,1,0:T(8,128)S(1)} %copy-done.3, ...), custom_call_target="tpu_custom_call" | custom-call | flops 503316480 | bytes 3538944 | tf_op jit(solution)/shard_map/second_step/pallas_call | solution.py:300
  28.5 1.7 %collective-permute-start.8 = (f32[7,4,2,1152]{3,2,1,0:T(2,128)S(1)}, f32[7,4,2,1152]{3,2,1,0:T(2,128)S(1)}, u32[]{:S(2)}, u32[]{:S(2)}) collective-permute-start(f32[7,4,2,1152]{3,2,1,0:T(2,128)S(1)} %get-tuple-element.45.refs_6_.refs_0_), channel_id=1, source_target_pairs={{0,2},{2,0},{1,3},{3,1},{4,6},{6,4},{5,7},{7,5},{8,10},{10,8},{9,1... | collective-permute-start | bytes 774152 | tf_op jit(solution)/shard_map/ppermute | solution.py:629
  30.2 1.3 %remap_parts.4 = (f32[4,4,16,1152]{3,2,1,0:T(8,128)S(1)}, f32[4,16,1152]{2,1,0:T(8,128)S(1)}) custom-call(f32[16,8,128]{2,1,0:T(8,128)S(1)} %broadcast_in_dim.4.weight_ref, f32[5,4,16,1152]{3,2,1,0:T(8,128)S(1)} %get-tuple-element.37.refs_0_.refs_2_, f32[5,4,16,1152]{3,2,1,0:T(8,128)S(1)} %collective-permute-done.refs_1_.refs_3_, ...), custom_call_target="tpu_custom_call" | custom-call | flops 7667712 | bytes 4423680 | tf_op jit(solution)/shard_map/remap_parts/pallas_call | solution.py:460
  31.5 3.0 %collective-permute-done.16.refs_9_.refs_0_ = f32[192,1152]{1,0:T(8,128)S(1)} collective-permute-done((f32[192,1152]{1,0:T(8,128)S(1)}, f32[192,1152]{1,0:T(8,128)S(1)}, u32[]{:S(2)}, u32[]{:S(2)}) %collective-permute-start.16) | collective-permute-done | bytes 884768 | tf_op jit(solution)/shard_map/ppermute | solution.py:629
  34.5 1.8 %remap_parts.5 = (f32[2,4,16,1152]{3,2,1,0:T(8,128)S(1)}, f32[112,1152]{1,0:T(8,128)S(1)}) custom-call(f32[16,8,128]{2,1,0:T(8,128)S(1)} %broadcast_in_dim.4.weight_ref, f32[5,4,16,1152]{3,2,1,0:T(8,128)S(1)} %get-tuple-element.37.refs_0_.refs_2_, f32[5,4,16,1152]{3,2,1,0:T(8,128)S(1)} %collective-permute-done.refs_1_.refs_3_, ...), custom_call_target="tpu_custom_call" | custom-call | flops 10616832 | bytes 3538944 | tf_op jit(solution)/shard_map/remap_parts/pallas_call | solution.py:460
  36.3 1.8 %collective-permute-start.17 = (f32[112,1152]{1,0:T(8,128)S(1)}, f32[112,1152]{1,0:T(8,128)S(1)}, u32[]{:S(2)}, u32[]{:S(2)}) collective-permute-start(f32[112,1152]{1,0:T(8,128)S(1)} %get-tuple-element.49.refs_12_), channel_id=1, source_target_pairs={{0,2},{2,0},{1,3},{3,1},{4,6},{6,4},{5,7},{7,5},{8,10},{10,8},{9,1... | collective-permute-start | bytes 1548296 | tf_op jit(solution)/shard_map/ppermute | solution.py:629
  38.2 1.9 %collective-permute-done.8.refs_2_ = f32[7,4,2,1152]{3,2,1,0:T(2,128)S(1)} collective-permute-done((f32[7,4,2,1152]{3,2,1,0:T(2,128)S(1)}, f32[7,4,2,1152]{3,2,1,0:T(2,128)S(1)}, u32[]{:S(2)}, u32[]{:S(2)}) %collective-permute-start.8) | collective-permute-done | bytes 258080 | tf_op jit(solution)/shard_map/ppermute | solution.py:629
  40.6 1.3 %collective-permute-done.10.refs_5_ = f32[2,4,2,1152]{3,2,1,0:T(2,128)S(1)} collective-permute-done((f32[2,4,2,1152]{3,2,1,0:T(2,128)S(1)}, f32[2,4,2,1152]{3,2,1,0:T(2,128)S(1)}, u32[]{:S(2)}, u32[]{:S(2)}) %collective-permute-start.10) | collective-permute-done | bytes 73760 | tf_op jit(solution)/shard_map/ppermute | solution.py:631
  42.4 0.9 %collective-permute-done.11.refs_7_ = f32[2,4,2,1152]{3,2,1,0:T(2,128)S(1)} collective-permute-done((f32[2,4,2,1152]{3,2,1,0:T(2,128)S(1)}, f32[2,4,2,1152]{3,2,1,0:T(2,128)S(1)}, u32[]{:S(2)}, u32[]{:S(2)}) %collective-permute-start.11) | collective-permute-done | bytes 73760 | tf_op jit(solution)/shard_map/ppermute | solution.py:631
  43.3 3.1 %remap_edges.1 = (f32[6,4,2,1152]{3,2,1,0:T(2,128)S(1)}, f32[4,2,1152]{2,1,0:T(2,128)S(1)}, f32[4,4,2,1152]{3,2,1,0:T(2,128)S(1)}) custom-call(f32[16,8,128]{2,1,0:T(8,128)S(1)} %broadcast_in_dim.4.weight_ref, f32[7,4,2,1152]{3,2,1,0:T(2,128)S(1)} %get-tuple-element.45.refs_6_.refs_0_, f32[7,4,2,1152]{3,2,1,0:T(2,128)S(1)} %collective-permute-done.7.refs_1_, ...), custom_call_target="tpu_custom_call" | custom-call | flops 5898240 | bytes 3096576 | tf_op jit(solution)/shard_map/remap_edges/pallas_call | solution.py:499
  46.4 1.4 %finish_tracers.1 = (f32[4,4,16,1152]{3,2,1,0:T(8,128)}, f32[4,16,1152]{2,1,0:T(8,128)}, f32[8,128]{1,0:T(8,128)S(1)}) custom-call(f32[4,4,16,1152]{3,2,1,0:T(8,128)S(1)} %get-tuple-element.46.refs_8_.own_ref, f32[4,4,2,1152]{3,2,1,0:T(2,128)S(1)} %get-tuple-element.50.near_ref, f32[6,4,2,1152]{3,2,1,0:T(2,128)S(1)} %get-tuple-element.51.edge_ref, ...), custom_call_target="tpu_custom_call" | custom-call | flops 589824 | bytes 3538944 | tf_op jit(solution)/shard_map/finish_tracers/pallas_call | solution.py:537
  47.8 2.9 %collective-permute-done.17.refs_0_ = f32[112,1152]{1,0:T(8,128)S(1)} collective-permute-done((f32[112,1152]{1,0:T(8,128)S(1)}, f32[112,1152]{1,0:T(8,128)S(1)}, u32[]{:S(2)}, u32[]{:S(2)}) %collective-permute-start.17) | collective-permute-done | bytes 516128 | tf_op jit(solution)/shard_map/ppermute | solution.py:629
  50.6 0.9 %finish_winds.1 = (f32[4,16,1152]{2,1,0:T(8,128)}, f32[4,16,1152]{2,1,0:T(8,128)}) custom-call(f32[2,4,16,1152]{3,2,1,0:T(8,128)S(1)} %get-tuple-element.55.own_ref, f32[6,4,2,1152]{3,2,1,0:T(2,128)S(1)} %get-tuple-element.51.edge_ref, f32[112,1152]{1,0:T(8,128)S(1)} %collective-permute-done.17.refs_0_, f32[8,128]{1,0:T(8,128)S(1)} %get-tuple-element.56.refs_1_), custom_call_target="tpu_custom_call" | custom-call | flops 147456 | bytes 1769472 | tf_op jit(solution)/shard_map/finish_winds/pallas_call | solution.py:567
  (43 shorter events, 2.9 us)
Async XLA Ops:
  2.5 6.9 %collective-permute-start.1 = (f32[16,1152]{1,0:T(8,128)S(1)}, f32[16,1152]{1,0:T(8,128)S(1)}, u32[]{:S(2)}, u32[]{:S(2)}) collective-permute-start(f32[16,1152]{1,0:T(8,128)S(1)} %get-tuple-element.38), channel_id=1, source_target_pairs={{0,2},{2,0},{1,3},{3,1},{4,6},{6,4},{5,7},{7,5},{8,10},{10,8},{9,1... | collective-permute-start | bytes 221192 | tf_op jit(solution)/shard_map/ppermute | solution.py:629
  5.5 4.3 %collective-permute-start.2 = (f32[16,1152]{1,0:T(8,128)S(1)}, f32[16,1152]{1,0:T(8,128)S(1)}, u32[]{:S(2)}, u32[]{:S(2)}) collective-permute-start(f32[16,1152]{1,0:T(8,128)S(1)} %get-tuple-element.38), channel_id=1, source_target_pairs={{0,3},{1,2},{2,1},{3,0},{4,7},{5,6},{6,5},{7,4},{8,11},{9,10},{10,... | collective-permute-start | bytes 221192 | tf_op jit(solution)/shard_map/ppermute | solution.py:637
  7.1 3.3 %collective-permute-start = (f32[5,4,16,1152]{3,2,1,0:T(8,128)S(1)}, f32[5,4,16,1152]{3,2,1,0:T(8,128)S(1)}, u32[]{:S(2)}, u32[]{:S(2)}) collective-permute-start(f32[5,4,16,1152]{3,2,1,0:T(8,128)S(1)} %get-tuple-element.37.refs_0_.refs_2_), channel_id=1, source_target_pairs={{0,1},{1,0},{2,3},{3,2},{4,5},{5,4},{6,7},{7,6},{8,9},{9,8},{10,11... | collective-permute-start | bytes 4423688 | tf_op jit(solution)/shard_map/ppermute | solution.py:631
  7.4 6.9 %collective-permute-start.4 = (f32[3,4,2,1152]{3,2,1,0:T(2,128)S(1)}, f32[3,4,2,1152]{3,2,1,0:T(2,128)S(1)}, u32[]{:S(2)}, u32[]{:S(2)}) collective-permute-start(f32[3,4,2,1152]{3,2,1,0:T(2,128)S(1)} %get-tuple-element.42.refs_8_), channel_id=1, source_target_pairs={{0,2},{2,0},{1,3},{3,1},{4,6},{6,4},{5,7},{7,5},{8,10},{10,8},{9,1... | collective-permute-start | bytes 331784 | tf_op jit(solution)/shard_map/ppermute | solution.py:629
  9.3 4.9 %collective-permute-start.3 = (f32[2,4,2,1152]{3,2,1,0:T(2,128)S(1)}, f32[2,4,2,1152]{3,2,1,0:T(2,128)S(1)}, u32[]{:S(2)}, u32[]{:S(2)}) collective-permute-start(f32[2,4,2,1152]{3,2,1,0:T(2,128)S(1)} %get-tuple-element.41.refs_4_), channel_id=1, source_target_pairs={{0,2},{2,0},{1,3},{3,1},{4,6},{6,4},{5,7},{7,5},{8,10},{10,8},{9,1... | collective-permute-start | bytes 221192 | tf_op jit(solution)/shard_map/ppermute | solution.py:629
  11.9 12.3 %copy-start = (f32[4,4,16,1152]{3,2,1,0:T(8,128)S(1)}, f32[4,4,16,1152]{3,2,1,0:T(8,128)}, u32[]{:S(2)}) copy-start(f32[4,4,16,1152]{3,2,1,0:T(8,128)} %tracer_ref.1) | copy-start | bytes 3538948
  12.0 12.3 %copy-start.1 = (f32[4,16,1152]{2,1,0:T(8,128)S(1)}, f32[4,16,1152]{2,1,0:T(8,128)}, u32[]{:S(2)}) copy-start(f32[4,16,1152]{2,1,0:T(8,128)} %thick_ref.1) | copy-start | bytes 884740
  12.0 12.3 %copy-start.2 = (f32[4,16,1152]{2,1,0:T(8,128)S(1)}, f32[4,16,1152]{2,1,0:T(8,128)}, u32[]{:S(2)}) copy-start(f32[4,16,1152]{2,1,0:T(8,128)} %u_ref.1) | copy-start | bytes 884740
  12.0 12.3 %copy-start.3 = (f32[4,16,1152]{2,1,0:T(8,128)S(1)}, f32[4,16,1152]{2,1,0:T(8,128)}, u32[]{:S(2)}) copy-start(f32[4,16,1152]{2,1,0:T(8,128)} %v_ref.1) | copy-start | bytes 884740
  12.0 12.3 %copy-start.4 = (bf16[5,256,256]{2,1,0:T(8,128)(2,1)S(1)}, bf16[5,256,256]{2,1,0:T(8,128)(2,1)}, u32[]{:S(2)}) copy-start(bf16[5,256,256]{2,1,0:T(8,128)(2,1)} %constant.7.clone.high_ref) | copy-start | bytes 1966084
  12.0 12.3 %copy-start.5 = (bf16[5,256,256]{2,1,0:T(8,128)(2,1)S(1)}, bf16[5,256,256]{2,1,0:T(8,128)(2,1)}, u32[]{:S(2)}) copy-start(bf16[5,256,256]{2,1,0:T(8,128)(2,1)} %constant.8.clone.low_ref) | copy-start | bytes 1966084
  12.0 22.5 %collective-permute-start.16 = (f32[192,1152]{1,0:T(8,128)S(1)}, f32[192,1152]{1,0:T(8,128)S(1)}, u32[]{:S(2)}, u32[]{:S(2)}) collective-permute-start(f32[192,1152]{1,0:T(8,128)S(1)} %remap_parts.3.refs_0_), channel_id=1, source_target_pairs={{0,2},{2,0},{1,3},{3,1},{4,6},{6,4},{5,7},{7,5},{8,10},{10,8},{9,1... | collective-permute-start | bytes 2654216 | tf_op jit(solution)/shard_map/ppermute | solution.py:629
  16.0 8.2 %collective-permute-start.6 = (f32[8,4,1,1152]{3,2,1,0:T(1,128)S(1)}, f32[8,4,1,1152]{3,2,1,0:T(1,128)S(1)}, u32[]{:S(2)}, u32[]{:S(2)}) collective-permute-start(f32[8,4,1,1152]{3,2,1,0:T(1,128)S(1)} %get-tuple-element.44), channel_id=1, source_target_pairs={{4,0},{8,4},{12,8},{5,1},{9,5},{13,9},{6,2},{10,6},{14,10},{7,3},{... | collective-permute-start | bytes 442376 | tf_op jit(solution)/shard_map/ppermute | solution.py:677
  17.3 6.9 %collective-permute-start.5 = (f32[6,4,1,1152]{3,2,1,0:T(1,128)S(1)}, f32[6,4,1,1152]{3,2,1,0:T(1,128)S(1)}, u32[]{:S(2)}, u32[]{:S(2)}) collective-permute-start(f32[6,4,1,1152]{3,2,1,0:T(1,128)S(1)} %get-tuple-element.43), channel_id=1, source_target_pairs={{0,4},{4,8},{8,12},{1,5},{5,9},{9,13},{2,6},{6,10},{10,14},{3,7},{... | collective-permute-start | bytes 331784 | tf_op jit(solution)/shard_map/ppermute | solution.py:676
  27.9 3.6 %collective-permute-start.14 = (f32[1,4,16,1152]{3,2,1,0:T(8,128)S(1)}, f32[1,4,16,1152]{3,2,1,0:T(8,128)S(1)}, u32[]{:S(2)}, u32[]{:S(2)}) collective-permute-start(f32[1,4,16,1152]{3,2,1,0:T(8,128)S(1)} %get-tuple-element.47.refs_2_), channel_id=1, source_target_pairs={{0,1},{1,0},{2,3},{3,2},{4,5},{5,4},{6,7},{7,6},{8,9},{9,8},{10,11... | collective-permute-start | bytes 884744 | tf_op jit(solution)/shard_map/ppermute | solution.py:631
  28.0 3.5 %collective-permute-start.15 = (f32[1,4,16,1152]{3,2,1,0:T(8,128)S(1)}, f32[1,4,16,1152]{3,2,1,0:T(8,128)S(1)}, u32[]{:S(2)}, u32[]{:S(2)}) collective-permute-start(f32[1,4,16,1152]{3,2,1,0:T(8,128)S(1)} %get-tuple-element.48.refs_4_), channel_id=1, source_target_pairs={{0,1},{1,0},{2,3},{3,2},{4,5},{5,4},{6,7},{7,6},{8,9},{9,8},{10,11... | collective-permute-start | bytes 884744 | tf_op jit(solution)/shard_map/ppermute | solution.py:631
  28.5 11.6 %collective-permute-start.8 = (f32[7,4,2,1152]{3,2,1,0:T(2,128)S(1)}, f32[7,4,2,1152]{3,2,1,0:T(2,128)S(1)}, u32[]{:S(2)}, u32[]{:S(2)}) collective-permute-start(f32[7,4,2,1152]{3,2,1,0:T(2,128)S(1)} %get-tuple-element.45.refs_6_.refs_0_), channel_id=1, source_target_pairs={{0,2},{2,0},{1,3},{3,1},{4,6},{6,4},{5,7},{7,5},{8,10},{10,8},{9,1... | collective-permute-start | bytes 774152 | tf_op jit(solution)/shard_map/ppermute | solution.py:629
  36.3 14.3 %collective-permute-start.17 = (f32[112,1152]{1,0:T(8,128)S(1)}, f32[112,1152]{1,0:T(8,128)S(1)}, u32[]{:S(2)}, u32[]{:S(2)}) collective-permute-start(f32[112,1152]{1,0:T(8,128)S(1)} %get-tuple-element.49.refs_12_), channel_id=1, source_target_pairs={{0,2},{2,0},{1,3},{3,1},{4,6},{6,4},{5,7},{7,5},{8,10},{10,8},{9,1... | collective-permute-start | bytes 1548296 | tf_op jit(solution)/shard_map/ppermute | solution.py:629
  38.2 5.1 %collective-permute-start.7 = (f32[7,4,2,1152]{3,2,1,0:T(2,128)S(1)}, f32[7,4,2,1152]{3,2,1,0:T(2,128)S(1)}, u32[]{:S(2)}, u32[]{:S(2)}) collective-permute-start(f32[7,4,2,1152]{3,2,1,0:T(2,128)S(1)} %get-tuple-element.45.refs_6_.refs_0_), channel_id=1, source_target_pairs={{0,1},{1,0},{2,3},{3,2},{4,5},{5,4},{6,7},{7,6},{8,9},{9,8},{10,11... | collective-permute-start | bytes 774152 | tf_op jit(solution)/shard_map/ppermute | solution.py:631
  40.1 3.2 %collective-permute-start.9 = (f32[7,4,2,1152]{3,2,1,0:T(2,128)S(1)}, f32[7,4,2,1152]{3,2,1,0:T(2,128)S(1)}, u32[]{:S(2)}, u32[]{:S(2)}) collective-permute-start(f32[7,4,2,1152]{3,2,1,0:T(2,128)S(1)} %collective-permute-done.8.refs_2_), channel_id=1, source_target_pairs={{0,1},{1,0},{2,3},{3,2},{4,5},{5,4},{6,7},{7,6},{8,9},{9,8},{10,11... | collective-permute-start | bytes 774152 | tf_op jit(solution)/shard_map/ppermute | solution.py:631
  40.1 1.9 %collective-permute-start.12 = (f32[3,4,2,1152]{3,2,1,0:T(2,128)S(1)}, f32[3,4,2,1152]{3,2,1,0:T(2,128)S(1)}, u32[]{:S(2)}, u32[]{:S(2)}) collective-permute-start(f32[3,4,2,1152]{3,2,1,0:T(2,128)S(1)} %get-tuple-element.42.refs_8_), channel_id=1, source_target_pairs={{0,1},{1,0},{2,3},{3,2},{4,5},{5,4},{6,7},{7,6},{8,9},{9,8},{10,11... | collective-permute-start | bytes 331784 | tf_op jit(solution)/shard_map/ppermute | solution.py:631
  40.6 1.3 %collective-permute-start.10 = (f32[2,4,2,1152]{3,2,1,0:T(2,128)S(1)}, f32[2,4,2,1152]{3,2,1,0:T(2,128)S(1)}, u32[]{:S(2)}, u32[]{:S(2)}) collective-permute-start(f32[2,4,2,1152]{3,2,1,0:T(2,128)S(1)} %get-tuple-element.41.refs_4_), channel_id=1, source_target_pairs={{0,1},{1,0},{2,3},{3,2},{4,5},{5,4},{6,7},{7,6},{8,9},{9,8},{10,11... | collective-permute-start | bytes 221192 | tf_op jit(solution)/shard_map/ppermute | solution.py:631
  41.9 1.4 %collective-permute-start.13 = (f32[3,4,2,1152]{3,2,1,0:T(2,128)S(1)}, f32[3,4,2,1152]{3,2,1,0:T(2,128)S(1)}, u32[]{:S(2)}, u32[]{:S(2)}) collective-permute-start(f32[3,4,2,1152]{3,2,1,0:T(2,128)S(1)} %collective-permute-done.4.refs_2_.refs_10_), channel_id=1, source_target_pairs={{0,1},{1,0},{2,3},{3,2},{4,5},{5,4},{6,7},{7,6},{8,9},{9,8},{10,11... | collective-permute-start | bytes 331784 | tf_op jit(solution)/shard_map/ppermute | solution.py:631
  42.0 1.3 %collective-permute-start.11 = (f32[2,4,2,1152]{3,2,1,0:T(2,128)S(1)}, f32[2,4,2,1152]{3,2,1,0:T(2,128)S(1)}, u32[]{:S(2)}, u32[]{:S(2)}) collective-permute-start(f32[2,4,2,1152]{3,2,1,0:T(2,128)S(1)} %collective-permute-done.3.refs_1_.refs_6_), channel_id=1, source_target_pairs={{0,1},{1,0},{2,3},{3,2},{4,5},{5,4},{6,7},{7,6},{8,9},{9,8},{10,11... | collective-permute-start | bytes 221192 | tf_op jit(solution)/shard_map/ppermute | solution.py:631
  (3 other events, 18.2 us)

commit v11 on v10

--- a/solution.py
+++ b/solution.py
@@ -79,7 +79,7 @@
 
 
 def first_kernel(table_hbm, thick_hbm, u_hbm, v_hbm, tracer_hbm, *refs):
-    new_ref, sum_ref, thick_ref, u_ref, v_ref, tracer_ref, geo_ref, sems = refs
+    new_ref, sum_ref, near_ref, thick_ref, u_ref, v_ref, tracer_ref, geo_ref, sems = refs
     L, rows, _ = thick_ref.shape
     table_copy = pltpu.make_async_copy(table_hbm.at[lax.axis_index("lat")], geo_ref, sems.at[3, 0])
     table_copy.start()
@@ -104,6 +104,8 @@
         east, north, _ = fluxes(geo, thick, u, v, None, None, None)
         new = thick - (east - west_of(east)) - (north - south_of(north, None)) * geo[0:rows, 2:3]
         new_ref[k] = new
+        near_ref[0, k, 0:1] = new[1:2]
+        near_ref[0, k, 1:2] = new[rows - 2 : rows - 1]
         sum_ref[...] += new
         return carry
 
@@ -115,7 +117,7 @@
     L, R, N = thickness.shape
     arguments = (thickness, wind_u, wind_v, tracers)
     operands = [pltpu.with_memory_space_constraint(a, pltpu.HBM) for a in (table, *arguments)]
-    shapes = [(L, R, N), (R, N)] + [a.shape for a in arguments]
+    shapes = [(L, R, N), (R, N), (1, L, 2, N)] + [a.shape for a in arguments]
     return pl.pallas_call(
         first_kernel,
         in_specs=after(operands),
@@ -137,19 +139,17 @@
         thick, u, v, new = thick_ref[k], u_ref[k], v_ref[k], new_ref[k]
         east, north, _ = fluxes(geo, thick, u, v, None, None, None)
 
-        def store(field, value):
-            out_ref[field, k] = value
-            ref, at = (near_ref, field) if field < 2 else (near_rest_ref, field - 2)
-            ref[at, k, 0:1] = value[1:2]
-            ref[at, k, 1:2] = value[rows - 2 : rows - 1]
-
-        store(0, new)
+        out_ref[0, k] = new
         scale = 1.0 / new
         for c in range(T):
             change = tracer_change(
                 tracer_ref[c, k], None, None, thick, u, v, None, east, north, None, inverse
             )
-            store(1 + c, change * scale)
+            value = change * scale
+            out_ref[1 + c, k] = value
+            ref, at = (near_ref, c) if c < T // 2 else (near_rest_ref, c - T // 2)
+            ref[at, k, 0:1] = value[1:2]
+            ref[at, k, 1:2] = value[rows - 2 : rows - 1]
         return carry
 
     lax.fori_loop(0, L, level, 0)
@@ -163,7 +163,7 @@
         inner_kernel,
         in_specs=[VMEM] * 6,
         out_specs=[VMEM] * 3,
-        out_shape=[shape(1 + T, R), shape(2, 2), shape(T - 1, 2)],
+        out_shape=[shape(1 + T, R), shape(T // 2, 2), shape(T - T // 2, 2)],
         compiler_params=params(),
         cost_estimate=cost(130 * L * R * N, 4 * L * R * N * (8 + 2 * T)),
         name="inner_step",
@@ -331,16 +331,16 @@
     mass_ref[...] = others_mass
 
 
-def other_chips(counts, others):
+def other_chips(counts, others, wait):
     return pl.pallas_call(
         functools.partial(mass_kernel, *counts),
-        in_specs=[VMEM] * len(others),
+        in_specs=[VMEM] * len(others) + after(wait),
         out_specs=[VMEM] * 2,
         out_shape=[jax.ShapeDtypeStruct(others[0].shape, jnp.float32)] * 2,
         compiler_params=params(),
         cost_estimate=cost(1e11, 1e9),
         name="other_chips",
-    )(*others)
+    )(*others, *wait)
 
 
 def add_weights(weight_ref, sum_ref):
@@ -472,7 +472,8 @@
 def remap_edge_kernel(counts, near_fields, weight_ref, *refs):
     *refs, sum_ref = refs
     G = counts[0] * counts[1]
-    edge_refs, near_refs, rest_refs = refs[:G], refs[G : 2 * G], refs[2 * G : 3 * G]
+    edge_refs, near_refs = refs[:G], refs[G : 2 * G]
+    bundles = (refs[2 * G : 3 * G], refs[3 * G : 4 * G])
     edge_out_ref, thick_out_ref, near_out_ref = refs[-3:]
 
     def store_edge(s, i, at, columns, target, means):
@@ -486,16 +487,15 @@
 
     fields = [[(ref, f) for ref in edge_refs] for f in range(1, edge_refs[0].shape[0])]
     remap_rows(weight_ref, sum_ref, counts, (0,), edge_refs, fields, [], store_edge)
-    bundles = (near_refs, rest_refs)
     fields = [[(ref, index) for ref in bundles[which]] for which, index in near_fields]
     remap_rows(weight_ref, sum_ref, counts, (0,), near_refs, fields, [], store_near)
 
 
-def remap_edges(counts, weights, edges, near, near_rest, wait=()):
+def remap_edges(counts, weights, edges, near_new, near, near_rest, wait=()):
     F, L, R, N = edges[0].shape
     T = F - 3
-    near_fields = tuple((0, 1) if f == 0 else (1, f - 1) for f in range(T))
-    operands = [*edges, *near, *near_rest]
+    near_fields = tuple((0, f) if f < T // 2 else (1, f - T // 2) for f in range(T))
+    operands = [*edges, *near_new, *near, *near_rest]
     return pl.pallas_call(
         functools.partial(remap_edge_kernel, counts, near_fields),
         in_specs=[VMEM] * (1 + len(operands)) + after(wait),
@@ -550,25 +550,32 @@
 
 
 def finish_winds_kernel(count, own_ref, edge_ref, *refs):
-    arrived_refs, out_refs = refs[:count], refs[-2:]
-    _, L, R, N = own_ref.shape
+    arrived_refs, (*out_refs, result_ref, sems) = refs[:count], refs[len(refs) - 4 :]
+    _, L, R, _ = own_ref.shape
+    copies = []
     for f, out_ref in enumerate(out_refs):
         for i in range(L):
             start = (f * L + i) * (R - 2)
             total = own_ref[f, i, 1 : R - 1]
             for ref in arrived_refs:
                 total = total + ref[start : start + R - 2]
-            out_ref[i, 1 : R - 1] = total
-            out_ref[i, 0:1] = edge_ref[f, i, 0:1]
-            out_ref[i, R - 1 : R] = edge_ref[f, i, 1:2]
+            result_ref[f, i, 1 : R - 1] = total
+            result_ref[f, i, 0:1] = edge_ref[f, i, 0:1]
+            result_ref[f, i, R - 1 : R] = edge_ref[f, i, 1:2]
+            copies.append(pltpu.make_async_copy(result_ref.at[f, i], out_ref.at[i], sems.at[f, i]))
+            copies[-1].start()
+    for copy in copies:
+        copy.wait()
 
 
 def finish_winds(own, arrived, edge, wait):
+    F, L = own.shape[:2]
     return pl.pallas_call(
         functools.partial(finish_winds_kernel, len(arrived)),
         in_specs=[VMEM] * (2 + len(arrived)) + after(wait),
-        out_specs=[VMEM] * 2,
-        out_shape=[jax.ShapeDtypeStruct(own.shape[1:], jnp.float32)] * 2,
+        out_specs=[pl.BlockSpec(memory_space=pl.ANY)] * F,
+        out_shape=[jax.ShapeDtypeStruct(own.shape[1:], jnp.float32)] * F,
+        scratch_shapes=[pltpu.VMEM(own.shape, jnp.float32), pltpu.SemaphoreType.DMA((F, L))],
         compiler_params=params(),
         cost_estimate=cost(own.size, 12 * own.size),
         name="finish_winds",
@@ -659,13 +666,14 @@
 
     remap = functools.partial(remap_parts, (C, S), weights)
 
-    new, own_sum, *arguments = first_step(table, thickness, wind_u, wind_v, tracers)
+    new, own_sum, near_new, *arguments = first_step(table, thickness, wind_u, wind_v, tracers)
     others = [send(own_sum, s=s, t=t) for s in away for t in range(S)]
+    near_new = [near_new] + [send(near_new, s=s, t=0) for s in away]
     inner, near, near_rest = inner_step(table, new, *arguments)
     group = with_others_of_chip(inner)
     near = [near] + [send(near, s=s, t=0) for s in away]
     near_rest = [near_rest] + [send(near_rest, s=s, t=0) for s in away]
-    others = other_chips((C, S), others)
+    others = other_chips((C, S), others, near_new[1:2])
     tracer_fields = [(0, 1 + c) for c in range(T)]
     away_parts = remap(group, [group], others, tracer_fields, away, 2)
     arrived = sent(away_parts)
@@ -683,11 +691,11 @@
         group, winds, others, [(0, 0), (1, 0)], range(C), 1, wait=[tracers_own, *arrived[:1]]
     )
     winds_arrived = sent(winds_away)
-    near, near_rest, edges = (
-        [a for own in sources for a in with_others_of_chip(own)] for sources in (near, near_rest, edges)
+    near_new, near, near_rest, edges = (
+        [a for own in sources for a in with_others_of_chip(own)] for sources in (near_new, near, near_rest, edges)
     )
     edge_out, thick_edge, near_out = remap_edges(
-        (C, S), weights, edges, near, near_rest, wait=winds_away[:1]
+        (C, S), weights, edges, near_new, near, near_rest, wait=winds_away[:1]
     )
 
     tracers_out, thickness_out, token = finish_tracers(

time: 51.8 us -> 53.2 us (1.027)
  waiting for transfers between devices: 13.7 us -> 16.2 us
  starting transfers between devices: 18.1 us -> 17.2 us
    ppermute x6 -> x7, waiting for transfers between devices: 8.17 us -> 11 us  [shifted(): lax.ppermute(value, 'lev', [(i, (i + s) % lev_count) for i in range(lev_c...]
    ppermute x6 -> x7, starting transfers between devices: 10.4 us -> 8.51 us  [shifted(): lax.ppermute(value, 'lev', [(i, (i + s) % lev_count) for i in range(lev_c...]
    ppermute x9 -> x11, starting transfers between devices: 1.85 us -> 2.8 us  [shifted(): lax.ppermute(value, 'sub', [(i, (i + t) % sub_count) for i in range(sub_c...]
    ppermute x9 -> x11, waiting for transfers between devices: 2.86 us -> 2.87 us  [shifted(): lax.ppermute(value, 'sub', [(i, (i + t) % sub_count) for i in range(sub_c...]
  transfers between devices with their start and end apart: 18 -> 21, of which waited for: 9 -> 12; matrix products, arithmetic and copies ran while one was open for 0% -> 0% of each run, Pallas kernels for 31% -> 30%
where the time goes in v11:
time: 53.2 us; the launch traced here: 53 us
  Pallas kernels  18.6 us (35%)
  starting transfers between devices  17.2 us (32%)
  waiting for transfers between devices  16.2 us (30%)
  between operations  0.84 us (2%)
    ppermute x7, waiting for transfers between devices, shifted(): lax.ppermute(value, 'lev', [(i, (i + s) % lev_count) for i in range(lev_c...  11 us
    ppermute x7, starting transfers between devices, shifted(): lax.ppermute(value, 'lev', [(i, (i + s) % lev_count) for i in range(lev_c...  8.51 us
    ppermute x1, starting transfers between devices, per_device(): up = lax.ppermute(last, 'lat', northward)  4.55 us
    pallas_call x3, Pallas kernels, remap_parts(): pl.pallas_call(functools.partial(remap_kernel, counts, tuple(steps), tupl...  4.46 us
    pallas_call x1, Pallas kernels, second_step(): pl.pallas_call(functools.partial(second_kernel, lat_rows), grid=(L,), in_...  3.62 us
    pallas_call x1, Pallas kernels, remap_edges(): pl.pallas_call(functools.partial(remap_edge_kernel, counts, near_fields),...  3.06 us
    ppermute x11, waiting for transfers between devices, shifted(): lax.ppermute(value, 'sub', [(i, (i + t) % sub_count) for i in range(sub_c...  2.87 us
    ppermute x11, starting transfers between devices, shifted(): lax.ppermute(value, 'sub', [(i, (i + t) % sub_count) for i in range(sub_c...  2.8 us
  transfers between devices with their start and end apart: 21, of which 12 were waited for; matrix products, arithmetic and copies ran while one was open for 0% of the time, Pallas kernels for 30%

profile of v11, /device:TPU:0, one launch (start us, length us, event | category | flops | bytes accessed | tf_op | source)
XLA Modules:
  0.0 53.0 jit_solution(6562860460004815958)
XLA Ops:
  0.6 1.9 %first_step.1 = (f32[4,16,1152]{2,1,0:T(8,128)S(1)}, f32[16,1152]{1,0:T(8,128)S(1)}, f32[1,4,2,1152]{3,2,1,0:T(2,128)S(1)}, f32[4,16,1152]{2,1,0:T(8,128)S(1)}, ...) custom-call(f32[4,24,128]{2,1,0:T(8,128)} %constant.6.clone.table_hbm.table_ref, ...), custom_call_target="tpu_custom_call" | custom-call | flops 2949120 | bytes 4423680 | tf_op jit(solution)/shard_map/first_step/pallas_call | solution.py:121
  2.5 3.0 %collective-permute-start.1 = (f32[16,1152]{1,0:T(8,128)S(1)}, f32[16,1152]{1,0:T(8,128)S(1)}, u32[]{:S(2)}, u32[]{:S(2)}) collective-permute-start(f32[16,1152]{1,0:T(8,128)S(1)} %get-tuple-element.39), channel_id=1, source_target_pairs={{0,2},{2,0},{1,3},{3,1},{4,6},{6,4},{5,7},{7,5},{8,10},{10,8},{9,1... | collective-permute-start | bytes 221192 | tf_op jit(solution)/shard_map/ppermute | solution.py:636
  5.5 1.2 %collective-permute-start.3 = (f32[1,4,2,1152]{3,2,1,0:T(2,128)S(1)}, f32[1,4,2,1152]{3,2,1,0:T(2,128)S(1)}, u32[]{:S(2)}, u32[]{:S(2)}) collective-permute-start(f32[1,4,2,1152]{3,2,1,0:T(2,128)S(1)} %get-tuple-element.40.refs_4_), channel_id=1, source_target_pairs={{0,2},{2,0},{1,3},{3,1},{4,6},{6,4},{5,7},{7,5},{8,10},{10,8},{9,1... | collective-permute-start | bytes 110600 | tf_op jit(solution)/shard_map/ppermute | solution.py:636
  6.7 1.6 %inner_step.1 = (f32[5,4,16,1152]{3,2,1,0:T(8,128)S(1)}, f32[2,4,2,1152]{3,2,1,0:T(2,128)S(1)}, f32[2,4,2,1152]{3,2,1,0:T(2,128)S(1)}) custom-call(f32[4,24,128]{2,1,0:T(8,128)S(1)} %copy-done.6, f32[4,16,1152]{2,1,0:T(8,128)S(1)} %get-tuple-element.33.new_ref, f32[4,16,1152]{2,1,0:T(8,128)S(1)} %get-tuple-element.34.thick_ref, ...), custom_call_target="tpu_custom_call" | custom-call | flops 9584640 | bytes 4718592 | tf_op jit(solution)/shard_map/inner_step/pallas_call | solution.py:162
  9.4 1.0 %collective-permute-done.3.refs_2_.refs_6_ = f32[1,4,2,1152]{3,2,1,0:T(2,128)S(1)} collective-permute-done((f32[1,4,2,1152]{3,2,1,0:T(2,128)S(1)}, f32[1,4,2,1152]{3,2,1,0:T(2,128)S(1)}, u32[]{:S(2)}, u32[]{:S(2)}) %collective-permute-start.3) | collective-permute-done | bytes 36896 | tf_op jit(solution)/shard_map/ppermute | solution.py:636
  10.3 1.6 %collective-permute-start.5 = (f32[2,4,2,1152]{3,2,1,0:T(2,128)S(1)}, f32[2,4,2,1152]{3,2,1,0:T(2,128)S(1)}, u32[]{:S(2)}, u32[]{:S(2)}) collective-permute-start(f32[2,4,2,1152]{3,2,1,0:T(2,128)S(1)} %get-tuple-element.44.refs_12_), channel_id=1, source_target_pairs={{0,2},{2,0},{1,3},{3,1},{4,6},{6,4},{5,7},{7,5},{8,10},{10,8},{9,1... | collective-permute-start | bytes 221192 | tf_op jit(solution)/shard_map/ppermute | solution.py:636
  12.1 1.4 %remap_parts.3.refs_0_ = f32[192,1152]{1,0:T(8,128)S(1)} custom-call(f32[16,8,128]{2,1,0:T(8,128)S(1)} %broadcast_in_dim.4.weight_ref, f32[5,4,16,1152]{3,2,1,0:T(8,128)S(1)} %get-tuple-element.38.refs_0_.refs_2_, f32[5,4,16,1152]{3,2,1,0:T(8,128)S(1)} %collective-permute-done.refs_1_.refs_3_, f32[5,4,16,1152]{3,2,1,0:T(8,128)S(1)} %get-tuple-element.38.refs_0_.refs_2_, ...), custom_call_target="tpu_custom_call" | custom-call | flops 7667712 | bytes 4423680 | tf_op jit(solution)/shard_map/remap_parts/pallas_call | solution.py:460
  14.2 0.9 %collective-permute-done.5.refs_2_.refs_14_ = f32[2,4,2,1152]{3,2,1,0:T(2,128)S(1)} collective-permute-done((f32[2,4,2,1152]{3,2,1,0:T(2,128)S(1)}, f32[2,4,2,1152]{3,2,1,0:T(2,128)S(1)}, u32[]{:S(2)}, u32[]{:S(2)}) %collective-permute-start.5) | collective-permute-done | bytes 73760 | tf_op jit(solution)/shard_map/ppermute | solution.py:636
  15.0 1.7 %edge_rows.1 = (f32[6,4,1,1152]{3,2,1,0:T(1,128)S(1)}, f32[8,4,1,1152]{3,2,1,0:T(1,128)S(1)}) custom-call(f32[4,16,1152]{2,1,0:T(8,128)} %thick_ref.1, f32[4,16,1152]{2,1,0:T(8,128)} %u_ref.1, f32[4,16,1152]{2,1,0:T(8,128)} %v_ref.1, f32[4,4,16,1152]{3,2,1,0:T(8,128)} %tracer_ref.1, f32[192,1152]{1,0:T(8,128)S(1)} %remap_parts.3.refs_0_, ...), custom_call_target="tpu_custom_call" | custom-call | flops 10000000000 | bytes 1000000000 | tf_op jit(solution)/shard_map/edge_rows/pallas_call | solution.py:614
  16.8 1.3 %collective-permute-start.7 = (f32[8,4,1,1152]{3,2,1,0:T(1,128)S(1)}, f32[8,4,1,1152]{3,2,1,0:T(1,128)S(1)}, u32[]{:S(2)}, u32[]{:S(2)}) collective-permute-start(f32[8,4,1,1152]{3,2,1,0:T(1,128)S(1)} %get-tuple-element.46), channel_id=1, source_target_pairs={{4,0},{8,4},{12,8},{5,1},{9,5},{13,9},{6,2},{10,6},{14,10},{7,3},{... | collective-permute-start | bytes 442376 | tf_op jit(solution)/shard_map/ppermute | solution.py:685
  18.1 4.6 %collective-permute-start.6 = (f32[6,4,1,1152]{3,2,1,0:T(1,128)S(1)}, f32[6,4,1,1152]{3,2,1,0:T(1,128)S(1)}, u32[]{:S(2)}, u32[]{:S(2)}) collective-permute-start(f32[6,4,1,1152]{3,2,1,0:T(1,128)S(1)} %get-tuple-element.45), channel_id=1, source_target_pairs={{0,4},{4,8},{8,12},{1,5},{5,9},{9,13},{2,6},{6,10},{10,14},{3,7},{... | collective-permute-start | bytes 331784 | tf_op jit(solution)/shard_map/ppermute | solution.py:684
  22.6 2.3 %collective-permute-done.6.up_ref = f32[6,4,1,1152]{3,2,1,0:T(1,128)S(1)} collective-permute-done((f32[6,4,1,1152]{3,2,1,0:T(1,128)S(1)}, f32[6,4,1,1152]{3,2,1,0:T(1,128)S(1)}, u32[]{:S(2)}, u32[]{:S(2)}) %collective-permute-start.6) | collective-permute-done | bytes 110624 | tf_op jit(solution)/shard_map/ppermute | solution.py:684
  25.0 3.6 %second_step.1 = (f32[1,4,16,1152]{3,2,1,0:T(8,128)S(1)}, f32[1,4,16,1152]{3,2,1,0:T(8,128)S(1)}, f32[7,4,2,1152]{3,2,1,0:T(2,128)S(1)}) custom-call(f32[4,24,128]{2,1,0:T(8,128)S(1)} %copy-done.6, f32[4,16,1152]{2,1,0:T(8,128)S(1)} %copy-done.1, f32[4,16,1152]{2,1,0:T(8,128)S(1)} %copy-done.2, f32[4,16,1152]{2,1,0:T(8,128)S(1)} %copy-done.3, ...), custom_call_target="tpu_custom_call" | custom-call | flops 503316480 | bytes 3538944 | tf_op jit(solution)/shard_map/second_step/pallas_call | solution.py:300
  29.2 1.2 %collective-permute-start.9 = (f32[7,4,2,1152]{3,2,1,0:T(2,128)S(1)}, f32[7,4,2,1152]{3,2,1,0:T(2,128)S(1)}, u32[]{:S(2)}, u32[]{:S(2)}) collective-permute-start(f32[7,4,2,1152]{3,2,1,0:T(2,128)S(1)} %get-tuple-element.47.refs_6_.refs_0_), channel_id=1, source_target_pairs={{0,2},{2,0},{1,3},{3,1},{4,6},{6,4},{5,7},{7,5},{8,10},{10,8},{9,1... | collective-permute-start | bytes 774152 | tf_op jit(solution)/shard_map/ppermute | solution.py:636
  30.4 1.3 %remap_parts.4 = (f32[4,4,16,1152]{3,2,1,0:T(8,128)S(1)}, f32[4,16,1152]{2,1,0:T(8,128)S(1)}) custom-call(f32[16,8,128]{2,1,0:T(8,128)S(1)} %broadcast_in_dim.4.weight_ref, f32[5,4,16,1152]{3,2,1,0:T(8,128)S(1)} %get-tuple-element.38.refs_0_.refs_2_, f32[5,4,16,1152]{3,2,1,0:T(8,128)S(1)} %collective-permute-done.refs_1_.refs_3_, ...), custom_call_target="tpu_custom_call" | custom-call | flops 7667712 | bytes 4423680 | tf_op jit(solution)/shard_map/remap_parts/pallas_call | solution.py:460
  31.8 4.3 %collective-permute-done.19.refs_9_.refs_0_ = f32[192,1152]{1,0:T(8,128)S(1)} collective-permute-done((f32[192,1152]{1,0:T(8,128)S(1)}, f32[192,1152]{1,0:T(8,128)S(1)}, u32[]{:S(2)}, u32[]{:S(2)}) %collective-permute-start.19) | collective-permute-done | bytes 884768 | tf_op jit(solution)/shard_map/ppermute | solution.py:636
  36.1 1.8 %remap_parts.5 = (f32[2,4,16,1152]{3,2,1,0:T(8,128)S(1)}, f32[112,1152]{1,0:T(8,128)S(1)}) custom-call(f32[16,8,128]{2,1,0:T(8,128)S(1)} %broadcast_in_dim.4.weight_ref, f32[5,4,16,1152]{3,2,1,0:T(8,128)S(1)} %get-tuple-element.38.refs_0_.refs_2_, f32[5,4,16,1152]{3,2,1,0:T(8,128)S(1)} %collective-permute-done.refs_1_.refs_3_, ...), custom_call_target="tpu_custom_call" | custom-call | flops 10616832 | bytes 3538944 | tf_op jit(solution)/shard_map/remap_parts/pallas_call | solution.py:460
  38.5 3.1 %collective-permute-done.9.refs_2_ = f32[7,4,2,1152]{3,2,1,0:T(2,128)S(1)} collective-permute-done((f32[7,4,2,1152]{3,2,1,0:T(2,128)S(1)}, f32[7,4,2,1152]{3,2,1,0:T(2,128)S(1)}, u32[]{:S(2)}, u32[]{:S(2)}) %collective-permute-start.9) | collective-permute-done | bytes 258080 | tf_op jit(solution)/shard_map/ppermute | solution.py:636
  42.1 1.1 %collective-permute-done.11.refs_5_ = f32[1,4,2,1152]{3,2,1,0:T(2,128)S(1)} collective-permute-done((f32[1,4,2,1152]{3,2,1,0:T(2,128)S(1)}, f32[1,4,2,1152]{3,2,1,0:T(2,128)S(1)}, u32[]{:S(2)}, u32[]{:S(2)}) %collective-permute-start.11) | collective-permute-done | bytes 36896 | tf_op jit(solution)/shard_map/ppermute | solution.py:638
  43.7 0.8 %collective-permute-done.15.refs_13_ = f32[2,4,2,1152]{3,2,1,0:T(2,128)S(1)} collective-permute-done((f32[2,4,2,1152]{3,2,1,0:T(2,128)S(1)}, f32[2,4,2,1152]{3,2,1,0:T(2,128)S(1)}, u32[]{:S(2)}, u32[]{:S(2)}) %collective-permute-start.15) | collective-permute-done | bytes 73760 | tf_op jit(solution)/shard_map/ppermute | solution.py:638
  45.9 3.1 %remap_edges.1 = (f32[6,4,2,1152]{3,2,1,0:T(2,128)S(1)}, f32[4,2,1152]{2,1,0:T(2,128)S(1)}, f32[4,4,2,1152]{3,2,1,0:T(2,128)S(1)}) custom-call(f32[16,8,128]{2,1,0:T(8,128)S(1)} %broadcast_in_dim.4.weight_ref, f32[7,4,2,1152]{3,2,1,0:T(2,128)S(1)} %get-tuple-element.47.refs_6_.refs_0_, f32[7,4,2,1152]{3,2,1,0:T(2,128)S(1)} %collective-permute-done.8.refs_1_, ...), custom_call_target="tpu_custom_call" | custom-call | flops 5898240 | bytes 4128768 | tf_op jit(solution)/shard_map/remap_edges/pallas_call | solution.py:499
  49.0 1.4 %finish_tracers.1 = (f32[4,4,16,1152]{3,2,1,0:T(8,128)}, f32[4,16,1152]{2,1,0:T(8,128)}, f32[8,128]{1,0:T(8,128)S(1)}) custom-call(f32[4,4,16,1152]{3,2,1,0:T(8,128)S(1)} %get-tuple-element.48.refs_8_.own_ref, f32[4,4,2,1152]{3,2,1,0:T(2,128)S(1)} %get-tuple-element.52.near_ref, f32[6,4,2,1152]{3,2,1,0:T(2,128)S(1)} %get-tuple-element.53.edge_ref, ...), custom_call_target="tpu_custom_call" | custom-call | flops 589824 | bytes 3538944 | tf_op jit(solution)/shard_map/finish_tracers/pallas_call | solution.py:537
  50.3 1.8 %collective-permute-done.20.refs_0_ = f32[112,1152]{1,0:T(8,128)S(1)} collective-permute-done((f32[112,1152]{1,0:T(8,128)S(1)}, f32[112,1152]{1,0:T(8,128)S(1)}, u32[]{:S(2)}, u32[]{:S(2)}) %collective-permute-start.20) | collective-permute-done | bytes 516128 | tf_op jit(solution)/shard_map/ppermute | solution.py:636
  52.1 0.9 %finish_winds.1 = (f32[4,16,1152]{2,1,0:T(8,128)}, f32[4,16,1152]{2,1,0:T(8,128)}) custom-call(f32[2,4,16,1152]{3,2,1,0:T(8,128)S(1)} %get-tuple-element.57.own_ref, f32[6,4,2,1152]{3,2,1,0:T(2,128)S(1)} %get-tuple-element.53.edge_ref, f32[112,1152]{1,0:T(8,128)S(1)} %collective-permute-done.20.refs_0_, f32[8,128]{1,0:T(8,128)S(1)} %get-tuple-element.58.refs_1_), custom_call_target="tpu_custom_call" | custom-call | flops 147456 | bytes 1769472 | tf_op jit(solution)/shard_map/finish_winds/pallas_call | solution.py:573
  (49 shorter events, 5.6 us)
Async XLA Ops:
  2.5 9.4 %collective-permute-start.1 = (f32[16,1152]{1,0:T(8,128)S(1)}, f32[16,1152]{1,0:T(8,128)S(1)}, u32[]{:S(2)}, u32[]{:S(2)}) collective-permute-start(f32[16,1152]{1,0:T(8,128)S(1)} %get-tuple-element.39), channel_id=1, source_target_pairs={{0,2},{2,0},{1,3},{3,1},{4,6},{6,4},{5,7},{7,5},{8,10},{10,8},{9,1... | collective-permute-start | bytes 221192 | tf_op jit(solution)/shard_map/ppermute | solution.py:636
  5.5 6.4 %collective-permute-start.2 = (f32[16,1152]{1,0:T(8,128)S(1)}, f32[16,1152]{1,0:T(8,128)S(1)}, u32[]{:S(2)}, u32[]{:S(2)}) collective-permute-start(f32[16,1152]{1,0:T(8,128)S(1)} %get-tuple-element.39), channel_id=1, source_target_pairs={{0,3},{1,2},{2,1},{3,0},{4,7},{5,6},{6,5},{7,4},{8,11},{9,10},{10,... | collective-permute-start | bytes 221192 | tf_op jit(solution)/shard_map/ppermute | solution.py:644
  5.5 4.8 %collective-permute-start.3 = (f32[1,4,2,1152]{3,2,1,0:T(2,128)S(1)}, f32[1,4,2,1152]{3,2,1,0:T(2,128)S(1)}, u32[]{:S(2)}, u32[]{:S(2)}) collective-permute-start(f32[1,4,2,1152]{3,2,1,0:T(2,128)S(1)} %get-tuple-element.40.refs_4_), channel_id=1, source_target_pairs={{0,2},{2,0},{1,3},{3,1},{4,6},{6,4},{5,7},{7,5},{8,10},{10,8},{9,1... | collective-permute-start | bytes 110600 | tf_op jit(solution)/shard_map/ppermute | solution.py:636
  8.4 3.6 %collective-permute-start = (f32[5,4,16,1152]{3,2,1,0:T(8,128)S(1)}, f32[5,4,16,1152]{3,2,1,0:T(8,128)S(1)}, u32[]{:S(2)}, u32[]{:S(2)}) collective-permute-start(f32[5,4,16,1152]{3,2,1,0:T(8,128)S(1)} %get-tuple-element.38.refs_0_.refs_2_), channel_id=1, source_target_pairs={{0,1},{1,0},{2,3},{3,2},{4,5},{5,4},{6,7},{7,6},{8,9},{9,8},{10,11... | collective-permute-start | bytes 4423688 | tf_op jit(solution)/shard_map/ppermute | solution.py:638
  9.1 5.1 %collective-permute-start.4 = (f32[2,4,2,1152]{3,2,1,0:T(2,128)S(1)}, f32[2,4,2,1152]{3,2,1,0:T(2,128)S(1)}, u32[]{:S(2)}, u32[]{:S(2)}) collective-permute-start(f32[2,4,2,1152]{3,2,1,0:T(2,128)S(1)} %get-tuple-element.43.refs_8_), channel_id=1, source_target_pairs={{0,2},{2,0},{1,3},{3,1},{4,6},{6,4},{5,7},{7,5},{8,10},{10,8},{9,1... | collective-permute-start | bytes 221192 | tf_op jit(solution)/shard_map/ppermute | solution.py:636
  10.3 4.7 %collective-permute-start.5 = (f32[2,4,2,1152]{3,2,1,0:T(2,128)S(1)}, f32[2,4,2,1152]{3,2,1,0:T(2,128)S(1)}, u32[]{:S(2)}, u32[]{:S(2)}) collective-permute-start(f32[2,4,2,1152]{3,2,1,0:T(2,128)S(1)} %get-tuple-element.44.refs_12_), channel_id=1, source_target_pairs={{0,2},{2,0},{1,3},{3,1},{4,6},{6,4},{5,7},{7,5},{8,10},{10,8},{9,1... | collective-permute-start | bytes 221192 | tf_op jit(solution)/shard_map/ppermute | solution.py:636
  13.5 11.5 %copy-start = (f32[4,4,16,1152]{3,2,1,0:T(8,128)S(1)}, f32[4,4,16,1152]{3,2,1,0:T(8,128)}, u32[]{:S(2)}) copy-start(f32[4,4,16,1152]{3,2,1,0:T(8,128)} %tracer_ref.1) | copy-start | bytes 3538948
  13.5 11.5 %copy-start.1 = (f32[4,16,1152]{2,1,0:T(8,128)S(1)}, f32[4,16,1152]{2,1,0:T(8,128)}, u32[]{:S(2)}) copy-start(f32[4,16,1152]{2,1,0:T(8,128)} %thick_ref.1) | copy-start | bytes 884740
  13.5 11.5 %copy-start.2 = (f32[4,16,1152]{2,1,0:T(8,128)S(1)}, f32[4,16,1152]{2,1,0:T(8,128)}, u32[]{:S(2)}) copy-start(f32[4,16,1152]{2,1,0:T(8,128)} %u_ref.1) | copy-start | bytes 884740
  13.5 22.5 %collective-permute-start.19 = (f32[192,1152]{1,0:T(8,128)S(1)}, f32[192,1152]{1,0:T(8,128)S(1)}, u32[]{:S(2)}, u32[]{:S(2)}) collective-permute-start(f32[192,1152]{1,0:T(8,128)S(1)} %remap_parts.3.refs_0_), channel_id=1, source_target_pairs={{0,2},{2,0},{1,3},{3,1},{4,6},{6,4},{5,7},{7,5},{8,10},{10,8},{9,1... | collective-permute-start | bytes 2654216 | tf_op jit(solution)/shard_map/ppermute | solution.py:636
  16.8 8.2 %collective-permute-start.7 = (f32[8,4,1,1152]{3,2,1,0:T(1,128)S(1)}, f32[8,4,1,1152]{3,2,1,0:T(1,128)S(1)}, u32[]{:S(2)}, u32[]{:S(2)}) collective-permute-start(f32[8,4,1,1152]{3,2,1,0:T(1,128)S(1)} %get-tuple-element.46), channel_id=1, source_target_pairs={{4,0},{8,4},{12,8},{5,1},{9,5},{13,9},{6,2},{10,6},{14,10},{7,3},{... | collective-permute-start | bytes 442376 | tf_op jit(solution)/shard_map/ppermute | solution.py:685
  18.1 6.9 %collective-permute-start.6 = (f32[6,4,1,1152]{3,2,1,0:T(1,128)S(1)}, f32[6,4,1,1152]{3,2,1,0:T(1,128)S(1)}, u32[]{:S(2)}, u32[]{:S(2)}) collective-permute-start(f32[6,4,1,1152]{3,2,1,0:T(1,128)S(1)} %get-tuple-element.45), channel_id=1, source_target_pairs={{0,4},{4,8},{8,12},{1,5},{5,9},{9,13},{2,6},{6,10},{10,14},{3,7},{... | collective-permute-start | bytes 331784 | tf_op jit(solution)/shard_map/ppermute | solution.py:684
  28.7 3.1 %collective-permute-start.17 = (f32[1,4,16,1152]{3,2,1,0:T(8,128)S(1)}, f32[1,4,16,1152]{3,2,1,0:T(8,128)S(1)}, u32[]{:S(2)}, u32[]{:S(2)}) collective-permute-start(f32[1,4,16,1152]{3,2,1,0:T(8,128)S(1)} %get-tuple-element.49.refs_2_), channel_id=1, source_target_pairs={{0,1},{1,0},{2,3},{3,2},{4,5},{5,4},{6,7},{7,6},{8,9},{9,8},{10,11... | collective-permute-start | bytes 884744 | tf_op jit(solution)/shard_map/ppermute | solution.py:638
  28.7 3.0 %collective-permute-start.18 = (f32[1,4,16,1152]{3,2,1,0:T(8,128)S(1)}, f32[1,4,16,1152]{3,2,1,0:T(8,128)S(1)}, u32[]{:S(2)}, u32[]{:S(2)}) collective-permute-start(f32[1,4,16,1152]{3,2,1,0:T(8,128)S(1)} %get-tuple-element.50.refs_4_), channel_id=1, source_target_pairs={{0,1},{1,0},{2,3},{3,2},{4,5},{5,4},{6,7},{7,6},{8,9},{9,8},{10,11... | collective-permute-start | bytes 884744 | tf_op jit(solution)/shard_map/ppermute | solution.py:638
  29.2 12.4 %collective-permute-start.9 = (f32[7,4,2,1152]{3,2,1,0:T(2,128)S(1)}, f32[7,4,2,1152]{3,2,1,0:T(2,128)S(1)}, u32[]{:S(2)}, u32[]{:S(2)}) collective-permute-start(f32[7,4,2,1152]{3,2,1,0:T(2,128)S(1)} %get-tuple-element.47.refs_6_.refs_0_), channel_id=1, source_target_pairs={{0,2},{2,0},{1,3},{3,1},{4,6},{6,4},{5,7},{7,5},{8,10},{10,8},{9,1... | collective-permute-start | bytes 774152 | tf_op jit(solution)/shard_map/ppermute | solution.py:636
  37.9 14.3 %collective-permute-start.20 = (f32[112,1152]{1,0:T(8,128)S(1)}, f32[112,1152]{1,0:T(8,128)S(1)}, u32[]{:S(2)}, u32[]{:S(2)}) collective-permute-start(f32[112,1152]{1,0:T(8,128)S(1)} %get-tuple-element.51.refs_16_), channel_id=1, source_target_pairs={{0,2},{2,0},{1,3},{3,1},{4,6},{6,4},{5,7},{7,5},{8,10},{10,8},{9,1... | collective-permute-start | bytes 1548296 | tf_op jit(solution)/shard_map/ppermute | solution.py:636
  38.5 7.4 %collective-permute-start.8 = (f32[7,4,2,1152]{3,2,1,0:T(2,128)S(1)}, f32[7,4,2,1152]{3,2,1,0:T(2,128)S(1)}, u32[]{:S(2)}, u32[]{:S(2)}) collective-permute-start(f32[7,4,2,1152]{3,2,1,0:T(2,128)S(1)} %get-tuple-element.47.refs_6_.refs_0_), channel_id=1, source_target_pairs={{0,1},{1,0},{2,3},{3,2},{4,5},{5,4},{6,7},{7,6},{8,9},{9,8},{10,11... | collective-permute-start | bytes 774152 | tf_op jit(solution)/shard_map/ppermute | solution.py:638
  41.6 4.3 %collective-permute-start.10 = (f32[7,4,2,1152]{3,2,1,0:T(2,128)S(1)}, f32[7,4,2,1152]{3,2,1,0:T(2,128)S(1)}, u32[]{:S(2)}, u32[]{:S(2)}) collective-permute-start(f32[7,4,2,1152]{3,2,1,0:T(2,128)S(1)} %collective-permute-done.9.refs_2_), channel_id=1, source_target_pairs={{0,1},{1,0},{2,3},{3,2},{4,5},{5,4},{6,7},{7,6},{8,9},{9,8},{10,11... | collective-permute-start | bytes 774152 | tf_op jit(solution)/shard_map/ppermute | solution.py:638
  41.6 1.6 %collective-permute-start.11 = (f32[1,4,2,1152]{3,2,1,0:T(2,128)S(1)}, f32[1,4,2,1152]{3,2,1,0:T(2,128)S(1)}, u32[]{:S(2)}, u32[]{:S(2)}) collective-permute-start(f32[1,4,2,1152]{3,2,1,0:T(2,128)S(1)} %get-tuple-element.40.refs_4_), channel_id=1, source_target_pairs={{0,1},{1,0},{2,3},{3,2},{4,5},{5,4},{6,7},{7,6},{8,9},{9,8},{10,11... | collective-permute-start | bytes 110600 | tf_op jit(solution)/shard_map/ppermute | solution.py:638
  42.1 1.3 %collective-permute-start.13 = (f32[2,4,2,1152]{3,2,1,0:T(2,128)S(1)}, f32[2,4,2,1152]{3,2,1,0:T(2,128)S(1)}, u32[]{:S(2)}, u32[]{:S(2)}) collective-permute-start(f32[2,4,2,1152]{3,2,1,0:T(2,128)S(1)} %get-tuple-element.43.refs_8_), channel_id=1, source_target_pairs={{0,1},{1,0},{2,3},{3,2},{4,5},{5,4},{6,7},{7,6},{8,9},{9,8},{10,11... | collective-permute-start | bytes 221192 | tf_op jit(solution)/shard_map/ppermute | solution.py:638
  43.2 1.3 %collective-permute-start.15 = (f32[2,4,2,1152]{3,2,1,0:T(2,128)S(1)}, f32[2,4,2,1152]{3,2,1,0:T(2,128)S(1)}, u32[]{:S(2)}, u32[]{:S(2)}) collective-permute-start(f32[2,4,2,1152]{3,2,1,0:T(2,128)S(1)} %get-tuple-element.44.refs_12_), channel_id=1, source_target_pairs={{0,1},{1,0},{2,3},{3,2},{4,5},{5,4},{6,7},{7,6},{8,9},{9,8},{10,11... | collective-permute-start | bytes 221192 | tf_op jit(solution)/shard_map/ppermute | solution.py:638
  43.4 1.2 %collective-permute-start.12 = (f32[1,4,2,1152]{3,2,1,0:T(2,128)S(1)}, f32[1,4,2,1152]{3,2,1,0:T(2,128)S(1)}, u32[]{:S(2)}, u32[]{:S(2)}) collective-permute-start(f32[1,4,2,1152]{3,2,1,0:T(2,128)S(1)} %collective-permute-done.3.refs_2_.refs_6_), channel_id=1, source_target_pairs={{0,1},{1,0},{2,3},{3,2},{4,5},{5,4},{6,7},{7,6},{8,9},{9,8},{10,11... | collective-permute-start | bytes 110600 | tf_op jit(solution)/shard_map/ppermute | solution.py:638
  44.5 1.3 %collective-permute-start.14 = (f32[2,4,2,1152]{3,2,1,0:T(2,128)S(1)}, f32[2,4,2,1152]{3,2,1,0:T(2,128)S(1)}, u32[]{:S(2)}, u32[]{:S(2)}) collective-permute-start(f32[2,4,2,1152]{3,2,1,0:T(2,128)S(1)} %collective-permute-done.4.refs_1_.refs_10_), channel_id=1, source_target_pairs={{0,1},{1,0},{2,3},{3,2},{4,5},{5,4},{6,7},{7,6},{8,9},{9,8},{10,11... | collective-permute-start | bytes 221192 | tf_op jit(solution)/shard_map/ppermute | solution.py:638
  44.6 1.3 %collective-permute-start.16 = (f32[2,4,2,1152]{3,2,1,0:T(2,128)S(1)}, f32[2,4,2,1152]{3,2,1,0:T(2,128)S(1)}, u32[]{:S(2)}, u32[]{:S(2)}) collective-permute-start(f32[2,4,2,1152]{3,2,1,0:T(2,128)S(1)} %collective-permute-done.5.refs_2_.refs_14_), channel_id=1, source_target_pairs={{0,1},{1,0},{2,3},{3,2},{4,5},{5,4},{6,7},{7,6},{8,9},{9,8},{10,11... | collective-permute-start | bytes 221192 | tf_op jit(solution)/shard_map/ppermute | solution.py:638
  (6 other events, 53.7 us)

commit v12 on v10

--- a/solution.py
+++ b/solution.py
@@ -23,6 +23,10 @@
 
 def after(arrays):
     return [pl.BlockSpec(memory_space=pl.ANY)] * len(arrays)
+
+
+def near_rows(rows):
+    return (1, 2, rows - 2), (3, 2)
 
 
 def geometry_table(lat_rows, band_rows):
@@ -79,8 +83,9 @@
 
 
 def first_kernel(table_hbm, thick_hbm, u_hbm, v_hbm, tracer_hbm, *refs):
-    new_ref, sum_ref, thick_ref, u_ref, v_ref, tracer_ref, geo_ref, sems = refs
+    new_ref, sum_ref, both_ref, near_ref, thick_ref, u_ref, v_ref, tracer_ref, geo_ref, sems = refs
     L, rows, _ = thick_ref.shape
+    near, _ = near_rows(rows)
     table_copy = pltpu.make_async_copy(table_hbm.at[lax.axis_index("lat")], geo_ref, sems.at[3, 0])
     table_copy.start()
     pairs = ((thick_hbm, thick_ref), (u_hbm, u_ref), (v_hbm, v_ref))
@@ -104,10 +109,16 @@
         east, north, _ = fluxes(geo, thick, u, v, None, None, None)
         new = thick - (east - west_of(east)) - (north - south_of(north, None)) * geo[0:rows, 2:3]
         new_ref[k] = new
+        for j, row in enumerate(near):
+            near_ref[0, k, j : j + 1] = new[row : row + 1]
         sum_ref[...] += new
         return carry
 
     lax.fori_loop(0, L, level, 0)
+    both_ref[0:rows] = sum_ref[...]
+    for k in range(L):
+        at = rows + k * len(near)
+        both_ref[at : at + len(near)] = near_ref[0, k]
     tracer_copy.wait()
 
 
@@ -115,7 +126,8 @@
     L, R, N = thickness.shape
     arguments = (thickness, wind_u, wind_v, tracers)
     operands = [pltpu.with_memory_space_constraint(a, pltpu.HBM) for a in (table, *arguments)]
-    shapes = [(L, R, N), (R, N)] + [a.shape for a in arguments]
+    near = len(near_rows(R)[0])
+    shapes = [(L, R, N), (R, N), (-(-(R + L * near) // 8) * 8, N), (1, L, near, N)] + [a.shape for a in arguments]
     return pl.pallas_call(
         first_kernel,
         in_specs=after(operands),
@@ -130,6 +142,7 @@
 
 def inner_kernel(table_ref, new_ref, thick_ref, u_ref, v_ref, tracer_ref, out_ref, near_ref, near_rest_ref):
     T, L, rows, _ = tracer_ref.shape
+    near, _ = near_rows(rows)
     geo = table_ref[lax.axis_index("lat")]
     inverse = geo[0:rows, 2:3]
 
@@ -137,19 +150,17 @@
         thick, u, v, new = thick_ref[k], u_ref[k], v_ref[k], new_ref[k]
         east, north, _ = fluxes(geo, thick, u, v, None, None, None)
 
-        def store(field, value):
-            out_ref[field, k] = value
-            ref, at = (near_ref, field) if field < 2 else (near_rest_ref, field - 2)
-            ref[at, k, 0:1] = value[1:2]
-            ref[at, k, 1:2] = value[rows - 2 : rows - 1]
-
-        store(0, new)
+        out_ref[0, k] = new
         scale = 1.0 / new
         for c in range(T):
             change = tracer_change(
                 tracer_ref[c, k], None, None, thick, u, v, None, east, north, None, inverse
             )
-            store(1 + c, change * scale)
+            value = change * scale
+            out_ref[1 + c, k] = value
+            ref, at = (near_ref, c) if c < T // 2 else (near_rest_ref, c - T // 2)
+            for j, row in enumerate(near):
+                ref[pl.ds((at * L + k) * len(near) + j, 1)] = value[row : row + 1]
         return carry
 
     lax.fori_loop(0, L, level, 0)
@@ -158,12 +169,13 @@
 def inner_step(table, new, thickness, wind_u, wind_v, tracers):
     L, R, N = thickness.shape
     T = tracers.shape[0]
+    rows = lambda n: jax.ShapeDtypeStruct((n * L * len(near_rows(R)[0]), N), jnp.float32)
     shape = lambda n, rows: jax.ShapeDtypeStruct((n, L, rows, N), jnp.float32)
     return pl.pallas_call(
         inner_kernel,
         in_specs=[VMEM] * 6,
         out_specs=[VMEM] * 3,
-        out_shape=[shape(1 + T, R), shape(2, 2), shape(T - 1, 2)],
+        out_shape=[shape(1 + T, R), rows(T // 2), rows(T - T // 2)],
         compiler_params=params(),
         cost_estimate=cost(130 * L * R * N, 4 * L * R * N * (8 + 2 * T)),
         name="inner_step",
@@ -319,24 +331,33 @@
 
 
 def mass_kernel(C, S, *refs):
-    base_ref, mass_ref = refs[-2:]
+    other_refs, (base_ref, mass_ref, *near_refs) = refs[: (C - 1) * S], refs[(C - 1) * S :]
+    rows = base_ref.shape[0]
     lev = lax.axis_index("lev")
     others_mass, base = None, None
     for s in range(1, C):
-        other = functools.reduce(jnp.add, [ref[...] for ref in refs[(s - 1) * S : s * S]])
+        first, *rest = other_refs[(s - 1) * S : s * S]
+        other = functools.reduce(jnp.add, [first[0:rows]] + [ref[...] for ref in rest])
         below = jnp.where(lev >= s, other, 0.0)
         others_mass = other if others_mass is None else others_mass + other
         base = below if base is None else base + below
+        _, L, near, _ = near_refs[s - 1].shape
+        for k in range(L):
+            near_refs[s - 1][0, k] = first[rows + k * near : rows + (k + 1) * near]
     base_ref[...] = base
     mass_ref[...] = others_mass
 
 
-def other_chips(counts, others):
-    return pl.pallas_call(
-        functools.partial(mass_kernel, *counts),
+def other_chips(counts, others, levels):
+    C, S = counts
+    R, N = others[1].shape
+    near = len(near_rows(R)[0])
+    return pl.pallas_call(
+        functools.partial(mass_kernel, C, S),
         in_specs=[VMEM] * len(others),
-        out_specs=[VMEM] * 2,
-        out_shape=[jax.ShapeDtypeStruct(others[0].shape, jnp.float32)] * 2,
+        out_specs=[VMEM] * (1 + C),
+        out_shape=[jax.ShapeDtypeStruct((R, N), jnp.float32)] * 2
+        + [jax.ShapeDtypeStruct((1, levels, near, N), jnp.float32)] * (C - 1),
         compiler_params=params(),
         cost_estimate=cost(1e11, 1e9),
         name="other_chips",
@@ -377,6 +398,14 @@
     return [jnp.minimum(jnp.maximum(top - low, 0.0), value) for _, _, low, value in sources]
 
 
+def level_of(ref, index):
+    return lambda m, at, columns: ref[index, m, at, columns]
+
+
+def packed_level_of(ref, index, L, rows):
+    return lambda m, at, columns: ref[(index * L + m) * rows : (index * L + m + 1) * rows, columns]
+
+
 def remap_rows(weight_ref, sum_ref, counts, steps, thick_refs, field_refs, other_refs, store):
     C, S = counts
     _, L, R, N = thick_refs[0].shape
@@ -400,7 +429,7 @@
                 scale = 1.0 / target
                 means = []
                 for refs in field_refs:
-                    terms = [refs[g][0][refs[g][1], m, at, columns] * w for (g, m, _, _), w in zip(sources, part)]
+                    terms = [refs[g](m, at, columns) * w for (g, m, _, _), w in zip(sources, part)]
                     means.append(functools.reduce(jnp.add, terms) * scale)
                 store(s, i, at, columns, target, means)
 
@@ -414,7 +443,7 @@
 
 
 def inner_part(at, margin, rows):
-    return max(at.start, margin), min(at.stop, rows - margin)
+    return max(at.start, margin[0]), min(at.stop, rows - margin[1])
 
 
 def remap_kernel(counts, steps, fields, margin, with_thickness, sizes, weight_ref, *refs):
@@ -428,7 +457,7 @@
     other_refs, out_refs = refs[:2], refs[len(refs) - len(steps) - with_thickness :]
     _, L, R, _ = thick_refs[0].shape
     thick_out_ref = out_refs[-1]
-    field_refs = [[(ref, index) for ref in bundles[which]] for which, index in fields]
+    field_refs = [[level_of(ref, index) for ref in bundles[which]] for which, index in fields]
 
     def store(s, i, at, columns, target, means):
         out_ref = out_refs[steps.index(s)]
@@ -439,7 +468,7 @@
                 out_ref[f, i, at, columns] = value
             else:
                 lower, upper = inner_part(at, margin, R)
-                start = (f * L + i) * (R - 2 * margin) - margin
+                start = (f * L + i) * (R - sum(margin)) - margin[0]
                 out_ref[start + lower : start + upper, columns] = value[lower - at.start : upper - at.start]
 
     remap_rows(
@@ -452,7 +481,7 @@
     _, L, R, N = thick[0].shape
     F = len(fields)
     whole = jax.ShapeDtypeStruct((F, L, R, N), jnp.float32)
-    inner = jax.ShapeDtypeStruct((F * L * (R - 2 * margin), N), jnp.float32)
+    inner = jax.ShapeDtypeStruct((F * L * (R - sum(margin)), N), jnp.float32)
     flat = [a for bundle in bundles for a in bundle]
     out_shape = [whole if s == 0 else inner for s in steps]
     if with_thickness:
@@ -472,7 +501,8 @@
 def remap_edge_kernel(counts, near_fields, weight_ref, *refs):
     *refs, sum_ref = refs
     G = counts[0] * counts[1]
-    edge_refs, near_refs, rest_refs = refs[:G], refs[G : 2 * G], refs[2 * G : 3 * G]
+    edge_refs, near_refs = refs[:G], refs[G : 2 * G]
+    bundles = (refs[2 * G : 3 * G], refs[3 * G : 4 * G])
     edge_out_ref, thick_out_ref, near_out_ref = refs[-3:]
 
     def store_edge(s, i, at, columns, target, means):
@@ -484,18 +514,18 @@
         for f, value in enumerate(means):
             near_out_ref[f, i, at, columns] = value
 
-    fields = [[(ref, f) for ref in edge_refs] for f in range(1, edge_refs[0].shape[0])]
+    fields = [[level_of(ref, f) for ref in edge_refs] for f in range(1, edge_refs[0].shape[0])]
     remap_rows(weight_ref, sum_ref, counts, (0,), edge_refs, fields, [], store_edge)
-    bundles = (near_refs, rest_refs)
-    fields = [[(ref, index) for ref in bundles[which]] for which, index in near_fields]
+    _, L, R, _ = near_refs[0].shape
+    fields = [[packed_level_of(ref, index, L, R) for ref in bundles[which]] for which, index in near_fields]
     remap_rows(weight_ref, sum_ref, counts, (0,), near_refs, fields, [], store_near)
 
 
-def remap_edges(counts, weights, edges, near, near_rest, wait=()):
+def remap_edges(counts, weights, edges, near_new, near, near_rest, wait=()):
     F, L, R, N = edges[0].shape
     T = F - 3
-    near_fields = tuple((0, 1) if f == 0 else (1, f - 1) for f in range(T))
-    operands = [*edges, *near, *near_rest]
+    near_fields = tuple((0, f) if f < T // 2 else (1, f - T // 2) for f in range(T))
+    operands = [*edges, *near_new, *near, *near_rest]
     return pl.pallas_call(
         functools.partial(remap_edge_kernel, counts, near_fields),
         in_specs=[VMEM] * (1 + len(operands)) + after(wait),
@@ -503,7 +533,7 @@
         out_shape=[
             jax.ShapeDtypeStruct((F - 1, L, R, N), jnp.float32),
             jax.ShapeDtypeStruct((L, R, N), jnp.float32),
-            jax.ShapeDtypeStruct((T, L, R, N), jnp.float32),
+            jax.ShapeDtypeStruct((T, *near_new[0].shape[1:]), jnp.float32),
         ],
         scratch_shapes=[pltpu.VMEM((weights.shape[0] + 1, 8, LANES), jnp.float32)],
         compiler_params=params(),
@@ -522,20 +552,20 @@
             thick_out_ref[i, row : row + 1] = thick_edge_ref[i, j : j + 1]
     for f in range(T):
         for i in range(L):
-            start = (f * L + i) * (R - 2 * margin)
-            total = own_ref[f, i, margin : R - margin]
+            start, first, end = (f * L + i) * (R - sum(margin)), margin[0], R - margin[1]
+            total = own_ref[f, i, first:end]
             for ref in arrived_refs:
-                total = total + ref[start : start + R - 2 * margin]
-            out_ref[f, i, margin : R - margin] = total
+                total = total + ref[start : start + end - first]
+            out_ref[f, i, first:end] = total
             for row, j in ((0, 0), (R - 1, 1)):
                 out_ref[f, i, row : row + 1] = edge_ref[2 + f, i, j : j + 1]
-            for row, j in ((1, 0), (R - 2, 1)):
+            for j, row in enumerate(near_rows(R)[0]):
                 out_ref[f, i, row : row + 1] = near_ref[f, i, j : j + 1]
 
 
 def finish_tracers(own, near, edge, thick, thick_edge, arrived):
     return pl.pallas_call(
-        functools.partial(finish_kernel, 2),
+        functools.partial(finish_kernel, near_rows(own.shape[2])[1]),
         in_specs=[VMEM] * (5 + len(arrived)),
         out_specs=[VMEM] * 3,
         out_shape=[
@@ -659,15 +689,17 @@
 
     remap = functools.partial(remap_parts, (C, S), weights)
 
-    new, own_sum, *arguments = first_step(table, thickness, wind_u, wind_v, tracers)
-    others = [send(own_sum, s=s, t=t) for s in away for t in range(S)]
+    new, own_sum, own_both, near_new, *arguments = first_step(table, thickness, wind_u, wind_v, tracers)
+    others = [send(own_sum if t else own_both, s=s, t=t) for s in away for t in range(S)]
     inner, near, near_rest = inner_step(table, new, *arguments)
     group = with_others_of_chip(inner)
     near = [near] + [send(near, s=s, t=0) for s in away]
     near_rest = [near_rest] + [send(near_rest, s=s, t=0) for s in away]
-    others = other_chips((C, S), others)
+    base, rest_mass, *near_arrived = other_chips((C, S), others, L)
+    others = [base, rest_mass]
+    near_new = [near_new, *near_arrived]
     tracer_fields = [(0, 1 + c) for c in range(T)]
-    away_parts = remap(group, [group], others, tracer_fields, away, 2)
+    away_parts = remap(group, [group], others, tracer_fields, away, near_rows(R)[1])
     arrived = sent(away_parts)
 
     last, leading = edge_rows(
@@ -678,16 +710,16 @@
     u, v, edge = second_step(table, lat_rows, thickness, wind_u, wind_v, tracers, up, down, cutoff)
     edges = [edge] + [send(edge, s=s, t=0) for s in away]
     winds = [with_others_of_chip(u), with_others_of_chip(v)]
-    tracers_own, thick_inner = remap(group, [group], others, tracer_fields, (0,), 0, with_thickness=True, wait=[edge])
+    tracers_own, thick_inner = remap(group, [group], others, tracer_fields, (0,), (0, 0), with_thickness=True, wait=[edge])
     winds_own, *winds_away = remap(
-        group, winds, others, [(0, 0), (1, 0)], range(C), 1, wait=[tracers_own, *arrived[:1]]
+        group, winds, others, [(0, 0), (1, 0)], range(C), (1, 1), wait=[tracers_own, *arrived[:1]]
     )
     winds_arrived = sent(winds_away)
-    near, near_rest, edges = (
-        [a for own in sources for a in with_others_of_chip(own)] for sources in (near, near_rest, edges)
+    near_new, near, near_rest, edges = (
+        [a for own in sources for a in with_others_of_chip(own)] for sources in (near_new, near, near_rest, edges)
     )
     edge_out, thick_edge, near_out = remap_edges(
-        (C, S), weights, edges, near, near_rest, wait=winds_away[:1]
+        (C, S), weights, edges, near_new, near, near_rest, wait=winds_away[:1]
     )
 
     tracers_out, thickness_out, token = finish_tracers(

time: 51.8 us -> 50.8 us (0.981)
  waiting for transfers between devices: 13.7 us -> 11.9 us
  Pallas kernels: 18.7 us -> 19.5 us
    ppermute x6, waiting for transfers between devices: 8.17 us -> 6.25 us  [shifted(): lax.ppermute(value, 'lev', [(i, (i + s) % lev_count) for i in range(lev_c...]
    ppermute x1, waiting for transfers between devices: 0.37 us -> 1.24 us  [shifted(): return lax.ppermute(value, ('lev', 'sub'), pairs)]
    ppermute x9 -> x11, waiting for transfers between devices: 2.86 us -> 2.08 us  [shifted(): lax.ppermute(value, 'sub', [(i, (i + t) % sub_count) for i in range(sub_c...]
    pallas_call x1, Pallas kernels: 3.07 us -> 3.72 us  [remap_edges(): pl.pallas_call(functools.partial(remap_edge_kernel, counts, near_fields),...]
    ppermute x9 -> x11, starting transfers between devices: 1.85 us -> 2.43 us  [shifted(): lax.ppermute(value, 'sub', [(i, (i + t) % sub_count) for i in range(sub_c...]
  transfers between devices with their start and end apart: 18 -> 20, of which waited for: 9 -> 9; matrix products, arithmetic and copies ran while one was open for 0% -> 0% of each run, Pallas kernels for 31% -> 33%
where the time goes in v12:
time: 50.8 us; the launch traced here: 50.6 us
  Pallas kernels  19.5 us (38%)
  starting transfers between devices  18.2 us (36%)
  waiting for transfers between devices  11.9 us (23%)
  between operations  0.87 us (2%)
    ppermute x6, starting transfers between devices, shifted(): lax.ppermute(value, 'lev', [(i, (i + s) % lev_count) for i in range(lev_c...  9.93 us
    ppermute x6, waiting for transfers between devices, shifted(): lax.ppermute(value, 'lev', [(i, (i + s) % lev_count) for i in range(lev_c...  6.25 us
    ppermute x1, starting transfers between devices, per_device(): up = lax.ppermute(last, 'lat', northward)  4.55 us
    pallas_call x3, Pallas kernels, remap_parts(): pl.pallas_call(functools.partial(remap_kernel, counts, tuple(steps), tupl...  4.45 us
    pallas_call x1, Pallas kernels, remap_edges(): pl.pallas_call(functools.partial(remap_edge_kernel, counts, near_fields),...  3.72 us
    pallas_call x1, Pallas kernels, second_step(): pl.pallas_call(functools.partial(second_kernel, lat_rows), grid=(L,), in_...  3.62 us
    ppermute x11, starting transfers between devices, shifted(): lax.ppermute(value, 'sub', [(i, (i + t) % sub_count) for i in range(sub_c...  2.43 us
    ppermute x1, waiting for transfers between devices, per_device(): up = lax.ppermute(last, 'lat', northward)  2.3 us
  transfers between devices with their start and end apart: 20, of which 9 were waited for; matrix products, arithmetic and copies ran while one was open for 0% of the time, Pallas kernels for 33%

profile of v12, /device:TPU:0, one launch (start us, length us, event | category | flops | bytes accessed | tf_op | source)
XLA Modules:
  0.0 50.6 jit_solution(9139617645017716250)
XLA Ops:
  0.6 1.9 %first_step.1 = (f32[4,16,1152]{2,1,0:T(8,128)S(1)}, f32[16,1152]{1,0:T(8,128)S(1)}, f32[32,1152]{1,0:T(8,128)S(1)}, f32[1,4,3,1152]{3,2,1,0:T(4,128)S(1)}, f32[...) custom-call(f32[4,24,128]{2,1,0:T(8,128)} %constant.6.clone.table_hb, ...), custom_call_target="tpu_custom_call" | custom-call | flops 2949120 | bytes 4423680 | tf_op jit(solution)/shard_map/first_step/pallas_call | solution.py:131
  2.5 3.0 %collective-permute-start.1 = (f32[32,1152]{1,0:T(8,128)S(1)}, f32[32,1152]{1,0:T(8,128)S(1)}, u32[]{:S(2)}, u32[]{:S(2)}) collective-permute-start(f32[32,1152]{1,0:T(8,128)S(1)} %get-tuple-element.41), channel_id=1, source_target_pairs={{0,2},{2,0},{1,3},{3,1},{4,6},{6,4},{5,7},{7,5},{8,10},{10,8},{9,1... | collective-permute-start | bytes 442376 | tf_op jit(solution)/shard_map/ppermute | solution.py:659
  5.5 1.7 %inner_step.1 = (f32[5,4,16,1152]{3,2,1,0:T(8,128)S(1)}, f32[24,1152]{1,0:T(8,128)S(1)}, f32[24,1152]{1,0:T(8,128)S(1)}) custom-call(f32[4,24,128]{2,1,0:T(8,128)S(1)} %copy-done.6, f32[4,16,1152]{2,1,0:T(8,128)S(1)} %get-tuple-element.35.new_ref, f32[4,16,1152]{2,1,0:T(8,128)S(1)} %get-tuple-element.36.thick_ref, ...), custom_call_target="tpu_custom_call" | custom-call | flops 9584640 | bytes 4718592 | tf_op jit(solution)/shard_map/inner_step/pallas_call | solution.py:174
  7.5 1.9 %collective-permute-start.3 = (f32[24,1152]{1,0:T(8,128)S(1)}, f32[24,1152]{1,0:T(8,128)S(1)}, u32[]{:S(2)}, u32[]{:S(2)}) collective-permute-start(f32[24,1152]{1,0:T(8,128)S(1)} %get-tuple-element.45.refs_8_), channel_id=1, source_target_pairs={{0,2},{2,0},{1,3},{3,1},{4,6},{6,4},{5,7},{7,5},{8,10},{10,8},{9,1... | collective-permute-start | bytes 331784 | tf_op jit(solution)/shard_map/ppermute | solution.py:659
  9.5 1.2 %collective-permute-done.2.refs_1_ = f32[16,1152]{1,0:T(8,128)S(1)} collective-permute-done((f32[16,1152]{1,0:T(8,128)S(1)}, f32[16,1152]{1,0:T(8,128)S(1)}, u32[]{:S(2)}, u32[]{:S(2)}) %collective-permute-start.2) | collective-permute-done | bytes 73760 | tf_op jit(solution)/shard_map/ppermute | solution.py:667
  10.9 1.4 %remap_parts.3.refs_0_ = f32[176,1152]{1,0:T(8,128)S(1)} custom-call(f32[16,8,128]{2,1,0:T(8,128)S(1)} %broadcast_in_dim.4.weight_ref, f32[5,4,16,1152]{3,2,1,0:T(8,128)S(1)} %get-tuple-element.40.refs_0_.refs_2_, f32[5,4,16,1152]{3,2,1,0:T(8,128)S(1)} %collective-permute-done.refs_1_.refs_3_, f32[5,4,16,1152]{3,2,1,0:T(8,128)S(1)} %get-tuple-element.40.refs_0_.refs_2_, ...), custom_call_target="tpu_custom_call" | custom-call | flops 7667712 | bytes 4423680 | tf_op jit(solution)/shard_map/remap_parts/pallas_call | solution.py:489
  12.4 1.6 %collective-permute-start.18 = (f32[176,1152]{1,0:T(8,128)S(1)}, f32[176,1152]{1,0:T(8,128)S(1)}, u32[]{:S(2)}, u32[]{:S(2)}) collective-permute-start(f32[176,1152]{1,0:T(8,128)S(1)} %remap_parts.3.refs_0_), channel_id=1, source_target_pairs={{0,2},{2,0},{1,3},{3,1},{4,6},{6,4},{5,7},{7,5},{8,10},{10,8},{9,1... | collective-permute-start | bytes 2433032 | tf_op jit(solution)/shard_map/ppermute | solution.py:659
  13.9 1.8 %collective-permute-done.4.refs_2_.refs_14_ = f32[24,1152]{1,0:T(8,128)S(1)} collective-permute-done((f32[24,1152]{1,0:T(8,128)S(1)}, f32[24,1152]{1,0:T(8,128)S(1)}, u32[]{:S(2)}, u32[]{:S(2)}) %collective-permute-start.4) | collective-permute-done | bytes 110624 | tf_op jit(solution)/shard_map/ppermute | solution.py:659
  15.7 1.7 %edge_rows.1 = (f32[6,4,1,1152]{3,2,1,0:T(1,128)S(1)}, f32[8,4,1,1152]{3,2,1,0:T(1,128)S(1)}) custom-call(f32[4,16,1152]{2,1,0:T(8,128)} %thick_ref.1, f32[4,16,1152]{2,1,0:T(8,128)} %u_ref.1, f32[4,16,1152]{2,1,0:T(8,128)} %v_ref.1, f32[4,4,16,1152]{3,2,1,0:T(8,128)} %tracer_ref.1, f32[176,1152]{1,0:T(8,128)S(1)} %remap_parts.3.refs_0_, ...), custom_call_target="tpu_custom_call" | custom-call | flops 10000000000 | bytes 1000000000 | tf_op jit(solution)/shard_map/edge_rows/pallas_call | solution.py:637
  17.5 1.3 %collective-permute-start.6 = (f32[8,4,1,1152]{3,2,1,0:T(1,128)S(1)}, f32[8,4,1,1152]{3,2,1,0:T(1,128)S(1)}, u32[]{:S(2)}, u32[]{:S(2)}) collective-permute-start(f32[8,4,1,1152]{3,2,1,0:T(1,128)S(1)} %get-tuple-element.48), channel_id=1, source_target_pairs={{4,0},{8,4},{12,8},{5,1},{9,5},{13,9},{6,2},{10,6},{14,10},{7,3},{... | collective-permute-start | bytes 442376 | tf_op jit(solution)/shard_map/ppermute | solution.py:709
  18.8 4.6 %collective-permute-start.5 = (f32[6,4,1,1152]{3,2,1,0:T(1,128)S(1)}, f32[6,4,1,1152]{3,2,1,0:T(1,128)S(1)}, u32[]{:S(2)}, u32[]{:S(2)}) collective-permute-start(f32[6,4,1,1152]{3,2,1,0:T(1,128)S(1)} %get-tuple-element.47), channel_id=1, source_target_pairs={{0,4},{4,8},{8,12},{1,5},{5,9},{9,13},{2,6},{6,10},{10,14},{3,7},{... | collective-permute-start | bytes 331784 | tf_op jit(solution)/shard_map/ppermute | solution.py:708
  23.3 2.3 %collective-permute-done.5.up_ref = f32[6,4,1,1152]{3,2,1,0:T(1,128)S(1)} collective-permute-done((f32[6,4,1,1152]{3,2,1,0:T(1,128)S(1)}, f32[6,4,1,1152]{3,2,1,0:T(1,128)S(1)}, u32[]{:S(2)}, u32[]{:S(2)}) %collective-permute-start.5) | collective-permute-done | bytes 110624 | tf_op jit(solution)/shard_map/ppermute | solution.py:708
  25.8 3.6 %second_step.1 = (f32[1,4,16,1152]{3,2,1,0:T(8,128)S(1)}, f32[1,4,16,1152]{3,2,1,0:T(8,128)S(1)}, f32[7,4,2,1152]{3,2,1,0:T(2,128)S(1)}) custom-call(f32[4,24,128]{2,1,0:T(8,128)S(1)} %copy-done.6, f32[4,16,1152]{2,1,0:T(8,128)S(1)} %copy-done.1, f32[4,16,1152]{2,1,0:T(8,128)S(1)} %copy-done.2, f32[4,16,1152]{2,1,0:T(8,128)S(1)} %copy-done.3, ...), custom_call_target="tpu_custom_call" | custom-call | flops 503316480 | bytes 3538944 | tf_op jit(solution)/shard_map/second_step/pallas_call | solution.py:312
  30.0 1.7 %collective-permute-start.8 = (f32[7,4,2,1152]{3,2,1,0:T(2,128)S(1)}, f32[7,4,2,1152]{3,2,1,0:T(2,128)S(1)}, u32[]{:S(2)}, u32[]{:S(2)}) collective-permute-start(f32[7,4,2,1152]{3,2,1,0:T(2,128)S(1)} %get-tuple-element.49.refs_6_.refs_0_), channel_id=1, source_target_pairs={{0,2},{2,0},{1,3},{3,1},{4,6},{6,4},{5,7},{7,5},{8,10},{10,8},{9,1... | collective-permute-start | bytes 774152 | tf_op jit(solution)/shard_map/ppermute | solution.py:659
  31.7 1.3 %remap_parts.4 = (f32[4,4,16,1152]{3,2,1,0:T(8,128)S(1)}, f32[4,16,1152]{2,1,0:T(8,128)S(1)}) custom-call(f32[16,8,128]{2,1,0:T(8,128)S(1)} %broadcast_in_dim.4.weight_ref, f32[5,4,16,1152]{3,2,1,0:T(8,128)S(1)} %get-tuple-element.40.refs_0_.refs_2_, f32[5,4,16,1152]{3,2,1,0:T(8,128)S(1)} %collective-permute-done.refs_1_.refs_3_, ...), custom_call_target="tpu_custom_call" | custom-call | flops 7667712 | bytes 4423680 | tf_op jit(solution)/shard_map/remap_parts/pallas_call | solution.py:489
  33.4 1.8 %remap_parts.5 = (f32[2,4,16,1152]{3,2,1,0:T(8,128)S(1)}, f32[112,1152]{1,0:T(8,128)S(1)}) custom-call(f32[16,8,128]{2,1,0:T(8,128)S(1)} %broadcast_in_dim.4.weight_ref, f32[5,4,16,1152]{3,2,1,0:T(8,128)S(1)} %get-tuple-element.40.refs_0_.refs_2_, f32[5,4,16,1152]{3,2,1,0:T(8,128)S(1)} %collective-permute-done.refs_1_.refs_3_, ...), custom_call_target="tpu_custom_call" | custom-call | flops 10616832 | bytes 3538944 | tf_op jit(solution)/shard_map/remap_parts/pallas_call | solution.py:489
  35.1 1.6 %collective-permute-start.19 = (f32[112,1152]{1,0:T(8,128)S(1)}, f32[112,1152]{1,0:T(8,128)S(1)}, u32[]{:S(2)}, u32[]{:S(2)}) collective-permute-start(f32[112,1152]{1,0:T(8,128)S(1)} %get-tuple-element.55.refs_16_), channel_id=1, source_target_pairs={{0,2},{2,0},{1,3},{3,1},{4,6},{6,4},{5,7},{7,5},{8,10},{10,8},{9,1... | collective-permute-start | bytes 1548296 | tf_op jit(solution)/shard_map/ppermute | solution.py:659
  37.2 1.9 %collective-permute-done.8.refs_2_ = f32[7,4,2,1152]{3,2,1,0:T(2,128)S(1)} collective-permute-done((f32[7,4,2,1152]{3,2,1,0:T(2,128)S(1)}, f32[7,4,2,1152]{3,2,1,0:T(2,128)S(1)}, u32[]{:S(2)}, u32[]{:S(2)}) %collective-permute-start.8) | collective-permute-done | bytes 258080 | tf_op jit(solution)/shard_map/ppermute | solution.py:659
  39.7 1.1 %collective-permute-done.14.refs_13_ = f32[24,1152]{1,0:T(8,128)S(1)} collective-permute-done((f32[24,1152]{1,0:T(8,128)S(1)}, f32[24,1152]{1,0:T(8,128)S(1)}, u32[]{:S(2)}, u32[]{:S(2)}) %collective-permute-start.14) | collective-permute-done | bytes 110624 | tf_op jit(solution)/shard_map/ppermute | solution.py:661
  41.3 0.8 %collective-permute-done.13.refs_11_ = f32[24,1152]{1,0:T(8,128)S(1)} collective-permute-done((f32[24,1152]{1,0:T(8,128)S(1)}, f32[24,1152]{1,0:T(8,128)S(1)}, u32[]{:S(2)}, u32[]{:S(2)}) %collective-permute-start.13) | collective-permute-done | bytes 110624 | tf_op jit(solution)/shard_map/ppermute | solution.py:661
  42.3 3.7 %remap_edges.1 = (f32[6,4,2,1152]{3,2,1,0:T(2,128)S(1)}, f32[4,2,1152]{2,1,0:T(2,128)S(1)}, f32[4,4,3,1152]{3,2,1,0:T(4,128)S(1)}) custom-call(f32[16,8,128]{2,1,0:T(8,128)S(1)} %broadcast_in_dim.4.weight_ref, f32[7,4,2,1152]{3,2,1,0:T(2,128)S(1)} %get-tuple-element.49.refs_6_.refs_0_, f32[7,4,2,1152]{3,2,1,0:T(2,128)S(1)} %collective-permute-done.7.refs_1_, ...), custom_call_target="tpu_custom_call" | custom-call | flops 5898240 | bytes 4128768 | tf_op jit(solution)/shard_map/remap_edges/pallas_call | solution.py:529
  46.0 1.4 %finish_tracers.1 = (f32[4,4,16,1152]{3,2,1,0:T(8,128)}, f32[4,16,1152]{2,1,0:T(8,128)}, f32[8,128]{1,0:T(8,128)S(1)}) custom-call(f32[4,4,16,1152]{3,2,1,0:T(8,128)S(1)} %get-tuple-element.50.refs_8_.own_ref, f32[4,4,3,1152]{3,2,1,0:T(4,128)S(1)} %get-tuple-element.56.near_ref, f32[6,4,2,1152]{3,2,1,0:T(2,128)S(1)} %get-tuple-element.57.edge_ref, ...), custom_call_target="tpu_custom_call" | custom-call | flops 589824 | bytes 3538944 | tf_op jit(solution)/shard_map/finish_tracers/pallas_call | solution.py:567
  47.4 2.2 %collective-permute-done.19.refs_0_ = f32[112,1152]{1,0:T(8,128)S(1)} collective-permute-done((f32[112,1152]{1,0:T(8,128)S(1)}, f32[112,1152]{1,0:T(8,128)S(1)}, u32[]{:S(2)}, u32[]{:S(2)}) %collective-permute-start.19) | collective-permute-done | bytes 516128 | tf_op jit(solution)/shard_map/ppermute | solution.py:659
  49.7 0.9 %finish_winds.1 = (f32[4,16,1152]{2,1,0:T(8,128)}, f32[4,16,1152]{2,1,0:T(8,128)}) custom-call(f32[2,4,16,1152]{3,2,1,0:T(8,128)S(1)} %get-tuple-element.61.own_ref, f32[6,4,2,1152]{3,2,1,0:T(2,128)S(1)} %get-tuple-element.57.edge_ref, f32[112,1152]{1,0:T(8,128)S(1)} %collective-permute-done.19.refs_0_, f32[8,128]{1,0:T(8,128)S(1)} %get-tuple-element.62.refs_1_), custom_call_target="tpu_custom_call" | custom-call | flops 147456 | bytes 1769472 | tf_op jit(solution)/shard_map/finish_winds/pallas_call | solution.py:597
  (47 shorter events, 3.2 us)
Async XLA Ops:
  2.5 8.2 %collective-permute-start.1 = (f32[32,1152]{1,0:T(8,128)S(1)}, f32[32,1152]{1,0:T(8,128)S(1)}, u32[]{:S(2)}, u32[]{:S(2)}) collective-permute-start(f32[32,1152]{1,0:T(8,128)S(1)} %get-tuple-element.41), channel_id=1, source_target_pairs={{0,2},{2,0},{1,3},{3,1},{4,6},{6,4},{5,7},{7,5},{8,10},{10,8},{9,1... | collective-permute-start | bytes 442376 | tf_op jit(solution)/shard_map/ppermute | solution.py:659
  5.5 5.2 %collective-permute-start.2 = (f32[16,1152]{1,0:T(8,128)S(1)}, f32[16,1152]{1,0:T(8,128)S(1)}, u32[]{:S(2)}, u32[]{:S(2)}) collective-permute-start(f32[16,1152]{1,0:T(8,128)S(1)} %get-tuple-element.42), channel_id=1, source_target_pairs={{0,3},{1,2},{2,1},{3,0},{4,7},{5,6},{6,5},{7,4},{8,11},{9,10},{10,... | collective-permute-start | bytes 221192 | tf_op jit(solution)/shard_map/ppermute | solution.py:667
  7.2 3.6 %collective-permute-start = (f32[5,4,16,1152]{3,2,1,0:T(8,128)S(1)}, f32[5,4,16,1152]{3,2,1,0:T(8,128)S(1)}, u32[]{:S(2)}, u32[]{:S(2)}) collective-permute-start(f32[5,4,16,1152]{3,2,1,0:T(8,128)S(1)} %get-tuple-element.40.refs_0_.refs_2_), channel_id=1, source_target_pairs={{0,1},{1,0},{2,3},{3,2},{4,5},{5,4},{6,7},{7,6},{8,9},{9,8},{10,11... | collective-permute-start | bytes 4423688 | tf_op jit(solution)/shard_map/ppermute | solution.py:661
  7.5 6.5 %collective-permute-start.3 = (f32[24,1152]{1,0:T(8,128)S(1)}, f32[24,1152]{1,0:T(8,128)S(1)}, u32[]{:S(2)}, u32[]{:S(2)}) collective-permute-start(f32[24,1152]{1,0:T(8,128)S(1)} %get-tuple-element.45.refs_8_), channel_id=1, source_target_pairs={{0,2},{2,0},{1,3},{3,1},{4,6},{6,4},{5,7},{7,5},{8,10},{10,8},{9,1... | collective-permute-start | bytes 331784 | tf_op jit(solution)/shard_map/ppermute | solution.py:659
  9.4 6.3 %collective-permute-start.4 = (f32[24,1152]{1,0:T(8,128)S(1)}, f32[24,1152]{1,0:T(8,128)S(1)}, u32[]{:S(2)}, u32[]{:S(2)}) collective-permute-start(f32[24,1152]{1,0:T(8,128)S(1)} %get-tuple-element.46.refs_12_), channel_id=1, source_target_pairs={{0,2},{2,0},{1,3},{3,1},{4,6},{6,4},{5,7},{7,5},{8,10},{10,8},{9,1... | collective-permute-start | bytes 331784 | tf_op jit(solution)/shard_map/ppermute | solution.py:659
  12.3 13.4 %copy-start = (f32[4,4,16,1152]{3,2,1,0:T(8,128)S(1)}, f32[4,4,16,1152]{3,2,1,0:T(8,128)}, u32[]{:S(2)}) copy-start(f32[4,4,16,1152]{3,2,1,0:T(8,128)} %tracer_ref.1) | copy-start | bytes 3538948
  12.3 13.4 %copy-start.1 = (f32[4,16,1152]{2,1,0:T(8,128)S(1)}, f32[4,16,1152]{2,1,0:T(8,128)}, u32[]{:S(2)}) copy-start(f32[4,16,1152]{2,1,0:T(8,128)} %thick_ref.1) | copy-start | bytes 884740
  12.3 13.4 %copy-start.2 = (f32[4,16,1152]{2,1,0:T(8,128)S(1)}, f32[4,16,1152]{2,1,0:T(8,128)}, u32[]{:S(2)}) copy-start(f32[4,16,1152]{2,1,0:T(8,128)} %u_ref.1) | copy-start | bytes 884740
  12.3 13.4 %copy-start.3 = (f32[4,16,1152]{2,1,0:T(8,128)S(1)}, f32[4,16,1152]{2,1,0:T(8,128)}, u32[]{:S(2)}) copy-start(f32[4,16,1152]{2,1,0:T(8,128)} %v_ref.1) | copy-start | bytes 884740
  12.4 21.0 %collective-permute-start.18 = (f32[176,1152]{1,0:T(8,128)S(1)}, f32[176,1152]{1,0:T(8,128)S(1)}, u32[]{:S(2)}, u32[]{:S(2)}) collective-permute-start(f32[176,1152]{1,0:T(8,128)S(1)} %remap_parts.3.refs_0_), channel_id=1, source_target_pairs={{0,2},{2,0},{1,3},{3,1},{4,6},{6,4},{5,7},{7,5},{8,10},{10,8},{9,1... | collective-permute-start | bytes 2433032 | tf_op jit(solution)/shard_map/ppermute | solution.py:659
  17.5 8.2 %collective-permute-start.6 = (f32[8,4,1,1152]{3,2,1,0:T(1,128)S(1)}, f32[8,4,1,1152]{3,2,1,0:T(1,128)S(1)}, u32[]{:S(2)}, u32[]{:S(2)}) collective-permute-start(f32[8,4,1,1152]{3,2,1,0:T(1,128)S(1)} %get-tuple-element.48), channel_id=1, source_target_pairs={{4,0},{8,4},{12,8},{5,1},{9,5},{13,9},{6,2},{10,6},{14,10},{7,3},{... | collective-permute-start | bytes 442376 | tf_op jit(solution)/shard_map/ppermute | solution.py:709
  18.8 6.9 %collective-permute-start.5 = (f32[6,4,1,1152]{3,2,1,0:T(1,128)S(1)}, f32[6,4,1,1152]{3,2,1,0:T(1,128)S(1)}, u32[]{:S(2)}, u32[]{:S(2)}) collective-permute-start(f32[6,4,1,1152]{3,2,1,0:T(1,128)S(1)} %get-tuple-element.47), channel_id=1, source_target_pairs={{0,4},{4,8},{8,12},{1,5},{5,9},{9,13},{2,6},{6,10},{10,14},{3,7},{... | collective-permute-start | bytes 331784 | tf_op jit(solution)/shard_map/ppermute | solution.py:708
  29.4 3.6 %collective-permute-start.16 = (f32[1,4,16,1152]{3,2,1,0:T(8,128)S(1)}, f32[1,4,16,1152]{3,2,1,0:T(8,128)S(1)}, u32[]{:S(2)}, u32[]{:S(2)}) collective-permute-start(f32[1,4,16,1152]{3,2,1,0:T(8,128)S(1)} %get-tuple-element.53.refs_2_), channel_id=1, source_target_pairs={{0,1},{1,0},{2,3},{3,2},{4,5},{5,4},{6,7},{7,6},{8,9},{9,8},{10,11... | collective-permute-start | bytes 884744 | tf_op jit(solution)/shard_map/ppermute | solution.py:661
  29.5 3.6 %collective-permute-start.17 = (f32[1,4,16,1152]{3,2,1,0:T(8,128)S(1)}, f32[1,4,16,1152]{3,2,1,0:T(8,128)S(1)}, u32[]{:S(2)}, u32[]{:S(2)}) collective-permute-start(f32[1,4,16,1152]{3,2,1,0:T(8,128)S(1)} %get-tuple-element.54.refs_4_), channel_id=1, source_target_pairs={{0,1},{1,0},{2,3},{3,2},{4,5},{5,4},{6,7},{7,6},{8,9},{9,8},{10,11... | collective-permute-start | bytes 884744 | tf_op jit(solution)/shard_map/ppermute | solution.py:661
  30.0 9.2 %collective-permute-start.8 = (f32[7,4,2,1152]{3,2,1,0:T(2,128)S(1)}, f32[7,4,2,1152]{3,2,1,0:T(2,128)S(1)}, u32[]{:S(2)}, u32[]{:S(2)}) collective-permute-start(f32[7,4,2,1152]{3,2,1,0:T(2,128)S(1)} %get-tuple-element.49.refs_6_.refs_0_), channel_id=1, source_target_pairs={{0,2},{2,0},{1,3},{3,1},{4,6},{6,4},{5,7},{7,5},{8,10},{10,8},{9,1... | collective-permute-start | bytes 774152 | tf_op jit(solution)/shard_map/ppermute | solution.py:659
  35.1 14.5 %collective-permute-start.19 = (f32[112,1152]{1,0:T(8,128)S(1)}, f32[112,1152]{1,0:T(8,128)S(1)}, u32[]{:S(2)}, u32[]{:S(2)}) collective-permute-start(f32[112,1152]{1,0:T(8,128)S(1)} %get-tuple-element.55.refs_16_), channel_id=1, source_target_pairs={{0,2},{2,0},{1,3},{3,1},{4,6},{6,4},{5,7},{7,5},{8,10},{10,8},{9,1... | collective-permute-start | bytes 1548296 | tf_op jit(solution)/shard_map/ppermute | solution.py:659
  36.7 2.4 %collective-permute-start.10 = (f32[1,4,3,1152]{3,2,1,0:T(4,128)S(1)}, f32[1,4,3,1152]{3,2,1,0:T(4,128)S(1)}, u32[]{:S(2)}, u32[]{:S(2)}) collective-permute-start(f32[1,4,3,1152]{3,2,1,0:T(4,128)S(1)} %get-tuple-element.51.refs_4_), channel_id=1, source_target_pairs={{0,1},{1,0},{2,3},{3,2},{4,5},{5,4},{6,7},{7,6},{8,9},{9,8},{10,11... | collective-permute-start | bytes 165896 | tf_op jit(solution)/shard_map/ppermute | solution.py:661
  36.7 2.9 %collective-permute-start.12 = (f32[24,1152]{1,0:T(8,128)S(1)}, f32[24,1152]{1,0:T(8,128)S(1)}, u32[]{:S(2)}, u32[]{:S(2)}) collective-permute-start(f32[24,1152]{1,0:T(8,128)S(1)} %get-tuple-element.45.refs_8_), channel_id=1, source_target_pairs={{0,1},{1,0},{2,3},{3,2},{4,5},{5,4},{6,7},{7,6},{8,9},{9,8},{10,11... | collective-permute-start | bytes 331784 | tf_op jit(solution)/shard_map/ppermute | solution.py:661
  37.2 5.1 %collective-permute-start.7 = (f32[7,4,2,1152]{3,2,1,0:T(2,128)S(1)}, f32[7,4,2,1152]{3,2,1,0:T(2,128)S(1)}, u32[]{:S(2)}, u32[]{:S(2)}) collective-permute-start(f32[7,4,2,1152]{3,2,1,0:T(2,128)S(1)} %get-tuple-element.49.refs_6_.refs_0_), channel_id=1, source_target_pairs={{0,1},{1,0},{2,3},{3,2},{4,5},{5,4},{6,7},{7,6},{8,9},{9,8},{10,11... | collective-permute-start | bytes 774152 | tf_op jit(solution)/shard_map/ppermute | solution.py:661
  39.1 3.2 %collective-permute-start.9 = (f32[7,4,2,1152]{3,2,1,0:T(2,128)S(1)}, f32[7,4,2,1152]{3,2,1,0:T(2,128)S(1)}, u32[]{:S(2)}, u32[]{:S(2)}) collective-permute-start(f32[7,4,2,1152]{3,2,1,0:T(2,128)S(1)} %collective-permute-done.8.refs_2_), channel_id=1, source_target_pairs={{0,1},{1,0},{2,3},{3,2},{4,5},{5,4},{6,7},{7,6},{8,9},{9,8},{10,11... | collective-permute-start | bytes 774152 | tf_op jit(solution)/shard_map/ppermute | solution.py:661
  39.1 1.7 %collective-permute-start.14 = (f32[24,1152]{1,0:T(8,128)S(1)}, f32[24,1152]{1,0:T(8,128)S(1)}, u32[]{:S(2)}, u32[]{:S(2)}) collective-permute-start(f32[24,1152]{1,0:T(8,128)S(1)} %get-tuple-element.46.refs_12_), channel_id=1, source_target_pairs={{0,1},{1,0},{2,3},{3,2},{4,5},{5,4},{6,7},{7,6},{8,9},{9,8},{10,11... | collective-permute-start | bytes 331784 | tf_op jit(solution)/shard_map/ppermute | solution.py:661
  39.6 1.3 %collective-permute-start.11 = (f32[1,4,3,1152]{3,2,1,0:T(4,128)S(1)}, f32[1,4,3,1152]{3,2,1,0:T(4,128)S(1)}, u32[]{:S(2)}, u32[]{:S(2)}) collective-permute-start(f32[1,4,3,1152]{3,2,1,0:T(4,128)S(1)} %get-tuple-element.52.refs_6_), channel_id=1, source_target_pairs={{0,1},{1,0},{2,3},{3,2},{4,5},{5,4},{6,7},{7,6},{8,9},{9,8},{10,11... | collective-permute-start | bytes 165896 | tf_op jit(solution)/shard_map/ppermute | solution.py:661
  40.8 1.3 %collective-permute-start.13 = (f32[24,1152]{1,0:T(8,128)S(1)}, f32[24,1152]{1,0:T(8,128)S(1)}, u32[]{:S(2)}, u32[]{:S(2)}) collective-permute-start(f32[24,1152]{1,0:T(8,128)S(1)} %collective-permute-done.3.refs_1_.refs_10_), channel_id=1, source_target_pairs={{0,1},{1,0},{2,3},{3,2},{4,5},{5,4},{6,7},{7,6},{8,9},{9,8},{10,11... | collective-permute-start | bytes 331784 | tf_op jit(solution)/shard_map/ppermute | solution.py:661
  41.0 1.3 %collective-permute-start.15 = (f32[24,1152]{1,0:T(8,128)S(1)}, f32[24,1152]{1,0:T(8,128)S(1)}, u32[]{:S(2)}, u32[]{:S(2)}) collective-permute-start(f32[24,1152]{1,0:T(8,128)S(1)} %collective-permute-done.4.refs_2_.refs_14_), channel_id=1, source_target_pairs={{0,1},{1,0},{2,3},{3,2},{4,5},{5,4},{6,7},{7,6},{8,9},{9,8},{10,11... | collective-permute-start | bytes 331784 | tf_op jit(solution)/shard_map/ppermute | solution.py:661
  (5 other events, 46.5 us)

commit v13 on v12

--- a/solution.py
+++ b/solution.py
@@ -26,7 +26,7 @@
 
 
 def near_rows(rows):
-    return (1, 2, rows - 2), (3, 2)
+    return (1, 2, rows - 3, rows - 2), (3, 3)
 
 
 def geometry_table(lat_rows, band_rows):
@@ -83,7 +83,7 @@
 
 
 def first_kernel(table_hbm, thick_hbm, u_hbm, v_hbm, tracer_hbm, *refs):
-    new_ref, sum_ref, both_ref, near_ref, thick_ref, u_ref, v_ref, tracer_ref, geo_ref, sems = refs
+    new_ref, both_ref, near_ref, thick_ref, u_ref, v_ref, tracer_ref, geo_ref, sems = refs
     L, rows, _ = thick_ref.shape
     near, _ = near_rows(rows)
     table_copy = pltpu.make_async_copy(table_hbm.at[lax.axis_index("lat")], geo_ref, sems.at[3, 0])
@@ -100,7 +100,7 @@
     tracer_copy.start()
     table_copy.wait()
     geo = geo_ref[...]
-    sum_ref[...] = jnp.zeros_like(sum_ref)
+    both_ref[...] = jnp.zeros_like(both_ref)
 
     def level(k, carry):
         for copy in copies(k):
@@ -111,11 +111,10 @@
         new_ref[k] = new
         for j, row in enumerate(near):
             near_ref[0, k, j : j + 1] = new[row : row + 1]
-        sum_ref[...] += new
+        both_ref[0:rows] += new
         return carry
 
     lax.fori_loop(0, L, level, 0)
-    both_ref[0:rows] = sum_ref[...]
     for k in range(L):
         at = rows + k * len(near)
         both_ref[at : at + len(near)] = near_ref[0, k]
@@ -127,7 +126,7 @@
     arguments = (thickness, wind_u, wind_v, tracers)
     operands = [pltpu.with_memory_space_constraint(a, pltpu.HBM) for a in (table, *arguments)]
     near = len(near_rows(R)[0])
-    shapes = [(L, R, N), (R, N), (-(-(R + L * near) // 8) * 8, N), (1, L, near, N)] + [a.shape for a in arguments]
+    shapes = [(L, R, N), (-(-(R + L * near) // 8) * 8, N), (1, L, near, N)] + [a.shape for a in arguments]
     return pl.pallas_call(
         first_kernel,
         in_specs=after(operands),
@@ -330,36 +329,52 @@
     )
 
 
+def part_kernel(both_ref, *refs):
+    sum_ref, near_ref = refs[-2:]
+    rows = sum_ref.shape[0]
+    sum_ref[...] = both_ref[0:rows]
+    _, L, near, _ = near_ref.shape
+    for k in range(L):
+        near_ref[0, k] = both_ref[rows + k * near : rows + (k + 1) * near]
+
+
+def part(both, shape, wait):
+    L, R, N = shape
+    return pl.pallas_call(
+        part_kernel,
+        in_specs=[VMEM] + after(wait),
+        out_specs=[VMEM] * 2,
+        out_shape=[
+            jax.ShapeDtypeStruct((R, N), jnp.float32),
+            jax.ShapeDtypeStruct((1, L, len(near_rows(R)[0]), N), jnp.float32),
+        ],
+        compiler_params=params(),
+        cost_estimate=cost(1e11, 1e9),
+        name="part",
+    )(both, *wait)
+
+
 def mass_kernel(C, S, *refs):
-    other_refs, (base_ref, mass_ref, *near_refs) = refs[: (C - 1) * S], refs[(C - 1) * S :]
-    rows = base_ref.shape[0]
+    other_refs, (base_ref, mass_ref) = refs[: (C - 1) * S], refs[(C - 1) * S :]
     lev = lax.axis_index("lev")
     others_mass, base = None, None
     for s in range(1, C):
-        first, *rest = other_refs[(s - 1) * S : s * S]
-        other = functools.reduce(jnp.add, [first[0:rows]] + [ref[...] for ref in rest])
+        other = functools.reduce(jnp.add, [ref[...] for ref in other_refs[(s - 1) * S : s * S]])
         below = jnp.where(lev >= s, other, 0.0)
         others_mass = other if others_mass is None else others_mass + other
         base = below if base is None else base + below
-        _, L, near, _ = near_refs[s - 1].shape
-        for k in range(L):
-            near_refs[s - 1][0, k] = first[rows + k * near : rows + (k + 1) * near]
     base_ref[...] = base
     mass_ref[...] = others_mass
 
 
-def other_chips(counts, others, levels):
-    C, S = counts
-    R, N = others[1].shape
-    near = len(near_rows(R)[0])
-    return pl.pallas_call(
-        functools.partial(mass_kernel, C, S),
+def other_chips(counts, others):
+    return pl.pallas_call(
+        functools.partial(mass_kernel, *counts),
         in_specs=[VMEM] * len(others),
-        out_specs=[VMEM] * (1 + C),
-        out_shape=[jax.ShapeDtypeStruct((R, N), jnp.float32)] * 2
-        + [jax.ShapeDtypeStruct((1, levels, near, N), jnp.float32)] * (C - 1),
-        compiler_params=params(),
-        cost_estimate=cost(1e11, 1e9),
+        out_specs=[VMEM] * 2,
+        out_shape=[jax.ShapeDtypeStruct(others[0].shape, jnp.float32)] * 2,
+        compiler_params=params(),
+        cost_estimate=cost(1, 1),
         name="other_chips",
     )(*others)
 
@@ -689,15 +704,15 @@
 
     remap = functools.partial(remap_parts, (C, S), weights)
 
-    new, own_sum, own_both, near_new, *arguments = first_step(table, thickness, wind_u, wind_v, tracers)
-    others = [send(own_sum if t else own_both, s=s, t=t) for s in away for t in range(S)]
+    new, both, near_new, *arguments = first_step(table, thickness, wind_u, wind_v, tracers)
+    both = [send(both, s=s, t=0) for s in away]
     inner, near, near_rest = inner_step(table, new, *arguments)
     group = with_others_of_chip(inner)
     near = [near] + [send(near, s=s, t=0) for s in away]
     near_rest = [near_rest] + [send(near_rest, s=s, t=0) for s in away]
-    base, rest_mass, *near_arrived = other_chips((C, S), others, L)
-    others = [base, rest_mass]
-    near_new = [near_new, *near_arrived]
+    parted = [part(each, (L, R, N), [near[0]]) for each in both]
+    near_new = [near_new] + [each[1] for each in parted]
+    others = other_chips((C, S), [a for each in parted for a in with_others_of_chip(each[0])])
     tracer_fields = [(0, 1 + c) for c in range(T)]
     away_parts = remap(group, [group], others, tracer_fields, away, near_rows(R)[1])
     arrived = sent(away_parts)

time: 50.8 us -> 51.6 us (1.016)
  waiting for transfers between devices: 11.9 us -> 13.8 us
  Pallas kernels: 19.5 us -> 18.7 us
    ppermute x11 -> x12, waiting for transfers between devices: 2.08 us -> 4.51 us  [shifted(): lax.ppermute(value, 'sub', [(i, (i + t) % sub_count) for i in range(sub_c...]
    ppermute x1 -> x0, waiting for transfers between devices: 1.24 us -> none  [shifted(): return lax.ppermute(value, ('lev', 'sub'), pairs)]
    ppermute x6, waiting for transfers between devices: 6.25 us -> 7.02 us  [shifted(): lax.ppermute(value, 'lev', [(i, (i + s) % lev_count) for i in range(lev_c...]
    ppermute x11 -> x12, starting transfers between devices: 2.43 us -> 2.25 us  [shifted(): lax.ppermute(value, 'sub', [(i, (i + t) % sub_count) for i in range(sub_c...]
  transfers between devices with their start and end apart: 20 -> 20, of which waited for: 9 -> 10; matrix products, arithmetic and copies ran while one was open for 0% -> 0% of each run, Pallas kernels for 33% -> 31%
where the time goes in v13:
time: 51.6 us; the launch traced here: 51.4 us
  Pallas kernels  18.7 us (36%)
  starting transfers between devices  17.7 us (34%)
  waiting for transfers between devices  13.8 us (27%)
  between operations  0.88 us (2%)
    ppermute x6, starting transfers between devices, shifted(): lax.ppermute(value, 'lev', [(i, (i + s) % lev_count) for i in range(lev_c...  9.61 us
    ppermute x6, waiting for transfers between devices, shifted(): lax.ppermute(value, 'lev', [(i, (i + s) % lev_count) for i in range(lev_c...  7.02 us
    ppermute x1, starting transfers between devices, per_device(): up = lax.ppermute(last, 'lat', northward)  4.55 us
    ppermute x12, waiting for transfers between devices, shifted(): lax.ppermute(value, 'sub', [(i, (i + t) % sub_count) for i in range(sub_c...  4.51 us
    pallas_call x3, Pallas kernels, remap_parts(): pl.pallas_call(functools.partial(remap_kernel, counts, tuple(steps), tupl...  4.46 us
    pallas_call x1, Pallas kernels, second_step(): pl.pallas_call(functools.partial(second_kernel, lat_rows), grid=(L,), in_...  3.62 us
    pallas_call x1, Pallas kernels, remap_edges(): pl.pallas_call(functools.partial(remap_edge_kernel, counts, near_fields),...  3.22 us
    ppermute x1, waiting for transfers between devices, per_device(): up = lax.ppermute(last, 'lat', northward)  2.3 us
  transfers between devices with their start and end apart: 20, of which 10 were waited for; matrix products, arithmetic and copies ran while one was open for 0% of the time, Pallas kernels for 31%

profile of v13, /device:TPU:0, one launch (start us, length us, event | category | flops | bytes accessed | tf_op | source)
XLA Modules:
  0.0 51.4 jit_solution(9535556355573077051)
XLA Ops:
  0.6 1.9 %first_step.1 = (f32[4,16,1152]{2,1,0:T(8,128)S(1)}, f32[32,1152]{1,0:T(8,128)S(1)}, f32[1,4,4,1152]{3,2,1,0:T(4,128)S(1)}, f32[4,16,1152]{2,1,0:T(8,128)S(1)}, ...) custom-call(f32[4,24,128]{2,1,0:T(8,128)} %constant.6.clone.table_hbm.table_ref, ...), custom_call_target="tpu_custom_call" | custom-call | flops 2949120 | bytes 4423680 | tf_op jit(solution)/shard_map/first_step/pallas_call | solution.py:130
  2.5 3.0 %collective-permute-start.1 = (f32[32,1152]{1,0:T(8,128)S(1)}, f32[32,1152]{1,0:T(8,128)S(1)}, u32[]{:S(2)}, u32[]{:S(2)}) collective-permute-start(f32[32,1152]{1,0:T(8,128)S(1)} %get-tuple-element.41), channel_id=1, source_target_pairs={{0,2},{2,0},{1,3},{3,1},{4,6},{6,4},{5,7},{7,5},{8,10},{10,8},{9,1... | collective-permute-start | bytes 442376 | tf_op jit(solution)/shard_map/ppermute | solution.py:674
  5.5 1.5 %inner_step.1 = (f32[5,4,16,1152]{3,2,1,0:T(8,128)S(1)}, f32[32,1152]{1,0:T(8,128)S(1)}, f32[32,1152]{1,0:T(8,128)S(1)}) custom-call(f32[4,24,128]{2,1,0:T(8,128)S(1)} %copy-done.6, f32[4,16,1152]{2,1,0:T(8,128)S(1)} %get-tuple-element.35.new_ref, f32[4,16,1152]{2,1,0:T(8,128)S(1)} %get-tuple-element.36.thick_ref, ...), custom_call_target="tpu_custom_call" | custom-call | flops 9584640 | bytes 4718592 | tf_op jit(solution)/shard_map/inner_step/pallas_call | solution.py:173
  7.2 2.0 %collective-permute-start.4 = (f32[32,1152]{1,0:T(8,128)S(1)}, f32[32,1152]{1,0:T(8,128)S(1)}, u32[]{:S(2)}, u32[]{:S(2)}) collective-permute-start(f32[32,1152]{1,0:T(8,128)S(1)} %get-tuple-element.46.refs_12_), channel_id=1, source_target_pairs={{0,2},{2,0},{1,3},{3,1},{4,6},{6,4},{5,7},{7,5},{8,10},{10,8},{9,1... | collective-permute-start | bytes 442376 | tf_op jit(solution)/shard_map/ppermute | solution.py:674
  9.5 1.3 %collective-permute-done.2.refs_1_ = f32[16,1152]{1,0:T(8,128)S(1)} collective-permute-done((f32[16,1152]{1,0:T(8,128)S(1)}, f32[16,1152]{1,0:T(8,128)S(1)}, u32[]{:S(2)}, u32[]{:S(2)}) %collective-permute-start.2) | collective-permute-done | bytes 73760 | tf_op jit(solution)/shard_map/ppermute | solution.py:676
  10.8 1.4 %remap_parts.3.refs_0_ = f32[160,1152]{1,0:T(8,128)S(1)} custom-call(f32[16,8,128]{2,1,0:T(8,128)S(1)} %broadcast_in_dim.4.weight_ref, f32[5,4,16,1152]{3,2,1,0:T(8,128)S(1)} %get-tuple-element.40.refs_0_.refs_2_, f32[5,4,16,1152]{3,2,1,0:T(8,128)S(1)} %collective-permute-done.refs_1_.refs_3_, f32[5,4,16,1152]{3,2,1,0:T(8,128)S(1)} %get-tuple-element.40.refs_0_.refs_2_, ...), custom_call_target="tpu_custom_call" | custom-call | flops 7667712 | bytes 4423680 | tf_op jit(solution)/shard_map/remap_parts/pallas_call | solution.py:504
  12.3 2.4 %collective-permute-start.18 = (f32[160,1152]{1,0:T(8,128)S(1)}, f32[160,1152]{1,0:T(8,128)S(1)}, u32[]{:S(2)}, u32[]{:S(2)}) collective-permute-start(f32[160,1152]{1,0:T(8,128)S(1)} %remap_parts.3.refs_0_), channel_id=1, source_target_pairs={{0,2},{2,0},{1,3},{3,1},{4,6},{6,4},{5,7},{7,5},{8,10},{10,8},{9,1... | collective-permute-start | bytes 2211848 | tf_op jit(solution)/shard_map/ppermute | solution.py:674
  14.7 2.2 %collective-permute-done.4.refs_2_.refs_14_ = f32[32,1152]{1,0:T(8,128)S(1)} collective-permute-done((f32[32,1152]{1,0:T(8,128)S(1)}, f32[32,1152]{1,0:T(8,128)S(1)}, u32[]{:S(2)}, u32[]{:S(2)}) %collective-permute-start.4) | collective-permute-done | bytes 147488 | tf_op jit(solution)/shard_map/ppermute | solution.py:674
  16.9 1.7 %edge_rows.1 = (f32[6,4,1,1152]{3,2,1,0:T(1,128)S(1)}, f32[8,4,1,1152]{3,2,1,0:T(1,128)S(1)}) custom-call(f32[4,16,1152]{2,1,0:T(8,128)} %thick_ref.1, f32[4,16,1152]{2,1,0:T(8,128)} %u_ref.1, f32[4,16,1152]{2,1,0:T(8,128)} %v_ref.1, f32[4,4,16,1152]{3,2,1,0:T(8,128)} %tracer_ref.1, f32[160,1152]{1,0:T(8,128)S(1)} %remap_parts.3.refs_0_, ...), custom_call_target="tpu_custom_call" | custom-call | flops 10000000000 | bytes 1000000000 | tf_op jit(solution)/shard_map/edge_rows/pallas_call | solution.py:652
  18.7 1.3 %collective-permute-start.6 = (f32[8,4,1,1152]{3,2,1,0:T(1,128)S(1)}, f32[8,4,1,1152]{3,2,1,0:T(1,128)S(1)}, u32[]{:S(2)}, u32[]{:S(2)}) collective-permute-start(f32[8,4,1,1152]{3,2,1,0:T(1,128)S(1)} %get-tuple-element.48), channel_id=1, source_target_pairs={{4,0},{8,4},{12,8},{5,1},{9,5},{13,9},{6,2},{10,6},{14,10},{7,3},{... | collective-permute-start | bytes 442376 | tf_op jit(solution)/shard_map/ppermute | solution.py:724
  20.0 4.6 %collective-permute-start.5 = (f32[6,4,1,1152]{3,2,1,0:T(1,128)S(1)}, f32[6,4,1,1152]{3,2,1,0:T(1,128)S(1)}, u32[]{:S(2)}, u32[]{:S(2)}) collective-permute-start(f32[6,4,1,1152]{3,2,1,0:T(1,128)S(1)} %get-tuple-element.47), channel_id=1, source_target_pairs={{0,4},{4,8},{8,12},{1,5},{5,9},{9,13},{2,6},{6,10},{10,14},{3,7},{... | collective-permute-start | bytes 331784 | tf_op jit(solution)/shard_map/ppermute | solution.py:723
  24.5 2.3 %collective-permute-done.5.up_ref = f32[6,4,1,1152]{3,2,1,0:T(1,128)S(1)} collective-permute-done((f32[6,4,1,1152]{3,2,1,0:T(1,128)S(1)}, f32[6,4,1,1152]{3,2,1,0:T(1,128)S(1)}, u32[]{:S(2)}, u32[]{:S(2)}) %collective-permute-start.5) | collective-permute-done | bytes 110624 | tf_op jit(solution)/shard_map/ppermute | solution.py:723
  27.0 3.6 %second_step.1 = (f32[1,4,16,1152]{3,2,1,0:T(8,128)S(1)}, f32[1,4,16,1152]{3,2,1,0:T(8,128)S(1)}, f32[7,4,2,1152]{3,2,1,0:T(2,128)S(1)}) custom-call(f32[4,24,128]{2,1,0:T(8,128)S(1)} %copy-done.6, f32[4,16,1152]{2,1,0:T(8,128)S(1)} %copy-done.1, f32[4,16,1152]{2,1,0:T(8,128)S(1)} %copy-done.2, f32[4,16,1152]{2,1,0:T(8,128)S(1)} %copy-done.3, ...), custom_call_target="tpu_custom_call" | custom-call | flops 503316480 | bytes 3538944 | tf_op jit(solution)/shard_map/second_step/pallas_call | solution.py:311
  31.6 1.3 %remap_parts.4 = (f32[4,4,16,1152]{3,2,1,0:T(8,128)S(1)}, f32[4,16,1152]{2,1,0:T(8,128)S(1)}) custom-call(f32[16,8,128]{2,1,0:T(8,128)S(1)} %broadcast_in_dim.4.weight_ref, f32[5,4,16,1152]{3,2,1,0:T(8,128)S(1)} %get-tuple-element.40.refs_0_.refs_2_, f32[5,4,16,1152]{3,2,1,0:T(8,128)S(1)} %collective-permute-done.refs_1_.refs_3_, ...), custom_call_target="tpu_custom_call" | custom-call | flops 7667712 | bytes 4423680 | tf_op jit(solution)/shard_map/remap_parts/pallas_call | solution.py:504
  33.0 1.8 %remap_parts.5 = (f32[2,4,16,1152]{3,2,1,0:T(8,128)S(1)}, f32[112,1152]{1,0:T(8,128)S(1)}) custom-call(f32[16,8,128]{2,1,0:T(8,128)S(1)} %broadcast_in_dim.4.weight_ref, f32[5,4,16,1152]{3,2,1,0:T(8,128)S(1)} %get-tuple-element.40.refs_0_.refs_2_, f32[5,4,16,1152]{3,2,1,0:T(8,128)S(1)} %collective-permute-done.refs_1_.refs_3_, ...), custom_call_target="tpu_custom_call" | custom-call | flops 10616832 | bytes 3538944 | tf_op jit(solution)/shard_map/remap_parts/pallas_call | solution.py:504
  34.8 1.6 %collective-permute-start.19 = (f32[112,1152]{1,0:T(8,128)S(1)}, f32[112,1152]{1,0:T(8,128)S(1)}, u32[]{:S(2)}, u32[]{:S(2)}) collective-permute-start(f32[112,1152]{1,0:T(8,128)S(1)} %get-tuple-element.55.refs_16_), channel_id=1, source_target_pairs={{0,2},{2,0},{1,3},{3,1},{4,6},{6,4},{5,7},{7,5},{8,10},{10,8},{9,1... | collective-permute-start | bytes 1548296 | tf_op jit(solution)/shard_map/ppermute | solution.py:674
  36.9 1.0 %collective-permute-done.10.refs_5_ = f32[1,4,4,1152]{3,2,1,0:T(4,128)S(1)} collective-permute-done((f32[1,4,4,1152]{3,2,1,0:T(4,128)S(1)}, f32[1,4,4,1152]{3,2,1,0:T(4,128)S(1)}, u32[]{:S(2)}, u32[]{:S(2)}) %collective-permute-start.10) | collective-permute-done | bytes 73760 | tf_op jit(solution)/shard_map/ppermute | solution.py:676
  38.2 2.1 %collective-permute-done.8.refs_2_ = f32[7,4,2,1152]{3,2,1,0:T(2,128)S(1)} collective-permute-done((f32[7,4,2,1152]{3,2,1,0:T(2,128)S(1)}, f32[7,4,2,1152]{3,2,1,0:T(2,128)S(1)}, u32[]{:S(2)}, u32[]{:S(2)}) %collective-permute-start.8) | collective-permute-done | bytes 258080 | tf_op jit(solution)/shard_map/ppermute | solution.py:674
  40.8 1.0 %collective-permute-done.11.refs_7_ = f32[1,4,4,1152]{3,2,1,0:T(4,128)S(1)} collective-permute-done((f32[1,4,4,1152]{3,2,1,0:T(4,128)S(1)}, f32[1,4,4,1152]{3,2,1,0:T(4,128)S(1)}, u32[]{:S(2)}, u32[]{:S(2)}) %collective-permute-start.11) | collective-permute-done | bytes 73760 | tf_op jit(solution)/shard_map/ppermute | solution.py:676
  42.1 1.1 %collective-permute-done.15.refs_15_ = f32[32,1152]{1,0:T(8,128)S(1)} collective-permute-done((f32[32,1152]{1,0:T(8,128)S(1)}, f32[32,1152]{1,0:T(8,128)S(1)}, u32[]{:S(2)}, u32[]{:S(2)}) %collective-permute-start.15) | collective-permute-done | bytes 147488 | tf_op jit(solution)/shard_map/ppermute | solution.py:676
  43.2 3.2 %remap_edges.1 = (f32[6,4,2,1152]{3,2,1,0:T(2,128)S(1)}, f32[4,2,1152]{2,1,0:T(2,128)S(1)}, f32[4,4,4,1152]{3,2,1,0:T(4,128)S(1)}) custom-call(f32[16,8,128]{2,1,0:T(8,128)S(1)} %broadcast_in_dim.4.weight_ref, f32[7,4,2,1152]{3,2,1,0:T(2,128)S(1)} %get-tuple-element.49.refs_6_.refs_0_, f32[7,4,2,1152]{3,2,1,0:T(2,128)S(1)} %collective-permute-done.7.refs_1_, ...), custom_call_target="tpu_custom_call" | custom-call | flops 5898240 | bytes 4128768 | tf_op jit(solution)/shard_map/remap_edges/pallas_call | solution.py:544
  46.5 1.4 %finish_tracers.1 = (f32[4,4,16,1152]{3,2,1,0:T(8,128)}, f32[4,16,1152]{2,1,0:T(8,128)}, f32[8,128]{1,0:T(8,128)S(1)}) custom-call(f32[4,4,16,1152]{3,2,1,0:T(8,128)S(1)} %get-tuple-element.50.refs_8_.own_ref, f32[4,4,4,1152]{3,2,1,0:T(4,128)S(1)} %get-tuple-element.56.near_ref, f32[6,4,2,1152]{3,2,1,0:T(2,128)S(1)} %get-tuple-element.57.edge_ref, ...), custom_call_target="tpu_custom_call" | custom-call | flops 589824 | bytes 3538944 | tf_op jit(solution)/shard_map/finish_tracers/pallas_call | solution.py:582
  47.9 2.5 %collective-permute-done.19.refs_0_ = f32[112,1152]{1,0:T(8,128)S(1)} collective-permute-done((f32[112,1152]{1,0:T(8,128)S(1)}, f32[112,1152]{1,0:T(8,128)S(1)}, u32[]{:S(2)}, u32[]{:S(2)}) %collective-permute-start.19) | collective-permute-done | bytes 516128 | tf_op jit(solution)/shard_map/ppermute | solution.py:674
  50.4 0.9 %finish_winds.1 = (f32[4,16,1152]{2,1,0:T(8,128)}, f32[4,16,1152]{2,1,0:T(8,128)}) custom-call(f32[2,4,16,1152]{3,2,1,0:T(8,128)S(1)} %get-tuple-element.61.own_ref, f32[6,4,2,1152]{3,2,1,0:T(2,128)S(1)} %get-tuple-element.57.edge_ref, f32[112,1152]{1,0:T(8,128)S(1)} %collective-permute-done.19.refs_0_, f32[8,128]{1,0:T(8,128)S(1)} %get-tuple-element.62.refs_1_), custom_call_target="tpu_custom_call" | custom-call | flops 147456 | bytes 1769472 | tf_op jit(solution)/shard_map/finish_winds/pallas_call | solution.py:612
  (48 shorter events, 3.4 us)
Async XLA Ops:
  2.5 6.9 %collective-permute-start.1 = (f32[32,1152]{1,0:T(8,128)S(1)}, f32[32,1152]{1,0:T(8,128)S(1)}, u32[]{:S(2)}, u32[]{:S(2)}) collective-permute-start(f32[32,1152]{1,0:T(8,128)S(1)} %get-tuple-element.41), channel_id=1, source_target_pairs={{0,2},{2,0},{1,3},{3,1},{4,6},{6,4},{5,7},{7,5},{8,10},{10,8},{9,1... | collective-permute-start | bytes 442376 | tf_op jit(solution)/shard_map/ppermute | solution.py:674
  7.0 3.8 %collective-permute-start = (f32[5,4,16,1152]{3,2,1,0:T(8,128)S(1)}, f32[5,4,16,1152]{3,2,1,0:T(8,128)S(1)}, u32[]{:S(2)}, u32[]{:S(2)}) collective-permute-start(f32[5,4,16,1152]{3,2,1,0:T(8,128)S(1)} %get-tuple-element.40.refs_0_.refs_2_), channel_id=1, source_target_pairs={{0,1},{1,0},{2,3},{3,2},{4,5},{5,4},{6,7},{7,6},{8,9},{9,8},{10,11... | collective-permute-start | bytes 4423688 | tf_op jit(solution)/shard_map/ppermute | solution.py:676
  7.1 7.7 %collective-permute-start.3 = (f32[32,1152]{1,0:T(8,128)S(1)}, f32[32,1152]{1,0:T(8,128)S(1)}, u32[]{:S(2)}, u32[]{:S(2)}) collective-permute-start(f32[32,1152]{1,0:T(8,128)S(1)} %get-tuple-element.42.refs_0_.refs_8_), channel_id=1, source_target_pairs={{0,2},{2,0},{1,3},{3,1},{4,6},{6,4},{5,7},{7,5},{8,10},{10,8},{9,1... | collective-permute-start | bytes 442376 | tf_op jit(solution)/shard_map/ppermute | solution.py:674
  7.2 9.8 %collective-permute-start.4 = (f32[32,1152]{1,0:T(8,128)S(1)}, f32[32,1152]{1,0:T(8,128)S(1)}, u32[]{:S(2)}, u32[]{:S(2)}) collective-permute-start(f32[32,1152]{1,0:T(8,128)S(1)} %get-tuple-element.46.refs_12_), channel_id=1, source_target_pairs={{0,2},{2,0},{1,3},{3,1},{4,6},{6,4},{5,7},{7,5},{8,10},{10,8},{9,1... | collective-permute-start | bytes 442376 | tf_op jit(solution)/shard_map/ppermute | solution.py:674
  9.4 1.3 %collective-permute-start.2 = (f32[16,1152]{1,0:T(8,128)S(1)}, f32[16,1152]{1,0:T(8,128)S(1)}, u32[]{:S(2)}, u32[]{:S(2)}) collective-permute-start(f32[16,1152]{1,0:T(8,128)S(1)} %get-tuple-element.43.refs_0_), channel_id=1, source_target_pairs={{0,1},{1,0},{2,3},{3,2},{4,5},{5,4},{6,7},{7,6},{8,9},{9,8},{10,11... | collective-permute-start | bytes 221192 | tf_op jit(solution)/shard_map/ppermute | solution.py:676
  12.2 14.7 %copy-start = (f32[4,4,16,1152]{3,2,1,0:T(8,128)S(1)}, f32[4,4,16,1152]{3,2,1,0:T(8,128)}, u32[]{:S(2)}) copy-start(f32[4,4,16,1152]{3,2,1,0:T(8,128)} %tracer_ref.1) | copy-start | bytes 3538948
  12.2 14.7 %copy-start.1 = (f32[4,16,1152]{2,1,0:T(8,128)S(1)}, f32[4,16,1152]{2,1,0:T(8,128)}, u32[]{:S(2)}) copy-start(f32[4,16,1152]{2,1,0:T(8,128)} %thick_ref.1) | copy-start | bytes 884740
  12.3 14.7 %copy-start.2 = (f32[4,16,1152]{2,1,0:T(8,128)S(1)}, f32[4,16,1152]{2,1,0:T(8,128)}, u32[]{:S(2)}) copy-start(f32[4,16,1152]{2,1,0:T(8,128)} %u_ref.1) | copy-start | bytes 884740
  12.3 14.7 %copy-start.3 = (f32[4,16,1152]{2,1,0:T(8,128)S(1)}, f32[4,16,1152]{2,1,0:T(8,128)}, u32[]{:S(2)}) copy-start(f32[4,16,1152]{2,1,0:T(8,128)} %v_ref.1) | copy-start | bytes 884740
  12.3 20.7 %collective-permute-start.18 = (f32[160,1152]{1,0:T(8,128)S(1)}, f32[160,1152]{1,0:T(8,128)S(1)}, u32[]{:S(2)}, u32[]{:S(2)}) collective-permute-start(f32[160,1152]{1,0:T(8,128)S(1)} %remap_parts.3.refs_0_), channel_id=1, source_target_pairs={{0,2},{2,0},{1,3},{3,1},{4,6},{6,4},{5,7},{7,5},{8,10},{10,8},{9,1... | collective-permute-start | bytes 2211848 | tf_op jit(solution)/shard_map/ppermute | solution.py:674
  18.7 8.2 %collective-permute-start.6 = (f32[8,4,1,1152]{3,2,1,0:T(1,128)S(1)}, f32[8,4,1,1152]{3,2,1,0:T(1,128)S(1)}, u32[]{:S(2)}, u32[]{:S(2)}) collective-permute-start(f32[8,4,1,1152]{3,2,1,0:T(1,128)S(1)} %get-tuple-element.48), channel_id=1, source_target_pairs={{4,0},{8,4},{12,8},{5,1},{9,5},{13,9},{6,2},{10,6},{14,10},{7,3},{... | collective-permute-start | bytes 442376 | tf_op jit(solution)/shard_map/ppermute | solution.py:724
  20.0 6.9 %collective-permute-start.5 = (f32[6,4,1,1152]{3,2,1,0:T(1,128)S(1)}, f32[6,4,1,1152]{3,2,1,0:T(1,128)S(1)}, u32[]{:S(2)}, u32[]{:S(2)}) collective-permute-start(f32[6,4,1,1152]{3,2,1,0:T(1,128)S(1)} %get-tuple-element.47), channel_id=1, source_target_pairs={{0,4},{4,8},{8,12},{1,5},{5,9},{9,13},{2,6},{6,10},{10,14},{3,7},{... | collective-permute-start | bytes 331784 | tf_op jit(solution)/shard_map/ppermute | solution.py:723
  30.6 2.4 %collective-permute-start.16 = (f32[1,4,16,1152]{3,2,1,0:T(8,128)S(1)}, f32[1,4,16,1152]{3,2,1,0:T(8,128)S(1)}, u32[]{:S(2)}, u32[]{:S(2)}) collective-permute-start(f32[1,4,16,1152]{3,2,1,0:T(8,128)S(1)} %get-tuple-element.53.refs_2_), channel_id=1, source_target_pairs={{0,1},{1,0},{2,3},{3,2},{4,5},{5,4},{6,7},{7,6},{8,9},{9,8},{10,11... | collective-permute-start | bytes 884744 | tf_op jit(solution)/shard_map/ppermute | solution.py:676
  30.7 2.3 %collective-permute-start.17 = (f32[1,4,16,1152]{3,2,1,0:T(8,128)S(1)}, f32[1,4,16,1152]{3,2,1,0:T(8,128)S(1)}, u32[]{:S(2)}, u32[]{:S(2)}) collective-permute-start(f32[1,4,16,1152]{3,2,1,0:T(8,128)S(1)} %get-tuple-element.54.refs_4_), channel_id=1, source_target_pairs={{0,1},{1,0},{2,3},{3,2},{4,5},{5,4},{6,7},{7,6},{8,9},{9,8},{10,11... | collective-permute-start | bytes 884744 | tf_op jit(solution)/shard_map/ppermute | solution.py:676
  31.2 9.1 %collective-permute-start.8 = (f32[7,4,2,1152]{3,2,1,0:T(2,128)S(1)}, f32[7,4,2,1152]{3,2,1,0:T(2,128)S(1)}, u32[]{:S(2)}, u32[]{:S(2)}) collective-permute-start(f32[7,4,2,1152]{3,2,1,0:T(2,128)S(1)} %get-tuple-element.49.refs_6_.refs_0_), channel_id=1, source_target_pairs={{0,2},{2,0},{1,3},{3,1},{4,6},{6,4},{5,7},{7,5},{8,10},{10,8},{9,1... | collective-permute-start | bytes 774152 | tf_op jit(solution)/shard_map/ppermute | solution.py:674
  34.8 15.7 %collective-permute-start.19 = (f32[112,1152]{1,0:T(8,128)S(1)}, f32[112,1152]{1,0:T(8,128)S(1)}, u32[]{:S(2)}, u32[]{:S(2)}) collective-permute-start(f32[112,1152]{1,0:T(8,128)S(1)} %get-tuple-element.55.refs_16_), channel_id=1, source_target_pairs={{0,2},{2,0},{1,3},{3,1},{4,6},{6,4},{5,7},{7,5},{8,10},{10,8},{9,1... | collective-permute-start | bytes 1548296 | tf_op jit(solution)/shard_map/ppermute | solution.py:674
  36.4 3.9 %collective-permute-start.12 = (f32[32,1152]{1,0:T(8,128)S(1)}, f32[32,1152]{1,0:T(8,128)S(1)}, u32[]{:S(2)}, u32[]{:S(2)}) collective-permute-start(f32[32,1152]{1,0:T(8,128)S(1)} %get-tuple-element.42.refs_0_.refs_8_), channel_id=1, source_target_pairs={{0,1},{1,0},{2,3},{3,2},{4,5},{5,4},{6,7},{7,6},{8,9},{9,8},{10,11... | collective-permute-start | bytes 442376 | tf_op jit(solution)/shard_map/ppermute | solution.py:676
  36.4 1.5 %collective-permute-start.10 = (f32[1,4,4,1152]{3,2,1,0:T(4,128)S(1)}, f32[1,4,4,1152]{3,2,1,0:T(4,128)S(1)}, u32[]{:S(2)}, u32[]{:S(2)}) collective-permute-start(f32[1,4,4,1152]{3,2,1,0:T(4,128)S(1)} %get-tuple-element.51.refs_4_), channel_id=1, source_target_pairs={{0,1},{1,0},{2,3},{3,2},{4,5},{5,4},{6,7},{7,6},{8,9},{9,8},{10,11... | collective-permute-start | bytes 221192 | tf_op jit(solution)/shard_map/ppermute | solution.py:676
  36.9 3.9 %collective-permute-start.14 = (f32[32,1152]{1,0:T(8,128)S(1)}, f32[32,1152]{1,0:T(8,128)S(1)}, u32[]{:S(2)}, u32[]{:S(2)}) collective-permute-start(f32[32,1152]{1,0:T(8,128)S(1)} %get-tuple-element.46.refs_12_), channel_id=1, source_target_pairs={{0,1},{1,0},{2,3},{3,2},{4,5},{5,4},{6,7},{7,6},{8,9},{9,8},{10,11... | collective-permute-start | bytes 442376 | tf_op jit(solution)/shard_map/ppermute | solution.py:676
  37.9 5.4 %collective-permute-start.7 = (f32[7,4,2,1152]{3,2,1,0:T(2,128)S(1)}, f32[7,4,2,1152]{3,2,1,0:T(2,128)S(1)}, u32[]{:S(2)}, u32[]{:S(2)}) collective-permute-start(f32[7,4,2,1152]{3,2,1,0:T(2,128)S(1)} %get-tuple-element.49.refs_6_.refs_0_), channel_id=1, source_target_pairs={{0,1},{1,0},{2,3},{3,2},{4,5},{5,4},{6,7},{7,6},{8,9},{9,8},{10,11... | collective-permute-start | bytes 774152 | tf_op jit(solution)/shard_map/ppermute | solution.py:676
  40.2 3.0 %collective-permute-start.9 = (f32[7,4,2,1152]{3,2,1,0:T(2,128)S(1)}, f32[7,4,2,1152]{3,2,1,0:T(2,128)S(1)}, u32[]{:S(2)}, u32[]{:S(2)}) collective-permute-start(f32[7,4,2,1152]{3,2,1,0:T(2,128)S(1)} %collective-permute-done.8.refs_2_), channel_id=1, source_target_pairs={{0,1},{1,0},{2,3},{3,2},{4,5},{5,4},{6,7},{7,6},{8,9},{9,8},{10,11... | collective-permute-start | bytes 774152 | tf_op jit(solution)/shard_map/ppermute | solution.py:676
  40.2 1.6 %collective-permute-start.11 = (f32[1,4,4,1152]{3,2,1,0:T(4,128)S(1)}, f32[1,4,4,1152]{3,2,1,0:T(4,128)S(1)}, u32[]{:S(2)}, u32[]{:S(2)}) collective-permute-start(f32[1,4,4,1152]{3,2,1,0:T(4,128)S(1)} %get-tuple-element.52.refs_6_), channel_id=1, source_target_pairs={{0,1},{1,0},{2,3},{3,2},{4,5},{5,4},{6,7},{7,6},{8,9},{9,8},{10,11... | collective-permute-start | bytes 221192 | tf_op jit(solution)/shard_map/ppermute | solution.py:676
  40.8 1.4 %collective-permute-start.13 = (f32[32,1152]{1,0:T(8,128)S(1)}, f32[32,1152]{1,0:T(8,128)S(1)}, u32[]{:S(2)}, u32[]{:S(2)}) collective-permute-start(f32[32,1152]{1,0:T(8,128)S(1)} %collective-permute-done.3.refs_1_.refs_10_), channel_id=1, source_target_pairs={{0,1},{1,0},{2,3},{3,2},{4,5},{5,4},{6,7},{7,6},{8,9},{9,8},{10,11... | collective-permute-start | bytes 442376 | tf_op jit(solution)/shard_map/ppermute | solution.py:676
  41.9 1.4 %collective-permute-start.15 = (f32[32,1152]{1,0:T(8,128)S(1)}, f32[32,1152]{1,0:T(8,128)S(1)}, u32[]{:S(2)}, u32[]{:S(2)}) collective-permute-start(f32[32,1152]{1,0:T(8,128)S(1)} %collective-permute-done.4.refs_2_.refs_14_), channel_id=1, source_target_pairs={{0,1},{1,0},{2,3},{3,2},{4,5},{5,4},{6,7},{7,6},{8,9},{9,8},{10,11... | collective-permute-start | bytes 442376 | tf_op jit(solution)/shard_map/ppermute | solution.py:676
  (5 other events, 52.4 us)

commit v14 on v13

--- a/solution.py
+++ b/solution.py
@@ -26,7 +26,7 @@
 
 
 def near_rows(rows):
-    return (1, 2, rows - 3, rows - 2), (3, 3)
+    return (1, 2, rows - 2), (3, 2)
 
 
 def geometry_table(lat_rows, band_rows):

time: 51.6 us -> 50.6 us (0.981)
  waiting for transfers between devices: 13.8 us -> 11.6 us
  Pallas kernels: 18.7 us -> 19.4 us
  starting transfers between devices: 17.7 us -> 18.3 us
    ppermute x12, waiting for transfers between devices: 4.51 us -> 3.34 us  [shifted(): lax.ppermute(value, 'sub', [(i, (i + t) % sub_count) for i in range(sub_c...]
    ppermute x6, waiting for transfers between devices: 7.02 us -> 5.99 us  [shifted(): lax.ppermute(value, 'lev', [(i, (i + s) % lev_count) for i in range(lev_c...]
    ppermute x6, starting transfers between devices: 9.61 us -> 10.1 us  [shifted(): lax.ppermute(value, 'lev', [(i, (i + s) % lev_count) for i in range(lev_c...]
  transfers between devices with their start and end apart: 20 -> 20, of which waited for: 10 -> 9; matrix products, arithmetic and copies ran while one was open for 0% -> 0% of each run, Pallas kernels for 31% -> 33%
where the time goes in v14:
time: 50.6 us; the launch traced here: 50.4 us
  Pallas kernels  19.4 us (38%)
  starting transfers between devices  18.3 us (36%)
  waiting for transfers between devices  11.6 us (23%)
  between operations  0.88 us (2%)
    ppermute x6, starting transfers between devices, shifted(): lax.ppermute(value, 'lev', [(i, (i + s) % lev_count) for i in range(lev_c...  10.1 us
    ppermute x6, waiting for transfers between devices, shifted(): lax.ppermute(value, 'lev', [(i, (i + s) % lev_count) for i in range(lev_c...  5.99 us
    ppermute x1, starting transfers between devices, per_device(): up = lax.ppermute(last, 'lat', northward)  4.55 us
    pallas_call x3, Pallas kernels, remap_parts(): pl.pallas_call(functools.partial(remap_kernel, counts, tuple(steps), tupl...  4.45 us
    pallas_call x1, Pallas kernels, remap_edges(): pl.pallas_call(functools.partial(remap_edge_kernel, counts, near_fields),...  3.71 us
    pallas_call x1, Pallas kernels, second_step(): pl.pallas_call(functools.partial(second_kernel, lat_rows), grid=(L,), in_...  3.62 us
    ppermute x12, waiting for transfers between devices, shifted(): lax.ppermute(value, 'sub', [(i, (i + t) % sub_count) for i in range(sub_c...  3.34 us
    ppermute x12, starting transfers between devices, shifted(): lax.ppermute(value, 'sub', [(i, (i + t) % sub_count) for i in range(sub_c...  2.31 us
  transfers between devices with their start and end apart: 20, of which 9 were waited for; matrix products, arithmetic and copies ran while one was open for 0% of the time, Pallas kernels for 33%

profile of v14, /device:TPU:0, one launch (start us, length us, event | category | flops | bytes accessed | tf_op | source)
XLA Modules:
  0.0 50.4 jit_solution(14271322417064649150)
XLA Ops:
  0.6 1.9 %first_step.1 = (f32[4,16,1152]{2,1,0:T(8,128)S(1)}, f32[32,1152]{1,0:T(8,128)S(1)}, f32[1,4,3,1152]{3,2,1,0:T(4,128)S(1)}, f32[4,16,1152]{2,1,0:T(8,128)S(1)}, ...) custom-call(f32[4,24,128]{2,1,0:T(8,128)} %constant.6.clone.table_hbm.table_ref, ...), custom_call_target="tpu_custom_call" | custom-call | flops 2949120 | bytes 4423680 | tf_op jit(solution)/shard_map/first_step/pallas_call | solution.py:130
  2.5 3.0 %collective-permute-start.1 = (f32[32,1152]{1,0:T(8,128)S(1)}, f32[32,1152]{1,0:T(8,128)S(1)}, u32[]{:S(2)}, u32[]{:S(2)}) collective-permute-start(f32[32,1152]{1,0:T(8,128)S(1)} %get-tuple-element.41), channel_id=1, source_target_pairs={{0,2},{2,0},{1,3},{3,1},{4,6},{6,4},{5,7},{7,5},{8,10},{10,8},{9,1... | collective-permute-start | bytes 442376 | tf_op jit(solution)/shard_map/ppermute | solution.py:674
  5.5 1.7 %inner_step.1 = (f32[5,4,16,1152]{3,2,1,0:T(8,128)S(1)}, f32[24,1152]{1,0:T(8,128)S(1)}, f32[24,1152]{1,0:T(8,128)S(1)}) custom-call(f32[4,24,128]{2,1,0:T(8,128)S(1)} %copy-done.6, f32[4,16,1152]{2,1,0:T(8,128)S(1)} %get-tuple-element.35.new_ref, f32[4,16,1152]{2,1,0:T(8,128)S(1)} %get-tuple-element.36.thick_ref, ...), custom_call_target="tpu_custom_call" | custom-call | flops 9584640 | bytes 4718592 | tf_op jit(solution)/shard_map/inner_step/pallas_call | solution.py:173
  7.4 2.0 %collective-permute-start.4 = (f32[24,1152]{1,0:T(8,128)S(1)}, f32[24,1152]{1,0:T(8,128)S(1)}, u32[]{:S(2)}, u32[]{:S(2)}) collective-permute-start(f32[24,1152]{1,0:T(8,128)S(1)} %get-tuple-element.46.refs_12_), channel_id=1, source_target_pairs={{0,2},{2,0},{1,3},{3,1},{4,6},{6,4},{5,7},{7,5},{8,10},{10,8},{9,1... | collective-permute-start | bytes 331784 | tf_op jit(solution)/shard_map/ppermute | solution.py:674
  9.5 1.3 %collective-permute-done.2.refs_1_ = f32[16,1152]{1,0:T(8,128)S(1)} collective-permute-done((f32[16,1152]{1,0:T(8,128)S(1)}, f32[16,1152]{1,0:T(8,128)S(1)}, u32[]{:S(2)}, u32[]{:S(2)}) %collective-permute-start.2) | collective-permute-done | bytes 73760 | tf_op jit(solution)/shard_map/ppermute | solution.py:676
  10.9 1.4 %remap_parts.3.refs_0_ = f32[176,1152]{1,0:T(8,128)S(1)} custom-call(f32[16,8,128]{2,1,0:T(8,128)S(1)} %broadcast_in_dim.4.weight_ref, f32[5,4,16,1152]{3,2,1,0:T(8,128)S(1)} %get-tuple-element.40.refs_0_.refs_2_, f32[5,4,16,1152]{3,2,1,0:T(8,128)S(1)} %collective-permute-done.refs_1_.refs_3_, f32[5,4,16,1152]{3,2,1,0:T(8,128)S(1)} %get-tuple-element.40.refs_0_.refs_2_, ...), custom_call_target="tpu_custom_call" | custom-call | flops 7667712 | bytes 4423680 | tf_op jit(solution)/shard_map/remap_parts/pallas_call | solution.py:504
  12.3 2.2 %collective-permute-start.18 = (f32[176,1152]{1,0:T(8,128)S(1)}, f32[176,1152]{1,0:T(8,128)S(1)}, u32[]{:S(2)}, u32[]{:S(2)}) collective-permute-start(f32[176,1152]{1,0:T(8,128)S(1)} %remap_parts.3.refs_0_), channel_id=1, source_target_pairs={{0,2},{2,0},{1,3},{3,1},{4,6},{6,4},{5,7},{7,5},{8,10},{10,8},{9,1... | collective-permute-start | bytes 2433032 | tf_op jit(solution)/shard_map/ppermute | solution.py:674
  15.1 1.7 %edge_rows.1 = (f32[6,4,1,1152]{3,2,1,0:T(1,128)S(1)}, f32[8,4,1,1152]{3,2,1,0:T(1,128)S(1)}) custom-call(f32[4,16,1152]{2,1,0:T(8,128)} %thick_ref.1, f32[4,16,1152]{2,1,0:T(8,128)} %u_ref.1, f32[4,16,1152]{2,1,0:T(8,128)} %v_ref.1, f32[4,4,16,1152]{3,2,1,0:T(8,128)} %tracer_ref.1, f32[176,1152]{1,0:T(8,128)S(1)} %remap_parts.3.refs_0_, ...), custom_call_target="tpu_custom_call" | custom-call | flops 10000000000 | bytes 1000000000 | tf_op jit(solution)/shard_map/edge_rows/pallas_call | solution.py:652
  16.9 1.3 %collective-permute-start.6 = (f32[8,4,1,1152]{3,2,1,0:T(1,128)S(1)}, f32[8,4,1,1152]{3,2,1,0:T(1,128)S(1)}, u32[]{:S(2)}, u32[]{:S(2)}) collective-permute-start(f32[8,4,1,1152]{3,2,1,0:T(1,128)S(1)} %get-tuple-element.48), channel_id=1, source_target_pairs={{4,0},{8,4},{12,8},{5,1},{9,5},{13,9},{6,2},{10,6},{14,10},{7,3},{... | collective-permute-start | bytes 442376 | tf_op jit(solution)/shard_map/ppermute | solution.py:724
  18.2 4.6 %collective-permute-start.5 = (f32[6,4,1,1152]{3,2,1,0:T(1,128)S(1)}, f32[6,4,1,1152]{3,2,1,0:T(1,128)S(1)}, u32[]{:S(2)}, u32[]{:S(2)}) collective-permute-start(f32[6,4,1,1152]{3,2,1,0:T(1,128)S(1)} %get-tuple-element.47), channel_id=1, source_target_pairs={{0,4},{4,8},{8,12},{1,5},{5,9},{9,13},{2,6},{6,10},{10,14},{3,7},{... | collective-permute-start | bytes 331784 | tf_op jit(solution)/shard_map/ppermute | solution.py:723
  22.7 2.3 %collective-permute-done.5.up_ref = f32[6,4,1,1152]{3,2,1,0:T(1,128)S(1)} collective-permute-done((f32[6,4,1,1152]{3,2,1,0:T(1,128)S(1)}, f32[6,4,1,1152]{3,2,1,0:T(1,128)S(1)}, u32[]{:S(2)}, u32[]{:S(2)}) %collective-permute-start.5) | collective-permute-done | bytes 110624 | tf_op jit(solution)/shard_map/ppermute | solution.py:723
  25.1 3.6 %second_step.1 = (f32[1,4,16,1152]{3,2,1,0:T(8,128)S(1)}, f32[1,4,16,1152]{3,2,1,0:T(8,128)S(1)}, f32[7,4,2,1152]{3,2,1,0:T(2,128)S(1)}) custom-call(f32[4,24,128]{2,1,0:T(8,128)S(1)} %copy-done.6, f32[4,16,1152]{2,1,0:T(8,128)S(1)} %copy-done.1, f32[4,16,1152]{2,1,0:T(8,128)S(1)} %copy-done.2, f32[4,16,1152]{2,1,0:T(8,128)S(1)} %copy-done.3, ...), custom_call_target="tpu_custom_call" | custom-call | flops 503316480 | bytes 3538944 | tf_op jit(solution)/shard_map/second_step/pallas_call | solution.py:311
  29.3 0.7 %collective-permute-start.8 = (f32[7,4,2,1152]{3,2,1,0:T(2,128)S(1)}, f32[7,4,2,1152]{3,2,1,0:T(2,128)S(1)}, u32[]{:S(2)}, u32[]{:S(2)}) collective-permute-start(f32[7,4,2,1152]{3,2,1,0:T(2,128)S(1)} %get-tuple-element.49.refs_6_.refs_0_), channel_id=1, source_target_pairs={{0,2},{2,0},{1,3},{3,1},{4,6},{6,4},{5,7},{7,5},{8,10},{10,8},{9,1... | collective-permute-start | bytes 774152 | tf_op jit(solution)/shard_map/ppermute | solution.py:674
  30.1 1.3 %remap_parts.4 = (f32[4,4,16,1152]{3,2,1,0:T(8,128)S(1)}, f32[4,16,1152]{2,1,0:T(8,128)S(1)}) custom-call(f32[16,8,128]{2,1,0:T(8,128)S(1)} %broadcast_in_dim.4.weight_ref, f32[5,4,16,1152]{3,2,1,0:T(8,128)S(1)} %get-tuple-element.40.refs_0_.refs_2_, f32[5,4,16,1152]{3,2,1,0:T(8,128)S(1)} %collective-permute-done.refs_1_.refs_3_, ...), custom_call_target="tpu_custom_call" | custom-call | flops 7667712 | bytes 4423680 | tf_op jit(solution)/shard_map/remap_parts/pallas_call | solution.py:504
  31.4 2.0 %collective-permute-done.18.refs_9_.refs_0_ = f32[176,1152]{1,0:T(8,128)S(1)} collective-permute-done((f32[176,1152]{1,0:T(8,128)S(1)}, f32[176,1152]{1,0:T(8,128)S(1)}, u32[]{:S(2)}, u32[]{:S(2)}) %collective-permute-start.18) | collective-permute-done | bytes 811040 | tf_op jit(solution)/shard_map/ppermute | solution.py:674
  33.4 1.8 %remap_parts.5 = (f32[2,4,16,1152]{3,2,1,0:T(8,128)S(1)}, f32[112,1152]{1,0:T(8,128)S(1)}) custom-call(f32[16,8,128]{2,1,0:T(8,128)S(1)} %broadcast_in_dim.4.weight_ref, f32[5,4,16,1152]{3,2,1,0:T(8,128)S(1)} %get-tuple-element.40.refs_0_.refs_2_, f32[5,4,16,1152]{3,2,1,0:T(8,128)S(1)} %collective-permute-done.refs_1_.refs_3_, ...), custom_call_target="tpu_custom_call" | custom-call | flops 10616832 | bytes 3538944 | tf_op jit(solution)/shard_map/remap_parts/pallas_call | solution.py:504
  35.1 2.1 %collective-permute-start.19 = (f32[112,1152]{1,0:T(8,128)S(1)}, f32[112,1152]{1,0:T(8,128)S(1)}, u32[]{:S(2)}, u32[]{:S(2)}) collective-permute-start(f32[112,1152]{1,0:T(8,128)S(1)} %get-tuple-element.55.refs_16_), channel_id=1, source_target_pairs={{0,2},{2,0},{1,3},{3,1},{4,6},{6,4},{5,7},{7,5},{8,10},{10,8},{9,1... | collective-permute-start | bytes 1548296 | tf_op jit(solution)/shard_map/ppermute | solution.py:674
  37.8 1.1 %collective-permute-done.8.refs_2_ = f32[7,4,2,1152]{3,2,1,0:T(2,128)S(1)} collective-permute-done((f32[7,4,2,1152]{3,2,1,0:T(2,128)S(1)}, f32[7,4,2,1152]{3,2,1,0:T(2,128)S(1)}, u32[]{:S(2)}, u32[]{:S(2)}) %collective-permute-start.8) | collective-permute-done | bytes 258080 | tf_op jit(solution)/shard_map/ppermute | solution.py:674
  39.5 1.1 %collective-permute-done.14.refs_13_ = f32[24,1152]{1,0:T(8,128)S(1)} collective-permute-done((f32[24,1152]{1,0:T(8,128)S(1)}, f32[24,1152]{1,0:T(8,128)S(1)}, u32[]{:S(2)}, u32[]{:S(2)}) %collective-permute-start.14) | collective-permute-done | bytes 110624 | tf_op jit(solution)/shard_map/ppermute | solution.py:676
  41.1 0.8 %collective-permute-done.13.refs_11_ = f32[24,1152]{1,0:T(8,128)S(1)} collective-permute-done((f32[24,1152]{1,0:T(8,128)S(1)}, f32[24,1152]{1,0:T(8,128)S(1)}, u32[]{:S(2)}, u32[]{:S(2)}) %collective-permute-start.13) | collective-permute-done | bytes 110624 | tf_op jit(solution)/shard_map/ppermute | solution.py:676
  42.1 3.7 %remap_edges.1 = (f32[6,4,2,1152]{3,2,1,0:T(2,128)S(1)}, f32[4,2,1152]{2,1,0:T(2,128)S(1)}, f32[4,4,3,1152]{3,2,1,0:T(4,128)S(1)}) custom-call(f32[16,8,128]{2,1,0:T(8,128)S(1)} %broadcast_in_dim.4.weight_ref, f32[7,4,2,1152]{3,2,1,0:T(2,128)S(1)} %get-tuple-element.49.refs_6_.refs_0_, f32[7,4,2,1152]{3,2,1,0:T(2,128)S(1)} %collective-permute-done.7.refs_1_, ...), custom_call_target="tpu_custom_call" | custom-call | flops 5898240 | bytes 4128768 | tf_op jit(solution)/shard_map/remap_edges/pallas_call | solution.py:544
  45.8 1.4 %finish_tracers.1 = (f32[4,4,16,1152]{3,2,1,0:T(8,128)}, f32[4,16,1152]{2,1,0:T(8,128)}, f32[8,128]{1,0:T(8,128)S(1)}) custom-call(f32[4,4,16,1152]{3,2,1,0:T(8,128)S(1)} %get-tuple-element.50.refs_8_.own_ref, f32[4,4,3,1152]{3,2,1,0:T(4,128)S(1)} %get-tuple-element.56.near_ref, f32[6,4,2,1152]{3,2,1,0:T(2,128)S(1)} %get-tuple-element.57.edge_ref, ...), custom_call_target="tpu_custom_call" | custom-call | flops 589824 | bytes 3538944 | tf_op jit(solution)/shard_map/finish_tracers/pallas_call | solution.py:582
  47.2 2.3 %collective-permute-done.19.refs_0_ = f32[112,1152]{1,0:T(8,128)S(1)} collective-permute-done((f32[112,1152]{1,0:T(8,128)S(1)}, f32[112,1152]{1,0:T(8,128)S(1)}, u32[]{:S(2)}, u32[]{:S(2)}) %collective-permute-start.19) | collective-permute-done | bytes 516128 | tf_op jit(solution)/shard_map/ppermute | solution.py:674
  49.5 0.9 %finish_winds.1 = (f32[4,16,1152]{2,1,0:T(8,128)}, f32[4,16,1152]{2,1,0:T(8,128)}) custom-call(f32[2,4,16,1152]{3,2,1,0:T(8,128)S(1)} %get-tuple-element.61.own_ref, f32[6,4,2,1152]{3,2,1,0:T(2,128)S(1)} %get-tuple-element.57.edge_ref, f32[112,1152]{1,0:T(8,128)S(1)} %collective-permute-done.19.refs_0_, f32[8,128]{1,0:T(8,128)S(1)} %get-tuple-element.62.refs_1_), custom_call_target="tpu_custom_call" | custom-call | flops 147456 | bytes 1769472 | tf_op jit(solution)/shard_map/finish_winds/pallas_call | solution.py:612
  (48 shorter events, 3.4 us)
Async XLA Ops:
  2.5 6.9 %collective-permute-start.1 = (f32[32,1152]{1,0:T(8,128)S(1)}, f32[32,1152]{1,0:T(8,128)S(1)}, u32[]{:S(2)}, u32[]{:S(2)}) collective-permute-start(f32[32,1152]{1,0:T(8,128)S(1)} %get-tuple-element.41), channel_id=1, source_target_pairs={{0,2},{2,0},{1,3},{3,1},{4,6},{6,4},{5,7},{7,5},{8,10},{10,8},{9,1... | collective-permute-start | bytes 442376 | tf_op jit(solution)/shard_map/ppermute | solution.py:674
  7.2 3.6 %collective-permute-start = (f32[5,4,16,1152]{3,2,1,0:T(8,128)S(1)}, f32[5,4,16,1152]{3,2,1,0:T(8,128)S(1)}, u32[]{:S(2)}, u32[]{:S(2)}) collective-permute-start(f32[5,4,16,1152]{3,2,1,0:T(8,128)S(1)} %get-tuple-element.40.refs_0_.refs_2_), channel_id=1, source_target_pairs={{0,1},{1,0},{2,3},{3,2},{4,5},{5,4},{6,7},{7,6},{8,9},{9,8},{10,11... | collective-permute-start | bytes 4423688 | tf_op jit(solution)/shard_map/ppermute | solution.py:676
  7.3 7.2 %collective-permute-start.3 = (f32[24,1152]{1,0:T(8,128)S(1)}, f32[24,1152]{1,0:T(8,128)S(1)}, u32[]{:S(2)}, u32[]{:S(2)}) collective-permute-start(f32[24,1152]{1,0:T(8,128)S(1)} %get-tuple-element.42.refs_0_.refs_8_), channel_id=1, source_target_pairs={{0,2},{2,0},{1,3},{3,1},{4,6},{6,4},{5,7},{7,5},{8,10},{10,8},{9,1... | collective-permute-start | bytes 331784 | tf_op jit(solution)/shard_map/ppermute | solution.py:674
  7.4 7.7 %collective-permute-start.4 = (f32[24,1152]{1,0:T(8,128)S(1)}, f32[24,1152]{1,0:T(8,128)S(1)}, u32[]{:S(2)}, u32[]{:S(2)}) collective-permute-start(f32[24,1152]{1,0:T(8,128)S(1)} %get-tuple-element.46.refs_12_), channel_id=1, source_target_pairs={{0,2},{2,0},{1,3},{3,1},{4,6},{6,4},{5,7},{7,5},{8,10},{10,8},{9,1... | collective-permute-start | bytes 331784 | tf_op jit(solution)/shard_map/ppermute | solution.py:674
  9.4 1.3 %collective-permute-start.2 = (f32[16,1152]{1,0:T(8,128)S(1)}, f32[16,1152]{1,0:T(8,128)S(1)}, u32[]{:S(2)}, u32[]{:S(2)}) collective-permute-start(f32[16,1152]{1,0:T(8,128)S(1)} %get-tuple-element.43.refs_0_), channel_id=1, source_target_pairs={{0,1},{1,0},{2,3},{3,2},{4,5},{5,4},{6,7},{7,6},{8,9},{9,8},{10,11... | collective-permute-start | bytes 221192 | tf_op jit(solution)/shard_map/ppermute | solution.py:676
  12.3 12.8 %copy-start = (f32[4,4,16,1152]{3,2,1,0:T(8,128)S(1)}, f32[4,4,16,1152]{3,2,1,0:T(8,128)}, u32[]{:S(2)}) copy-start(f32[4,4,16,1152]{3,2,1,0:T(8,128)} %tracer_ref.1) | copy-start | bytes 3538948
  12.3 12.8 %copy-start.1 = (f32[4,16,1152]{2,1,0:T(8,128)S(1)}, f32[4,16,1152]{2,1,0:T(8,128)}, u32[]{:S(2)}) copy-start(f32[4,16,1152]{2,1,0:T(8,128)} %thick_ref.1) | copy-start | bytes 884740
  12.3 12.8 %copy-start.2 = (f32[4,16,1152]{2,1,0:T(8,128)S(1)}, f32[4,16,1152]{2,1,0:T(8,128)}, u32[]{:S(2)}) copy-start(f32[4,16,1152]{2,1,0:T(8,128)} %u_ref.1) | copy-start | bytes 884740
  12.3 12.8 %copy-start.3 = (f32[4,16,1152]{2,1,0:T(8,128)S(1)}, f32[4,16,1152]{2,1,0:T(8,128)}, u32[]{:S(2)}) copy-start(f32[4,16,1152]{2,1,0:T(8,128)} %v_ref.1) | copy-start | bytes 884740
  12.3 21.0 %collective-permute-start.18 = (f32[176,1152]{1,0:T(8,128)S(1)}, f32[176,1152]{1,0:T(8,128)S(1)}, u32[]{:S(2)}, u32[]{:S(2)}) collective-permute-start(f32[176,1152]{1,0:T(8,128)S(1)} %remap_parts.3.refs_0_), channel_id=1, source_target_pairs={{0,2},{2,0},{1,3},{3,1},{4,6},{6,4},{5,7},{7,5},{8,10},{10,8},{9,1... | collective-permute-start | bytes 2433032 | tf_op jit(solution)/shard_map/ppermute | solution.py:674
  16.9 8.2 %collective-permute-start.6 = (f32[8,4,1,1152]{3,2,1,0:T(1,128)S(1)}, f32[8,4,1,1152]{3,2,1,0:T(1,128)S(1)}, u32[]{:S(2)}, u32[]{:S(2)}) collective-permute-start(f32[8,4,1,1152]{3,2,1,0:T(1,128)S(1)} %get-tuple-element.48), channel_id=1, source_target_pairs={{4,0},{8,4},{12,8},{5,1},{9,5},{13,9},{6,2},{10,6},{14,10},{7,3},{... | collective-permute-start | bytes 442376 | tf_op jit(solution)/shard_map/ppermute | solution.py:724
  18.2 6.9 %collective-permute-start.5 = (f32[6,4,1,1152]{3,2,1,0:T(1,128)S(1)}, f32[6,4,1,1152]{3,2,1,0:T(1,128)S(1)}, u32[]{:S(2)}, u32[]{:S(2)}) collective-permute-start(f32[6,4,1,1152]{3,2,1,0:T(1,128)S(1)} %get-tuple-element.47), channel_id=1, source_target_pairs={{0,4},{4,8},{8,12},{1,5},{5,9},{9,13},{2,6},{6,10},{10,14},{3,7},{... | collective-permute-start | bytes 331784 | tf_op jit(solution)/shard_map/ppermute | solution.py:723
  28.8 2.6 %collective-permute-start.16 = (f32[1,4,16,1152]{3,2,1,0:T(8,128)S(1)}, f32[1,4,16,1152]{3,2,1,0:T(8,128)S(1)}, u32[]{:S(2)}, u32[]{:S(2)}) collective-permute-start(f32[1,4,16,1152]{3,2,1,0:T(8,128)S(1)} %get-tuple-element.53.refs_2_), channel_id=1, source_target_pairs={{0,1},{1,0},{2,3},{3,2},{4,5},{5,4},{6,7},{7,6},{8,9},{9,8},{10,11... | collective-permute-start | bytes 884744 | tf_op jit(solution)/shard_map/ppermute | solution.py:676
  28.8 2.6 %collective-permute-start.17 = (f32[1,4,16,1152]{3,2,1,0:T(8,128)S(1)}, f32[1,4,16,1152]{3,2,1,0:T(8,128)S(1)}, u32[]{:S(2)}, u32[]{:S(2)}) collective-permute-start(f32[1,4,16,1152]{3,2,1,0:T(8,128)S(1)} %get-tuple-element.54.refs_4_), channel_id=1, source_target_pairs={{0,1},{1,0},{2,3},{3,2},{4,5},{5,4},{6,7},{7,6},{8,9},{9,8},{10,11... | collective-permute-start | bytes 884744 | tf_op jit(solution)/shard_map/ppermute | solution.py:676
  29.3 9.6 %collective-permute-start.8 = (f32[7,4,2,1152]{3,2,1,0:T(2,128)S(1)}, f32[7,4,2,1152]{3,2,1,0:T(2,128)S(1)}, u32[]{:S(2)}, u32[]{:S(2)}) collective-permute-start(f32[7,4,2,1152]{3,2,1,0:T(2,128)S(1)} %get-tuple-element.49.refs_6_.refs_0_), channel_id=1, source_target_pairs={{0,2},{2,0},{1,3},{3,1},{4,6},{6,4},{5,7},{7,5},{8,10},{10,8},{9,1... | collective-permute-start | bytes 774152 | tf_op jit(solution)/shard_map/ppermute | solution.py:674
  35.1 14.4 %collective-permute-start.19 = (f32[112,1152]{1,0:T(8,128)S(1)}, f32[112,1152]{1,0:T(8,128)S(1)}, u32[]{:S(2)}, u32[]{:S(2)}) collective-permute-start(f32[112,1152]{1,0:T(8,128)S(1)} %get-tuple-element.55.refs_16_), channel_id=1, source_target_pairs={{0,2},{2,0},{1,3},{3,1},{4,6},{6,4},{5,7},{7,5},{8,10},{10,8},{9,1... | collective-permute-start | bytes 1548296 | tf_op jit(solution)/shard_map/ppermute | solution.py:674
  37.3 1.7 %collective-permute-start.10 = (f32[1,4,3,1152]{3,2,1,0:T(4,128)S(1)}, f32[1,4,3,1152]{3,2,1,0:T(4,128)S(1)}, u32[]{:S(2)}, u32[]{:S(2)}) collective-permute-start(f32[1,4,3,1152]{3,2,1,0:T(4,128)S(1)} %get-tuple-element.51.refs_4_), channel_id=1, source_target_pairs={{0,1},{1,0},{2,3},{3,2},{4,5},{5,4},{6,7},{7,6},{8,9},{9,8},{10,11... | collective-permute-start | bytes 165896 | tf_op jit(solution)/shard_map/ppermute | solution.py:676
  37.3 2.2 %collective-permute-start.12 = (f32[24,1152]{1,0:T(8,128)S(1)}, f32[24,1152]{1,0:T(8,128)S(1)}, u32[]{:S(2)}, u32[]{:S(2)}) collective-permute-start(f32[24,1152]{1,0:T(8,128)S(1)} %get-tuple-element.42.refs_0_.refs_8_), channel_id=1, source_target_pairs={{0,1},{1,0},{2,3},{3,2},{4,5},{5,4},{6,7},{7,6},{8,9},{9,8},{10,11... | collective-permute-start | bytes 331784 | tf_op jit(solution)/shard_map/ppermute | solution.py:676
  37.8 4.3 %collective-permute-start.7 = (f32[7,4,2,1152]{3,2,1,0:T(2,128)S(1)}, f32[7,4,2,1152]{3,2,1,0:T(2,128)S(1)}, u32[]{:S(2)}, u32[]{:S(2)}) collective-permute-start(f32[7,4,2,1152]{3,2,1,0:T(2,128)S(1)} %get-tuple-element.49.refs_6_.refs_0_), channel_id=1, source_target_pairs={{0,1},{1,0},{2,3},{3,2},{4,5},{5,4},{6,7},{7,6},{8,9},{9,8},{10,11... | collective-permute-start | bytes 774152 | tf_op jit(solution)/shard_map/ppermute | solution.py:676
  38.9 3.2 %collective-permute-start.9 = (f32[7,4,2,1152]{3,2,1,0:T(2,128)S(1)}, f32[7,4,2,1152]{3,2,1,0:T(2,128)S(1)}, u32[]{:S(2)}, u32[]{:S(2)}) collective-permute-start(f32[7,4,2,1152]{3,2,1,0:T(2,128)S(1)} %collective-permute-done.8.refs_2_), channel_id=1, source_target_pairs={{0,1},{1,0},{2,3},{3,2},{4,5},{5,4},{6,7},{7,6},{8,9},{9,8},{10,11... | collective-permute-start | bytes 774152 | tf_op jit(solution)/shard_map/ppermute | solution.py:676
  38.9 1.7 %collective-permute-start.14 = (f32[24,1152]{1,0:T(8,128)S(1)}, f32[24,1152]{1,0:T(8,128)S(1)}, u32[]{:S(2)}, u32[]{:S(2)}) collective-permute-start(f32[24,1152]{1,0:T(8,128)S(1)} %get-tuple-element.46.refs_12_), channel_id=1, source_target_pairs={{0,1},{1,0},{2,3},{3,2},{4,5},{5,4},{6,7},{7,6},{8,9},{9,8},{10,11... | collective-permute-start | bytes 331784 | tf_op jit(solution)/shard_map/ppermute | solution.py:676
  39.4 1.3 %collective-permute-start.11 = (f32[1,4,3,1152]{3,2,1,0:T(4,128)S(1)}, f32[1,4,3,1152]{3,2,1,0:T(4,128)S(1)}, u32[]{:S(2)}, u32[]{:S(2)}) collective-permute-start(f32[1,4,3,1152]{3,2,1,0:T(4,128)S(1)} %get-tuple-element.52.refs_6_), channel_id=1, source_target_pairs={{0,1},{1,0},{2,3},{3,2},{4,5},{5,4},{6,7},{7,6},{8,9},{9,8},{10,11... | collective-permute-start | bytes 165896 | tf_op jit(solution)/shard_map/ppermute | solution.py:676
  40.6 1.3 %collective-permute-start.13 = (f32[24,1152]{1,0:T(8,128)S(1)}, f32[24,1152]{1,0:T(8,128)S(1)}, u32[]{:S(2)}, u32[]{:S(2)}) collective-permute-start(f32[24,1152]{1,0:T(8,128)S(1)} %collective-permute-done.3.refs_1_.refs_10_), channel_id=1, source_target_pairs={{0,1},{1,0},{2,3},{3,2},{4,5},{5,4},{6,7},{7,6},{8,9},{9,8},{10,11... | collective-permute-start | bytes 331784 | tf_op jit(solution)/shard_map/ppermute | solution.py:676
  40.7 1.3 %collective-permute-start.15 = (f32[24,1152]{1,0:T(8,128)S(1)}, f32[24,1152]{1,0:T(8,128)S(1)}, u32[]{:S(2)}, u32[]{:S(2)}) collective-permute-start(f32[24,1152]{1,0:T(8,128)S(1)} %collective-permute-done.4.refs_2_.refs_14_), channel_id=1, source_target_pairs={{0,1},{1,0},{2,3},{3,2},{4,5},{5,4},{6,7},{7,6},{8,9},{9,8},{10,11... | collective-permute-start | bytes 331784 | tf_op jit(solution)/shard_map/ppermute | solution.py:676
  (5 other events, 46.7 us)

commit v15 on v14

--- a/solution.py
+++ b/solution.py
@@ -82,8 +82,15 @@
     return change - (t_north - south_of(t_north, t_below)) * inverse
 
 
+def packed_at(rows, levels, width):
+    near = len(near_rows(rows)[0])
+    size = rows - 2 + levels * near
+    for a in range(width // LANES):
+        yield a, a * size, [a * size + rows - 2 + k * near for k in range(levels)]
+
+
 def first_kernel(table_hbm, thick_hbm, u_hbm, v_hbm, tracer_hbm, *refs):
-    new_ref, both_ref, near_ref, thick_ref, u_ref, v_ref, tracer_ref, geo_ref, sems = refs
+    new_ref, both_ref, near_ref, thick_ref, u_ref, v_ref, tracer_ref, sum_ref, geo_ref, sems = refs
     L, rows, _ = thick_ref.shape
     near, _ = near_rows(rows)
     table_copy = pltpu.make_async_copy(table_hbm.at[lax.axis_index("lat")], geo_ref, sems.at[3, 0])
@@ -100,7 +107,7 @@
     tracer_copy.start()
     table_copy.wait()
     geo = geo_ref[...]
-    both_ref[...] = jnp.zeros_like(both_ref)
+    sum_ref[...] = jnp.zeros_like(sum_ref)
 
     def level(k, carry):
         for copy in copies(k):
@@ -111,13 +118,15 @@
         new_ref[k] = new
         for j, row in enumerate(near):
             near_ref[0, k, j : j + 1] = new[row : row + 1]
-        both_ref[0:rows] += new
+        sum_ref[...] += new
         return carry
 
     lax.fori_loop(0, L, level, 0)
-    for k in range(L):
-        at = rows + k * len(near)
-        both_ref[at : at + len(near)] = near_ref[0, k]
+    for a, at, each in packed_at(rows, L, thick_ref.shape[2]):
+        lanes = slice(a * LANES, (a + 1) * LANES)
+        both_ref[at : at + rows - 2] = sum_ref[1 : rows - 1, lanes]
+        for k in range(L):
+            both_ref[each[k] : each[k] + len(near)] = near_ref[0, k, :, lanes]
     tracer_copy.wait()
 
 
@@ -126,13 +135,17 @@
     arguments = (thickness, wind_u, wind_v, tracers)
     operands = [pltpu.with_memory_space_constraint(a, pltpu.HBM) for a in (table, *arguments)]
     near = len(near_rows(R)[0])
-    shapes = [(L, R, N), (-(-(R + L * near) // 8) * 8, N), (1, L, near, N)] + [a.shape for a in arguments]
+    shapes = [(L, R, N), ((R - 2 + L * near) * N // LANES, LANES), (1, L, near, N)] + [a.shape for a in arguments]
     return pl.pallas_call(
         first_kernel,
         in_specs=after(operands),
         out_specs=[VMEM] * len(shapes),
         out_shape=[jax.ShapeDtypeStruct(shape, jnp.float32) for shape in shapes],
-        scratch_shapes=[pltpu.VMEM(table.shape[1:], jnp.float32), pltpu.SemaphoreType.DMA((4, max(L, 2)))],
+        scratch_shapes=[
+            pltpu.VMEM((R, N), jnp.float32),
+            pltpu.VMEM(table.shape[1:], jnp.float32),
+            pltpu.SemaphoreType.DMA((4, max(L, 2))),
+        ],
         compiler_params=params(),
         cost_estimate=cost(40 * L * R * N, 4 * L * R * N * (7 + 2 * tracers.shape[0])),
         name="first_step",
@@ -331,11 +344,14 @@
 
 def part_kernel(both_ref, *refs):
     sum_ref, near_ref = refs[-2:]
-    rows = sum_ref.shape[0]
-    sum_ref[...] = both_ref[0:rows]
+    rows, width = sum_ref.shape
     _, L, near, _ = near_ref.shape
-    for k in range(L):
-        near_ref[0, k] = both_ref[rows + k * near : rows + (k + 1) * near]
+    sum_ref[...] = jnp.zeros_like(sum_ref)
+    for a, at, each in packed_at(rows, L, width):
+        lanes = slice(a * LANES, (a + 1) * LANES)
+        sum_ref[1 : rows - 1, lanes] = both_ref[at : at + rows - 2]
+        for k in range(L):
+            near_ref[0, k, :, lanes] = both_ref[each[k] : each[k] + near]
 
 
 def part(both, shape, wait):
@@ -461,7 +477,7 @@
     return max(at.start, margin[0]), min(at.stop, rows - margin[1])
 
 
-def remap_kernel(counts, steps, fields, margin, with_thickness, sizes, weight_ref, *refs):
+def remap_kernel(counts, steps, fields, margin, cut, with_thickness, sizes, weight_ref, *refs):
     *refs, sum_ref = refs
     C, S = counts
     thick_refs, refs = refs[:S], refs[S:]
@@ -469,21 +485,24 @@
     for _ in range(sizes[0]):
         bundles.append(refs[:S])
         refs = refs[S:]
-    other_refs, out_refs = refs[:2], refs[len(refs) - len(steps) - with_thickness :]
+    other_refs, out_refs = refs[:2], refs[len(refs) - sum(2 if cut and s > 0 else 1 for s in steps) - with_thickness :]
     _, L, R, _ = thick_refs[0].shape
     thick_out_ref = out_refs[-1]
     field_refs = [[level_of(ref, index) for ref in bundles[which]] for which, index in fields]
 
     def store(s, i, at, columns, target, means):
-        out_ref = out_refs[steps.index(s)]
+        at_out = sum(2 if cut and s > 0 else 1 for s in steps[: steps.index(s)])
         if with_thickness and s == 0:
             thick_out_ref[i, at, columns] = target
         for f, value in enumerate(means):
             if s == 0:
-                out_ref[f, i, at, columns] = value
+                out_refs[at_out][f, i, at, columns] = value
             else:
                 lower, upper = inner_part(at, margin, R)
-                start = (f * L + i) * (R - sum(margin)) - margin[0]
+                group = f * L + i
+                late = cut > 0 and group >= cut
+                out_ref = out_refs[at_out + late]
+                start = (group - cut * late) * (R - sum(margin)) - margin[0]
                 out_ref[start + lower : start + upper, columns] = value[lower - at.start : upper - at.start]
 
     remap_rows(
@@ -491,18 +510,20 @@
     )
 
 
-def remap_parts(counts, weights, thick, bundles, others, fields, steps, margin, with_thickness=False, wait=()):
+def remap_parts(counts, weights, thick, bundles, others, fields, steps, margin, cut=0, with_thickness=False, wait=()):
     C, S = counts
     _, L, R, N = thick[0].shape
     F = len(fields)
     whole = jax.ShapeDtypeStruct((F, L, R, N), jnp.float32)
-    inner = jax.ShapeDtypeStruct((F * L * (R - sum(margin)), N), jnp.float32)
+    inner = [
+        jax.ShapeDtypeStruct((n * (R - sum(margin)), N), jnp.float32) for n in ((cut, F * L - cut) if cut else (F * L,))
+    ]
     flat = [a for bundle in bundles for a in bundle]
-    out_shape = [whole if s == 0 else inner for s in steps]
+    out_shape = [a for s in steps for a in ([whole] if s == 0 else inner)]
     if with_thickness:
         out_shape.append(jax.ShapeDtypeStruct((L, R, N), jnp.float32))
     return pl.pallas_call(
-        functools.partial(remap_kernel, counts, tuple(steps), tuple(fields), margin, with_thickness, (len(bundles),)),
+        functools.partial(remap_kernel, counts, tuple(steps), tuple(fields), margin, cut, with_thickness, (len(bundles),)),
         in_specs=[VMEM] * (1 + len(thick) + len(flat) + len(others)) + after(wait),
         out_specs=[VMEM] * len(out_shape),
         out_shape=out_shape,
@@ -513,47 +534,63 @@
     )(weights, *thick, *flat, *others, *wait)
 
 
-def remap_edge_kernel(counts, near_fields, weight_ref, *refs):
+def remap_edge_kernel(counts, weight_ref, *refs):
     *refs, sum_ref = refs
-    G = counts[0] * counts[1]
-    edge_refs, near_refs = refs[:G], refs[G : 2 * G]
-    bundles = (refs[2 * G : 3 * G], refs[3 * G : 4 * G])
-    edge_out_ref, thick_out_ref, near_out_ref = refs[-3:]
-
-    def store_edge(s, i, at, columns, target, means):
+    edge_refs = refs[: counts[0] * counts[1]]
+    edge_out_ref, thick_out_ref = refs[-2:]
+
+    def store(s, i, at, columns, target, means):
         thick_out_ref[i, at, columns] = target
         for f, value in enumerate(means):
             edge_out_ref[f, i, at, columns] = value
 
-    def store_near(s, i, at, columns, target, means):
-        for f, value in enumerate(means):
-            near_out_ref[f, i, at, columns] = value
-
     fields = [[level_of(ref, f) for ref in edge_refs] for f in range(1, edge_refs[0].shape[0])]
-    remap_rows(weight_ref, sum_ref, counts, (0,), edge_refs, fields, [], store_edge)
-    _, L, R, _ = near_refs[0].shape
-    fields = [[packed_level_of(ref, index, L, R) for ref in bundles[which]] for which, index in near_fields]
-    remap_rows(weight_ref, sum_ref, counts, (0,), near_refs, fields, [], store_near)
-
-
-def remap_edges(counts, weights, edges, near_new, near, near_rest, wait=()):
+    remap_rows(weight_ref, sum_ref, counts, (0,), edge_refs, fields, [], store)
+
+
+def remap_edges(counts, weights, edges, wait=()):
     F, L, R, N = edges[0].shape
-    T = F - 3
-    near_fields = tuple((0, f) if f < T // 2 else (1, f - T // 2) for f in range(T))
-    operands = [*edges, *near_new, *near, *near_rest]
-    return pl.pallas_call(
-        functools.partial(remap_edge_kernel, counts, near_fields),
-        in_specs=[VMEM] * (1 + len(operands)) + after(wait),
-        out_specs=[VMEM] * 3,
+    return pl.pallas_call(
+        functools.partial(remap_edge_kernel, counts),
+        in_specs=[VMEM] * (1 + len(edges)) + after(wait),
+        out_specs=[VMEM] * 2,
         out_shape=[
             jax.ShapeDtypeStruct((F - 1, L, R, N), jnp.float32),
             jax.ShapeDtypeStruct((L, R, N), jnp.float32),
-            jax.ShapeDtypeStruct((T, *near_new[0].shape[1:]), jnp.float32),
         ],
         scratch_shapes=[pltpu.VMEM((weights.shape[0] + 1, 8, LANES), jnp.float32)],
         compiler_params=params(),
-        cost_estimate=cost(len(edges) * L * L * R * N * 40, 4 * R * N * L * len(operands) * F),
+        cost_estimate=cost(len(edges) * L * L * R * N * 20, 4 * R * N * L * len(edges) * F),
         name="remap_edges",
+    )(weights, *edges, *wait)
+
+
+def remap_near_kernel(counts, weight_ref, *refs):
+    *refs, near_out_ref, sum_ref = refs
+    G = counts[0] * counts[1]
+    near_refs, bundles = refs[:G], (refs[G : 2 * G], refs[2 * G : 3 * G])
+    T, L, R, _ = near_out_ref.shape
+
+    def store(s, i, at, columns, target, means):
+        for f, value in enumerate(means):
+            near_out_ref[f, i, at, columns] = value
+
+    fields = [[packed_level_of(ref, f % (T // 2), L, R) for ref in bundles[f // (T // 2)]] for f in range(T)]
+    remap_rows(weight_ref, sum_ref, counts, (0,), near_refs, fields, [], store)
+
+
+def remap_near(counts, weights, total, near_new, near, near_rest, wait=()):
+    _, L, R, N = near_new[0].shape
+    operands = [*near_new, *near, *near_rest]
+    return pl.pallas_call(
+        functools.partial(remap_near_kernel, counts),
+        in_specs=[VMEM] * (1 + len(operands)) + after(wait),
+        out_specs=VMEM,
+        out_shape=jax.ShapeDtypeStruct((total, L, R, N), jnp.float32),
+        scratch_shapes=[pltpu.VMEM((weights.shape[0] + 1, 8, LANES), jnp.float32)],
+        compiler_params=params(),
+        cost_estimate=cost(len(near) * L * L * R * N * 20, 4 * R * N * L * len(near) * (1 + total)),
+        name="remap_near",
     )(weights, *operands, *wait)
 
 
@@ -594,30 +631,70 @@
     )(own, near, edge, thick, thick_edge, *arrived)
 
 
-def finish_winds_kernel(count, own_ref, edge_ref, *refs):
-    arrived_refs, out_refs = refs[:count], refs[-2:]
-    _, L, R, N = own_ref.shape
+def finish_level(own_ref, edge_ref, arrived_refs, result, f, i, start):
+    R = own_ref.shape[2]
+    total = own_ref[f, i, 1 : R - 1]
+    for ref in arrived_refs:
+        total = total + ref[start : start + R - 2]
+    result[1 : R - 1] = total
+    result[0:1] = edge_ref[f, i, 0:1]
+    result[R - 1 : R] = edge_ref[f, i, 1:2]
+
+
+def finish_winds_kernel(count, cut, own_ref, edge_ref, *refs):
+    arrived_refs, (*out_refs, result_ref, sems) = refs[:count], refs[len(refs) - 4 :]
+    _, L, R, _ = own_ref.shape
+    copies = []
     for f, out_ref in enumerate(out_refs):
         for i in range(L):
-            start = (f * L + i) * (R - 2)
-            total = own_ref[f, i, 1 : R - 1]
-            for ref in arrived_refs:
-                total = total + ref[start : start + R - 2]
-            out_ref[i, 1 : R - 1] = total
-            out_ref[i, 0:1] = edge_ref[f, i, 0:1]
-            out_ref[i, R - 1 : R] = edge_ref[f, i, 1:2]
-
-
-def finish_winds(own, arrived, edge, wait):
-    return pl.pallas_call(
-        functools.partial(finish_winds_kernel, len(arrived)),
+            if f * L + i < cut:
+                finish_level(own_ref, edge_ref, arrived_refs, result_ref.at[f, i], f, i, (f * L + i) * (R - 2))
+                copies.append(pltpu.make_async_copy(result_ref.at[f, i], out_ref.at[i], sems.at[f, i]))
+                copies[-1].start()
+    for copy in copies:
+        copy.wait()
+
+
+def finish_winds(own, arrived, edge, cut, wait):
+    F, L = own.shape[:2]
+    return pl.pallas_call(
+        functools.partial(finish_winds_kernel, len(arrived), cut),
         in_specs=[VMEM] * (2 + len(arrived)) + after(wait),
-        out_specs=[VMEM] * 2,
-        out_shape=[jax.ShapeDtypeStruct(own.shape[1:], jnp.float32)] * 2,
-        compiler_params=params(),
-        cost_estimate=cost(own.size, 12 * own.size),
+        out_specs=[pl.BlockSpec(memory_space=pl.ANY)] * F,
+        out_shape=[jax.ShapeDtypeStruct(own.shape[1:], jnp.float32)] * F,
+        scratch_shapes=[pltpu.VMEM(own.shape, jnp.float32), pltpu.SemaphoreType.DMA((F, L))],
+        compiler_params=params(),
+        cost_estimate=cost(1, 1),
         name="finish_winds",
     )(own, edge, *arrived, *wait)
+
+
+def finish_late_kernel(count, cut, own_ref, edge_ref, *refs):
+    arrived_refs, (out_ref, result_ref, sems) = refs[:count], refs[len(refs) - 3 :]
+    F, L, R, _ = own_ref.shape
+    copies = []
+    for g in range(cut, F * L):
+        i = g % L
+        finish_level(own_ref, edge_ref, arrived_refs, result_ref.at[i], F - 1, i, (g - cut) * (R - 2))
+        copies.append(pltpu.make_async_copy(result_ref.at[i], out_ref.at[i], sems.at[i]))
+        copies[-1].start()
+    for copy in copies:
+        copy.wait()
+
+
+def finish_late(own, arrived, edge, cut, out):
+    L = own.shape[1]
+    return pl.pallas_call(
+        functools.partial(finish_late_kernel, len(arrived), cut),
+        in_specs=[VMEM] * (2 + len(arrived)) + after([out]),
+        out_specs=pl.BlockSpec(memory_space=pl.ANY),
+        out_shape=jax.ShapeDtypeStruct(out.shape, jnp.float32),
+        input_output_aliases={2 + len(arrived): 0},
+        scratch_shapes=[pltpu.VMEM(out.shape, jnp.float32), pltpu.SemaphoreType.DMA((L,))],
+        compiler_params=params(),
+        cost_estimate=cost(1, 1),
+        name="finish_late",
+    )(own, edge, *arrived, out)
 
 
 def edge_kernel(thick_hbm, u_hbm, v_hbm, tracer_hbm, *refs):
@@ -725,22 +802,24 @@
     u, v, edge = second_step(table, lat_rows, thickness, wind_u, wind_v, tracers, up, down, cutoff)
     edges = [edge] + [send(edge, s=s, t=0) for s in away]
     winds = [with_others_of_chip(u), with_others_of_chip(v)]
+    cut = 2 * L - 3
     tracers_own, thick_inner = remap(group, [group], others, tracer_fields, (0,), (0, 0), with_thickness=True, wait=[edge])
+    near_new, near, near_rest = (
+        [a for own in sources for a in with_others_of_chip(own)] for sources in (near_new, near, near_rest)
+    )
+    near_out = remap_near((C, S), weights, T, near_new, near, near_rest, wait=[tracers_own])
     winds_own, *winds_away = remap(
-        group, winds, others, [(0, 0), (1, 0)], range(C), (1, 1), wait=[tracers_own, *arrived[:1]]
+        group, winds, others, [(0, 0), (1, 0)], range(C), (1, 1), cut=cut, wait=[near_out, *arrived[:1]]
     )
-    winds_arrived = sent(winds_away)
-    near_new, near, near_rest, edges = (
-        [a for own in sources for a in with_others_of_chip(own)] for sources in (near_new, near, near_rest, edges)
-    )
-    edge_out, thick_edge, near_out = remap_edges(
-        (C, S), weights, edges, near_new, near, near_rest, wait=winds_away[:1]
-    )
+    winds_arrived, late_arrived = sent(winds_away[0::2]), sent(winds_away[1::2])
+    edges = [a for own in edges for a in with_others_of_chip(own)]
+    edge_out, thick_edge = remap_edges((C, S), weights, edges, wait=winds_away[:1])
 
     tracers_out, thickness_out, token = finish_tracers(
         tracers_own, near_out, edge_out, thick_inner, thick_edge, arrived
     )
-    u_out, v_out = finish_winds(winds_own, winds_arrived, edge_out, [token])
+    u_out, v_out = finish_winds(winds_own, winds_arrived, edge_out, cut, [token])
+    v_out = finish_late(winds_own, late_arrived, edge_out, cut, v_out)
     return thickness_out, u_out, v_out, tracers_out
 
 

time: 50.6 us -> 52.5 us (1.038)
  waiting for transfers between devices: 11.6 us -> 14.3 us
  starting transfers between devices: 18.3 us -> 16.7 us
  Pallas kernels: 19.4 us -> 20.2 us
    ppermute x6 -> x7, waiting for transfers between devices: 5.99 us -> 8.94 us  [shifted(): lax.ppermute(value, 'lev', [(i, (i + s) % lev_count) for i in range(lev_c...]
    ppermute x6 -> x7, starting transfers between devices: 10.1 us -> 8.58 us  [shifted(): lax.ppermute(value, 'lev', [(i, (i + s) % lev_count) for i in range(lev_c...]
    pallas_call x2 -> x4, Pallas kernels: 4.65 us -> 5.35 us  [the longest x1 2.02 us: remap_near(): pl.pallas_call(functools.partial(remap_near_kernel, counts), in_specs=[VM...]
    ppermute x1, waiting for transfers between devices: 2.3 us -> 1.73 us  [per_device(): up = lax.ppermute(last, 'lat', northward)]
  transfers between devices with their start and end apart: 20 -> 21, of which waited for: 9 -> 9; matrix products, arithmetic and copies ran while one was open for 0% -> 0% of each run, Pallas kernels for 33% -> 34%
where the time goes in v15:
time: 52.5 us; the launch traced here: 52.3 us
  Pallas kernels  20.2 us (38%)
  starting transfers between devices  16.7 us (32%)
  waiting for transfers between devices  14.3 us (27%)
  between operations  0.91 us (2%)
    ppermute x7, waiting for transfers between devices, shifted(): lax.ppermute(value, 'lev', [(i, (i + s) % lev_count) for i in range(lev_c...  8.94 us
    ppermute x7, starting transfers between devices, shifted(): lax.ppermute(value, 'lev', [(i, (i + s) % lev_count) for i in range(lev_c...  8.58 us
    ppermute x1, starting transfers between devices, per_device(): up = lax.ppermute(last, 'lat', northward)  4.55 us
    pallas_call x3, Pallas kernels, remap_parts(): pl.pallas_call(functools.partial(remap_kernel, counts, tuple(steps), tupl...  4.46 us
    ppermute x12, waiting for transfers between devices, shifted(): lax.ppermute(value, 'sub', [(i, (i + t) % sub_count) for i in range(sub_c...  3.64 us
    pallas_call x1, Pallas kernels, second_step(): pl.pallas_call(functools.partial(second_kernel, lat_rows), grid=(L,), in_...  3.61 us
    ppermute x12, starting transfers between devices, shifted(): lax.ppermute(value, 'sub', [(i, (i + t) % sub_count) for i in range(sub_c...  2.29 us
    pallas_call x1, Pallas kernels, remap_near(): pl.pallas_call(functools.partial(remap_near_kernel, counts), in_specs=[VM...  2.02 us
  transfers between devices with their start and end apart: 21, of which 9 were waited for; matrix products, arithmetic and copies ran while one was open for 0% of the time, Pallas kernels for 34%

profile of v15, /device:TPU:0, one launch (start us, length us, event | category | flops | bytes accessed | tf_op | source)
XLA Modules:
  0.0 52.3 jit_solution(1593804409036487937)
XLA Ops:
  0.6 1.9 %first_step.1 = (f32[4,16,1152]{2,1,0:T(8,128)S(1)}, f32[234,128]{1,0:T(8,128)S(1)}, f32[1,4,3,1152]{3,2,1,0:T(4,128)S(1)}, f32[4,16,1152]{2,1,0:T(8,128)S(1)}, ...) custom-call(f32[4,24,128]{2,1,0:T(8,128)} %constant.6.clone.table_hbm.table_ref, ...), custom_call_target="tpu_custom_call" | custom-call | flops 2949120 | bytes 4423680 | tf_op jit(solution)/shard_map/first_step/pallas_call | solution.py:139
  2.5 3.0 %collective-permute-start.1 = (f32[234,128]{1,0:T(8,128)S(1)}, f32[234,128]{1,0:T(8,128)S(1)}, u32[]{:S(2)}, u32[]{:S(2)}) collective-permute-start(f32[234,128]{1,0:T(8,128)S(1)} %get-tuple-element.41), channel_id=1, source_target_pairs={{0,2},{2,0},{1,3},{3,1},{4,6},{6,4},{5,7},{7,5},{8,10},{10,8},{9,1... | collective-permute-start | bytes 359432 | tf_op jit(solution)/shard_map/ppermute | solution.py:751
  5.5 1.7 %inner_step.1 = (f32[5,4,16,1152]{3,2,1,0:T(8,128)S(1)}, f32[24,1152]{1,0:T(8,128)S(1)}, f32[24,1152]{1,0:T(8,128)S(1)}) custom-call(f32[4,24,128]{2,1,0:T(8,128)S(1)} %copy-done.6, f32[4,16,1152]{2,1,0:T(8,128)S(1)} %get-tuple-element.35.new_ref, f32[4,16,1152]{2,1,0:T(8,128)S(1)} %get-tuple-element.36.thick_ref, ...), custom_call_target="tpu_custom_call" | custom-call | flops 9584640 | bytes 4718592 | tf_op jit(solution)/shard_map/inner_step/pallas_call | solution.py:186
  7.4 2.0 %collective-permute-start.4 = (f32[24,1152]{1,0:T(8,128)S(1)}, f32[24,1152]{1,0:T(8,128)S(1)}, u32[]{:S(2)}, u32[]{:S(2)}) collective-permute-start(f32[24,1152]{1,0:T(8,128)S(1)} %get-tuple-element.46.refs_8_), channel_id=1, source_target_pairs={{0,2},{2,0},{1,3},{3,1},{4,6},{6,4},{5,7},{7,5},{8,10},{10,8},{9,1... | collective-permute-start | bytes 331784 | tf_op jit(solution)/shard_map/ppermute | solution.py:751
  9.5 1.3 %collective-permute-done.2.refs_1_ = f32[16,1152]{1,0:T(8,128)S(1)} collective-permute-done((f32[16,1152]{1,0:T(8,128)S(1)}, f32[16,1152]{1,0:T(8,128)S(1)}, u32[]{:S(2)}, u32[]{:S(2)}) %collective-permute-start.2) | collective-permute-done | bytes 73760 | tf_op jit(solution)/shard_map/ppermute | solution.py:753
  10.9 1.4 %remap_parts.3.refs_0_ = f32[176,1152]{1,0:T(8,128)S(1)} custom-call(f32[16,8,128]{2,1,0:T(8,128)S(1)} %broadcast_in_dim.4.weight_ref, f32[5,4,16,1152]{3,2,1,0:T(8,128)S(1)} %get-tuple-element.40.refs_0_.refs_2_, f32[5,4,16,1152]{3,2,1,0:T(8,128)S(1)} %collective-permute-done.refs_1_.refs_3_, f32[5,4,16,1152]{3,2,1,0:T(8,128)S(1)} %get-tuple-element.40.refs_0_.refs_2_, ...), custom_call_target="tpu_custom_call" | custom-call | flops 7667712 | bytes 4423680 | tf_op jit(solution)/shard_map/remap_parts/pallas_call | solution.py:525
  12.4 1.3 %collective-permute-start.18 = (f32[176,1152]{1,0:T(8,128)S(1)}, f32[176,1152]{1,0:T(8,128)S(1)}, u32[]{:S(2)}, u32[]{:S(2)}) collective-permute-start(f32[176,1152]{1,0:T(8,128)S(1)} %remap_parts.3.refs_0_), channel_id=1, source_target_pairs={{0,2},{2,0},{1,3},{3,1},{4,6},{6,4},{5,7},{7,5},{8,10},{10,8},{9,1... | collective-permute-start | bytes 2433032 | tf_op jit(solution)/shard_map/ppermute | solution.py:751
  13.6 1.5 %collective-permute-done.4.refs_2_.refs_10_ = f32[24,1152]{1,0:T(8,128)S(1)} collective-permute-done((f32[24,1152]{1,0:T(8,128)S(1)}, f32[24,1152]{1,0:T(8,128)S(1)}, u32[]{:S(2)}, u32[]{:S(2)}) %collective-permute-start.4) | collective-permute-done | bytes 110624 | tf_op jit(solution)/shard_map/ppermute | solution.py:751
  15.1 1.7 %edge_rows.1 = (f32[6,4,1,1152]{3,2,1,0:T(1,128)S(1)}, f32[8,4,1,1152]{3,2,1,0:T(1,128)S(1)}) custom-call(f32[4,16,1152]{2,1,0:T(8,128)} %thick_ref.1, f32[4,16,1152]{2,1,0:T(8,128)} %u_ref.1, f32[4,16,1152]{2,1,0:T(8,128)} %v_ref.1, f32[4,4,16,1152]{3,2,1,0:T(8,128)} %tracer_ref.1, f32[176,1152]{1,0:T(8,128)S(1)} %remap_parts.3.refs_0_, ...), custom_call_target="tpu_custom_call" | custom-call | flops 10000000000 | bytes 1000000000 | tf_op jit(solution)/shard_map/edge_rows/pallas_call | solution.py:729
  16.9 1.3 %collective-permute-start.6 = (f32[8,4,1,1152]{3,2,1,0:T(1,128)S(1)}, f32[8,4,1,1152]{3,2,1,0:T(1,128)S(1)}, u32[]{:S(2)}, u32[]{:S(2)}) collective-permute-start(f32[8,4,1,1152]{3,2,1,0:T(1,128)S(1)} %get-tuple-element.48), channel_id=1, source_target_pairs={{4,0},{8,4},{12,8},{5,1},{9,5},{13,9},{6,2},{10,6},{14,10},{7,3},{... | collective-permute-start | bytes 442376 | tf_op jit(solution)/shard_map/ppermute | solution.py:801
  18.2 4.6 %collective-permute-start.5 = (f32[6,4,1,1152]{3,2,1,0:T(1,128)S(1)}, f32[6,4,1,1152]{3,2,1,0:T(1,128)S(1)}, u32[]{:S(2)}, u32[]{:S(2)}) collective-permute-start(f32[6,4,1,1152]{3,2,1,0:T(1,128)S(1)} %get-tuple-element.47), channel_id=1, source_target_pairs={{0,4},{4,8},{8,12},{1,5},{5,9},{9,13},{2,6},{6,10},{10,14},{3,7},{... | collective-permute-start | bytes 331784 | tf_op jit(solution)/shard_map/ppermute | solution.py:800
  23.3 1.7 %collective-permute-done.5.up_ref = f32[6,4,1,1152]{3,2,1,0:T(1,128)S(1)} collective-permute-done((f32[6,4,1,1152]{3,2,1,0:T(1,128)S(1)}, f32[6,4,1,1152]{3,2,1,0:T(1,128)S(1)}, u32[]{:S(2)}, u32[]{:S(2)}) %collective-permute-start.5) | collective-permute-done | bytes 110624 | tf_op jit(solution)/shard_map/ppermute | solution.py:800
  25.2 3.6 %second_step.1 = (f32[1,4,16,1152]{3,2,1,0:T(8,128)S(1)}, f32[1,4,16,1152]{3,2,1,0:T(8,128)S(1)}, f32[7,4,2,1152]{3,2,1,0:T(2,128)S(1)}) custom-call(f32[4,24,128]{2,1,0:T(8,128)S(1)} %copy-done.6, f32[4,16,1152]{2,1,0:T(8,128)S(1)} %copy-done.1, f32[4,16,1152]{2,1,0:T(8,128)S(1)} %copy-done.2, f32[4,16,1152]{2,1,0:T(8,128)S(1)} %copy-done.3, ...), custom_call_target="tpu_custom_call" | custom-call | flops 503316480 | bytes 3538944 | tf_op jit(solution)/shard_map/second_step/pallas_call | solution.py:324
  30.0 1.1 %collective-permute-done.8.refs_3_ = f32[1,4,3,1152]{3,2,1,0:T(4,128)S(1)} collective-permute-done((f32[1,4,3,1152]{3,2,1,0:T(4,128)S(1)}, f32[1,4,3,1152]{3,2,1,0:T(4,128)S(1)}, u32[]{:S(2)}, u32[]{:S(2)}) %collective-permute-start.8) | collective-permute-done | bytes 55328 | tf_op jit(solution)/shard_map/ppermute | solution.py:753
  31.6 1.3 %remap_parts.4 = (f32[4,4,16,1152]{3,2,1,0:T(8,128)S(1)}, f32[4,16,1152]{2,1,0:T(8,128)S(1)}) custom-call(f32[16,8,128]{2,1,0:T(8,128)S(1)} %broadcast_in_dim.4.weight_ref, f32[5,4,16,1152]{3,2,1,0:T(8,128)S(1)} %get-tuple-element.40.refs_0_.refs_2_, f32[5,4,16,1152]{3,2,1,0:T(8,128)S(1)} %collective-permute-done.refs_1_.refs_3_, ...), custom_call_target="tpu_custom_call" | custom-call | flops 7667712 | bytes 4423680 | tf_op jit(solution)/shard_map/remap_parts/pallas_call | solution.py:525
  33.0 2.0 %remap_near.1.refs_8_.near_ref = f32[4,4,3,1152]{3,2,1,0:T(4,128)S(1)} custom-call(f32[16,8,128]{2,1,0:T(8,128)S(1)} %broadcast_in_dim.4.weight_ref, f32[1,4,3,1152]{3,2,1,0:T(4,128)S(1)} %get-tuple-element.51.refs_0_, f32[1,4,3,1152]{3,2,1,0:T(4,128)S(1)} %collective-permute-done.7.refs_1_, f32[1,4,3,1152]{3,2,1,0:T(4,128)S(1)} %get-tuple-element.52.refs_2_, ...), custom_call_target="tpu_custom_call" | custom-call | flops 4423680 | bytes 1105920 | tf_op jit(solution)/shard_map/remap_near/pallas_call | solution.py:585
  35.0 1.8 %remap_parts.5 = (f32[2,4,16,1152]{3,2,1,0:T(8,128)S(1)}, f32[70,1152]{1,0:T(8,128)S(1)}, f32[42,1152]{1,0:T(8,128)S(1)}) custom-call(f32[16,8,128]{2,1,0:T(8,128)S(1)} %broadcast_in_dim.4.weight_ref, f32[5,4,16,1152]{3,2,1,0:T(8,128)S(1)} %get-tuple-element.40.refs_0_.refs_2_, f32[5,4,16,1152]{3,2,1,0:T(8,128)S(1)} %collective-permute-done.refs_1_.refs_3_, ...), custom_call_target="tpu_custom_call" | custom-call | flops 10616832 | bytes 3538944 | tf_op jit(solution)/shard_map/remap_parts/pallas_call | solution.py:525
  36.8 1.7 %collective-permute-start.19 = (f32[70,1152]{1,0:T(8,128)S(1)}, f32[70,1152]{1,0:T(8,128)S(1)}, u32[]{:S(2)}, u32[]{:S(2)}) collective-permute-start(f32[70,1152]{1,0:T(8,128)S(1)} %get-tuple-element.55.refs_4_), channel_id=1, source_target_pairs={{0,2},{2,0},{1,3},{3,1},{4,6},{6,4},{5,7},{7,5},{8,10},{10,8},{9,1... | collective-permute-start | bytes 967688 | tf_op jit(solution)/shard_map/ppermute | solution.py:751
  38.6 1.0 %collective-permute-done.14.refs_2_ = f32[7,4,2,1152]{3,2,1,0:T(2,128)S(1)} collective-permute-done((f32[7,4,2,1152]{3,2,1,0:T(2,128)S(1)}, f32[7,4,2,1152]{3,2,1,0:T(2,128)S(1)}, u32[]{:S(2)}, u32[]{:S(2)}) %collective-permute-start.14) | collective-permute-done | bytes 258080 | tf_op jit(solution)/shard_map/ppermute | solution.py:751
  40.0 1.2 %collective-permute-done.15.refs_3_ = f32[7,4,2,1152]{3,2,1,0:T(2,128)S(1)} collective-permute-done((f32[7,4,2,1152]{3,2,1,0:T(2,128)S(1)}, f32[7,4,2,1152]{3,2,1,0:T(2,128)S(1)}, u32[]{:S(2)}, u32[]{:S(2)}) %collective-permute-start.15) | collective-permute-done | bytes 258080 | tf_op jit(solution)/shard_map/ppermute | solution.py:753
  41.1 1.8 %remap_edges.1 = (f32[6,4,2,1152]{3,2,1,0:T(2,128)S(1)}, f32[4,2,1152]{2,1,0:T(2,128)S(1)}) custom-call(f32[16,8,128]{2,1,0:T(8,128)S(1)} %broadcast_in_dim.4.weight_ref, f32[7,4,2,1152]{3,2,1,0:T(2,128)S(1)} %get-tuple-element.49.refs_6_.refs_0_, f32[7,4,2,1152]{3,2,1,0:T(2,128)S(1)} %collective-permute-done.13.refs_1_, ...), custom_call_target="tpu_custom_call" | custom-call | flops 2949120 | bytes 1032192 | tf_op jit(solution)/shard_map/remap_edges/pallas_call | solution.py:553
  42.9 1.4 %finish_tracers.1 = (f32[4,4,16,1152]{3,2,1,0:T(8,128)}, f32[4,16,1152]{2,1,0:T(8,128)}, f32[8,128]{1,0:T(8,128)S(1)}) custom-call(f32[4,4,16,1152]{3,2,1,0:T(8,128)S(1)} %get-tuple-element.50.refs_12_.own_ref, f32[4,4,3,1152]{3,2,1,0:T(4,128)S(1)} %remap_near.1.refs_8_.near_ref, f32[6,4,2,1152]{3,2,1,0:T(2,128)S(1)} %get-tuple-element.56.edge_ref, ...), custom_call_target="tpu_custom_call" | custom-call | flops 589824 | bytes 3538944 | tf_op jit(solution)/shard_map/finish_tracers/pallas_call | solution.py:619
  44.3 3.1 %collective-permute-done.19.refs_0_ = f32[70,1152]{1,0:T(8,128)S(1)} collective-permute-done((f32[70,1152]{1,0:T(8,128)S(1)}, f32[70,1152]{1,0:T(8,128)S(1)}, u32[]{:S(2)}, u32[]{:S(2)}) %collective-permute-start.19) | collective-permute-done | bytes 322592 | tf_op jit(solution)/shard_map/ppermute | solution.py:751
  48.3 3.3 %collective-permute-done.20.refs_0_ = f32[42,1152]{1,0:T(8,128)S(1)} collective-permute-done((f32[42,1152]{1,0:T(8,128)S(1)}, f32[42,1152]{1,0:T(8,128)S(1)}, u32[]{:S(2)}, u32[]{:S(2)}) %collective-permute-start.20) | collective-permute-done | bytes 193568 | tf_op jit(solution)/shard_map/ppermute | solution.py:751
  (52 shorter events, 4.9 us)
Async XLA Ops:
  2.5 6.9 %collective-permute-start.1 = (f32[234,128]{1,0:T(8,128)S(1)}, f32[234,128]{1,0:T(8,128)S(1)}, u32[]{:S(2)}, u32[]{:S(2)}) collective-permute-start(f32[234,128]{1,0:T(8,128)S(1)} %get-tuple-element.41), channel_id=1, source_target_pairs={{0,2},{2,0},{1,3},{3,1},{4,6},{6,4},{5,7},{7,5},{8,10},{10,8},{9,1... | collective-permute-start | bytes 359432 | tf_op jit(solution)/shard_map/ppermute | solution.py:751
  7.2 3.6 %collective-permute-start = (f32[5,4,16,1152]{3,2,1,0:T(8,128)S(1)}, f32[5,4,16,1152]{3,2,1,0:T(8,128)S(1)}, u32[]{:S(2)}, u32[]{:S(2)}) collective-permute-start(f32[5,4,16,1152]{3,2,1,0:T(8,128)S(1)} %get-tuple-element.40.refs_0_.refs_2_), channel_id=1, source_target_pairs={{0,1},{1,0},{2,3},{3,2},{4,5},{5,4},{6,7},{7,6},{8,9},{9,8},{10,11... | collective-permute-start | bytes 4423688 | tf_op jit(solution)/shard_map/ppermute | solution.py:753
  7.3 6.3 %collective-permute-start.3 = (f32[24,1152]{1,0:T(8,128)S(1)}, f32[24,1152]{1,0:T(8,128)S(1)}, u32[]{:S(2)}, u32[]{:S(2)}) collective-permute-start(f32[24,1152]{1,0:T(8,128)S(1)} %get-tuple-element.42.refs_0_.refs_4_), channel_id=1, source_target_pairs={{0,2},{2,0},{1,3},{3,1},{4,6},{6,4},{5,7},{7,5},{8,10},{10,8},{9,1... | collective-permute-start | bytes 331784 | tf_op jit(solution)/shard_map/ppermute | solution.py:751
  7.4 7.7 %collective-permute-start.4 = (f32[24,1152]{1,0:T(8,128)S(1)}, f32[24,1152]{1,0:T(8,128)S(1)}, u32[]{:S(2)}, u32[]{:S(2)}) collective-permute-start(f32[24,1152]{1,0:T(8,128)S(1)} %get-tuple-element.46.refs_8_), channel_id=1, source_target_pairs={{0,2},{2,0},{1,3},{3,1},{4,6},{6,4},{5,7},{7,5},{8,10},{10,8},{9,1... | collective-permute-start | bytes 331784 | tf_op jit(solution)/shard_map/ppermute | solution.py:751
  9.4 1.3 %collective-permute-start.2 = (f32[16,1152]{1,0:T(8,128)S(1)}, f32[16,1152]{1,0:T(8,128)S(1)}, u32[]{:S(2)}, u32[]{:S(2)}) collective-permute-start(f32[16,1152]{1,0:T(8,128)S(1)} %get-tuple-element.43.refs_0_), channel_id=1, source_target_pairs={{0,1},{1,0},{2,3},{3,2},{4,5},{5,4},{6,7},{7,6},{8,9},{9,8},{10,11... | collective-permute-start | bytes 221192 | tf_op jit(solution)/shard_map/ppermute | solution.py:753
  12.3 12.8 %copy-start = (f32[4,4,16,1152]{3,2,1,0:T(8,128)S(1)}, f32[4,4,16,1152]{3,2,1,0:T(8,128)}, u32[]{:S(2)}) copy-start(f32[4,4,16,1152]{3,2,1,0:T(8,128)} %tracer_ref.1) | copy-start | bytes 3538948
  12.3 12.8 %copy-start.1 = (f32[4,16,1152]{2,1,0:T(8,128)S(1)}, f32[4,16,1152]{2,1,0:T(8,128)}, u32[]{:S(2)}) copy-start(f32[4,16,1152]{2,1,0:T(8,128)} %thick_ref.1) | copy-start | bytes 884740
  12.3 12.8 %copy-start.2 = (f32[4,16,1152]{2,1,0:T(8,128)S(1)}, f32[4,16,1152]{2,1,0:T(8,128)}, u32[]{:S(2)}) copy-start(f32[4,16,1152]{2,1,0:T(8,128)} %u_ref.1) | copy-start | bytes 884740
  12.4 22.6 %collective-permute-start.18 = (f32[176,1152]{1,0:T(8,128)S(1)}, f32[176,1152]{1,0:T(8,128)S(1)}, u32[]{:S(2)}, u32[]{:S(2)}) collective-permute-start(f32[176,1152]{1,0:T(8,128)S(1)} %remap_parts.3.refs_0_), channel_id=1, source_target_pairs={{0,2},{2,0},{1,3},{3,1},{4,6},{6,4},{5,7},{7,5},{8,10},{10,8},{9,1... | collective-permute-start | bytes 2433032 | tf_op jit(solution)/shard_map/ppermute | solution.py:751
  16.9 8.2 %collective-permute-start.6 = (f32[8,4,1,1152]{3,2,1,0:T(1,128)S(1)}, f32[8,4,1,1152]{3,2,1,0:T(1,128)S(1)}, u32[]{:S(2)}, u32[]{:S(2)}) collective-permute-start(f32[8,4,1,1152]{3,2,1,0:T(1,128)S(1)} %get-tuple-element.48), channel_id=1, source_target_pairs={{4,0},{8,4},{12,8},{5,1},{9,5},{13,9},{6,2},{10,6},{14,10},{7,3},{... | collective-permute-start | bytes 442376 | tf_op jit(solution)/shard_map/ppermute | solution.py:801
  18.2 6.9 %collective-permute-start.5 = (f32[6,4,1,1152]{3,2,1,0:T(1,128)S(1)}, f32[6,4,1,1152]{3,2,1,0:T(1,128)S(1)}, u32[]{:S(2)}, u32[]{:S(2)}) collective-permute-start(f32[6,4,1,1152]{3,2,1,0:T(1,128)S(1)} %get-tuple-element.47), channel_id=1, source_target_pairs={{0,4},{4,8},{8,12},{1,5},{5,9},{9,13},{2,6},{6,10},{10,14},{3,7},{... | collective-permute-start | bytes 331784 | tf_op jit(solution)/shard_map/ppermute | solution.py:800
  22.7 6.7 %collective-permute-start.9 = (f32[24,1152]{1,0:T(8,128)S(1)}, f32[24,1152]{1,0:T(8,128)S(1)}, u32[]{:S(2)}, u32[]{:S(2)}) collective-permute-start(f32[24,1152]{1,0:T(8,128)S(1)} %get-tuple-element.42.refs_0_.refs_4_), channel_id=1, source_target_pairs={{0,1},{1,0},{2,3},{3,2},{4,5},{5,4},{6,7},{7,6},{8,9},{9,8},{10,11... | collective-permute-start | bytes 331784 | tf_op jit(solution)/shard_map/ppermute | solution.py:753
  22.8 6.5 %collective-permute-start.7 = (f32[1,4,3,1152]{3,2,1,0:T(4,128)S(1)}, f32[1,4,3,1152]{3,2,1,0:T(4,128)S(1)}, u32[]{:S(2)}, u32[]{:S(2)}) collective-permute-start(f32[1,4,3,1152]{3,2,1,0:T(4,128)S(1)} %get-tuple-element.51.refs_0_), channel_id=1, source_target_pairs={{0,1},{1,0},{2,3},{3,2},{4,5},{5,4},{6,7},{7,6},{8,9},{9,8},{10,11... | collective-permute-start | bytes 165896 | tf_op jit(solution)/shard_map/ppermute | solution.py:753
  25.0 4.8 %collective-permute-start.11 = (f32[24,1152]{1,0:T(8,128)S(1)}, f32[24,1152]{1,0:T(8,128)S(1)}, u32[]{:S(2)}, u32[]{:S(2)}) collective-permute-start(f32[24,1152]{1,0:T(8,128)S(1)} %get-tuple-element.46.refs_8_), channel_id=1, source_target_pairs={{0,1},{1,0},{2,3},{3,2},{4,5},{5,4},{6,7},{7,6},{8,9},{9,8},{10,11... | collective-permute-start | bytes 331784 | tf_op jit(solution)/shard_map/ppermute | solution.py:753
  28.8 6.2 %collective-permute-start.16 = (f32[1,4,16,1152]{3,2,1,0:T(8,128)S(1)}, f32[1,4,16,1152]{3,2,1,0:T(8,128)S(1)}, u32[]{:S(2)}, u32[]{:S(2)}) collective-permute-start(f32[1,4,16,1152]{3,2,1,0:T(8,128)S(1)} %get-tuple-element.53.refs_2_), channel_id=1, source_target_pairs={{0,1},{1,0},{2,3},{3,2},{4,5},{5,4},{6,7},{7,6},{8,9},{9,8},{10,11... | collective-permute-start | bytes 884744 | tf_op jit(solution)/shard_map/ppermute | solution.py:753
  29.4 5.6 %collective-permute-start.17 = (f32[1,4,16,1152]{3,2,1,0:T(8,128)S(1)}, f32[1,4,16,1152]{3,2,1,0:T(8,128)S(1)}, u32[]{:S(2)}, u32[]{:S(2)}) collective-permute-start(f32[1,4,16,1152]{3,2,1,0:T(8,128)S(1)} %get-tuple-element.54.refs_4_), channel_id=1, source_target_pairs={{0,1},{1,0},{2,3},{3,2},{4,5},{5,4},{6,7},{7,6},{8,9},{9,8},{10,11... | collective-permute-start | bytes 884744 | tf_op jit(solution)/shard_map/ppermute | solution.py:753
  29.4 1.6 %collective-permute-start.8 = (f32[1,4,3,1152]{3,2,1,0:T(4,128)S(1)}, f32[1,4,3,1152]{3,2,1,0:T(4,128)S(1)}, u32[]{:S(2)}, u32[]{:S(2)}) collective-permute-start(f32[1,4,3,1152]{3,2,1,0:T(4,128)S(1)} %get-tuple-element.52.refs_2_), channel_id=1, source_target_pairs={{0,1},{1,0},{2,3},{3,2},{4,5},{5,4},{6,7},{7,6},{8,9},{9,8},{10,11... | collective-permute-start | bytes 165896 | tf_op jit(solution)/shard_map/ppermute | solution.py:753
  29.9 1.5 %collective-permute-start.10 = (f32[24,1152]{1,0:T(8,128)S(1)}, f32[24,1152]{1,0:T(8,128)S(1)}, u32[]{:S(2)}, u32[]{:S(2)}) collective-permute-start(f32[24,1152]{1,0:T(8,128)S(1)} %collective-permute-done.3.refs_1_.refs_6_), channel_id=1, source_target_pairs={{0,1},{1,0},{2,3},{3,2},{4,5},{5,4},{6,7},{7,6},{8,9},{9,8},{10,11... | collective-permute-start | bytes 331784 | tf_op jit(solution)/shard_map/ppermute | solution.py:753
  31.1 8.5 %collective-permute-start.14 = (f32[7,4,2,1152]{3,2,1,0:T(2,128)S(1)}, f32[7,4,2,1152]{3,2,1,0:T(2,128)S(1)}, u32[]{:S(2)}, u32[]{:S(2)}) collective-permute-start(f32[7,4,2,1152]{3,2,1,0:T(2,128)S(1)} %get-tuple-element.49.refs_6_.refs_0_), channel_id=1, source_target_pairs={{0,2},{2,0},{1,3},{3,1},{4,6},{6,4},{5,7},{7,5},{8,10},{10,8},{9,1... | collective-permute-start | bytes 774152 | tf_op jit(solution)/shard_map/ppermute | solution.py:751
  31.4 1.6 %collective-permute-start.12 = (f32[24,1152]{1,0:T(8,128)S(1)}, f32[24,1152]{1,0:T(8,128)S(1)}, u32[]{:S(2)}, u32[]{:S(2)}) collective-permute-start(f32[24,1152]{1,0:T(8,128)S(1)} %collective-permute-done.4.refs_2_.refs_10_), channel_id=1, source_target_pairs={{0,1},{1,0},{2,3},{3,2},{4,5},{5,4},{6,7},{7,6},{8,9},{9,8},{10,11... | collective-permute-start | bytes 331784 | tf_op jit(solution)/shard_map/ppermute | solution.py:753
  36.8 10.7 %collective-permute-start.19 = (f32[70,1152]{1,0:T(8,128)S(1)}, f32[70,1152]{1,0:T(8,128)S(1)}, u32[]{:S(2)}, u32[]{:S(2)}) collective-permute-start(f32[70,1152]{1,0:T(8,128)S(1)} %get-tuple-element.55.refs_4_), channel_id=1, source_target_pairs={{0,2},{2,0},{1,3},{3,1},{4,6},{6,4},{5,7},{7,5},{8,10},{10,8},{9,1... | collective-permute-start | bytes 967688 | tf_op jit(solution)/shard_map/ppermute | solution.py:751
  38.4 1.5 %collective-permute-start.13 = (f32[7,4,2,1152]{3,2,1,0:T(2,128)S(1)}, f32[7,4,2,1152]{3,2,1,0:T(2,128)S(1)}, u32[]{:S(2)}, u32[]{:S(2)}) collective-permute-start(f32[7,4,2,1152]{3,2,1,0:T(2,128)S(1)} %get-tuple-element.49.refs_6_.refs_0_), channel_id=1, source_target_pairs={{0,1},{1,0},{2,3},{3,2},{4,5},{5,4},{6,7},{7,6},{8,9},{9,8},{10,11... | collective-permute-start | bytes 774152 | tf_op jit(solution)/shard_map/ppermute | solution.py:753
  39.6 1.5 %collective-permute-start.15 = (f32[7,4,2,1152]{3,2,1,0:T(2,128)S(1)}, f32[7,4,2,1152]{3,2,1,0:T(2,128)S(1)}, u32[]{:S(2)}, u32[]{:S(2)}) collective-permute-start(f32[7,4,2,1152]{3,2,1,0:T(2,128)S(1)} %collective-permute-done.14.refs_2_), channel_id=1, source_target_pairs={{0,1},{1,0},{2,3},{3,2},{4,5},{5,4},{6,7},{7,6},{8,9},{9,8},{10,11... | collective-permute-start | bytes 774152 | tf_op jit(solution)/shard_map/ppermute | solution.py:753
  39.6 12.0 %collective-permute-start.20 = (f32[42,1152]{1,0:T(8,128)S(1)}, f32[42,1152]{1,0:T(8,128)S(1)}, u32[]{:S(2)}, u32[]{:S(2)}) collective-permute-start(f32[42,1152]{1,0:T(8,128)S(1)} %get-tuple-element.63), channel_id=1, source_target_pairs={{0,2},{2,0},{1,3},{3,1},{4,6},{6,4},{5,7},{7,5},{8,10},{10,8},{9,1... | collective-permute-start | bytes 580616 | tf_op jit(solution)/shard_map/ppermute | solution.py:751
  (6 other events, 59.5 us)

commit v16 on v14

--- a/solution.py
+++ b/solution.py
@@ -82,8 +82,15 @@
     return change - (t_north - south_of(t_north, t_below)) * inverse
 
 
+def packed_at(rows, levels, width):
+    near = len(near_rows(rows)[0])
+    size = rows - 2 + levels * near
+    for a in range(width // LANES):
+        yield a, a * size, [a * size + rows - 2 + k * near for k in range(levels)]
+
+
 def first_kernel(table_hbm, thick_hbm, u_hbm, v_hbm, tracer_hbm, *refs):
-    new_ref, both_ref, near_ref, thick_ref, u_ref, v_ref, tracer_ref, geo_ref, sems = refs
+    new_ref, both_ref, near_ref, thick_ref, u_ref, v_ref, tracer_ref, sum_ref, geo_ref, sems = refs
     L, rows, _ = thick_ref.shape
     near, _ = near_rows(rows)
     table_copy = pltpu.make_async_copy(table_hbm.at[lax.axis_index("lat")], geo_ref, sems.at[3, 0])
@@ -100,7 +107,7 @@
     tracer_copy.start()
     table_copy.wait()
     geo = geo_ref[...]
-    both_ref[...] = jnp.zeros_like(both_ref)
+    sum_ref[...] = jnp.zeros_like(sum_ref)
 
     def level(k, carry):
         for copy in copies(k):
@@ -111,13 +118,15 @@
         new_ref[k] = new
         for j, row in enumerate(near):
             near_ref[0, k, j : j + 1] = new[row : row + 1]
-        both_ref[0:rows] += new
+        sum_ref[...] += new
         return carry
 
     lax.fori_loop(0, L, level, 0)
-    for k in range(L):
-        at = rows + k * len(near)
-        both_ref[at : at + len(near)] = near_ref[0, k]
+    for a, at, each in packed_at(rows, L, thick_ref.shape[2]):
+        lanes = slice(a * LANES, (a + 1) * LANES)
+        both_ref[at : at + rows - 2] = sum_ref[1 : rows - 1, lanes]
+        for k in range(L):
+            both_ref[each[k] : each[k] + len(near)] = near_ref[0, k, :, lanes]
     tracer_copy.wait()
 
 
@@ -126,13 +135,17 @@
     arguments = (thickness, wind_u, wind_v, tracers)
     operands = [pltpu.with_memory_space_constraint(a, pltpu.HBM) for a in (table, *arguments)]
     near = len(near_rows(R)[0])
-    shapes = [(L, R, N), (-(-(R + L * near) // 8) * 8, N), (1, L, near, N)] + [a.shape for a in arguments]
+    shapes = [(L, R, N), ((R - 2 + L * near) * N // LANES, LANES), (1, L, near, N)] + [a.shape for a in arguments]
     return pl.pallas_call(
         first_kernel,
         in_specs=after(operands),
         out_specs=[VMEM] * len(shapes),
         out_shape=[jax.ShapeDtypeStruct(shape, jnp.float32) for shape in shapes],
-        scratch_shapes=[pltpu.VMEM(table.shape[1:], jnp.float32), pltpu.SemaphoreType.DMA((4, max(L, 2)))],
+        scratch_shapes=[
+            pltpu.VMEM((R, N), jnp.float32),
+            pltpu.VMEM(table.shape[1:], jnp.float32),
+            pltpu.SemaphoreType.DMA((4, max(L, 2))),
+        ],
         compiler_params=params(),
         cost_estimate=cost(40 * L * R * N, 4 * L * R * N * (7 + 2 * tracers.shape[0])),
         name="first_step",
@@ -331,11 +344,14 @@
 
 def part_kernel(both_ref, *refs):
     sum_ref, near_ref = refs[-2:]
-    rows = sum_ref.shape[0]
-    sum_ref[...] = both_ref[0:rows]
+    rows, width = sum_ref.shape
     _, L, near, _ = near_ref.shape
-    for k in range(L):
-        near_ref[0, k] = both_ref[rows + k * near : rows + (k + 1) * near]
+    sum_ref[...] = jnp.zeros_like(sum_ref)
+    for a, at, each in packed_at(rows, L, width):
+        lanes = slice(a * LANES, (a + 1) * LANES)
+        sum_ref[1 : rows - 1, lanes] = both_ref[at : at + rows - 2]
+        for k in range(L):
+            near_ref[0, k, :, lanes] = both_ref[each[k] : each[k] + near]
 
 
 def part(both, shape, wait):

time: 50.6 us -> 50.3 us (level)
  starting transfers between devices: 18.3 us -> 16.4 us
  waiting for transfers between devices: 11.6 us -> 13.2 us
    ppermute x6, starting transfers between devices: 10.1 us -> 8.22 us  [shifted(): lax.ppermute(value, 'lev', [(i, (i + s) % lev_count) for i in range(lev_c...]
    ppermute x6, waiting for transfers between devices: 5.99 us -> 7.51 us  [shifted(): lax.ppermute(value, 'lev', [(i, (i + s) % lev_count) for i in range(lev_c...]
where the time goes in v16:
time: 50.3 us; the launch traced here: 50.1 us
  Pallas kernels  19.5 us (39%)
  starting transfers between devices  16.4 us (33%)
  waiting for transfers between devices  13.2 us (26%)
  between operations  0.88 us (2%)
    ppermute x6, starting transfers between devices, shifted(): lax.ppermute(value, 'lev', [(i, (i + s) % lev_count) for i in range(lev_c...  8.22 us
    ppermute x6, waiting for transfers between devices, shifted(): lax.ppermute(value, 'lev', [(i, (i + s) % lev_count) for i in range(lev_c...  7.51 us
    ppermute x1, starting transfers between devices, per_device(): up = lax.ppermute(last, 'lat', northward)  4.55 us
    pallas_call x3, Pallas kernels, remap_parts(): pl.pallas_call(functools.partial(remap_kernel, counts, tuple(steps), tupl...  4.45 us
    pallas_call x1, Pallas kernels, remap_edges(): pl.pallas_call(functools.partial(remap_edge_kernel, counts, near_fields),...  3.71 us
    pallas_call x1, Pallas kernels, second_step(): pl.pallas_call(functools.partial(second_kernel, lat_rows), grid=(L,), in_...  3.62 us
    ppermute x12, waiting for transfers between devices, shifted(): lax.ppermute(value, 'sub', [(i, (i + t) % sub_count) for i in range(sub_c...  3.34 us
    ppermute x12, starting transfers between devices, shifted(): lax.ppermute(value, 'sub', [(i, (i + t) % sub_count) for i in range(sub_c...  2.31 us
  transfers between devices with their start and end apart: 20, of which 9 were waited for; matrix products, arithmetic and copies ran while one was open for 0% of the time, Pallas kernels for 33%

profile of v16, /device:TPU:0, one launch (start us, length us, event | category | flops | bytes accessed | tf_op | source)
XLA Modules:
  0.0 50.1 jit_solution(12568644558161624632)
XLA Ops:
  0.6 1.9 %first_step.1 = (f32[4,16,1152]{2,1,0:T(8,128)S(1)}, f32[234,128]{1,0:T(8,128)S(1)}, f32[1,4,3,1152]{3,2,1,0:T(4,128)S(1)}, f32[4,16,1152]{2,1,0:T(8,128)S(1)}, ...) custom-call(f32[4,24,128]{2,1,0:T(8,128)} %constant.6.clone.table_hbm.table_ref, ...), custom_call_target="tpu_custom_call" | custom-call | flops 2949120 | bytes 4423680 | tf_op jit(solution)/shard_map/first_step/pallas_call | solution.py:139
  2.5 3.0 %collective-permute-start.1 = (f32[234,128]{1,0:T(8,128)S(1)}, f32[234,128]{1,0:T(8,128)S(1)}, u32[]{:S(2)}, u32[]{:S(2)}) collective-permute-start(f32[234,128]{1,0:T(8,128)S(1)} %get-tuple-element.41), channel_id=1, source_target_pairs={{0,2},{2,0},{1,3},{3,1},{4,6},{6,4},{5,7},{7,5},{8,10},{10,8},{9,1... | collective-permute-start | bytes 359432 | tf_op jit(solution)/shard_map/ppermute | solution.py:690
  5.5 1.7 %inner_step.1 = (f32[5,4,16,1152]{3,2,1,0:T(8,128)S(1)}, f32[24,1152]{1,0:T(8,128)S(1)}, f32[24,1152]{1,0:T(8,128)S(1)}) custom-call(f32[4,24,128]{2,1,0:T(8,128)S(1)} %copy-done.6, f32[4,16,1152]{2,1,0:T(8,128)S(1)} %get-tuple-element.35.new_ref, f32[4,16,1152]{2,1,0:T(8,128)S(1)} %get-tuple-element.36.thick_ref, ...), custom_call_target="tpu_custom_call" | custom-call | flops 9584640 | bytes 4718592 | tf_op jit(solution)/shard_map/inner_step/pallas_call | solution.py:186
  7.4 2.0 %collective-permute-start.4 = (f32[24,1152]{1,0:T(8,128)S(1)}, f32[24,1152]{1,0:T(8,128)S(1)}, u32[]{:S(2)}, u32[]{:S(2)}) collective-permute-start(f32[24,1152]{1,0:T(8,128)S(1)} %get-tuple-element.46.refs_12_), channel_id=1, source_target_pairs={{0,2},{2,0},{1,3},{3,1},{4,6},{6,4},{5,7},{7,5},{8,10},{10,8},{9,1... | collective-permute-start | bytes 331784 | tf_op jit(solution)/shard_map/ppermute | solution.py:690
  9.5 1.3 %collective-permute-done.2.refs_1_ = f32[16,1152]{1,0:T(8,128)S(1)} collective-permute-done((f32[16,1152]{1,0:T(8,128)S(1)}, f32[16,1152]{1,0:T(8,128)S(1)}, u32[]{:S(2)}, u32[]{:S(2)}) %collective-permute-start.2) | collective-permute-done | bytes 73760 | tf_op jit(solution)/shard_map/ppermute | solution.py:692
  10.9 1.4 %remap_parts.3.refs_0_ = f32[176,1152]{1,0:T(8,128)S(1)} custom-call(f32[16,8,128]{2,1,0:T(8,128)S(1)} %broadcast_in_dim.4.weight_ref, f32[5,4,16,1152]{3,2,1,0:T(8,128)S(1)} %get-tuple-element.40.refs_0_.refs_2_, f32[5,4,16,1152]{3,2,1,0:T(8,128)S(1)} %collective-permute-done.refs_1_.refs_3_, f32[5,4,16,1152]{3,2,1,0:T(8,128)S(1)} %get-tuple-element.40.refs_0_.refs_2_, ...), custom_call_target="tpu_custom_call" | custom-call | flops 7667712 | bytes 4423680 | tf_op jit(solution)/shard_map/remap_parts/pallas_call | solution.py:520
  12.3 1.3 %collective-permute-start.18 = (f32[176,1152]{1,0:T(8,128)S(1)}, f32[176,1152]{1,0:T(8,128)S(1)}, u32[]{:S(2)}, u32[]{:S(2)}) collective-permute-start(f32[176,1152]{1,0:T(8,128)S(1)} %remap_parts.3.refs_0_), channel_id=1, source_target_pairs={{0,2},{2,0},{1,3},{3,1},{4,6},{6,4},{5,7},{7,5},{8,10},{10,8},{9,1... | collective-permute-start | bytes 2433032 | tf_op jit(solution)/shard_map/ppermute | solution.py:690
  13.6 1.5 %collective-permute-done.4.refs_2_.refs_14_ = f32[24,1152]{1,0:T(8,128)S(1)} collective-permute-done((f32[24,1152]{1,0:T(8,128)S(1)}, f32[24,1152]{1,0:T(8,128)S(1)}, u32[]{:S(2)}, u32[]{:S(2)}) %collective-permute-start.4) | collective-permute-done | bytes 110624 | tf_op jit(solution)/shard_map/ppermute | solution.py:690
  15.1 1.7 %edge_rows.1 = (f32[6,4,1,1152]{3,2,1,0:T(1,128)S(1)}, f32[8,4,1,1152]{3,2,1,0:T(1,128)S(1)}) custom-call(f32[4,16,1152]{2,1,0:T(8,128)} %thick_ref.1, f32[4,16,1152]{2,1,0:T(8,128)} %u_ref.1, f32[4,16,1152]{2,1,0:T(8,128)} %v_ref.1, f32[4,4,16,1152]{3,2,1,0:T(8,128)} %tracer_ref.1, f32[176,1152]{1,0:T(8,128)S(1)} %remap_parts.3.refs_0_, ...), custom_call_target="tpu_custom_call" | custom-call | flops 10000000000 | bytes 1000000000 | tf_op jit(solution)/shard_map/edge_rows/pallas_call | solution.py:668
  16.9 1.3 %collective-permute-start.6 = (f32[8,4,1,1152]{3,2,1,0:T(1,128)S(1)}, f32[8,4,1,1152]{3,2,1,0:T(1,128)S(1)}, u32[]{:S(2)}, u32[]{:S(2)}) collective-permute-start(f32[8,4,1,1152]{3,2,1,0:T(1,128)S(1)} %get-tuple-element.48), channel_id=1, source_target_pairs={{4,0},{8,4},{12,8},{5,1},{9,5},{13,9},{6,2},{10,6},{14,10},{7,3},{... | collective-permute-start | bytes 442376 | tf_op jit(solution)/shard_map/ppermute | solution.py:740
  18.2 4.6 %collective-permute-start.5 = (f32[6,4,1,1152]{3,2,1,0:T(1,128)S(1)}, f32[6,4,1,1152]{3,2,1,0:T(1,128)S(1)}, u32[]{:S(2)}, u32[]{:S(2)}) collective-permute-start(f32[6,4,1,1152]{3,2,1,0:T(1,128)S(1)} %get-tuple-element.47), channel_id=1, source_target_pairs={{0,4},{4,8},{8,12},{1,5},{5,9},{9,13},{2,6},{6,10},{10,14},{3,7},{... | collective-permute-start | bytes 331784 | tf_op jit(solution)/shard_map/ppermute | solution.py:739
  22.7 2.3 %collective-permute-done.5.up_ref = f32[6,4,1,1152]{3,2,1,0:T(1,128)S(1)} collective-permute-done((f32[6,4,1,1152]{3,2,1,0:T(1,128)S(1)}, f32[6,4,1,1152]{3,2,1,0:T(1,128)S(1)}, u32[]{:S(2)}, u32[]{:S(2)}) %collective-permute-start.5) | collective-permute-done | bytes 110624 | tf_op jit(solution)/shard_map/ppermute | solution.py:739
  25.2 3.6 %second_step.1 = (f32[1,4,16,1152]{3,2,1,0:T(8,128)S(1)}, f32[1,4,16,1152]{3,2,1,0:T(8,128)S(1)}, f32[7,4,2,1152]{3,2,1,0:T(2,128)S(1)}) custom-call(f32[4,24,128]{2,1,0:T(8,128)S(1)} %copy-done.6, f32[4,16,1152]{2,1,0:T(8,128)S(1)} %copy-done.1, f32[4,16,1152]{2,1,0:T(8,128)S(1)} %copy-done.2, f32[4,16,1152]{2,1,0:T(8,128)S(1)} %copy-done.3, ...), custom_call_target="tpu_custom_call" | custom-call | flops 503316480 | bytes 3538944 | tf_op jit(solution)/shard_map/second_step/pallas_call | solution.py:324
  29.6 1.3 %remap_parts.4 = (f32[4,4,16,1152]{3,2,1,0:T(8,128)S(1)}, f32[4,16,1152]{2,1,0:T(8,128)S(1)}) custom-call(f32[16,8,128]{2,1,0:T(8,128)S(1)} %broadcast_in_dim.4.weight_ref, f32[5,4,16,1152]{3,2,1,0:T(8,128)S(1)} %get-tuple-element.40.refs_0_.refs_2_, f32[5,4,16,1152]{3,2,1,0:T(8,128)S(1)} %collective-permute-done.refs_1_.refs_3_, ...), custom_call_target="tpu_custom_call" | custom-call | flops 7667712 | bytes 4423680 | tf_op jit(solution)/shard_map/remap_parts/pallas_call | solution.py:520
  31.0 2.0 %collective-permute-done.18.refs_9_.refs_0_ = f32[176,1152]{1,0:T(8,128)S(1)} collective-permute-done((f32[176,1152]{1,0:T(8,128)S(1)}, f32[176,1152]{1,0:T(8,128)S(1)}, u32[]{:S(2)}, u32[]{:S(2)}) %collective-permute-start.18) | collective-permute-done | bytes 811040 | tf_op jit(solution)/shard_map/ppermute | solution.py:690
  33.0 1.8 %remap_parts.5 = (f32[2,4,16,1152]{3,2,1,0:T(8,128)S(1)}, f32[112,1152]{1,0:T(8,128)S(1)}) custom-call(f32[16,8,128]{2,1,0:T(8,128)S(1)} %broadcast_in_dim.4.weight_ref, f32[5,4,16,1152]{3,2,1,0:T(8,128)S(1)} %get-tuple-element.40.refs_0_.refs_2_, f32[5,4,16,1152]{3,2,1,0:T(8,128)S(1)} %collective-permute-done.refs_1_.refs_3_, ...), custom_call_target="tpu_custom_call" | custom-call | flops 10616832 | bytes 3538944 | tf_op jit(solution)/shard_map/remap_parts/pallas_call | solution.py:520
  34.7 1.6 %collective-permute-start.19 = (f32[112,1152]{1,0:T(8,128)S(1)}, f32[112,1152]{1,0:T(8,128)S(1)}, u32[]{:S(2)}, u32[]{:S(2)}) collective-permute-start(f32[112,1152]{1,0:T(8,128)S(1)} %get-tuple-element.55.refs_16_), channel_id=1, source_target_pairs={{0,2},{2,0},{1,3},{3,1},{4,6},{6,4},{5,7},{7,5},{8,10},{10,8},{9,1... | collective-permute-start | bytes 1548296 | tf_op jit(solution)/shard_map/ppermute | solution.py:690
  36.9 1.7 %collective-permute-done.8.refs_2_ = f32[7,4,2,1152]{3,2,1,0:T(2,128)S(1)} collective-permute-done((f32[7,4,2,1152]{3,2,1,0:T(2,128)S(1)}, f32[7,4,2,1152]{3,2,1,0:T(2,128)S(1)}, u32[]{:S(2)}, u32[]{:S(2)}) %collective-permute-start.8) | collective-permute-done | bytes 258080 | tf_op jit(solution)/shard_map/ppermute | solution.py:690
  39.1 1.1 %collective-permute-done.14.refs_13_ = f32[24,1152]{1,0:T(8,128)S(1)} collective-permute-done((f32[24,1152]{1,0:T(8,128)S(1)}, f32[24,1152]{1,0:T(8,128)S(1)}, u32[]{:S(2)}, u32[]{:S(2)}) %collective-permute-start.14) | collective-permute-done | bytes 110624 | tf_op jit(solution)/shard_map/ppermute | solution.py:692
  40.7 0.8 %collective-permute-done.13.refs_11_ = f32[24,1152]{1,0:T(8,128)S(1)} collective-permute-done((f32[24,1152]{1,0:T(8,128)S(1)}, f32[24,1152]{1,0:T(8,128)S(1)}, u32[]{:S(2)}, u32[]{:S(2)}) %collective-permute-start.13) | collective-permute-done | bytes 110624 | tf_op jit(solution)/shard_map/ppermute | solution.py:692
  41.7 3.7 %remap_edges.1 = (f32[6,4,2,1152]{3,2,1,0:T(2,128)S(1)}, f32[4,2,1152]{2,1,0:T(2,128)S(1)}, f32[4,4,3,1152]{3,2,1,0:T(4,128)S(1)}) custom-call(f32[16,8,128]{2,1,0:T(8,128)S(1)} %broadcast_in_dim.4.weight_ref, f32[7,4,2,1152]{3,2,1,0:T(2,128)S(1)} %get-tuple-element.49.refs_6_.refs_0_, f32[7,4,2,1152]{3,2,1,0:T(2,128)S(1)} %collective-permute-done.7.refs_1_, ...), custom_call_target="tpu_custom_call" | custom-call | flops 5898240 | bytes 4128768 | tf_op jit(solution)/shard_map/remap_edges/pallas_call | solution.py:560
  45.4 1.4 %finish_tracers.1 = (f32[4,4,16,1152]{3,2,1,0:T(8,128)}, f32[4,16,1152]{2,1,0:T(8,128)}, f32[8,128]{1,0:T(8,128)S(1)}) custom-call(f32[4,4,16,1152]{3,2,1,0:T(8,128)S(1)} %get-tuple-element.50.refs_8_.own_ref, f32[4,4,3,1152]{3,2,1,0:T(4,128)S(1)} %get-tuple-element.56.near_ref, f32[6,4,2,1152]{3,2,1,0:T(2,128)S(1)} %get-tuple-element.57.edge_ref, ...), custom_call_target="tpu_custom_call" | custom-call | flops 589824 | bytes 3538944 | tf_op jit(solution)/shard_map/finish_tracers/pallas_call | solution.py:598
  46.8 2.3 %collective-permute-done.19.refs_0_ = f32[112,1152]{1,0:T(8,128)S(1)} collective-permute-done((f32[112,1152]{1,0:T(8,128)S(1)}, f32[112,1152]{1,0:T(8,128)S(1)}, u32[]{:S(2)}, u32[]{:S(2)}) %collective-permute-start.19) | collective-permute-done | bytes 516128 | tf_op jit(solution)/shard_map/ppermute | solution.py:690
  49.1 0.9 %finish_winds.1 = (f32[4,16,1152]{2,1,0:T(8,128)}, f32[4,16,1152]{2,1,0:T(8,128)}) custom-call(f32[2,4,16,1152]{3,2,1,0:T(8,128)S(1)} %get-tuple-element.61.own_ref, f32[6,4,2,1152]{3,2,1,0:T(2,128)S(1)} %get-tuple-element.57.edge_ref, f32[112,1152]{1,0:T(8,128)S(1)} %collective-permute-done.19.refs_0_, f32[8,128]{1,0:T(8,128)S(1)} %get-tuple-element.62.refs_1_), custom_call_target="tpu_custom_call" | custom-call | flops 147456 | bytes 1769472 | tf_op jit(solution)/shard_map/finish_winds/pallas_call | solution.py:628
  (48 shorter events, 3.1 us)
Async XLA Ops:
  2.5 6.9 %collective-permute-start.1 = (f32[234,128]{1,0:T(8,128)S(1)}, f32[234,128]{1,0:T(8,128)S(1)}, u32[]{:S(2)}, u32[]{:S(2)}) collective-permute-start(f32[234,128]{1,0:T(8,128)S(1)} %get-tuple-element.41), channel_id=1, source_target_pairs={{0,2},{2,0},{1,3},{3,1},{4,6},{6,4},{5,7},{7,5},{8,10},{10,8},{9,1... | collective-permute-start | bytes 359432 | tf_op jit(solution)/shard_map/ppermute | solution.py:690
  7.2 3.6 %collective-permute-start = (f32[5,4,16,1152]{3,2,1,0:T(8,128)S(1)}, f32[5,4,16,1152]{3,2,1,0:T(8,128)S(1)}, u32[]{:S(2)}, u32[]{:S(2)}) collective-permute-start(f32[5,4,16,1152]{3,2,1,0:T(8,128)S(1)} %get-tuple-element.40.refs_0_.refs_2_), channel_id=1, source_target_pairs={{0,1},{1,0},{2,3},{3,2},{4,5},{5,4},{6,7},{7,6},{8,9},{9,8},{10,11... | collective-permute-start | bytes 4423688 | tf_op jit(solution)/shard_map/ppermute | solution.py:692
  7.3 6.3 %collective-permute-start.3 = (f32[24,1152]{1,0:T(8,128)S(1)}, f32[24,1152]{1,0:T(8,128)S(1)}, u32[]{:S(2)}, u32[]{:S(2)}) collective-permute-start(f32[24,1152]{1,0:T(8,128)S(1)} %get-tuple-element.42.refs_0_.refs_8_), channel_id=1, source_target_pairs={{0,2},{2,0},{1,3},{3,1},{4,6},{6,4},{5,7},{7,5},{8,10},{10,8},{9,1... | collective-permute-start | bytes 331784 | tf_op jit(solution)/shard_map/ppermute | solution.py:690
  7.4 7.7 %collective-permute-start.4 = (f32[24,1152]{1,0:T(8,128)S(1)}, f32[24,1152]{1,0:T(8,128)S(1)}, u32[]{:S(2)}, u32[]{:S(2)}) collective-permute-start(f32[24,1152]{1,0:T(8,128)S(1)} %get-tuple-element.46.refs_12_), channel_id=1, source_target_pairs={{0,2},{2,0},{1,3},{3,1},{4,6},{6,4},{5,7},{7,5},{8,10},{10,8},{9,1... | collective-permute-start | bytes 331784 | tf_op jit(solution)/shard_map/ppermute | solution.py:690
  9.4 1.3 %collective-permute-start.2 = (f32[16,1152]{1,0:T(8,128)S(1)}, f32[16,1152]{1,0:T(8,128)S(1)}, u32[]{:S(2)}, u32[]{:S(2)}) collective-permute-start(f32[16,1152]{1,0:T(8,128)S(1)} %get-tuple-element.43.refs_0_), channel_id=1, source_target_pairs={{0,1},{1,0},{2,3},{3,2},{4,5},{5,4},{6,7},{7,6},{8,9},{9,8},{10,11... | collective-permute-start | bytes 221192 | tf_op jit(solution)/shard_map/ppermute | solution.py:692
  12.3 12.8 %copy-start = (f32[4,4,16,1152]{3,2,1,0:T(8,128)S(1)}, f32[4,4,16,1152]{3,2,1,0:T(8,128)}, u32[]{:S(2)}) copy-start(f32[4,4,16,1152]{3,2,1,0:T(8,128)} %tracer_ref.1) | copy-start | bytes 3538948
  12.3 12.8 %copy-start.1 = (f32[4,16,1152]{2,1,0:T(8,128)S(1)}, f32[4,16,1152]{2,1,0:T(8,128)}, u32[]{:S(2)}) copy-start(f32[4,16,1152]{2,1,0:T(8,128)} %thick_ref.1) | copy-start | bytes 884740
  12.3 12.8 %copy-start.2 = (f32[4,16,1152]{2,1,0:T(8,128)S(1)}, f32[4,16,1152]{2,1,0:T(8,128)}, u32[]{:S(2)}) copy-start(f32[4,16,1152]{2,1,0:T(8,128)} %u_ref.1) | copy-start | bytes 884740
  12.3 12.8 %copy-start.3 = (f32[4,16,1152]{2,1,0:T(8,128)S(1)}, f32[4,16,1152]{2,1,0:T(8,128)}, u32[]{:S(2)}) copy-start(f32[4,16,1152]{2,1,0:T(8,128)} %v_ref.1) | copy-start | bytes 884740
  12.3 20.6 %collective-permute-start.18 = (f32[176,1152]{1,0:T(8,128)S(1)}, f32[176,1152]{1,0:T(8,128)S(1)}, u32[]{:S(2)}, u32[]{:S(2)}) collective-permute-start(f32[176,1152]{1,0:T(8,128)S(1)} %remap_parts.3.refs_0_), channel_id=1, source_target_pairs={{0,2},{2,0},{1,3},{3,1},{4,6},{6,4},{5,7},{7,5},{8,10},{10,8},{9,1... | collective-permute-start | bytes 2433032 | tf_op jit(solution)/shard_map/ppermute | solution.py:690
  16.9 8.2 %collective-permute-start.6 = (f32[8,4,1,1152]{3,2,1,0:T(1,128)S(1)}, f32[8,4,1,1152]{3,2,1,0:T(1,128)S(1)}, u32[]{:S(2)}, u32[]{:S(2)}) collective-permute-start(f32[8,4,1,1152]{3,2,1,0:T(1,128)S(1)} %get-tuple-element.48), channel_id=1, source_target_pairs={{4,0},{8,4},{12,8},{5,1},{9,5},{13,9},{6,2},{10,6},{14,10},{7,3},{... | collective-permute-start | bytes 442376 | tf_op jit(solution)/shard_map/ppermute | solution.py:740
  18.2 6.9 %collective-permute-start.5 = (f32[6,4,1,1152]{3,2,1,0:T(1,128)S(1)}, f32[6,4,1,1152]{3,2,1,0:T(1,128)S(1)}, u32[]{:S(2)}, u32[]{:S(2)}) collective-permute-start(f32[6,4,1,1152]{3,2,1,0:T(1,128)S(1)} %get-tuple-element.47), channel_id=1, source_target_pairs={{0,4},{4,8},{8,12},{1,5},{5,9},{9,13},{2,6},{6,10},{10,14},{3,7},{... | collective-permute-start | bytes 331784 | tf_op jit(solution)/shard_map/ppermute | solution.py:739
  28.8 2.2 %collective-permute-start.16 = (f32[1,4,16,1152]{3,2,1,0:T(8,128)S(1)}, f32[1,4,16,1152]{3,2,1,0:T(8,128)S(1)}, u32[]{:S(2)}, u32[]{:S(2)}) collective-permute-start(f32[1,4,16,1152]{3,2,1,0:T(8,128)S(1)} %get-tuple-element.53.refs_2_), channel_id=1, source_target_pairs={{0,1},{1,0},{2,3},{3,2},{4,5},{5,4},{6,7},{7,6},{8,9},{9,8},{10,11... | collective-permute-start | bytes 884744 | tf_op jit(solution)/shard_map/ppermute | solution.py:692
  28.9 2.1 %collective-permute-start.17 = (f32[1,4,16,1152]{3,2,1,0:T(8,128)S(1)}, f32[1,4,16,1152]{3,2,1,0:T(8,128)S(1)}, u32[]{:S(2)}, u32[]{:S(2)}) collective-permute-start(f32[1,4,16,1152]{3,2,1,0:T(8,128)S(1)} %get-tuple-element.54.refs_4_), channel_id=1, source_target_pairs={{0,1},{1,0},{2,3},{3,2},{4,5},{5,4},{6,7},{7,6},{8,9},{9,8},{10,11... | collective-permute-start | bytes 884744 | tf_op jit(solution)/shard_map/ppermute | solution.py:692
  29.4 9.2 %collective-permute-start.8 = (f32[7,4,2,1152]{3,2,1,0:T(2,128)S(1)}, f32[7,4,2,1152]{3,2,1,0:T(2,128)S(1)}, u32[]{:S(2)}, u32[]{:S(2)}) collective-permute-start(f32[7,4,2,1152]{3,2,1,0:T(2,128)S(1)} %get-tuple-element.49.refs_6_.refs_0_), channel_id=1, source_target_pairs={{0,2},{2,0},{1,3},{3,1},{4,6},{6,4},{5,7},{7,5},{8,10},{10,8},{9,1... | collective-permute-start | bytes 774152 | tf_op jit(solution)/shard_map/ppermute | solution.py:690
  34.7 14.4 %collective-permute-start.19 = (f32[112,1152]{1,0:T(8,128)S(1)}, f32[112,1152]{1,0:T(8,128)S(1)}, u32[]{:S(2)}, u32[]{:S(2)}) collective-permute-start(f32[112,1152]{1,0:T(8,128)S(1)} %get-tuple-element.55.refs_16_), channel_id=1, source_target_pairs={{0,2},{2,0},{1,3},{3,1},{4,6},{6,4},{5,7},{7,5},{8,10},{10,8},{9,1... | collective-permute-start | bytes 1548296 | tf_op jit(solution)/shard_map/ppermute | solution.py:690
  36.3 2.2 %collective-permute-start.10 = (f32[1,4,3,1152]{3,2,1,0:T(4,128)S(1)}, f32[1,4,3,1152]{3,2,1,0:T(4,128)S(1)}, u32[]{:S(2)}, u32[]{:S(2)}) collective-permute-start(f32[1,4,3,1152]{3,2,1,0:T(4,128)S(1)} %get-tuple-element.51.refs_4_), channel_id=1, source_target_pairs={{0,1},{1,0},{2,3},{3,2},{4,5},{5,4},{6,7},{7,6},{8,9},{9,8},{10,11... | collective-permute-start | bytes 165896 | tf_op jit(solution)/shard_map/ppermute | solution.py:692
  36.4 2.7 %collective-permute-start.12 = (f32[24,1152]{1,0:T(8,128)S(1)}, f32[24,1152]{1,0:T(8,128)S(1)}, u32[]{:S(2)}, u32[]{:S(2)}) collective-permute-start(f32[24,1152]{1,0:T(8,128)S(1)} %get-tuple-element.42.refs_0_.refs_8_), channel_id=1, source_target_pairs={{0,1},{1,0},{2,3},{3,2},{4,5},{5,4},{6,7},{7,6},{8,9},{9,8},{10,11... | collective-permute-start | bytes 331784 | tf_op jit(solution)/shard_map/ppermute | solution.py:692
  36.9 4.8 %collective-permute-start.7 = (f32[7,4,2,1152]{3,2,1,0:T(2,128)S(1)}, f32[7,4,2,1152]{3,2,1,0:T(2,128)S(1)}, u32[]{:S(2)}, u32[]{:S(2)}) collective-permute-start(f32[7,4,2,1152]{3,2,1,0:T(2,128)S(1)} %get-tuple-element.49.refs_6_.refs_0_), channel_id=1, source_target_pairs={{0,1},{1,0},{2,3},{3,2},{4,5},{5,4},{6,7},{7,6},{8,9},{9,8},{10,11... | collective-permute-start | bytes 774152 | tf_op jit(solution)/shard_map/ppermute | solution.py:692
  38.5 3.2 %collective-permute-start.9 = (f32[7,4,2,1152]{3,2,1,0:T(2,128)S(1)}, f32[7,4,2,1152]{3,2,1,0:T(2,128)S(1)}, u32[]{:S(2)}, u32[]{:S(2)}) collective-permute-start(f32[7,4,2,1152]{3,2,1,0:T(2,128)S(1)} %collective-permute-done.8.refs_2_), channel_id=1, source_target_pairs={{0,1},{1,0},{2,3},{3,2},{4,5},{5,4},{6,7},{7,6},{8,9},{9,8},{10,11... | collective-permute-start | bytes 774152 | tf_op jit(solution)/shard_map/ppermute | solution.py:692
  38.5 1.7 %collective-permute-start.14 = (f32[24,1152]{1,0:T(8,128)S(1)}, f32[24,1152]{1,0:T(8,128)S(1)}, u32[]{:S(2)}, u32[]{:S(2)}) collective-permute-start(f32[24,1152]{1,0:T(8,128)S(1)} %get-tuple-element.46.refs_12_), channel_id=1, source_target_pairs={{0,1},{1,0},{2,3},{3,2},{4,5},{5,4},{6,7},{7,6},{8,9},{9,8},{10,11... | collective-permute-start | bytes 331784 | tf_op jit(solution)/shard_map/ppermute | solution.py:692
  39.0 1.3 %collective-permute-start.11 = (f32[1,4,3,1152]{3,2,1,0:T(4,128)S(1)}, f32[1,4,3,1152]{3,2,1,0:T(4,128)S(1)}, u32[]{:S(2)}, u32[]{:S(2)}) collective-permute-start(f32[1,4,3,1152]{3,2,1,0:T(4,128)S(1)} %get-tuple-element.52.refs_6_), channel_id=1, source_target_pairs={{0,1},{1,0},{2,3},{3,2},{4,5},{5,4},{6,7},{7,6},{8,9},{9,8},{10,11... | collective-permute-start | bytes 165896 | tf_op jit(solution)/shard_map/ppermute | solution.py:692
  40.2 1.3 %collective-permute-start.13 = (f32[24,1152]{1,0:T(8,128)S(1)}, f32[24,1152]{1,0:T(8,128)S(1)}, u32[]{:S(2)}, u32[]{:S(2)}) collective-permute-start(f32[24,1152]{1,0:T(8,128)S(1)} %collective-permute-done.3.refs_1_.refs_10_), channel_id=1, source_target_pairs={{0,1},{1,0},{2,3},{3,2},{4,5},{5,4},{6,7},{7,6},{8,9},{9,8},{10,11... | collective-permute-start | bytes 331784 | tf_op jit(solution)/shard_map/ppermute | solution.py:692
  40.4 1.3 %collective-permute-start.15 = (f32[24,1152]{1,0:T(8,128)S(1)}, f32[24,1152]{1,0:T(8,128)S(1)}, u32[]{:S(2)}, u32[]{:S(2)}) collective-permute-start(f32[24,1152]{1,0:T(8,128)S(1)} %collective-permute-done.4.refs_2_.refs_14_), channel_id=1, source_target_pairs={{0,1},{1,0},{2,3},{3,2},{4,5},{5,4},{6,7},{7,6},{8,9},{9,8},{10,11... | collective-permute-start | bytes 331784 | tf_op jit(solution)/shard_map/ppermute | solution.py:692
  (5 other events, 46.7 us)

commit v17 on v16

--- a/solution.py
+++ b/solution.py
@@ -152,7 +152,7 @@
     )(*operands)
 
 
-def inner_kernel(table_ref, new_ref, thick_ref, u_ref, v_ref, tracer_ref, out_ref, near_ref, near_rest_ref):
+def inner_kernel(table_ref, new_ref, thick_ref, u_ref, v_ref, tracer_ref, out_ref, near_ref):
     T, L, rows, _ = tracer_ref.shape
     near, _ = near_rows(rows)
     geo = table_ref[lax.axis_index("lat")]
@@ -170,9 +170,8 @@
             )
             value = change * scale
             out_ref[1 + c, k] = value
-            ref, at = (near_ref, c) if c < T // 2 else (near_rest_ref, c - T // 2)
             for j, row in enumerate(near):
-                ref[pl.ds((at * L + k) * len(near) + j, 1)] = value[row : row + 1]
+                near_ref[pl.ds((c * L + k) * len(near) + j, 1)] = value[row : row + 1]
         return carry
 
     lax.fori_loop(0, L, level, 0)
@@ -181,13 +180,13 @@
 def inner_step(table, new, thickness, wind_u, wind_v, tracers):
     L, R, N = thickness.shape
     T = tracers.shape[0]
-    rows = lambda n: jax.ShapeDtypeStruct((n * L * len(near_rows(R)[0]), N), jnp.float32)
+    rows = jax.ShapeDtypeStruct((T * L * len(near_rows(R)[0]), N), jnp.float32)
     shape = lambda n, rows: jax.ShapeDtypeStruct((n, L, rows, N), jnp.float32)
     return pl.pallas_call(
         inner_kernel,
         in_specs=[VMEM] * 6,
-        out_specs=[VMEM] * 3,
-        out_shape=[shape(1 + T, R), rows(T // 2), rows(T - T // 2)],
+        out_specs=[VMEM] * 2,
+        out_shape=[shape(1 + T, R), rows],
         compiler_params=params(),
         cost_estimate=cost(130 * L * R * N, 4 * L * R * N * (8 + 2 * T)),
         name="inner_step",
@@ -529,11 +528,10 @@
     )(weights, *thick, *flat, *others, *wait)
 
 
-def remap_edge_kernel(counts, near_fields, weight_ref, *refs):
+def remap_edge_kernel(counts, weight_ref, *refs):
     *refs, sum_ref = refs
     G = counts[0] * counts[1]
-    edge_refs, near_refs = refs[:G], refs[G : 2 * G]
-    bundles = (refs[2 * G : 3 * G], refs[3 * G : 4 * G])
+    edge_refs, near_refs, tracer_refs = refs[:G], refs[G : 2 * G], refs[2 * G : 3 * G]
     edge_out_ref, thick_out_ref, near_out_ref = refs[-3:]
 
     def store_edge(s, i, at, columns, target, means):
@@ -548,17 +546,16 @@
     fields = [[level_of(ref, f) for ref in edge_refs] for f in range(1, edge_refs[0].shape[0])]
     remap_rows(weight_ref, sum_ref, counts, (0,), edge_refs, fields, [], store_edge)
     _, L, R, _ = near_refs[0].shape
-    fields = [[packed_level_of(ref, index, L, R) for ref in bundles[which]] for which, index in near_fields]
+    fields = [[packed_level_of(ref, f, L, R) for ref in tracer_refs] for f in range(near_out_ref.shape[0])]
     remap_rows(weight_ref, sum_ref, counts, (0,), near_refs, fields, [], store_near)
 
 
-def remap_edges(counts, weights, edges, near_new, near, near_rest, wait=()):
+def remap_edges(counts, weights, edges, near_new, near, wait=()):
     F, L, R, N = edges[0].shape
     T = F - 3
-    near_fields = tuple((0, f) if f < T // 2 else (1, f - T // 2) for f in range(T))
-    operands = [*edges, *near_new, *near, *near_rest]
-    return pl.pallas_call(
-        functools.partial(remap_edge_kernel, counts, near_fields),
+    operands = [*edges, *near_new, *near]
+    return pl.pallas_call(
+        functools.partial(remap_edge_kernel, counts),
         in_specs=[VMEM] * (1 + len(operands)) + after(wait),
         out_specs=[VMEM] * 3,
         out_shape=[
@@ -722,10 +719,9 @@
 
     new, both, near_new, *arguments = first_step(table, thickness, wind_u, wind_v, tracers)
     both = [send(both, s=s, t=0) for s in away]
-    inner, near, near_rest = inner_step(table, new, *arguments)
+    inner, near = inner_step(table, new, *arguments)
     group = with_others_of_chip(inner)
     near = [near] + [send(near, s=s, t=0) for s in away]
-    near_rest = [near_rest] + [send(near_rest, s=s, t=0) for s in away]
     parted = [part(each, (L, R, N), [near[0]]) for each in both]
     near_new = [near_new] + [each[1] for each in parted]
     others = other_chips((C, S), [a for each in parted for a in with_others_of_chip(each[0])])
@@ -734,7 +730,7 @@
     arrived = sent(away_parts)
 
     last, leading = edge_rows(
-        thickness, wind_u, wind_v, tracers, [away_parts[0], *near[1:2], *near_rest[1:2]]
+        thickness, wind_u, wind_v, tracers, [away_parts[0], *near[1:2]]
     )
     up = lax.ppermute(last, "lat", northward)
     down = lax.ppermute(leading, "lat", southward)
@@ -746,11 +742,11 @@
         group, winds, others, [(0, 0), (1, 0)], range(C), (1, 1), wait=[tracers_own, *arrived[:1]]
     )
     winds_arrived = sent(winds_away)
-    near_new, near, near_rest, edges = (
-        [a for own in sources for a in with_others_of_chip(own)] for sources in (near_new, near, near_rest, edges)
+    near_new, near, edges = (
+        [a for own in sources for a in with_others_of_chip(own)] for sources in (near_new, near, edges)
     )
     edge_out, thick_edge, near_out = remap_edges(
-        (C, S), weights, edges, near_new, near, near_rest, wait=winds_away[:1]
+        (C, S), weights, edges, near_new, near, wait=winds_away[:1]
     )
 
     tracers_out, thickness_out, token = finish_tracers(

time: 50.3 us -> 50.2 us (level)
  starting transfers between devices: 16.4 us -> 14.1 us
  waiting for transfers between devices: 13.2 us -> 15.4 us
    ppermute x6 -> x5, waiting for transfers between devices: 7.51 us -> 9.86 us  [shifted(): lax.ppermute(value, 'lev', [(i, (i + s) % lev_count) for i in range(lev_c...]
    ppermute x6 -> x5, starting transfers between devices: 8.22 us -> 6.45 us  [shifted(): lax.ppermute(value, 'lev', [(i, (i + s) % lev_count) for i in range(lev_c...]
    ppermute x12 -> x10, starting transfers between devices: 2.31 us -> 1.8 us  [shifted(): lax.ppermute(value, 'sub', [(i, (i + t) % sub_count) for i in range(sub_c...]
    ppermute x12 -> x10, waiting for transfers between devices: 3.34 us -> 3.25 us  [shifted(): lax.ppermute(value, 'sub', [(i, (i + t) % sub_count) for i in range(sub_c...]
  transfers between devices with their start and end apart: 20 -> 17, of which waited for: 9 -> 9; matrix products, arithmetic and copies ran while one was open for 0% -> 0% of each run, Pallas kernels for 33% -> 33%
where the time goes in v17:
time: 50.2 us; the launch traced here: 50 us
  Pallas kernels  19.4 us (39%)
  waiting for transfers between devices  15.4 us (31%)
  starting transfers between devices  14.1 us (28%)
  between operations  0.88 us (2%)
    ppermute x5, waiting for transfers between devices, shifted(): lax.ppermute(value, 'lev', [(i, (i + s) % lev_count) for i in range(lev_c...  9.86 us
    ppermute x5, starting transfers between devices, shifted(): lax.ppermute(value, 'lev', [(i, (i + s) % lev_count) for i in range(lev_c...  6.45 us
    ppermute x1, starting transfers between devices, per_device(): up = lax.ppermute(last, 'lat', northward)  4.55 us
    pallas_call x3, Pallas kernels, remap_parts(): pl.pallas_call(functools.partial(remap_kernel, counts, tuple(steps), tupl...  4.45 us
    pallas_call x1, Pallas kernels, remap_edges(): pl.pallas_call(functools.partial(remap_edge_kernel, counts), in_specs=[VM...  3.7 us
    pallas_call x1, Pallas kernels, second_step(): pl.pallas_call(functools.partial(second_kernel, lat_rows), grid=(L,), in_...  3.62 us
    ppermute x10, waiting for transfers between devices, shifted(): lax.ppermute(value, 'sub', [(i, (i + t) % sub_count) for i in range(sub_c...  3.25 us
    ppermute x1, waiting for transfers between devices, per_device(): up = lax.ppermute(last, 'lat', northward)  2.3 us
  transfers between devices with their start and end apart: 17, of which 9 were waited for; matrix products, arithmetic and copies ran while one was open for 0% of the time, Pallas kernels for 33%

profile of v17, /device:TPU:0, one launch (start us, length us, event | category | flops | bytes accessed | tf_op | source)
XLA Modules:
  0.0 50.0 jit_solution(2450638575055160135)
XLA Ops:
  0.6 1.9 %first_step.1 = (f32[4,16,1152]{2,1,0:T(8,128)S(1)}, f32[234,128]{1,0:T(8,128)S(1)}, f32[1,4,3,1152]{3,2,1,0:T(4,128)S(1)}, f32[4,16,1152]{2,1,0:T(8,128)S(1)}, ...) custom-call(f32[4,24,128]{2,1,0:T(8,128)} %constant.6.clone.table_hbm.table_ref, ...), custom_call_target="tpu_custom_call" | custom-call | flops 2949120 | bytes 4423680 | tf_op jit(solution)/shard_map/first_step/pallas_call | solution.py:139
  2.5 3.0 %collective-permute-start.1 = (f32[234,128]{1,0:T(8,128)S(1)}, f32[234,128]{1,0:T(8,128)S(1)}, u32[]{:S(2)}, u32[]{:S(2)}) collective-permute-start(f32[234,128]{1,0:T(8,128)S(1)} %get-tuple-element.40), channel_id=1, source_target_pairs={{0,2},{2,0},{1,3},{3,1},{4,6},{6,4},{5,7},{7,5},{8,10},{10,8},{9,1... | collective-permute-start | bytes 359432 | tf_op jit(solution)/shard_map/ppermute | solution.py:687
  5.5 1.6 %inner_step.1 = (f32[5,4,16,1152]{3,2,1,0:T(8,128)S(1)}, f32[48,1152]{1,0:T(8,128)S(1)}) custom-call(f32[4,24,128]{2,1,0:T(8,128)S(1)} %copy-done.6, f32[4,16,1152]{2,1,0:T(8,128)S(1)} %get-tuple-element.34.new_ref, f32[4,16,1152]{2,1,0:T(8,128)S(1)} %get-tuple-element.35.thick_ref, f32[4,16,1152]{2,1,0:T(8,128)S(1)} %get-tuple-element.36.u_ref, ...), custom_call_target="tpu_custom_call" | custom-call | flops 9584640 | bytes 4718592 | tf_op jit(solution)/shard_map/inner_step/pallas_call | solution.py:185
  7.4 1.5 %collective-permute-done.1.both_ref = f32[234,128]{1,0:T(8,128)S(1)} collective-permute-done((f32[234,128]{1,0:T(8,128)S(1)}, f32[234,128]{1,0:T(8,128)S(1)}, u32[]{:S(2)}, u32[]{:S(2)}) %collective-permute-start.1) | collective-permute-done | bytes 119840 | tf_op jit(solution)/shard_map/ppermute | solution.py:687
  9.0 1.7 %collective-permute-done.2.refs_1_ = f32[16,1152]{1,0:T(8,128)S(1)} collective-permute-done((f32[16,1152]{1,0:T(8,128)S(1)}, f32[16,1152]{1,0:T(8,128)S(1)}, u32[]{:S(2)}, u32[]{:S(2)}) %collective-permute-start.2) | collective-permute-done | bytes 73760 | tf_op jit(solution)/shard_map/ppermute | solution.py:689
  10.7 1.4 %remap_parts.3.refs_0_ = f32[176,1152]{1,0:T(8,128)S(1)} custom-call(f32[16,8,128]{2,1,0:T(8,128)S(1)} %broadcast_in_dim.4.weight_ref, f32[5,4,16,1152]{3,2,1,0:T(8,128)S(1)} %get-tuple-element.39.refs_0_.refs_2_, f32[5,4,16,1152]{3,2,1,0:T(8,128)S(1)} %collective-permute-done.refs_1_.refs_3_, f32[5,4,16,1152]{3,2,1,0:T(8,128)S(1)} %get-tuple-element.39.refs_0_.refs_2_, ...), custom_call_target="tpu_custom_call" | custom-call | flops 7667712 | bytes 4423680 | tf_op jit(solution)/shard_map/remap_parts/pallas_call | solution.py:519
  12.2 1.4 %collective-permute-start.15 = (f32[176,1152]{1,0:T(8,128)S(1)}, f32[176,1152]{1,0:T(8,128)S(1)}, u32[]{:S(2)}, u32[]{:S(2)}) collective-permute-start(f32[176,1152]{1,0:T(8,128)S(1)} %remap_parts.3.refs_0_), channel_id=1, source_target_pairs={{0,2},{2,0},{1,3},{3,1},{4,6},{6,4},{5,7},{7,5},{8,10},{10,8},{9,1... | collective-permute-start | bytes 2433032 | tf_op jit(solution)/shard_map/ppermute | solution.py:687
  13.6 1.5 %collective-permute-done.3.refs_1_.refs_10_ = f32[48,1152]{1,0:T(8,128)S(1)} collective-permute-done((f32[48,1152]{1,0:T(8,128)S(1)}, f32[48,1152]{1,0:T(8,128)S(1)}, u32[]{:S(2)}, u32[]{:S(2)}) %collective-permute-start.3) | collective-permute-done | bytes 221216 | tf_op jit(solution)/shard_map/ppermute | solution.py:687
  15.1 1.7 %edge_rows.1 = (f32[6,4,1,1152]{3,2,1,0:T(1,128)S(1)}, f32[8,4,1,1152]{3,2,1,0:T(1,128)S(1)}) custom-call(f32[4,16,1152]{2,1,0:T(8,128)} %thick_ref.1, f32[4,16,1152]{2,1,0:T(8,128)} %u_ref.1, f32[4,16,1152]{2,1,0:T(8,128)} %v_ref.1, f32[4,4,16,1152]{3,2,1,0:T(8,128)} %tracer_ref.1, f32[176,1152]{1,0:T(8,128)S(1)} %remap_parts.3.refs_0_, ...), custom_call_target="tpu_custom_call" | custom-call | flops 10000000000 | bytes 1000000000 | tf_op jit(solution)/shard_map/edge_rows/pallas_call | solution.py:665
  16.9 1.3 %collective-permute-start.5 = (f32[8,4,1,1152]{3,2,1,0:T(1,128)S(1)}, f32[8,4,1,1152]{3,2,1,0:T(1,128)S(1)}, u32[]{:S(2)}, u32[]{:S(2)}) collective-permute-start(f32[8,4,1,1152]{3,2,1,0:T(1,128)S(1)} %get-tuple-element.46), channel_id=1, source_target_pairs={{4,0},{8,4},{12,8},{5,1},{9,5},{13,9},{6,2},{10,6},{14,10},{7,3},{... | collective-permute-start | bytes 442376 | tf_op jit(solution)/shard_map/ppermute | solution.py:736
  18.2 4.6 %collective-permute-start.4 = (f32[6,4,1,1152]{3,2,1,0:T(1,128)S(1)}, f32[6,4,1,1152]{3,2,1,0:T(1,128)S(1)}, u32[]{:S(2)}, u32[]{:S(2)}) collective-permute-start(f32[6,4,1,1152]{3,2,1,0:T(1,128)S(1)} %get-tuple-element.45), channel_id=1, source_target_pairs={{0,4},{4,8},{8,12},{1,5},{5,9},{9,13},{2,6},{6,10},{10,14},{3,7},{... | collective-permute-start | bytes 331784 | tf_op jit(solution)/shard_map/ppermute | solution.py:735
  22.7 2.3 %collective-permute-done.4.up_ref = f32[6,4,1,1152]{3,2,1,0:T(1,128)S(1)} collective-permute-done((f32[6,4,1,1152]{3,2,1,0:T(1,128)S(1)}, f32[6,4,1,1152]{3,2,1,0:T(1,128)S(1)}, u32[]{:S(2)}, u32[]{:S(2)}) %collective-permute-start.4) | collective-permute-done | bytes 110624 | tf_op jit(solution)/shard_map/ppermute | solution.py:735
  25.1 3.6 %second_step.1 = (f32[1,4,16,1152]{3,2,1,0:T(8,128)S(1)}, f32[1,4,16,1152]{3,2,1,0:T(8,128)S(1)}, f32[7,4,2,1152]{3,2,1,0:T(2,128)S(1)}) custom-call(f32[4,24,128]{2,1,0:T(8,128)S(1)} %copy-done.6, f32[4,16,1152]{2,1,0:T(8,128)S(1)} %copy-done.1, f32[4,16,1152]{2,1,0:T(8,128)S(1)} %copy-done.2, f32[4,16,1152]{2,1,0:T(8,128)S(1)} %copy-done.3, ...), custom_call_target="tpu_custom_call" | custom-call | flops 503316480 | bytes 3538944 | tf_op jit(solution)/shard_map/second_step/pallas_call | solution.py:323
  29.6 1.3 %remap_parts.4 = (f32[4,4,16,1152]{3,2,1,0:T(8,128)S(1)}, f32[4,16,1152]{2,1,0:T(8,128)S(1)}) custom-call(f32[16,8,128]{2,1,0:T(8,128)S(1)} %broadcast_in_dim.4.weight_ref, f32[5,4,16,1152]{3,2,1,0:T(8,128)S(1)} %get-tuple-element.39.refs_0_.refs_2_, f32[5,4,16,1152]{3,2,1,0:T(8,128)S(1)} %collective-permute-done.refs_1_.refs_3_, ...), custom_call_target="tpu_custom_call" | custom-call | flops 7667712 | bytes 4423680 | tf_op jit(solution)/shard_map/remap_parts/pallas_call | solution.py:519
  30.9 2.0 %collective-permute-done.15.refs_9_.refs_0_ = f32[176,1152]{1,0:T(8,128)S(1)} collective-permute-done((f32[176,1152]{1,0:T(8,128)S(1)}, f32[176,1152]{1,0:T(8,128)S(1)}, u32[]{:S(2)}, u32[]{:S(2)}) %collective-permute-start.15) | collective-permute-done | bytes 811040 | tf_op jit(solution)/shard_map/ppermute | solution.py:687
  32.9 1.8 %remap_parts.5 = (f32[2,4,16,1152]{3,2,1,0:T(8,128)S(1)}, f32[112,1152]{1,0:T(8,128)S(1)}) custom-call(f32[16,8,128]{2,1,0:T(8,128)S(1)} %broadcast_in_dim.4.weight_ref, f32[5,4,16,1152]{3,2,1,0:T(8,128)S(1)} %get-tuple-element.39.refs_0_.refs_2_, f32[5,4,16,1152]{3,2,1,0:T(8,128)S(1)} %collective-permute-done.refs_1_.refs_3_, ...), custom_call_target="tpu_custom_call" | custom-call | flops 10616832 | bytes 3538944 | tf_op jit(solution)/shard_map/remap_parts/pallas_call | solution.py:519
  34.6 1.7 %collective-permute-start.16 = (f32[112,1152]{1,0:T(8,128)S(1)}, f32[112,1152]{1,0:T(8,128)S(1)}, u32[]{:S(2)}, u32[]{:S(2)}) collective-permute-start(f32[112,1152]{1,0:T(8,128)S(1)} %get-tuple-element.53.refs_12_), channel_id=1, source_target_pairs={{0,2},{2,0},{1,3},{3,1},{4,6},{6,4},{5,7},{7,5},{8,10},{10,8},{9,1... | collective-permute-start | bytes 1548296 | tf_op jit(solution)/shard_map/ppermute | solution.py:687
  36.9 1.6 %collective-permute-done.7.refs_2_ = f32[7,4,2,1152]{3,2,1,0:T(2,128)S(1)} collective-permute-done((f32[7,4,2,1152]{3,2,1,0:T(2,128)S(1)}, f32[7,4,2,1152]{3,2,1,0:T(2,128)S(1)}, u32[]{:S(2)}, u32[]{:S(2)}) %collective-permute-start.7) | collective-permute-done | bytes 258080 | tf_op jit(solution)/shard_map/ppermute | solution.py:687
  38.4 0.5 %collective-permute-start.11 = (f32[48,1152]{1,0:T(8,128)S(1)}, f32[48,1152]{1,0:T(8,128)S(1)}, u32[]{:S(2)}, u32[]{:S(2)}) collective-permute-start(f32[48,1152]{1,0:T(8,128)S(1)} %get-tuple-element.41.refs_0_.refs_8_), channel_id=1, source_target_pairs={{0,1},{1,0},{2,3},{3,2},{4,5},{5,4},{6,7},{7,6},{8,9},{9,8},{10,11... | collective-permute-start | bytes 663560 | tf_op jit(solution)/shard_map/ppermute | solution.py:689
  39.0 1.3 %collective-permute-done.11.refs_9_ = f32[48,1152]{1,0:T(8,128)S(1)} collective-permute-done((f32[48,1152]{1,0:T(8,128)S(1)}, f32[48,1152]{1,0:T(8,128)S(1)}, u32[]{:S(2)}, u32[]{:S(2)}) %collective-permute-start.11) | collective-permute-done | bytes 221216 | tf_op jit(solution)/shard_map/ppermute | solution.py:689
  40.6 3.7 %remap_edges.1 = (f32[6,4,2,1152]{3,2,1,0:T(2,128)S(1)}, f32[4,2,1152]{2,1,0:T(2,128)S(1)}, f32[4,4,3,1152]{3,2,1,0:T(4,128)S(1)}) custom-call(f32[16,8,128]{2,1,0:T(8,128)S(1)} %broadcast_in_dim.4.weight_ref, f32[7,4,2,1152]{3,2,1,0:T(2,128)S(1)} %get-tuple-element.47.refs_6_.refs_0_, f32[7,4,2,1152]{3,2,1,0:T(2,128)S(1)} %collective-permute-done.6.refs_1_, ...), custom_call_target="tpu_custom_call" | custom-call | flops 5898240 | bytes 3096576 | tf_op jit(solution)/shard_map/remap_edges/pallas_call | solution.py:557
  44.3 1.4 %finish_tracers.1 = (f32[4,4,16,1152]{3,2,1,0:T(8,128)}, f32[4,16,1152]{2,1,0:T(8,128)}, f32[8,128]{1,0:T(8,128)S(1)}) custom-call(f32[4,4,16,1152]{3,2,1,0:T(8,128)S(1)} %get-tuple-element.48.refs_8_.own_ref, f32[4,4,3,1152]{3,2,1,0:T(4,128)S(1)} %get-tuple-element.54.near_ref, f32[6,4,2,1152]{3,2,1,0:T(2,128)S(1)} %get-tuple-element.55.edge_ref, ...), custom_call_target="tpu_custom_call" | custom-call | flops 589824 | bytes 3538944 | tf_op jit(solution)/shard_map/finish_tracers/pallas_call | solution.py:595
  45.7 3.3 %collective-permute-done.16.refs_0_ = f32[112,1152]{1,0:T(8,128)S(1)} collective-permute-done((f32[112,1152]{1,0:T(8,128)S(1)}, f32[112,1152]{1,0:T(8,128)S(1)}, u32[]{:S(2)}, u32[]{:S(2)}) %collective-permute-start.16) | collective-permute-done | bytes 516128 | tf_op jit(solution)/shard_map/ppermute | solution.py:687
  49.1 0.9 %finish_winds.1 = (f32[4,16,1152]{2,1,0:T(8,128)}, f32[4,16,1152]{2,1,0:T(8,128)}) custom-call(f32[2,4,16,1152]{3,2,1,0:T(8,128)S(1)} %get-tuple-element.59.own_ref, f32[6,4,2,1152]{3,2,1,0:T(2,128)S(1)} %get-tuple-element.55.edge_ref, f32[112,1152]{1,0:T(8,128)S(1)} %collective-permute-done.16.refs_0_, f32[8,128]{1,0:T(8,128)S(1)} %get-tuple-element.60.refs_1_), custom_call_target="tpu_custom_call" | custom-call | flops 147456 | bytes 1769472 | tf_op jit(solution)/shard_map/finish_winds/pallas_call | solution.py:625
  (42 shorter events, 2.2 us)
Async XLA Ops:
  2.5 6.3 %collective-permute-start.1 = (f32[234,128]{1,0:T(8,128)S(1)}, f32[234,128]{1,0:T(8,128)S(1)}, u32[]{:S(2)}, u32[]{:S(2)}) collective-permute-start(f32[234,128]{1,0:T(8,128)S(1)} %get-tuple-element.40), channel_id=1, source_target_pairs={{0,2},{2,0},{1,3},{3,1},{4,6},{6,4},{5,7},{7,5},{8,10},{10,8},{9,1... | collective-permute-start | bytes 359432 | tf_op jit(solution)/shard_map/ppermute | solution.py:687
  7.2 3.5 %collective-permute-start = (f32[5,4,16,1152]{3,2,1,0:T(8,128)S(1)}, f32[5,4,16,1152]{3,2,1,0:T(8,128)S(1)}, u32[]{:S(2)}, u32[]{:S(2)}) collective-permute-start(f32[5,4,16,1152]{3,2,1,0:T(8,128)S(1)} %get-tuple-element.39.refs_0_.refs_2_), channel_id=1, source_target_pairs={{0,1},{1,0},{2,3},{3,2},{4,5},{5,4},{6,7},{7,6},{8,9},{9,8},{10,11... | collective-permute-start | bytes 4423688 | tf_op jit(solution)/shard_map/ppermute | solution.py:689
  7.3 7.9 %collective-permute-start.3 = (f32[48,1152]{1,0:T(8,128)S(1)}, f32[48,1152]{1,0:T(8,128)S(1)}, u32[]{:S(2)}, u32[]{:S(2)}) collective-permute-start(f32[48,1152]{1,0:T(8,128)S(1)} %get-tuple-element.41.refs_0_.refs_8_), channel_id=1, source_target_pairs={{0,2},{2,0},{1,3},{3,1},{4,6},{6,4},{5,7},{7,5},{8,10},{10,8},{9,1... | collective-permute-start | bytes 663560 | tf_op jit(solution)/shard_map/ppermute | solution.py:687
  8.9 1.7 %collective-permute-start.2 = (f32[16,1152]{1,0:T(8,128)S(1)}, f32[16,1152]{1,0:T(8,128)S(1)}, u32[]{:S(2)}, u32[]{:S(2)}) collective-permute-start(f32[16,1152]{1,0:T(8,128)S(1)} %get-tuple-element.42.refs_0_), channel_id=1, source_target_pairs={{0,1},{1,0},{2,3},{3,2},{4,5},{5,4},{6,7},{7,6},{8,9},{9,8},{10,11... | collective-permute-start | bytes 221192 | tf_op jit(solution)/shard_map/ppermute | solution.py:689
  12.1 12.9 %copy-start.8 = (s32[16]{0:T(128)S(1)}, s32[16]{0:T(128)}, u32[]{:S(2)}) copy-start(s32[16]{0:T(128)} %param.14) | copy-start | bytes 196
  12.1 13.0 %copy-start = (f32[4,4,16,1152]{3,2,1,0:T(8,128)S(1)}, f32[4,4,16,1152]{3,2,1,0:T(8,128)}, u32[]{:S(2)}) copy-start(f32[4,4,16,1152]{3,2,1,0:T(8,128)} %tracer_ref.1) | copy-start | bytes 3538948
  12.1 13.0 %copy-start.1 = (f32[4,16,1152]{2,1,0:T(8,128)S(1)}, f32[4,16,1152]{2,1,0:T(8,128)}, u32[]{:S(2)}) copy-start(f32[4,16,1152]{2,1,0:T(8,128)} %thick_ref.1) | copy-start | bytes 884740
  12.2 12.9 %copy-start.2 = (f32[4,16,1152]{2,1,0:T(8,128)S(1)}, f32[4,16,1152]{2,1,0:T(8,128)}, u32[]{:S(2)}) copy-start(f32[4,16,1152]{2,1,0:T(8,128)} %u_ref.1) | copy-start | bytes 884740
  12.2 12.9 %copy-start.3 = (f32[4,16,1152]{2,1,0:T(8,128)S(1)}, f32[4,16,1152]{2,1,0:T(8,128)}, u32[]{:S(2)}) copy-start(f32[4,16,1152]{2,1,0:T(8,128)} %v_ref.1) | copy-start | bytes 884740
  12.2 12.9 %copy-start.4 = (bf16[5,256,256]{2,1,0:T(8,128)(2,1)S(1)}, bf16[5,256,256]{2,1,0:T(8,128)(2,1)}, u32[]{:S(2)}) copy-start(bf16[5,256,256]{2,1,0:T(8,128)(2,1)} %constant.7.clone.high_ref) | copy-start | bytes 1966084
  12.2 12.9 %copy-start.5 = (bf16[5,256,256]{2,1,0:T(8,128)(2,1)S(1)}, bf16[5,256,256]{2,1,0:T(8,128)(2,1)}, u32[]{:S(2)}) copy-start(bf16[5,256,256]{2,1,0:T(8,128)(2,1)} %constant.8.clone.low_ref) | copy-start | bytes 1966084
  12.2 20.7 %collective-permute-start.15 = (f32[176,1152]{1,0:T(8,128)S(1)}, f32[176,1152]{1,0:T(8,128)S(1)}, u32[]{:S(2)}, u32[]{:S(2)}) collective-permute-start(f32[176,1152]{1,0:T(8,128)S(1)} %remap_parts.3.refs_0_), channel_id=1, source_target_pairs={{0,2},{2,0},{1,3},{3,1},{4,6},{6,4},{5,7},{7,5},{8,10},{10,8},{9,1... | collective-permute-start | bytes 2433032 | tf_op jit(solution)/shard_map/ppermute | solution.py:687
  16.9 8.2 %collective-permute-start.5 = (f32[8,4,1,1152]{3,2,1,0:T(1,128)S(1)}, f32[8,4,1,1152]{3,2,1,0:T(1,128)S(1)}, u32[]{:S(2)}, u32[]{:S(2)}) collective-permute-start(f32[8,4,1,1152]{3,2,1,0:T(1,128)S(1)} %get-tuple-element.46), channel_id=1, source_target_pairs={{4,0},{8,4},{12,8},{5,1},{9,5},{13,9},{6,2},{10,6},{14,10},{7,3},{... | collective-permute-start | bytes 442376 | tf_op jit(solution)/shard_map/ppermute | solution.py:736
  18.2 6.9 %collective-permute-start.4 = (f32[6,4,1,1152]{3,2,1,0:T(1,128)S(1)}, f32[6,4,1,1152]{3,2,1,0:T(1,128)S(1)}, u32[]{:S(2)}, u32[]{:S(2)}) collective-permute-start(f32[6,4,1,1152]{3,2,1,0:T(1,128)S(1)} %get-tuple-element.45), channel_id=1, source_target_pairs={{0,4},{4,8},{8,12},{1,5},{5,9},{9,13},{2,6},{6,10},{10,14},{3,7},{... | collective-permute-start | bytes 331784 | tf_op jit(solution)/shard_map/ppermute | solution.py:735
  28.8 2.1 %collective-permute-start.13 = (f32[1,4,16,1152]{3,2,1,0:T(8,128)S(1)}, f32[1,4,16,1152]{3,2,1,0:T(8,128)S(1)}, u32[]{:S(2)}, u32[]{:S(2)}) collective-permute-start(f32[1,4,16,1152]{3,2,1,0:T(8,128)S(1)} %get-tuple-element.51.refs_2_), channel_id=1, source_target_pairs={{0,1},{1,0},{2,3},{3,2},{4,5},{5,4},{6,7},{7,6},{8,9},{9,8},{10,11... | collective-permute-start | bytes 884744 | tf_op jit(solution)/shard_map/ppermute | solution.py:689
  28.8 2.1 %collective-permute-start.14 = (f32[1,4,16,1152]{3,2,1,0:T(8,128)S(1)}, f32[1,4,16,1152]{3,2,1,0:T(8,128)S(1)}, u32[]{:S(2)}, u32[]{:S(2)}) collective-permute-start(f32[1,4,16,1152]{3,2,1,0:T(8,128)S(1)} %get-tuple-element.52.refs_4_), channel_id=1, source_target_pairs={{0,1},{1,0},{2,3},{3,2},{4,5},{5,4},{6,7},{7,6},{8,9},{9,8},{10,11... | collective-permute-start | bytes 884744 | tf_op jit(solution)/shard_map/ppermute | solution.py:689
  29.3 9.1 %collective-permute-start.7 = (f32[7,4,2,1152]{3,2,1,0:T(2,128)S(1)}, f32[7,4,2,1152]{3,2,1,0:T(2,128)S(1)}, u32[]{:S(2)}, u32[]{:S(2)}) collective-permute-start(f32[7,4,2,1152]{3,2,1,0:T(2,128)S(1)} %get-tuple-element.47.refs_6_.refs_0_), channel_id=1, source_target_pairs={{0,2},{2,0},{1,3},{3,1},{4,6},{6,4},{5,7},{7,5},{8,10},{10,8},{9,1... | collective-permute-start | bytes 774152 | tf_op jit(solution)/shard_map/ppermute | solution.py:687
  34.6 14.4 %collective-permute-start.16 = (f32[112,1152]{1,0:T(8,128)S(1)}, f32[112,1152]{1,0:T(8,128)S(1)}, u32[]{:S(2)}, u32[]{:S(2)}) collective-permute-start(f32[112,1152]{1,0:T(8,128)S(1)} %get-tuple-element.53.refs_12_), channel_id=1, source_target_pairs={{0,2},{2,0},{1,3},{3,1},{4,6},{6,4},{5,7},{7,5},{8,10},{10,8},{9,1... | collective-permute-start | bytes 1548296 | tf_op jit(solution)/shard_map/ppermute | solution.py:687
  36.3 2.1 %collective-permute-start.9 = (f32[1,4,3,1152]{3,2,1,0:T(4,128)S(1)}, f32[1,4,3,1152]{3,2,1,0:T(4,128)S(1)}, u32[]{:S(2)}, u32[]{:S(2)}) collective-permute-start(f32[1,4,3,1152]{3,2,1,0:T(4,128)S(1)} %get-tuple-element.49.refs_4_), channel_id=1, source_target_pairs={{0,1},{1,0},{2,3},{3,2},{4,5},{5,4},{6,7},{7,6},{8,9},{9,8},{10,11... | collective-permute-start | bytes 165896 | tf_op jit(solution)/shard_map/ppermute | solution.py:689
  36.4 2.6 %collective-permute-start.10 = (f32[1,4,3,1152]{3,2,1,0:T(4,128)S(1)}, f32[1,4,3,1152]{3,2,1,0:T(4,128)S(1)}, u32[]{:S(2)}, u32[]{:S(2)}) collective-permute-start(f32[1,4,3,1152]{3,2,1,0:T(4,128)S(1)} %get-tuple-element.50.refs_6_), channel_id=1, source_target_pairs={{0,1},{1,0},{2,3},{3,2},{4,5},{5,4},{6,7},{7,6},{8,9},{9,8},{10,11... | collective-permute-start | bytes 165896 | tf_op jit(solution)/shard_map/ppermute | solution.py:689
  36.9 3.7 %collective-permute-start.6 = (f32[7,4,2,1152]{3,2,1,0:T(2,128)S(1)}, f32[7,4,2,1152]{3,2,1,0:T(2,128)S(1)}, u32[]{:S(2)}, u32[]{:S(2)}) collective-permute-start(f32[7,4,2,1152]{3,2,1,0:T(2,128)S(1)} %get-tuple-element.47.refs_6_.refs_0_), channel_id=1, source_target_pairs={{0,1},{1,0},{2,3},{3,2},{4,5},{5,4},{6,7},{7,6},{8,9},{9,8},{10,11... | collective-permute-start | bytes 774152 | tf_op jit(solution)/shard_map/ppermute | solution.py:689
  38.4 2.2 %collective-permute-start.8 = (f32[7,4,2,1152]{3,2,1,0:T(2,128)S(1)}, f32[7,4,2,1152]{3,2,1,0:T(2,128)S(1)}, u32[]{:S(2)}, u32[]{:S(2)}) collective-permute-start(f32[7,4,2,1152]{3,2,1,0:T(2,128)S(1)} %collective-permute-done.7.refs_2_), channel_id=1, source_target_pairs={{0,1},{1,0},{2,3},{3,2},{4,5},{5,4},{6,7},{7,6},{8,9},{9,8},{10,11... | collective-permute-start | bytes 774152 | tf_op jit(solution)/shard_map/ppermute | solution.py:689
  38.4 1.8 %collective-permute-start.11 = (f32[48,1152]{1,0:T(8,128)S(1)}, f32[48,1152]{1,0:T(8,128)S(1)}, u32[]{:S(2)}, u32[]{:S(2)}) collective-permute-start(f32[48,1152]{1,0:T(8,128)S(1)} %get-tuple-element.41.refs_0_.refs_8_), channel_id=1, source_target_pairs={{0,1},{1,0},{2,3},{3,2},{4,5},{5,4},{6,7},{7,6},{8,9},{9,8},{10,11... | collective-permute-start | bytes 663560 | tf_op jit(solution)/shard_map/ppermute | solution.py:689
  38.9 1.6 %collective-permute-start.12 = (f32[48,1152]{1,0:T(8,128)S(1)}, f32[48,1152]{1,0:T(8,128)S(1)}, u32[]{:S(2)}, u32[]{:S(2)}) collective-permute-start(f32[48,1152]{1,0:T(8,128)S(1)} %collective-permute-done.3.refs_1_.refs_10_), channel_id=1, source_target_pairs={{0,1},{1,0},{2,3},{3,2},{4,5},{5,4},{6,7},{7,6},{8,9},{9,8},{10,11... | collective-permute-start | bytes 663560 | tf_op jit(solution)/shard_map/ppermute | solution.py:689
  (2 other events, 8.3 us)

commit v18 on v17

--- a/solution.py
+++ b/solution.py
@@ -93,25 +93,18 @@
     new_ref, both_ref, near_ref, thick_ref, u_ref, v_ref, tracer_ref, sum_ref, geo_ref, sems = refs
     L, rows, _ = thick_ref.shape
     near, _ = near_rows(rows)
-    table_copy = pltpu.make_async_copy(table_hbm.at[lax.axis_index("lat")], geo_ref, sems.at[3, 0])
-    table_copy.start()
-    pairs = ((thick_hbm, thick_ref), (u_hbm, u_ref), (v_hbm, v_ref))
-
-    def copies(k):
-        return [pltpu.make_async_copy(a.at[k], b.at[k], sems.at[i, k]) for i, (a, b) in enumerate(pairs)]
-
-    for k in range(L):
-        for copy in copies(k):
-            copy.start()
-    tracer_copy = pltpu.make_async_copy(tracer_hbm, tracer_ref, sems.at[3, 1])
+    pairs = ((thick_hbm, thick_ref), (u_hbm, u_ref), (v_hbm, v_ref), (table_hbm.at[lax.axis_index("lat")], geo_ref))
+    copies = [pltpu.make_async_copy(a, b, sems.at[i]) for i, (a, b) in enumerate(pairs)]
+    for copy in copies:
+        copy.start()
+    tracer_copy = pltpu.make_async_copy(tracer_hbm, tracer_ref, sems.at[len(copies)])
     tracer_copy.start()
-    table_copy.wait()
+    for copy in copies:
+        copy.wait()
     geo = geo_ref[...]
     sum_ref[...] = jnp.zeros_like(sum_ref)
 
     def level(k, carry):
-        for copy in copies(k):
-            copy.wait()
         thick, u, v = thick_ref[k], u_ref[k], v_ref[k]
         east, north, _ = fluxes(geo, thick, u, v, None, None, None)
         new = thick - (east - west_of(east)) - (north - south_of(north, None)) * geo[0:rows, 2:3]
@@ -144,7 +137,7 @@
         scratch_shapes=[
             pltpu.VMEM((R, N), jnp.float32),
             pltpu.VMEM(table.shape[1:], jnp.float32),
-            pltpu.SemaphoreType.DMA((4, max(L, 2))),
+            pltpu.SemaphoreType.DMA((5,)),
         ],
         compiler_params=params(),
         cost_estimate=cost(40 * L * R * N, 4 * L * R * N * (7 + 2 * tracers.shape[0])),

time: 50.2 us -> 50.3 us (level)
  no operation moved by 1% of the time
where the time goes in v18:
time: 50.3 us; the launch traced here: 50.1 us
  Pallas kernels  19.5 us (39%)
  waiting for transfers between devices  15.4 us (31%)
  starting transfers between devices  14.1 us (28%)
  between operations  0.88 us (2%)
    ppermute x5, waiting for transfers between devices, shifted(): lax.ppermute(value, 'lev', [(i, (i + s) % lev_count) for i in range(lev_c...  9.87 us
    ppermute x5, starting transfers between devices, shifted(): lax.ppermute(value, 'lev', [(i, (i + s) % lev_count) for i in range(lev_c...  6.44 us
    ppermute x1, starting transfers between devices, per_device(): up = lax.ppermute(last, 'lat', northward)  4.55 us
    pallas_call x3, Pallas kernels, remap_parts(): pl.pallas_call(functools.partial(remap_kernel, counts, tuple(steps), tupl...  4.45 us
    pallas_call x1, Pallas kernels, remap_edges(): pl.pallas_call(functools.partial(remap_edge_kernel, counts), in_specs=[VM...  3.7 us
    pallas_call x1, Pallas kernels, second_step(): pl.pallas_call(functools.partial(second_kernel, lat_rows), grid=(L,), in_...  3.62 us
    ppermute x10, waiting for transfers between devices, shifted(): lax.ppermute(value, 'sub', [(i, (i + t) % sub_count) for i in range(sub_c...  3.25 us
    ppermute x1, waiting for transfers between devices, per_device(): up = lax.ppermute(last, 'lat', northward)  2.3 us
  transfers between devices with their start and end apart: 17, of which 9 were waited for; matrix products, arithmetic and copies ran while one was open for 0% of the time, Pallas kernels for 33%

profile of v18, /device:TPU:0, one launch (start us, length us, event | category | flops | bytes accessed | tf_op | source)
XLA Modules:
  0.0 50.1 jit_solution(11849219870018814362)
XLA Ops:
  0.6 2.0 %first_step.1 = (f32[4,16,1152]{2,1,0:T(8,128)S(1)}, f32[234,128]{1,0:T(8,128)S(1)}, f32[1,4,3,1152]{3,2,1,0:T(4,128)S(1)}, f32[4,16,1152]{2,1,0:T(8,128)S(1)}, ...) custom-call(f32[4,24,128]{2,1,0:T(8,128)} %constant.6.clone.table_hbm.table_ref, ...), custom_call_target="tpu_custom_call" | custom-call | flops 2949120 | bytes 4423680 | tf_op jit(solution)/shard_map/first_step/pallas_call | solution.py:132
  2.6 3.0 %collective-permute-start.1 = (f32[234,128]{1,0:T(8,128)S(1)}, f32[234,128]{1,0:T(8,128)S(1)}, u32[]{:S(2)}, u32[]{:S(2)}) collective-permute-start(f32[234,128]{1,0:T(8,128)S(1)} %get-tuple-element.40), channel_id=1, source_target_pairs={{0,2},{2,0},{1,3},{3,1},{4,6},{6,4},{5,7},{7,5},{8,10},{10,8},{9,1... | collective-permute-start | bytes 359432 | tf_op jit(solution)/shard_map/ppermute | solution.py:680
  5.6 1.6 %inner_step.1 = (f32[5,4,16,1152]{3,2,1,0:T(8,128)S(1)}, f32[48,1152]{1,0:T(8,128)S(1)}) custom-call(f32[4,24,128]{2,1,0:T(8,128)S(1)} %copy-done.6, f32[4,16,1152]{2,1,0:T(8,128)S(1)} %get-tuple-element.34.new_ref, f32[4,16,1152]{2,1,0:T(8,128)S(1)} %get-tuple-element.35.thick_ref, f32[4,16,1152]{2,1,0:T(8,128)S(1)} %get-tuple-element.36.u_ref, ...), custom_call_target="tpu_custom_call" | custom-call | flops 9584640 | bytes 4718592 | tf_op jit(solution)/shard_map/inner_step/pallas_call | solution.py:178
  7.5 1.5 %collective-permute-done.1.both_ref = f32[234,128]{1,0:T(8,128)S(1)} collective-permute-done((f32[234,128]{1,0:T(8,128)S(1)}, f32[234,128]{1,0:T(8,128)S(1)}, u32[]{:S(2)}, u32[]{:S(2)}) %collective-permute-start.1) | collective-permute-done | bytes 119840 | tf_op jit(solution)/shard_map/ppermute | solution.py:680
  9.1 1.7 %collective-permute-done.2.refs_1_ = f32[16,1152]{1,0:T(8,128)S(1)} collective-permute-done((f32[16,1152]{1,0:T(8,128)S(1)}, f32[16,1152]{1,0:T(8,128)S(1)}, u32[]{:S(2)}, u32[]{:S(2)}) %collective-permute-start.2) | collective-permute-done | bytes 73760 | tf_op jit(solution)/shard_map/ppermute | solution.py:682
  10.8 1.4 %remap_parts.3.refs_0_ = f32[176,1152]{1,0:T(8,128)S(1)} custom-call(f32[16,8,128]{2,1,0:T(8,128)S(1)} %broadcast_in_dim.4.weight_ref, f32[5,4,16,1152]{3,2,1,0:T(8,128)S(1)} %get-tuple-element.39.refs_0_.refs_2_, f32[5,4,16,1152]{3,2,1,0:T(8,128)S(1)} %collective-permute-done.refs_1_.refs_3_, f32[5,4,16,1152]{3,2,1,0:T(8,128)S(1)} %get-tuple-element.39.refs_0_.refs_2_, ...), custom_call_target="tpu_custom_call" | custom-call | flops 7667712 | bytes 4423680 | tf_op jit(solution)/shard_map/remap_parts/pallas_call | solution.py:512
  12.3 1.4 %collective-permute-start.15 = (f32[176,1152]{1,0:T(8,128)S(1)}, f32[176,1152]{1,0:T(8,128)S(1)}, u32[]{:S(2)}, u32[]{:S(2)}) collective-permute-start(f32[176,1152]{1,0:T(8,128)S(1)} %remap_parts.3.refs_0_), channel_id=1, source_target_pairs={{0,2},{2,0},{1,3},{3,1},{4,6},{6,4},{5,7},{7,5},{8,10},{10,8},{9,1... | collective-permute-start | bytes 2433032 | tf_op jit(solution)/shard_map/ppermute | solution.py:680
  13.7 1.5 %collective-permute-done.3.refs_1_.refs_10_ = f32[48,1152]{1,0:T(8,128)S(1)} collective-permute-done((f32[48,1152]{1,0:T(8,128)S(1)}, f32[48,1152]{1,0:T(8,128)S(1)}, u32[]{:S(2)}, u32[]{:S(2)}) %collective-permute-start.3) | collective-permute-done | bytes 221216 | tf_op jit(solution)/shard_map/ppermute | solution.py:680
  15.2 1.7 %edge_rows.1 = (f32[6,4,1,1152]{3,2,1,0:T(1,128)S(1)}, f32[8,4,1,1152]{3,2,1,0:T(1,128)S(1)}) custom-call(f32[4,16,1152]{2,1,0:T(8,128)} %thick_ref.1, f32[4,16,1152]{2,1,0:T(8,128)} %u_ref.1, f32[4,16,1152]{2,1,0:T(8,128)} %v_ref.1, f32[4,4,16,1152]{3,2,1,0:T(8,128)} %tracer_ref.1, f32[176,1152]{1,0:T(8,128)S(1)} %remap_parts.3.refs_0_, ...), custom_call_target="tpu_custom_call" | custom-call | flops 10000000000 | bytes 1000000000 | tf_op jit(solution)/shard_map/edge_rows/pallas_call | solution.py:658
  17.0 1.3 %collective-permute-start.5 = (f32[8,4,1,1152]{3,2,1,0:T(1,128)S(1)}, f32[8,4,1,1152]{3,2,1,0:T(1,128)S(1)}, u32[]{:S(2)}, u32[]{:S(2)}) collective-permute-start(f32[8,4,1,1152]{3,2,1,0:T(1,128)S(1)} %get-tuple-element.46), channel_id=1, source_target_pairs={{4,0},{8,4},{12,8},{5,1},{9,5},{13,9},{6,2},{10,6},{14,10},{7,3},{... | collective-permute-start | bytes 442376 | tf_op jit(solution)/shard_map/ppermute | solution.py:729
  18.3 4.6 %collective-permute-start.4 = (f32[6,4,1,1152]{3,2,1,0:T(1,128)S(1)}, f32[6,4,1,1152]{3,2,1,0:T(1,128)S(1)}, u32[]{:S(2)}, u32[]{:S(2)}) collective-permute-start(f32[6,4,1,1152]{3,2,1,0:T(1,128)S(1)} %get-tuple-element.45), channel_id=1, source_target_pairs={{0,4},{4,8},{8,12},{1,5},{5,9},{9,13},{2,6},{6,10},{10,14},{3,7},{... | collective-permute-start | bytes 331784 | tf_op jit(solution)/shard_map/ppermute | solution.py:728
  22.8 2.3 %collective-permute-done.4.up_ref = f32[6,4,1,1152]{3,2,1,0:T(1,128)S(1)} collective-permute-done((f32[6,4,1,1152]{3,2,1,0:T(1,128)S(1)}, f32[6,4,1,1152]{3,2,1,0:T(1,128)S(1)}, u32[]{:S(2)}, u32[]{:S(2)}) %collective-permute-start.4) | collective-permute-done | bytes 110624 | tf_op jit(solution)/shard_map/ppermute | solution.py:728
  25.3 3.6 %second_step.1 = (f32[1,4,16,1152]{3,2,1,0:T(8,128)S(1)}, f32[1,4,16,1152]{3,2,1,0:T(8,128)S(1)}, f32[7,4,2,1152]{3,2,1,0:T(2,128)S(1)}) custom-call(f32[4,24,128]{2,1,0:T(8,128)S(1)} %copy-done.6, f32[4,16,1152]{2,1,0:T(8,128)S(1)} %copy-done.1, f32[4,16,1152]{2,1,0:T(8,128)S(1)} %copy-done.2, f32[4,16,1152]{2,1,0:T(8,128)S(1)} %copy-done.3, ...), custom_call_target="tpu_custom_call" | custom-call | flops 503316480 | bytes 3538944 | tf_op jit(solution)/shard_map/second_step/pallas_call | solution.py:316
  29.7 1.3 %remap_parts.4 = (f32[4,4,16,1152]{3,2,1,0:T(8,128)S(1)}, f32[4,16,1152]{2,1,0:T(8,128)S(1)}) custom-call(f32[16,8,128]{2,1,0:T(8,128)S(1)} %broadcast_in_dim.4.weight_ref, f32[5,4,16,1152]{3,2,1,0:T(8,128)S(1)} %get-tuple-element.39.refs_0_.refs_2_, f32[5,4,16,1152]{3,2,1,0:T(8,128)S(1)} %collective-permute-done.refs_1_.refs_3_, ...), custom_call_target="tpu_custom_call" | custom-call | flops 7667712 | bytes 4423680 | tf_op jit(solution)/shard_map/remap_parts/pallas_call | solution.py:512
  31.0 2.0 %collective-permute-done.15.refs_9_.refs_0_ = f32[176,1152]{1,0:T(8,128)S(1)} collective-permute-done((f32[176,1152]{1,0:T(8,128)S(1)}, f32[176,1152]{1,0:T(8,128)S(1)}, u32[]{:S(2)}, u32[]{:S(2)}) %collective-permute-start.15) | collective-permute-done | bytes 811040 | tf_op jit(solution)/shard_map/ppermute | solution.py:680
  33.0 1.8 %remap_parts.5 = (f32[2,4,16,1152]{3,2,1,0:T(8,128)S(1)}, f32[112,1152]{1,0:T(8,128)S(1)}) custom-call(f32[16,8,128]{2,1,0:T(8,128)S(1)} %broadcast_in_dim.4.weight_ref, f32[5,4,16,1152]{3,2,1,0:T(8,128)S(1)} %get-tuple-element.39.refs_0_.refs_2_, f32[5,4,16,1152]{3,2,1,0:T(8,128)S(1)} %collective-permute-done.refs_1_.refs_3_, ...), custom_call_target="tpu_custom_call" | custom-call | flops 10616832 | bytes 3538944 | tf_op jit(solution)/shard_map/remap_parts/pallas_call | solution.py:512
  34.8 1.7 %collective-permute-start.16 = (f32[112,1152]{1,0:T(8,128)S(1)}, f32[112,1152]{1,0:T(8,128)S(1)}, u32[]{:S(2)}, u32[]{:S(2)}) collective-permute-start(f32[112,1152]{1,0:T(8,128)S(1)} %get-tuple-element.53.refs_12_), channel_id=1, source_target_pairs={{0,2},{2,0},{1,3},{3,1},{4,6},{6,4},{5,7},{7,5},{8,10},{10,8},{9,1... | collective-permute-start | bytes 1548296 | tf_op jit(solution)/shard_map/ppermute | solution.py:680
  37.0 1.6 %collective-permute-done.7.refs_2_ = f32[7,4,2,1152]{3,2,1,0:T(2,128)S(1)} collective-permute-done((f32[7,4,2,1152]{3,2,1,0:T(2,128)S(1)}, f32[7,4,2,1152]{3,2,1,0:T(2,128)S(1)}, u32[]{:S(2)}, u32[]{:S(2)}) %collective-permute-start.7) | collective-permute-done | bytes 258080 | tf_op jit(solution)/shard_map/ppermute | solution.py:680
  38.5 0.5 %collective-permute-start.11 = (f32[48,1152]{1,0:T(8,128)S(1)}, f32[48,1152]{1,0:T(8,128)S(1)}, u32[]{:S(2)}, u32[]{:S(2)}) collective-permute-start(f32[48,1152]{1,0:T(8,128)S(1)} %get-tuple-element.41.refs_0_.refs_8_), channel_id=1, source_target_pairs={{0,1},{1,0},{2,3},{3,2},{4,5},{5,4},{6,7},{7,6},{8,9},{9,8},{10,11... | collective-permute-start | bytes 663560 | tf_op jit(solution)/shard_map/ppermute | solution.py:682
  39.1 1.3 %collective-permute-done.11.refs_9_ = f32[48,1152]{1,0:T(8,128)S(1)} collective-permute-done((f32[48,1152]{1,0:T(8,128)S(1)}, f32[48,1152]{1,0:T(8,128)S(1)}, u32[]{:S(2)}, u32[]{:S(2)}) %collective-permute-start.11) | collective-permute-done | bytes 221216 | tf_op jit(solution)/shard_map/ppermute | solution.py:682
  40.7 3.7 %remap_edges.1 = (f32[6,4,2,1152]{3,2,1,0:T(2,128)S(1)}, f32[4,2,1152]{2,1,0:T(2,128)S(1)}, f32[4,4,3,1152]{3,2,1,0:T(4,128)S(1)}) custom-call(f32[16,8,128]{2,1,0:T(8,128)S(1)} %broadcast_in_dim.4.weight_ref, f32[7,4,2,1152]{3,2,1,0:T(2,128)S(1)} %get-tuple-element.47.refs_6_.refs_0_, f32[7,4,2,1152]{3,2,1,0:T(2,128)S(1)} %collective-permute-done.6.refs_1_, ...), custom_call_target="tpu_custom_call" | custom-call | flops 5898240 | bytes 3096576 | tf_op jit(solution)/shard_map/remap_edges/pallas_call | solution.py:550
  44.4 1.4 %finish_tracers.1 = (f32[4,4,16,1152]{3,2,1,0:T(8,128)}, f32[4,16,1152]{2,1,0:T(8,128)}, f32[8,128]{1,0:T(8,128)S(1)}) custom-call(f32[4,4,16,1152]{3,2,1,0:T(8,128)S(1)} %get-tuple-element.48.refs_8_.own_ref, f32[4,4,3,1152]{3,2,1,0:T(4,128)S(1)} %get-tuple-element.54.near_ref, f32[6,4,2,1152]{3,2,1,0:T(2,128)S(1)} %get-tuple-element.55.edge_ref, ...), custom_call_target="tpu_custom_call" | custom-call | flops 589824 | bytes 3538944 | tf_op jit(solution)/shard_map/finish_tracers/pallas_call | solution.py:588
  45.8 3.3 %collective-permute-done.16.refs_0_ = f32[112,1152]{1,0:T(8,128)S(1)} collective-permute-done((f32[112,1152]{1,0:T(8,128)S(1)}, f32[112,1152]{1,0:T(8,128)S(1)}, u32[]{:S(2)}, u32[]{:S(2)}) %collective-permute-start.16) | collective-permute-done | bytes 516128 | tf_op jit(solution)/shard_map/ppermute | solution.py:680
  49.2 0.9 %finish_winds.1 = (f32[4,16,1152]{2,1,0:T(8,128)}, f32[4,16,1152]{2,1,0:T(8,128)}) custom-call(f32[2,4,16,1152]{3,2,1,0:T(8,128)S(1)} %get-tuple-element.59.own_ref, f32[6,4,2,1152]{3,2,1,0:T(2,128)S(1)} %get-tuple-element.55.edge_ref, f32[112,1152]{1,0:T(8,128)S(1)} %collective-permute-done.16.refs_0_, f32[8,128]{1,0:T(8,128)S(1)} %get-tuple-element.60.refs_1_), custom_call_target="tpu_custom_call" | custom-call | flops 147456 | bytes 1769472 | tf_op jit(solution)/shard_map/finish_winds/pallas_call | solution.py:618
  (42 shorter events, 2.2 us)
Async XLA Ops:
  2.6 6.3 %collective-permute-start.1 = (f32[234,128]{1,0:T(8,128)S(1)}, f32[234,128]{1,0:T(8,128)S(1)}, u32[]{:S(2)}, u32[]{:S(2)}) collective-permute-start(f32[234,128]{1,0:T(8,128)S(1)} %get-tuple-element.40), channel_id=1, source_target_pairs={{0,2},{2,0},{1,3},{3,1},{4,6},{6,4},{5,7},{7,5},{8,10},{10,8},{9,1... | collective-permute-start | bytes 359432 | tf_op jit(solution)/shard_map/ppermute | solution.py:680
  7.3 3.5 %collective-permute-start = (f32[5,4,16,1152]{3,2,1,0:T(8,128)S(1)}, f32[5,4,16,1152]{3,2,1,0:T(8,128)S(1)}, u32[]{:S(2)}, u32[]{:S(2)}) collective-permute-start(f32[5,4,16,1152]{3,2,1,0:T(8,128)S(1)} %get-tuple-element.39.refs_0_.refs_2_), channel_id=1, source_target_pairs={{0,1},{1,0},{2,3},{3,2},{4,5},{5,4},{6,7},{7,6},{8,9},{9,8},{10,11... | collective-permute-start | bytes 4423688 | tf_op jit(solution)/shard_map/ppermute | solution.py:682
  7.4 7.9 %collective-permute-start.3 = (f32[48,1152]{1,0:T(8,128)S(1)}, f32[48,1152]{1,0:T(8,128)S(1)}, u32[]{:S(2)}, u32[]{:S(2)}) collective-permute-start(f32[48,1152]{1,0:T(8,128)S(1)} %get-tuple-element.41.refs_0_.refs_8_), channel_id=1, source_target_pairs={{0,2},{2,0},{1,3},{3,1},{4,6},{6,4},{5,7},{7,5},{8,10},{10,8},{9,1... | collective-permute-start | bytes 663560 | tf_op jit(solution)/shard_map/ppermute | solution.py:680
  9.0 1.7 %collective-permute-start.2 = (f32[16,1152]{1,0:T(8,128)S(1)}, f32[16,1152]{1,0:T(8,128)S(1)}, u32[]{:S(2)}, u32[]{:S(2)}) collective-permute-start(f32[16,1152]{1,0:T(8,128)S(1)} %get-tuple-element.42.refs_0_), channel_id=1, source_target_pairs={{0,1},{1,0},{2,3},{3,2},{4,5},{5,4},{6,7},{7,6},{8,9},{9,8},{10,11... | collective-permute-start | bytes 221192 | tf_op jit(solution)/shard_map/ppermute | solution.py:682
  12.2 12.9 %copy-start.8 = (s32[16]{0:T(128)S(1)}, s32[16]{0:T(128)}, u32[]{:S(2)}) copy-start(s32[16]{0:T(128)} %param.14) | copy-start | bytes 196
  12.3 13.0 %copy-start = (f32[4,4,16,1152]{3,2,1,0:T(8,128)S(1)}, f32[4,4,16,1152]{3,2,1,0:T(8,128)}, u32[]{:S(2)}) copy-start(f32[4,4,16,1152]{3,2,1,0:T(8,128)} %tracer_ref.1) | copy-start | bytes 3538948
  12.3 13.0 %copy-start.1 = (f32[4,16,1152]{2,1,0:T(8,128)S(1)}, f32[4,16,1152]{2,1,0:T(8,128)}, u32[]{:S(2)}) copy-start(f32[4,16,1152]{2,1,0:T(8,128)} %thick_ref.1) | copy-start | bytes 884740
  12.3 12.9 %copy-start.2 = (f32[4,16,1152]{2,1,0:T(8,128)S(1)}, f32[4,16,1152]{2,1,0:T(8,128)}, u32[]{:S(2)}) copy-start(f32[4,16,1152]{2,1,0:T(8,128)} %u_ref.1) | copy-start | bytes 884740
  12.3 12.9 %copy-start.3 = (f32[4,16,1152]{2,1,0:T(8,128)S(1)}, f32[4,16,1152]{2,1,0:T(8,128)}, u32[]{:S(2)}) copy-start(f32[4,16,1152]{2,1,0:T(8,128)} %v_ref.1) | copy-start | bytes 884740
  12.3 12.9 %copy-start.4 = (bf16[5,256,256]{2,1,0:T(8,128)(2,1)S(1)}, bf16[5,256,256]{2,1,0:T(8,128)(2,1)}, u32[]{:S(2)}) copy-start(bf16[5,256,256]{2,1,0:T(8,128)(2,1)} %constant.7.clone.high_ref) | copy-start | bytes 1966084
  12.3 12.9 %copy-start.5 = (bf16[5,256,256]{2,1,0:T(8,128)(2,1)S(1)}, bf16[5,256,256]{2,1,0:T(8,128)(2,1)}, u32[]{:S(2)}) copy-start(bf16[5,256,256]{2,1,0:T(8,128)(2,1)} %constant.8.clone.low_ref) | copy-start | bytes 1966084
  12.3 20.7 %collective-permute-start.15 = (f32[176,1152]{1,0:T(8,128)S(1)}, f32[176,1152]{1,0:T(8,128)S(1)}, u32[]{:S(2)}, u32[]{:S(2)}) collective-permute-start(f32[176,1152]{1,0:T(8,128)S(1)} %remap_parts.3.refs_0_), channel_id=1, source_target_pairs={{0,2},{2,0},{1,3},{3,1},{4,6},{6,4},{5,7},{7,5},{8,10},{10,8},{9,1... | collective-permute-start | bytes 2433032 | tf_op jit(solution)/shard_map/ppermute | solution.py:680
  17.0 8.2 %collective-permute-start.5 = (f32[8,4,1,1152]{3,2,1,0:T(1,128)S(1)}, f32[8,4,1,1152]{3,2,1,0:T(1,128)S(1)}, u32[]{:S(2)}, u32[]{:S(2)}) collective-permute-start(f32[8,4,1,1152]{3,2,1,0:T(1,128)S(1)} %get-tuple-element.46), channel_id=1, source_target_pairs={{4,0},{8,4},{12,8},{5,1},{9,5},{13,9},{6,2},{10,6},{14,10},{7,3},{... | collective-permute-start | bytes 442376 | tf_op jit(solution)/shard_map/ppermute | solution.py:729
  18.3 6.9 %collective-permute-start.4 = (f32[6,4,1,1152]{3,2,1,0:T(1,128)S(1)}, f32[6,4,1,1152]{3,2,1,0:T(1,128)S(1)}, u32[]{:S(2)}, u32[]{:S(2)}) collective-permute-start(f32[6,4,1,1152]{3,2,1,0:T(1,128)S(1)} %get-tuple-element.45), channel_id=1, source_target_pairs={{0,4},{4,8},{8,12},{1,5},{5,9},{9,13},{2,6},{6,10},{10,14},{3,7},{... | collective-permute-start | bytes 331784 | tf_op jit(solution)/shard_map/ppermute | solution.py:728
  28.9 2.1 %collective-permute-start.13 = (f32[1,4,16,1152]{3,2,1,0:T(8,128)S(1)}, f32[1,4,16,1152]{3,2,1,0:T(8,128)S(1)}, u32[]{:S(2)}, u32[]{:S(2)}) collective-permute-start(f32[1,4,16,1152]{3,2,1,0:T(8,128)S(1)} %get-tuple-element.51.refs_2_), channel_id=1, source_target_pairs={{0,1},{1,0},{2,3},{3,2},{4,5},{5,4},{6,7},{7,6},{8,9},{9,8},{10,11... | collective-permute-start | bytes 884744 | tf_op jit(solution)/shard_map/ppermute | solution.py:682
  29.0 2.1 %collective-permute-start.14 = (f32[1,4,16,1152]{3,2,1,0:T(8,128)S(1)}, f32[1,4,16,1152]{3,2,1,0:T(8,128)S(1)}, u32[]{:S(2)}, u32[]{:S(2)}) collective-permute-start(f32[1,4,16,1152]{3,2,1,0:T(8,128)S(1)} %get-tuple-element.52.refs_4_), channel_id=1, source_target_pairs={{0,1},{1,0},{2,3},{3,2},{4,5},{5,4},{6,7},{7,6},{8,9},{9,8},{10,11... | collective-permute-start | bytes 884744 | tf_op jit(solution)/shard_map/ppermute | solution.py:682
  29.5 9.1 %collective-permute-start.7 = (f32[7,4,2,1152]{3,2,1,0:T(2,128)S(1)}, f32[7,4,2,1152]{3,2,1,0:T(2,128)S(1)}, u32[]{:S(2)}, u32[]{:S(2)}) collective-permute-start(f32[7,4,2,1152]{3,2,1,0:T(2,128)S(1)} %get-tuple-element.47.refs_6_.refs_0_), channel_id=1, source_target_pairs={{0,2},{2,0},{1,3},{3,1},{4,6},{6,4},{5,7},{7,5},{8,10},{10,8},{9,1... | collective-permute-start | bytes 774152 | tf_op jit(solution)/shard_map/ppermute | solution.py:680
  34.8 14.4 %collective-permute-start.16 = (f32[112,1152]{1,0:T(8,128)S(1)}, f32[112,1152]{1,0:T(8,128)S(1)}, u32[]{:S(2)}, u32[]{:S(2)}) collective-permute-start(f32[112,1152]{1,0:T(8,128)S(1)} %get-tuple-element.53.refs_12_), channel_id=1, source_target_pairs={{0,2},{2,0},{1,3},{3,1},{4,6},{6,4},{5,7},{7,5},{8,10},{10,8},{9,1... | collective-permute-start | bytes 1548296 | tf_op jit(solution)/shard_map/ppermute | solution.py:680
  36.5 2.1 %collective-permute-start.9 = (f32[1,4,3,1152]{3,2,1,0:T(4,128)S(1)}, f32[1,4,3,1152]{3,2,1,0:T(4,128)S(1)}, u32[]{:S(2)}, u32[]{:S(2)}) collective-permute-start(f32[1,4,3,1152]{3,2,1,0:T(4,128)S(1)} %get-tuple-element.49.refs_4_), channel_id=1, source_target_pairs={{0,1},{1,0},{2,3},{3,2},{4,5},{5,4},{6,7},{7,6},{8,9},{9,8},{10,11... | collective-permute-start | bytes 165896 | tf_op jit(solution)/shard_map/ppermute | solution.py:682
  36.5 2.6 %collective-permute-start.10 = (f32[1,4,3,1152]{3,2,1,0:T(4,128)S(1)}, f32[1,4,3,1152]{3,2,1,0:T(4,128)S(1)}, u32[]{:S(2)}, u32[]{:S(2)}) collective-permute-start(f32[1,4,3,1152]{3,2,1,0:T(4,128)S(1)} %get-tuple-element.50.refs_6_), channel_id=1, source_target_pairs={{0,1},{1,0},{2,3},{3,2},{4,5},{5,4},{6,7},{7,6},{8,9},{9,8},{10,11... | collective-permute-start | bytes 165896 | tf_op jit(solution)/shard_map/ppermute | solution.py:682
  37.0 3.7 %collective-permute-start.6 = (f32[7,4,2,1152]{3,2,1,0:T(2,128)S(1)}, f32[7,4,2,1152]{3,2,1,0:T(2,128)S(1)}, u32[]{:S(2)}, u32[]{:S(2)}) collective-permute-start(f32[7,4,2,1152]{3,2,1,0:T(2,128)S(1)} %get-tuple-element.47.refs_6_.refs_0_), channel_id=1, source_target_pairs={{0,1},{1,0},{2,3},{3,2},{4,5},{5,4},{6,7},{7,6},{8,9},{9,8},{10,11... | collective-permute-start | bytes 774152 | tf_op jit(solution)/shard_map/ppermute | solution.py:682
  38.5 2.2 %collective-permute-start.8 = (f32[7,4,2,1152]{3,2,1,0:T(2,128)S(1)}, f32[7,4,2,1152]{3,2,1,0:T(2,128)S(1)}, u32[]{:S(2)}, u32[]{:S(2)}) collective-permute-start(f32[7,4,2,1152]{3,2,1,0:T(2,128)S(1)} %collective-permute-done.7.refs_2_), channel_id=1, source_target_pairs={{0,1},{1,0},{2,3},{3,2},{4,5},{5,4},{6,7},{7,6},{8,9},{9,8},{10,11... | collective-permute-start | bytes 774152 | tf_op jit(solution)/shard_map/ppermute | solution.py:682
  38.5 1.8 %collective-permute-start.11 = (f32[48,1152]{1,0:T(8,128)S(1)}, f32[48,1152]{1,0:T(8,128)S(1)}, u32[]{:S(2)}, u32[]{:S(2)}) collective-permute-start(f32[48,1152]{1,0:T(8,128)S(1)} %get-tuple-element.41.refs_0_.refs_8_), channel_id=1, source_target_pairs={{0,1},{1,0},{2,3},{3,2},{4,5},{5,4},{6,7},{7,6},{8,9},{9,8},{10,11... | collective-permute-start | bytes 663560 | tf_op jit(solution)/shard_map/ppermute | solution.py:682
  39.1 1.6 %collective-permute-start.12 = (f32[48,1152]{1,0:T(8,128)S(1)}, f32[48,1152]{1,0:T(8,128)S(1)}, u32[]{:S(2)}, u32[]{:S(2)}) collective-permute-start(f32[48,1152]{1,0:T(8,128)S(1)} %collective-permute-done.3.refs_1_.refs_10_), channel_id=1, source_target_pairs={{0,1},{1,0},{2,3},{3,2},{4,5},{5,4},{6,7},{7,6},{8,9},{9,8},{10,11... | collective-permute-start | bytes 663560 | tf_op jit(solution)/shard_map/ppermute | solution.py:682
  (2 other events, 8.4 us)

commit v19 on v17

--- a/solution.py
+++ b/solution.py
@@ -608,25 +608,34 @@
 
 
 def finish_winds_kernel(count, own_ref, edge_ref, *refs):
-    arrived_refs, out_refs = refs[:count], refs[-2:]
+    arrived_refs, (*out_refs, result_ref, sems) = refs[:count], refs[len(refs) - 4 :]
     _, L, R, N = own_ref.shape
+    row = row_ids((R, N))
+    copies = []
     for f, out_ref in enumerate(out_refs):
         for i in range(L):
             start = (f * L + i) * (R - 2)
-            total = own_ref[f, i, 1 : R - 1]
+            first = start // 8 * 8
+            total = own_ref[f, i]
             for ref in arrived_refs:
-                total = total + ref[start : start + R - 2]
-            out_ref[i, 1 : R - 1] = total
-            out_ref[i, 0:1] = edge_ref[f, i, 0:1]
-            out_ref[i, R - 1 : R] = edge_ref[f, i, 1:2]
+                size = min(R + 8, ref.shape[0] - first)
+                total = total + pltpu.roll(ref[first : first + size], (1 - (start - first)) % size, 0)[0:R]
+            total = jnp.where(row == 0, edge_ref[f, i, 0:1], jnp.where(row == R - 1, edge_ref[f, i, 1:2], total))
+            result_ref[f, i] = total
+            copies.append(pltpu.make_async_copy(result_ref.at[f, i], out_ref.at[i], sems.at[f, i]))
+            copies[-1].start()
+    for copy in copies:
+        copy.wait()
 
 
 def finish_winds(own, arrived, edge, wait):
+    F, L = own.shape[:2]
     return pl.pallas_call(
         functools.partial(finish_winds_kernel, len(arrived)),
         in_specs=[VMEM] * (2 + len(arrived)) + after(wait),
-        out_specs=[VMEM] * 2,
-        out_shape=[jax.ShapeDtypeStruct(own.shape[1:], jnp.float32)] * 2,
+        out_specs=[pl.BlockSpec(memory_space=pl.ANY)] * F,
+        out_shape=[jax.ShapeDtypeStruct(own.shape[1:], jnp.float32)] * F,
+        scratch_shapes=[pltpu.VMEM(own.shape, jnp.float32), pltpu.SemaphoreType.DMA((F, L))],
         compiler_params=params(),
         cost_estimate=cost(own.size, 12 * own.size),
         name="finish_winds",

time: 50.2 us -> 50.2 us (level)
  no operation moved by 1% of the time
where the time goes in v19:
time: 50.2 us; the launch traced here: 50 us
  Pallas kernels  19.4 us (39%)
  waiting for transfers between devices  15.4 us (31%)
  starting transfers between devices  14.1 us (28%)
  between operations  0.88 us (2%)
    ppermute x5, waiting for transfers between devices, shifted(): lax.ppermute(value, 'lev', [(i, (i + s) % lev_count) for i in range(lev_c...  9.86 us
    ppermute x5, starting transfers between devices, shifted(): lax.ppermute(value, 'lev', [(i, (i + s) % lev_count) for i in range(lev_c...  6.45 us
    ppermute x1, starting transfers between devices, per_device(): up = lax.ppermute(last, 'lat', northward)  4.55 us
    pallas_call x3, Pallas kernels, remap_parts(): pl.pallas_call(functools.partial(remap_kernel, counts, tuple(steps), tupl...  4.45 us
    pallas_call x1, Pallas kernels, remap_edges(): pl.pallas_call(functools.partial(remap_edge_kernel, counts), in_specs=[VM...  3.7 us
    pallas_call x1, Pallas kernels, second_step(): pl.pallas_call(functools.partial(second_kernel, lat_rows), grid=(L,), in_...  3.62 us
    ppermute x10, waiting for transfers between devices, shifted(): lax.ppermute(value, 'sub', [(i, (i + t) % sub_count) for i in range(sub_c...  3.25 us
    ppermute x1, waiting for transfers between devices, per_device(): up = lax.ppermute(last, 'lat', northward)  2.3 us
  transfers between devices with their start and end apart: 17, of which 9 were waited for; matrix products, arithmetic and copies ran while one was open for 0% of the time, Pallas kernels for 33%

profile of v19, /device:TPU:0, one launch (start us, length us, event | category | flops | bytes accessed | tf_op | source)
XLA Modules:
  0.0 50.0 jit_solution(13320723158128205247)
XLA Ops:
  0.6 1.9 %first_step.1 = (f32[4,16,1152]{2,1,0:T(8,128)S(1)}, f32[234,128]{1,0:T(8,128)S(1)}, f32[1,4,3,1152]{3,2,1,0:T(4,128)S(1)}, f32[4,16,1152]{2,1,0:T(8,128)S(1)}, ...) custom-call(f32[4,24,128]{2,1,0:T(8,128)} %constant.6.clone.table_hbm.table_ref, ...), custom_call_target="tpu_custom_call" | custom-call | flops 2949120 | bytes 4423680 | tf_op jit(solution)/shard_map/first_step/pallas_call | solution.py:139
  2.5 3.0 %collective-permute-start.1 = (f32[234,128]{1,0:T(8,128)S(1)}, f32[234,128]{1,0:T(8,128)S(1)}, u32[]{:S(2)}, u32[]{:S(2)}) collective-permute-start(f32[234,128]{1,0:T(8,128)S(1)} %get-tuple-element.40), channel_id=1, source_target_pairs={{0,2},{2,0},{1,3},{3,1},{4,6},{6,4},{5,7},{7,5},{8,10},{10,8},{9,1... | collective-permute-start | bytes 359432 | tf_op jit(solution)/shard_map/ppermute | solution.py:696
  5.5 1.6 %inner_step.1 = (f32[5,4,16,1152]{3,2,1,0:T(8,128)S(1)}, f32[48,1152]{1,0:T(8,128)S(1)}) custom-call(f32[4,24,128]{2,1,0:T(8,128)S(1)} %copy-done.6, f32[4,16,1152]{2,1,0:T(8,128)S(1)} %get-tuple-element.34.new_ref, f32[4,16,1152]{2,1,0:T(8,128)S(1)} %get-tuple-element.35.thick_ref, f32[4,16,1152]{2,1,0:T(8,128)S(1)} %get-tuple-element.36.u_ref, ...), custom_call_target="tpu_custom_call" | custom-call | flops 9584640 | bytes 4718592 | tf_op jit(solution)/shard_map/inner_step/pallas_call | solution.py:185
  7.4 1.5 %collective-permute-done.1.both_ref = f32[234,128]{1,0:T(8,128)S(1)} collective-permute-done((f32[234,128]{1,0:T(8,128)S(1)}, f32[234,128]{1,0:T(8,128)S(1)}, u32[]{:S(2)}, u32[]{:S(2)}) %collective-permute-start.1) | collective-permute-done | bytes 119840 | tf_op jit(solution)/shard_map/ppermute | solution.py:696
  9.0 1.7 %collective-permute-done.2.refs_1_ = f32[16,1152]{1,0:T(8,128)S(1)} collective-permute-done((f32[16,1152]{1,0:T(8,128)S(1)}, f32[16,1152]{1,0:T(8,128)S(1)}, u32[]{:S(2)}, u32[]{:S(2)}) %collective-permute-start.2) | collective-permute-done | bytes 73760 | tf_op jit(solution)/shard_map/ppermute | solution.py:698
  10.7 1.4 %remap_parts.3.refs_0_ = f32[176,1152]{1,0:T(8,128)S(1)} custom-call(f32[16,8,128]{2,1,0:T(8,128)S(1)} %broadcast_in_dim.4.weight_ref, f32[5,4,16,1152]{3,2,1,0:T(8,128)S(1)} %get-tuple-element.39.refs_0_.refs_2_, f32[5,4,16,1152]{3,2,1,0:T(8,128)S(1)} %collective-permute-done.refs_1_.refs_3_, f32[5,4,16,1152]{3,2,1,0:T(8,128)S(1)} %get-tuple-element.39.refs_0_.refs_2_, ...), custom_call_target="tpu_custom_call" | custom-call | flops 7667712 | bytes 4423680 | tf_op jit(solution)/shard_map/remap_parts/pallas_call | solution.py:519
  12.2 1.4 %collective-permute-start.15 = (f32[176,1152]{1,0:T(8,128)S(1)}, f32[176,1152]{1,0:T(8,128)S(1)}, u32[]{:S(2)}, u32[]{:S(2)}) collective-permute-start(f32[176,1152]{1,0:T(8,128)S(1)} %remap_parts.3.refs_0_), channel_id=1, source_target_pairs={{0,2},{2,0},{1,3},{3,1},{4,6},{6,4},{5,7},{7,5},{8,10},{10,8},{9,1... | collective-permute-start | bytes 2433032 | tf_op jit(solution)/shard_map/ppermute | solution.py:696
  13.6 1.5 %collective-permute-done.3.refs_1_.refs_10_ = f32[48,1152]{1,0:T(8,128)S(1)} collective-permute-done((f32[48,1152]{1,0:T(8,128)S(1)}, f32[48,1152]{1,0:T(8,128)S(1)}, u32[]{:S(2)}, u32[]{:S(2)}) %collective-permute-start.3) | collective-permute-done | bytes 221216 | tf_op jit(solution)/shard_map/ppermute | solution.py:696
  15.1 1.7 %edge_rows.1 = (f32[6,4,1,1152]{3,2,1,0:T(1,128)S(1)}, f32[8,4,1,1152]{3,2,1,0:T(1,128)S(1)}) custom-call(f32[4,16,1152]{2,1,0:T(8,128)} %thick_ref.1, f32[4,16,1152]{2,1,0:T(8,128)} %u_ref.1, f32[4,16,1152]{2,1,0:T(8,128)} %v_ref.1, f32[4,4,16,1152]{3,2,1,0:T(8,128)} %tracer_ref.1, f32[176,1152]{1,0:T(8,128)S(1)} %remap_parts.3.refs_0_, ...), custom_call_target="tpu_custom_call" | custom-call | flops 10000000000 | bytes 1000000000 | tf_op jit(solution)/shard_map/edge_rows/pallas_call | solution.py:674
  16.9 1.3 %collective-permute-start.5 = (f32[8,4,1,1152]{3,2,1,0:T(1,128)S(1)}, f32[8,4,1,1152]{3,2,1,0:T(1,128)S(1)}, u32[]{:S(2)}, u32[]{:S(2)}) collective-permute-start(f32[8,4,1,1152]{3,2,1,0:T(1,128)S(1)} %get-tuple-element.46), channel_id=1, source_target_pairs={{4,0},{8,4},{12,8},{5,1},{9,5},{13,9},{6,2},{10,6},{14,10},{7,3},{... | collective-permute-start | bytes 442376 | tf_op jit(solution)/shard_map/ppermute | solution.py:745
  18.2 4.6 %collective-permute-start.4 = (f32[6,4,1,1152]{3,2,1,0:T(1,128)S(1)}, f32[6,4,1,1152]{3,2,1,0:T(1,128)S(1)}, u32[]{:S(2)}, u32[]{:S(2)}) collective-permute-start(f32[6,4,1,1152]{3,2,1,0:T(1,128)S(1)} %get-tuple-element.45), channel_id=1, source_target_pairs={{0,4},{4,8},{8,12},{1,5},{5,9},{9,13},{2,6},{6,10},{10,14},{3,7},{... | collective-permute-start | bytes 331784 | tf_op jit(solution)/shard_map/ppermute | solution.py:744
  22.7 2.3 %collective-permute-done.4.up_ref = f32[6,4,1,1152]{3,2,1,0:T(1,128)S(1)} collective-permute-done((f32[6,4,1,1152]{3,2,1,0:T(1,128)S(1)}, f32[6,4,1,1152]{3,2,1,0:T(1,128)S(1)}, u32[]{:S(2)}, u32[]{:S(2)}) %collective-permute-start.4) | collective-permute-done | bytes 110624 | tf_op jit(solution)/shard_map/ppermute | solution.py:744
  25.1 3.6 %second_step.1 = (f32[1,4,16,1152]{3,2,1,0:T(8,128)S(1)}, f32[1,4,16,1152]{3,2,1,0:T(8,128)S(1)}, f32[7,4,2,1152]{3,2,1,0:T(2,128)S(1)}) custom-call(f32[4,24,128]{2,1,0:T(8,128)S(1)} %copy-done.6, f32[4,16,1152]{2,1,0:T(8,128)S(1)} %copy-done.1, f32[4,16,1152]{2,1,0:T(8,128)S(1)} %copy-done.2, f32[4,16,1152]{2,1,0:T(8,128)S(1)} %copy-done.3, ...), custom_call_target="tpu_custom_call" | custom-call | flops 503316480 | bytes 3538944 | tf_op jit(solution)/shard_map/second_step/pallas_call | solution.py:323
  29.6 1.3 %remap_parts.4 = (f32[4,4,16,1152]{3,2,1,0:T(8,128)S(1)}, f32[4,16,1152]{2,1,0:T(8,128)S(1)}) custom-call(f32[16,8,128]{2,1,0:T(8,128)S(1)} %broadcast_in_dim.4.weight_ref, f32[5,4,16,1152]{3,2,1,0:T(8,128)S(1)} %get-tuple-element.39.refs_0_.refs_2_, f32[5,4,16,1152]{3,2,1,0:T(8,128)S(1)} %collective-permute-done.refs_1_.refs_3_, ...), custom_call_target="tpu_custom_call" | custom-call | flops 7667712 | bytes 4423680 | tf_op jit(solution)/shard_map/remap_parts/pallas_call | solution.py:519
  30.9 2.0 %collective-permute-done.15.refs_9_.refs_0_ = f32[176,1152]{1,0:T(8,128)S(1)} collective-permute-done((f32[176,1152]{1,0:T(8,128)S(1)}, f32[176,1152]{1,0:T(8,128)S(1)}, u32[]{:S(2)}, u32[]{:S(2)}) %collective-permute-start.15) | collective-permute-done | bytes 811040 | tf_op jit(solution)/shard_map/ppermute | solution.py:696
  32.9 1.8 %remap_parts.5 = (f32[2,4,16,1152]{3,2,1,0:T(8,128)S(1)}, f32[112,1152]{1,0:T(8,128)S(1)}) custom-call(f32[16,8,128]{2,1,0:T(8,128)S(1)} %broadcast_in_dim.4.weight_ref, f32[5,4,16,1152]{3,2,1,0:T(8,128)S(1)} %get-tuple-element.39.refs_0_.refs_2_, f32[5,4,16,1152]{3,2,1,0:T(8,128)S(1)} %collective-permute-done.refs_1_.refs_3_, ...), custom_call_target="tpu_custom_call" | custom-call | flops 10616832 | bytes 3538944 | tf_op jit(solution)/shard_map/remap_parts/pallas_call | solution.py:519
  34.6 1.7 %collective-permute-start.16 = (f32[112,1152]{1,0:T(8,128)S(1)}, f32[112,1152]{1,0:T(8,128)S(1)}, u32[]{:S(2)}, u32[]{:S(2)}) collective-permute-start(f32[112,1152]{1,0:T(8,128)S(1)} %get-tuple-element.53.refs_12_), channel_id=1, source_target_pairs={{0,2},{2,0},{1,3},{3,1},{4,6},{6,4},{5,7},{7,5},{8,10},{10,8},{9,1... | collective-permute-start | bytes 1548296 | tf_op jit(solution)/shard_map/ppermute | solution.py:696
  36.9 1.6 %collective-permute-done.7.refs_2_ = f32[7,4,2,1152]{3,2,1,0:T(2,128)S(1)} collective-permute-done((f32[7,4,2,1152]{3,2,1,0:T(2,128)S(1)}, f32[7,4,2,1152]{3,2,1,0:T(2,128)S(1)}, u32[]{:S(2)}, u32[]{:S(2)}) %collective-permute-start.7) | collective-permute-done | bytes 258080 | tf_op jit(solution)/shard_map/ppermute | solution.py:696
  38.4 0.5 %collective-permute-start.11 = (f32[48,1152]{1,0:T(8,128)S(1)}, f32[48,1152]{1,0:T(8,128)S(1)}, u32[]{:S(2)}, u32[]{:S(2)}) collective-permute-start(f32[48,1152]{1,0:T(8,128)S(1)} %get-tuple-element.41.refs_0_.refs_8_), channel_id=1, source_target_pairs={{0,1},{1,0},{2,3},{3,2},{4,5},{5,4},{6,7},{7,6},{8,9},{9,8},{10,11... | collective-permute-start | bytes 663560 | tf_op jit(solution)/shard_map/ppermute | solution.py:698
  39.0 1.3 %collective-permute-done.11.refs_9_ = f32[48,1152]{1,0:T(8,128)S(1)} collective-permute-done((f32[48,1152]{1,0:T(8,128)S(1)}, f32[48,1152]{1,0:T(8,128)S(1)}, u32[]{:S(2)}, u32[]{:S(2)}) %collective-permute-start.11) | collective-permute-done | bytes 221216 | tf_op jit(solution)/shard_map/ppermute | solution.py:698
  40.6 3.7 %remap_edges.1 = (f32[6,4,2,1152]{3,2,1,0:T(2,128)S(1)}, f32[4,2,1152]{2,1,0:T(2,128)S(1)}, f32[4,4,3,1152]{3,2,1,0:T(4,128)S(1)}) custom-call(f32[16,8,128]{2,1,0:T(8,128)S(1)} %broadcast_in_dim.4.weight_ref, f32[7,4,2,1152]{3,2,1,0:T(2,128)S(1)} %get-tuple-element.47.refs_6_.refs_0_, f32[7,4,2,1152]{3,2,1,0:T(2,128)S(1)} %collective-permute-done.6.refs_1_, ...), custom_call_target="tpu_custom_call" | custom-call | flops 5898240 | bytes 3096576 | tf_op jit(solution)/shard_map/remap_edges/pallas_call | solution.py:557
  44.3 1.4 %finish_tracers.1 = (f32[4,4,16,1152]{3,2,1,0:T(8,128)}, f32[4,16,1152]{2,1,0:T(8,128)}, f32[8,128]{1,0:T(8,128)S(1)}) custom-call(f32[4,4,16,1152]{3,2,1,0:T(8,128)S(1)} %get-tuple-element.48.refs_8_.own_ref, f32[4,4,3,1152]{3,2,1,0:T(4,128)S(1)} %get-tuple-element.54.near_ref, f32[6,4,2,1152]{3,2,1,0:T(2,128)S(1)} %get-tuple-element.55.edge_ref, ...), custom_call_target="tpu_custom_call" | custom-call | flops 589824 | bytes 3538944 | tf_op jit(solution)/shard_map/finish_tracers/pallas_call | solution.py:595
  45.7 3.3 %collective-permute-done.16.refs_0_ = f32[112,1152]{1,0:T(8,128)S(1)} collective-permute-done((f32[112,1152]{1,0:T(8,128)S(1)}, f32[112,1152]{1,0:T(8,128)S(1)}, u32[]{:S(2)}, u32[]{:S(2)}) %collective-permute-start.16) | collective-permute-done | bytes 516128 | tf_op jit(solution)/shard_map/ppermute | solution.py:696
  49.1 0.9 %finish_winds.1 = (f32[4,16,1152]{2,1,0:T(8,128)}, f32[4,16,1152]{2,1,0:T(8,128)}) custom-call(f32[2,4,16,1152]{3,2,1,0:T(8,128)S(1)} %get-tuple-element.59.own_ref, f32[6,4,2,1152]{3,2,1,0:T(2,128)S(1)} %get-tuple-element.55.edge_ref, f32[112,1152]{1,0:T(8,128)S(1)} %collective-permute-done.16.refs_0_, f32[8,128]{1,0:T(8,128)S(1)} %get-tuple-element.60.refs_1_), custom_call_target="tpu_custom_call" | custom-call | flops 147456 | bytes 1769472 | tf_op jit(solution)/shard_map/finish_winds/pallas_call | solution.py:633
  (42 shorter events, 2.2 us)
Async XLA Ops:
  2.5 6.3 %collective-permute-start.1 = (f32[234,128]{1,0:T(8,128)S(1)}, f32[234,128]{1,0:T(8,128)S(1)}, u32[]{:S(2)}, u32[]{:S(2)}) collective-permute-start(f32[234,128]{1,0:T(8,128)S(1)} %get-tuple-element.40), channel_id=1, source_target_pairs={{0,2},{2,0},{1,3},{3,1},{4,6},{6,4},{5,7},{7,5},{8,10},{10,8},{9,1... | collective-permute-start | bytes 359432 | tf_op jit(solution)/shard_map/ppermute | solution.py:696
  7.2 3.5 %collective-permute-start = (f32[5,4,16,1152]{3,2,1,0:T(8,128)S(1)}, f32[5,4,16,1152]{3,2,1,0:T(8,128)S(1)}, u32[]{:S(2)}, u32[]{:S(2)}) collective-permute-start(f32[5,4,16,1152]{3,2,1,0:T(8,128)S(1)} %get-tuple-element.39.refs_0_.refs_2_), channel_id=1, source_target_pairs={{0,1},{1,0},{2,3},{3,2},{4,5},{5,4},{6,7},{7,6},{8,9},{9,8},{10,11... | collective-permute-start | bytes 4423688 | tf_op jit(solution)/shard_map/ppermute | solution.py:698
  7.3 7.9 %collective-permute-start.3 = (f32[48,1152]{1,0:T(8,128)S(1)}, f32[48,1152]{1,0:T(8,128)S(1)}, u32[]{:S(2)}, u32[]{:S(2)}) collective-permute-start(f32[48,1152]{1,0:T(8,128)S(1)} %get-tuple-element.41.refs_0_.refs_8_), channel_id=1, source_target_pairs={{0,2},{2,0},{1,3},{3,1},{4,6},{6,4},{5,7},{7,5},{8,10},{10,8},{9,1... | collective-permute-start | bytes 663560 | tf_op jit(solution)/shard_map/ppermute | solution.py:696
  8.9 1.7 %collective-permute-start.2 = (f32[16,1152]{1,0:T(8,128)S(1)}, f32[16,1152]{1,0:T(8,128)S(1)}, u32[]{:S(2)}, u32[]{:S(2)}) collective-permute-start(f32[16,1152]{1,0:T(8,128)S(1)} %get-tuple-element.42.refs_0_), channel_id=1, source_target_pairs={{0,1},{1,0},{2,3},{3,2},{4,5},{5,4},{6,7},{7,6},{8,9},{9,8},{10,11... | collective-permute-start | bytes 221192 | tf_op jit(solution)/shard_map/ppermute | solution.py:698
  12.1 12.9 %copy-start.8 = (s32[16]{0:T(128)S(1)}, s32[16]{0:T(128)}, u32[]{:S(2)}) copy-start(s32[16]{0:T(128)} %param.14) | copy-start | bytes 196
  12.1 13.0 %copy-start = (f32[4,4,16,1152]{3,2,1,0:T(8,128)S(1)}, f32[4,4,16,1152]{3,2,1,0:T(8,128)}, u32[]{:S(2)}) copy-start(f32[4,4,16,1152]{3,2,1,0:T(8,128)} %tracer_ref.1) | copy-start | bytes 3538948
  12.1 13.0 %copy-start.1 = (f32[4,16,1152]{2,1,0:T(8,128)S(1)}, f32[4,16,1152]{2,1,0:T(8,128)}, u32[]{:S(2)}) copy-start(f32[4,16,1152]{2,1,0:T(8,128)} %thick_ref.1) | copy-start | bytes 884740
  12.2 12.9 %copy-start.2 = (f32[4,16,1152]{2,1,0:T(8,128)S(1)}, f32[4,16,1152]{2,1,0:T(8,128)}, u32[]{:S(2)}) copy-start(f32[4,16,1152]{2,1,0:T(8,128)} %u_ref.1) | copy-start | bytes 884740
  12.2 12.9 %copy-start.3 = (f32[4,16,1152]{2,1,0:T(8,128)S(1)}, f32[4,16,1152]{2,1,0:T(8,128)}, u32[]{:S(2)}) copy-start(f32[4,16,1152]{2,1,0:T(8,128)} %v_ref.1) | copy-start | bytes 884740
  12.2 12.9 %copy-start.4 = (bf16[5,256,256]{2,1,0:T(8,128)(2,1)S(1)}, bf16[5,256,256]{2,1,0:T(8,128)(2,1)}, u32[]{:S(2)}) copy-start(bf16[5,256,256]{2,1,0:T(8,128)(2,1)} %constant.7.clone.high_ref) | copy-start | bytes 1966084
  12.2 12.9 %copy-start.5 = (bf16[5,256,256]{2,1,0:T(8,128)(2,1)S(1)}, bf16[5,256,256]{2,1,0:T(8,128)(2,1)}, u32[]{:S(2)}) copy-start(bf16[5,256,256]{2,1,0:T(8,128)(2,1)} %constant.8.clone.low_ref) | copy-start | bytes 1966084
  12.2 20.7 %collective-permute-start.15 = (f32[176,1152]{1,0:T(8,128)S(1)}, f32[176,1152]{1,0:T(8,128)S(1)}, u32[]{:S(2)}, u32[]{:S(2)}) collective-permute-start(f32[176,1152]{1,0:T(8,128)S(1)} %remap_parts.3.refs_0_), channel_id=1, source_target_pairs={{0,2},{2,0},{1,3},{3,1},{4,6},{6,4},{5,7},{7,5},{8,10},{10,8},{9,1... | collective-permute-start | bytes 2433032 | tf_op jit(solution)/shard_map/ppermute | solution.py:696
  16.9 8.2 %collective-permute-start.5 = (f32[8,4,1,1152]{3,2,1,0:T(1,128)S(1)}, f32[8,4,1,1152]{3,2,1,0:T(1,128)S(1)}, u32[]{:S(2)}, u32[]{:S(2)}) collective-permute-start(f32[8,4,1,1152]{3,2,1,0:T(1,128)S(1)} %get-tuple-element.46), channel_id=1, source_target_pairs={{4,0},{8,4},{12,8},{5,1},{9,5},{13,9},{6,2},{10,6},{14,10},{7,3},{... | collective-permute-start | bytes 442376 | tf_op jit(solution)/shard_map/ppermute | solution.py:745
  18.2 6.9 %collective-permute-start.4 = (f32[6,4,1,1152]{3,2,1,0:T(1,128)S(1)}, f32[6,4,1,1152]{3,2,1,0:T(1,128)S(1)}, u32[]{:S(2)}, u32[]{:S(2)}) collective-permute-start(f32[6,4,1,1152]{3,2,1,0:T(1,128)S(1)} %get-tuple-element.45), channel_id=1, source_target_pairs={{0,4},{4,8},{8,12},{1,5},{5,9},{9,13},{2,6},{6,10},{10,14},{3,7},{... | collective-permute-start | bytes 331784 | tf_op jit(solution)/shard_map/ppermute | solution.py:744
  28.8 2.1 %collective-permute-start.13 = (f32[1,4,16,1152]{3,2,1,0:T(8,128)S(1)}, f32[1,4,16,1152]{3,2,1,0:T(8,128)S(1)}, u32[]{:S(2)}, u32[]{:S(2)}) collective-permute-start(f32[1,4,16,1152]{3,2,1,0:T(8,128)S(1)} %get-tuple-element.51.refs_2_), channel_id=1, source_target_pairs={{0,1},{1,0},{2,3},{3,2},{4,5},{5,4},{6,7},{7,6},{8,9},{9,8},{10,11... | collective-permute-start | bytes 884744 | tf_op jit(solution)/shard_map/ppermute | solution.py:698
  28.8 2.1 %collective-permute-start.14 = (f32[1,4,16,1152]{3,2,1,0:T(8,128)S(1)}, f32[1,4,16,1152]{3,2,1,0:T(8,128)S(1)}, u32[]{:S(2)}, u32[]{:S(2)}) collective-permute-start(f32[1,4,16,1152]{3,2,1,0:T(8,128)S(1)} %get-tuple-element.52.refs_4_), channel_id=1, source_target_pairs={{0,1},{1,0},{2,3},{3,2},{4,5},{5,4},{6,7},{7,6},{8,9},{9,8},{10,11... | collective-permute-start | bytes 884744 | tf_op jit(solution)/shard_map/ppermute | solution.py:698
  29.3 9.1 %collective-permute-start.7 = (f32[7,4,2,1152]{3,2,1,0:T(2,128)S(1)}, f32[7,4,2,1152]{3,2,1,0:T(2,128)S(1)}, u32[]{:S(2)}, u32[]{:S(2)}) collective-permute-start(f32[7,4,2,1152]{3,2,1,0:T(2,128)S(1)} %get-tuple-element.47.refs_6_.refs_0_), channel_id=1, source_target_pairs={{0,2},{2,0},{1,3},{3,1},{4,6},{6,4},{5,7},{7,5},{8,10},{10,8},{9,1... | collective-permute-start | bytes 774152 | tf_op jit(solution)/shard_map/ppermute | solution.py:696
  34.6 14.4 %collective-permute-start.16 = (f32[112,1152]{1,0:T(8,128)S(1)}, f32[112,1152]{1,0:T(8,128)S(1)}, u32[]{:S(2)}, u32[]{:S(2)}) collective-permute-start(f32[112,1152]{1,0:T(8,128)S(1)} %get-tuple-element.53.refs_12_), channel_id=1, source_target_pairs={{0,2},{2,0},{1,3},{3,1},{4,6},{6,4},{5,7},{7,5},{8,10},{10,8},{9,1... | collective-permute-start | bytes 1548296 | tf_op jit(solution)/shard_map/ppermute | solution.py:696
  36.3 2.1 %collective-permute-start.9 = (f32[1,4,3,1152]{3,2,1,0:T(4,128)S(1)}, f32[1,4,3,1152]{3,2,1,0:T(4,128)S(1)}, u32[]{:S(2)}, u32[]{:S(2)}) collective-permute-start(f32[1,4,3,1152]{3,2,1,0:T(4,128)S(1)} %get-tuple-element.49.refs_4_), channel_id=1, source_target_pairs={{0,1},{1,0},{2,3},{3,2},{4,5},{5,4},{6,7},{7,6},{8,9},{9,8},{10,11... | collective-permute-start | bytes 165896 | tf_op jit(solution)/shard_map/ppermute | solution.py:698
  36.4 2.6 %collective-permute-start.10 = (f32[1,4,3,1152]{3,2,1,0:T(4,128)S(1)}, f32[1,4,3,1152]{3,2,1,0:T(4,128)S(1)}, u32[]{:S(2)}, u32[]{:S(2)}) collective-permute-start(f32[1,4,3,1152]{3,2,1,0:T(4,128)S(1)} %get-tuple-element.50.refs_6_), channel_id=1, source_target_pairs={{0,1},{1,0},{2,3},{3,2},{4,5},{5,4},{6,7},{7,6},{8,9},{9,8},{10,11... | collective-permute-start | bytes 165896 | tf_op jit(solution)/shard_map/ppermute | solution.py:698
  36.9 3.7 %collective-permute-start.6 = (f32[7,4,2,1152]{3,2,1,0:T(2,128)S(1)}, f32[7,4,2,1152]{3,2,1,0:T(2,128)S(1)}, u32[]{:S(2)}, u32[]{:S(2)}) collective-permute-start(f32[7,4,2,1152]{3,2,1,0:T(2,128)S(1)} %get-tuple-element.47.refs_6_.refs_0_), channel_id=1, source_target_pairs={{0,1},{1,0},{2,3},{3,2},{4,5},{5,4},{6,7},{7,6},{8,9},{9,8},{10,11... | collective-permute-start | bytes 774152 | tf_op jit(solution)/shard_map/ppermute | solution.py:698
  38.4 2.2 %collective-permute-start.8 = (f32[7,4,2,1152]{3,2,1,0:T(2,128)S(1)}, f32[7,4,2,1152]{3,2,1,0:T(2,128)S(1)}, u32[]{:S(2)}, u32[]{:S(2)}) collective-permute-start(f32[7,4,2,1152]{3,2,1,0:T(2,128)S(1)} %collective-permute-done.7.refs_2_), channel_id=1, source_target_pairs={{0,1},{1,0},{2,3},{3,2},{4,5},{5,4},{6,7},{7,6},{8,9},{9,8},{10,11... | collective-permute-start | bytes 774152 | tf_op jit(solution)/shard_map/ppermute | solution.py:698
  38.4 1.8 %collective-permute-start.11 = (f32[48,1152]{1,0:T(8,128)S(1)}, f32[48,1152]{1,0:T(8,128)S(1)}, u32[]{:S(2)}, u32[]{:S(2)}) collective-permute-start(f32[48,1152]{1,0:T(8,128)S(1)} %get-tuple-element.41.refs_0_.refs_8_), channel_id=1, source_target_pairs={{0,1},{1,0},{2,3},{3,2},{4,5},{5,4},{6,7},{7,6},{8,9},{9,8},{10,11... | collective-permute-start | bytes 663560 | tf_op jit(solution)/shard_map/ppermute | solution.py:698
  38.9 1.6 %collective-permute-start.12 = (f32[48,1152]{1,0:T(8,128)S(1)}, f32[48,1152]{1,0:T(8,128)S(1)}, u32[]{:S(2)}, u32[]{:S(2)}) collective-permute-start(f32[48,1152]{1,0:T(8,128)S(1)} %collective-permute-done.3.refs_1_.refs_10_), channel_id=1, source_target_pairs={{0,1},{1,0},{2,3},{3,2},{4,5},{5,4},{6,7},{7,6},{8,9},{9,8},{10,11... | collective-permute-start | bytes 663560 | tf_op jit(solution)/shard_map/ppermute | solution.py:698
  (2 other events, 8.3 us)

commit v20 on v19

--- a/solution.py
+++ b/solution.py
@@ -642,18 +642,18 @@
     )(own, edge, *arrived, *wait)
 
 
-def edge_kernel(thick_hbm, u_hbm, v_hbm, tracer_hbm, *refs):
+def edge_kernel(thick_any, u_any, v_any, tracer_any, *refs):
     last_ref, leading_ref, top_ref, low_ref, tracer_ref, sems = refs[-6:]
-    T, L, R, _ = tracer_hbm.shape
+    T, L, R, _ = tracer_any.shape
     top = pl.ds(R - 8, 8)
     copies = [
-        pltpu.make_async_copy(thick_hbm.at[:, top], top_ref.at[0], sems.at[0]),
-        pltpu.make_async_copy(v_hbm.at[:, top], top_ref.at[1], sems.at[1]),
-        pltpu.make_async_copy(thick_hbm.at[:, pl.ds(0, 8)], low_ref.at[0], sems.at[2]),
-        pltpu.make_async_copy(u_hbm.at[:, pl.ds(0, 8)], low_ref.at[1], sems.at[3]),
-        pltpu.make_async_copy(v_hbm.at[:, pl.ds(0, 8)], low_ref.at[2], sems.at[4]),
-        pltpu.make_async_copy(tracer_hbm.at[:, :, top], tracer_ref.at[0], sems.at[5]),
-        pltpu.make_async_copy(tracer_hbm.at[:, :, pl.ds(0, 8)], tracer_ref.at[1], sems.at[6]),
+        pltpu.make_async_copy(thick_any.at[:, top], top_ref.at[0], sems.at[0]),
+        pltpu.make_async_copy(v_any.at[:, top], top_ref.at[1], sems.at[1]),
+        pltpu.make_async_copy(thick_any.at[:, pl.ds(0, 8)], low_ref.at[0], sems.at[2]),
+        pltpu.make_async_copy(u_any.at[:, pl.ds(0, 8)], low_ref.at[1], sems.at[3]),
+        pltpu.make_async_copy(v_any.at[:, pl.ds(0, 8)], low_ref.at[2], sems.at[4]),
+        pltpu.make_async_copy(tracer_any.at[:, :, top], tracer_ref.at[0], sems.at[5]),
+        pltpu.make_async_copy(tracer_any.at[:, :, pl.ds(0, 8)], tracer_ref.at[1], sems.at[6]),
     ]
     for copy in copies:
         copy.start()
@@ -670,7 +670,7 @@
 def edge_rows(thickness, wind_u, wind_v, tracers, wait):
     L, R, N = thickness.shape
     T = tracers.shape[0]
-    operands = [pltpu.with_memory_space_constraint(a, pltpu.HBM) for a in (thickness, wind_u, wind_v, tracers)]
+    operands = [thickness, wind_u, wind_v, tracers]
     return pl.pallas_call(
         edge_kernel,
         in_specs=after(operands) + after(wait),
@@ -739,11 +739,11 @@
     arrived = sent(away_parts)
 
     last, leading = edge_rows(
-        thickness, wind_u, wind_v, tracers, [away_parts[0], *near[1:2]]
+        *arguments, [away_parts[0], *near[1:2]]
     )
     up = lax.ppermute(last, "lat", northward)
     down = lax.ppermute(leading, "lat", southward)
-    u, v, edge = second_step(table, lat_rows, thickness, wind_u, wind_v, tracers, up, down, cutoff)
+    u, v, edge = second_step(table, lat_rows, *arguments, up, down, cutoff)
     edges = [edge] + [send(edge, s=s, t=0) for s in away]
     winds = [with_others_of_chip(u), with_others_of_chip(v)]
     tracers_own, thick_inner = remap(group, [group], others, tracer_fields, (0,), (0, 0), with_thickness=True, wait=[edge])

time: 50.2 us -> 50.1 us (level)
  waiting for transfers between devices: 15.4 us -> 17.2 us
  Pallas kernels: 19.4 us -> 18 us
    ppermute x5, waiting for transfers between devices: 9.86 us -> 11.6 us  [shifted(): lax.ppermute(value, 'lev', [(i, (i + s) % lev_count) for i in range(lev_c...]
    pallas_call x1, Pallas kernels: 1.72 us -> 0.45 us  [edge_rows(): pl.pallas_call(edge_kernel, in_specs=after(operands) + after(wait), out_s...]
  transfers between devices with their start and end apart: 17 -> 17, of which waited for: 9 -> 9; matrix products, arithmetic and copies ran while one was open for 0% -> 0% of each run, Pallas kernels for 33% -> 30%
where the time goes in v20:
time: 50.1 us; the launch traced here: 50 us
  Pallas kernels  18 us (36%)
  waiting for transfers between devices  17.2 us (34%)
  starting transfers between devices  13.8 us (28%)
  between operations  0.83 us (2%)
    ppermute x5, waiting for transfers between devices, shifted(): lax.ppermute(value, 'lev', [(i, (i + s) % lev_count) for i in range(lev_c...  11.6 us
    ppermute x5, starting transfers between devices, shifted(): lax.ppermute(value, 'lev', [(i, (i + s) % lev_count) for i in range(lev_c...  6.12 us
    ppermute x1, starting transfers between devices, per_device(): up = lax.ppermute(last, 'lat', northward)  4.55 us
    pallas_call x3, Pallas kernels, remap_parts(): pl.pallas_call(functools.partial(remap_kernel, counts, tuple(steps), tupl...  4.45 us
    pallas_call x1, Pallas kernels, remap_edges(): pl.pallas_call(functools.partial(remap_edge_kernel, counts), in_specs=[VM...  3.7 us
    pallas_call x1, Pallas kernels, second_step(): pl.pallas_call(functools.partial(second_kernel, lat_rows), grid=(L,), in_...  3.54 us
    ppermute x10, waiting for transfers between devices, shifted(): lax.ppermute(value, 'sub', [(i, (i + t) % sub_count) for i in range(sub_c...  3.24 us
    ppermute x1, waiting for transfers between devices, per_device(): up = lax.ppermute(last, 'lat', northward)  2.3 us
  transfers between devices with their start and end apart: 17, of which 9 were waited for; matrix products, arithmetic and copies ran while one was open for 0% of the time, Pallas kernels for 30%

profile of v20, /device:TPU:0, one launch (start us, length us, event | category | flops | bytes accessed | tf_op | source)
XLA Modules:
  0.0 50.0 jit_solution(14652520006196426520)
XLA Ops:
  0.6 1.9 %first_step.1 = (f32[4,16,1152]{2,1,0:T(8,128)S(1)}, f32[234,128]{1,0:T(8,128)S(1)}, f32[1,4,3,1152]{3,2,1,0:T(4,128)S(1)}, f32[4,16,1152]{2,1,0:T(8,128)S(1)}, ...) custom-call(f32[4,24,128]{2,1,0:T(8,128)} %constant.6.clone.table_hbm.table_ref, ...), custom_call_target="tpu_custom_call" | custom-call | flops 2949120 | bytes 4423680 | tf_op jit(solution)/shard_map/first_step/pallas_call | solution.py:139
  2.5 3.0 %collective-permute-start.1 = (f32[234,128]{1,0:T(8,128)S(1)}, f32[234,128]{1,0:T(8,128)S(1)}, u32[]{:S(2)}, u32[]{:S(2)}) collective-permute-start(f32[234,128]{1,0:T(8,128)S(1)} %get-tuple-element.40), channel_id=1, source_target_pairs={{0,2},{2,0},{1,3},{3,1},{4,6},{6,4},{5,7},{7,5},{8,10},{10,8},{9,1... | collective-permute-start | bytes 359432 | tf_op jit(solution)/shard_map/ppermute | solution.py:696
  5.5 1.6 %inner_step.1 = (f32[5,4,16,1152]{3,2,1,0:T(8,128)S(1)}, f32[48,1152]{1,0:T(8,128)S(1)}) custom-call(f32[4,24,128]{2,1,0:T(8,128)S(1)} %copy-done.2, f32[4,16,1152]{2,1,0:T(8,128)S(1)} %get-tuple-element.34.new_ref, f32[4,16,1152]{2,1,0:T(8,128)S(1)} %get-tuple-element.35.thick_ref.thick_any, f32[4,16,1152]{2,1,0:T(8,128)S(1)} %get-tuple-element.36.u_ref.u_any, ...), custom_call_target="tpu_custom_call" | custom-call | flops 9584640 | bytes 4718592 | tf_op jit(solution)/shard_map/inner_step/pallas_call | solution.py:185
  7.4 1.5 %collective-permute-done.1.both_ref = f32[234,128]{1,0:T(8,128)S(1)} collective-permute-done((f32[234,128]{1,0:T(8,128)S(1)}, f32[234,128]{1,0:T(8,128)S(1)}, u32[]{:S(2)}, u32[]{:S(2)}) %collective-permute-start.1) | collective-permute-done | bytes 119840 | tf_op jit(solution)/shard_map/ppermute | solution.py:696
  9.0 1.6 %collective-permute-done.2.refs_1_ = f32[16,1152]{1,0:T(8,128)S(1)} collective-permute-done((f32[16,1152]{1,0:T(8,128)S(1)}, f32[16,1152]{1,0:T(8,128)S(1)}, u32[]{:S(2)}, u32[]{:S(2)}) %collective-permute-start.2) | collective-permute-done | bytes 73760 | tf_op jit(solution)/shard_map/ppermute | solution.py:698
  10.7 1.4 %remap_parts.3.refs_0_ = f32[176,1152]{1,0:T(8,128)S(1)} custom-call(f32[16,8,128]{2,1,0:T(8,128)S(1)} %broadcast_in_dim.4.weight_ref, f32[5,4,16,1152]{3,2,1,0:T(8,128)S(1)} %get-tuple-element.39.refs_0_.refs_2_, f32[5,4,16,1152]{3,2,1,0:T(8,128)S(1)} %collective-permute-done.refs_1_.refs_3_, f32[5,4,16,1152]{3,2,1,0:T(8,128)S(1)} %get-tuple-element.39.refs_0_.refs_2_, ...), custom_call_target="tpu_custom_call" | custom-call | flops 7667712 | bytes 4423680 | tf_op jit(solution)/shard_map/remap_parts/pallas_call | solution.py:519
  12.1 1.4 %collective-permute-start.15 = (f32[176,1152]{1,0:T(8,128)S(1)}, f32[176,1152]{1,0:T(8,128)S(1)}, u32[]{:S(2)}, u32[]{:S(2)}) collective-permute-start(f32[176,1152]{1,0:T(8,128)S(1)} %remap_parts.3.refs_0_), channel_id=1, source_target_pairs={{0,2},{2,0},{1,3},{3,1},{4,6},{6,4},{5,7},{7,5},{8,10},{10,8},{9,1... | collective-permute-start | bytes 2433032 | tf_op jit(solution)/shard_map/ppermute | solution.py:696
  13.6 1.6 %collective-permute-done.3.refs_1_.refs_10_ = f32[48,1152]{1,0:T(8,128)S(1)} collective-permute-done((f32[48,1152]{1,0:T(8,128)S(1)}, f32[48,1152]{1,0:T(8,128)S(1)}, u32[]{:S(2)}, u32[]{:S(2)}) %collective-permute-start.3) | collective-permute-done | bytes 221216 | tf_op jit(solution)/shard_map/ppermute | solution.py:696
  15.6 1.3 %collective-permute-start.5 = (f32[8,4,1,1152]{3,2,1,0:T(1,128)S(1)}, f32[8,4,1,1152]{3,2,1,0:T(1,128)S(1)}, u32[]{:S(2)}, u32[]{:S(2)}) collective-permute-start(f32[8,4,1,1152]{3,2,1,0:T(1,128)S(1)} %get-tuple-element.46), channel_id=1, source_target_pairs={{4,0},{8,4},{12,8},{5,1},{9,5},{13,9},{6,2},{10,6},{14,10},{7,3},{... | collective-permute-start | bytes 442376 | tf_op jit(solution)/shard_map/ppermute | solution.py:745
  16.9 4.6 %collective-permute-start.4 = (f32[6,4,1,1152]{3,2,1,0:T(1,128)S(1)}, f32[6,4,1,1152]{3,2,1,0:T(1,128)S(1)}, u32[]{:S(2)}, u32[]{:S(2)}) collective-permute-start(f32[6,4,1,1152]{3,2,1,0:T(1,128)S(1)} %get-tuple-element.45), channel_id=1, source_target_pairs={{0,4},{4,8},{8,12},{1,5},{5,9},{9,13},{2,6},{6,10},{10,14},{3,7},{... | collective-permute-start | bytes 331784 | tf_op jit(solution)/shard_map/ppermute | solution.py:744
  21.5 2.3 %collective-permute-done.4.up_ref = f32[6,4,1,1152]{3,2,1,0:T(1,128)S(1)} collective-permute-done((f32[6,4,1,1152]{3,2,1,0:T(1,128)S(1)}, f32[6,4,1,1152]{3,2,1,0:T(1,128)S(1)}, u32[]{:S(2)}, u32[]{:S(2)}) %collective-permute-start.4) | collective-permute-done | bytes 110624 | tf_op jit(solution)/shard_map/ppermute | solution.py:744
  23.9 3.5 %second_step.1 = (f32[1,4,16,1152]{3,2,1,0:T(8,128)S(1)}, f32[1,4,16,1152]{3,2,1,0:T(8,128)S(1)}, f32[7,4,2,1152]{3,2,1,0:T(2,128)S(1)}) custom-call(f32[4,24,128]{2,1,0:T(8,128)S(1)} %copy-done.2, f32[4,16,1152]{2,1,0:T(8,128)S(1)} %get-tuple-element.35.thick_ref.thick_any, f32[4,16,1152]{2,1,0:T(8,128)S(1)} %get-tuple-element.36.u_ref.u_any, ...), custom_call_target="tpu_custom_call" | custom-call | flops 503316480 | bytes 3538944 | tf_op jit(solution)/shard_map/second_step/pallas_call | solution.py:323
  28.2 1.3 %remap_parts.4 = (f32[4,4,16,1152]{3,2,1,0:T(8,128)S(1)}, f32[4,16,1152]{2,1,0:T(8,128)S(1)}) custom-call(f32[16,8,128]{2,1,0:T(8,128)S(1)} %broadcast_in_dim.4.weight_ref, f32[5,4,16,1152]{3,2,1,0:T(8,128)S(1)} %get-tuple-element.39.refs_0_.refs_2_, f32[5,4,16,1152]{3,2,1,0:T(8,128)S(1)} %collective-permute-done.refs_1_.refs_3_, ...), custom_call_target="tpu_custom_call" | custom-call | flops 7667712 | bytes 4423680 | tf_op jit(solution)/shard_map/remap_parts/pallas_call | solution.py:519
  29.5 3.6 %collective-permute-done.15.refs_9_.refs_0_ = f32[176,1152]{1,0:T(8,128)S(1)} collective-permute-done((f32[176,1152]{1,0:T(8,128)S(1)}, f32[176,1152]{1,0:T(8,128)S(1)}, u32[]{:S(2)}, u32[]{:S(2)}) %collective-permute-start.15) | collective-permute-done | bytes 811040 | tf_op jit(solution)/shard_map/ppermute | solution.py:696
  33.1 1.7 %remap_parts.5 = (f32[2,4,16,1152]{3,2,1,0:T(8,128)S(1)}, f32[112,1152]{1,0:T(8,128)S(1)}) custom-call(f32[16,8,128]{2,1,0:T(8,128)S(1)} %broadcast_in_dim.4.weight_ref, f32[5,4,16,1152]{3,2,1,0:T(8,128)S(1)} %get-tuple-element.39.refs_0_.refs_2_, f32[5,4,16,1152]{3,2,1,0:T(8,128)S(1)} %collective-permute-done.refs_1_.refs_3_, ...), custom_call_target="tpu_custom_call" | custom-call | flops 10616832 | bytes 3538944 | tf_op jit(solution)/shard_map/remap_parts/pallas_call | solution.py:519
  34.9 1.4 %collective-permute-start.16 = (f32[112,1152]{1,0:T(8,128)S(1)}, f32[112,1152]{1,0:T(8,128)S(1)}, u32[]{:S(2)}, u32[]{:S(2)}) collective-permute-start(f32[112,1152]{1,0:T(8,128)S(1)} %get-tuple-element.53.refs_12_), channel_id=1, source_target_pairs={{0,2},{2,0},{1,3},{3,1},{4,6},{6,4},{5,7},{7,5},{8,10},{10,8},{9,1... | collective-permute-start | bytes 1548296 | tf_op jit(solution)/shard_map/ppermute | solution.py:696
  36.3 0.5 %collective-permute-start.10 = (f32[1,4,3,1152]{3,2,1,0:T(4,128)S(1)}, f32[1,4,3,1152]{3,2,1,0:T(4,128)S(1)}, u32[]{:S(2)}, u32[]{:S(2)}) collective-permute-start(f32[1,4,3,1152]{3,2,1,0:T(4,128)S(1)} %get-tuple-element.50.refs_6_), channel_id=1, source_target_pairs={{0,1},{1,0},{2,3},{3,2},{4,5},{5,4},{6,7},{7,6},{8,9},{9,8},{10,11... | collective-permute-start | bytes 165896 | tf_op jit(solution)/shard_map/ppermute | solution.py:698
  36.8 1.8 %collective-permute-done.7.refs_2_ = f32[7,4,2,1152]{3,2,1,0:T(2,128)S(1)} collective-permute-done((f32[7,4,2,1152]{3,2,1,0:T(2,128)S(1)}, f32[7,4,2,1152]{3,2,1,0:T(2,128)S(1)}, u32[]{:S(2)}, u32[]{:S(2)}) %collective-permute-start.7) | collective-permute-done | bytes 258080 | tf_op jit(solution)/shard_map/ppermute | solution.py:696
  38.7 0.5 %collective-permute-start.11 = (f32[48,1152]{1,0:T(8,128)S(1)}, f32[48,1152]{1,0:T(8,128)S(1)}, u32[]{:S(2)}, u32[]{:S(2)}) collective-permute-start(f32[48,1152]{1,0:T(8,128)S(1)} %get-tuple-element.41.refs_0_.refs_8_), channel_id=1, source_target_pairs={{0,1},{1,0},{2,3},{3,2},{4,5},{5,4},{6,7},{7,6},{8,9},{9,8},{10,11... | collective-permute-start | bytes 663560 | tf_op jit(solution)/shard_map/ppermute | solution.py:698
  39.2 1.3 %collective-permute-done.11.refs_9_ = f32[48,1152]{1,0:T(8,128)S(1)} collective-permute-done((f32[48,1152]{1,0:T(8,128)S(1)}, f32[48,1152]{1,0:T(8,128)S(1)}, u32[]{:S(2)}, u32[]{:S(2)}) %collective-permute-start.11) | collective-permute-done | bytes 221216 | tf_op jit(solution)/shard_map/ppermute | solution.py:698
  40.8 3.7 %remap_edges.1 = (f32[6,4,2,1152]{3,2,1,0:T(2,128)S(1)}, f32[4,2,1152]{2,1,0:T(2,128)S(1)}, f32[4,4,3,1152]{3,2,1,0:T(4,128)S(1)}) custom-call(f32[16,8,128]{2,1,0:T(8,128)S(1)} %broadcast_in_dim.4.weight_ref, f32[7,4,2,1152]{3,2,1,0:T(2,128)S(1)} %get-tuple-element.47.refs_6_.refs_0_, f32[7,4,2,1152]{3,2,1,0:T(2,128)S(1)} %collective-permute-done.6.refs_1_, ...), custom_call_target="tpu_custom_call" | custom-call | flops 5898240 | bytes 3096576 | tf_op jit(solution)/shard_map/remap_edges/pallas_call | solution.py:557
  44.5 1.4 %finish_tracers.1 = (f32[4,4,16,1152]{3,2,1,0:T(8,128)}, f32[4,16,1152]{2,1,0:T(8,128)}, f32[8,128]{1,0:T(8,128)S(1)}) custom-call(f32[4,4,16,1152]{3,2,1,0:T(8,128)S(1)} %get-tuple-element.48.refs_8_.own_ref, f32[4,4,3,1152]{3,2,1,0:T(4,128)S(1)} %get-tuple-element.54.near_ref, f32[6,4,2,1152]{3,2,1,0:T(2,128)S(1)} %get-tuple-element.55.edge_ref, ...), custom_call_target="tpu_custom_call" | custom-call | flops 589824 | bytes 3538944 | tf_op jit(solution)/shard_map/finish_tracers/pallas_call | solution.py:595
  46.0 3.1 %collective-permute-done.16.refs_0_ = f32[112,1152]{1,0:T(8,128)S(1)} collective-permute-done((f32[112,1152]{1,0:T(8,128)S(1)}, f32[112,1152]{1,0:T(8,128)S(1)}, u32[]{:S(2)}, u32[]{:S(2)}) %collective-permute-start.16) | collective-permute-done | bytes 516128 | tf_op jit(solution)/shard_map/ppermute | solution.py:696
  49.1 0.9 %finish_winds.1 = (f32[4,16,1152]{2,1,0:T(8,128)}, f32[4,16,1152]{2,1,0:T(8,128)}) custom-call(f32[2,4,16,1152]{3,2,1,0:T(8,128)S(1)} %get-tuple-element.59.own_ref, f32[6,4,2,1152]{3,2,1,0:T(2,128)S(1)} %get-tuple-element.55.edge_ref, f32[112,1152]{1,0:T(8,128)S(1)} %collective-permute-done.16.refs_0_, f32[8,128]{1,0:T(8,128)S(1)} %get-tuple-element.60.refs_1_), custom_call_target="tpu_custom_call" | custom-call | flops 147456 | bytes 1769472 | tf_op jit(solution)/shard_map/finish_winds/pallas_call | solution.py:633
  (34 shorter events, 2.1 us)
Async XLA Ops:
  0.6 4.9 %copy-start.2 = (f32[4,24,128]{2,1,0:T(8,128)S(1)}, f32[4,24,128]{2,1,0:T(8,128)}, u32[]{:S(2)}) copy-start(f32[4,24,128]{2,1,0:T(8,128)} %constant.6.clone.table_hbm.table_ref) | copy-start | bytes 147460
  2.5 6.3 %collective-permute-start.1 = (f32[234,128]{1,0:T(8,128)S(1)}, f32[234,128]{1,0:T(8,128)S(1)}, u32[]{:S(2)}, u32[]{:S(2)}) collective-permute-start(f32[234,128]{1,0:T(8,128)S(1)} %get-tuple-element.40), channel_id=1, source_target_pairs={{0,2},{2,0},{1,3},{3,1},{4,6},{6,4},{5,7},{7,5},{8,10},{10,8},{9,1... | collective-permute-start | bytes 359432 | tf_op jit(solution)/shard_map/ppermute | solution.py:696
  7.2 3.5 %collective-permute-start = (f32[5,4,16,1152]{3,2,1,0:T(8,128)S(1)}, f32[5,4,16,1152]{3,2,1,0:T(8,128)S(1)}, u32[]{:S(2)}, u32[]{:S(2)}) collective-permute-start(f32[5,4,16,1152]{3,2,1,0:T(8,128)S(1)} %get-tuple-element.39.refs_0_.refs_2_), channel_id=1, source_target_pairs={{0,1},{1,0},{2,3},{3,2},{4,5},{5,4},{6,7},{7,6},{8,9},{9,8},{10,11... | collective-permute-start | bytes 4423688 | tf_op jit(solution)/shard_map/ppermute | solution.py:698
  7.2 3.4 %copy-start.3 = (f32[16]{0:T(128)S(1)}, f32[16]{0:T(128)}, u32[]{:S(2)}) copy-start(f32[16]{0:T(128)} %param.13) | copy-start | bytes 196
  7.3 7.9 %collective-permute-start.3 = (f32[48,1152]{1,0:T(8,128)S(1)}, f32[48,1152]{1,0:T(8,128)S(1)}, u32[]{:S(2)}, u32[]{:S(2)}) collective-permute-start(f32[48,1152]{1,0:T(8,128)S(1)} %get-tuple-element.41.refs_0_.refs_8_), channel_id=1, source_target_pairs={{0,2},{2,0},{1,3},{3,1},{4,6},{6,4},{5,7},{7,5},{8,10},{10,8},{9,1... | collective-permute-start | bytes 663560 | tf_op jit(solution)/shard_map/ppermute | solution.py:696
  8.9 1.7 %collective-permute-start.2 = (f32[16,1152]{1,0:T(8,128)S(1)}, f32[16,1152]{1,0:T(8,128)S(1)}, u32[]{:S(2)}, u32[]{:S(2)}) collective-permute-start(f32[16,1152]{1,0:T(8,128)S(1)} %get-tuple-element.42.refs_0_), channel_id=1, source_target_pairs={{0,1},{1,0},{2,3},{3,2},{4,5},{5,4},{6,7},{7,6},{8,9},{9,8},{10,11... | collective-permute-start | bytes 221192 | tf_op jit(solution)/shard_map/ppermute | solution.py:698
  12.1 11.7 %copy-start.4 = (s32[16]{0:T(128)S(1)}, s32[16]{0:T(128)}, u32[]{:S(2)}) copy-start(s32[16]{0:T(128)} %param.14) | copy-start | bytes 196
  12.1 11.7 %copy-start = (bf16[5,256,256]{2,1,0:T(8,128)(2,1)S(1)}, bf16[5,256,256]{2,1,0:T(8,128)(2,1)}, u32[]{:S(2)}) copy-start(bf16[5,256,256]{2,1,0:T(8,128)(2,1)} %constant.7.clone.high_ref) | copy-start | bytes 1966084
  12.1 11.7 %copy-start.1 = (bf16[5,256,256]{2,1,0:T(8,128)(2,1)S(1)}, bf16[5,256,256]{2,1,0:T(8,128)(2,1)}, u32[]{:S(2)}) copy-start(bf16[5,256,256]{2,1,0:T(8,128)(2,1)} %constant.8.clone.low_ref) | copy-start | bytes 1966084
  12.1 21.0 %collective-permute-start.15 = (f32[176,1152]{1,0:T(8,128)S(1)}, f32[176,1152]{1,0:T(8,128)S(1)}, u32[]{:S(2)}, u32[]{:S(2)}) collective-permute-start(f32[176,1152]{1,0:T(8,128)S(1)} %remap_parts.3.refs_0_), channel_id=1, source_target_pairs={{0,2},{2,0},{1,3},{3,1},{4,6},{6,4},{5,7},{7,5},{8,10},{10,8},{9,1... | collective-permute-start | bytes 2433032 | tf_op jit(solution)/shard_map/ppermute | solution.py:696
  15.6 8.2 %collective-permute-start.5 = (f32[8,4,1,1152]{3,2,1,0:T(1,128)S(1)}, f32[8,4,1,1152]{3,2,1,0:T(1,128)S(1)}, u32[]{:S(2)}, u32[]{:S(2)}) collective-permute-start(f32[8,4,1,1152]{3,2,1,0:T(1,128)S(1)} %get-tuple-element.46), channel_id=1, source_target_pairs={{4,0},{8,4},{12,8},{5,1},{9,5},{13,9},{6,2},{10,6},{14,10},{7,3},{... | collective-permute-start | bytes 442376 | tf_op jit(solution)/shard_map/ppermute | solution.py:745
  16.9 6.9 %collective-permute-start.4 = (f32[6,4,1,1152]{3,2,1,0:T(1,128)S(1)}, f32[6,4,1,1152]{3,2,1,0:T(1,128)S(1)}, u32[]{:S(2)}, u32[]{:S(2)}) collective-permute-start(f32[6,4,1,1152]{3,2,1,0:T(1,128)S(1)} %get-tuple-element.45), channel_id=1, source_target_pairs={{0,4},{4,8},{8,12},{1,5},{5,9},{9,13},{2,6},{6,10},{10,14},{3,7},{... | collective-permute-start | bytes 331784 | tf_op jit(solution)/shard_map/ppermute | solution.py:744
  27.4 2.1 %collective-permute-start.13 = (f32[1,4,16,1152]{3,2,1,0:T(8,128)S(1)}, f32[1,4,16,1152]{3,2,1,0:T(8,128)S(1)}, u32[]{:S(2)}, u32[]{:S(2)}) collective-permute-start(f32[1,4,16,1152]{3,2,1,0:T(8,128)S(1)} %get-tuple-element.51.refs_2_), channel_id=1, source_target_pairs={{0,1},{1,0},{2,3},{3,2},{4,5},{5,4},{6,7},{7,6},{8,9},{9,8},{10,11... | collective-permute-start | bytes 884744 | tf_op jit(solution)/shard_map/ppermute | solution.py:698
  27.5 2.0 %collective-permute-start.14 = (f32[1,4,16,1152]{3,2,1,0:T(8,128)S(1)}, f32[1,4,16,1152]{3,2,1,0:T(8,128)S(1)}, u32[]{:S(2)}, u32[]{:S(2)}) collective-permute-start(f32[1,4,16,1152]{3,2,1,0:T(8,128)S(1)} %get-tuple-element.52.refs_4_), channel_id=1, source_target_pairs={{0,1},{1,0},{2,3},{3,2},{4,5},{5,4},{6,7},{7,6},{8,9},{9,8},{10,11... | collective-permute-start | bytes 884744 | tf_op jit(solution)/shard_map/ppermute | solution.py:698
  28.0 10.7 %collective-permute-start.7 = (f32[7,4,2,1152]{3,2,1,0:T(2,128)S(1)}, f32[7,4,2,1152]{3,2,1,0:T(2,128)S(1)}, u32[]{:S(2)}, u32[]{:S(2)}) collective-permute-start(f32[7,4,2,1152]{3,2,1,0:T(2,128)S(1)} %get-tuple-element.47.refs_6_.refs_0_), channel_id=1, source_target_pairs={{0,2},{2,0},{1,3},{3,1},{4,6},{6,4},{5,7},{7,5},{8,10},{10,8},{9,1... | collective-permute-start | bytes 774152 | tf_op jit(solution)/shard_map/ppermute | solution.py:696
  34.9 14.2 %collective-permute-start.16 = (f32[112,1152]{1,0:T(8,128)S(1)}, f32[112,1152]{1,0:T(8,128)S(1)}, u32[]{:S(2)}, u32[]{:S(2)}) collective-permute-start(f32[112,1152]{1,0:T(8,128)S(1)} %get-tuple-element.53.refs_12_), channel_id=1, source_target_pairs={{0,2},{2,0},{1,3},{3,1},{4,6},{6,4},{5,7},{7,5},{8,10},{10,8},{9,1... | collective-permute-start | bytes 1548296 | tf_op jit(solution)/shard_map/ppermute | solution.py:696
  36.3 2.4 %collective-permute-start.9 = (f32[1,4,3,1152]{3,2,1,0:T(4,128)S(1)}, f32[1,4,3,1152]{3,2,1,0:T(4,128)S(1)}, u32[]{:S(2)}, u32[]{:S(2)}) collective-permute-start(f32[1,4,3,1152]{3,2,1,0:T(4,128)S(1)} %get-tuple-element.49.refs_4_), channel_id=1, source_target_pairs={{0,1},{1,0},{2,3},{3,2},{4,5},{5,4},{6,7},{7,6},{8,9},{9,8},{10,11... | collective-permute-start | bytes 165896 | tf_op jit(solution)/shard_map/ppermute | solution.py:698
  36.3 2.9 %collective-permute-start.10 = (f32[1,4,3,1152]{3,2,1,0:T(4,128)S(1)}, f32[1,4,3,1152]{3,2,1,0:T(4,128)S(1)}, u32[]{:S(2)}, u32[]{:S(2)}) collective-permute-start(f32[1,4,3,1152]{3,2,1,0:T(4,128)S(1)} %get-tuple-element.50.refs_6_), channel_id=1, source_target_pairs={{0,1},{1,0},{2,3},{3,2},{4,5},{5,4},{6,7},{7,6},{8,9},{9,8},{10,11... | collective-permute-start | bytes 165896 | tf_op jit(solution)/shard_map/ppermute | solution.py:698
  36.8 4.0 %collective-permute-start.6 = (f32[7,4,2,1152]{3,2,1,0:T(2,128)S(1)}, f32[7,4,2,1152]{3,2,1,0:T(2,128)S(1)}, u32[]{:S(2)}, u32[]{:S(2)}) collective-permute-start(f32[7,4,2,1152]{3,2,1,0:T(2,128)S(1)} %get-tuple-element.47.refs_6_.refs_0_), channel_id=1, source_target_pairs={{0,1},{1,0},{2,3},{3,2},{4,5},{5,4},{6,7},{7,6},{8,9},{9,8},{10,11... | collective-permute-start | bytes 774152 | tf_op jit(solution)/shard_map/ppermute | solution.py:698
  38.7 2.2 %collective-permute-start.8 = (f32[7,4,2,1152]{3,2,1,0:T(2,128)S(1)}, f32[7,4,2,1152]{3,2,1,0:T(2,128)S(1)}, u32[]{:S(2)}, u32[]{:S(2)}) collective-permute-start(f32[7,4,2,1152]{3,2,1,0:T(2,128)S(1)} %collective-permute-done.7.refs_2_), channel_id=1, source_target_pairs={{0,1},{1,0},{2,3},{3,2},{4,5},{5,4},{6,7},{7,6},{8,9},{9,8},{10,11... | collective-permute-start | bytes 774152 | tf_op jit(solution)/shard_map/ppermute | solution.py:698
  38.7 1.8 %collective-permute-start.11 = (f32[48,1152]{1,0:T(8,128)S(1)}, f32[48,1152]{1,0:T(8,128)S(1)}, u32[]{:S(2)}, u32[]{:S(2)}) collective-permute-start(f32[48,1152]{1,0:T(8,128)S(1)} %get-tuple-element.41.refs_0_.refs_8_), channel_id=1, source_target_pairs={{0,1},{1,0},{2,3},{3,2},{4,5},{5,4},{6,7},{7,6},{8,9},{9,8},{10,11... | collective-permute-start | bytes 663560 | tf_op jit(solution)/shard_map/ppermute | solution.py:698
  39.2 1.6 %collective-permute-start.12 = (f32[48,1152]{1,0:T(8,128)S(1)}, f32[48,1152]{1,0:T(8,128)S(1)}, u32[]{:S(2)}, u32[]{:S(2)}) collective-permute-start(f32[48,1152]{1,0:T(8,128)S(1)} %collective-permute-done.3.refs_1_.refs_10_), channel_id=1, source_target_pairs={{0,1},{1,0},{2,3},{3,2},{4,5},{5,4},{6,7},{7,6},{8,9},{9,8},{10,11... | collective-permute-start | bytes 663560 | tf_op jit(solution)/shard_map/ppermute | solution.py:698

commit v21 on v20

--- a/solution.py
+++ b/solution.py
@@ -90,7 +90,7 @@
 
 
 def first_kernel(table_hbm, thick_hbm, u_hbm, v_hbm, tracer_hbm, *refs):
-    new_ref, both_ref, near_ref, thick_ref, u_ref, v_ref, tracer_ref, sum_ref, geo_ref, sems = refs
+    new_ref, both_ref, near_ref, east_ref, north_ref, thick_ref, u_ref, v_ref, tracer_ref, sum_ref, geo_ref, sems = refs
     L, rows, _ = thick_ref.shape
     near, _ = near_rows(rows)
     table_copy = pltpu.make_async_copy(table_hbm.at[lax.axis_index("lat")], geo_ref, sems.at[3, 0])
@@ -116,6 +116,8 @@
         east, north, _ = fluxes(geo, thick, u, v, None, None, None)
         new = thick - (east - west_of(east)) - (north - south_of(north, None)) * geo[0:rows, 2:3]
         new_ref[k] = new
+        east_ref[k] = east
+        north_ref[k] = north
         for j, row in enumerate(near):
             near_ref[0, k, j : j + 1] = new[row : row + 1]
         sum_ref[...] += new
@@ -135,7 +137,7 @@
     arguments = (thickness, wind_u, wind_v, tracers)
     operands = [pltpu.with_memory_space_constraint(a, pltpu.HBM) for a in (table, *arguments)]
     near = len(near_rows(R)[0])
-    shapes = [(L, R, N), ((R - 2 + L * near) * N // LANES, LANES), (1, L, near, N)] + [a.shape for a in arguments]
+    shapes = [(L, R, N), ((R - 2 + L * near) * N // LANES, LANES), (1, L, near, N), (L, R, N), (L, R, N)] + [a.shape for a in arguments]
     return pl.pallas_call(
         first_kernel,
         in_specs=after(operands),
@@ -152,7 +154,7 @@
     )(*operands)
 
 
-def inner_kernel(table_ref, new_ref, thick_ref, u_ref, v_ref, tracer_ref, out_ref, near_ref):
+def inner_kernel(table_ref, new_ref, east_ref, north_ref, thick_ref, u_ref, v_ref, tracer_ref, out_ref, near_ref):
     T, L, rows, _ = tracer_ref.shape
     near, _ = near_rows(rows)
     geo = table_ref[lax.axis_index("lat")]
@@ -160,7 +162,7 @@
 
     def level(k, carry):
         thick, u, v, new = thick_ref[k], u_ref[k], v_ref[k], new_ref[k]
-        east, north, _ = fluxes(geo, thick, u, v, None, None, None)
+        east, north = east_ref[k], north_ref[k]
 
         out_ref[0, k] = new
         scale = 1.0 / new
@@ -177,20 +179,20 @@
     lax.fori_loop(0, L, level, 0)
 
 
-def inner_step(table, new, thickness, wind_u, wind_v, tracers):
+def inner_step(table, new, east, north, thickness, wind_u, wind_v, tracers):
     L, R, N = thickness.shape
     T = tracers.shape[0]
     rows = jax.ShapeDtypeStruct((T * L * len(near_rows(R)[0]), N), jnp.float32)
     shape = lambda n, rows: jax.ShapeDtypeStruct((n, L, rows, N), jnp.float32)
     return pl.pallas_call(
         inner_kernel,
-        in_specs=[VMEM] * 6,
+        in_specs=[VMEM] * 8,
         out_specs=[VMEM] * 2,
         out_shape=[shape(1 + T, R), rows],
         compiler_params=params(),
         cost_estimate=cost(130 * L * R * N, 4 * L * R * N * (8 + 2 * T)),
         name="inner_step",
-    )(table, new, thickness, wind_u, wind_v, tracers)
+    )(table, new, east, north, thickness, wind_u, wind_v, tracers)
 
 
 def filter_tables(N):
@@ -726,9 +728,9 @@
 
     remap = functools.partial(remap_parts, (C, S), weights)
 
-    new, both, near_new, *arguments = first_step(table, thickness, wind_u, wind_v, tracers)
+    new, both, near_new, east, north, *arguments = first_step(table, thickness, wind_u, wind_v, tracers)
     both = [send(both, s=s, t=0) for s in away]
-    inner, near = inner_step(table, new, *arguments)
+    inner, near = inner_step(table, new, east, north, *arguments)
     group = with_others_of_chip(inner)
     near = [near] + [send(near, s=s, t=0) for s in away]
     parted = [part(each, (L, R, N), [near[0]]) for each in both]

time: 50.1 us -> 49.9 us (level)
  starting transfers between devices: 13.8 us -> 15.3 us
  waiting for transfers between devices: 17.2 us -> 15.7 us
    ppermute x5, starting transfers between devices: 6.12 us -> 7.62 us  [shifted(): lax.ppermute(value, 'lev', [(i, (i + s) % lev_count) for i in range(lev_c...]
    ppermute x5, waiting for transfers between devices: 11.6 us -> 10.4 us  [shifted(): lax.ppermute(value, 'lev', [(i, (i + s) % lev_count) for i in range(lev_c...]
where the time goes in v21:
time: 49.9 us; the launch traced here: 49.7 us
  Pallas kernels  17.8 us (36%)
  waiting for transfers between devices  15.7 us (31%)
  starting transfers between devices  15.3 us (31%)
  between operations  0.82 us (2%)
    ppermute x5, waiting for transfers between devices, shifted(): lax.ppermute(value, 'lev', [(i, (i + s) % lev_count) for i in range(lev_c...  10.4 us
    ppermute x5, starting transfers between devices, shifted(): lax.ppermute(value, 'lev', [(i, (i + s) % lev_count) for i in range(lev_c...  7.62 us
    ppermute x1, starting transfers between devices, per_device(): up = lax.ppermute(last, 'lat', northward)  4.55 us
    pallas_call x3, Pallas kernels, remap_parts(): pl.pallas_call(functools.partial(remap_kernel, counts, tuple(steps), tupl...  4.48 us
    pallas_call x1, Pallas kernels, remap_edges(): pl.pallas_call(functools.partial(remap_edge_kernel, counts), in_specs=[VM...  3.71 us
    pallas_call x1, Pallas kernels, second_step(): pl.pallas_call(functools.partial(second_kernel, lat_rows), grid=(L,), in_...  3.58 us
    ppermute x10, waiting for transfers between devices, shifted(): lax.ppermute(value, 'sub', [(i, (i + t) % sub_count) for i in range(sub_c...  2.93 us
    ppermute x1, waiting for transfers between devices, per_device(): up = lax.ppermute(last, 'lat', northward)  2.3 us
  transfers between devices with their start and end apart: 17, of which 9 were waited for; matrix products, arithmetic and copies ran while one was open for 0% of the time, Pallas kernels for 30%

profile of v21, /device:TPU:0, one launch (start us, length us, event | category | flops | bytes accessed | tf_op | source)
XLA Modules:
  0.0 49.7 jit_solution(5861117249420500100)
XLA Ops:
  0.6 1.9 %first_step.1 = (f32[4,16,1152]{2,1,0:T(8,128)S(1)}, f32[234,128]{1,0:T(8,128)S(1)}, f32[1,4,3,1152]{3,2,1,0:T(4,128)S(1)}, f32[4,16,1152]{2,1,0:T(8,128)S(1)}, ...) custom-call(f32[4,24,128]{2,1,0:T(8,128)} %constant.6.clone.table_hb, ...), custom_call_target="tpu_custom_call" | custom-call | flops 2949120 | bytes 4423680 | tf_op jit(solution)/shard_map/first_step/pallas_call | solution.py:141
  2.5 3.0 %collective-permute-start.1 = (f32[234,128]{1,0:T(8,128)S(1)}, f32[234,128]{1,0:T(8,128)S(1)}, u32[]{:S(2)}, u32[]{:S(2)}) collective-permute-start(f32[234,128]{1,0:T(8,128)S(1)} %get-tuple-element.44), channel_id=1, source_target_pairs={{0,2},{2,0},{1,3},{3,1},{4,6},{6,4},{5,7},{7,5},{8,10},{10,8},{9,1... | collective-permute-start | bytes 359432 | tf_op jit(solution)/shard_map/ppermute | solution.py:698
  5.5 1.3 %inner_step.1 = (f32[5,4,16,1152]{3,2,1,0:T(8,128)S(1)}, f32[48,1152]{1,0:T(8,128)S(1)}) custom-call(f32[4,24,128]{2,1,0:T(8,128)S(1)} %copy-done.2, f32[4,16,1152]{2,1,0:T(8,128)S(1)} %get-tuple-element.36.new_ref, f32[4,16,1152]{2,1,0:T(8,128)S(1)} %get-tuple-element.37.east_ref, f32[4,16,1152]{2,1,0:T(8,128)S(1)} %get-tuple-element.38.north_ref, ...), custom_call_target="tpu_custom_call" | custom-call | flops 9584640 | bytes 4718592 | tf_op jit(solution)/shard_map/inner_step/pallas_call | solution.py:187
  7.1 1.8 %collective-permute-done.1.both_ref = f32[234,128]{1,0:T(8,128)S(1)} collective-permute-done((f32[234,128]{1,0:T(8,128)S(1)}, f32[234,128]{1,0:T(8,128)S(1)}, u32[]{:S(2)}, u32[]{:S(2)}) %collective-permute-start.1) | collective-permute-done | bytes 119840 | tf_op jit(solution)/shard_map/ppermute | solution.py:698
  9.0 1.3 %collective-permute-done.2.refs_1_ = f32[16,1152]{1,0:T(8,128)S(1)} collective-permute-done((f32[16,1152]{1,0:T(8,128)S(1)}, f32[16,1152]{1,0:T(8,128)S(1)}, u32[]{:S(2)}, u32[]{:S(2)}) %collective-permute-start.2) | collective-permute-done | bytes 73760 | tf_op jit(solution)/shard_map/ppermute | solution.py:700
  10.4 1.4 %remap_parts.3.refs_0_ = f32[176,1152]{1,0:T(8,128)S(1)} custom-call(f32[16,8,128]{2,1,0:T(8,128)S(1)} %broadcast_in_dim.4.weight_ref, f32[5,4,16,1152]{3,2,1,0:T(8,128)S(1)} %get-tuple-element.43.refs_0_.refs_2_, f32[5,4,16,1152]{3,2,1,0:T(8,128)S(1)} %collective-permute-done.refs_1_.refs_3_, f32[5,4,16,1152]{3,2,1,0:T(8,128)S(1)} %get-tuple-element.43.refs_0_.refs_2_, ...), custom_call_target="tpu_custom_call" | custom-call | flops 7667712 | bytes 4423680 | tf_op jit(solution)/shard_map/remap_parts/pallas_call | solution.py:521
  11.9 2.0 %collective-permute-start.15 = (f32[176,1152]{1,0:T(8,128)S(1)}, f32[176,1152]{1,0:T(8,128)S(1)}, u32[]{:S(2)}, u32[]{:S(2)}) collective-permute-start(f32[176,1152]{1,0:T(8,128)S(1)} %remap_parts.3.refs_0_), channel_id=1, source_target_pairs={{0,2},{2,0},{1,3},{3,1},{4,6},{6,4},{5,7},{7,5},{8,10},{10,8},{9,1... | collective-permute-start | bytes 2433032 | tf_op jit(solution)/shard_map/ppermute | solution.py:698
  13.8 1.0 %collective-permute-done.3.refs_1_.refs_10_ = f32[48,1152]{1,0:T(8,128)S(1)} collective-permute-done((f32[48,1152]{1,0:T(8,128)S(1)}, f32[48,1152]{1,0:T(8,128)S(1)}, u32[]{:S(2)}, u32[]{:S(2)}) %collective-permute-start.3) | collective-permute-done | bytes 221216 | tf_op jit(solution)/shard_map/ppermute | solution.py:698
  15.2 1.3 %collective-permute-start.5 = (f32[8,4,1,1152]{3,2,1,0:T(1,128)S(1)}, f32[8,4,1,1152]{3,2,1,0:T(1,128)S(1)}, u32[]{:S(2)}, u32[]{:S(2)}) collective-permute-start(f32[8,4,1,1152]{3,2,1,0:T(1,128)S(1)} %get-tuple-element.50), channel_id=1, source_target_pairs={{4,0},{8,4},{12,8},{5,1},{9,5},{13,9},{6,2},{10,6},{14,10},{7,3},{... | collective-permute-start | bytes 442376 | tf_op jit(solution)/shard_map/ppermute | solution.py:747
  16.5 4.6 %collective-permute-start.4 = (f32[6,4,1,1152]{3,2,1,0:T(1,128)S(1)}, f32[6,4,1,1152]{3,2,1,0:T(1,128)S(1)}, u32[]{:S(2)}, u32[]{:S(2)}) collective-permute-start(f32[6,4,1,1152]{3,2,1,0:T(1,128)S(1)} %get-tuple-element.49), channel_id=1, source_target_pairs={{0,4},{4,8},{8,12},{1,5},{5,9},{9,13},{2,6},{6,10},{10,14},{3,7},{... | collective-permute-start | bytes 331784 | tf_op jit(solution)/shard_map/ppermute | solution.py:746
  21.1 2.3 %collective-permute-done.4.up_ref = f32[6,4,1,1152]{3,2,1,0:T(1,128)S(1)} collective-permute-done((f32[6,4,1,1152]{3,2,1,0:T(1,128)S(1)}, f32[6,4,1,1152]{3,2,1,0:T(1,128)S(1)}, u32[]{:S(2)}, u32[]{:S(2)}) %collective-permute-start.4) | collective-permute-done | bytes 110624 | tf_op jit(solution)/shard_map/ppermute | solution.py:746
  23.5 3.6 %second_step.1 = (f32[1,4,16,1152]{3,2,1,0:T(8,128)S(1)}, f32[1,4,16,1152]{3,2,1,0:T(8,128)S(1)}, f32[7,4,2,1152]{3,2,1,0:T(2,128)S(1)}) custom-call(f32[4,24,128]{2,1,0:T(8,128)S(1)} %copy-done.2, f32[4,16,1152]{2,1,0:T(8,128)S(1)} %get-tuple-element.39.thick_ref.thick_any, f32[4,16,1152]{2,1,0:T(8,128)S(1)} %get-tuple-element.40.u_ref.u_any, ...), custom_call_target="tpu_custom_call" | custom-call | flops 503316480 | bytes 3538944 | tf_op jit(solution)/shard_map/second_step/pallas_call | solution.py:325
  27.7 0.6 %collective-permute-start.7 = (f32[7,4,2,1152]{3,2,1,0:T(2,128)S(1)}, f32[7,4,2,1152]{3,2,1,0:T(2,128)S(1)}, u32[]{:S(2)}, u32[]{:S(2)}) collective-permute-start(f32[7,4,2,1152]{3,2,1,0:T(2,128)S(1)} %get-tuple-element.51.refs_6_.refs_0_), channel_id=1, source_target_pairs={{0,2},{2,0},{1,3},{3,1},{4,6},{6,4},{5,7},{7,5},{8,10},{10,8},{9,1... | collective-permute-start | bytes 774152 | tf_op jit(solution)/shard_map/ppermute | solution.py:698
  28.2 1.3 %remap_parts.4 = (f32[4,4,16,1152]{3,2,1,0:T(8,128)S(1)}, f32[4,16,1152]{2,1,0:T(8,128)S(1)}) custom-call(f32[16,8,128]{2,1,0:T(8,128)S(1)} %broadcast_in_dim.4.weight_ref, f32[5,4,16,1152]{3,2,1,0:T(8,128)S(1)} %get-tuple-element.43.refs_0_.refs_2_, f32[5,4,16,1152]{3,2,1,0:T(8,128)S(1)} %collective-permute-done.refs_1_.refs_3_, ...), custom_call_target="tpu_custom_call" | custom-call | flops 7667712 | bytes 4423680 | tf_op jit(solution)/shard_map/remap_parts/pallas_call | solution.py:521
  29.6 3.2 %collective-permute-done.15.refs_9_.refs_0_ = f32[176,1152]{1,0:T(8,128)S(1)} collective-permute-done((f32[176,1152]{1,0:T(8,128)S(1)}, f32[176,1152]{1,0:T(8,128)S(1)}, u32[]{:S(2)}, u32[]{:S(2)}) %collective-permute-start.15) | collective-permute-done | bytes 811040 | tf_op jit(solution)/shard_map/ppermute | solution.py:698
  32.8 1.8 %remap_parts.5 = (f32[2,4,16,1152]{3,2,1,0:T(8,128)S(1)}, f32[112,1152]{1,0:T(8,128)S(1)}) custom-call(f32[16,8,128]{2,1,0:T(8,128)S(1)} %broadcast_in_dim.4.weight_ref, f32[5,4,16,1152]{3,2,1,0:T(8,128)S(1)} %get-tuple-element.43.refs_0_.refs_2_, f32[5,4,16,1152]{3,2,1,0:T(8,128)S(1)} %collective-permute-done.refs_1_.refs_3_, ...), custom_call_target="tpu_custom_call" | custom-call | flops 10616832 | bytes 3538944 | tf_op jit(solution)/shard_map/remap_parts/pallas_call | solution.py:521
  34.6 2.0 %collective-permute-start.16 = (f32[112,1152]{1,0:T(8,128)S(1)}, f32[112,1152]{1,0:T(8,128)S(1)}, u32[]{:S(2)}, u32[]{:S(2)}) collective-permute-start(f32[112,1152]{1,0:T(8,128)S(1)} %get-tuple-element.57.refs_12_), channel_id=1, source_target_pairs={{0,2},{2,0},{1,3},{3,1},{4,6},{6,4},{5,7},{7,5},{8,10},{10,8},{9,1... | collective-permute-start | bytes 1548296 | tf_op jit(solution)/shard_map/ppermute | solution.py:698
  37.1 1.3 %collective-permute-done.7.refs_2_ = f32[7,4,2,1152]{3,2,1,0:T(2,128)S(1)} collective-permute-done((f32[7,4,2,1152]{3,2,1,0:T(2,128)S(1)}, f32[7,4,2,1152]{3,2,1,0:T(2,128)S(1)}, u32[]{:S(2)}, u32[]{:S(2)}) %collective-permute-start.7) | collective-permute-done | bytes 258080 | tf_op jit(solution)/shard_map/ppermute | solution.py:698
  38.3 0.5 %collective-permute-start.11 = (f32[48,1152]{1,0:T(8,128)S(1)}, f32[48,1152]{1,0:T(8,128)S(1)}, u32[]{:S(2)}, u32[]{:S(2)}) collective-permute-start(f32[48,1152]{1,0:T(8,128)S(1)} %get-tuple-element.45.refs_0_.refs_8_), channel_id=1, source_target_pairs={{0,1},{1,0},{2,3},{3,2},{4,5},{5,4},{6,7},{7,6},{8,9},{9,8},{10,11... | collective-permute-start | bytes 663560 | tf_op jit(solution)/shard_map/ppermute | solution.py:700
  38.9 1.3 %collective-permute-done.11.refs_9_ = f32[48,1152]{1,0:T(8,128)S(1)} collective-permute-done((f32[48,1152]{1,0:T(8,128)S(1)}, f32[48,1152]{1,0:T(8,128)S(1)}, u32[]{:S(2)}, u32[]{:S(2)}) %collective-permute-start.11) | collective-permute-done | bytes 221216 | tf_op jit(solution)/shard_map/ppermute | solution.py:700
  40.5 3.7 %remap_edges.1 = (f32[6,4,2,1152]{3,2,1,0:T(2,128)S(1)}, f32[4,2,1152]{2,1,0:T(2,128)S(1)}, f32[4,4,3,1152]{3,2,1,0:T(4,128)S(1)}) custom-call(f32[16,8,128]{2,1,0:T(8,128)S(1)} %broadcast_in_dim.4.weight_ref, f32[7,4,2,1152]{3,2,1,0:T(2,128)S(1)} %get-tuple-element.51.refs_6_.refs_0_, f32[7,4,2,1152]{3,2,1,0:T(2,128)S(1)} %collective-permute-done.6.refs_1_, ...), custom_call_target="tpu_custom_call" | custom-call | flops 5898240 | bytes 3096576 | tf_op jit(solution)/shard_map/remap_edges/pallas_call | solution.py:559
  44.2 1.4 %finish_tracers.1 = (f32[4,4,16,1152]{3,2,1,0:T(8,128)}, f32[4,16,1152]{2,1,0:T(8,128)}, f32[8,128]{1,0:T(8,128)S(1)}) custom-call(f32[4,4,16,1152]{3,2,1,0:T(8,128)S(1)} %get-tuple-element.52.refs_8_.own_ref, f32[4,4,3,1152]{3,2,1,0:T(4,128)S(1)} %get-tuple-element.58.near_ref, f32[6,4,2,1152]{3,2,1,0:T(2,128)S(1)} %get-tuple-element.59.edge_ref, ...), custom_call_target="tpu_custom_call" | custom-call | flops 589824 | bytes 3538944 | tf_op jit(solution)/shard_map/finish_tracers/pallas_call | solution.py:597
  45.7 3.1 %collective-permute-done.16.refs_0_ = f32[112,1152]{1,0:T(8,128)S(1)} collective-permute-done((f32[112,1152]{1,0:T(8,128)S(1)}, f32[112,1152]{1,0:T(8,128)S(1)}, u32[]{:S(2)}, u32[]{:S(2)}) %collective-permute-start.16) | collective-permute-done | bytes 516128 | tf_op jit(solution)/shard_map/ppermute | solution.py:698
  48.8 0.9 %finish_winds.1 = (f32[4,16,1152]{2,1,0:T(8,128)}, f32[4,16,1152]{2,1,0:T(8,128)}) custom-call(f32[2,4,16,1152]{3,2,1,0:T(8,128)S(1)} %get-tuple-element.63.own_ref, f32[6,4,2,1152]{3,2,1,0:T(2,128)S(1)} %get-tuple-element.59.edge_ref, f32[112,1152]{1,0:T(8,128)S(1)} %collective-permute-done.16.refs_0_, f32[8,128]{1,0:T(8,128)S(1)} %get-tuple-element.64.refs_1_), custom_call_target="tpu_custom_call" | custom-call | flops 147456 | bytes 1769472 | tf_op jit(solution)/shard_map/finish_winds/pallas_call | solution.py:635
  (34 shorter events, 2.4 us)
Async XLA Ops:
  0.6 4.9 %copy-start.2 = (f32[4,24,128]{2,1,0:T(8,128)S(1)}, f32[4,24,128]{2,1,0:T(8,128)}, u32[]{:S(2)}) copy-start(f32[4,24,128]{2,1,0:T(8,128)} %constant.6.clone.table_hbm.table_ref) | copy-start | bytes 147460
  2.5 6.3 %collective-permute-start.1 = (f32[234,128]{1,0:T(8,128)S(1)}, f32[234,128]{1,0:T(8,128)S(1)}, u32[]{:S(2)}, u32[]{:S(2)}) collective-permute-start(f32[234,128]{1,0:T(8,128)S(1)} %get-tuple-element.44), channel_id=1, source_target_pairs={{0,2},{2,0},{1,3},{3,1},{4,6},{6,4},{5,7},{7,5},{8,10},{10,8},{9,1... | collective-permute-start | bytes 359432 | tf_op jit(solution)/shard_map/ppermute | solution.py:698
  6.9 3.5 %collective-permute-start = (f32[5,4,16,1152]{3,2,1,0:T(8,128)S(1)}, f32[5,4,16,1152]{3,2,1,0:T(8,128)S(1)}, u32[]{:S(2)}, u32[]{:S(2)}) collective-permute-start(f32[5,4,16,1152]{3,2,1,0:T(8,128)S(1)} %get-tuple-element.43.refs_0_.refs_2_), channel_id=1, source_target_pairs={{0,1},{1,0},{2,3},{3,2},{4,5},{5,4},{6,7},{7,6},{8,9},{9,8},{10,11... | collective-permute-start | bytes 4423688 | tf_op jit(solution)/shard_map/ppermute | solution.py:700
  6.9 3.4 %copy-start.3 = (f32[16]{0:T(128)S(1)}, f32[16]{0:T(128)}, u32[]{:S(2)}) copy-start(f32[16]{0:T(128)} %param.13) | copy-start | bytes 196
  7.0 7.8 %collective-permute-start.3 = (f32[48,1152]{1,0:T(8,128)S(1)}, f32[48,1152]{1,0:T(8,128)S(1)}, u32[]{:S(2)}, u32[]{:S(2)}) collective-permute-start(f32[48,1152]{1,0:T(8,128)S(1)} %get-tuple-element.45.refs_0_.refs_8_), channel_id=1, source_target_pairs={{0,2},{2,0},{1,3},{3,1},{4,6},{6,4},{5,7},{7,5},{8,10},{10,8},{9,1... | collective-permute-start | bytes 663560 | tf_op jit(solution)/shard_map/ppermute | solution.py:698
  8.9 1.4 %collective-permute-start.2 = (f32[16,1152]{1,0:T(8,128)S(1)}, f32[16,1152]{1,0:T(8,128)S(1)}, u32[]{:S(2)}, u32[]{:S(2)}) collective-permute-start(f32[16,1152]{1,0:T(8,128)S(1)} %get-tuple-element.46.refs_0_), channel_id=1, source_target_pairs={{0,1},{1,0},{2,3},{3,2},{4,5},{5,4},{6,7},{7,6},{8,9},{9,8},{10,11... | collective-permute-start | bytes 221192 | tf_op jit(solution)/shard_map/ppermute | solution.py:700
  11.8 11.6 %copy-start.4 = (s32[16]{0:T(128)S(1)}, s32[16]{0:T(128)}, u32[]{:S(2)}) copy-start(s32[16]{0:T(128)} %param.14) | copy-start | bytes 196
  11.8 11.7 %copy-start = (bf16[5,256,256]{2,1,0:T(8,128)(2,1)S(1)}, bf16[5,256,256]{2,1,0:T(8,128)(2,1)}, u32[]{:S(2)}) copy-start(bf16[5,256,256]{2,1,0:T(8,128)(2,1)} %constant.7.clone.high_ref) | copy-start | bytes 1966084
  11.8 11.7 %copy-start.1 = (bf16[5,256,256]{2,1,0:T(8,128)(2,1)S(1)}, bf16[5,256,256]{2,1,0:T(8,128)(2,1)}, u32[]{:S(2)}) copy-start(bf16[5,256,256]{2,1,0:T(8,128)(2,1)} %constant.8.clone.low_ref) | copy-start | bytes 1966084
  11.9 21.0 %collective-permute-start.15 = (f32[176,1152]{1,0:T(8,128)S(1)}, f32[176,1152]{1,0:T(8,128)S(1)}, u32[]{:S(2)}, u32[]{:S(2)}) collective-permute-start(f32[176,1152]{1,0:T(8,128)S(1)} %remap_parts.3.refs_0_), channel_id=1, source_target_pairs={{0,2},{2,0},{1,3},{3,1},{4,6},{6,4},{5,7},{7,5},{8,10},{10,8},{9,1... | collective-permute-start | bytes 2433032 | tf_op jit(solution)/shard_map/ppermute | solution.py:698
  15.2 8.2 %collective-permute-start.5 = (f32[8,4,1,1152]{3,2,1,0:T(1,128)S(1)}, f32[8,4,1,1152]{3,2,1,0:T(1,128)S(1)}, u32[]{:S(2)}, u32[]{:S(2)}) collective-permute-start(f32[8,4,1,1152]{3,2,1,0:T(1,128)S(1)} %get-tuple-element.50), channel_id=1, source_target_pairs={{4,0},{8,4},{12,8},{5,1},{9,5},{13,9},{6,2},{10,6},{14,10},{7,3},{... | collective-permute-start | bytes 442376 | tf_op jit(solution)/shard_map/ppermute | solution.py:747
  16.5 6.9 %collective-permute-start.4 = (f32[6,4,1,1152]{3,2,1,0:T(1,128)S(1)}, f32[6,4,1,1152]{3,2,1,0:T(1,128)S(1)}, u32[]{:S(2)}, u32[]{:S(2)}) collective-permute-start(f32[6,4,1,1152]{3,2,1,0:T(1,128)S(1)} %get-tuple-element.49), channel_id=1, source_target_pairs={{0,4},{4,8},{8,12},{1,5},{5,9},{9,13},{2,6},{6,10},{10,14},{3,7},{... | collective-permute-start | bytes 331784 | tf_op jit(solution)/shard_map/ppermute | solution.py:746
  27.1 2.5 %collective-permute-start.13 = (f32[1,4,16,1152]{3,2,1,0:T(8,128)S(1)}, f32[1,4,16,1152]{3,2,1,0:T(8,128)S(1)}, u32[]{:S(2)}, u32[]{:S(2)}) collective-permute-start(f32[1,4,16,1152]{3,2,1,0:T(8,128)S(1)} %get-tuple-element.55.refs_2_), channel_id=1, source_target_pairs={{0,1},{1,0},{2,3},{3,2},{4,5},{5,4},{6,7},{7,6},{8,9},{9,8},{10,11... | collective-permute-start | bytes 884744 | tf_op jit(solution)/shard_map/ppermute | solution.py:700
  27.2 2.4 %collective-permute-start.14 = (f32[1,4,16,1152]{3,2,1,0:T(8,128)S(1)}, f32[1,4,16,1152]{3,2,1,0:T(8,128)S(1)}, u32[]{:S(2)}, u32[]{:S(2)}) collective-permute-start(f32[1,4,16,1152]{3,2,1,0:T(8,128)S(1)} %get-tuple-element.56.refs_4_), channel_id=1, source_target_pairs={{0,1},{1,0},{2,3},{3,2},{4,5},{5,4},{6,7},{7,6},{8,9},{9,8},{10,11... | collective-permute-start | bytes 884744 | tf_op jit(solution)/shard_map/ppermute | solution.py:700
  27.7 10.7 %collective-permute-start.7 = (f32[7,4,2,1152]{3,2,1,0:T(2,128)S(1)}, f32[7,4,2,1152]{3,2,1,0:T(2,128)S(1)}, u32[]{:S(2)}, u32[]{:S(2)}) collective-permute-start(f32[7,4,2,1152]{3,2,1,0:T(2,128)S(1)} %get-tuple-element.51.refs_6_.refs_0_), channel_id=1, source_target_pairs={{0,2},{2,0},{1,3},{3,1},{4,6},{6,4},{5,7},{7,5},{8,10},{10,8},{9,1... | collective-permute-start | bytes 774152 | tf_op jit(solution)/shard_map/ppermute | solution.py:698
  34.6 14.2 %collective-permute-start.16 = (f32[112,1152]{1,0:T(8,128)S(1)}, f32[112,1152]{1,0:T(8,128)S(1)}, u32[]{:S(2)}, u32[]{:S(2)}) collective-permute-start(f32[112,1152]{1,0:T(8,128)S(1)} %get-tuple-element.57.refs_12_), channel_id=1, source_target_pairs={{0,2},{2,0},{1,3},{3,1},{4,6},{6,4},{5,7},{7,5},{8,10},{10,8},{9,1... | collective-permute-start | bytes 1548296 | tf_op jit(solution)/shard_map/ppermute | solution.py:698
  36.6 1.8 %collective-permute-start.9 = (f32[1,4,3,1152]{3,2,1,0:T(4,128)S(1)}, f32[1,4,3,1152]{3,2,1,0:T(4,128)S(1)}, u32[]{:S(2)}, u32[]{:S(2)}) collective-permute-start(f32[1,4,3,1152]{3,2,1,0:T(4,128)S(1)} %get-tuple-element.53.refs_4_), channel_id=1, source_target_pairs={{0,1},{1,0},{2,3},{3,2},{4,5},{5,4},{6,7},{7,6},{8,9},{9,8},{10,11... | collective-permute-start | bytes 165896 | tf_op jit(solution)/shard_map/ppermute | solution.py:700
  36.6 2.3 %collective-permute-start.10 = (f32[1,4,3,1152]{3,2,1,0:T(4,128)S(1)}, f32[1,4,3,1152]{3,2,1,0:T(4,128)S(1)}, u32[]{:S(2)}, u32[]{:S(2)}) collective-permute-start(f32[1,4,3,1152]{3,2,1,0:T(4,128)S(1)} %get-tuple-element.54.refs_6_), channel_id=1, source_target_pairs={{0,1},{1,0},{2,3},{3,2},{4,5},{5,4},{6,7},{7,6},{8,9},{9,8},{10,11... | collective-permute-start | bytes 165896 | tf_op jit(solution)/shard_map/ppermute | solution.py:700
  37.1 3.4 %collective-permute-start.6 = (f32[7,4,2,1152]{3,2,1,0:T(2,128)S(1)}, f32[7,4,2,1152]{3,2,1,0:T(2,128)S(1)}, u32[]{:S(2)}, u32[]{:S(2)}) collective-permute-start(f32[7,4,2,1152]{3,2,1,0:T(2,128)S(1)} %get-tuple-element.51.refs_6_.refs_0_), channel_id=1, source_target_pairs={{0,1},{1,0},{2,3},{3,2},{4,5},{5,4},{6,7},{7,6},{8,9},{9,8},{10,11... | collective-permute-start | bytes 774152 | tf_op jit(solution)/shard_map/ppermute | solution.py:700
  38.3 2.2 %collective-permute-start.8 = (f32[7,4,2,1152]{3,2,1,0:T(2,128)S(1)}, f32[7,4,2,1152]{3,2,1,0:T(2,128)S(1)}, u32[]{:S(2)}, u32[]{:S(2)}) collective-permute-start(f32[7,4,2,1152]{3,2,1,0:T(2,128)S(1)} %collective-permute-done.7.refs_2_), channel_id=1, source_target_pairs={{0,1},{1,0},{2,3},{3,2},{4,5},{5,4},{6,7},{7,6},{8,9},{9,8},{10,11... | collective-permute-start | bytes 774152 | tf_op jit(solution)/shard_map/ppermute | solution.py:700
  38.3 1.8 %collective-permute-start.11 = (f32[48,1152]{1,0:T(8,128)S(1)}, f32[48,1152]{1,0:T(8,128)S(1)}, u32[]{:S(2)}, u32[]{:S(2)}) collective-permute-start(f32[48,1152]{1,0:T(8,128)S(1)} %get-tuple-element.45.refs_0_.refs_8_), channel_id=1, source_target_pairs={{0,1},{1,0},{2,3},{3,2},{4,5},{5,4},{6,7},{7,6},{8,9},{9,8},{10,11... | collective-permute-start | bytes 663560 | tf_op jit(solution)/shard_map/ppermute | solution.py:700
  38.9 1.6 %collective-permute-start.12 = (f32[48,1152]{1,0:T(8,128)S(1)}, f32[48,1152]{1,0:T(8,128)S(1)}, u32[]{:S(2)}, u32[]{:S(2)}) collective-permute-start(f32[48,1152]{1,0:T(8,128)S(1)} %collective-permute-done.3.refs_1_.refs_10_), channel_id=1, source_target_pairs={{0,1},{1,0},{2,3},{3,2},{4,5},{5,4},{6,7},{7,6},{8,9},{9,8},{10,11... | collective-permute-start | bytes 663560 | tf_op jit(solution)/shard_map/ppermute | solution.py:700

commit v22 on v21

--- a/solution.py
+++ b/solution.py
@@ -26,7 +26,7 @@
 
 
 def near_rows(rows):
-    return (1, 2, rows - 2), (3, 2)
+    return (1, rows - 2), (2, 2)
 
 
 def geometry_table(lat_rows, band_rows):

time: 49.9 us -> 51.2 us (1.026)
  waiting for transfers between devices: 15.7 us -> 18.6 us
  starting transfers between devices: 15.3 us -> 14.1 us
    ppermute x5, waiting for transfers between devices: 10.4 us -> 12.4 us  [shifted(): lax.ppermute(value, 'lev', [(i, (i + s) % lev_count) for i in range(lev_c...]
    ppermute x5, starting transfers between devices: 7.62 us -> 6.54 us  [shifted(): lax.ppermute(value, 'lev', [(i, (i + s) % lev_count) for i in range(lev_c...]
    ppermute x10, waiting for transfers between devices: 2.93 us -> 3.9 us  [shifted(): lax.ppermute(value, 'sub', [(i, (i + t) % sub_count) for i in range(sub_c...]
  transfers between devices with their start and end apart: 17 -> 17, of which waited for: 9 -> 9; matrix products, arithmetic and copies ran while one was open for 0% -> 0% of each run, Pallas kernels for 30% -> 29%
where the time goes in v22:
time: 51.2 us; the launch traced here: 51.1 us
  waiting for transfers between devices  18.6 us (36%)
  Pallas kernels  17.4 us (34%)
  starting transfers between devices  14.1 us (28%)
  between operations  0.82 us (2%)
    ppermute x5, waiting for transfers between devices, shifted(): lax.ppermute(value, 'lev', [(i, (i + s) % lev_count) for i in range(lev_c...  12.4 us
    ppermute x5, starting transfers between devices, shifted(): lax.ppermute(value, 'lev', [(i, (i + s) % lev_count) for i in range(lev_c...  6.54 us
    ppermute x1, starting transfers between devices, per_device(): up = lax.ppermute(last, 'lat', northward)  4.55 us
    pallas_call x3, Pallas kernels, remap_parts(): pl.pallas_call(functools.partial(remap_kernel, counts, tuple(steps), tupl...  4.45 us
    ppermute x10, waiting for transfers between devices, shifted(): lax.ppermute(value, 'sub', [(i, (i + t) % sub_count) for i in range(sub_c...  3.9 us
    pallas_call x1, Pallas kernels, second_step(): pl.pallas_call(functools.partial(second_kernel, lat_rows), grid=(L,), in_...  3.59 us
    pallas_call x1, Pallas kernels, remap_edges(): pl.pallas_call(functools.partial(remap_edge_kernel, counts), in_specs=[VM...  3.38 us
    ppermute x1, waiting for transfers between devices, per_device(): up = lax.ppermute(last, 'lat', northward)  2.3 us
  transfers between devices with their start and end apart: 17, of which 9 were waited for; matrix products, arithmetic and copies ran while one was open for 0% of the time, Pallas kernels for 29%

profile of v22, /device:TPU:0, one launch (start us, length us, event | category | flops | bytes accessed | tf_op | source)
XLA Modules:
  0.0 51.1 jit_solution(1870519303870652922)
XLA Ops:
  0.6 1.9 %first_step.1 = (f32[4,16,1152]{2,1,0:T(8,128)S(1)}, f32[198,128]{1,0:T(8,128)S(1)}, f32[1,4,2,1152]{3,2,1,0:T(2,128)S(1)}, f32[4,16,1152]{2,1,0:T(8,128)S(1)}, ...) custom-call(f32[4,24,128]{2,1,0:T(8,128)} %constant.6.clone.table_hb, ...), custom_call_target="tpu_custom_call" | custom-call | flops 2949120 | bytes 4423680 | tf_op jit(solution)/shard_map/first_step/pallas_call | solution.py:141
  2.5 3.0 %collective-permute-start.1 = (f32[198,128]{1,0:T(8,128)S(1)}, f32[198,128]{1,0:T(8,128)S(1)}, u32[]{:S(2)}, u32[]{:S(2)}) collective-permute-start(f32[198,128]{1,0:T(8,128)S(1)} %get-tuple-element.44), channel_id=1, source_target_pairs={{0,2},{2,0},{1,3},{3,1},{4,6},{6,4},{5,7},{7,5},{8,10},{10,8},{9,1... | collective-permute-start | bytes 304136 | tf_op jit(solution)/shard_map/ppermute | solution.py:698
  5.5 1.3 %inner_step.1 = (f32[5,4,16,1152]{3,2,1,0:T(8,128)S(1)}, f32[32,1152]{1,0:T(8,128)S(1)}) custom-call(f32[4,24,128]{2,1,0:T(8,128)S(1)} %copy-done.2, f32[4,16,1152]{2,1,0:T(8,128)S(1)} %get-tuple-element.36.new_ref, f32[4,16,1152]{2,1,0:T(8,128)S(1)} %get-tuple-element.37.east_ref, f32[4,16,1152]{2,1,0:T(8,128)S(1)} %get-tuple-element.38.north_ref, ...), custom_call_target="tpu_custom_call" | custom-call | flops 9584640 | bytes 4718592 | tf_op jit(solution)/shard_map/inner_step/pallas_call | solution.py:187
  7.0 1.4 %collective-permute-done.1.both_ref = f32[198,128]{1,0:T(8,128)S(1)} collective-permute-done((f32[198,128]{1,0:T(8,128)S(1)}, f32[198,128]{1,0:T(8,128)S(1)}, u32[]{:S(2)}, u32[]{:S(2)}) %collective-permute-start.1) | collective-permute-done | bytes 101408 | tf_op jit(solution)/shard_map/ppermute | solution.py:698
  8.5 1.8 %collective-permute-done.2.refs_1_ = f32[16,1152]{1,0:T(8,128)S(1)} collective-permute-done((f32[16,1152]{1,0:T(8,128)S(1)}, f32[16,1152]{1,0:T(8,128)S(1)}, u32[]{:S(2)}, u32[]{:S(2)}) %collective-permute-start.2) | collective-permute-done | bytes 73760 | tf_op jit(solution)/shard_map/ppermute | solution.py:700
  10.4 1.4 %remap_parts.3.refs_0_ = f32[192,1152]{1,0:T(8,128)S(1)} custom-call(f32[16,8,128]{2,1,0:T(8,128)S(1)} %broadcast_in_dim.4.weight_ref, f32[5,4,16,1152]{3,2,1,0:T(8,128)S(1)} %get-tuple-element.43.refs_0_.refs_2_, f32[5,4,16,1152]{3,2,1,0:T(8,128)S(1)} %collective-permute-done.refs_1_.refs_3_, f32[5,4,16,1152]{3,2,1,0:T(8,128)S(1)} %get-tuple-element.43.refs_0_.refs_2_, ...), custom_call_target="tpu_custom_call" | custom-call | flops 7667712 | bytes 4423680 | tf_op jit(solution)/shard_map/remap_parts/pallas_call | solution.py:521
  11.8 1.3 %collective-permute-start.15 = (f32[192,1152]{1,0:T(8,128)S(1)}, f32[192,1152]{1,0:T(8,128)S(1)}, u32[]{:S(2)}, u32[]{:S(2)}) collective-permute-start(f32[192,1152]{1,0:T(8,128)S(1)} %remap_parts.3.refs_0_), channel_id=1, source_target_pairs={{0,2},{2,0},{1,3},{3,1},{4,6},{6,4},{5,7},{7,5},{8,10},{10,8},{9,1... | collective-permute-start | bytes 2654216 | tf_op jit(solution)/shard_map/ppermute | solution.py:698
  13.6 1.3 %collective-permute-start.5 = (f32[8,4,1,1152]{3,2,1,0:T(1,128)S(1)}, f32[8,4,1,1152]{3,2,1,0:T(1,128)S(1)}, u32[]{:S(2)}, u32[]{:S(2)}) collective-permute-start(f32[8,4,1,1152]{3,2,1,0:T(1,128)S(1)} %get-tuple-element.50), channel_id=1, source_target_pairs={{4,0},{8,4},{12,8},{5,1},{9,5},{13,9},{6,2},{10,6},{14,10},{7,3},{... | collective-permute-start | bytes 442376 | tf_op jit(solution)/shard_map/ppermute | solution.py:747
  14.9 4.6 %collective-permute-start.4 = (f32[6,4,1,1152]{3,2,1,0:T(1,128)S(1)}, f32[6,4,1,1152]{3,2,1,0:T(1,128)S(1)}, u32[]{:S(2)}, u32[]{:S(2)}) collective-permute-start(f32[6,4,1,1152]{3,2,1,0:T(1,128)S(1)} %get-tuple-element.49), channel_id=1, source_target_pairs={{0,4},{4,8},{8,12},{1,5},{5,9},{9,13},{2,6},{6,10},{10,14},{3,7},{... | collective-permute-start | bytes 331784 | tf_op jit(solution)/shard_map/ppermute | solution.py:746
  19.5 2.3 %collective-permute-done.4.up_ref = f32[6,4,1,1152]{3,2,1,0:T(1,128)S(1)} collective-permute-done((f32[6,4,1,1152]{3,2,1,0:T(1,128)S(1)}, f32[6,4,1,1152]{3,2,1,0:T(1,128)S(1)}, u32[]{:S(2)}, u32[]{:S(2)}) %collective-permute-start.4) | collective-permute-done | bytes 110624 | tf_op jit(solution)/shard_map/ppermute | solution.py:746
  21.9 3.6 %second_step.1 = (f32[1,4,16,1152]{3,2,1,0:T(8,128)S(1)}, f32[1,4,16,1152]{3,2,1,0:T(8,128)S(1)}, f32[7,4,2,1152]{3,2,1,0:T(2,128)S(1)}) custom-call(f32[4,24,128]{2,1,0:T(8,128)S(1)} %copy-done.2, f32[4,16,1152]{2,1,0:T(8,128)S(1)} %get-tuple-element.39.thick_ref.thick_any, f32[4,16,1152]{2,1,0:T(8,128)S(1)} %get-tuple-element.40.u_ref.u_any, ...), custom_call_target="tpu_custom_call" | custom-call | flops 503316480 | bytes 3538944 | tf_op jit(solution)/shard_map/second_step/pallas_call | solution.py:325
  26.1 0.7 %collective-permute-start.7 = (f32[7,4,2,1152]{3,2,1,0:T(2,128)S(1)}, f32[7,4,2,1152]{3,2,1,0:T(2,128)S(1)}, u32[]{:S(2)}, u32[]{:S(2)}) collective-permute-start(f32[7,4,2,1152]{3,2,1,0:T(2,128)S(1)} %get-tuple-element.51.refs_6_.refs_0_), channel_id=1, source_target_pairs={{0,2},{2,0},{1,3},{3,1},{4,6},{6,4},{5,7},{7,5},{8,10},{10,8},{9,1... | collective-permute-start | bytes 774152 | tf_op jit(solution)/shard_map/ppermute | solution.py:698
  26.8 1.3 %remap_parts.4 = (f32[4,4,16,1152]{3,2,1,0:T(8,128)S(1)}, f32[4,16,1152]{2,1,0:T(8,128)S(1)}) custom-call(f32[16,8,128]{2,1,0:T(8,128)S(1)} %broadcast_in_dim.4.weight_ref, f32[5,4,16,1152]{3,2,1,0:T(8,128)S(1)} %get-tuple-element.43.refs_0_.refs_2_, f32[5,4,16,1152]{3,2,1,0:T(8,128)S(1)} %collective-permute-done.refs_1_.refs_3_, ...), custom_call_target="tpu_custom_call" | custom-call | flops 7667712 | bytes 4423680 | tf_op jit(solution)/shard_map/remap_parts/pallas_call | solution.py:521
  28.1 6.2 %collective-permute-done.15.refs_9_.refs_0_ = f32[192,1152]{1,0:T(8,128)S(1)} collective-permute-done((f32[192,1152]{1,0:T(8,128)S(1)}, f32[192,1152]{1,0:T(8,128)S(1)}, u32[]{:S(2)}, u32[]{:S(2)}) %collective-permute-start.15) | collective-permute-done | bytes 884768 | tf_op jit(solution)/shard_map/ppermute | solution.py:698
  34.4 1.8 %remap_parts.5 = (f32[2,4,16,1152]{3,2,1,0:T(8,128)S(1)}, f32[112,1152]{1,0:T(8,128)S(1)}) custom-call(f32[16,8,128]{2,1,0:T(8,128)S(1)} %broadcast_in_dim.4.weight_ref, f32[5,4,16,1152]{3,2,1,0:T(8,128)S(1)} %get-tuple-element.43.refs_0_.refs_2_, f32[5,4,16,1152]{3,2,1,0:T(8,128)S(1)} %collective-permute-done.refs_1_.refs_3_, ...), custom_call_target="tpu_custom_call" | custom-call | flops 10616832 | bytes 3538944 | tf_op jit(solution)/shard_map/remap_parts/pallas_call | solution.py:521
  36.1 1.3 %collective-permute-start.16 = (f32[112,1152]{1,0:T(8,128)S(1)}, f32[112,1152]{1,0:T(8,128)S(1)}, u32[]{:S(2)}, u32[]{:S(2)}) collective-permute-start(f32[112,1152]{1,0:T(8,128)S(1)} %get-tuple-element.57.refs_12_), channel_id=1, source_target_pairs={{0,2},{2,0},{1,3},{3,1},{4,6},{6,4},{5,7},{7,5},{8,10},{10,8},{9,1... | collective-permute-start | bytes 1548296 | tf_op jit(solution)/shard_map/ppermute | solution.py:698
  37.5 2.4 %collective-permute-done.7.refs_2_ = f32[7,4,2,1152]{3,2,1,0:T(2,128)S(1)} collective-permute-done((f32[7,4,2,1152]{3,2,1,0:T(2,128)S(1)}, f32[7,4,2,1152]{3,2,1,0:T(2,128)S(1)}, u32[]{:S(2)}, u32[]{:S(2)}) %collective-permute-start.7) | collective-permute-done | bytes 258080 | tf_op jit(solution)/shard_map/ppermute | solution.py:698
  39.9 0.5 collective-permute-start.9
  40.4 1.1 %collective-permute-done.9.refs_5_ = f32[1,4,2,1152]{3,2,1,0:T(2,128)S(1)} collective-permute-done((f32[1,4,2,1152]{3,2,1,0:T(2,128)S(1)}, f32[1,4,2,1152]{3,2,1,0:T(2,128)S(1)}, u32[]{:S(2)}, u32[]{:S(2)}) %collective-permute-start.9) | collective-permute-done | bytes 36896 | tf_op jit(solution)/shard_map/ppermute | solution.py:700
  42.0 0.9 %collective-permute-done.11.refs_9_ = f32[32,1152]{1,0:T(8,128)S(1)} collective-permute-done((f32[32,1152]{1,0:T(8,128)S(1)}, f32[32,1152]{1,0:T(8,128)S(1)}, u32[]{:S(2)}, u32[]{:S(2)}) %collective-permute-start.11) | collective-permute-done | bytes 147488 | tf_op jit(solution)/shard_map/ppermute | solution.py:700
  43.1 3.4 %remap_edges.1 = (f32[6,4,2,1152]{3,2,1,0:T(2,128)S(1)}, f32[4,2,1152]{2,1,0:T(2,128)S(1)}, f32[4,4,2,1152]{3,2,1,0:T(2,128)S(1)}) custom-call(f32[16,8,128]{2,1,0:T(8,128)S(1)} %broadcast_in_dim.4.weight_ref, f32[7,4,2,1152]{3,2,1,0:T(2,128)S(1)} %get-tuple-element.51.refs_6_.refs_0_, f32[7,4,2,1152]{3,2,1,0:T(2,128)S(1)} %collective-permute-done.6.refs_1_, ...), custom_call_target="tpu_custom_call" | custom-call | flops 5898240 | bytes 3096576 | tf_op jit(solution)/shard_map/remap_edges/pallas_call | solution.py:559
  46.5 1.4 %finish_tracers.1 = (f32[4,4,16,1152]{3,2,1,0:T(8,128)}, f32[4,16,1152]{2,1,0:T(8,128)}, f32[8,128]{1,0:T(8,128)S(1)}) custom-call(f32[4,4,16,1152]{3,2,1,0:T(8,128)S(1)} %get-tuple-element.52.refs_8_.own_ref, f32[4,4,2,1152]{3,2,1,0:T(2,128)S(1)} %get-tuple-element.58.near_ref, f32[6,4,2,1152]{3,2,1,0:T(2,128)S(1)} %get-tuple-element.59.edge_ref, ...), custom_call_target="tpu_custom_call" | custom-call | flops 589824 | bytes 3538944 | tf_op jit(solution)/shard_map/finish_tracers/pallas_call | solution.py:597
  47.8 2.3 %collective-permute-done.16.refs_0_ = f32[112,1152]{1,0:T(8,128)S(1)} collective-permute-done((f32[112,1152]{1,0:T(8,128)S(1)}, f32[112,1152]{1,0:T(8,128)S(1)}, u32[]{:S(2)}, u32[]{:S(2)}) %collective-permute-start.16) | collective-permute-done | bytes 516128 | tf_op jit(solution)/shard_map/ppermute | solution.py:698
  50.2 0.9 %finish_winds.1 = (f32[4,16,1152]{2,1,0:T(8,128)}, f32[4,16,1152]{2,1,0:T(8,128)}) custom-call(f32[2,4,16,1152]{3,2,1,0:T(8,128)S(1)} %get-tuple-element.63.own_ref, f32[6,4,2,1152]{3,2,1,0:T(2,128)S(1)} %get-tuple-element.59.edge_ref, f32[112,1152]{1,0:T(8,128)S(1)} %collective-permute-done.16.refs_0_, f32[8,128]{1,0:T(8,128)S(1)} %get-tuple-element.64.refs_1_), custom_call_target="tpu_custom_call" | custom-call | flops 147456 | bytes 1769472 | tf_op jit(solution)/shard_map/finish_winds/pallas_call | solution.py:635
  (34 shorter events, 2.2 us)
Async XLA Ops:
  0.6 4.9 %copy-start.2 = (f32[4,24,128]{2,1,0:T(8,128)S(1)}, f32[4,24,128]{2,1,0:T(8,128)}, u32[]{:S(2)}) copy-start(f32[4,24,128]{2,1,0:T(8,128)} %constant.6.clone.table_hbm.table_ref) | copy-start | bytes 147460
  2.5 5.9 %collective-permute-start.1 = (f32[198,128]{1,0:T(8,128)S(1)}, f32[198,128]{1,0:T(8,128)S(1)}, u32[]{:S(2)}, u32[]{:S(2)}) collective-permute-start(f32[198,128]{1,0:T(8,128)S(1)} %get-tuple-element.44), channel_id=1, source_target_pairs={{0,2},{2,0},{1,3},{3,1},{4,6},{6,4},{5,7},{7,5},{8,10},{10,8},{9,1... | collective-permute-start | bytes 304136 | tf_op jit(solution)/shard_map/ppermute | solution.py:698
  6.8 3.5 %collective-permute-start = (f32[5,4,16,1152]{3,2,1,0:T(8,128)S(1)}, f32[5,4,16,1152]{3,2,1,0:T(8,128)S(1)}, u32[]{:S(2)}, u32[]{:S(2)}) collective-permute-start(f32[5,4,16,1152]{3,2,1,0:T(8,128)S(1)} %get-tuple-element.43.refs_0_.refs_2_), channel_id=1, source_target_pairs={{0,1},{1,0},{2,3},{3,2},{4,5},{5,4},{6,7},{7,6},{8,9},{9,8},{10,11... | collective-permute-start | bytes 4423688 | tf_op jit(solution)/shard_map/ppermute | solution.py:700
  6.9 3.4 %copy-start.3 = (f32[16]{0:T(128)S(1)}, f32[16]{0:T(128)}, u32[]{:S(2)}) copy-start(f32[16]{0:T(128)} %param.13) | copy-start | bytes 196
  6.9 6.3 %collective-permute-start.3 = (f32[32,1152]{1,0:T(8,128)S(1)}, f32[32,1152]{1,0:T(8,128)S(1)}, u32[]{:S(2)}, u32[]{:S(2)}) collective-permute-start(f32[32,1152]{1,0:T(8,128)S(1)} %get-tuple-element.45.refs_0_.refs_8_), channel_id=1, source_target_pairs={{0,2},{2,0},{1,3},{3,1},{4,6},{6,4},{5,7},{7,5},{8,10},{10,8},{9,1... | collective-permute-start | bytes 442376 | tf_op jit(solution)/shard_map/ppermute | solution.py:698
  8.4 1.8 %collective-permute-start.2 = (f32[16,1152]{1,0:T(8,128)S(1)}, f32[16,1152]{1,0:T(8,128)S(1)}, u32[]{:S(2)}, u32[]{:S(2)}) collective-permute-start(f32[16,1152]{1,0:T(8,128)S(1)} %get-tuple-element.46.refs_0_), channel_id=1, source_target_pairs={{0,1},{1,0},{2,3},{3,2},{4,5},{5,4},{6,7},{7,6},{8,9},{9,8},{10,11... | collective-permute-start | bytes 221192 | tf_op jit(solution)/shard_map/ppermute | solution.py:700
  11.8 10.0 %copy-start.4 = (s32[16]{0:T(128)S(1)}, s32[16]{0:T(128)}, u32[]{:S(2)}) copy-start(s32[16]{0:T(128)} %param.14) | copy-start | bytes 196
  11.8 10.1 %copy-start = (bf16[5,256,256]{2,1,0:T(8,128)(2,1)S(1)}, bf16[5,256,256]{2,1,0:T(8,128)(2,1)}, u32[]{:S(2)}) copy-start(bf16[5,256,256]{2,1,0:T(8,128)(2,1)} %constant.7.clone.high_ref) | copy-start | bytes 1966084
  11.8 10.1 %copy-start.1 = (bf16[5,256,256]{2,1,0:T(8,128)(2,1)S(1)}, bf16[5,256,256]{2,1,0:T(8,128)(2,1)}, u32[]{:S(2)}) copy-start(bf16[5,256,256]{2,1,0:T(8,128)(2,1)} %constant.8.clone.low_ref) | copy-start | bytes 1966084
  11.8 22.6 %collective-permute-start.15 = (f32[192,1152]{1,0:T(8,128)S(1)}, f32[192,1152]{1,0:T(8,128)S(1)}, u32[]{:S(2)}, u32[]{:S(2)}) collective-permute-start(f32[192,1152]{1,0:T(8,128)S(1)} %remap_parts.3.refs_0_), channel_id=1, source_target_pairs={{0,2},{2,0},{1,3},{3,1},{4,6},{6,4},{5,7},{7,5},{8,10},{10,8},{9,1... | collective-permute-start | bytes 2654216 | tf_op jit(solution)/shard_map/ppermute | solution.py:698
  13.6 8.2 %collective-permute-start.5 = (f32[8,4,1,1152]{3,2,1,0:T(1,128)S(1)}, f32[8,4,1,1152]{3,2,1,0:T(1,128)S(1)}, u32[]{:S(2)}, u32[]{:S(2)}) collective-permute-start(f32[8,4,1,1152]{3,2,1,0:T(1,128)S(1)} %get-tuple-element.50), channel_id=1, source_target_pairs={{4,0},{8,4},{12,8},{5,1},{9,5},{13,9},{6,2},{10,6},{14,10},{7,3},{... | collective-permute-start | bytes 442376 | tf_op jit(solution)/shard_map/ppermute | solution.py:747
  14.9 6.9 %collective-permute-start.4 = (f32[6,4,1,1152]{3,2,1,0:T(1,128)S(1)}, f32[6,4,1,1152]{3,2,1,0:T(1,128)S(1)}, u32[]{:S(2)}, u32[]{:S(2)}) collective-permute-start(f32[6,4,1,1152]{3,2,1,0:T(1,128)S(1)} %get-tuple-element.49), channel_id=1, source_target_pairs={{0,4},{4,8},{8,12},{1,5},{5,9},{9,13},{2,6},{6,10},{10,14},{3,7},{... | collective-permute-start | bytes 331784 | tf_op jit(solution)/shard_map/ppermute | solution.py:746
  25.5 2.6 %collective-permute-start.13 = (f32[1,4,16,1152]{3,2,1,0:T(8,128)S(1)}, f32[1,4,16,1152]{3,2,1,0:T(8,128)S(1)}, u32[]{:S(2)}, u32[]{:S(2)}) collective-permute-start(f32[1,4,16,1152]{3,2,1,0:T(8,128)S(1)} %get-tuple-element.55.refs_2_), channel_id=1, source_target_pairs={{0,1},{1,0},{2,3},{3,2},{4,5},{5,4},{6,7},{7,6},{8,9},{9,8},{10,11... | collective-permute-start | bytes 884744 | tf_op jit(solution)/shard_map/ppermute | solution.py:700
  25.6 2.6 %collective-permute-start.14 = (f32[1,4,16,1152]{3,2,1,0:T(8,128)S(1)}, f32[1,4,16,1152]{3,2,1,0:T(8,128)S(1)}, u32[]{:S(2)}, u32[]{:S(2)}) collective-permute-start(f32[1,4,16,1152]{3,2,1,0:T(8,128)S(1)} %get-tuple-element.56.refs_4_), channel_id=1, source_target_pairs={{0,1},{1,0},{2,3},{3,2},{4,5},{5,4},{6,7},{7,6},{8,9},{9,8},{10,11... | collective-permute-start | bytes 884744 | tf_op jit(solution)/shard_map/ppermute | solution.py:700
  26.1 13.8 %collective-permute-start.7 = (f32[7,4,2,1152]{3,2,1,0:T(2,128)S(1)}, f32[7,4,2,1152]{3,2,1,0:T(2,128)S(1)}, u32[]{:S(2)}, u32[]{:S(2)}) collective-permute-start(f32[7,4,2,1152]{3,2,1,0:T(2,128)S(1)} %get-tuple-element.51.refs_6_.refs_0_), channel_id=1, source_target_pairs={{0,2},{2,0},{1,3},{3,1},{4,6},{6,4},{5,7},{7,5},{8,10},{10,8},{9,1... | collective-permute-start | bytes 774152 | tf_op jit(solution)/shard_map/ppermute | solution.py:698
  36.1 14.0 %collective-permute-start.16 = (f32[112,1152]{1,0:T(8,128)S(1)}, f32[112,1152]{1,0:T(8,128)S(1)}, u32[]{:S(2)}, u32[]{:S(2)}) collective-permute-start(f32[112,1152]{1,0:T(8,128)S(1)} %get-tuple-element.57.refs_12_), channel_id=1, source_target_pairs={{0,2},{2,0},{1,3},{3,1},{4,6},{6,4},{5,7},{7,5},{8,10},{10,8},{9,1... | collective-permute-start | bytes 1548296 | tf_op jit(solution)/shard_map/ppermute | solution.py:698
  37.5 5.6 %collective-permute-start.6 = (f32[7,4,2,1152]{3,2,1,0:T(2,128)S(1)}, f32[7,4,2,1152]{3,2,1,0:T(2,128)S(1)}, u32[]{:S(2)}, u32[]{:S(2)}) collective-permute-start(f32[7,4,2,1152]{3,2,1,0:T(2,128)S(1)} %get-tuple-element.51.refs_6_.refs_0_), channel_id=1, source_target_pairs={{0,1},{1,0},{2,3},{3,2},{4,5},{5,4},{6,7},{7,6},{8,9},{9,8},{10,11... | collective-permute-start | bytes 774152 | tf_op jit(solution)/shard_map/ppermute | solution.py:700
  39.9 3.2 %collective-permute-start.8 = (f32[7,4,2,1152]{3,2,1,0:T(2,128)S(1)}, f32[7,4,2,1152]{3,2,1,0:T(2,128)S(1)}, u32[]{:S(2)}, u32[]{:S(2)}) collective-permute-start(f32[7,4,2,1152]{3,2,1,0:T(2,128)S(1)} %collective-permute-done.7.refs_2_), channel_id=1, source_target_pairs={{0,1},{1,0},{2,3},{3,2},{4,5},{5,4},{6,7},{7,6},{8,9},{9,8},{10,11... | collective-permute-start | bytes 774152 | tf_op jit(solution)/shard_map/ppermute | solution.py:700
  39.9 1.6 %collective-permute-start.9 = (f32[1,4,2,1152]{3,2,1,0:T(2,128)S(1)}, f32[1,4,2,1152]{3,2,1,0:T(2,128)S(1)}, u32[]{:S(2)}, u32[]{:S(2)}) collective-permute-start(f32[1,4,2,1152]{3,2,1,0:T(2,128)S(1)} %get-tuple-element.53.refs_4_), channel_id=1, source_target_pairs={{0,1},{1,0},{2,3},{3,2},{4,5},{5,4},{6,7},{7,6},{8,9},{9,8},{10,11... | collective-permute-start | bytes 110600 | tf_op jit(solution)/shard_map/ppermute | solution.py:700
  40.4 1.2 %collective-permute-start.10 = (f32[1,4,2,1152]{3,2,1,0:T(2,128)S(1)}, f32[1,4,2,1152]{3,2,1,0:T(2,128)S(1)}, u32[]{:S(2)}, u32[]{:S(2)}) collective-permute-start(f32[1,4,2,1152]{3,2,1,0:T(2,128)S(1)} %get-tuple-element.54.refs_6_), channel_id=1, source_target_pairs={{0,1},{1,0},{2,3},{3,2},{4,5},{5,4},{6,7},{7,6},{8,9},{9,8},{10,11... | collective-permute-start | bytes 110600 | tf_op jit(solution)/shard_map/ppermute | solution.py:700
  41.5 1.4 %collective-permute-start.11 = (f32[32,1152]{1,0:T(8,128)S(1)}, f32[32,1152]{1,0:T(8,128)S(1)}, u32[]{:S(2)}, u32[]{:S(2)}) collective-permute-start(f32[32,1152]{1,0:T(8,128)S(1)} %get-tuple-element.45.refs_0_.refs_8_), channel_id=1, source_target_pairs={{0,1},{1,0},{2,3},{3,2},{4,5},{5,4},{6,7},{7,6},{8,9},{9,8},{10,11... | collective-permute-start | bytes 442376 | tf_op jit(solution)/shard_map/ppermute | solution.py:700
  41.6 1.4 %collective-permute-start.12 = (f32[32,1152]{1,0:T(8,128)S(1)}, f32[32,1152]{1,0:T(8,128)S(1)}, u32[]{:S(2)}, u32[]{:S(2)}) collective-permute-start(f32[32,1152]{1,0:T(8,128)S(1)} %collective-permute-done.3.refs_1_.refs_10_), channel_id=1, source_target_pairs={{0,1},{1,0},{2,3},{3,2},{4,5},{5,4},{6,7},{7,6},{8,9},{9,8},{10,11... | collective-permute-start | bytes 442376 | tf_op jit(solution)/shard_map/ppermute | solution.py:700

commit v23 on v22

--- a/solution.py
+++ b/solution.py
@@ -26,7 +26,7 @@
 
 
 def near_rows(rows):
-    return (1, rows - 2), (2, 2)
+    return (1, 2, rows - 3, rows - 2), (3, 3)
 
 
 def geometry_table(lat_rows, band_rows):

time: 51.2 us -> 50 us (0.977)
  waiting for transfers between devices: 18.6 us -> 16.8 us
  starting transfers between devices: 14.1 us -> 14.7 us
    ppermute x5, waiting for transfers between devices: 12.4 us -> 11 us  [shifted(): lax.ppermute(value, 'lev', [(i, (i + s) % lev_count) for i in range(lev_c...]
    ppermute x5, starting transfers between devices: 6.54 us -> 7.16 us  [shifted(): lax.ppermute(value, 'lev', [(i, (i + s) % lev_count) for i in range(lev_c...]
where the time goes in v23:
time: 50 us; the launch traced here: 49.9 us
  Pallas kernels  17.3 us (35%)
  waiting for transfers between devices  16.8 us (34%)
  starting transfers between devices  14.7 us (29%)
  between operations  0.83 us (2%)
    ppermute x5, waiting for transfers between devices, shifted(): lax.ppermute(value, 'lev', [(i, (i + s) % lev_count) for i in range(lev_c...  11 us
    ppermute x5, starting transfers between devices, shifted(): lax.ppermute(value, 'lev', [(i, (i + s) % lev_count) for i in range(lev_c...  7.16 us
    ppermute x1, starting transfers between devices, per_device(): up = lax.ppermute(last, 'lat', northward)  4.55 us
    pallas_call x3, Pallas kernels, remap_parts(): pl.pallas_call(functools.partial(remap_kernel, counts, tuple(steps), tupl...  4.46 us
    pallas_call x1, Pallas kernels, second_step(): pl.pallas_call(functools.partial(second_kernel, lat_rows), grid=(L,), in_...  3.59 us
    ppermute x10, waiting for transfers between devices, shifted(): lax.ppermute(value, 'sub', [(i, (i + t) % sub_count) for i in range(sub_c...  3.53 us
    pallas_call x1, Pallas kernels, remap_edges(): pl.pallas_call(functools.partial(remap_edge_kernel, counts), in_specs=[VM...  3.23 us
    ppermute x1, waiting for transfers between devices, per_device(): up = lax.ppermute(last, 'lat', northward)  2.3 us
  transfers between devices with their start and end apart: 17, of which 9 were waited for; matrix products, arithmetic and copies ran while one was open for 0% of the time, Pallas kernels for 29%

profile of v23, /device:TPU:0, one launch (start us, length us, event | category | flops | bytes accessed | tf_op | source)
XLA Modules:
  0.0 49.9 jit_solution(1032645816255788464)
XLA Ops:
  0.6 1.9 %first_step.1 = (f32[4,16,1152]{2,1,0:T(8,128)S(1)}, f32[270,128]{1,0:T(8,128)S(1)}, f32[1,4,4,1152]{3,2,1,0:T(4,128)S(1)}, f32[4,16,1152]{2,1,0:T(8,128)S(1)}, ...) custom-call(f32[4,24,128]{2,1,0:T(8,128)} %constant.6.clone.table_hb, ...), custom_call_target="tpu_custom_call" | custom-call | flops 2949120 | bytes 4423680 | tf_op jit(solution)/shard_map/first_step/pallas_call | solution.py:141
  2.5 3.0 %collective-permute-start.1 = (f32[270,128]{1,0:T(8,128)S(1)}, f32[270,128]{1,0:T(8,128)S(1)}, u32[]{:S(2)}, u32[]{:S(2)}) collective-permute-start(f32[270,128]{1,0:T(8,128)S(1)} %get-tuple-element.44), channel_id=1, source_target_pairs={{0,2},{2,0},{1,3},{3,1},{4,6},{6,4},{5,7},{7,5},{8,10},{10,8},{9,1... | collective-permute-start | bytes 414728 | tf_op jit(solution)/shard_map/ppermute | solution.py:698
  5.5 1.3 %inner_step.1 = (f32[5,4,16,1152]{3,2,1,0:T(8,128)S(1)}, f32[64,1152]{1,0:T(8,128)S(1)}) custom-call(f32[4,24,128]{2,1,0:T(8,128)S(1)} %copy-done.2, f32[4,16,1152]{2,1,0:T(8,128)S(1)} %get-tuple-element.36.new_ref, f32[4,16,1152]{2,1,0:T(8,128)S(1)} %get-tuple-element.37.east_ref, f32[4,16,1152]{2,1,0:T(8,128)S(1)} %get-tuple-element.38.north_ref, ...), custom_call_target="tpu_custom_call" | custom-call | flops 9584640 | bytes 4718592 | tf_op jit(solution)/shard_map/inner_step/pallas_call | solution.py:187
  7.0 2.2 %collective-permute-done.1.both_ref = f32[270,128]{1,0:T(8,128)S(1)} collective-permute-done((f32[270,128]{1,0:T(8,128)S(1)}, f32[270,128]{1,0:T(8,128)S(1)}, u32[]{:S(2)}, u32[]{:S(2)}) %collective-permute-start.1) | collective-permute-done | bytes 138272 | tf_op jit(solution)/shard_map/ppermute | solution.py:698
  9.3 1.3 %collective-permute-done.2.refs_1_ = f32[16,1152]{1,0:T(8,128)S(1)} collective-permute-done((f32[16,1152]{1,0:T(8,128)S(1)}, f32[16,1152]{1,0:T(8,128)S(1)}, u32[]{:S(2)}, u32[]{:S(2)}) %collective-permute-start.2) | collective-permute-done | bytes 73760 | tf_op jit(solution)/shard_map/ppermute | solution.py:700
  10.7 1.4 %remap_parts.3.refs_0_ = f32[160,1152]{1,0:T(8,128)S(1)} custom-call(f32[16,8,128]{2,1,0:T(8,128)S(1)} %broadcast_in_dim.4.weight_ref, f32[5,4,16,1152]{3,2,1,0:T(8,128)S(1)} %get-tuple-element.43.refs_0_.refs_2_, f32[5,4,16,1152]{3,2,1,0:T(8,128)S(1)} %collective-permute-done.refs_1_.refs_3_, f32[5,4,16,1152]{3,2,1,0:T(8,128)S(1)} %get-tuple-element.43.refs_0_.refs_2_, ...), custom_call_target="tpu_custom_call" | custom-call | flops 7667712 | bytes 4423680 | tf_op jit(solution)/shard_map/remap_parts/pallas_call | solution.py:521
  12.1 2.4 %collective-permute-start.15 = (f32[160,1152]{1,0:T(8,128)S(1)}, f32[160,1152]{1,0:T(8,128)S(1)}, u32[]{:S(2)}, u32[]{:S(2)}) collective-permute-start(f32[160,1152]{1,0:T(8,128)S(1)} %remap_parts.3.refs_0_), channel_id=1, source_target_pairs={{0,2},{2,0},{1,3},{3,1},{4,6},{6,4},{5,7},{7,5},{8,10},{10,8},{9,1... | collective-permute-start | bytes 2211848 | tf_op jit(solution)/shard_map/ppermute | solution.py:698
  14.5 2.3 %collective-permute-done.3.refs_1_.refs_10_ = f32[64,1152]{1,0:T(8,128)S(1)} collective-permute-done((f32[64,1152]{1,0:T(8,128)S(1)}, f32[64,1152]{1,0:T(8,128)S(1)}, u32[]{:S(2)}, u32[]{:S(2)}) %collective-permute-start.3) | collective-permute-done | bytes 294944 | tf_op jit(solution)/shard_map/ppermute | solution.py:698
  17.3 1.3 %collective-permute-start.5 = (f32[8,4,1,1152]{3,2,1,0:T(1,128)S(1)}, f32[8,4,1,1152]{3,2,1,0:T(1,128)S(1)}, u32[]{:S(2)}, u32[]{:S(2)}) collective-permute-start(f32[8,4,1,1152]{3,2,1,0:T(1,128)S(1)} %get-tuple-element.50), channel_id=1, source_target_pairs={{4,0},{8,4},{12,8},{5,1},{9,5},{13,9},{6,2},{10,6},{14,10},{7,3},{... | collective-permute-start | bytes 442376 | tf_op jit(solution)/shard_map/ppermute | solution.py:747
  18.6 4.6 %collective-permute-start.4 = (f32[6,4,1,1152]{3,2,1,0:T(1,128)S(1)}, f32[6,4,1,1152]{3,2,1,0:T(1,128)S(1)}, u32[]{:S(2)}, u32[]{:S(2)}) collective-permute-start(f32[6,4,1,1152]{3,2,1,0:T(1,128)S(1)} %get-tuple-element.49), channel_id=1, source_target_pairs={{0,4},{4,8},{8,12},{1,5},{5,9},{9,13},{2,6},{6,10},{10,14},{3,7},{... | collective-permute-start | bytes 331784 | tf_op jit(solution)/shard_map/ppermute | solution.py:746
  23.1 2.3 %collective-permute-done.4.up_ref = f32[6,4,1,1152]{3,2,1,0:T(1,128)S(1)} collective-permute-done((f32[6,4,1,1152]{3,2,1,0:T(1,128)S(1)}, f32[6,4,1,1152]{3,2,1,0:T(1,128)S(1)}, u32[]{:S(2)}, u32[]{:S(2)}) %collective-permute-start.4) | collective-permute-done | bytes 110624 | tf_op jit(solution)/shard_map/ppermute | solution.py:746
  25.5 3.6 %second_step.1 = (f32[1,4,16,1152]{3,2,1,0:T(8,128)S(1)}, f32[1,4,16,1152]{3,2,1,0:T(8,128)S(1)}, f32[7,4,2,1152]{3,2,1,0:T(2,128)S(1)}) custom-call(f32[4,24,128]{2,1,0:T(8,128)S(1)} %copy-done.2, f32[4,16,1152]{2,1,0:T(8,128)S(1)} %get-tuple-element.39.thick_ref.thick_any, f32[4,16,1152]{2,1,0:T(8,128)S(1)} %get-tuple-element.40.u_ref.u_any, ...), custom_call_target="tpu_custom_call" | custom-call | flops 503316480 | bytes 3538944 | tf_op jit(solution)/shard_map/second_step/pallas_call | solution.py:325
  30.2 1.3 %remap_parts.4 = (f32[4,4,16,1152]{3,2,1,0:T(8,128)S(1)}, f32[4,16,1152]{2,1,0:T(8,128)S(1)}) custom-call(f32[16,8,128]{2,1,0:T(8,128)S(1)} %broadcast_in_dim.4.weight_ref, f32[5,4,16,1152]{3,2,1,0:T(8,128)S(1)} %get-tuple-element.43.refs_0_.refs_2_, f32[5,4,16,1152]{3,2,1,0:T(8,128)S(1)} %collective-permute-done.refs_1_.refs_3_, ...), custom_call_target="tpu_custom_call" | custom-call | flops 7667712 | bytes 4423680 | tf_op jit(solution)/shard_map/remap_parts/pallas_call | solution.py:521
  31.5 0.7 %collective-permute-done.15.refs_9_.refs_0_ = f32[160,1152]{1,0:T(8,128)S(1)} collective-permute-done((f32[160,1152]{1,0:T(8,128)S(1)}, f32[160,1152]{1,0:T(8,128)S(1)}, u32[]{:S(2)}, u32[]{:S(2)}) %collective-permute-start.15) | collective-permute-done | bytes 737312 | tf_op jit(solution)/shard_map/ppermute | solution.py:698
  32.2 1.8 %remap_parts.5 = (f32[2,4,16,1152]{3,2,1,0:T(8,128)S(1)}, f32[112,1152]{1,0:T(8,128)S(1)}) custom-call(f32[16,8,128]{2,1,0:T(8,128)S(1)} %broadcast_in_dim.4.weight_ref, f32[5,4,16,1152]{3,2,1,0:T(8,128)S(1)} %get-tuple-element.43.refs_0_.refs_2_, f32[5,4,16,1152]{3,2,1,0:T(8,128)S(1)} %collective-permute-done.refs_1_.refs_3_, ...), custom_call_target="tpu_custom_call" | custom-call | flops 10616832 | bytes 3538944 | tf_op jit(solution)/shard_map/remap_parts/pallas_call | solution.py:521
  33.9 1.2 %collective-permute-start.16 = (f32[112,1152]{1,0:T(8,128)S(1)}, f32[112,1152]{1,0:T(8,128)S(1)}, u32[]{:S(2)}, u32[]{:S(2)}) collective-permute-start(f32[112,1152]{1,0:T(8,128)S(1)} %get-tuple-element.57.refs_12_), channel_id=1, source_target_pairs={{0,2},{2,0},{1,3},{3,1},{4,6},{6,4},{5,7},{7,5},{8,10},{10,8},{9,1... | collective-permute-start | bytes 1548296 | tf_op jit(solution)/shard_map/ppermute | solution.py:698
  35.1 0.5 %collective-permute-start.10 = (f32[1,4,4,1152]{3,2,1,0:T(4,128)S(1)}, f32[1,4,4,1152]{3,2,1,0:T(4,128)S(1)}, u32[]{:S(2)}, u32[]{:S(2)}) collective-permute-start(f32[1,4,4,1152]{3,2,1,0:T(4,128)S(1)} %get-tuple-element.54.refs_6_), channel_id=1, source_target_pairs={{0,1},{1,0},{2,3},{3,2},{4,5},{5,4},{6,7},{7,6},{8,9},{9,8},{10,11... | collective-permute-start | bytes 221192 | tf_op jit(solution)/shard_map/ppermute | solution.py:700
  35.6 0.8 %collective-permute-done.9.refs_5_ = f32[1,4,4,1152]{3,2,1,0:T(4,128)S(1)} collective-permute-done((f32[1,4,4,1152]{3,2,1,0:T(4,128)S(1)}, f32[1,4,4,1152]{3,2,1,0:T(4,128)S(1)}, u32[]{:S(2)}, u32[]{:S(2)}) %collective-permute-start.9) | collective-permute-done | bytes 73760 | tf_op jit(solution)/shard_map/ppermute | solution.py:700
  36.9 1.9 %collective-permute-done.7.refs_2_ = f32[7,4,2,1152]{3,2,1,0:T(2,128)S(1)} collective-permute-done((f32[7,4,2,1152]{3,2,1,0:T(2,128)S(1)}, f32[7,4,2,1152]{3,2,1,0:T(2,128)S(1)}, u32[]{:S(2)}, u32[]{:S(2)}) %collective-permute-start.7) | collective-permute-done | bytes 258080 | tf_op jit(solution)/shard_map/ppermute | solution.py:698
  38.8 1.5 %collective-permute-done.8.refs_3_ = f32[7,4,2,1152]{3,2,1,0:T(2,128)S(1)} collective-permute-done((f32[7,4,2,1152]{3,2,1,0:T(2,128)S(1)}, f32[7,4,2,1152]{3,2,1,0:T(2,128)S(1)}, u32[]{:S(2)}, u32[]{:S(2)}) %collective-permute-start.8) | collective-permute-done | bytes 258080 | tf_op jit(solution)/shard_map/ppermute | solution.py:700
  40.3 3.2 %remap_edges.1 = (f32[6,4,2,1152]{3,2,1,0:T(2,128)S(1)}, f32[4,2,1152]{2,1,0:T(2,128)S(1)}, f32[4,4,4,1152]{3,2,1,0:T(4,128)S(1)}) custom-call(f32[16,8,128]{2,1,0:T(8,128)S(1)} %broadcast_in_dim.4.weight_ref, f32[7,4,2,1152]{3,2,1,0:T(2,128)S(1)} %get-tuple-element.51.refs_6_.refs_0_, f32[7,4,2,1152]{3,2,1,0:T(2,128)S(1)} %collective-permute-done.6.refs_1_, ...), custom_call_target="tpu_custom_call" | custom-call | flops 5898240 | bytes 3096576 | tf_op jit(solution)/shard_map/remap_edges/pallas_call | solution.py:559
  43.5 1.4 %finish_tracers.1 = (f32[4,4,16,1152]{3,2,1,0:T(8,128)}, f32[4,16,1152]{2,1,0:T(8,128)}, f32[8,128]{1,0:T(8,128)S(1)}) custom-call(f32[4,4,16,1152]{3,2,1,0:T(8,128)S(1)} %get-tuple-element.52.refs_8_.own_ref, f32[4,4,4,1152]{3,2,1,0:T(4,128)S(1)} %get-tuple-element.58.near_ref, f32[6,4,2,1152]{3,2,1,0:T(2,128)S(1)} %get-tuple-element.59.edge_ref, ...), custom_call_target="tpu_custom_call" | custom-call | flops 589824 | bytes 3538944 | tf_op jit(solution)/shard_map/finish_tracers/pallas_call | solution.py:597
  45.0 4.0 %collective-permute-done.16.refs_0_ = f32[112,1152]{1,0:T(8,128)S(1)} collective-permute-done((f32[112,1152]{1,0:T(8,128)S(1)}, f32[112,1152]{1,0:T(8,128)S(1)}, u32[]{:S(2)}, u32[]{:S(2)}) %collective-permute-start.16) | collective-permute-done | bytes 516128 | tf_op jit(solution)/shard_map/ppermute | solution.py:698
  49.0 0.9 %finish_winds.1 = (f32[4,16,1152]{2,1,0:T(8,128)}, f32[4,16,1152]{2,1,0:T(8,128)}) custom-call(f32[2,4,16,1152]{3,2,1,0:T(8,128)S(1)} %get-tuple-element.63.own_ref, f32[6,4,2,1152]{3,2,1,0:T(2,128)S(1)} %get-tuple-element.59.edge_ref, f32[112,1152]{1,0:T(8,128)S(1)} %collective-permute-done.16.refs_0_, f32[8,128]{1,0:T(8,128)S(1)} %get-tuple-element.64.refs_1_), custom_call_target="tpu_custom_call" | custom-call | flops 147456 | bytes 1769472 | tf_op jit(solution)/shard_map/finish_winds/pallas_call | solution.py:635
  (34 shorter events, 2.5 us)
Async XLA Ops:
  0.6 4.9 %copy-start.2 = (f32[4,24,128]{2,1,0:T(8,128)S(1)}, f32[4,24,128]{2,1,0:T(8,128)}, u32[]{:S(2)}) copy-start(f32[4,24,128]{2,1,0:T(8,128)} %constant.6.clone.table_hbm.table_ref) | copy-start | bytes 147460
  2.5 6.7 %collective-permute-start.1 = (f32[270,128]{1,0:T(8,128)S(1)}, f32[270,128]{1,0:T(8,128)S(1)}, u32[]{:S(2)}, u32[]{:S(2)}) collective-permute-start(f32[270,128]{1,0:T(8,128)S(1)} %get-tuple-element.44), channel_id=1, source_target_pairs={{0,2},{2,0},{1,3},{3,1},{4,6},{6,4},{5,7},{7,5},{8,10},{10,8},{9,1... | collective-permute-start | bytes 414728 | tf_op jit(solution)/shard_map/ppermute | solution.py:698
  6.8 3.7 %collective-permute-start = (f32[5,4,16,1152]{3,2,1,0:T(8,128)S(1)}, f32[5,4,16,1152]{3,2,1,0:T(8,128)S(1)}, u32[]{:S(2)}, u32[]{:S(2)}) collective-permute-start(f32[5,4,16,1152]{3,2,1,0:T(8,128)S(1)} %get-tuple-element.43.refs_0_.refs_2_), channel_id=1, source_target_pairs={{0,1},{1,0},{2,3},{3,2},{4,5},{5,4},{6,7},{7,6},{8,9},{9,8},{10,11... | collective-permute-start | bytes 4423688 | tf_op jit(solution)/shard_map/ppermute | solution.py:700
  6.9 3.7 %copy-start.3 = (f32[16]{0:T(128)S(1)}, f32[16]{0:T(128)}, u32[]{:S(2)}) copy-start(f32[16]{0:T(128)} %param.13) | copy-start | bytes 196
  6.9 9.9 %collective-permute-start.3 = (f32[64,1152]{1,0:T(8,128)S(1)}, f32[64,1152]{1,0:T(8,128)S(1)}, u32[]{:S(2)}, u32[]{:S(2)}) collective-permute-start(f32[64,1152]{1,0:T(8,128)S(1)} %get-tuple-element.45.refs_0_.refs_8_), channel_id=1, source_target_pairs={{0,2},{2,0},{1,3},{3,1},{4,6},{6,4},{5,7},{7,5},{8,10},{10,8},{9,1... | collective-permute-start | bytes 884744 | tf_op jit(solution)/shard_map/ppermute | solution.py:698
  9.2 1.3 %collective-permute-start.2 = (f32[16,1152]{1,0:T(8,128)S(1)}, f32[16,1152]{1,0:T(8,128)S(1)}, u32[]{:S(2)}, u32[]{:S(2)}) collective-permute-start(f32[16,1152]{1,0:T(8,128)S(1)} %get-tuple-element.46.refs_0_), channel_id=1, source_target_pairs={{0,1},{1,0},{2,3},{3,2},{4,5},{5,4},{6,7},{7,6},{8,9},{9,8},{10,11... | collective-permute-start | bytes 221192 | tf_op jit(solution)/shard_map/ppermute | solution.py:700
  12.1 13.4 %copy-start.4 = (s32[16]{0:T(128)S(1)}, s32[16]{0:T(128)}, u32[]{:S(2)}) copy-start(s32[16]{0:T(128)} %param.14) | copy-start | bytes 196
  12.1 13.4 %copy-start = (bf16[5,256,256]{2,1,0:T(8,128)(2,1)S(1)}, bf16[5,256,256]{2,1,0:T(8,128)(2,1)}, u32[]{:S(2)}) copy-start(bf16[5,256,256]{2,1,0:T(8,128)(2,1)} %constant.7.clone.high_ref) | copy-start | bytes 1966084
  12.1 13.4 %copy-start.1 = (bf16[5,256,256]{2,1,0:T(8,128)(2,1)S(1)}, bf16[5,256,256]{2,1,0:T(8,128)(2,1)}, u32[]{:S(2)}) copy-start(bf16[5,256,256]{2,1,0:T(8,128)(2,1)} %constant.8.clone.low_ref) | copy-start | bytes 1966084
  12.1 20.0 %collective-permute-start.15 = (f32[160,1152]{1,0:T(8,128)S(1)}, f32[160,1152]{1,0:T(8,128)S(1)}, u32[]{:S(2)}, u32[]{:S(2)}) collective-permute-start(f32[160,1152]{1,0:T(8,128)S(1)} %remap_parts.3.refs_0_), channel_id=1, source_target_pairs={{0,2},{2,0},{1,3},{3,1},{4,6},{6,4},{5,7},{7,5},{8,10},{10,8},{9,1... | collective-permute-start | bytes 2211848 | tf_op jit(solution)/shard_map/ppermute | solution.py:698
  17.3 8.2 %collective-permute-start.5 = (f32[8,4,1,1152]{3,2,1,0:T(1,128)S(1)}, f32[8,4,1,1152]{3,2,1,0:T(1,128)S(1)}, u32[]{:S(2)}, u32[]{:S(2)}) collective-permute-start(f32[8,4,1,1152]{3,2,1,0:T(1,128)S(1)} %get-tuple-element.50), channel_id=1, source_target_pairs={{4,0},{8,4},{12,8},{5,1},{9,5},{13,9},{6,2},{10,6},{14,10},{7,3},{... | collective-permute-start | bytes 442376 | tf_op jit(solution)/shard_map/ppermute | solution.py:747
  18.6 6.9 %collective-permute-start.4 = (f32[6,4,1,1152]{3,2,1,0:T(1,128)S(1)}, f32[6,4,1,1152]{3,2,1,0:T(1,128)S(1)}, u32[]{:S(2)}, u32[]{:S(2)}) collective-permute-start(f32[6,4,1,1152]{3,2,1,0:T(1,128)S(1)} %get-tuple-element.49), channel_id=1, source_target_pairs={{0,4},{4,8},{8,12},{1,5},{5,9},{9,13},{2,6},{6,10},{10,14},{3,7},{... | collective-permute-start | bytes 331784 | tf_op jit(solution)/shard_map/ppermute | solution.py:746
  29.1 2.4 %collective-permute-start.13 = (f32[1,4,16,1152]{3,2,1,0:T(8,128)S(1)}, f32[1,4,16,1152]{3,2,1,0:T(8,128)S(1)}, u32[]{:S(2)}, u32[]{:S(2)}) collective-permute-start(f32[1,4,16,1152]{3,2,1,0:T(8,128)S(1)} %get-tuple-element.55.refs_2_), channel_id=1, source_target_pairs={{0,1},{1,0},{2,3},{3,2},{4,5},{5,4},{6,7},{7,6},{8,9},{9,8},{10,11... | collective-permute-start | bytes 884744 | tf_op jit(solution)/shard_map/ppermute | solution.py:700
  29.2 2.3 %collective-permute-start.14 = (f32[1,4,16,1152]{3,2,1,0:T(8,128)S(1)}, f32[1,4,16,1152]{3,2,1,0:T(8,128)S(1)}, u32[]{:S(2)}, u32[]{:S(2)}) collective-permute-start(f32[1,4,16,1152]{3,2,1,0:T(8,128)S(1)} %get-tuple-element.56.refs_4_), channel_id=1, source_target_pairs={{0,1},{1,0},{2,3},{3,2},{4,5},{5,4},{6,7},{7,6},{8,9},{9,8},{10,11... | collective-permute-start | bytes 884744 | tf_op jit(solution)/shard_map/ppermute | solution.py:700
  29.7 9.1 %collective-permute-start.7 = (f32[7,4,2,1152]{3,2,1,0:T(2,128)S(1)}, f32[7,4,2,1152]{3,2,1,0:T(2,128)S(1)}, u32[]{:S(2)}, u32[]{:S(2)}) collective-permute-start(f32[7,4,2,1152]{3,2,1,0:T(2,128)S(1)} %get-tuple-element.51.refs_6_.refs_0_), channel_id=1, source_target_pairs={{0,2},{2,0},{1,3},{3,1},{4,6},{6,4},{5,7},{7,5},{8,10},{10,8},{9,1... | collective-permute-start | bytes 774152 | tf_op jit(solution)/shard_map/ppermute | solution.py:698
  33.9 15.0 %collective-permute-start.16 = (f32[112,1152]{1,0:T(8,128)S(1)}, f32[112,1152]{1,0:T(8,128)S(1)}, u32[]{:S(2)}, u32[]{:S(2)}) collective-permute-start(f32[112,1152]{1,0:T(8,128)S(1)} %get-tuple-element.57.refs_12_), channel_id=1, source_target_pairs={{0,2},{2,0},{1,3},{3,1},{4,6},{6,4},{5,7},{7,5},{8,10},{10,8},{9,1... | collective-permute-start | bytes 1548296 | tf_op jit(solution)/shard_map/ppermute | solution.py:698
  35.1 1.3 %collective-permute-start.9 = (f32[1,4,4,1152]{3,2,1,0:T(4,128)S(1)}, f32[1,4,4,1152]{3,2,1,0:T(4,128)S(1)}, u32[]{:S(2)}, u32[]{:S(2)}) collective-permute-start(f32[1,4,4,1152]{3,2,1,0:T(4,128)S(1)} %get-tuple-element.53.refs_4_), channel_id=1, source_target_pairs={{0,1},{1,0},{2,3},{3,2},{4,5},{5,4},{6,7},{7,6},{8,9},{9,8},{10,11... | collective-permute-start | bytes 221192 | tf_op jit(solution)/shard_map/ppermute | solution.py:700
  35.1 1.4 %collective-permute-start.10 = (f32[1,4,4,1152]{3,2,1,0:T(4,128)S(1)}, f32[1,4,4,1152]{3,2,1,0:T(4,128)S(1)}, u32[]{:S(2)}, u32[]{:S(2)}) collective-permute-start(f32[1,4,4,1152]{3,2,1,0:T(4,128)S(1)} %get-tuple-element.54.refs_6_), channel_id=1, source_target_pairs={{0,1},{1,0},{2,3},{3,2},{4,5},{5,4},{6,7},{7,6},{8,9},{9,8},{10,11... | collective-permute-start | bytes 221192 | tf_op jit(solution)/shard_map/ppermute | solution.py:700
  35.6 3.2 %collective-permute-start.11 = (f32[64,1152]{1,0:T(8,128)S(1)}, f32[64,1152]{1,0:T(8,128)S(1)}, u32[]{:S(2)}, u32[]{:S(2)}) collective-permute-start(f32[64,1152]{1,0:T(8,128)S(1)} %get-tuple-element.45.refs_0_.refs_8_), channel_id=1, source_target_pairs={{0,1},{1,0},{2,3},{3,2},{4,5},{5,4},{6,7},{7,6},{8,9},{9,8},{10,11... | collective-permute-start | bytes 884744 | tf_op jit(solution)/shard_map/ppermute | solution.py:700
  36.4 2.4 %collective-permute-start.12 = (f32[64,1152]{1,0:T(8,128)S(1)}, f32[64,1152]{1,0:T(8,128)S(1)}, u32[]{:S(2)}, u32[]{:S(2)}) collective-permute-start(f32[64,1152]{1,0:T(8,128)S(1)} %collective-permute-done.3.refs_1_.refs_10_), channel_id=1, source_target_pairs={{0,1},{1,0},{2,3},{3,2},{4,5},{5,4},{6,7},{7,6},{8,9},{9,8},{10,11... | collective-permute-start | bytes 884744 | tf_op jit(solution)/shard_map/ppermute | solution.py:700
  36.5 2.3 %collective-permute-start.6 = (f32[7,4,2,1152]{3,2,1,0:T(2,128)S(1)}, f32[7,4,2,1152]{3,2,1,0:T(2,128)S(1)}, u32[]{:S(2)}, u32[]{:S(2)}) collective-permute-start(f32[7,4,2,1152]{3,2,1,0:T(2,128)S(1)} %get-tuple-element.51.refs_6_.refs_0_), channel_id=1, source_target_pairs={{0,1},{1,0},{2,3},{3,2},{4,5},{5,4},{6,7},{7,6},{8,9},{9,8},{10,11... | collective-permute-start | bytes 774152 | tf_op jit(solution)/shard_map/ppermute | solution.py:700
  38.8 1.5 %collective-permute-start.8 = (f32[7,4,2,1152]{3,2,1,0:T(2,128)S(1)}, f32[7,4,2,1152]{3,2,1,0:T(2,128)S(1)}, u32[]{:S(2)}, u32[]{:S(2)}) collective-permute-start(f32[7,4,2,1152]{3,2,1,0:T(2,128)S(1)} %collective-permute-done.7.refs_2_), channel_id=1, source_target_pairs={{0,1},{1,0},{2,3},{3,2},{4,5},{5,4},{6,7},{7,6},{8,9},{9,8},{10,11... | collective-permute-start | bytes 774152 | tf_op jit(solution)/shard_map/ppermute | solution.py:700

commit v24 on v21

--- a/solution.py
+++ b/solution.py
@@ -624,20 +624,20 @@
                 total = total + pltpu.roll(ref[first : first + size], (1 - (start - first)) % size, 0)[0:R]
             total = jnp.where(row == 0, edge_ref[f, i, 0:1], jnp.where(row == R - 1, edge_ref[f, i, 1:2], total))
             result_ref[f, i] = total
-            copies.append(pltpu.make_async_copy(result_ref.at[f, i], out_ref.at[i], sems.at[f, i]))
-            copies[-1].start()
+        copies.append(pltpu.make_async_copy(result_ref.at[f], out_ref, sems.at[f]))
+        copies[-1].start()
     for copy in copies:
         copy.wait()
 
 
 def finish_winds(own, arrived, edge, wait):
-    F, L = own.shape[:2]
+    F = own.shape[0]
     return pl.pallas_call(
         functools.partial(finish_winds_kernel, len(arrived)),
         in_specs=[VMEM] * (2 + len(arrived)) + after(wait),
         out_specs=[pl.BlockSpec(memory_space=pl.ANY)] * F,
         out_shape=[jax.ShapeDtypeStruct(own.shape[1:], jnp.float32)] * F,
-        scratch_shapes=[pltpu.VMEM(own.shape, jnp.float32), pltpu.SemaphoreType.DMA((F, L))],
+        scratch_shapes=[pltpu.VMEM(own.shape, jnp.float32), pltpu.SemaphoreType.DMA((F,))],
         compiler_params=params(),
         cost_estimate=cost(own.size, 12 * own.size),
         name="finish_winds",

time: 49.9 us -> 49.9 us (level)
  no operation moved by 1% of the time
where the time goes in v24:
time: 49.9 us; the launch traced here: 49.7 us
  Pallas kernels  17.8 us (36%)
  waiting for transfers between devices  15.7 us (31%)
  starting transfers between devices  15.3 us (31%)
  between operations  0.82 us (2%)
    ppermute x5, waiting for transfers between devices, shifted(): lax.ppermute(value, 'lev', [(i, (i + s) % lev_count) for i in range(lev_c...  10.4 us
    ppermute x5, starting transfers between devices, shifted(): lax.ppermute(value, 'lev', [(i, (i + s) % lev_count) for i in range(lev_c...  7.62 us
    ppermute x1, starting transfers between devices, per_device(): up = lax.ppermute(last, 'lat', northward)  4.55 us
    pallas_call x3, Pallas kernels, remap_parts(): pl.pallas_call(functools.partial(remap_kernel, counts, tuple(steps), tupl...  4.48 us
    pallas_call x1, Pallas kernels, remap_edges(): pl.pallas_call(functools.partial(remap_edge_kernel, counts), in_specs=[VM...  3.71 us
    pallas_call x1, Pallas kernels, second_step(): pl.pallas_call(functools.partial(second_kernel, lat_rows), grid=(L,), in_...  3.58 us
    ppermute x10, waiting for transfers between devices, shifted(): lax.ppermute(value, 'sub', [(i, (i + t) % sub_count) for i in range(sub_c...  2.93 us
    ppermute x1, waiting for transfers between devices, per_device(): up = lax.ppermute(last, 'lat', northward)  2.3 us
  transfers between devices with their start and end apart: 17, of which 9 were waited for; matrix products, arithmetic and copies ran while one was open for 0% of the time, Pallas kernels for 30%

profile of v24, /device:TPU:0, one launch (start us, length us, event | category | flops | bytes accessed | tf_op | source)
XLA Modules:
  0.0 49.7 jit_solution(6068924186037228722)
XLA Ops:
  0.6 1.9 %first_step.1 = (f32[4,16,1152]{2,1,0:T(8,128)S(1)}, f32[234,128]{1,0:T(8,128)S(1)}, f32[1,4,3,1152]{3,2,1,0:T(4,128)S(1)}, f32[4,16,1152]{2,1,0:T(8,128)S(1)}, ...) custom-call(f32[4,24,128]{2,1,0:T(8,128)} %constant.6.clone.table_hb, ...), custom_call_target="tpu_custom_call" | custom-call | flops 2949120 | bytes 4423680 | tf_op jit(solution)/shard_map/first_step/pallas_call | solution.py:141
  2.5 3.0 %collective-permute-start.1 = (f32[234,128]{1,0:T(8,128)S(1)}, f32[234,128]{1,0:T(8,128)S(1)}, u32[]{:S(2)}, u32[]{:S(2)}) collective-permute-start(f32[234,128]{1,0:T(8,128)S(1)} %get-tuple-element.44), channel_id=1, source_target_pairs={{0,2},{2,0},{1,3},{3,1},{4,6},{6,4},{5,7},{7,5},{8,10},{10,8},{9,1... | collective-permute-start | bytes 359432 | tf_op jit(solution)/shard_map/ppermute | solution.py:698
  5.5 1.3 %inner_step.1 = (f32[5,4,16,1152]{3,2,1,0:T(8,128)S(1)}, f32[48,1152]{1,0:T(8,128)S(1)}) custom-call(f32[4,24,128]{2,1,0:T(8,128)S(1)} %copy-done.2, f32[4,16,1152]{2,1,0:T(8,128)S(1)} %get-tuple-element.36.new_ref, f32[4,16,1152]{2,1,0:T(8,128)S(1)} %get-tuple-element.37.east_ref, f32[4,16,1152]{2,1,0:T(8,128)S(1)} %get-tuple-element.38.north_ref, ...), custom_call_target="tpu_custom_call" | custom-call | flops 9584640 | bytes 4718592 | tf_op jit(solution)/shard_map/inner_step/pallas_call | solution.py:187
  7.1 1.8 %collective-permute-done.1.both_ref = f32[234,128]{1,0:T(8,128)S(1)} collective-permute-done((f32[234,128]{1,0:T(8,128)S(1)}, f32[234,128]{1,0:T(8,128)S(1)}, u32[]{:S(2)}, u32[]{:S(2)}) %collective-permute-start.1) | collective-permute-done | bytes 119840 | tf_op jit(solution)/shard_map/ppermute | solution.py:698
  9.0 1.3 %collective-permute-done.2.refs_1_ = f32[16,1152]{1,0:T(8,128)S(1)} collective-permute-done((f32[16,1152]{1,0:T(8,128)S(1)}, f32[16,1152]{1,0:T(8,128)S(1)}, u32[]{:S(2)}, u32[]{:S(2)}) %collective-permute-start.2) | collective-permute-done | bytes 73760 | tf_op jit(solution)/shard_map/ppermute | solution.py:700
  10.4 1.4 %remap_parts.3.refs_0_ = f32[176,1152]{1,0:T(8,128)S(1)} custom-call(f32[16,8,128]{2,1,0:T(8,128)S(1)} %broadcast_in_dim.4.weight_ref, f32[5,4,16,1152]{3,2,1,0:T(8,128)S(1)} %get-tuple-element.43.refs_0_.refs_2_, f32[5,4,16,1152]{3,2,1,0:T(8,128)S(1)} %collective-permute-done.refs_1_.refs_3_, f32[5,4,16,1152]{3,2,1,0:T(8,128)S(1)} %get-tuple-element.43.refs_0_.refs_2_, ...), custom_call_target="tpu_custom_call" | custom-call | flops 7667712 | bytes 4423680 | tf_op jit(solution)/shard_map/remap_parts/pallas_call | solution.py:521
  11.9 2.0 %collective-permute-start.15 = (f32[176,1152]{1,0:T(8,128)S(1)}, f32[176,1152]{1,0:T(8,128)S(1)}, u32[]{:S(2)}, u32[]{:S(2)}) collective-permute-start(f32[176,1152]{1,0:T(8,128)S(1)} %remap_parts.3.refs_0_), channel_id=1, source_target_pairs={{0,2},{2,0},{1,3},{3,1},{4,6},{6,4},{5,7},{7,5},{8,10},{10,8},{9,1... | collective-permute-start | bytes 2433032 | tf_op jit(solution)/shard_map/ppermute | solution.py:698
  13.8 1.0 %collective-permute-done.3.refs_1_.refs_10_ = f32[48,1152]{1,0:T(8,128)S(1)} collective-permute-done((f32[48,1152]{1,0:T(8,128)S(1)}, f32[48,1152]{1,0:T(8,128)S(1)}, u32[]{:S(2)}, u32[]{:S(2)}) %collective-permute-start.3) | collective-permute-done | bytes 221216 | tf_op jit(solution)/shard_map/ppermute | solution.py:698
  15.2 1.3 %collective-permute-start.5 = (f32[8,4,1,1152]{3,2,1,0:T(1,128)S(1)}, f32[8,4,1,1152]{3,2,1,0:T(1,128)S(1)}, u32[]{:S(2)}, u32[]{:S(2)}) collective-permute-start(f32[8,4,1,1152]{3,2,1,0:T(1,128)S(1)} %get-tuple-element.50), channel_id=1, source_target_pairs={{4,0},{8,4},{12,8},{5,1},{9,5},{13,9},{6,2},{10,6},{14,10},{7,3},{... | collective-permute-start | bytes 442376 | tf_op jit(solution)/shard_map/ppermute | solution.py:747
  16.5 4.6 %collective-permute-start.4 = (f32[6,4,1,1152]{3,2,1,0:T(1,128)S(1)}, f32[6,4,1,1152]{3,2,1,0:T(1,128)S(1)}, u32[]{:S(2)}, u32[]{:S(2)}) collective-permute-start(f32[6,4,1,1152]{3,2,1,0:T(1,128)S(1)} %get-tuple-element.49), channel_id=1, source_target_pairs={{0,4},{4,8},{8,12},{1,5},{5,9},{9,13},{2,6},{6,10},{10,14},{3,7},{... | collective-permute-start | bytes 331784 | tf_op jit(solution)/shard_map/ppermute | solution.py:746
  21.1 2.3 %collective-permute-done.4.up_ref = f32[6,4,1,1152]{3,2,1,0:T(1,128)S(1)} collective-permute-done((f32[6,4,1,1152]{3,2,1,0:T(1,128)S(1)}, f32[6,4,1,1152]{3,2,1,0:T(1,128)S(1)}, u32[]{:S(2)}, u32[]{:S(2)}) %collective-permute-start.4) | collective-permute-done | bytes 110624 | tf_op jit(solution)/shard_map/ppermute | solution.py:746
  23.5 3.6 %second_step.1 = (f32[1,4,16,1152]{3,2,1,0:T(8,128)S(1)}, f32[1,4,16,1152]{3,2,1,0:T(8,128)S(1)}, f32[7,4,2,1152]{3,2,1,0:T(2,128)S(1)}) custom-call(f32[4,24,128]{2,1,0:T(8,128)S(1)} %copy-done.2, f32[4,16,1152]{2,1,0:T(8,128)S(1)} %get-tuple-element.39.thick_ref.thick_any, f32[4,16,1152]{2,1,0:T(8,128)S(1)} %get-tuple-element.40.u_ref.u_any, ...), custom_call_target="tpu_custom_call" | custom-call | flops 503316480 | bytes 3538944 | tf_op jit(solution)/shard_map/second_step/pallas_call | solution.py:325
  27.7 0.6 %collective-permute-start.7 = (f32[7,4,2,1152]{3,2,1,0:T(2,128)S(1)}, f32[7,4,2,1152]{3,2,1,0:T(2,128)S(1)}, u32[]{:S(2)}, u32[]{:S(2)}) collective-permute-start(f32[7,4,2,1152]{3,2,1,0:T(2,128)S(1)} %get-tuple-element.51.refs_6_.refs_0_), channel_id=1, source_target_pairs={{0,2},{2,0},{1,3},{3,1},{4,6},{6,4},{5,7},{7,5},{8,10},{10,8},{9,1... | collective-permute-start | bytes 774152 | tf_op jit(solution)/shard_map/ppermute | solution.py:698
  28.2 1.3 %remap_parts.4 = (f32[4,4,16,1152]{3,2,1,0:T(8,128)S(1)}, f32[4,16,1152]{2,1,0:T(8,128)S(1)}) custom-call(f32[16,8,128]{2,1,0:T(8,128)S(1)} %broadcast_in_dim.4.weight_ref, f32[5,4,16,1152]{3,2,1,0:T(8,128)S(1)} %get-tuple-element.43.refs_0_.refs_2_, f32[5,4,16,1152]{3,2,1,0:T(8,128)S(1)} %collective-permute-done.refs_1_.refs_3_, ...), custom_call_target="tpu_custom_call" | custom-call | flops 7667712 | bytes 4423680 | tf_op jit(solution)/shard_map/remap_parts/pallas_call | solution.py:521
  29.6 3.2 %collective-permute-done.15.refs_9_.refs_0_ = f32[176,1152]{1,0:T(8,128)S(1)} collective-permute-done((f32[176,1152]{1,0:T(8,128)S(1)}, f32[176,1152]{1,0:T(8,128)S(1)}, u32[]{:S(2)}, u32[]{:S(2)}) %collective-permute-start.15) | collective-permute-done | bytes 811040 | tf_op jit(solution)/shard_map/ppermute | solution.py:698
  32.8 1.8 %remap_parts.5 = (f32[2,4,16,1152]{3,2,1,0:T(8,128)S(1)}, f32[112,1152]{1,0:T(8,128)S(1)}) custom-call(f32[16,8,128]{2,1,0:T(8,128)S(1)} %broadcast_in_dim.4.weight_ref, f32[5,4,16,1152]{3,2,1,0:T(8,128)S(1)} %get-tuple-element.43.refs_0_.refs_2_, f32[5,4,16,1152]{3,2,1,0:T(8,128)S(1)} %collective-permute-done.refs_1_.refs_3_, ...), custom_call_target="tpu_custom_call" | custom-call | flops 10616832 | bytes 3538944 | tf_op jit(solution)/shard_map/remap_parts/pallas_call | solution.py:521
  34.6 2.0 %collective-permute-start.16 = (f32[112,1152]{1,0:T(8,128)S(1)}, f32[112,1152]{1,0:T(8,128)S(1)}, u32[]{:S(2)}, u32[]{:S(2)}) collective-permute-start(f32[112,1152]{1,0:T(8,128)S(1)} %get-tuple-element.57.refs_12_), channel_id=1, source_target_pairs={{0,2},{2,0},{1,3},{3,1},{4,6},{6,4},{5,7},{7,5},{8,10},{10,8},{9,1... | collective-permute-start | bytes 1548296 | tf_op jit(solution)/shard_map/ppermute | solution.py:698
  37.1 1.3 %collective-permute-done.7.refs_2_ = f32[7,4,2,1152]{3,2,1,0:T(2,128)S(1)} collective-permute-done((f32[7,4,2,1152]{3,2,1,0:T(2,128)S(1)}, f32[7,4,2,1152]{3,2,1,0:T(2,128)S(1)}, u32[]{:S(2)}, u32[]{:S(2)}) %collective-permute-start.7) | collective-permute-done | bytes 258080 | tf_op jit(solution)/shard_map/ppermute | solution.py:698
  38.3 0.5 %collective-permute-start.11 = (f32[48,1152]{1,0:T(8,128)S(1)}, f32[48,1152]{1,0:T(8,128)S(1)}, u32[]{:S(2)}, u32[]{:S(2)}) collective-permute-start(f32[48,1152]{1,0:T(8,128)S(1)} %get-tuple-element.45.refs_0_.refs_8_), channel_id=1, source_target_pairs={{0,1},{1,0},{2,3},{3,2},{4,5},{5,4},{6,7},{7,6},{8,9},{9,8},{10,11... | collective-permute-start | bytes 663560 | tf_op jit(solution)/shard_map/ppermute | solution.py:700
  38.9 1.3 %collective-permute-done.11.refs_9_ = f32[48,1152]{1,0:T(8,128)S(1)} collective-permute-done((f32[48,1152]{1,0:T(8,128)S(1)}, f32[48,1152]{1,0:T(8,128)S(1)}, u32[]{:S(2)}, u32[]{:S(2)}) %collective-permute-start.11) | collective-permute-done | bytes 221216 | tf_op jit(solution)/shard_map/ppermute | solution.py:700
  40.5 3.7 %remap_edges.1 = (f32[6,4,2,1152]{3,2,1,0:T(2,128)S(1)}, f32[4,2,1152]{2,1,0:T(2,128)S(1)}, f32[4,4,3,1152]{3,2,1,0:T(4,128)S(1)}) custom-call(f32[16,8,128]{2,1,0:T(8,128)S(1)} %broadcast_in_dim.4.weight_ref, f32[7,4,2,1152]{3,2,1,0:T(2,128)S(1)} %get-tuple-element.51.refs_6_.refs_0_, f32[7,4,2,1152]{3,2,1,0:T(2,128)S(1)} %collective-permute-done.6.refs_1_, ...), custom_call_target="tpu_custom_call" | custom-call | flops 5898240 | bytes 3096576 | tf_op jit(solution)/shard_map/remap_edges/pallas_call | solution.py:559
  44.2 1.4 %finish_tracers.1 = (f32[4,4,16,1152]{3,2,1,0:T(8,128)}, f32[4,16,1152]{2,1,0:T(8,128)}, f32[8,128]{1,0:T(8,128)S(1)}) custom-call(f32[4,4,16,1152]{3,2,1,0:T(8,128)S(1)} %get-tuple-element.52.refs_8_.own_ref, f32[4,4,3,1152]{3,2,1,0:T(4,128)S(1)} %get-tuple-element.58.near_ref, f32[6,4,2,1152]{3,2,1,0:T(2,128)S(1)} %get-tuple-element.59.edge_ref, ...), custom_call_target="tpu_custom_call" | custom-call | flops 589824 | bytes 3538944 | tf_op jit(solution)/shard_map/finish_tracers/pallas_call | solution.py:597
  45.7 3.1 %collective-permute-done.16.refs_0_ = f32[112,1152]{1,0:T(8,128)S(1)} collective-permute-done((f32[112,1152]{1,0:T(8,128)S(1)}, f32[112,1152]{1,0:T(8,128)S(1)}, u32[]{:S(2)}, u32[]{:S(2)}) %collective-permute-start.16) | collective-permute-done | bytes 516128 | tf_op jit(solution)/shard_map/ppermute | solution.py:698
  48.8 0.9 %finish_winds.1 = (f32[4,16,1152]{2,1,0:T(8,128)}, f32[4,16,1152]{2,1,0:T(8,128)}) custom-call(f32[2,4,16,1152]{3,2,1,0:T(8,128)S(1)} %get-tuple-element.63.own_ref, f32[6,4,2,1152]{3,2,1,0:T(2,128)S(1)} %get-tuple-element.59.edge_ref, f32[112,1152]{1,0:T(8,128)S(1)} %collective-permute-done.16.refs_0_, f32[8,128]{1,0:T(8,128)S(1)} %get-tuple-element.64.refs_1_), custom_call_target="tpu_custom_call" | custom-call | flops 147456 | bytes 1769472 | tf_op jit(solution)/shard_map/finish_winds/pallas_call | solution.py:635
  (34 shorter events, 2.4 us)
Async XLA Ops:
  0.6 4.9 %copy-start.2 = (f32[4,24,128]{2,1,0:T(8,128)S(1)}, f32[4,24,128]{2,1,0:T(8,128)}, u32[]{:S(2)}) copy-start(f32[4,24,128]{2,1,0:T(8,128)} %constant.6.clone.table_hbm.table_ref) | copy-start | bytes 147460
  2.5 6.3 %collective-permute-start.1 = (f32[234,128]{1,0:T(8,128)S(1)}, f32[234,128]{1,0:T(8,128)S(1)}, u32[]{:S(2)}, u32[]{:S(2)}) collective-permute-start(f32[234,128]{1,0:T(8,128)S(1)} %get-tuple-element.44), channel_id=1, source_target_pairs={{0,2},{2,0},{1,3},{3,1},{4,6},{6,4},{5,7},{7,5},{8,10},{10,8},{9,1... | collective-permute-start | bytes 359432 | tf_op jit(solution)/shard_map/ppermute | solution.py:698
  6.9 3.5 %collective-permute-start = (f32[5,4,16,1152]{3,2,1,0:T(8,128)S(1)}, f32[5,4,16,1152]{3,2,1,0:T(8,128)S(1)}, u32[]{:S(2)}, u32[]{:S(2)}) collective-permute-start(f32[5,4,16,1152]{3,2,1,0:T(8,128)S(1)} %get-tuple-element.43.refs_0_.refs_2_), channel_id=1, source_target_pairs={{0,1},{1,0},{2,3},{3,2},{4,5},{5,4},{6,7},{7,6},{8,9},{9,8},{10,11... | collective-permute-start | bytes 4423688 | tf_op jit(solution)/shard_map/ppermute | solution.py:700
  6.9 3.4 %copy-start.3 = (f32[16]{0:T(128)S(1)}, f32[16]{0:T(128)}, u32[]{:S(2)}) copy-start(f32[16]{0:T(128)} %param.13) | copy-start | bytes 196
  7.0 7.8 %collective-permute-start.3 = (f32[48,1152]{1,0:T(8,128)S(1)}, f32[48,1152]{1,0:T(8,128)S(1)}, u32[]{:S(2)}, u32[]{:S(2)}) collective-permute-start(f32[48,1152]{1,0:T(8,128)S(1)} %get-tuple-element.45.refs_0_.refs_8_), channel_id=1, source_target_pairs={{0,2},{2,0},{1,3},{3,1},{4,6},{6,4},{5,7},{7,5},{8,10},{10,8},{9,1... | collective-permute-start | bytes 663560 | tf_op jit(solution)/shard_map/ppermute | solution.py:698
  8.9 1.4 %collective-permute-start.2 = (f32[16,1152]{1,0:T(8,128)S(1)}, f32[16,1152]{1,0:T(8,128)S(1)}, u32[]{:S(2)}, u32[]{:S(2)}) collective-permute-start(f32[16,1152]{1,0:T(8,128)S(1)} %get-tuple-element.46.refs_0_), channel_id=1, source_target_pairs={{0,1},{1,0},{2,3},{3,2},{4,5},{5,4},{6,7},{7,6},{8,9},{9,8},{10,11... | collective-permute-start | bytes 221192 | tf_op jit(solution)/shard_map/ppermute | solution.py:700
  11.8 11.6 %copy-start.4 = (s32[16]{0:T(128)S(1)}, s32[16]{0:T(128)}, u32[]{:S(2)}) copy-start(s32[16]{0:T(128)} %param.14) | copy-start | bytes 196
  11.8 11.7 %copy-start = (bf16[5,256,256]{2,1,0:T(8,128)(2,1)S(1)}, bf16[5,256,256]{2,1,0:T(8,128)(2,1)}, u32[]{:S(2)}) copy-start(bf16[5,256,256]{2,1,0:T(8,128)(2,1)} %constant.7.clone.high_ref) | copy-start | bytes 1966084
  11.8 11.7 %copy-start.1 = (bf16[5,256,256]{2,1,0:T(8,128)(2,1)S(1)}, bf16[5,256,256]{2,1,0:T(8,128)(2,1)}, u32[]{:S(2)}) copy-start(bf16[5,256,256]{2,1,0:T(8,128)(2,1)} %constant.8.clone.low_ref) | copy-start | bytes 1966084
  11.9 21.0 %collective-permute-start.15 = (f32[176,1152]{1,0:T(8,128)S(1)}, f32[176,1152]{1,0:T(8,128)S(1)}, u32[]{:S(2)}, u32[]{:S(2)}) collective-permute-start(f32[176,1152]{1,0:T(8,128)S(1)} %remap_parts.3.refs_0_), channel_id=1, source_target_pairs={{0,2},{2,0},{1,3},{3,1},{4,6},{6,4},{5,7},{7,5},{8,10},{10,8},{9,1... | collective-permute-start | bytes 2433032 | tf_op jit(solution)/shard_map/ppermute | solution.py:698
  15.2 8.2 %collective-permute-start.5 = (f32[8,4,1,1152]{3,2,1,0:T(1,128)S(1)}, f32[8,4,1,1152]{3,2,1,0:T(1,128)S(1)}, u32[]{:S(2)}, u32[]{:S(2)}) collective-permute-start(f32[8,4,1,1152]{3,2,1,0:T(1,128)S(1)} %get-tuple-element.50), channel_id=1, source_target_pairs={{4,0},{8,4},{12,8},{5,1},{9,5},{13,9},{6,2},{10,6},{14,10},{7,3},{... | collective-permute-start | bytes 442376 | tf_op jit(solution)/shard_map/ppermute | solution.py:747
  16.5 6.9 %collective-permute-start.4 = (f32[6,4,1,1152]{3,2,1,0:T(1,128)S(1)}, f32[6,4,1,1152]{3,2,1,0:T(1,128)S(1)}, u32[]{:S(2)}, u32[]{:S(2)}) collective-permute-start(f32[6,4,1,1152]{3,2,1,0:T(1,128)S(1)} %get-tuple-element.49), channel_id=1, source_target_pairs={{0,4},{4,8},{8,12},{1,5},{5,9},{9,13},{2,6},{6,10},{10,14},{3,7},{... | collective-permute-start | bytes 331784 | tf_op jit(solution)/shard_map/ppermute | solution.py:746
  27.1 2.5 %collective-permute-start.13 = (f32[1,4,16,1152]{3,2,1,0:T(8,128)S(1)}, f32[1,4,16,1152]{3,2,1,0:T(8,128)S(1)}, u32[]{:S(2)}, u32[]{:S(2)}) collective-permute-start(f32[1,4,16,1152]{3,2,1,0:T(8,128)S(1)} %get-tuple-element.55.refs_2_), channel_id=1, source_target_pairs={{0,1},{1,0},{2,3},{3,2},{4,5},{5,4},{6,7},{7,6},{8,9},{9,8},{10,11... | collective-permute-start | bytes 884744 | tf_op jit(solution)/shard_map/ppermute | solution.py:700
  27.2 2.4 %collective-permute-start.14 = (f32[1,4,16,1152]{3,2,1,0:T(8,128)S(1)}, f32[1,4,16,1152]{3,2,1,0:T(8,128)S(1)}, u32[]{:S(2)}, u32[]{:S(2)}) collective-permute-start(f32[1,4,16,1152]{3,2,1,0:T(8,128)S(1)} %get-tuple-element.56.refs_4_), channel_id=1, source_target_pairs={{0,1},{1,0},{2,3},{3,2},{4,5},{5,4},{6,7},{7,6},{8,9},{9,8},{10,11... | collective-permute-start | bytes 884744 | tf_op jit(solution)/shard_map/ppermute | solution.py:700
  27.7 10.7 %collective-permute-start.7 = (f32[7,4,2,1152]{3,2,1,0:T(2,128)S(1)}, f32[7,4,2,1152]{3,2,1,0:T(2,128)S(1)}, u32[]{:S(2)}, u32[]{:S(2)}) collective-permute-start(f32[7,4,2,1152]{3,2,1,0:T(2,128)S(1)} %get-tuple-element.51.refs_6_.refs_0_), channel_id=1, source_target_pairs={{0,2},{2,0},{1,3},{3,1},{4,6},{6,4},{5,7},{7,5},{8,10},{10,8},{9,1... | collective-permute-start | bytes 774152 | tf_op jit(solution)/shard_map/ppermute | solution.py:698
  34.6 14.2 %collective-permute-start.16 = (f32[112,1152]{1,0:T(8,128)S(1)}, f32[112,1152]{1,0:T(8,128)S(1)}, u32[]{:S(2)}, u32[]{:S(2)}) collective-permute-start(f32[112,1152]{1,0:T(8,128)S(1)} %get-tuple-element.57.refs_12_), channel_id=1, source_target_pairs={{0,2},{2,0},{1,3},{3,1},{4,6},{6,4},{5,7},{7,5},{8,10},{10,8},{9,1... | collective-permute-start | bytes 1548296 | tf_op jit(solution)/shard_map/ppermute | solution.py:698
  36.6 1.8 %collective-permute-start.9 = (f32[1,4,3,1152]{3,2,1,0:T(4,128)S(1)}, f32[1,4,3,1152]{3,2,1,0:T(4,128)S(1)}, u32[]{:S(2)}, u32[]{:S(2)}) collective-permute-start(f32[1,4,3,1152]{3,2,1,0:T(4,128)S(1)} %get-tuple-element.53.refs_4_), channel_id=1, source_target_pairs={{0,1},{1,0},{2,3},{3,2},{4,5},{5,4},{6,7},{7,6},{8,9},{9,8},{10,11... | collective-permute-start | bytes 165896 | tf_op jit(solution)/shard_map/ppermute | solution.py:700
  36.6 2.3 %collective-permute-start.10 = (f32[1,4,3,1152]{3,2,1,0:T(4,128)S(1)}, f32[1,4,3,1152]{3,2,1,0:T(4,128)S(1)}, u32[]{:S(2)}, u32[]{:S(2)}) collective-permute-start(f32[1,4,3,1152]{3,2,1,0:T(4,128)S(1)} %get-tuple-element.54.refs_6_), channel_id=1, source_target_pairs={{0,1},{1,0},{2,3},{3,2},{4,5},{5,4},{6,7},{7,6},{8,9},{9,8},{10,11... | collective-permute-start | bytes 165896 | tf_op jit(solution)/shard_map/ppermute | solution.py:700
  37.1 3.4 %collective-permute-start.6 = (f32[7,4,2,1152]{3,2,1,0:T(2,128)S(1)}, f32[7,4,2,1152]{3,2,1,0:T(2,128)S(1)}, u32[]{:S(2)}, u32[]{:S(2)}) collective-permute-start(f32[7,4,2,1152]{3,2,1,0:T(2,128)S(1)} %get-tuple-element.51.refs_6_.refs_0_), channel_id=1, source_target_pairs={{0,1},{1,0},{2,3},{3,2},{4,5},{5,4},{6,7},{7,6},{8,9},{9,8},{10,11... | collective-permute-start | bytes 774152 | tf_op jit(solution)/shard_map/ppermute | solution.py:700
  38.3 2.2 %collective-permute-start.8 = (f32[7,4,2,1152]{3,2,1,0:T(2,128)S(1)}, f32[7,4,2,1152]{3,2,1,0:T(2,128)S(1)}, u32[]{:S(2)}, u32[]{:S(2)}) collective-permute-start(f32[7,4,2,1152]{3,2,1,0:T(2,128)S(1)} %collective-permute-done.7.refs_2_), channel_id=1, source_target_pairs={{0,1},{1,0},{2,3},{3,2},{4,5},{5,4},{6,7},{7,6},{8,9},{9,8},{10,11... | collective-permute-start | bytes 774152 | tf_op jit(solution)/shard_map/ppermute | solution.py:700
  38.3 1.8 %collective-permute-start.11 = (f32[48,1152]{1,0:T(8,128)S(1)}, f32[48,1152]{1,0:T(8,128)S(1)}, u32[]{:S(2)}, u32[]{:S(2)}) collective-permute-start(f32[48,1152]{1,0:T(8,128)S(1)} %get-tuple-element.45.refs_0_.refs_8_), channel_id=1, source_target_pairs={{0,1},{1,0},{2,3},{3,2},{4,5},{5,4},{6,7},{7,6},{8,9},{9,8},{10,11... | collective-permute-start | bytes 663560 | tf_op jit(solution)/shard_map/ppermute | solution.py:700
  38.9 1.6 %collective-permute-start.12 = (f32[48,1152]{1,0:T(8,128)S(1)}, f32[48,1152]{1,0:T(8,128)S(1)}, u32[]{:S(2)}, u32[]{:S(2)}) collective-permute-start(f32[48,1152]{1,0:T(8,128)S(1)} %collective-permute-done.3.refs_1_.refs_10_), channel_id=1, source_target_pairs={{0,1},{1,0},{2,3},{3,2},{4,5},{5,4},{6,7},{7,6},{8,9},{9,8},{10,11... | collective-permute-start | bytes 663560 | tf_op jit(solution)/shard_map/ppermute | solution.py:700
